TPU v7x, 32 devices: a whole 2x2x4 slice. The times are simulated.
32 devices in a mesh: group: 2 (over y), row: 4 (over z), col: 4 (over x, core).
Axes of the slice: x: 2, y: 2, z: 4, core: 2. Of those that a mesh axis runs over, the one named last changes fastest.
Arguments:
- tokens: bfloat16 [512, 10240], P(('group', 'col'), 'row'), parts along dimension 0, may hold values from -6 to 6
- token_job_index: int32 [512], P('group'), parts along dimension 0, may hold values from 0 to 3, never falling along the last dimension, each value on 1 to 128 neighbouring positions
- job_adapter_index: int32 [8], P('group'), parts along dimension 0, may hold values from 0 to 7
- first_weight: bfloat16 [10240, 24576], P('row', 'col'), may hold values from -0.0625 to 0.0625
- first_bias: float32 [24576], P('col'), may hold values from -3 to 3
- first_down_maps: bfloat16 [10240, 128], P('row'), may hold values from -0.0625 to 0.0625
- first_up_maps: bfloat16 [128, 24576], P(None, 'col'), may hold values from -1.5 to 1.5
- second_weight: bfloat16 [24576, 10240], P('col', 'row'), may hold values from -0.0390625 to 0.0390625
- second_bias: float32 [10240], P('row'), may hold values from -3 to 3
- second_down_maps: bfloat16 [24576, 128], P('col'), may hold values from -0.0390625 to 0.0390625
- second_up_maps: bfloat16 [128, 10240], P(None, 'row'), may hold values from -1.5 to 1.5
Outputs:
- ffn_out: bfloat16 [512, 10240], P(('group', 'col'), 'row'), parts along dimension 0
There are 2 independent parts, one for each index of `group`. A program takes and returns all parts, laid end to end along the dimension named above; an argument that names none is the same for every part. Nothing has to cross between parts.
Inputs may be any that keep to these rules, and one draw needn't show every extreme that they name: token_job_index never falls along the tokens; each of the 4 jobs holds 1 to 128 tokens.
All inputs are finite; a program needn't handle non-finite values.
Results may differ from a plain program's by a relative error of at most 0.018.
Values may be sent and summed in bfloat16 or wider, within the bound.
No kernel may reach another device: no remote copies, remote signals or barrier semaphores. Data moves between devices by JAX's collectives and lax.ppermute only.
A program may use at most 192 MiB of HBM per device.

v0:
```python
import jax
import jax.numpy as jnp
from jax import lax
from jax.sharding import PartitionSpec as P

ADAPTER_RANK = 16
ADAPTER_COUNT = 8
JOBS = 4


def gelu_tanh(values):
    return (
        0.5
        * values
        * (1.0 + jnp.tanh(0.7978845608 * (values + 0.044715 * values * values * values)))
    )


def token_mask(token_job_index, job_adapter_index):
    one_hot = token_job_index[:, None] == jnp.arange(JOBS, dtype=jnp.int32)[None, :]
    chosen = jnp.sum(jnp.where(one_hot, job_adapter_index[None, :], 0), axis=1)
    slot_ids = jnp.arange(ADAPTER_COUNT * ADAPTER_RANK, dtype=jnp.int32) // ADAPTER_RANK
    return (slot_ids[None, :] == chosen[:, None]).astype(jnp.int32)


def spread_own(columns, row_job_mask):
    return jnp.where(row_job_mask == 1, columns, 0.0).astype(jnp.bfloat16)


def apply_gelu(combined_totals, row_job_mask, first_bias, first_up_maps):
    width = first_bias.shape[0]
    reduced_state = spread_own(combined_totals[:, width:], row_job_mask)
    preactivation_sum = (
        combined_totals[:, :width]
        + first_bias[None, :]
        + jnp.dot(reduced_state, first_up_maps, preferred_element_type=jnp.float32)
    )
    return gelu_tanh(preactivation_sum).astype(jnp.bfloat16)


def local(
    tokens,
    token_job_index,
    job_adapter_index,
    first_weight,
    first_bias,
    first_down_maps,
    first_up_maps,
    second_weight,
    second_bias,
    second_down_maps,
    second_up_maps,
):
    mask_all = token_mask(token_job_index, job_adapter_index)
    out_rows = tokens.shape[0]
    row_block_slice = lax.all_gather(tokens, "col", axis=0, tiled=True)
    joined = jnp.concatenate(
        [
            jnp.dot(row_block_slice, first_weight, preferred_element_type=jnp.float32),
            jnp.dot(row_block_slice, first_down_maps, preferred_element_type=jnp.float32),
        ],
        axis=1,
    )
    combined_totals = lax.psum_scatter(
        joined.astype(jnp.bfloat16), "row", scatter_dimension=0, tiled=True
    ).astype(jnp.float32)
    row_count = combined_totals.shape[0]
    row_job_mask = lax.dynamic_slice_in_dim(
        mask_all, lax.axis_index("row") * row_count, row_count, 0
    )
    local_token_rows = apply_gelu(combined_totals, row_job_mask, first_bias, first_up_maps)
    hidden_state = lax.all_gather(local_token_rows, "row", axis=0, tiled=True)
    row_block_slice = hidden_state
    outputs = lax.psum_scatter(
        jnp.concatenate(
            [
                jnp.dot(row_block_slice, second_weight, preferred_element_type=jnp.float32),
                jnp.dot(row_block_slice, second_down_maps, preferred_element_type=jnp.float32),
            ],
            axis=1,
        ).astype(jnp.bfloat16),
        "col",
        scatter_dimension=0,
        tiled=True,
    ).astype(jnp.float32)
    mask_out = lax.dynamic_slice_in_dim(mask_all, lax.axis_index("col") * out_rows, out_rows, 0)
    out_width = second_weight.shape[1]
    reduced_state = spread_own(outputs[:, out_width:], mask_out)
    layer_output = (
        outputs[:, :out_width]
        + second_bias[None, :]
        + jnp.dot(reduced_state, second_up_maps, preferred_element_type=jnp.float32)
    )
    return layer_output.astype(jnp.bfloat16)


def solution(mesh):
    return jax.shard_map(
        local,
        mesh=mesh,
        in_specs=(
            P(("group", "col"), "row"),
            P("group"),
            P("group"),
            P("row", "col"),
            P("col"),
            P("row", None),
            P(None, "col"),
            P("col", "row"),
            P("row"),
            P("col", None),
            P(None, "row"),
        ),
        out_specs=P(("group", "col"), "row"),
        check_vma=False,
    )
```

profile of v0, /device:TPU:0, one launch (start us, length us, event | category | flops | bytes accessed | tf_op | source)
XLA Modules:
  0.0 228.8 jit_solution(17016781411800550896)
XLA Ops:
  6.5 0.0 copy-start
  6.5 0.0 all-gather.3.cloned.1.call-start
  6.5 0.7 all-gather.3.cloned.1.call-update
  7.3 0.0 reduce-scatter.3.cloned.1.call-start
  7.3 22.5 %all-gather.3.cloned.1.call-done = bf16[256,2560]{1,0:T(8,128)(2,1)} async-done(((bf16[64,2560]{1,0:T(8,128)(2,1)}), bf16[256,2560]{1,0:T(8,128)(2,1)}) %all-gather.3.cloned.1.call-update) | async-done | bytes 1310736 | tf_op jit(solution)/shard_map/all_gather | solution.py:56
  29.8 0.0 copy-start.4
  29.8 2.1 convolution_convert_fusion.3
  31.9 0.0 copy-done.4
  31.9 14.2 %convolution_convert_fusion = bf16[256,6144]{1,0:T(8,128)(2,1)S(1)} fusion(bf16[256,2560]{1,0:T(8,128)(2,1)S(1)} %copy-done.4, bf16[2560,6144]{1,0:T(8,128)(2,1)} %param.14), kind=kOutput, calls=%fused_computation | convolution fusion | flops 8054636544 | bytes 35913728 | tf_op jit(solution)/shard_map/dot_general | solution.py:59
  46.1 1.9 pad_maximum_fusion
  48.1 0.0 copy-start.7
  48.1 0.0 copy-start.8
  48.1 0.0 reduce-scatter.3.cloned.1.call-update
  48.1 0.0 copy-start.9
  48.1 0.0 all-gather.5.cloned.1.call-start
  48.2 0.6 copy-done.7
  48.7 0.0 copy-done.8
  48.7 0.1 select_reduce_fusion
  48.8 0.1 compare_convert_fusion
  48.9 60.6 %reduce-scatter.3.cloned.1.call-done = bf16[64,6272]{1,0:T(8,128)(2,1)} async-done(((bf16[256,6272]{1,0:T(8,128)(2,1)}), bf16[64,6272]{1,0:T(8,128)(2,1)}) %reduce-scatter.3.cloned.1.call-update) | async-done | bytes 802832 | tf_op jit(solution)/shard_map/reduce_scatter | solution.py:64
  109.5 1.2 convert_element_type.23
  110.8 0.0 copy-done
  110.8 0.0 copy-done.9
  110.8 0.0 copy-start.3
  110.8 1.7 fusion.5
  112.6 0.0 all-gather.5.cloned.1.call-update
  112.6 0.0 reduce-scatter.5.cloned.1.call-start
  112.6 63.7 %all-gather.5.cloned.1.call-done = bf16[256,6144]{1,0:T(8,128)(2,1)} async-done(((bf16[64,6144]{1,0:T(8,128)(2,1)}), bf16[256,6144]{1,0:T(8,128)(2,1)}) %all-gather.5.cloned.1.call-update) | async-done | bytes 3145744 | tf_op jit(solution)/shard_map/all_gather | solution.py:72
  176.3 0.0 copy-done.3
  176.3 0.0 copy-start.2
  176.3 3.0 %convolution_convert_fusion.2 = bf16[256,128]{1,0:T(8,128)(2,1)S(1)} fusion(bf16[256,6144]{1,0:T(8,128)(2,1)} %all-gather.5.cloned.1.call-done, bf16[6144,128]{1,0:T(8,128)(2,1)S(1)} %copy-done.3), kind=kOutput, calls=%fused_computation.14 | convolution fusion | flops 402685952 | bytes 4784128 | tf_op jit(solution)/shard_map/dot_general | solution.py:78
  179.3 0.0 copy-done.2
  179.3 13.9 %convolution_convert_fusion.1 = bf16[256,2560]{1,0:T(8,128)(2,1)S(1)} fusion(bf16[256,6144]{1,0:T(8,128)(2,1)S(1)} %copy-done.2, bf16[6144,2560]{1,0:T(8,128)(2,1)} %param.18), kind=kOutput, calls=%fused_computation.2 | convolution fusion | flops 8053719040 | bytes 35913728 | tf_op jit(solution)/shard_map/dot_general | solution.py:77
  193.2 1.2 pad_maximum_fusion.1
  194.4 0.0 copy-start.5
  194.4 0.0 copy-start.6
  194.4 0.0 copy-start.1
  194.4 0.0 reduce-scatter.5.cloned.1.call-update
  194.4 25.8 %reduce-scatter.5.cloned.1.call-done = bf16[64,2688]{1,0:T(8,128)(2,1)} async-done(((bf16[256,2688]{1,0:T(8,128)(2,1)}), bf16[64,2688]{1,0:T(8,128)(2,1)}) %reduce-scatter.5.cloned.1.call-update) | async-done | bytes 344080 | tf_op jit(solution)/shard_map/reduce_scatter | solution.py:74
  220.2 1.0 convert_element_type.27
  221.2 0.0 copy-done.5
  221.2 0.0 copy-done.6
  221.2 1.0 fusion
  222.2 0.0 copy-done.1
  (1 shorter events, 0.0 us)
Async XLA Ops:
  6.5 104.2 %copy-start = (bf16[128,6144]{1,0:T(8,128)(2,1)S(1)}, bf16[128,6144]{1,0:T(8,128)(2,1)}, u32[]{:S(2)}) copy-start(bf16[128,6144]{1,0:T(8,128)(2,1)} %param.17) | copy-start | bytes 4718596
  6.5 23.3 %all-gather.3.cloned.1.call-start = ((), (), s32[]{:S(2)}) async-start(), calls=%async_computation.2 | async-start | bytes 1638400 | tf_op jit(solution)/shard_map/all_gather | solution.py:56
  7.3 102.3 %reduce-scatter.3.cloned.1.call-start = ((), (), s32[]{:S(2)}) async-start(), calls=%async_computation.3 | async-start | bytes 4014080 | tf_op jit(solution)/shard_map/reduce_scatter | solution.py:64
  29.8 2.1 copy-start.4
  48.1 0.7 copy-start.7
  48.1 0.7 copy-start.8
  48.1 62.7 %copy-start.9 = (f32[6144]{0:T(1024)S(1)}, f32[6144]{0:T(1024)}, u32[]{:S(2)}) copy-start(f32[6144]{0:T(1024)} %param.15) | copy-start | bytes 73732
  48.1 128.2 %all-gather.5.cloned.1.call-start = ((), (), s32[]{:S(2)}) async-start(), calls=%async_computation.4 | async-start | bytes 3932160 | tf_op jit(solution)/shard_map/all_gather | solution.py:72
  110.8 65.5 %copy-start.3 = (bf16[6144,128]{1,0:T(8,128)(2,1)S(1)}, bf16[6144,128]{1,0:T(8,128)(2,1)}, u32[]{:S(2)}) copy-start(bf16[6144,128]{1,0:T(8,128)(2,1)} %param.20) | copy-start | bytes 4718596
  112.6 107.6 %reduce-scatter.5.cloned.1.call-start = ((), (), s32[]{:S(2)}) async-start(), calls=%async_computation.5 | async-start | bytes 1720320 | tf_op jit(solution)/shard_map/reduce_scatter | solution.py:74
  176.3 3.0 %copy-start.2 = (bf16[256,6144]{1,0:T(8,128)(2,1)S(1)}, bf16[256,6144]{1,0:T(8,128)(2,1)}, u32[]{:S(2)}) copy-start(bf16[256,6144]{1,0:T(8,128)(2,1)} %all-gather.5.cloned.1.call-done) | copy-start | bytes 9437188
  194.4 26.8 %copy-start.5 = (bf16[128,2560]{1,0:T(8,128)(2,1)S(1)}, bf16[128,2560]{1,0:T(8,128)(2,1)}, u32[]{:S(2)}) copy-start(bf16[128,2560]{1,0:T(8,128)(2,1)} %param.21) | copy-start | bytes 1966084
  194.4 26.8 %copy-start.6 = (f32[2560]{0:T(1024)S(1)}, f32[2560]{0:T(1024)}, u32[]{:S(2)}) copy-start(f32[2560]{0:T(1024)} %param.19) | copy-start | bytes 30724
  194.4 27.8 %copy-start.1 = (bf16[128,6144]{1,0:T(8,128)(2,1)S(1)}, bf16[128,6144]{1,0:T(8,128)(2,1)}, u32[]{:S(2)}) copy-start(bf16[128,6144]{1,0:T(8,128)(2,1)} %param.17) | copy-start | bytes 4718596
Sparse Core Ops, SparseCore 0:
  8.9 20.8 all-gather.2
  48.2 61.2 reduce-scatter.2
  112.7 63.5 all-gather.4
  194.6 25.5 reduce-scatter.4
where the time goes:
time: 229 us
  waiting for transfers between devices  173 us (76%)
  matrix products  35.9 us (16%)
  between operations  13.3 us (6%)
  other arithmetic  5.56 us (2%)
    all_gather x1, waiting for transfers between devices, local(): hidden_state = lax.all_gather(local_token_rows, 'row', axis=0, tiled=True)  63.7 us
    reduce_scatter x1, waiting for transfers between devices, local(): lax.psum_scatter(joined.astype(jnp.bfloat16), 'row', scatter_dimension=0,...  60.6 us
    reduce_scatter x1, waiting for transfers between devices, local(): lax.psum_scatter(jnp.concatenate([jnp.dot(row_block_slice, second_weight,...  25.8 us
    all_gather x1, waiting for transfers between devices, local(): row_block_slice = lax.all_gather(tokens, 'col', axis=0, tiled=True)  22.5 us
    dot_general x1, matrix products, local(): jnp.dot(row_block_slice, first_weight, preferred_element_type=jnp.float32)  14.2 us
    dot_general x1, matrix products, local(): jnp.dot(row_block_slice, second_weight, preferred_element_type=jnp.float32)  13.9 us
  transfers between devices with their start and end apart: 4, of which 4 were waited for; matrix products, arithmetic and copies ran while one was open for 0% of the time, Pallas kernels for 0%

commit v1 on v0

v1 whole, which is shorter than its diff:
```python
import jax
import jax.numpy as jnp
from jax import lax
from jax.sharding import PartitionSpec as P

ADAPTER_RANK = 16
ADAPTER_COUNT = 8
JOBS = 4
CHUNKS = 8
F32 = jnp.float32
BF16 = jnp.bfloat16


def gelu_tanh(values):
    return (
        0.5
        * values
        * (1.0 + jnp.tanh(0.7978845608 * (values + 0.044715 * values * values * values)))
    )


def token_mask(token_job_index, job_adapter_index):
    one_hot = token_job_index[:, None] == jnp.arange(JOBS, dtype=jnp.int32)[None, :]
    chosen = jnp.sum(jnp.where(one_hot, job_adapter_index[None, :], 0), axis=1)
    slot_ids = jnp.arange(ADAPTER_COUNT * ADAPTER_RANK, dtype=jnp.int32) // ADAPTER_RANK
    return slot_ids[None, :] == chosen[:, None]


def dot(left, right):
    return jnp.dot(left, right, preferred_element_type=F32)


def add_rounded(left, right):
    return (left.astype(F32) + right.astype(F32)).astype(BF16)


def make_local(n_row, n_col):
    chips = n_col // 2
    half = n_row // 2

    def col_swap(value, flip):
        return lax.ppermute(value, "col", [(i, i ^ flip) for i in range(n_col)])

    def gather_tokens(tokens):
        shards = [tokens, col_swap(tokens, 1)]
        for step in range(1, chips):
            far = col_swap(tokens, 2 * step)
            shards += [far, col_swap(far, 1)]
        return jnp.concatenate(shards, axis=0)

    def fold_rows(value):
        for step in range(half - 1):
            pairs = [(step, step + 1), (n_row - 1 - step, n_row - 2 - step)]
            value = add_rounded(value, lax.ppermute(value, "row", pairs))
        return value

    def cross_rows(value):
        if n_row == 1:
            return value.astype(F32)
        other = lax.ppermute(value, "row", [(half - 1, half), (half, half - 1)])
        return value.astype(F32) + other.astype(F32)

    def spread_rows(value, place):
        for step in reversed(range(half - 1)):
            pairs = [(step + 1, step), (n_row - 2 - step, n_row - 1 - step)]
            come = lax.ppermute(value, "row", pairs)
            value = jnp.where((place <= step) | (place >= n_row - 1 - step), come, value)
        return value

    def local(
        tokens,
        token_job_index,
        job_adapter_index,
        first_weight,
        first_bias,
        first_down_maps,
        first_up_maps,
        second_weight,
        second_bias,
        second_down_maps,
        second_up_maps,
    ):
        rows = tokens.shape[0]
        hidden = first_weight.shape[1]
        width = hidden // CHUNKS
        out_width = second_weight.shape[1]
        place = lax.axis_index("row")
        mine = lax.axis_index("col")
        mask_all = token_mask(token_job_index, job_adapter_index)
        mask = jnp.concatenate(
            [
                lax.dynamic_slice_in_dim(mask_all, (mine ^ i) * rows, rows, 0)
                for i in range(n_col)
            ],
            axis=0,
        )
        gathered = gather_tokens(tokens)
        total = None
        low_in = None
        for chunk in range(CHUNKS):
            span = slice(chunk * width, (chunk + 1) * width)
            partial = dot(gathered, first_weight[:, span]).astype(BF16)
            if chunk == 0:
                low = dot(gathered, first_down_maps).astype(BF16)
                partial = jnp.concatenate([partial, low], axis=1)
            summed = cross_rows(fold_rows(partial))
            if chunk == 0:
                low_in = jnp.where(mask, summed[:, width:], 0.0).astype(BF16)
                summed = summed[:, :width]
            before = summed + first_bias[None, span] + dot(low_in, first_up_maps[:, span])
            states = spread_rows(gelu_tanh(before).astype(BF16), place)
            part = dot(states, second_weight[span])
            low_part = dot(states, second_down_maps[span])
            total = part if total is None else total + part
            low_total = low_part if chunk == 0 else low_total + low_part
        outputs = jnp.concatenate([total, low_total], axis=1)
        blocks = [outputs[i * rows : (i + 1) * rows] for i in range(n_col)]
        ours = jnp.concatenate(blocks[0::2], axis=0)
        theirs = jnp.concatenate(blocks[1::2], axis=0).astype(BF16)
        ours = ours + col_swap(theirs, 1).astype(F32)
        result = ours[:rows]
        for step in range(1, chips):
            piece = ours[step * rows : (step + 1) * rows].astype(BF16)
            result = result + col_swap(piece, 2 * step).astype(F32)
        low_out = jnp.where(mask[:rows], result[:, out_width:], 0.0).astype(BF16)
        layer_output = result[:, :out_width] + second_bias[None, :] + dot(low_out, second_up_maps)
        return layer_output.astype(BF16)

    return local


def solution(mesh):
    return jax.shard_map(
        make_local(mesh.shape["row"], mesh.shape["col"]),
        mesh=mesh,
        in_specs=(
            P(("group", "col"), "row"),
            P("group"),
            P("group"),
            P("row", "col"),
            P("col"),
            P("row", None),
            P(None, "col"),
            P("col", "row"),
            P("row"),
            P("col", None),
            P(None, "row"),
        ),
        out_specs=P(("group", "col"), "row"),
        check_vma=False,
    )
```

time: 229 us -> 260 us (1.14)
  starting transfers between devices: 0.12 us -> 43 us
  matrix products: 35.9 us -> 54.7 us
  waiting for transfers between devices: 173 us -> 156 us
  between operations: 13.3 us -> 0.75 us
  other arithmetic: 5.56 us -> 2.33 us
    ppermute x0 -> x29, waiting for transfers between devices: none -> 156 us  [the longest x8 89.8 us: spread_rows(): come = lax.ppermute(value, 'row', pairs)]
    reduce_scatter x2 -> x0, waiting for transfers between devices: 86.4 us -> none  [the longest x1 60.6 us: local(): lax.psum_scatter(joined.astype(jnp.bfloat16), 'row', scatter_dimension=0,...]
    all_gather x2 -> x0, waiting for transfers between devices: 86.2 us -> none  [the longest x1 63.7 us: local(): hidden_state = lax.all_gather(local_token_rows, 'row', axis=0, tiled=True)]
    ppermute x0 -> x29, starting transfers between devices: none -> 43 us  [the longest x8 22.2 us: fold_rows(): value = add_rounded(value, lax.ppermute(value, 'row', pairs))]
    dot_general x6 -> x34, matrix products: 35.9 us -> 54.7 us  [dot(): return jnp.dot(left, right, preferred_element_type=F32)]
    concatenate x2 -> x3, other arithmetic: 3.11 us -> 0.18 us  [the longest x1 0.09 us: local(): outputs = jnp.concatenate([total, low_total], axis=1)]
  transfers between devices with their start and end apart: 4 -> 29, of which waited for: 4 -> 14; matrix products, arithmetic and copies ran while one was open for 0% -> 13% of each run, Pallas kernels for 0% -> 0%
where the time goes in v1:
time: 260 us; the launch traced here: 259 us
  waiting for transfers between devices  156 us (60%)
  matrix products  54.7 us (21%)
  starting transfers between devices  43 us (17%)
    ppermute x8, waiting for transfers between devices, spread_rows(): come = lax.ppermute(value, 'row', pairs)  89.8 us
    dot_general x34, matrix products, dot(): return jnp.dot(left, right, preferred_element_type=F32)  54.7 us
    ppermute x8, waiting for transfers between devices, fold_rows(): value = add_rounded(value, lax.ppermute(value, 'row', pairs))  48.1 us
    ppermute x8, starting transfers between devices, fold_rows(): value = add_rounded(value, lax.ppermute(value, 'row', pairs))  22.2 us
    ppermute x5, waiting for transfers between devices, col_swap(): return lax.ppermute(value, 'col', [(i, i ^ flip) for i in range(n_col)])  18 us
    ppermute x8, starting transfers between devices, spread_rows(): come = lax.ppermute(value, 'row', pairs)  10.5 us
    ppermute x8, starting transfers between devices, cross_rows(): other = lax.ppermute(value, 'row', [(half - 1, half), (half, half - 1)])  5.63 us
  transfers between devices with their start and end apart: 29, of which 14 were waited for; matrix products, arithmetic and copies ran while one was open for 13% of the time, Pallas kernels for 0%

profile of v1, /device:TPU:0, one launch (start us, length us, event | category | flops | bytes accessed | tf_op | source)
XLA Modules:
  0.0 258.7 jit_solution(14832631091290456632)
XLA Ops:
  0.5 2.6 collective-permute-start.1
  3.0 0.8 fusion.169
  3.8 0.8 select_reduce_fusion
  4.8 1.0 constant_dynamic-update-slice_fusion.3
  5.8 5.8 %collective-permute-done.1 = bf16[64,2560]{1,0:T(8,128)(2,1)S(1)} collective-permute-done((bf16[64,2560]{1,0:T(8,128)(2,1)}, bf16[64,2560]{1,0:T(8,128)(2,1)S(1)}, u32[]{:S(2)}, u32[]{:S(2)}) %collective-permute-start.1) | collective-permute-done | bytes 327712 | tf_op jit(solution)/shard_map/ppermute | solution.py:42
  11.6 1.6 collective-permute-done.2
  13.2 3.4 %fusion.59 = bf16[256,768]{1,0:T(8,128)(2,1)S(1)} fusion(bf16[256,2560]{1,0:T(8,128)(2,1)S(1)} %constant_dynamic-update-slice_fusion, bf16[2560,6144]{1,0:T(8,128)(2,1)} %param.14), kind=kOutput, calls=%fused_computation.52 | convolution fusion | flops 1006829568 | bytes 5636096 | tf_op jit(solution)/shard_map/dot_general | solution.py:30
  16.7 4.0 %fusion.56 = bf16[256,768]{1,0:T(8,128)(2,1)S(1)} fusion(bf16[256,2560]{1,0:T(8,128)(2,1)S(1)} %constant_dynamic-update-slice_fusion, bf16[2560,6144]{1,0:T(8,128)(2,1)} %param.14), kind=kOutput, calls=%fused_computation.51 | convolution fusion | flops 1006829568 | bytes 5636096 | tf_op jit(solution)/shard_map/dot_general | solution.py:30
  20.7 4.0 %fusion.53 = bf16[256,768]{1,0:T(8,128)(2,1)S(1)} fusion(bf16[256,2560]{1,0:T(8,128)(2,1)S(1)} %constant_dynamic-update-slice_fusion, bf16[2560,6144]{1,0:T(8,128)(2,1)} %param.14), kind=kOutput, calls=%fused_computation.50 | convolution fusion | flops 1006829568 | bytes 5636096 | tf_op jit(solution)/shard_map/dot_general | solution.py:30
  24.7 4.0 %fusion.50 = bf16[256,768]{1,0:T(8,128)(2,1)S(1)} fusion(bf16[256,2560]{1,0:T(8,128)(2,1)S(1)} %constant_dynamic-update-slice_fusion, bf16[2560,6144]{1,0:T(8,128)(2,1)} %param.14), kind=kOutput, calls=%fused_computation.49 | convolution fusion | flops 1006829568 | bytes 5636096 | tf_op jit(solution)/shard_map/dot_general | solution.py:30
  28.8 1.2 fusion.47
  30.0 1.2 fusion.44
  31.2 1.2 fusion.41
  32.4 1.2 fusion.38
  33.6 3.8 %collective-permute-start.6 = (bf16[256,768]{1,0:T(8,128)(2,1)S(1)}, bf16[256,768]{1,0:T(8,128)(2,1)S(1)}, u32[]{:S(2)}, u32[]{:S(2)}) collective-permute-start(bf16[256,768]{1,0:T(8,128)(2,1)S(1)} %fusion.41), channel_id=1, source_target_pairs={{0,4},{12,8},{1,5},{13,9},{2,6},{14,10},{3,7},{15,11},{16,20},{28,... | collective-permute-start | bytes 1179656 | tf_op jit(solution)/shard_map/ppermute | solution.py:54
  37.4 1.3 collective-permute-start.9
  39.2 1.3 collective-permute-start.12
  40.5 1.3 collective-permute-start.15
  41.8 1.3 collective-permute-start.18
  43.2 3.6 %collective-permute-done.6 = bf16[256,768]{1,0:T(8,128)(2,1)S(1)} collective-permute-done((bf16[256,768]{1,0:T(8,128)(2,1)S(1)}, bf16[256,768]{1,0:T(8,128)(2,1)S(1)}, u32[]{:S(2)}, u32[]{:S(2)}) %collective-permute-start.6) | collective-permute-done | bytes 393248 | tf_op jit(solution)/shard_map/ppermute | solution.py:54
  46.8 4.4 %collective-permute-start.21 = (bf16[256,768]{1,0:T(8,128)(2,1)S(1)}, bf16[256,768]{1,0:T(8,128)(2,1)S(1)}, u32[]{:S(2)}, u32[]{:S(2)}) collective-permute-start(bf16[256,768]{1,0:T(8,128)(2,1)S(1)} %fusion.56), channel_id=1, source_target_pairs={{0,4},{12,8},{1,5},{13,9},{2,6},{14,10},{3,7},{15,11},{16,20},{28,... | collective-permute-start | bytes 1179656 | tf_op jit(solution)/shard_map/ppermute | solution.py:54
  51.3 3.9 %collective-permute-done.9 = bf16[256,768]{1,0:T(8,128)(2,1)S(1)} collective-permute-done((bf16[256,768]{1,0:T(8,128)(2,1)S(1)}, bf16[256,768]{1,0:T(8,128)(2,1)S(1)}, u32[]{:S(2)}, u32[]{:S(2)}) %collective-permute-start.9) | collective-permute-done | bytes 393248 | tf_op jit(solution)/shard_map/ppermute | solution.py:54
  55.2 4.4 %collective-permute-start.24 = (bf16[256,768]{1,0:T(8,128)(2,1)S(1)}, bf16[256,768]{1,0:T(8,128)(2,1)S(1)}, u32[]{:S(2)}, u32[]{:S(2)}) collective-permute-start(bf16[256,768]{1,0:T(8,128)(2,1)S(1)} %fusion.59), channel_id=1, source_target_pairs={{0,4},{12,8},{1,5},{13,9},{2,6},{14,10},{3,7},{15,11},{16,20},{28,... | collective-permute-start | bytes 1179656 | tf_op jit(solution)/shard_map/ppermute | solution.py:54
  59.7 3.9 %collective-permute-done.12 = bf16[256,768]{1,0:T(8,128)(2,1)S(1)} collective-permute-done((bf16[256,768]{1,0:T(8,128)(2,1)S(1)}, bf16[256,768]{1,0:T(8,128)(2,1)S(1)}, u32[]{:S(2)}, u32[]{:S(2)}) %collective-permute-start.12) | collective-permute-done | bytes 393248 | tf_op jit(solution)/shard_map/ppermute | solution.py:54
  63.7 4.4 %collective-permute-start.3 = (bf16[256,896]{1,0:T(8,128)(2,1)S(1)}, bf16[256,896]{1,0:T(8,128)(2,1)S(1)}, u32[]{:S(2)}, u32[]{:S(2)}) collective-permute-start(bf16[256,896]{1,0:T(8,128)(2,1)S(1)} %pad_maximum_fusion.2), channel_id=1, source_target_pairs={{0,4},{12,8},{1,5},{13,9},{2,6},{14,10},{3,7},{15,11},{16,20},{28,... | collective-permute-start | bytes 1376264 | tf_op jit(solution)/shard_map/ppermute | solution.py:54
  68.2 3.9 %collective-permute-done.15 = bf16[256,768]{1,0:T(8,128)(2,1)S(1)} collective-permute-done((bf16[256,768]{1,0:T(8,128)(2,1)S(1)}, bf16[256,768]{1,0:T(8,128)(2,1)S(1)}, u32[]{:S(2)}, u32[]{:S(2)}) %collective-permute-start.15) | collective-permute-done | bytes 393248 | tf_op jit(solution)/shard_map/ppermute | solution.py:54
  72.1 0.7 collective-permute-start.7
  72.9 7.6 %collective-permute-done.18 = bf16[256,768]{1,0:T(8,128)(2,1)S(1)} collective-permute-done((bf16[256,768]{1,0:T(8,128)(2,1)S(1)}, bf16[256,768]{1,0:T(8,128)(2,1)S(1)}, u32[]{:S(2)}, u32[]{:S(2)}) %collective-permute-start.18) | collective-permute-done | bytes 393248 | tf_op jit(solution)/shard_map/ppermute | solution.py:54
  80.5 0.7 collective-permute-start.10
  81.3 25.1 %collective-permute-done.3 = bf16[256,896]{1,0:T(8,128)(2,1)S(1)} collective-permute-done((bf16[256,896]{1,0:T(8,128)(2,1)S(1)}, bf16[256,896]{1,0:T(8,128)(2,1)S(1)}, u32[]{:S(2)}, u32[]{:S(2)}) %collective-permute-start.3) | collective-permute-done | bytes 458784 | tf_op jit(solution)/shard_map/ppermute | solution.py:54
  106.4 0.7 collective-permute-start.13
  107.2 0.7 collective-permute-start.4
  108.0 0.7 collective-permute-start.16
  108.8 0.7 collective-permute-start.19
  109.6 0.7 collective-permute-start.22
  110.3 0.5 fusion.82
  110.9 0.9 collective-permute-start.25
  111.7 0.5 fusion.87
  112.7 1.3 collective-permute-start.5
  114.5 1.3 collective-permute-start.8
  116.3 1.3 collective-permute-start.26
  118.1 1.3 collective-permute-start.14
  119.5 0.5 fusion.97
  120.0 1.3 collective-permute-start.11
  121.3 0.5 fusion.102
  121.8 71.0 %collective-permute-done.14 = bf16[256,768]{1,0:T(8,128)(2,1)S(1)} collective-permute-done((bf16[256,768]{1,0:T(8,128)(2,1)S(1)}, bf16[256,768]{1,0:T(8,128)(2,1)S(1)}, u32[]{:S(2)}, u32[]{:S(2)}) %collective-permute-start.14) | collective-permute-done | bytes 393248 | tf_op jit(solution)/shard_map/ppermute | solution.py:66
  192.8 1.3 collective-permute-start.23
  194.3 6.9 %collective-permute-done.11 = bf16[256,768]{1,0:T(8,128)(2,1)S(1)} collective-permute-done((bf16[256,768]{1,0:T(8,128)(2,1)S(1)}, bf16[256,768]{1,0:T(8,128)(2,1)S(1)}, u32[]{:S(2)}, u32[]{:S(2)}) %collective-permute-start.11) | collective-permute-done | bytes 393248 | tf_op jit(solution)/shard_map/ppermute | solution.py:66
  201.2 1.3 collective-permute-start.17
  202.7 3.3 %fusion.26 = f32[256,2560]{1,0:T(8,128)S(1)} fusion(bf16[6144,2560]{1,0:T(8,128)(2,1)} %param.18, bf16[256,768]{1,0:T(8,128)(2,1)S(1)} %collective-permute-done.11, bf16[256,768]{1,0:T(8,128)(2,1)S(1)} %fusion.82, pred[]{:T(512)S(6)} %or.2), kind=kOutput, calls=%fused_computation.30 | convolution fusion | flops 1006829568 | bytes 7340033 | tf_op jit(solution)/shard_map/dot_general | solution.py:30
  206.0 3.3 %fusion.22 = f32[256,2560]{1,0:T(8,128)S(1)} fusion(bf16[6144,2560]{1,0:T(8,128)(2,1)} %param.18, bf16[256,768]{1,0:T(8,128)(2,1)S(1)} %collective-permute-done.14, bf16[256,768]{1,0:T(8,128)(2,1)S(1)} %fusion.87, pred[]{:T(512)S(6)} %or.2), kind=kOutput, calls=%fused_computation.26 | convolution fusion | flops 1006829568 | bytes 7340033 | tf_op jit(solution)/shard_map/dot_general | solution.py:30
  209.3 6.3 %collective-permute-done.17 = bf16[256,768]{1,0:T(8,128)(2,1)S(1)} collective-permute-done((bf16[256,768]{1,0:T(8,128)(2,1)S(1)}, bf16[256,768]{1,0:T(8,128)(2,1)S(1)}, u32[]{:S(2)}, u32[]{:S(2)}) %collective-permute-start.17) | collective-permute-done | bytes 393248 | tf_op jit(solution)/shard_map/ppermute | solution.py:66
  215.7 1.5 collective-permute-start.20
  217.5 3.3 %fusion.18 = f32[256,2560]{1,0:T(8,128)S(1)} fusion(bf16[6144,2560]{1,0:T(8,128)(2,1)} %param.18, bf16[256,768]{1,0:T(8,128)(2,1)S(1)} %collective-permute-done.17, bf16[256,768]{1,0:T(8,128)(2,1)S(1)} %fusion.92, pred[]{:T(512)S(6)} %or.2), kind=kOutput, calls=%fused_computation.22 | convolution fusion | flops 1006829568 | bytes 7340033 | tf_op jit(solution)/shard_map/dot_general | solution.py:30
  220.8 5.6 %collective-permute-done.20 = bf16[256,768]{1,0:T(8,128)(2,1)S(1)} collective-permute-done((bf16[256,768]{1,0:T(8,128)(2,1)S(1)}, bf16[256,768]{1,0:T(8,128)(2,1)S(1)}, u32[]{:S(2)}, u32[]{:S(2)}) %collective-permute-start.20) | collective-permute-done | bytes 393248 | tf_op jit(solution)/shard_map/ppermute | solution.py:66
  226.6 3.3 %fusion.14 = f32[256,2560]{1,0:T(8,128)S(1)} fusion(bf16[6144,2560]{1,0:T(8,128)(2,1)} %param.18, bf16[256,768]{1,0:T(8,128)(2,1)S(1)} %collective-permute-done.20, bf16[256,768]{1,0:T(8,128)(2,1)S(1)} %fusion.97, pred[]{:T(512)S(6)} %or.2), kind=kOutput, calls=%fused_computation.18 | convolution fusion | flops 1006829568 | bytes 7340033 | tf_op jit(solution)/shard_map/dot_general | solution.py:30
  230.2 3.3 %fusion.10 = f32[256,2560]{1,0:T(8,128)S(1)} fusion(bf16[6144,2560]{1,0:T(8,128)(2,1)} %param.18, bf16[256,768]{1,0:T(8,128)(2,1)S(1)} %collective-permute-done.23, bf16[256,768]{1,0:T(8,128)(2,1)S(1)} %fusion.102, pred[]{:T(512)S(6)} %or.2), kind=kOutput, calls=%fused_computation.14 | convolution fusion | flops 1006829568 | bytes 7340033 | tf_op jit(solution)/shard_map/dot_general | solution.py:30
  233.7 3.3 %fusion.6 = f32[256,2560]{1,0:T(8,128)S(1)} fusion(bf16[6144,2560]{1,0:T(8,128)(2,1)} %param.18, bf16[256,768]{1,0:T(8,128)(2,1)S(1)} %collective-permute-done.26, bf16[256,768]{1,0:T(8,128)(2,1)S(1)} %fusion.107, pred[]{:T(512)S(6)} %or.2), kind=kOutput, calls=%fused_computation.10 | convolution fusion | flops 1006829568 | bytes 7340033 | tf_op jit(solution)/shard_map/dot_general | solution.py:30
  237.3 3.3 %fusion.30 = f32[256,2560]{1,0:T(8,128)S(1)} fusion(bf16[6144,2560]{1,0:T(8,128)(2,1)} %param.18, bf16[256,768]{1,0:T(8,128)(2,1)S(1)} %collective-permute-done.8, bf16[256,768]{1,0:T(8,128)(2,1)S(1)} %fusion.77, pred[]{:T(512)S(6)} %or.2), kind=kOutput, calls=%fused_computation.34 | convolution fusion | flops 1006829568 | bytes 7340033 | tf_op jit(solution)/shard_map/dot_general | solution.py:30
  240.9 3.9 %fusion.5 = f32[256,2560]{1,0:T(8,128)S(1)} fusion(f32[256,2560]{1,0:T(8,128)S(1)} %fusion.6, f32[256,2560]{1,0:T(8,128)S(1)} %fusion.10, f32[256,2560]{1,0:T(8,128)S(1)} %fusion.14, f32[256,2560]{1,0:T(8,128)S(1)} %fusion.18, f32[256,2560]{1,0:T(8,128)S(1)} %fusion.22, f32[256,2560]{1,0:T(8,128)S(1)} %fusion.26, f32[256,2560]{1,0:T(8,128)S(1)} %fusion.30, ...), kind=kOutput, calls=%fused_computation.9 | convolution fusion | flops 1011417088 | bytes 25690112 | tf_op jit(solution)/shard_map/dot_general | solution.py:30
  245.2 2.0 collective-permute-done.27
  247.4 1.5 collective-permute-start.28
  249.0 8.6 %collective-permute-done.28 = bf16[64,2688]{1,0:T(8,128)(2,1)S(1)} collective-permute-done((bf16[64,2688]{1,0:T(8,128)(2,1)S(1)}, bf16[64,2688]{1,0:T(8,128)(2,1)S(1)}, u32[]{:S(2)}, u32[]{:S(2)}) %collective-permute-start.28) | collective-permute-done | bytes 344096 | tf_op jit(solution)/shard_map/ppermute | solution.py:42
  257.7 1.0 fusion.112
  (66 shorter events, 6.8 us)
Async XLA Ops:
  0.0 257.7 %copy-start = (bf16[128,2560]{1,0:T(8,128)(2,1)S(1)}, bf16[128,2560]{1,0:T(8,128)(2,1)}, u32[]{:S(2)}) copy-start(bf16[128,2560]{1,0:T(8,128)(2,1)} %param.21) | copy-start | bytes 1966084
  0.0 11.5 %collective-permute-start = (bf16[64,2560]{1,0:T(8,128)(2,1)}, bf16[64,2560]{1,0:T(8,128)(2,1)S(1)}, u32[]{:S(2)}, u32[]{:S(2)}) collective-permute-start(bf16[64,2560]{1,0:T(8,128)(2,1)} %param.11), channel_id=1, source_target_pairs={{0,1},{1,0},{2,3},{3,2},{4,5},{5,4},{6,7},{7,6},{8,9},{9,8},{10,11... | collective-permute-start | bytes 983048 | tf_op jit(solution)/shard_map/ppermute | solution.py:42
  0.5 11.1 %collective-permute-start.1 = (bf16[64,2560]{1,0:T(8,128)(2,1)}, bf16[64,2560]{1,0:T(8,128)(2,1)S(1)}, u32[]{:S(2)}, u32[]{:S(2)}) collective-permute-start(bf16[64,2560]{1,0:T(8,128)(2,1)} %param.11), channel_id=1, source_target_pairs={{0,2},{1,3},{2,0},{3,1},{4,6},{5,7},{6,4},{7,5},{8,10},{9,11},{10,... | collective-permute-start | bytes 983048 | tf_op jit(solution)/shard_map/ppermute | solution.py:42
  11.5 1.6 collective-permute-start.2
  13.2 15.6 %copy-start.4 = (bf16[2560,6144]{1,0:T(8,128)(2,1)S(1)}, bf16[2560,6144]{1,0:T(8,128)(2,1)}, u32[]{:S(2)}) copy-start(bf16[2560,6144]{1,0:T(8,128)(2,1)} %param.14) | copy-start | bytes 94371840
  32.4 6.3 %copy-start.1 = (bf16[2560,128]{1,0:T(8,128)(2,1)S(1)}, bf16[2560,128]{1,0:T(8,128)(2,1)}, u32[]{:S(2)}) copy-start(bf16[2560,128]{1,0:T(8,128)(2,1)} %param.16) | copy-start | bytes 1966084
  33.6 13.2 %collective-permute-start.6 = (bf16[256,768]{1,0:T(8,128)(2,1)S(1)}, bf16[256,768]{1,0:T(8,128)(2,1)S(1)}, u32[]{:S(2)}, u32[]{:S(2)}) collective-permute-start(bf16[256,768]{1,0:T(8,128)(2,1)S(1)} %fusion.41), channel_id=1, source_target_pairs={{0,4},{12,8},{1,5},{13,9},{2,6},{14,10},{3,7},{15,11},{16,20},{28,... | collective-permute-start | bytes 1179656 | tf_op jit(solution)/shard_map/ppermute | solution.py:54
  37.4 17.9 %collective-permute-start.9 = (bf16[256,768]{1,0:T(8,128)(2,1)S(1)}, bf16[256,768]{1,0:T(8,128)(2,1)S(1)}, u32[]{:S(2)}, u32[]{:S(2)}) collective-permute-start(bf16[256,768]{1,0:T(8,128)(2,1)S(1)} %fusion.44), channel_id=1, source_target_pairs={{0,4},{12,8},{1,5},{13,9},{2,6},{14,10},{3,7},{15,11},{16,20},{28,... | collective-permute-start | bytes 1179656 | tf_op jit(solution)/shard_map/ppermute | solution.py:54
  39.2 24.5 %collective-permute-start.12 = (bf16[256,768]{1,0:T(8,128)(2,1)S(1)}, bf16[256,768]{1,0:T(8,128)(2,1)S(1)}, u32[]{:S(2)}, u32[]{:S(2)}) collective-permute-start(bf16[256,768]{1,0:T(8,128)(2,1)S(1)} %fusion.47), channel_id=1, source_target_pairs={{0,4},{12,8},{1,5},{13,9},{2,6},{14,10},{3,7},{15,11},{16,20},{28,... | collective-permute-start | bytes 1179656 | tf_op jit(solution)/shard_map/ppermute | solution.py:54
  40.5 31.6 %collective-permute-start.15 = (bf16[256,768]{1,0:T(8,128)(2,1)S(1)}, bf16[256,768]{1,0:T(8,128)(2,1)S(1)}, u32[]{:S(2)}, u32[]{:S(2)}) collective-permute-start(bf16[256,768]{1,0:T(8,128)(2,1)S(1)} %fusion.50), channel_id=1, source_target_pairs={{0,4},{12,8},{1,5},{13,9},{2,6},{14,10},{3,7},{15,11},{16,20},{28,... | collective-permute-start | bytes 1179656 | tf_op jit(solution)/shard_map/ppermute | solution.py:54
  41.8 38.7 %collective-permute-start.18 = (bf16[256,768]{1,0:T(8,128)(2,1)S(1)}, bf16[256,768]{1,0:T(8,128)(2,1)S(1)}, u32[]{:S(2)}, u32[]{:S(2)}) collective-permute-start(bf16[256,768]{1,0:T(8,128)(2,1)S(1)} %fusion.53), channel_id=1, source_target_pairs={{0,4},{12,8},{1,5},{13,9},{2,6},{14,10},{3,7},{15,11},{16,20},{28,... | collective-permute-start | bytes 1179656 | tf_op jit(solution)/shard_map/ppermute | solution.py:54
  46.8 60.4 %collective-permute-start.21 = (bf16[256,768]{1,0:T(8,128)(2,1)S(1)}, bf16[256,768]{1,0:T(8,128)(2,1)S(1)}, u32[]{:S(2)}, u32[]{:S(2)}) collective-permute-start(bf16[256,768]{1,0:T(8,128)(2,1)S(1)} %fusion.56), channel_id=1, source_target_pairs={{0,4},{12,8},{1,5},{13,9},{2,6},{14,10},{3,7},{15,11},{16,20},{28,... | collective-permute-start | bytes 1179656 | tf_op jit(solution)/shard_map/ppermute | solution.py:54
  55.2 52.8 %collective-permute-start.24 = (bf16[256,768]{1,0:T(8,128)(2,1)S(1)}, bf16[256,768]{1,0:T(8,128)(2,1)S(1)}, u32[]{:S(2)}, u32[]{:S(2)}) collective-permute-start(bf16[256,768]{1,0:T(8,128)(2,1)S(1)} %fusion.59), channel_id=1, source_target_pairs={{0,4},{12,8},{1,5},{13,9},{2,6},{14,10},{3,7},{15,11},{16,20},{28,... | collective-permute-start | bytes 1179656 | tf_op jit(solution)/shard_map/ppermute | solution.py:54
  63.7 42.7 %collective-permute-start.3 = (bf16[256,896]{1,0:T(8,128)(2,1)S(1)}, bf16[256,896]{1,0:T(8,128)(2,1)S(1)}, u32[]{:S(2)}, u32[]{:S(2)}) collective-permute-start(bf16[256,896]{1,0:T(8,128)(2,1)S(1)} %pad_maximum_fusion.2), channel_id=1, source_target_pairs={{0,4},{12,8},{1,5},{13,9},{2,6},{14,10},{3,7},{15,11},{16,20},{28,... | collective-permute-start | bytes 1376264 | tf_op jit(solution)/shard_map/ppermute | solution.py:54
  72.1 40.6 %collective-permute-start.7 = (bf16[256,768]{1,0:T(8,128)(2,1)S(1)}, bf16[256,768]{1,0:T(8,128)(2,1)S(1)}, u32[]{:S(2)}, u32[]{:S(2)}) collective-permute-start(bf16[256,768]{1,0:T(8,128)(2,1)S(1)} %add_convert_fusion.7), channel_id=1, source_target_pairs={{4,8},{8,4},{5,9},{9,5},{6,10},{10,6},{7,11},{11,7},{20,24},{24,20... | collective-permute-start | bytes 1179656 | tf_op jit(solution)/shard_map/ppermute | solution.py:60
  80.5 29.1 %collective-permute-start.10 = (bf16[256,768]{1,0:T(8,128)(2,1)S(1)}, bf16[256,768]{1,0:T(8,128)(2,1)S(1)}, u32[]{:S(2)}, u32[]{:S(2)}) collective-permute-start(bf16[256,768]{1,0:T(8,128)(2,1)S(1)} %add_convert_fusion.6), channel_id=1, source_target_pairs={{4,8},{8,4},{5,9},{9,5},{6,10},{10,6},{7,11},{11,7},{20,24},{24,20... | collective-permute-start | bytes 1179656 | tf_op jit(solution)/shard_map/ppermute | solution.py:60
  81.3 29.0 %copy-start.5 = (bf16[128,6144]{1,0:T(8,128)(2,1)S(1)}, bf16[128,6144]{1,0:T(8,128)(2,1)}, u32[]{:S(2)}) copy-start(bf16[128,6144]{1,0:T(8,128)(2,1)} %param.17) | copy-start | bytes 4718596
  106.4 4.5 %collective-permute-start.13 = (bf16[256,768]{1,0:T(8,128)(2,1)S(1)}, bf16[256,768]{1,0:T(8,128)(2,1)S(1)}, u32[]{:S(2)}, u32[]{:S(2)}) collective-permute-start(bf16[256,768]{1,0:T(8,128)(2,1)S(1)} %add_convert_fusion.5), channel_id=1, source_target_pairs={{4,8},{8,4},{5,9},{9,5},{6,10},{10,6},{7,11},{11,7},{20,24},{24,20... | collective-permute-start | bytes 1179656 | tf_op jit(solution)/shard_map/ppermute | solution.py:60
  107.2 1.6 collective-permute-start.4
  108.0 8.3 %collective-permute-start.16 = (bf16[256,768]{1,0:T(8,128)(2,1)S(1)}, bf16[256,768]{1,0:T(8,128)(2,1)S(1)}, u32[]{:S(2)}, u32[]{:S(2)}) collective-permute-start(bf16[256,768]{1,0:T(8,128)(2,1)S(1)} %add_convert_fusion.4), channel_id=1, source_target_pairs={{4,8},{8,4},{5,9},{9,5},{6,10},{10,6},{7,11},{11,7},{20,24},{24,20... | collective-permute-start | bytes 1179656 | tf_op jit(solution)/shard_map/ppermute | solution.py:60
  108.8 9.3 %collective-permute-start.19 = (bf16[256,768]{1,0:T(8,128)(2,1)S(1)}, bf16[256,768]{1,0:T(8,128)(2,1)S(1)}, u32[]{:S(2)}, u32[]{:S(2)}) collective-permute-start(bf16[256,768]{1,0:T(8,128)(2,1)S(1)} %add_convert_fusion.3), channel_id=1, source_target_pairs={{4,8},{8,4},{5,9},{9,5},{6,10},{10,6},{7,11},{11,7},{20,24},{24,20... | collective-permute-start | bytes 1179656 | tf_op jit(solution)/shard_map/ppermute | solution.py:60
  109.6 10.3 %collective-permute-start.22 = (bf16[256,768]{1,0:T(8,128)(2,1)S(1)}, bf16[256,768]{1,0:T(8,128)(2,1)S(1)}, u32[]{:S(2)}, u32[]{:S(2)}) collective-permute-start(bf16[256,768]{1,0:T(8,128)(2,1)S(1)} %add_convert_fusion.2), channel_id=1, source_target_pairs={{4,8},{8,4},{5,9},{9,5},{6,10},{10,6},{7,11},{11,7},{20,24},{24,20... | collective-permute-start | bytes 1179656 | tf_op jit(solution)/shard_map/ppermute | solution.py:60
  110.9 3.6 %collective-permute-start.25 = (bf16[256,768]{1,0:T(8,128)(2,1)S(1)}, bf16[256,768]{1,0:T(8,128)(2,1)S(1)}, u32[]{:S(2)}, u32[]{:S(2)}) collective-permute-start(bf16[256,768]{1,0:T(8,128)(2,1)S(1)} %add_convert_fusion.1), channel_id=1, source_target_pairs={{4,8},{8,4},{5,9},{9,5},{6,10},{10,6},{7,11},{11,7},{20,24},{24,20... | collective-permute-start | bytes 1179656 | tf_op jit(solution)/shard_map/ppermute | solution.py:60
  112.7 127.9 %collective-permute-start.5 = (bf16[256,768]{1,0:T(8,128)(2,1)S(1)}, bf16[256,768]{1,0:T(8,128)(2,1)S(1)}, u32[]{:S(2)}, u32[]{:S(2)}) collective-permute-start(bf16[256,768]{1,0:T(8,128)(2,1)S(1)} %fusion.72), channel_id=1, source_target_pairs={{4,0},{8,12},{5,1},{9,13},{6,2},{10,14},{7,3},{11,15},{20,16},{24,... | collective-permute-start | bytes 1179656 | tf_op jit(solution)/shard_map/ppermute | solution.py:66
  114.5 122.5 %collective-permute-start.8 = (bf16[256,768]{1,0:T(8,128)(2,1)S(1)}, bf16[256,768]{1,0:T(8,128)(2,1)S(1)}, u32[]{:S(2)}, u32[]{:S(2)}) collective-permute-start(bf16[256,768]{1,0:T(8,128)(2,1)S(1)} %fusion.77), channel_id=1, source_target_pairs={{4,0},{8,12},{5,1},{9,13},{6,2},{10,14},{7,3},{11,15},{20,16},{24,... | collective-permute-start | bytes 1179656 | tf_op jit(solution)/shard_map/ppermute | solution.py:66
  116.3 117.1 %collective-permute-start.26 = (bf16[256,768]{1,0:T(8,128)(2,1)S(1)}, bf16[256,768]{1,0:T(8,128)(2,1)S(1)}, u32[]{:S(2)}, u32[]{:S(2)}) collective-permute-start(bf16[256,768]{1,0:T(8,128)(2,1)S(1)} %fusion.107), channel_id=1, source_target_pairs={{4,0},{8,12},{5,1},{9,13},{6,2},{10,14},{7,3},{11,15},{20,16},{24,... | collective-permute-start | bytes 1179656 | tf_op jit(solution)/shard_map/ppermute | solution.py:66
  118.1 74.6 %collective-permute-start.14 = (bf16[256,768]{1,0:T(8,128)(2,1)S(1)}, bf16[256,768]{1,0:T(8,128)(2,1)S(1)}, u32[]{:S(2)}, u32[]{:S(2)}) collective-permute-start(bf16[256,768]{1,0:T(8,128)(2,1)S(1)} %fusion.87), channel_id=1, source_target_pairs={{4,0},{8,12},{5,1},{9,13},{6,2},{10,14},{7,3},{11,15},{20,16},{24,... | collective-permute-start | bytes 1179656 | tf_op jit(solution)/shard_map/ppermute | solution.py:66
  119.4 74.6 %copy-start.2 = (bf16[6144,128]{1,0:T(8,128)(2,1)S(1)}, bf16[6144,128]{1,0:T(8,128)(2,1)}, u32[]{:S(2)}) copy-start(bf16[6144,128]{1,0:T(8,128)(2,1)} %param.20) | copy-start | bytes 4718596
  120.0 81.2 %collective-permute-start.11 = (bf16[256,768]{1,0:T(8,128)(2,1)S(1)}, bf16[256,768]{1,0:T(8,128)(2,1)S(1)}, u32[]{:S(2)}, u32[]{:S(2)}) collective-permute-start(bf16[256,768]{1,0:T(8,128)(2,1)S(1)} %fusion.82), channel_id=1, source_target_pairs={{4,0},{8,12},{5,1},{9,13},{6,2},{10,14},{7,3},{11,15},{20,16},{24,... | collective-permute-start | bytes 1179656 | tf_op jit(solution)/shard_map/ppermute | solution.py:66
  192.8 37.1 %collective-permute-start.23 = (bf16[256,768]{1,0:T(8,128)(2,1)S(1)}, bf16[256,768]{1,0:T(8,128)(2,1)S(1)}, u32[]{:S(2)}, u32[]{:S(2)}) collective-permute-start(bf16[256,768]{1,0:T(8,128)(2,1)S(1)} %fusion.102), channel_id=1, source_target_pairs={{4,0},{8,12},{5,1},{9,13},{6,2},{10,14},{7,3},{11,15},{20,16},{24,... | collective-permute-start | bytes 1179656 | tf_op jit(solution)/shard_map/ppermute | solution.py:66
  201.2 14.5 %collective-permute-start.17 = (bf16[256,768]{1,0:T(8,128)(2,1)S(1)}, bf16[256,768]{1,0:T(8,128)(2,1)S(1)}, u32[]{:S(2)}, u32[]{:S(2)}) collective-permute-start(bf16[256,768]{1,0:T(8,128)(2,1)S(1)} %fusion.92), channel_id=1, source_target_pairs={{4,0},{8,12},{5,1},{9,13},{6,2},{10,14},{7,3},{11,15},{20,16},{24,... | collective-permute-start | bytes 1179656 | tf_op jit(solution)/shard_map/ppermute | solution.py:66
  215.7 10.6 %collective-permute-start.20 = (bf16[256,768]{1,0:T(8,128)(2,1)S(1)}, bf16[256,768]{1,0:T(8,128)(2,1)S(1)}, u32[]{:S(2)}, u32[]{:S(2)}) collective-permute-start(bf16[256,768]{1,0:T(8,128)(2,1)S(1)} %fusion.97), channel_id=1, source_target_pairs={{4,0},{8,12},{5,1},{9,13},{6,2},{10,14},{7,3},{11,15},{20,16},{24,... | collective-permute-start | bytes 1179656 | tf_op jit(solution)/shard_map/ppermute | solution.py:66
  245.0 2.2 collective-permute-start.27
  247.3 10.4 %copy-start.3 = (f32[2560]{0:T(1024)S(1)}, f32[2560]{0:T(1024)}, u32[]{:S(2)}) copy-start(f32[2560]{0:T(1024)} %param.19) | copy-start | bytes 30724
  247.4 10.2 %collective-permute-start.28 = (bf16[64,2688]{1,0:T(8,128)(2,1)S(1)}, bf16[64,2688]{1,0:T(8,128)(2,1)S(1)}, u32[]{:S(2)}, u32[]{:S(2)}) collective-permute-start(bf16[64,2688]{1,0:T(8,128)(2,1)S(1)} %slice.344), channel_id=1, source_target_pairs={{0,2},{1,3},{2,0},{3,1},{4,6},{5,7},{6,4},{7,5},{8,10},{9,11},{10,... | collective-permute-start | bytes 1032200 | tf_op jit(solution)/shard_map/ppermute | solution.py:42

commit v2 on v1

v2 whole, which is shorter than its diff:
```python
import functools

import jax
import jax.numpy as jnp
from jax import lax
from jax.experimental import pallas as pl
from jax.experimental.pallas import tpu as pltpu
from jax.sharding import PartitionSpec as P

ADAPTER_RANK = 16
ADAPTER_COUNT = 8
JOBS = 4
LANES = 128
AHEAD = 2
F32 = jnp.float32
BF16 = jnp.bfloat16
ANY = pl.BlockSpec(memory_space=pl.ANY)
COST = pl.CostEstimate(flops=1000, bytes_accessed=1000, transcendentals=0)
PARAMS = pltpu.CompilerParams(vmem_limit_bytes=30 << 20)


def gelu_tanh(values):
    return (
        0.5
        * values
        * (1.0 + jnp.tanh(0.7978845608 * (values + 0.044715 * values * values * values)))
    )


def token_mask(token_job_index, job_adapter_index):
    one_hot = token_job_index[:, None] == jnp.arange(JOBS, dtype=jnp.int32)[None, :]
    chosen = jnp.sum(jnp.where(one_hot, job_adapter_index[None, :], 0), axis=1)
    slot_ids = jnp.arange(ADAPTER_COUNT * ADAPTER_RANK, dtype=jnp.int32) // ADAPTER_RANK
    return slot_ids[None, :] == chosen[:, None]


def dot(left, right):
    return jnp.dot(left, right, preferred_element_type=F32)


def tile_of(width, most):
    tile = LANES
    for count in range(2, most // LANES + 1):
        if width % (count * LANES) == 0:
            tile = count * LANES
    return tile


def whole(shape):
    return pl.BlockSpec(shape, lambda *_: (0,) * len(shape))


def chunk_spans(hidden):
    units = hidden // LANES
    count = max(n for n in range(1, 9) if units % n == 0)
    width = hidden // count
    return [(start, width) for start in range(0, hidden, width)]


def first_kernel(x_ref, w_ref, after_ref, out_ref):
    out_ref[...] = dot(x_ref[...], w_ref[...]).astype(BF16)


def first_product(x, weight, span, after):
    start, width = span
    tile = tile_of(width, 256)
    while start % tile:
        tile -= LANES
    base = start // tile
    return pl.pallas_call(
        first_kernel,
        grid=(width // tile,),
        in_specs=[
            whole(x.shape),
            pl.BlockSpec((x.shape[1], tile), lambda j: (0, base + j)),
            ANY,
        ],
        out_specs=pl.BlockSpec((x.shape[0], tile), lambda j: (0, j)),
        out_shape=jax.ShapeDtypeStruct((x.shape[0], width), BF16),
        compiler_params=PARAMS,
        cost_estimate=COST,
    )(x, weight, after)


def low_kernel(x_ref, w_ref, d_ref, after_ref, out_ref, *, tiles, width):
    j = pl.program_id(0)

    @pl.when(j < tiles)
    def _():
        out_ref[...] = dot(x_ref[...], w_ref[...]).astype(BF16)

    @pl.when(j == tiles)
    def _():
        out_ref[...] = dot(x_ref[...], d_ref[...]).astype(BF16)


def first_product_low(x, weight, down, span, after):
    start, width = span
    tile = LANES
    tiles = width // tile
    low = down.shape[1]
    return pl.pallas_call(
        functools.partial(low_kernel, tiles=tiles, width=width),
        grid=(tiles + 1,),
        in_specs=[
            whole(x.shape),
            pl.BlockSpec((x.shape[1], tile), lambda j: (0, start // tile + jnp.minimum(j, tiles - 1))),
            whole(down.shape),
            ANY,
        ],
        out_specs=pl.BlockSpec((x.shape[0], tile), lambda j: (0, j)),
        out_shape=jax.ShapeDtypeStruct((x.shape[0], width + low), BF16),
        compiler_params=PARAMS,
        cost_estimate=COST,
    )(x, weight, down, after)


def add_kernel(a_ref, b_ref, after_ref, out_ref):
    out_ref[...] = (a_ref[...].astype(F32) + b_ref[...].astype(F32)).astype(BF16)


def add_rounded(a, b, after):
    return pl.pallas_call(
        add_kernel,
        grid=(1,),
        in_specs=[whole(a.shape), whole(b.shape), ANY],
        out_specs=whole(a.shape),
        out_shape=jax.ShapeDtypeStruct(a.shape, BF16),
        compiler_params=PARAMS,
        cost_estimate=COST,
    )(a, b, after)


def gelu_kernel(m_ref, low_ref, up_ref, bias_ref, after_ref, out_ref):
    summed = m_ref[0].astype(F32) + m_ref[1].astype(F32)
    before = summed + bias_ref[...] + dot(low_ref[...], up_ref[...])
    out_ref[...] = gelu_tanh(before).astype(BF16)


def gelu_chunk(pair, low_in, up_maps, bias, span, after):
    start, width = span
    rows = pair.shape[1]
    tile = tile_of(width, 256)
    while start % tile:
        tile -= LANES
    base = start // tile
    return pl.pallas_call(
        gelu_kernel,
        grid=(width // tile,),
        in_specs=[
            pl.BlockSpec((2, rows, tile), lambda j: (0, 0, j)),
            whole(low_in.shape),
            pl.BlockSpec((up_maps.shape[0], tile), lambda j: (0, base + j)),
            pl.BlockSpec((1, tile), lambda j: (0, base + j)),
            ANY,
        ],
        out_specs=pl.BlockSpec((rows, tile), lambda j: (0, j)),
        out_shape=jax.ShapeDtypeStruct((rows, width), BF16),
        compiler_params=PARAMS,
        cost_estimate=COST,
    )(pair, low_in, up_maps, bias, after)


def second_kernel(end_ref, h_ref, r_ref, w_ref, d_ref, acc_ref, low_ref, after_ref, out_ref, low_out_ref, state, *, first):
    j = pl.program_id(0)

    @pl.when(j == 0)
    def _():
        @pl.when(end_ref[0] == 1)
        def _():
            state[...] = r_ref[...]

        @pl.when(end_ref[0] == 0)
        def _():
            state[...] = h_ref[...]

        low = dot(state[...], d_ref[...])
        low_out_ref[...] = low if first else low + low_ref[...]

    part = dot(state[...], w_ref[...])
    out_ref[...] = part if first else part + acc_ref[...]


def second_product(is_end, h, r, weight, down, total, low_total, span, after):
    start, width = span
    rows = h.shape[0]
    out_width = weight.shape[1]
    tile = tile_of(out_width, 512)
    first = total is None
    base = start // width
    if first:
        total, low_total = after, after
        total_spec, low_spec = ANY, ANY
    else:
        total_spec = pl.BlockSpec((rows, tile), lambda j: (0, j))
        low_spec = whole((rows, down.shape[1]))
    return pl.pallas_call(
        functools.partial(second_kernel, first=first),
        grid=(out_width // tile,),
        in_specs=[
            pl.BlockSpec(memory_space=pltpu.SMEM),
            whole(h.shape),
            whole(r.shape),
            pl.BlockSpec((width, tile), lambda j: (base, j)),
            pl.BlockSpec((width, down.shape[1]), lambda j: (base, 0)),
            total_spec,
            low_spec,
            ANY,
        ],
        out_specs=[
            pl.BlockSpec((rows, tile), lambda j: (0, j)),
            whole((rows, down.shape[1])),
        ],
        out_shape=[
            jax.ShapeDtypeStruct((rows, out_width), F32),
            jax.ShapeDtypeStruct((rows, down.shape[1]), F32),
        ],
        scratch_shapes=[pltpu.VMEM(h.shape, BF16)],
        compiler_params=PARAMS,
        cost_estimate=COST,
    )(is_end, h, r, weight, down, total, low_total, after)


def make_local(n_group, n_row, n_col):
    chips = n_col // 2
    half = n_row // 2

    def place_of(group, row, col):
        return (group * n_row + row) * n_col + col

    cross_groups = []
    for group in range(n_group):
        for col in range(n_col):
            cross_groups.append([place_of(group, half - 1, col), place_of(group, half, col)])
        for row in range(n_row):
            if row not in (half - 1, half):
                for col in range(0, n_col, 2):
                    cross_groups.append([place_of(group, row, col), place_of(group, row, col + 1)])

    def col_swap(value, flip):
        return lax.ppermute(value, "col", [(i, i ^ flip) for i in range(n_col)])

    def gather_tokens(tokens):
        shards = [tokens, col_swap(tokens, 1)]
        for step in range(1, chips):
            far = col_swap(tokens, 2 * step)
            shards += [far, col_swap(far, 1)]
        return jnp.concatenate(shards, axis=0)

    def fold(value, step):
        pairs = [(step, step + 1), (n_row - 1 - step, n_row - 2 - step)]
        return lax.ppermute(value, "row", pairs)

    def cross(value):
        return lax.all_gather(
            value, ("group", "row", "col"), axis=0, tiled=False, axis_index_groups=cross_groups
        )

    def spread(value, place):
        for step in reversed(range(half - 1)):
            pairs = [(step + 1, step), (n_row - 2 - step, n_row - 1 - step)]
            come = lax.ppermute(value, "row", pairs)
            if step > 0:
                value = jnp.where((place <= step) | (place >= n_row - 1 - step), come, value)
            else:
                value = come
        return value

    def local(
        tokens,
        token_job_index,
        job_adapter_index,
        first_weight,
        first_bias,
        first_down_maps,
        first_up_maps,
        second_weight,
        second_bias,
        second_down_maps,
        second_up_maps,
    ):
        rows = tokens.shape[0]
        hidden = first_weight.shape[1]
        out_width = second_weight.shape[1]
        spans = chunk_spans(hidden)
        count = len(spans)
        place = lax.axis_index("row")
        mine = lax.axis_index("col")
        edge = (place == 0) | (place == n_row - 1)
        is_end = edge.astype(jnp.int32).reshape(1)
        bias = first_bias[None, :]
        mask_all = token_mask(token_job_index, job_adapter_index)
        mask = jnp.concatenate(
            [
                lax.dynamic_slice_in_dim(mask_all, (mine ^ i) * rows, rows, 0)
                for i in range(n_col)
            ],
            axis=0,
        )
        gathered = gather_tokens(tokens)
        last = gathered
        partials, folded, pairs, states, returned = {}, {}, {}, {}, {}
        total, low_total, low_in = None, None, None

        def start_chunk(t):
            nonlocal last
            if t == 0:
                last = first_product_low(gathered, first_weight, first_down_maps, spans[t], last)
            else:
                last = first_product(gathered, first_weight, spans[t], last)
            partials[t] = last
            folded[t] = fold(last, 0)

        for t in range(min(AHEAD, count)):
            start_chunk(t)
        for t in range(count + 2):
            if t < count:
                value = add_rounded(partials[t], folded[t], last)
                for step in range(1, half - 1):
                    value = add_rounded(value, fold(value, step), value)
                last = value
                pairs[t] = cross(value)
            if t + AHEAD < count:
                start_chunk(t + AHEAD)
            if 0 <= t - 1 < count:
                k = t - 1
                width = spans[k][1]
                if k == 0:
                    low = pairs[k][:, :, width:].astype(F32)
                    low_in = jnp.where(mask, low[0] + low[1], 0.0).astype(BF16)
                last = gelu_chunk(pairs[k], low_in, first_up_maps, bias, spans[k], last)
                states[k] = last
                returned[k] = spread(last, place)
            if 0 <= t - 2 < count:
                k = t - 2
                total, low_total = second_product(
                    is_end, states[k], returned[k], second_weight, second_down_maps,
                    total, low_total, spans[k], last,
                )
                last = low_total
        outputs = jnp.concatenate([total, low_total], axis=1)
        blocks = [outputs[i * rows : (i + 1) * rows] for i in range(n_col)]
        ours = jnp.concatenate(blocks[0::2], axis=0)
        theirs = jnp.concatenate(blocks[1::2], axis=0).astype(BF16)
        ours = ours + col_swap(theirs, 1).astype(F32)
        result = ours[:rows]
        for step in range(1, chips):
            piece = ours[step * rows : (step + 1) * rows].astype(BF16)
            result = result + col_swap(piece, 2 * step).astype(F32)
        low_out = jnp.where(mask[:rows], result[:, out_width:], 0.0).astype(BF16)
        layer_output = result[:, :out_width] + second_bias[None, :] + dot(low_out, second_up_maps)
        return layer_output.astype(BF16)

    return local


def solution(mesh):
    shape = mesh.shape
    return jax.shard_map(
        make_local(shape["group"], shape["row"], shape["col"]),
        mesh=mesh,
        in_specs=(
            P(("group", "col"), "row"),
            P("group"),
            P("group"),
            P("row", "col"),
            P("col"),
            P("row", None),
            P(None, "col"),
            P("col", "row"),
            P("row"),
            P("col", None),
            P(None, "row"),
        ),
        out_specs=P(("group", "col"), "row"),
        check_vma=False,
    )
```

time: 260 us -> 226 us (0.87)
  waiting for transfers between devices: 156 us -> 42.7 us
  Pallas kernels: 0 us -> 85.7 us
  matrix products: 54.7 us -> 0.97 us
  starting transfers between devices: 43 us -> 73.4 us
  blocking collectives: 0 us -> 19 us
    ppermute x24 -> x16, waiting for transfers between devices: 138 us -> 23.6 us  [the longest x8 18.7 us: spread(): come = lax.ppermute(value, 'row', pairs)]
    pallas_call x0 -> x32, Pallas kernels: none -> 85.7 us  [the longest x8 39.9 us: second_product(): pl.pallas_call(functools.partial(second_kernel, first=first), grid=(out_w...]
    dot_general x34 -> x1, matrix products: 54.7 us -> 0.97 us  [dot(): return jnp.dot(left, right, preferred_element_type=F32)]
    ppermute x24 -> x16, starting transfers between devices: 38.4 us -> 68.8 us  [the longest x8 58.5 us: fold(): return lax.ppermute(value, 'row', pairs)]
    all_gather x0 -> x8, blocking collectives: none -> 19 us  [cross(): lax.all_gather(value, ('group', 'row', 'col'), axis=0, tiled=False, axis_...]
  transfers between devices with their start and end apart: 29 -> 21, of which waited for: 14 -> 7; matrix products, arithmetic and copies ran while one was open for 13% -> 1% of each run, Pallas kernels for 0% -> 33%
where the time goes in v2:
time: 226 us; the launch traced here: 225 us
  Pallas kernels  85.7 us (38%)
  starting transfers between devices  73.4 us (32%)
  waiting for transfers between devices  42.7 us (19%)
  blocking collectives  19 us (8%)
    ppermute x8, starting transfers between devices, fold(): return lax.ppermute(value, 'row', pairs)  58.5 us
    pallas_call x8, Pallas kernels, second_product(): pl.pallas_call(functools.partial(second_kernel, first=first), grid=(out_w...  39.9 us
    pallas_call x7, Pallas kernels, first_product(): pl.pallas_call(first_kernel, grid=(width // tile,), in_specs=[whole(x.sha...  27.4 us
    ppermute x5, waiting for transfers between devices, col_swap(): return lax.ppermute(value, 'col', [(i, i ^ flip) for i in range(n_col)])  19.1 us
    all_gather x8, blocking collectives, cross(): lax.all_gather(value, ('group', 'row', 'col'), axis=0, tiled=False, axis_...  19 us
    ppermute x8, waiting for transfers between devices, spread(): come = lax.ppermute(value, 'row', pairs)  18.7 us
    ppermute x8, starting transfers between devices, spread(): come = lax.ppermute(value, 'row', pairs)  10.3 us
    pallas_call x8, Pallas kernels, gelu_chunk(): pl.pallas_call(gelu_kernel, grid=(width // tile,), in_specs=[pl.BlockSpec...  8.34 us
  transfers between devices with their start and end apart: 21, of which 7 were waited for; matrix products, arithmetic and copies ran while one was open for 1% of the time, Pallas kernels for 33%

profile of v2, /device:TPU:0, one launch (start us, length us, event | category | flops | bytes accessed | tf_op | source)
XLA Modules:
  0.0 224.6 jit_solution(7502227618455500256)
XLA Ops:
  0.0 2.9 %collective-permute-start.1 = (bf16[64,2560]{1,0:T(8,128)(2,1)}, bf16[64,2560]{1,0:T(8,128)(2,1)S(1)}, u32[]{:S(2)}, u32[]{:S(2)}) collective-permute-start(bf16[64,2560]{1,0:T(8,128)(2,1)} %param.11), channel_id=1, source_target_pairs={{0,2},{1,3},{2,0},{3,1},{4,6},{5,7},{6,4},{7,5},{8,10},{9,11},{10,... | collective-permute-start | bytes 983048 | tf_op jit(solution)/shard_map/ppermute | solution.py:241
  2.9 1.0 constant_dynamic-update-slice_fusion.3
  4.0 6.9 %collective-permute-done.1 = bf16[64,2560]{1,0:T(8,128)(2,1)S(1)} collective-permute-done((bf16[64,2560]{1,0:T(8,128)(2,1)}, bf16[64,2560]{1,0:T(8,128)(2,1)S(1)}, u32[]{:S(2)}, u32[]{:S(2)}) %collective-permute-start.1) | collective-permute-done | bytes 327712 | tf_op jit(solution)/shard_map/ppermute | solution.py:241
  10.9 1.6 collective-permute-done.2
  12.6 6.0 %shard_map.109.after_ref.a_ref = bf16[256,896]{1,0:T(8,128)(2,1)S(1)} custom-call(bf16[256,2560]{1,0:T(8,128)(2,1)S(1)} %constant_dynamic-update-slice_fusion.x_ref.after_ref, bf16[2560,6144]{1,0:T(8,128)(2,1)} %w_ref.26, bf16[2560,128]{1,0:T(8,128)(2,1)S(1)} %copy-done.9, bf16[256,2560]{1,0:T(8,128)(2,1)S(1)} %constant_dynamic-update-slice_fusion.x_ref.after_ref), custom_call_target="tpu_custom_call" | custom-call | flops 1000 | bytes 1000 | tf_op jit(solution)/shard_map/pallas_call | solution.py:102
  18.5 3.8 %collective-permute-start.4 = (bf16[256,896]{1,0:T(8,128)(2,1)S(1)}, bf16[256,896]{1,0:T(8,128)(2,1)S(1)}, u32[]{:S(2)}, u32[]{:S(2)}) collective-permute-start(bf16[256,896]{1,0:T(8,128)(2,1)S(1)} %shard_map.109.after_ref.a_ref), channel_id=1, source_target_pairs={{0,4},{12,8},{1,5},{13,9},{2,6},{14,10},{3,7},{15,11},{16,20},{28,... | collective-permute-start | bytes 1376264 | tf_op jit(solution)/shard_map/ppermute | solution.py:252
  22.4 3.7 %shard_map.110.after_ref.a_ref = bf16[256,768]{1,0:T(8,128)(2,1)S(1)} custom-call(bf16[256,2560]{1,0:T(8,128)(2,1)S(1)} %constant_dynamic-update-slice_fusion.x_ref.after_ref, bf16[2560,6144]{1,0:T(8,128)(2,1)} %w_ref.26, bf16[256,896]{1,0:T(8,128)(2,1)S(1)} %shard_map.109.after_ref.a_ref), custom_call_target="tpu_custom_call" | custom-call | flops 1000 | bytes 1000 | tf_op jit(solution)/shard_map/pallas_call | solution.py:70
  26.1 2.0 collective-permute-start.3
  28.3 4.9 %collective-permute-done.4.b_ref = bf16[256,896]{1,0:T(8,128)(2,1)S(1)} collective-permute-done((bf16[256,896]{1,0:T(8,128)(2,1)S(1)}, bf16[256,896]{1,0:T(8,128)(2,1)S(1)}, u32[]{:S(2)}, u32[]{:S(2)}) %collective-permute-start.4) | collective-permute-done | bytes 458784 | tf_op jit(solution)/shard_map/ppermute | solution.py:252
  33.3 4.4 %shard_map.112.after_ref.a_ref = bf16[256,768]{1,0:T(8,128)(2,1)} custom-call(bf16[256,2560]{1,0:T(8,128)(2,1)S(1)} %constant_dynamic-update-slice_fusion.x_ref.after_ref, bf16[2560,6144]{1,0:T(8,128)(2,1)} %w_ref.26, bf16[256,896]{1,0:T(8,128)(2,1)S(1)} %shard_map.111.after_ref), custom_call_target="tpu_custom_call" | custom-call | flops 1000 | bytes 1000 | tf_op jit(solution)/shard_map/pallas_call | solution.py:70
  37.7 5.1 %collective-permute-start.7 = (bf16[256,768]{1,0:T(8,128)(2,1)}, bf16[256,768]{1,0:T(8,128)(2,1)}, u32[]{:S(2)}, u32[]{:S(2)}) collective-permute-start(bf16[256,768]{1,0:T(8,128)(2,1)} %shard_map.112.after_ref.a_ref), channel_id=1, source_target_pairs={{0,4},{12,8},{1,5},{13,9},{2,6},{14,10},{3,7},{15,11},{16,20},{28,... | collective-permute-start | bytes 1179656 | tf_op jit(solution)/shard_map/ppermute | solution.py:252
  42.8 2.4 %all-gather = bf16[512,896]{1,0:T(8,128)(2,1)S(1)} all-gather(bf16[256,896]{1,0:T(8,128)(2,1)S(1)} %shard_map.111.after_ref), channel_id=2, replica_groups={{4,8},{5,9},{6,10},{7,11},{0,1},{2,3},{12,13},{14,15},{20,24},{21,25},{..., dimensions={0}, use_global_device_ids=true | all-gather | bytes 1376256 | tf_op jit(solution)/shard_map/all_gather | solution.py:255
  45.3 1.1 shard_map.113.after_ref
  46.4 4.5 %shard_map.114.after_ref.a_ref = bf16[256,768]{1,0:T(8,128)(2,1)} custom-call(bf16[256,2560]{1,0:T(8,128)(2,1)S(1)} %constant_dynamic-update-slice_fusion.x_ref.after_ref, bf16[2560,6144]{1,0:T(8,128)(2,1)} %w_ref.26, bf16[256,768]{1,0:T(8,128)(2,1)S(1)} %shard_map.113.after_ref), custom_call_target="tpu_custom_call" | custom-call | flops 1000 | bytes 1000 | tf_op jit(solution)/shard_map/pallas_call | solution.py:70
  51.0 2.0 shard_map.115.after_ref.h_ref
  53.0 1.3 collective-permute-start.6
  54.3 11.2 %collective-permute-start.5 = (bf16[256,768]{1,0:T(8,128)(2,1)}, bf16[256,768]{1,0:T(8,128)(2,1)}, u32[]{:S(2)}, u32[]{:S(2)}) collective-permute-start(bf16[256,768]{1,0:T(8,128)(2,1)} %shard_map.114.after_ref.a_ref), channel_id=1, source_target_pairs={{0,4},{12,8},{1,5},{13,9},{2,6},{14,10},{3,7},{15,11},{16,20},{28,... | collective-permute-start | bytes 1179656 | tf_op jit(solution)/shard_map/ppermute | solution.py:252
  65.5 1.3 shard_map.116.after_ref
  66.7 2.4 %all-gather.1 = bf16[512,768]{1,0:T(8,128)(2,1)S(1)} all-gather(bf16[256,768]{1,0:T(8,128)(2,1)S(1)} %copy-done.6), channel_id=3, replica_groups={{4,8},{5,9},{6,10},{7,11},{0,1},{2,3},{12,13},{14,15},{20,24},{21,25},{..., dimensions={0}, use_global_device_ids=true | all-gather | bytes 1179648 | tf_op jit(solution)/shard_map/all_gather | solution.py:255
  69.1 3.7 %shard_map.117.after_ref.a_ref = bf16[256,768]{1,0:T(8,128)(2,1)S(1)} custom-call(bf16[256,2560]{1,0:T(8,128)(2,1)S(1)} %constant_dynamic-update-slice_fusion.x_ref.after_ref, bf16[2560,6144]{1,0:T(8,128)(2,1)} %w_ref.26, bf16[256,768]{1,0:T(8,128)(2,1)S(1)} %shard_map.116.after_ref), custom_call_target="tpu_custom_call" | custom-call | flops 1000 | bytes 1000 | tf_op jit(solution)/shard_map/pallas_call | solution.py:70
  72.8 7.6 %collective-permute-start.11 = (bf16[256,768]{1,0:T(8,128)(2,1)S(1)}, bf16[256,768]{1,0:T(8,128)(2,1)S(1)}, u32[]{:S(2)}, u32[]{:S(2)}) collective-permute-start(bf16[256,768]{1,0:T(8,128)(2,1)S(1)} %shard_map.117.after_ref.a_ref), channel_id=1, source_target_pairs={{0,4},{12,8},{1,5},{13,9},{2,6},{14,10},{3,7},{15,11},{16,20},{28,... | collective-permute-start | bytes 1179656 | tf_op jit(solution)/shard_map/ppermute | solution.py:252
  80.5 0.9 shard_map.118.acc_ref.low_ref.after_ref.h_ref
  81.4 1.3 collective-permute-start.10
  82.7 5.2 %shard_map.119 = (f32[256,2560]{1,0:T(8,128)S(1)}, f32[256,128]{1,0:T(8,128)S(1)}) custom-call(s32[1]{0:T(128)} %bitcast.end_ref, bf16[256,768]{1,0:T(8,128)(2,1)} %shard_map.115.after_ref.h_ref, bf16[256,768]{1,0:T(8,128)(2,1)} %collective-permute-done.6.r_ref, bf16[6144,2560]{1,0:T(8,128)(2,1)} %w_ref.31, bf16[6144,128]{1,0:T(8,128)(2,1)S(1)} %copy-done.1, ...), custom_call_target="tpu_custom_call" | custom-call | flops 1000 | bytes 1000 | tf_op jit(solution)/shard_map/pallas_call | solution.py:197
  87.9 1.2 shard_map.120.after_ref
  89.1 3.7 %shard_map.121.after_ref.a_ref = bf16[256,768]{1,0:T(8,128)(2,1)S(1)} custom-call(bf16[256,2560]{1,0:T(8,128)(2,1)S(1)} %constant_dynamic-update-slice_fusion.x_ref.after_ref, bf16[2560,6144]{1,0:T(8,128)(2,1)} %w_ref.26, bf16[256,768]{1,0:T(8,128)(2,1)S(1)} %shard_map.120.after_ref), custom_call_target="tpu_custom_call" | custom-call | flops 1000 | bytes 1000 | tf_op jit(solution)/shard_map/pallas_call | solution.py:70
  92.8 2.4 %all-gather.2 = bf16[512,768]{1,0:T(8,128)(2,1)S(1)} all-gather(bf16[256,768]{1,0:T(8,128)(2,1)S(1)} %shard_map.116.after_ref), channel_id=4, replica_groups={{4,8},{5,9},{6,10},{7,11},{0,1},{2,3},{12,13},{14,15},{20,24},{21,25},{..., dimensions={0}, use_global_device_ids=true | all-gather | bytes 1179648 | tf_op jit(solution)/shard_map/all_gather | solution.py:255
  95.2 0.9 shard_map.122.after_ref.h_ref
  96.1 1.3 collective-permute-start.9
  97.4 10.7 %collective-permute-start.8 = (bf16[256,768]{1,0:T(8,128)(2,1)S(1)}, bf16[256,768]{1,0:T(8,128)(2,1)S(1)}, u32[]{:S(2)}, u32[]{:S(2)}) collective-permute-start(bf16[256,768]{1,0:T(8,128)(2,1)S(1)} %shard_map.121.after_ref.a_ref), channel_id=1, source_target_pairs={{0,4},{12,8},{1,5},{13,9},{2,6},{14,10},{3,7},{15,11},{16,20},{28,... | collective-permute-start | bytes 1179656 | tf_op jit(solution)/shard_map/ppermute | solution.py:252
  108.1 5.0 %shard_map.123 = (f32[256,2560]{1,0:T(8,128)S(1)}, f32[256,128]{1,0:T(8,128)S(1)}) custom-call(s32[1]{0:T(128)} %bitcast.end_ref, bf16[256,768]{1,0:T(8,128)(2,1)S(1)} %shard_map.118.acc_ref.low_ref.after_ref.h_ref, bf16[256,768]{1,0:T(8,128)(2,1)S(1)} %collective-permute-done.10.r_ref, bf16[6144,2560]{1,0:T(8,128)(2,1)} %w_ref.31, ...), custom_call_target="tpu_custom_call" | custom-call | flops 1000 | bytes 1000 | tf_op jit(solution)/shard_map/pallas_call | solution.py:197
  113.2 2.4 %all-gather.3 = bf16[512,768]{1,0:T(8,128)(2,1)S(1)} all-gather(bf16[256,768]{1,0:T(8,128)(2,1)S(1)} %shard_map.120.after_ref), channel_id=5, replica_groups={{4,8},{5,9},{6,10},{7,11},{0,1},{2,3},{12,13},{14,15},{20,24},{21,25},{..., dimensions={0}, use_global_device_ids=true | all-gather | bytes 1179648 | tf_op jit(solution)/shard_map/all_gather | solution.py:255
  115.6 3.7 %shard_map.125.after_ref.a_ref = bf16[256,768]{1,0:T(8,128)(2,1)S(1)} custom-call(bf16[256,2560]{1,0:T(8,128)(2,1)S(1)} %constant_dynamic-update-slice_fusion.x_ref.after_ref, bf16[2560,6144]{1,0:T(8,128)(2,1)} %w_ref.26, bf16[256,768]{1,0:T(8,128)(2,1)S(1)} %shard_map.124.after_ref), custom_call_target="tpu_custom_call" | custom-call | flops 1000 | bytes 1000 | tf_op jit(solution)/shard_map/pallas_call | solution.py:70
  119.3 7.4 %collective-permute-start.15 = (bf16[256,768]{1,0:T(8,128)(2,1)S(1)}, bf16[256,768]{1,0:T(8,128)(2,1)S(1)}, u32[]{:S(2)}, u32[]{:S(2)}) collective-permute-start(bf16[256,768]{1,0:T(8,128)(2,1)S(1)} %shard_map.125.after_ref.a_ref), channel_id=1, source_target_pairs={{0,4},{12,8},{1,5},{13,9},{2,6},{14,10},{3,7},{15,11},{16,20},{28,... | collective-permute-start | bytes 1179656 | tf_op jit(solution)/shard_map/ppermute | solution.py:252
  126.7 0.9 shard_map.126.after_ref.h_ref
  127.6 1.3 collective-permute-start.14
  128.9 5.0 %shard_map.127 = (f32[256,2560]{1,0:T(8,128)S(1)}, f32[256,128]{1,0:T(8,128)S(1)}) custom-call(s32[1]{0:T(128)} %bitcast.end_ref, bf16[256,768]{1,0:T(8,128)(2,1)S(1)} %shard_map.122.after_ref.h_ref, bf16[256,768]{1,0:T(8,128)(2,1)S(1)} %collective-permute-done.9.r_ref, bf16[6144,2560]{1,0:T(8,128)(2,1)} %w_ref.31, bf16[6144,128]{1,0:T(8,128)(2,1)S(1)} %copy-done.1, ...), custom_call_target="tpu_custom_call" | custom-call | flops 1000 | bytes 1000 | tf_op jit(solution)/shard_map/pallas_call | solution.py:197
  134.0 2.4 %all-gather.4 = bf16[512,768]{1,0:T(8,128)(2,1)S(1)} all-gather(bf16[256,768]{1,0:T(8,128)(2,1)S(1)} %shard_map.124.after_ref), channel_id=6, replica_groups={{4,8},{5,9},{6,10},{7,11},{0,1},{2,3},{12,13},{14,15},{20,24},{21,25},{..., dimensions={0}, use_global_device_ids=true | all-gather | bytes 1179648 | tf_op jit(solution)/shard_map/all_gather | solution.py:255
  136.4 3.7 %shard_map.129.after_ref.a_ref = bf16[256,768]{1,0:T(8,128)(2,1)S(1)} custom-call(bf16[256,2560]{1,0:T(8,128)(2,1)S(1)} %constant_dynamic-update-slice_fusion.x_ref.after_ref, bf16[2560,6144]{1,0:T(8,128)(2,1)} %w_ref.26, bf16[256,768]{1,0:T(8,128)(2,1)S(1)} %shard_map.128.after_ref), custom_call_target="tpu_custom_call" | custom-call | flops 1000 | bytes 1000 | tf_op jit(solution)/shard_map/pallas_call | solution.py:70
  140.1 0.9 shard_map.130.after_ref.h_ref
  141.0 1.3 collective-permute-start.13
  142.3 10.7 %collective-permute-start.12 = (bf16[256,768]{1,0:T(8,128)(2,1)S(1)}, bf16[256,768]{1,0:T(8,128)(2,1)S(1)}, u32[]{:S(2)}, u32[]{:S(2)}) collective-permute-start(bf16[256,768]{1,0:T(8,128)(2,1)S(1)} %shard_map.129.after_ref.a_ref), channel_id=1, source_target_pairs={{0,4},{12,8},{1,5},{13,9},{2,6},{14,10},{3,7},{15,11},{16,20},{28,... | collective-permute-start | bytes 1179656 | tf_op jit(solution)/shard_map/ppermute | solution.py:252
  153.0 2.4 %all-gather.5 = bf16[512,768]{1,0:T(8,128)(2,1)S(1)} all-gather(bf16[256,768]{1,0:T(8,128)(2,1)S(1)} %shard_map.128.after_ref), channel_id=7, replica_groups={{4,8},{5,9},{6,10},{7,11},{0,1},{2,3},{12,13},{14,15},{20,24},{21,25},{..., dimensions={0}, use_global_device_ids=true | all-gather | bytes 1179648 | tf_op jit(solution)/shard_map/all_gather | solution.py:255
  155.4 5.0 %shard_map.131 = (f32[256,2560]{1,0:T(8,128)S(1)}, f32[256,128]{1,0:T(8,128)S(1)}) custom-call(s32[1]{0:T(128)} %bitcast.end_ref, bf16[256,768]{1,0:T(8,128)(2,1)S(1)} %shard_map.126.after_ref.h_ref, bf16[256,768]{1,0:T(8,128)(2,1)S(1)} %collective-permute-done.14.r_ref, bf16[6144,2560]{1,0:T(8,128)(2,1)} %w_ref.31, bf16[6144,128]{1,0:T(8,128)(2,1)S(1)} %copy-done.1, ...), custom_call_target="tpu_custom_call" | custom-call | flops 1000 | bytes 1000 | tf_op jit(solution)/shard_map/pallas_call | solution.py:197
  160.4 0.9 shard_map.133.after_ref.h_ref
  161.4 1.3 collective-permute-start.16
  162.7 5.0 %shard_map.134 = (f32[256,2560]{1,0:T(8,128)S(1)}, f32[256,128]{1,0:T(8,128)S(1)}) custom-call(s32[1]{0:T(128)} %bitcast.end_ref, bf16[256,768]{1,0:T(8,128)(2,1)S(1)} %shard_map.130.after_ref.h_ref, bf16[256,768]{1,0:T(8,128)(2,1)S(1)} %collective-permute-done.13.r_ref, bf16[6144,2560]{1,0:T(8,128)(2,1)} %w_ref.31, bf16[6144,128]{1,0:T(8,128)(2,1)S(1)} %copy-done.1, ...), custom_call_target="tpu_custom_call" | custom-call | flops 1000 | bytes 1000 | tf_op jit(solution)/shard_map/pallas_call | solution.py:197
  167.8 2.4 %all-gather.7 = bf16[512,768]{1,0:T(8,128)(2,1)S(1)} all-gather(bf16[256,768]{1,0:T(8,128)(2,1)S(1)} %shard_map.132.after_ref), channel_id=9, replica_groups={{4,8},{5,9},{6,10},{7,11},{0,1},{2,3},{12,13},{14,15},{20,24},{21,25},{..., dimensions={0}, use_global_device_ids=true | all-gather | bytes 1179648 | tf_op jit(solution)/shard_map/all_gather | solution.py:255
  170.1 0.9 shard_map.136.after_ref.h_ref
  171.0 1.3 collective-permute-start.18
  172.3 2.4 %all-gather.6 = bf16[512,768]{1,0:T(8,128)(2,1)S(1)} all-gather(bf16[256,768]{1,0:T(8,128)(2,1)S(1)} %shard_map.135.after_ref), channel_id=8, replica_groups={{4,8},{5,9},{6,10},{7,11},{0,1},{2,3},{12,13},{14,15},{20,24},{21,25},{..., dimensions={0}, use_global_device_ids=true | all-gather | bytes 1179648 | tf_op jit(solution)/shard_map/all_gather | solution.py:255
  174.7 5.0 %shard_map.137 = (f32[256,2560]{1,0:T(8,128)S(1)}, f32[256,128]{1,0:T(8,128)S(1)}) custom-call(s32[1]{0:T(128)} %bitcast.end_ref, bf16[256,768]{1,0:T(8,128)(2,1)S(1)} %shard_map.133.after_ref.h_ref, bf16[256,768]{1,0:T(8,128)(2,1)S(1)} %collective-permute-done.16.r_ref, bf16[6144,2560]{1,0:T(8,128)(2,1)} %w_ref.31, bf16[6144,128]{1,0:T(8,128)(2,1)S(1)} %copy-done.1, ...), custom_call_target="tpu_custom_call" | custom-call | flops 1000 | bytes 1000 | tf_op jit(solution)/shard_map/pallas_call | solution.py:197
  179.7 0.9 shard_map.138.after_ref.h_ref
  180.6 1.3 collective-permute-start.17
  181.9 8.0 %collective-permute-done.18.r_ref = bf16[256,768]{1,0:T(8,128)(2,1)S(1)} collective-permute-done((bf16[256,768]{1,0:T(8,128)(2,1)S(1)}, bf16[256,768]{1,0:T(8,128)(2,1)S(1)}, u32[]{:S(2)}, u32[]{:S(2)}) %collective-permute-start.18) | collective-permute-done | bytes 393248 | tf_op jit(solution)/shard_map/ppermute | solution.py:262
  189.9 5.0 %shard_map.139 = (f32[256,2560]{1,0:T(8,128)S(1)}, f32[256,128]{1,0:T(8,128)S(1)}) custom-call(s32[1]{0:T(128)} %bitcast.end_ref, bf16[256,768]{1,0:T(8,128)(2,1)S(1)} %shard_map.136.after_ref.h_ref, bf16[256,768]{1,0:T(8,128)(2,1)S(1)} %collective-permute-done.18.r_ref, bf16[6144,2560]{1,0:T(8,128)(2,1)} %w_ref.31, bf16[6144,128]{1,0:T(8,128)(2,1)S(1)} %copy-done.1, ...), custom_call_target="tpu_custom_call" | custom-call | flops 1000 | bytes 1000 | tf_op jit(solution)/shard_map/pallas_call | solution.py:197
  194.9 10.7 %collective-permute-done.17.r_ref = bf16[256,768]{1,0:T(8,128)(2,1)S(1)} collective-permute-done((bf16[256,768]{1,0:T(8,128)(2,1)S(1)}, bf16[256,768]{1,0:T(8,128)(2,1)S(1)}, u32[]{:S(2)}, u32[]{:S(2)}) %collective-permute-start.17) | collective-permute-done | bytes 393248 | tf_op jit(solution)/shard_map/ppermute | solution.py:262
  205.6 5.0 %shard_map.140 = (f32[256,2560]{1,0:T(8,128)S(1)}, f32[256,128]{1,0:T(8,128)S(1)}) custom-call(s32[1]{0:T(128)} %bitcast.end_ref, bf16[256,768]{1,0:T(8,128)(2,1)S(1)} %shard_map.138.after_ref.h_ref, bf16[256,768]{1,0:T(8,128)(2,1)S(1)} %collective-permute-done.17.r_ref, bf16[6144,2560]{1,0:T(8,128)(2,1)} %w_ref.31, bf16[6144,128]{1,0:T(8,128)(2,1)S(1)} %copy-done.1, ...), custom_call_target="tpu_custom_call" | custom-call | flops 1000 | bytes 1000 | tf_op jit(solution)/shard_map/pallas_call | solution.py:197
  210.6 0.2 constant_dynamic-update-slice_fusion.5
  210.8 0.1 convert.10
  211.2 2.0 collective-permute-done.19
  213.4 1.6 collective-permute-start.20
  215.0 8.6 %collective-permute-done.20 = bf16[64,2688]{1,0:T(8,128)(2,1)S(1)} collective-permute-done((bf16[64,2688]{1,0:T(8,128)(2,1)S(1)}, bf16[64,2688]{1,0:T(8,128)(2,1)S(1)}, u32[]{:S(2)}, u32[]{:S(2)}) %collective-permute-start.20) | collective-permute-done | bytes 344096 | tf_op jit(solution)/shard_map/ppermute | solution.py:241
  223.7 1.0 fusion.1
  (64 shorter events, 1.4 us)
Async XLA Ops:
  0.0 223.7 %copy-start = (bf16[128,2560]{1,0:T(8,128)(2,1)S(1)}, bf16[128,2560]{1,0:T(8,128)(2,1)}, u32[]{:S(2)}) copy-start(bf16[128,2560]{1,0:T(8,128)(2,1)} %param.21) | copy-start | bytes 1966084
  0.0 12.5 %copy-start.9 = (bf16[2560,128]{1,0:T(8,128)(2,1)S(1)}, bf16[2560,128]{1,0:T(8,128)(2,1)}, u32[]{:S(2)}) copy-start(bf16[2560,128]{1,0:T(8,128)(2,1)} %d_ref.9) | copy-start | bytes 1966084
  0.0 10.9 %collective-permute-start.1 = (bf16[64,2560]{1,0:T(8,128)(2,1)}, bf16[64,2560]{1,0:T(8,128)(2,1)S(1)}, u32[]{:S(2)}, u32[]{:S(2)}) collective-permute-start(bf16[64,2560]{1,0:T(8,128)(2,1)} %param.11), channel_id=1, source_target_pairs={{0,2},{1,3},{2,0},{3,1},{4,6},{5,7},{6,4},{7,5},{8,10},{9,11},{10,... | collective-permute-start | bytes 983048 | tf_op jit(solution)/shard_map/ppermute | solution.py:241
  2.9 7.9 %collective-permute-start = (bf16[64,2560]{1,0:T(8,128)(2,1)}, bf16[64,2560]{1,0:T(8,128)(2,1)S(1)}, u32[]{:S(2)}, u32[]{:S(2)}) collective-permute-start(bf16[64,2560]{1,0:T(8,128)(2,1)} %param.11), channel_id=1, source_target_pairs={{0,1},{1,0},{2,3},{3,2},{4,5},{5,4},{6,7},{7,6},{8,9},{9,8},{10,11... | collective-permute-start | bytes 983048 | tf_op jit(solution)/shard_map/ppermute | solution.py:241
  10.9 1.6 collective-permute-start.2
  12.5 9.8 %copy-start.11 = (s32[256]{0:T(256)S(1)}, s32[256]{0:T(256)}, u32[]{:S(2)}) copy-start(s32[256]{0:T(256)} %param.12) | copy-start | bytes 3076
  12.5 9.8 %copy-start.12 = (s32[4]{0:T(128)S(1)}, s32[4]{0:T(128)}, u32[]{:S(2)}) copy-start(s32[4]{0:T(128)} %param.13) | copy-start | bytes 52
  18.5 14.6 %collective-permute-start.4 = (bf16[256,896]{1,0:T(8,128)(2,1)S(1)}, bf16[256,896]{1,0:T(8,128)(2,1)S(1)}, u32[]{:S(2)}, u32[]{:S(2)}) collective-permute-start(bf16[256,896]{1,0:T(8,128)(2,1)S(1)} %shard_map.109.after_ref.a_ref), channel_id=1, source_target_pairs={{0,4},{12,8},{1,5},{13,9},{2,6},{14,10},{3,7},{15,11},{16,20},{28,... | collective-permute-start | bytes 1376264 | tf_op jit(solution)/shard_map/ppermute | solution.py:252
  26.1 19.1 %collective-permute-start.3 = (bf16[256,768]{1,0:T(8,128)(2,1)S(1)}, bf16[256,768]{1,0:T(8,128)(2,1)}, u32[]{:S(2)}, u32[]{:S(2)}) collective-permute-start(bf16[256,768]{1,0:T(8,128)(2,1)S(1)} %shard_map.110.after_ref.a_ref), channel_id=1, source_target_pairs={{0,4},{12,8},{1,5},{13,9},{2,6},{14,10},{3,7},{15,11},{16,20},{28,... | collective-permute-start | bytes 1179656 | tf_op jit(solution)/shard_map/ppermute | solution.py:252
  37.7 27.8 %collective-permute-start.7 = (bf16[256,768]{1,0:T(8,128)(2,1)}, bf16[256,768]{1,0:T(8,128)(2,1)}, u32[]{:S(2)}, u32[]{:S(2)}) collective-permute-start(bf16[256,768]{1,0:T(8,128)(2,1)} %shard_map.112.after_ref.a_ref), channel_id=1, source_target_pairs={{0,4},{12,8},{1,5},{13,9},{2,6},{14,10},{3,7},{15,11},{16,20},{28,... | collective-permute-start | bytes 1179656 | tf_op jit(solution)/shard_map/ppermute | solution.py:252
  46.4 4.6 %copy-start.5 = (bf16[256,768]{1,0:T(8,128)(2,1)}, bf16[256,768]{1,0:T(8,128)(2,1)S(1)}, u32[]{:S(2)}) copy-start(bf16[256,768]{1,0:T(8,128)(2,1)S(1)} %shard_map.113.after_ref) | copy-start | bytes 1179652
  46.4 4.6 %copy-start.2 = (bf16[128,6144]{1,0:T(8,128)(2,1)S(1)}, bf16[128,6144]{1,0:T(8,128)(2,1)}, u32[]{:S(2)}) copy-start(bf16[128,6144]{1,0:T(8,128)(2,1)} %up_ref.15) | copy-start | bytes 4718596
  46.4 4.6 %copy-start.7 = (f32[6144]{0:T(1024)S(1)}, f32[6144]{0:T(1024)}, u32[]{:S(2)}) copy-start(f32[6144]{0:T(1024)} %param.15) | copy-start | bytes 73732
  51.0 2.0 copy-start.3
  53.0 29.7 %collective-permute-start.6 = (bf16[256,768]{1,0:T(8,128)(2,1)}, bf16[256,768]{1,0:T(8,128)(2,1)}, u32[]{:S(2)}, u32[]{:S(2)}) collective-permute-start(bf16[256,768]{1,0:T(8,128)(2,1)} %shard_map.115.after_ref.h_ref), channel_id=1, source_target_pairs={{4,0},{8,12},{5,1},{9,13},{6,2},{10,14},{7,3},{11,15},{20,16},{24,... | collective-permute-start | bytes 1179656 | tf_op jit(solution)/shard_map/ppermute | solution.py:262
  54.3 33.7 %collective-permute-start.5 = (bf16[256,768]{1,0:T(8,128)(2,1)}, bf16[256,768]{1,0:T(8,128)(2,1)}, u32[]{:S(2)}, u32[]{:S(2)}) collective-permute-start(bf16[256,768]{1,0:T(8,128)(2,1)} %shard_map.114.after_ref.a_ref), channel_id=1, source_target_pairs={{0,4},{12,8},{1,5},{13,9},{2,6},{14,10},{3,7},{15,11},{16,20},{28,... | collective-permute-start | bytes 1179656 | tf_op jit(solution)/shard_map/ppermute | solution.py:252
  65.5 1.3 copy-start.6
  69.1 11.3 %copy-start.4 = (bf16[256,128]{1,0:T(8,128)(2,1)S(1)}, bf16[256,128]{1,0:T(8,128)(2,1)}, u32[]{:S(2)}) copy-start(bf16[256,128]{1,0:T(8,128)(2,1)} %copy-done.3) | copy-start | bytes 196612
  69.1 11.3 %copy-start.8 = (f32[6144]{0:T(1024)S(1)}, f32[6144]{0:T(1024)}, u32[]{:S(2)}) copy-start(f32[6144]{0:T(1024)} %param.15) | copy-start | bytes 73732
  72.8 40.3 %collective-permute-start.11 = (bf16[256,768]{1,0:T(8,128)(2,1)S(1)}, bf16[256,768]{1,0:T(8,128)(2,1)S(1)}, u32[]{:S(2)}, u32[]{:S(2)}) collective-permute-start(bf16[256,768]{1,0:T(8,128)(2,1)S(1)} %shard_map.117.after_ref.a_ref), channel_id=1, source_target_pairs={{0,4},{12,8},{1,5},{13,9},{2,6},{14,10},{3,7},{15,11},{16,20},{28,... | collective-permute-start | bytes 1179656 | tf_op jit(solution)/shard_map/ppermute | solution.py:252
  80.5 2.2 %copy-start.1 = (bf16[6144,128]{1,0:T(8,128)(2,1)S(1)}, bf16[6144,128]{1,0:T(8,128)(2,1)}, u32[]{:S(2)}) copy-start(bf16[6144,128]{1,0:T(8,128)(2,1)} %d_ref.17) | copy-start | bytes 4718596
  81.4 26.7 %collective-permute-start.10 = (bf16[256,768]{1,0:T(8,128)(2,1)S(1)}, bf16[256,768]{1,0:T(8,128)(2,1)S(1)}, u32[]{:S(2)}, u32[]{:S(2)}) collective-permute-start(bf16[256,768]{1,0:T(8,128)(2,1)S(1)} %shard_map.118.acc_ref.low_ref.after_ref.h_ref), channel_id=1, source_target_pairs={{4,0},{8,12},{5,1},{9,13},{6,2},{10,14},{7,3},{11,15},{20,16},{24,... | collective-permute-start | bytes 1179656 | tf_op jit(solution)/shard_map/ppermute | solution.py:262
  96.1 32.8 %collective-permute-start.9 = (bf16[256,768]{1,0:T(8,128)(2,1)S(1)}, bf16[256,768]{1,0:T(8,128)(2,1)S(1)}, u32[]{:S(2)}, u32[]{:S(2)}) collective-permute-start(bf16[256,768]{1,0:T(8,128)(2,1)S(1)} %shard_map.122.after_ref.h_ref), channel_id=1, source_target_pairs={{4,0},{8,12},{5,1},{9,13},{6,2},{10,14},{7,3},{11,15},{20,16},{24,... | collective-permute-start | bytes 1179656 | tf_op jit(solution)/shard_map/ppermute | solution.py:262
  97.4 36.5 %collective-permute-start.8 = (bf16[256,768]{1,0:T(8,128)(2,1)S(1)}, bf16[256,768]{1,0:T(8,128)(2,1)S(1)}, u32[]{:S(2)}, u32[]{:S(2)}) collective-permute-start(bf16[256,768]{1,0:T(8,128)(2,1)S(1)} %shard_map.121.after_ref.a_ref), channel_id=1, source_target_pairs={{0,4},{12,8},{1,5},{13,9},{2,6},{14,10},{3,7},{15,11},{16,20},{28,... | collective-permute-start | bytes 1179656 | tf_op jit(solution)/shard_map/ppermute | solution.py:252
  119.3 41.1 %collective-permute-start.15 = (bf16[256,768]{1,0:T(8,128)(2,1)S(1)}, bf16[256,768]{1,0:T(8,128)(2,1)S(1)}, u32[]{:S(2)}, u32[]{:S(2)}) collective-permute-start(bf16[256,768]{1,0:T(8,128)(2,1)S(1)} %shard_map.125.after_ref.a_ref), channel_id=1, source_target_pairs={{0,4},{12,8},{1,5},{13,9},{2,6},{14,10},{3,7},{15,11},{16,20},{28,... | collective-permute-start | bytes 1179656 | tf_op jit(solution)/shard_map/ppermute | solution.py:252
  127.6 27.8 %collective-permute-start.14 = (bf16[256,768]{1,0:T(8,128)(2,1)S(1)}, bf16[256,768]{1,0:T(8,128)(2,1)S(1)}, u32[]{:S(2)}, u32[]{:S(2)}) collective-permute-start(bf16[256,768]{1,0:T(8,128)(2,1)S(1)} %shard_map.126.after_ref.h_ref), channel_id=1, source_target_pairs={{4,0},{8,12},{5,1},{9,13},{6,2},{10,14},{7,3},{11,15},{20,16},{24,... | collective-permute-start | bytes 1179656 | tf_op jit(solution)/shard_map/ppermute | solution.py:262
  141.0 21.7 %collective-permute-start.13 = (bf16[256,768]{1,0:T(8,128)(2,1)S(1)}, bf16[256,768]{1,0:T(8,128)(2,1)S(1)}, u32[]{:S(2)}, u32[]{:S(2)}) collective-permute-start(bf16[256,768]{1,0:T(8,128)(2,1)S(1)} %shard_map.130.after_ref.h_ref), channel_id=1, source_target_pairs={{4,0},{8,12},{5,1},{9,13},{6,2},{10,14},{7,3},{11,15},{20,16},{24,... | collective-permute-start | bytes 1179656 | tf_op jit(solution)/shard_map/ppermute | solution.py:262
  142.3 25.4 %collective-permute-start.12 = (bf16[256,768]{1,0:T(8,128)(2,1)S(1)}, bf16[256,768]{1,0:T(8,128)(2,1)S(1)}, u32[]{:S(2)}, u32[]{:S(2)}) collective-permute-start(bf16[256,768]{1,0:T(8,128)(2,1)S(1)} %shard_map.129.after_ref.a_ref), channel_id=1, source_target_pairs={{0,4},{12,8},{1,5},{13,9},{2,6},{14,10},{3,7},{15,11},{16,20},{28,... | collective-permute-start | bytes 1179656 | tf_op jit(solution)/shard_map/ppermute | solution.py:252
  161.4 13.3 %collective-permute-start.16 = (bf16[256,768]{1,0:T(8,128)(2,1)S(1)}, bf16[256,768]{1,0:T(8,128)(2,1)S(1)}, u32[]{:S(2)}, u32[]{:S(2)}) collective-permute-start(bf16[256,768]{1,0:T(8,128)(2,1)S(1)} %shard_map.133.after_ref.h_ref), channel_id=1, source_target_pairs={{4,0},{8,12},{5,1},{9,13},{6,2},{10,14},{7,3},{11,15},{20,16},{24,... | collective-permute-start | bytes 1179656 | tf_op jit(solution)/shard_map/ppermute | solution.py:262
  171.0 18.9 %collective-permute-start.18 = (bf16[256,768]{1,0:T(8,128)(2,1)S(1)}, bf16[256,768]{1,0:T(8,128)(2,1)S(1)}, u32[]{:S(2)}, u32[]{:S(2)}) collective-permute-start(bf16[256,768]{1,0:T(8,128)(2,1)S(1)} %shard_map.136.after_ref.h_ref), channel_id=1, source_target_pairs={{4,0},{8,12},{5,1},{9,13},{6,2},{10,14},{7,3},{11,15},{20,16},{24,... | collective-permute-start | bytes 1179656 | tf_op jit(solution)/shard_map/ppermute | solution.py:262
  180.6 25.0 %collective-permute-start.17 = (bf16[256,768]{1,0:T(8,128)(2,1)S(1)}, bf16[256,768]{1,0:T(8,128)(2,1)S(1)}, u32[]{:S(2)}, u32[]{:S(2)}) collective-permute-start(bf16[256,768]{1,0:T(8,128)(2,1)S(1)} %shard_map.138.after_ref.h_ref), channel_id=1, source_target_pairs={{4,0},{8,12},{5,1},{9,13},{6,2},{10,14},{7,3},{11,15},{20,16},{24,... | collective-permute-start | bytes 1179656 | tf_op jit(solution)/shard_map/ppermute | solution.py:262
  211.0 2.2 collective-permute-start.19
  213.4 10.3 %copy-start.10 = (f32[2560]{0:T(1024)S(1)}, f32[2560]{0:T(1024)}, u32[]{:S(2)}) copy-start(f32[2560]{0:T(1024)} %param.19) | copy-start | bytes 30724
  213.4 10.2 %collective-permute-start.20 = (bf16[64,2688]{1,0:T(8,128)(2,1)S(1)}, bf16[64,2688]{1,0:T(8,128)(2,1)S(1)}, u32[]{:S(2)}, u32[]{:S(2)}) collective-permute-start(bf16[64,2688]{1,0:T(8,128)(2,1)S(1)} %slice.80), channel_id=1, source_target_pairs={{0,2},{1,3},{2,0},{3,1},{4,6},{5,7},{6,4},{7,5},{8,10},{9,11},{10,... | collective-permute-start | bytes 1032200 | tf_op jit(solution)/shard_map/ppermute | solution.py:241

commit v3 on v2

--- a/solution.py
+++ b/solution.py
@@ -52,7 +52,7 @@
 
 def chunk_spans(hidden):
     units = hidden // LANES
-    count = max(n for n in range(1, 9) if units % n == 0)
+    count = max(n for n in range(1, 5) if units % n == 0)
     width = hidden // count
     return [(start, width) for start in range(0, hidden, width)]
 
@@ -115,50 +115,20 @@
     )(x, weight, down, after)
 
 
-def add_kernel(a_ref, b_ref, after_ref, out_ref):
-    out_ref[...] = (a_ref[...].astype(F32) + b_ref[...].astype(F32)).astype(BF16)
+def tie(value, after):
+    return lax.optimization_barrier((value, after))[0]
 
 
 def add_rounded(a, b, after):
-    return pl.pallas_call(
-        add_kernel,
-        grid=(1,),
-        in_specs=[whole(a.shape), whole(b.shape), ANY],
-        out_specs=whole(a.shape),
-        out_shape=jax.ShapeDtypeStruct(a.shape, BF16),
-        compiler_params=PARAMS,
-        cost_estimate=COST,
-    )(a, b, after)
-
-
-def gelu_kernel(m_ref, low_ref, up_ref, bias_ref, after_ref, out_ref):
-    summed = m_ref[0].astype(F32) + m_ref[1].astype(F32)
-    before = summed + bias_ref[...] + dot(low_ref[...], up_ref[...])
-    out_ref[...] = gelu_tanh(before).astype(BF16)
+    return (tie(a, after).astype(F32) + b.astype(F32)).astype(BF16)
 
 
 def gelu_chunk(pair, low_in, up_maps, bias, span, after):
     start, width = span
-    rows = pair.shape[1]
-    tile = tile_of(width, 256)
-    while start % tile:
-        tile -= LANES
-    base = start // tile
-    return pl.pallas_call(
-        gelu_kernel,
-        grid=(width // tile,),
-        in_specs=[
-            pl.BlockSpec((2, rows, tile), lambda j: (0, 0, j)),
-            whole(low_in.shape),
-            pl.BlockSpec((up_maps.shape[0], tile), lambda j: (0, base + j)),
-            pl.BlockSpec((1, tile), lambda j: (0, base + j)),
-            ANY,
-        ],
-        out_specs=pl.BlockSpec((rows, tile), lambda j: (0, j)),
-        out_shape=jax.ShapeDtypeStruct((rows, width), BF16),
-        compiler_params=PARAMS,
-        cost_estimate=COST,
-    )(pair, low_in, up_maps, bias, after)
+    part = slice(start, start + width)
+    pair = tie(pair, after)[:, :, :width].astype(F32)
+    before = pair[0] + pair[1] + bias[:, part] + dot(low_in, up_maps[:, part])
+    return gelu_tanh(before).astype(BF16)
 
 
 def second_kernel(end_ref, h_ref, r_ref, w_ref, d_ref, acc_ref, low_ref, after_ref, out_ref, low_out_ref, state, *, first):

time: 226 us -> 224 us (level)
  starting transfers between devices: 73.4 us -> 30.9 us
  waiting for transfers between devices: 42.7 us -> 85 us
  Pallas kernels: 85.7 us -> 58.5 us
  blocking collectives: 19 us -> 0 us
  other arithmetic: 0.62 us -> 16.7 us
  between operations: 0.69 us -> 13.6 us
  matrix products: 0.97 us -> 10.3 us
  local copies, waits for them, and re-layouts: 1.55 us -> 7.66 us
    ppermute x8 -> x4, starting transfers between devices: 58.5 us -> 20.9 us  [fold(): return lax.ppermute(value, 'row', pairs)]
    ppermute x8 -> x4, waiting for transfers between devices: 18.7 us -> 46.9 us  [spread(): come = lax.ppermute(value, 'row', pairs)]
    all_gather x8 -> x0, blocking collectives: 19 us -> none  [cross(): lax.all_gather(value, ('group', 'row', 'col'), axis=0, tiled=False, axis_...]
    convert_element_type x0 -> x8, other arithmetic: none -> 14.4 us  [the longest x4 7.23 us: gelu_chunk(): pair = tie(pair, after)[:, :, :width].astype(F32)]
    ppermute x8 -> x4, waiting for transfers between devices: 4.87 us -> 18.9 us  [fold(): return lax.ppermute(value, 'row', pairs)]
    pallas_call x16 -> x0, Pallas kernels: 12.4 us -> none  [the longest x8 8.34 us: gelu_chunk(): pl.pallas_call(gelu_kernel, grid=(width // tile,), in_specs=[pl.BlockSpec...]
    pallas_call x8 -> x4, Pallas kernels: 39.9 us -> 27.6 us  [second_product(): pl.pallas_call(functools.partial(second_kernel, first=first), grid=(out_w...]
    dot_general x1 -> x5, matrix products: 0.97 us -> 10.3 us  [dot(): return jnp.dot(left, right, preferred_element_type=F32)]
  transfers between devices with their start and end apart: 21 -> 17, of which waited for: 7 -> 11; matrix products, arithmetic and copies ran while one was open for 1% -> 12% of each run, Pallas kernels for 33% -> 18%
where the time goes in v3:
time: 224 us; the launch traced here: 223 us
  waiting for transfers between devices  85 us (38%)
  Pallas kernels  58.5 us (26%)
  starting transfers between devices  30.9 us (14%)
  other arithmetic  16.7 us (7%)
  between operations  13.6 us (6%)
  matrix products  10.3 us (5%)
  local copies, waits for them, and re-layouts  7.66 us (3%)
    ppermute x4, waiting for transfers between devices, spread(): come = lax.ppermute(value, 'row', pairs)  46.9 us
    pallas_call x4, Pallas kernels, second_product(): pl.pallas_call(functools.partial(second_kernel, first=first), grid=(out_w...  27.6 us
    ppermute x4, starting transfers between devices, fold(): return lax.ppermute(value, 'row', pairs)  20.9 us
    pallas_call x3, Pallas kernels, first_product(): pl.pallas_call(first_kernel, grid=(width // tile,), in_specs=[whole(x.sha...  20 us
    ppermute x5, waiting for transfers between devices, col_swap(): return lax.ppermute(value, 'col', [(i, i ^ flip) for i in range(n_col)])  19.1 us
    ppermute x4, waiting for transfers between devices, fold(): return lax.ppermute(value, 'row', pairs)  18.9 us
    pallas_call x1, Pallas kernels, first_product_low(): pl.pallas_call(functools.partial(low_kernel, tiles=tiles, width=width), g...  11 us
    dot_general x5, matrix products, dot(): return jnp.dot(left, right, preferred_element_type=F32)  10.3 us
  transfers between devices with their start and end apart: 17, of which 11 were waited for; matrix products, arithmetic and copies ran while one was open for 12% of the time, Pallas kernels for 18%

profile of v3, /device:TPU:0, one launch (start us, length us, event | category | flops | bytes accessed | tf_op | source)
XLA Modules:
  0.0 222.7 jit_solution(8258418273196912355)
XLA Ops:
  6.5 2.9 %collective-permute-start.1 = (bf16[64,2560]{1,0:T(8,128)(2,1)}, bf16[64,2560]{1,0:T(8,128)(2,1)S(1)}, u32[]{:S(2)}, u32[]{:S(2)}) collective-permute-start(bf16[64,2560]{1,0:T(8,128)(2,1)} %param.11), channel_id=1, source_target_pairs={{0,2},{1,3},{2,0},{3,1},{4,6},{5,7},{6,4},{7,5},{8,10},{9,11},{10,... | collective-permute-start | bytes 983048 | tf_op jit(solution)/shard_map/ppermute | solution.py:211
  9.5 1.0 constant_dynamic-update-slice_fusion.3
  10.5 6.9 %collective-permute-done.1 = bf16[64,2560]{1,0:T(8,128)(2,1)S(1)} collective-permute-done((bf16[64,2560]{1,0:T(8,128)(2,1)}, bf16[64,2560]{1,0:T(8,128)(2,1)S(1)}, u32[]{:S(2)}, u32[]{:S(2)}) %collective-permute-start.1) | collective-permute-done | bytes 327712 | tf_op jit(solution)/shard_map/ppermute | solution.py:211
  17.5 1.6 collective-permute-done.2
  19.1 11.0 %shard_map.109.after_ref = bf16[256,1664]{1,0:T(8,128)(2,1)S(1)} custom-call(bf16[256,2560]{1,0:T(8,128)(2,1)S(1)} %constant_dynamic-update-slice_fusion.x_ref.after_ref, bf16[2560,6144]{1,0:T(8,128)(2,1)} %w_ref.11, bf16[2560,128]{1,0:T(8,128)(2,1)S(1)} %copy-done.12, bf16[256,2560]{1,0:T(8,128)(2,1)S(1)} %constant_dynamic-update-slice_fusion.x_ref.after_ref), custom_call_target="tpu_custom_call" | custom-call | flops 1000 | bytes 1000 | tf_op jit(solution)/shard_map/pallas_call | solution.py:102
  30.0 3.8 %collective-permute-start.3 = (bf16[256,1664]{1,0:T(8,128)(2,1)S(1)}, bf16[256,1664]{1,0:T(8,128)(2,1)S(1)}, u32[]{:S(2)}, u32[]{:S(2)}) collective-permute-start(bf16[256,1664]{1,0:T(8,128)(2,1)S(1)} %shard_map.109.after_ref), channel_id=1, source_target_pairs={{0,4},{12,8},{1,5},{13,9},{2,6},{14,10},{3,7},{15,11},{16,20},{28,... | collective-permute-start | bytes 2555912 | tf_op jit(solution)/shard_map/ppermute | solution.py:222
  33.8 6.3 %shard_map.110 = bf16[256,1536]{1,0:T(8,128)(2,1)S(1)} custom-call(bf16[256,2560]{1,0:T(8,128)(2,1)S(1)} %constant_dynamic-update-slice_fusion.x_ref.after_ref, bf16[2560,6144]{1,0:T(8,128)(2,1)} %w_ref.11, bf16[256,1664]{1,0:T(8,128)(2,1)S(1)} %shard_map.109.after_ref), custom_call_target="tpu_custom_call" | custom-call | flops 1000 | bytes 1000 | tf_op jit(solution)/shard_map/pallas_call | solution.py:70
  40.1 0.9 copy-done.4
  41.0 11.3 %collective-permute-done.3 = bf16[256,1664]{1,0:T(8,128)(2,1)S(1)} collective-permute-done((bf16[256,1664]{1,0:T(8,128)(2,1)S(1)}, bf16[256,1664]{1,0:T(8,128)(2,1)S(1)}, u32[]{:S(2)}, u32[]{:S(2)}) %collective-permute-start.3) | collective-permute-done | bytes 852000 | tf_op jit(solution)/shard_map/ppermute | solution.py:222
  52.3 1.1 add_convert_fusion.after_ref
  53.4 0.0 all-gather.11.cloned.1.call-start
  53.4 5.4 %collective-permute-start.4 = (bf16[256,1536]{1,0:T(8,128)(2,1)}, bf16[256,1536]{1,0:T(8,128)(2,1)}, u32[]{:S(2)}, u32[]{:S(2)}) collective-permute-start(bf16[256,1536]{1,0:T(8,128)(2,1)} %copy-done.4), channel_id=1, source_target_pairs={{0,4},{12,8},{1,5},{13,9},{2,6},{14,10},{3,7},{15,11},{16,20},{28,... | collective-permute-start | bytes 2359304 | tf_op jit(solution)/shard_map/ppermute | solution.py:222
  58.8 0.1 select_reduce_fusion
  58.9 0.1 broadcast_compare_fusion
  59.0 0.6 constant_dynamic-slice_fusion.2
  59.7 0.7 slice_reduce_fusion
  60.3 6.6 %shard_map.111 = bf16[256,1536]{1,0:T(8,128)(2,1)S(1)} custom-call(bf16[256,2560]{1,0:T(8,128)(2,1)S(1)} %constant_dynamic-update-slice_fusion.x_ref.after_ref, bf16[2560,6144]{1,0:T(8,128)(2,1)} %w_ref.11, bf16[256,1664]{1,0:T(8,128)(2,1)S(1)} %copy-done.2), custom_call_target="tpu_custom_call" | custom-call | flops 1000 | bytes 1000 | tf_op jit(solution)/shard_map/pallas_call | solution.py:70
  67.0 0.9 copy-done.6
  67.9 6.6 %collective-permute-done.4 = bf16[256,1536]{1,0:T(8,128)(2,1)} collective-permute-done((bf16[256,1536]{1,0:T(8,128)(2,1)}, bf16[256,1536]{1,0:T(8,128)(2,1)}, u32[]{:S(2)}, u32[]{:S(2)}) %collective-permute-start.4) | collective-permute-done | bytes 786464 | tf_op jit(solution)/shard_map/ppermute | solution.py:222
  74.5 1.4 add_convert_fusion.3.after_ref
  75.9 5.3 %collective-permute-start.6 = (bf16[256,1536]{1,0:T(8,128)(2,1)S(1)}, bf16[256,1536]{1,0:T(8,128)(2,1)}, u32[]{:S(2)}, u32[]{:S(2)}) collective-permute-start(bf16[256,1536]{1,0:T(8,128)(2,1)S(1)} %copy-done.7), channel_id=1, source_target_pairs={{0,4},{12,8},{1,5},{13,9},{2,6},{14,10},{3,7},{15,11},{16,20},{28,... | collective-permute-start | bytes 2359304 | tf_op jit(solution)/shard_map/ppermute | solution.py:222
  81.2 7.1 %shard_map.112 = bf16[256,1536]{1,0:T(8,128)(2,1)} custom-call(bf16[256,2560]{1,0:T(8,128)(2,1)S(1)} %constant_dynamic-update-slice_fusion.x_ref.after_ref, bf16[2560,6144]{1,0:T(8,128)(2,1)} %w_ref.11, bf16[256,1536]{1,0:T(8,128)(2,1)S(1)} %add_convert_fusion.3.after_ref), custom_call_target="tpu_custom_call" | custom-call | flops 1000 | bytes 1000 | tf_op jit(solution)/shard_map/pallas_call | solution.py:70
  88.4 0.0 all-gather.15.cloned.1.call-start
  88.4 0.9 slice_convert_fusion.2
  89.4 0.7 fusion.36
  90.1 1.8 slice_convert_fusion
  91.9 2.7 %fusion.4.h_ref = bf16[256,1536]{1,0:T(8,128)(2,1)} fusion(bf16[256,128]{1,0:T(8,128)(2,1)S(1)} %fusion.36, f32[2,256,1536]{2,1,0:T(8,128)S(1)} %slice_convert_fusion, f32[1536]{0:T(1024)S(1)} %copy-done.18, bf16[128,6144]{1,0:T(8,128)(2,1)} %param.17), kind=kOutput, calls=%fused_computation.13 | convolution fusion | flops 105381888 | bytes 4397056 | tf_op jit(solution)/shard_map/dot_general | solution.py:38
  94.6 1.0 collective-permute-done.6
  95.7 2.2 %add_convert_fusion.2 = bf16[256,1536]{1,0:T(8,128)(2,1)} fusion(bf16[256,1536]{1,0:T(8,128)(2,1)} %collective-permute-done.6, bf16[256,1536]{1,0:T(8,128)(2,1)S(1)} %copy-done.7), kind=kLoop, calls=%fused_computation.42 | loop fusion | flops 1572864 | bytes 2359296 | tf_op jit(solution)/shard_map/convert_element_type | solution.py:123
  97.9 0.0 all-gather.13.cloned.1.call-start
  98.0 1.3 collective-permute-start.5
  99.3 6.4 %collective-permute-start.7 = (bf16[256,1536]{1,0:T(8,128)(2,1)}, bf16[256,1536]{1,0:T(8,128)(2,1)}, u32[]{:S(2)}, u32[]{:S(2)}) collective-permute-start(bf16[256,1536]{1,0:T(8,128)(2,1)} %shard_map.112), channel_id=1, source_target_pairs={{0,4},{12,8},{1,5},{13,9},{2,6},{14,10},{3,7},{15,11},{16,20},{28,... | collective-permute-start | bytes 2359304 | tf_op jit(solution)/shard_map/ppermute | solution.py:222
  105.7 1.8 convert_element_type.94
  107.6 1.9 fusion.9.acc_ref.low_ref.after_ref.h_ref
  109.5 7.9 %collective-permute-done.5.r_ref = bf16[256,1536]{1,0:T(8,128)(2,1)} collective-permute-done((bf16[256,1536]{1,0:T(8,128)(2,1)}, bf16[256,1536]{1,0:T(8,128)(2,1)}, u32[]{:S(2)}, u32[]{:S(2)}) %collective-permute-start.5) | collective-permute-done | bytes 786464 | tf_op jit(solution)/shard_map/ppermute | solution.py:232
  117.4 7.1 %shard_map.113 = (f32[256,2560]{1,0:T(8,128)S(1)}, f32[256,128]{1,0:T(8,128)S(1)}) custom-call(s32[1]{0:T(128)} %bitcast.end_ref, bf16[256,1536]{1,0:T(8,128)(2,1)} %fusion.4.h_ref, bf16[256,1536]{1,0:T(8,128)(2,1)} %collective-permute-done.5.r_ref, bf16[6144,2560]{1,0:T(8,128)(2,1)} %w_ref.15, bf16[6144,128]{1,0:T(8,128)(2,1)S(1)} %copy-done.1, ...), custom_call_target="tpu_custom_call" | custom-call | flops 1000 | bytes 1000 | tf_op jit(solution)/shard_map/pallas_call | solution.py:167
  124.5 1.5 copy-done.8
  126.0 2.4 %add_convert_fusion.1 = bf16[256,1536]{1,0:T(8,128)(2,1)} fusion(bf16[256,1536]{1,0:T(8,128)(2,1)} %collective-permute-done.7, bf16[256,1536]{1,0:T(8,128)(2,1)} %shard_map.112), kind=kLoop, calls=%fused_computation.41 | loop fusion | flops 1572864 | bytes 2359296 | tf_op jit(solution)/shard_map/convert_element_type | solution.py:123
  128.5 1.3 collective-permute-start.8
  129.8 1.8 convert_element_type.99
  131.6 2.8 %fusion.14.after_ref.h_ref = bf16[256,1536]{1,0:T(8,128)(2,1)} fusion(bf16[256,128]{1,0:T(8,128)(2,1)S(1)} %fusion.36, f32[2,256,1536]{2,1,0:T(8,128)S(1)} %convert_element_type.99, f32[1536]{0:T(1024)S(1)} %copy-done.16, bf16[128,6144]{1,0:T(8,128)(2,1)} %param.17), kind=kOutput, calls=%fused_computation.23 | convolution fusion | flops 105381888 | bytes 4397056 | tf_op jit(solution)/shard_map/dot_general | solution.py:38
  134.5 1.3 collective-permute-start.10
  135.8 15.5 %collective-permute-done.8.r_ref = bf16[256,1536]{1,0:T(8,128)(2,1)} collective-permute-done((bf16[256,1536]{1,0:T(8,128)(2,1)S(1)}, bf16[256,1536]{1,0:T(8,128)(2,1)}, u32[]{:S(2)}, u32[]{:S(2)}) %collective-permute-start.8) | collective-permute-done | bytes 786464 | tf_op jit(solution)/shard_map/ppermute | solution.py:232
  151.2 6.9 %shard_map.114 = (f32[256,2560]{1,0:T(8,128)S(1)}, f32[256,128]{1,0:T(8,128)S(1)}) custom-call(s32[1]{0:T(128)} %bitcast.end_ref, bf16[256,1536]{1,0:T(8,128)(2,1)S(1)} %fusion.9.acc_ref.low_ref.after_ref.h_ref, bf16[256,1536]{1,0:T(8,128)(2,1)} %collective-permute-done.8.r_ref, bf16[6144,2560]{1,0:T(8,128)(2,1)} %w_ref.15, bf16[6144,128]{1,0:T(8,128)(2,1)S(1)} %copy-done.1, ...), custom_call_target="tpu_custom_call" | custom-call | flops 1000 | bytes 1000 | tf_op jit(solution)/shard_map/pallas_call | solution.py:167
  158.2 1.6 copy-done.10
  159.7 1.8 convert_element_type.101
  161.6 1.9 fusion.19.after_ref.h_ref
  163.5 1.5 collective-permute-start.9
  165.0 4.0 %collective-permute-done.10.r_ref = bf16[256,1536]{1,0:T(8,128)(2,1)} collective-permute-done((bf16[256,1536]{1,0:T(8,128)(2,1)}, bf16[256,1536]{1,0:T(8,128)(2,1)}, u32[]{:S(2)}, u32[]{:S(2)}) %collective-permute-start.10) | collective-permute-done | bytes 786464 | tf_op jit(solution)/shard_map/ppermute | solution.py:232
  169.0 7.0 %shard_map.115 = (f32[256,2560]{1,0:T(8,128)S(1)}, f32[256,128]{1,0:T(8,128)S(1)}) custom-call(s32[1]{0:T(128)} %bitcast.end_ref, bf16[256,1536]{1,0:T(8,128)(2,1)} %fusion.14.after_ref.h_ref, bf16[256,1536]{1,0:T(8,128)(2,1)} %collective-permute-done.10.r_ref, bf16[6144,2560]{1,0:T(8,128)(2,1)} %w_ref.15, bf16[6144,128]{1,0:T(8,128)(2,1)S(1)} %copy-done.1, ...), custom_call_target="tpu_custom_call" | custom-call | flops 1000 | bytes 1000 | tf_op jit(solution)/shard_map/pallas_call | solution.py:167
  176.0 19.5 %collective-permute-done.9.r_ref = bf16[256,1536]{1,0:T(8,128)(2,1)S(1)} collective-permute-done((bf16[256,1536]{1,0:T(8,128)(2,1)S(1)}, bf16[256,1536]{1,0:T(8,128)(2,1)S(1)}, u32[]{:S(2)}, u32[]{:S(2)}) %collective-permute-start.9) | collective-permute-done | bytes 786464 | tf_op jit(solution)/shard_map/ppermute | solution.py:232
  195.5 6.5 %shard_map.116 = (f32[256,2560]{1,0:T(8,128)S(1)}, f32[256,128]{1,0:T(8,128)S(1)}) custom-call(s32[1]{0:T(128)} %bitcast.end_ref, bf16[256,1536]{1,0:T(8,128)(2,1)S(1)} %fusion.19.after_ref.h_ref, bf16[256,1536]{1,0:T(8,128)(2,1)S(1)} %collective-permute-done.9.r_ref, bf16[6144,2560]{1,0:T(8,128)(2,1)} %w_ref.15, bf16[6144,128]{1,0:T(8,128)(2,1)S(1)} %copy-done.1, ...), custom_call_target="tpu_custom_call" | custom-call | flops 1000 | bytes 1000 | tf_op jit(solution)/shard_map/pallas_call | solution.py:167
  202.1 0.2 constant_dynamic-update-slice_fusion.5
  202.3 0.1 convert.10
  202.4 0.1 fusion.45
  202.5 0.1 pad_maximum_fusion
  202.6 0.1 collective-permute-start.11
  202.6 0.1 fusion.44
  202.7 2.0 collective-permute-done.11
  204.8 0.1 maximum_add_fusion
  205.0 1.5 collective-permute-start.12
  206.5 8.6 %collective-permute-done.12 = bf16[64,2688]{1,0:T(8,128)(2,1)S(1)} collective-permute-done((bf16[64,2688]{1,0:T(8,128)(2,1)S(1)}, bf16[64,2688]{1,0:T(8,128)(2,1)S(1)}, u32[]{:S(2)}, u32[]{:S(2)}) %collective-permute-start.12) | collective-permute-done | bytes 344096 | tf_op jit(solution)/shard_map/ppermute | solution.py:211
  215.1 0.1 slice_add_fusion.4
  215.2 1.0 fusion.29
  (57 shorter events, 0.3 us)
Async XLA Ops:
  6.5 208.7 %copy-start = (bf16[128,2560]{1,0:T(8,128)(2,1)S(1)}, bf16[128,2560]{1,0:T(8,128)(2,1)}, u32[]{:S(2)}) copy-start(bf16[128,2560]{1,0:T(8,128)(2,1)} %param.21) | copy-start | bytes 1966084
  6.5 12.5 %copy-start.12 = (bf16[2560,128]{1,0:T(8,128)(2,1)S(1)}, bf16[2560,128]{1,0:T(8,128)(2,1)}, u32[]{:S(2)}) copy-start(bf16[2560,128]{1,0:T(8,128)(2,1)} %d_ref.5) | copy-start | bytes 1966084
  6.5 81.9 %all-gather.9.cloned.1.call-start = ((), (), s32[]{:S(2)}) async-start(), calls=%async_computation | async-start | bytes 2555904 | tf_op jit(solution)/shard_map/all_gather | solution.py:225
  6.5 10.9 %collective-permute-start.1 = (bf16[64,2560]{1,0:T(8,128)(2,1)}, bf16[64,2560]{1,0:T(8,128)(2,1)S(1)}, u32[]{:S(2)}, u32[]{:S(2)}) collective-permute-start(bf16[64,2560]{1,0:T(8,128)(2,1)} %param.11), channel_id=1, source_target_pairs={{0,2},{1,3},{2,0},{3,1},{4,6},{5,7},{6,4},{7,5},{8,10},{9,11},{10,... | collective-permute-start | bytes 983048 | tf_op jit(solution)/shard_map/ppermute | solution.py:211
  9.5 7.9 %collective-permute-start = (bf16[64,2560]{1,0:T(8,128)(2,1)}, bf16[64,2560]{1,0:T(8,128)(2,1)S(1)}, u32[]{:S(2)}, u32[]{:S(2)}) collective-permute-start(bf16[64,2560]{1,0:T(8,128)(2,1)} %param.11), channel_id=1, source_target_pairs={{0,1},{1,0},{2,3},{3,2},{4,5},{5,4},{6,7},{7,6},{8,9},{9,8},{10,11... | collective-permute-start | bytes 983048 | tf_op jit(solution)/shard_map/ppermute | solution.py:211
  17.4 1.6 collective-permute-start.2
  30.0 22.2 %collective-permute-start.3 = (bf16[256,1664]{1,0:T(8,128)(2,1)S(1)}, bf16[256,1664]{1,0:T(8,128)(2,1)S(1)}, u32[]{:S(2)}, u32[]{:S(2)}) collective-permute-start(bf16[256,1664]{1,0:T(8,128)(2,1)S(1)} %shard_map.109.after_ref), channel_id=1, source_target_pairs={{0,4},{12,8},{1,5},{13,9},{2,6},{14,10},{3,7},{15,11},{16,20},{28,... | collective-permute-start | bytes 2555912 | tf_op jit(solution)/shard_map/ppermute | solution.py:222
  40.1 0.9 copy-start.4
  41.0 17.9 %copy-start.19 = (s32[256]{0:T(256)S(1)}, s32[256]{0:T(256)}, u32[]{:S(2)}) copy-start(s32[256]{0:T(256)} %param.12) | copy-start | bytes 3076
  41.0 17.9 %copy-start.20 = (s32[4]{0:T(128)S(1)}, s32[4]{0:T(128)}, u32[]{:S(2)}) copy-start(s32[4]{0:T(128)} %param.13) | copy-start | bytes 52
  41.0 18.7 %copy-start.13 = (f32[6144]{0:T(1024)S(1)}, f32[6144]{0:T(1024)}, u32[]{:S(2)}) copy-start(f32[6144]{0:T(1024)} %param.15) | copy-start | bytes 73732
  53.3 7.0 %copy-start.2 = (bf16[256,1664]{1,0:T(8,128)(2,1)S(1)}, bf16[256,1664]{1,0:T(8,128)(2,1)}, u32[]{:S(2)}) copy-start(bf16[256,1664]{1,0:T(8,128)(2,1)} %add_convert_fusion.after_ref) | copy-start | bytes 2555908
  53.4 52.4 %all-gather.11.cloned.1.call-start = ((), (), s32[]{:S(2)}) async-start(), calls=%async_computation.1 | async-start | bytes 2359296 | tf_op jit(solution)/shard_map/all_gather | solution.py:225
  53.4 21.1 %collective-permute-start.4 = (bf16[256,1536]{1,0:T(8,128)(2,1)}, bf16[256,1536]{1,0:T(8,128)(2,1)}, u32[]{:S(2)}, u32[]{:S(2)}) collective-permute-start(bf16[256,1536]{1,0:T(8,128)(2,1)} %copy-done.4), channel_id=1, source_target_pairs={{0,4},{12,8},{1,5},{13,9},{2,6},{14,10},{3,7},{15,11},{16,20},{28,... | collective-permute-start | bytes 2359304 | tf_op jit(solution)/shard_map/ppermute | solution.py:222
  60.3 14.2 %copy-start.5 = (bf16[256,1536]{1,0:T(8,128)(2,1)S(1)}, bf16[256,1536]{1,0:T(8,128)(2,1)}, u32[]{:S(2)}) copy-start(bf16[256,1536]{1,0:T(8,128)(2,1)} %copy-done.4) | copy-start | bytes 2359300
  66.9 0.9 copy-start.6
  74.5 1.4 copy-start.7
  75.9 12.4 %copy-start.3 = (bf16[256,1536]{1,0:T(8,128)(2,1)}, bf16[256,1536]{1,0:T(8,128)(2,1)S(1)}, u32[]{:S(2)}) copy-start(bf16[256,1536]{1,0:T(8,128)(2,1)S(1)} %add_convert_fusion.3.after_ref) | copy-start | bytes 2359300
  75.9 19.7 %collective-permute-start.6 = (bf16[256,1536]{1,0:T(8,128)(2,1)S(1)}, bf16[256,1536]{1,0:T(8,128)(2,1)}, u32[]{:S(2)}, u32[]{:S(2)}) collective-permute-start(bf16[256,1536]{1,0:T(8,128)(2,1)S(1)} %copy-done.7), channel_id=1, source_target_pairs={{0,4},{12,8},{1,5},{13,9},{2,6},{14,10},{3,7},{15,11},{16,20},{28,... | collective-permute-start | bytes 2359304 | tf_op jit(solution)/shard_map/ppermute | solution.py:222
  88.4 41.4 %all-gather.15.cloned.1.call-start = ((), (), s32[]{:S(2)}) async-start(), calls=%async_computation.3 | async-start | bytes 2359296 | tf_op jit(solution)/shard_map/all_gather | solution.py:225
  90.1 1.8 copy-start.18
  97.9 61.8 %all-gather.13.cloned.1.call-start = ((), (), s32[]{:S(2)}) async-start(), calls=%async_computation.2 | async-start | bytes 2359296 | tf_op jit(solution)/shard_map/all_gather | solution.py:225
  98.0 19.4 %collective-permute-start.5 = (bf16[256,1536]{1,0:T(8,128)(2,1)}, bf16[256,1536]{1,0:T(8,128)(2,1)}, u32[]{:S(2)}, u32[]{:S(2)}) collective-permute-start(bf16[256,1536]{1,0:T(8,128)(2,1)} %fusion.4.h_ref), channel_id=1, source_target_pairs={{4,0},{8,12},{5,1},{9,13},{6,2},{10,14},{7,3},{11,15},{20,16},{24,... | collective-permute-start | bytes 2359304 | tf_op jit(solution)/shard_map/ppermute | solution.py:232
  99.3 26.7 %collective-permute-start.7 = (bf16[256,1536]{1,0:T(8,128)(2,1)}, bf16[256,1536]{1,0:T(8,128)(2,1)}, u32[]{:S(2)}, u32[]{:S(2)}) collective-permute-start(bf16[256,1536]{1,0:T(8,128)(2,1)} %shard_map.112), channel_id=1, source_target_pairs={{0,4},{12,8},{1,5},{13,9},{2,6},{14,10},{3,7},{15,11},{16,20},{28,... | collective-permute-start | bytes 2359304 | tf_op jit(solution)/shard_map/ppermute | solution.py:222
  105.7 1.8 copy-start.17
  107.6 9.8 %copy-start.1 = (bf16[6144,128]{1,0:T(8,128)(2,1)S(1)}, bf16[6144,128]{1,0:T(8,128)(2,1)}, u32[]{:S(2)}) copy-start(bf16[6144,128]{1,0:T(8,128)(2,1)} %d_ref.9) | copy-start | bytes 4718596
  124.5 1.5 copy-start.8
  128.5 22.8 %collective-permute-start.8 = (bf16[256,1536]{1,0:T(8,128)(2,1)S(1)}, bf16[256,1536]{1,0:T(8,128)(2,1)}, u32[]{:S(2)}, u32[]{:S(2)}) collective-permute-start(bf16[256,1536]{1,0:T(8,128)(2,1)S(1)} %fusion.9.acc_ref.low_ref.after_ref.h_ref), channel_id=1, source_target_pairs={{4,0},{8,12},{5,1},{9,13},{6,2},{10,14},{7,3},{11,15},{20,16},{24,... | collective-permute-start | bytes 2359304 | tf_op jit(solution)/shard_map/ppermute | solution.py:232
  129.8 1.8 copy-start.16
  131.6 19.6 %copy-start.9 = (f32[256,2560]{1,0:T(8,128)S(1)}, f32[256,2560]{1,0:T(8,128)}, u32[]{:S(2)}) copy-start(f32[256,2560]{1,0:T(8,128)} %copy-done.8) | copy-start | bytes 7864324
  134.5 34.6 %collective-permute-start.10 = (bf16[256,1536]{1,0:T(8,128)(2,1)}, bf16[256,1536]{1,0:T(8,128)(2,1)}, u32[]{:S(2)}, u32[]{:S(2)}) collective-permute-start(bf16[256,1536]{1,0:T(8,128)(2,1)} %fusion.14.after_ref.h_ref), channel_id=1, source_target_pairs={{4,0},{8,12},{5,1},{9,13},{6,2},{10,14},{7,3},{11,15},{20,16},{24,... | collective-permute-start | bytes 2359304 | tf_op jit(solution)/shard_map/ppermute | solution.py:232
  158.2 1.6 copy-start.10
  159.7 1.8 copy-start.15
  161.6 7.5 %copy-start.11 = (f32[256,2560]{1,0:T(8,128)S(1)}, f32[256,2560]{1,0:T(8,128)}, u32[]{:S(2)}) copy-start(f32[256,2560]{1,0:T(8,128)} %copy-done.10) | copy-start | bytes 7864324
  163.5 32.0 %collective-permute-start.9 = (bf16[256,1536]{1,0:T(8,128)(2,1)S(1)}, bf16[256,1536]{1,0:T(8,128)(2,1)S(1)}, u32[]{:S(2)}, u32[]{:S(2)}) collective-permute-start(bf16[256,1536]{1,0:T(8,128)(2,1)S(1)} %fusion.19.after_ref.h_ref), channel_id=1, source_target_pairs={{4,0},{8,12},{5,1},{9,13},{6,2},{10,14},{7,3},{11,15},{20,16},{24,... | collective-permute-start | bytes 2359304 | tf_op jit(solution)/shard_map/ppermute | solution.py:232
  202.6 2.2 collective-permute-start.11
  204.9 10.3 %copy-start.14 = (f32[2560]{0:T(1024)S(1)}, f32[2560]{0:T(1024)}, u32[]{:S(2)}) copy-start(f32[2560]{0:T(1024)} %param.19) | copy-start | bytes 30724
  205.0 10.2 %collective-permute-start.12 = (bf16[64,2688]{1,0:T(8,128)(2,1)S(1)}, bf16[64,2688]{1,0:T(8,128)(2,1)S(1)}, u32[]{:S(2)}, u32[]{:S(2)}) collective-permute-start(bf16[64,2688]{1,0:T(8,128)(2,1)S(1)} %slice.221), channel_id=1, source_target_pairs={{0,2},{1,3},{2,0},{3,1},{4,6},{5,7},{6,4},{7,5},{8,10},{9,11},{10,... | collective-permute-start | bytes 1032200 | tf_op jit(solution)/shard_map/ppermute | solution.py:211
Sparse Core Ops, SparseCore 0:
  53.5 11.1 all-gather.8
  88.5 9.9 all-gather.10
  100.0 26.2 all-gather.14
  128.6 25.4 all-gather.12

commit v4 on v1

v4 whole, which is shorter than its diff:
```python
import functools

import jax
import jax.numpy as jnp
import numpy as np
from jax import lax
from jax.experimental import pallas as pl
from jax.experimental.pallas import tpu as pltpu
from jax.sharding import PartitionSpec as P

ADAPTER_RANK = 16
ADAPTER_COUNT = 8
JOBS = 4
LANES = 128
AHEAD = 2
SHARES = (6, 8, 8, 8, 8, 6, 4)
PER_CALL = 2
F32 = jnp.float32
BF16 = jnp.bfloat16
ANY = pl.BlockSpec(memory_space=pl.ANY)
COST = pl.CostEstimate(flops=1000, bytes_accessed=1000, transcendentals=0)
PARAMS = pltpu.CompilerParams(vmem_limit_bytes=34 << 20)


def gelu_tanh(values):
    return (
        0.5
        * values
        * (1.0 + jnp.tanh(0.7978845608 * (values + 0.044715 * values * values * values)))
    )


def token_mask(token_job_index, job_adapter_index):
    one_hot = token_job_index[:, None] == jnp.arange(JOBS, dtype=jnp.int32)[None, :]
    chosen = jnp.sum(jnp.where(one_hot, job_adapter_index[None, :], 0), axis=1)
    slot_ids = jnp.arange(ADAPTER_COUNT * ADAPTER_RANK, dtype=jnp.int32) // ADAPTER_RANK
    return slot_ids[None, :] == chosen[:, None]


def dot(left, right):
    return jnp.dot(left, right, preferred_element_type=F32)


def tiles_of(width, most):
    tiles, start = [], 0
    while start < width:
        size = min(most, width - start)
        tiles.append((start, size))
        start += size
    return tiles


def chunk_spans(hidden):
    units = hidden // LANES
    cuts = [round(units * part / sum(SHARES)) for part in np.cumsum((0,) + SHARES)]
    return [(lo * LANES, (hi - lo) * LANES) for lo, hi in zip(cuts, cuts[1:]) if hi > lo]


def first_kernel(*refs, start, tiles, low):
    x_hbm, w_hbm = refs[:2]
    d_hbm = refs[2] if low else None
    out_hbm, x_v, w_v, d_v, o_v, x_sem, w_sem, d_sem, o_sem = refs[-9:]
    width = tiles[-1][0] + tiles[-1][1]
    x_copy = pltpu.make_async_copy(x_hbm, x_v, x_sem)
    w_copies = [
        pltpu.make_async_copy(
            w_hbm.at[:, pl.ds(start + at, size)], w_v.at[:, pl.ds(at, size)], w_sem.at[i]
        )
        for i, (at, size) in enumerate(tiles)
    ]
    w_copies[0].start()
    x_copy.start()
    for copy in w_copies[1:]:
        copy.start()
    sent = []

    def finish(at, size, right, sem):
        o_v[:, pl.ds(at, size)] = dot(x_v[...], right).astype(BF16)
        copy = pltpu.make_async_copy(o_v.at[:, pl.ds(at, size)], out_hbm.at[:, pl.ds(at, size)], sem)
        copy.start()
        sent.append(copy)

    if low:
        d_copy = pltpu.make_async_copy(d_hbm, d_v, d_sem)
        d_copy.start()
    x_copy.wait()
    for i, (at, size) in enumerate(tiles):
        w_copies[i].wait()
        finish(at, size, w_v[:, pl.ds(at, size)], o_sem.at[i])
    if low:
        d_copy.wait()
        finish(width, LANES, d_v[...], o_sem.at[len(tiles)])
    for copy in sent:
        copy.wait()


def first_product(x, weight, down, span, after):
    start, width = span
    rows, depth = x.shape
    low = down is not None
    tiles = tiles_of(width, 256)
    total = width + (LANES if low else 0)
    operands = [x, weight] + ([down] if low else []) + [after]
    return pl.pallas_call(
        functools.partial(first_kernel, start=start, tiles=tiles, low=low),
        in_specs=[ANY] * len(operands),
        out_specs=ANY,
        out_shape=jax.ShapeDtypeStruct((rows, total), BF16),
        scratch_shapes=[
            pltpu.VMEM((rows, depth), BF16),
            pltpu.VMEM((depth, width), BF16),
            pltpu.VMEM((depth if low else 16, LANES), BF16),
            pltpu.VMEM((rows, total), BF16),
            pltpu.SemaphoreType.DMA,
            pltpu.SemaphoreType.DMA((len(tiles),)),
            pltpu.SemaphoreType.DMA,
            pltpu.SemaphoreType.DMA((len(tiles) + 1,)),
        ],
        compiler_params=PARAMS,
        cost_estimate=COST,
    )(*operands)


def tie(value, after):
    return lax.optimization_barrier((value, after))[0]


def add_rounded(a, b, after):
    return (tie(a, after).astype(F32) + b.astype(F32)).astype(BF16)


def gelu_chunk(ours, theirs, low_in, up_maps, bias, span, after):
    start, width = span
    part = slice(start, start + width)
    summed = tie(ours, after)[:, :width].astype(F32) + theirs[:, :width].astype(F32)
    before = summed + bias[:, part] + dot(low_in, up_maps[:, part])
    return gelu_tanh(before).astype(BF16)


def second_kernel(*refs, count, widths, start, tiles, first):
    end_ref = refs[0]
    own_refs = refs[1 : 1 + count]
    come_refs = refs[1 + count : 1 + 2 * count]
    w_hbm, d_hbm = refs[1 + 2 * count : 3 + 2 * count]
    acc_hbm, low_hbm = (None, None) if first else refs[3 + 2 * count : 5 + 2 * count]
    (out_hbm, low_out_hbm, state, w_v, d_v, acc_v, low_v,
     s_sem, w_sem, d_sem, a_sem, l_sem, o_sem) = refs[-13:]
    depth = sum(widths)
    w_copies = [
        pltpu.make_async_copy(
            w_hbm.at[pl.ds(start, depth), pl.ds(at, size)], w_v.at[:, pl.ds(at, size)], w_sem.at[i]
        )
        for i, (at, size) in enumerate(tiles)
    ]
    w_copies[0].start()

    def load_states(sources):
        copies, at = [], 0
        for i, source in enumerate(sources):
            copy = pltpu.make_async_copy(source, state.at[:, pl.ds(at, widths[i])], s_sem.at[i])
            copy.start()
            copies.append(copy)
            at += widths[i]
        for copy in copies:
            copy.wait()

    for copy in w_copies[1:]:
        copy.start()
    d_copy = pltpu.make_async_copy(d_hbm.at[pl.ds(start, depth), :], d_v, d_sem)
    d_copy.start()
    if not first:
        a_copies = [
            pltpu.make_async_copy(acc_hbm.at[:, pl.ds(at, size)], acc_v.at[:, pl.ds(at, size)], a_sem.at[i])
            for i, (at, size) in enumerate(tiles)
        ]
        l_copy = pltpu.make_async_copy(low_hbm, low_v, l_sem)
        for copy in a_copies:
            copy.start()
        l_copy.start()

    @pl.when(end_ref[0] == 1)
    def _():
        load_states(come_refs)

    @pl.when(end_ref[0] == 0)
    def _():
        load_states(own_refs)

    sent = []
    for i, (at, size) in enumerate(tiles):
        part = pl.ds(at, size)
        w_copies[i].wait()
        if first:
            acc_v[:, part] = dot(state[...], w_v[:, part])
        else:
            a_copies[i].wait()
            acc_v[:, part] += dot(state[...], w_v[:, part])
        copy = pltpu.make_async_copy(acc_v.at[:, part], out_hbm.at[:, part], o_sem.at[i])
        copy.start()
        sent.append(copy)
    d_copy.wait()
    if first:
        low_v[...] = dot(state[...], d_v[...])
    else:
        l_copy.wait()
        low_v[...] += dot(state[...], d_v[...])
    copy = pltpu.make_async_copy(low_v, low_out_hbm, o_sem.at[len(tiles)])
    copy.start()
    sent.append(copy)
    for copy in sent:
        copy.wait()


def second_product(is_end, own, come, weight, down, total, low_total, start, after):
    rows = own[0].shape[0]
    widths = [h.shape[1] for h in own]
    depth = sum(widths)
    out_width = weight.shape[1]
    tiles = tiles_of(out_width, 512)
    first = total is None
    operands = [*own, *come, weight, down] + ([] if first else [total, low_total]) + [after]
    return pl.pallas_call(
        functools.partial(
            second_kernel, count=len(own), widths=widths, start=start, tiles=tiles, first=first
        ),
        in_specs=[pl.BlockSpec(memory_space=pltpu.SMEM)] + [ANY] * len(operands),
        out_specs=[ANY, ANY],
        out_shape=[
            jax.ShapeDtypeStruct((rows, out_width), F32),
            jax.ShapeDtypeStruct((rows, LANES), F32),
        ],
        scratch_shapes=[
            pltpu.VMEM((rows, depth), BF16),
            pltpu.VMEM((depth, out_width), BF16),
            pltpu.VMEM((depth, LANES), BF16),
            pltpu.VMEM((rows, out_width), F32),
            pltpu.VMEM((rows, LANES), F32),
            pltpu.SemaphoreType.DMA((len(own),)),
            pltpu.SemaphoreType.DMA((len(tiles),)),
            pltpu.SemaphoreType.DMA,
            pltpu.SemaphoreType.DMA((len(tiles),)),
            pltpu.SemaphoreType.DMA,
            pltpu.SemaphoreType.DMA((len(tiles) + 1,)),
        ],
        compiler_params=PARAMS,
        cost_estimate=COST,
    )(is_end, *operands)


def make_local(n_group, n_row, n_col):
    chips = n_col // 2
    half = n_row // 2

    def place_of(group, row, col):
        return (group * n_row + row) * n_col + col

    cross_pairs = []
    for group in range(n_group):
        for row in range(n_row):
            for col in range(n_col):
                if row in (half - 1, half):
                    other = place_of(group, n_row - 1 - row, col)
                else:
                    other = place_of(group, row, col ^ 1)
                cross_pairs.append((place_of(group, row, col), other))

    def col_swap(value, flip):
        return lax.ppermute(value, "col", [(i, i ^ flip) for i in range(n_col)])

    def gather_tokens(tokens):
        shards = [tokens, col_swap(tokens, 1)]
        for step in range(1, chips):
            far = col_swap(tokens, 2 * step)
            shards += [far, col_swap(far, 1)]
        return jnp.concatenate(shards, axis=0)

    def fold(value, step):
        pairs = [(step, step + 1), (n_row - 1 - step, n_row - 2 - step)]
        return lax.ppermute(value, "row", pairs)

    def cross(value):
        return lax.ppermute(value, ("group", "row", "col"), cross_pairs)

    def spread(value, place):
        for step in reversed(range(half - 1)):
            pairs = [(step + 1, step), (n_row - 2 - step, n_row - 1 - step)]
            come = lax.ppermute(value, "row", pairs)
            if step > 0:
                value = jnp.where((place <= step) | (place >= n_row - 1 - step), come, value)
            else:
                value = come
        return value

    def local(
        tokens,
        token_job_index,
        job_adapter_index,
        first_weight,
        first_bias,
        first_down_maps,
        first_up_maps,
        second_weight,
        second_bias,
        second_down_maps,
        second_up_maps,
    ):
        rows = tokens.shape[0]
        hidden = first_weight.shape[1]
        out_width = second_weight.shape[1]
        spans = chunk_spans(hidden)
        count = len(spans)
        place = lax.axis_index("row")
        mine = lax.axis_index("col")
        edge = (place == 0) | (place == n_row - 1)
        is_end = edge.astype(jnp.int32).reshape(1)
        bias = first_bias[None, :]
        mask_all = token_mask(token_job_index, job_adapter_index)
        mask = jnp.concatenate(
            [
                lax.dynamic_slice_in_dim(mask_all, (mine ^ i) * rows, rows, 0)
                for i in range(n_col)
            ],
            axis=0,
        )
        gathered = gather_tokens(tokens)
        last = gathered
        partials, folded, sums, crossed, states, returned = {}, {}, {}, {}, {}, {}
        total, low_total, low_in = None, None, None
        ready = []

        def start_chunk(t):
            nonlocal last
            down = first_down_maps if t == 0 else None
            last = first_product(gathered, first_weight, down, spans[t], last)
            partials[t] = last
            folded[t] = fold(last, 0)

        for t in range(min(AHEAD, count)):
            start_chunk(t)
        for t in range(count + 2):
            if t < count:
                value = add_rounded(partials[t], folded[t], last)
                for step in range(1, half - 1):
                    value = add_rounded(value, fold(value, step), value)
                last = value
                sums[t] = value
                crossed[t] = cross(value)
            if t + AHEAD < count:
                start_chunk(t + AHEAD)
            if 0 <= t - 1 < count:
                k = t - 1
                width = spans[k][1]
                if k == 0:
                    low = sums[k][:, width:].astype(F32) + crossed[k][:, width:].astype(F32)
                    low_in = jnp.where(mask, low, 0.0).astype(BF16)
                last = gelu_chunk(sums[k], crossed[k], low_in, first_up_maps, bias, spans[k], last)
                states[k] = last
                returned[k] = spread(last, place)
            if 0 <= t - 2 < count:
                ready.append(t - 2)
                if len(ready) == PER_CALL or t - 2 == count - 1:
                    total, low_total = second_product(
                        is_end, [states[k] for k in ready], [returned[k] for k in ready],
                        second_weight, second_down_maps, total, low_total, spans[ready[0]][0], last,
                    )
                    last = low_total
                    ready = []
        outputs = jnp.concatenate([total, low_total], axis=1)
        blocks = [outputs[i * rows : (i + 1) * rows] for i in range(n_col)]
        ours = jnp.concatenate(blocks[0::2], axis=0)
        theirs = jnp.concatenate(blocks[1::2], axis=0).astype(BF16)
        ours = ours + col_swap(theirs, 1).astype(F32)
        result = ours[:rows]
        for step in range(1, chips):
            piece = ours[step * rows : (step + 1) * rows].astype(BF16)
            result = result + col_swap(piece, 2 * step).astype(F32)
        low_out = jnp.where(mask[:rows], result[:, out_width:], 0.0).astype(BF16)
        layer_output = result[:, :out_width] + second_bias[None, :] + dot(low_out, second_up_maps)
        return layer_output.astype(BF16)

    return local


def solution(mesh):
    shape = mesh.shape
    return jax.shard_map(
        make_local(shape["group"], shape["row"], shape["col"]),
        mesh=mesh,
        in_specs=(
            P(("group", "col"), "row"),
            P("group"),
            P("group"),
            P("row", "col"),
            P("col"),
            P("row", None),
            P(None, "col"),
            P("col", "row"),
            P("row"),
            P("col", None),
            P(None, "row"),
        ),
        out_specs=P(("group", "col"), "row"),
        check_vma=False,
    )
```

time: 260 us -> 178 us (0.68)
  waiting for transfers between devices: 156 us -> 52.7 us
  Pallas kernels: 0 us -> 54.6 us
  matrix products: 54.7 us -> 8.81 us
  starting transfers between devices: 43 us -> 49.9 us
  other arithmetic: 2.33 us -> 7.64 us
    ppermute x24 -> x21, waiting for transfers between devices: 138 us -> 34.3 us  [the longest x7 31.3 us: spread(): come = lax.ppermute(value, 'row', pairs)]
    pallas_call x0 -> x11, Pallas kernels: none -> 54.6 us  [the longest x7 31.3 us: first_product(): pl.pallas_call(functools.partial(first_kernel, start=start, tiles=tiles,...]
    dot_general x34 -> x8, matrix products: 54.7 us -> 8.81 us  [dot(): return jnp.dot(left, right, preferred_element_type=F32)]
    ppermute x24 -> x21, starting transfers between devices: 38.4 us -> 45.3 us  [the longest x7 35.5 us: fold(): return lax.ppermute(value, 'row', pairs)]
    convert_element_type x8, other arithmetic: 0.84 us -> 6.35 us  [the longest x7 6.32 us: add_rounded(): return (tie(a, after).astype(F32) + b.astype(F32)).astype(BF16)]
  transfers between devices with their start and end apart: 29 -> 26, of which waited for: 14 -> 9; matrix products, arithmetic and copies ran while one was open for 13% -> 10% of each run, Pallas kernels for 0% -> 26%
where the time goes in v4:
time: 178 us; the launch traced here: 177 us
  Pallas kernels  54.6 us (31%)
  waiting for transfers between devices  52.7 us (30%)
  starting transfers between devices  49.9 us (28%)
  matrix products  8.81 us (5%)
  other arithmetic  7.64 us (4%)
  local copies, waits for them, and re-layouts  2.84 us (2%)
    ppermute x7, starting transfers between devices, fold(): return lax.ppermute(value, 'row', pairs)  35.5 us
    ppermute x7, waiting for transfers between devices, spread(): come = lax.ppermute(value, 'row', pairs)  31.3 us
    pallas_call x7, Pallas kernels, first_product(): pl.pallas_call(functools.partial(first_kernel, start=start, tiles=tiles,...  31.3 us
    pallas_call x4, Pallas kernels, second_product(): pl.pallas_call(functools.partial(second_kernel, count=len(own), widths=wi...  23.3 us
    ppermute x5, waiting for transfers between devices, col_swap(): return lax.ppermute(value, 'col', [(i, i ^ flip) for i in range(n_col)])  18.4 us
    ppermute x7, starting transfers between devices, spread(): come = lax.ppermute(value, 'row', pairs)  9.37 us
    dot_general x8, matrix products, dot(): return jnp.dot(left, right, preferred_element_type=F32)  8.81 us
    convert_element_type x7, other arithmetic, add_rounded(): return (tie(a, after).astype(F32) + b.astype(F32)).astype(BF16)  6.32 us
  transfers between devices with their start and end apart: 26, of which 9 were waited for; matrix products, arithmetic and copies ran while one was open for 10% of the time, Pallas kernels for 26%

profile of v4, /device:TPU:0, one launch (start us, length us, event | category | flops | bytes accessed | tf_op | source)
XLA Modules:
  0.0 177.1 jit_solution(9565777325462225546)
XLA Ops:
  0.0 2.9 %collective-permute-start.1 = (bf16[64,2560]{1,0:T(8,128)(2,1)}, bf16[64,2560]{1,0:T(8,128)(2,1)S(1)}, u32[]{:S(2)}, u32[]{:S(2)}) collective-permute-start(bf16[64,2560]{1,0:T(8,128)(2,1)} %param.11), channel_id=1, source_target_pairs={{0,2},{1,3},{2,0},{3,1},{4,6},{5,7},{6,4},{7,5},{8,10},{9,11},{10,... | collective-permute-start | bytes 983048 | tf_op jit(solution)/shard_map/ppermute | solution.py:268
  2.9 0.8 select_reduce_fusion
  3.7 1.0 constant_dynamic-update-slice_fusion.3
  4.7 6.1 %collective-permute-done.1 = bf16[64,2560]{1,0:T(8,128)(2,1)S(1)} collective-permute-done((bf16[64,2560]{1,0:T(8,128)(2,1)}, bf16[64,2560]{1,0:T(8,128)(2,1)S(1)}, u32[]{:S(2)}, u32[]{:S(2)}) %collective-permute-start.1) | collective-permute-done | bytes 327712 | tf_op jit(solution)/shard_map/ppermute | solution.py:268
  10.9 1.6 collective-permute-done.2
  12.5 4.8 %shard_map.109.refs_2_ = bf16[256,896]{1,0:T(8,128)(2,1)S(1)} custom-call(bf16[256,2560]{1,0:T(8,128)(2,1)S(1)} %constant_dynamic-update-slice_fusion.refs_0_.refs_3_, bf16[2560,6144]{1,0:T(8,128)(2,1)} %refs_1_.13, bf16[2560,128]{1,0:T(8,128)(2,1)S(1)} %copy-done.3, bf16[256,2560]{1,0:T(8,128)(2,1)S(1)} %constant_dynamic-update-slice_fusion.refs_0_.refs_3_), custom_call_target="tpu_custom_call" | custom-call | flops 1000 | bytes 1000 | tf_op jit(solution)/shard_map/pallas_call | solution.py:104
  17.3 4.5 %collective-permute-start.3 = (bf16[256,896]{1,0:T(8,128)(2,1)S(1)}, bf16[256,896]{1,0:T(8,128)(2,1)}, u32[]{:S(2)}, u32[]{:S(2)}) collective-permute-start(bf16[256,896]{1,0:T(8,128)(2,1)S(1)} %shard_map.109.refs_2_), channel_id=1, source_target_pairs={{0,4},{12,8},{1,5},{13,9},{2,6},{14,10},{3,7},{15,11},{16,20},{28,... | collective-permute-start | bytes 1376264 | tf_op jit(solution)/shard_map/ppermute | solution.py:279
  21.8 0.1 broadcast_compare_fusion
  22.0 4.8 %shard_map.110 = bf16[256,1024]{1,0:T(8,128)(2,1)S(1)} custom-call(bf16[256,2560]{1,0:T(8,128)(2,1)S(1)} %constant_dynamic-update-slice_fusion.refs_0_.refs_3_, bf16[2560,6144]{1,0:T(8,128)(2,1)} %refs_1_.13, bf16[256,896]{1,0:T(8,128)(2,1)S(1)} %shard_map.109.refs_2_), custom_call_target="tpu_custom_call" | custom-call | flops 1000 | bytes 1000 | tf_op jit(solution)/shard_map/pallas_call | solution.py:104
  26.8 2.1 %collective-permute-start.4 = (bf16[256,1024]{1,0:T(8,128)(2,1)S(1)}, bf16[256,1024]{1,0:T(8,128)(2,1)}, u32[]{:S(2)}, u32[]{:S(2)}) collective-permute-start(bf16[256,1024]{1,0:T(8,128)(2,1)S(1)} %shard_map.110), channel_id=1, source_target_pairs={{0,4},{12,8},{1,5},{13,9},{2,6},{14,10},{3,7},{15,11},{16,20},{28,... | collective-permute-start | bytes 1572872 | tf_op jit(solution)/shard_map/ppermute | solution.py:279
  28.9 3.0 %collective-permute-done.3 = bf16[256,896]{1,0:T(8,128)(2,1)} collective-permute-done((bf16[256,896]{1,0:T(8,128)(2,1)S(1)}, bf16[256,896]{1,0:T(8,128)(2,1)}, u32[]{:S(2)}, u32[]{:S(2)}) %collective-permute-start.3) | collective-permute-done | bytes 458784 | tf_op jit(solution)/shard_map/ppermute | solution.py:279
  31.9 1.1 add_convert_fusion.4.refs_2_
  33.0 0.1 collective-permute-start.5
  33.1 0.6 fusion.62
  33.7 5.4 %shard_map.111 = bf16[256,1024]{1,0:T(8,128)(2,1)} custom-call(bf16[256,2560]{1,0:T(8,128)(2,1)S(1)} %constant_dynamic-update-slice_fusion.refs_0_.refs_3_, bf16[2560,6144]{1,0:T(8,128)(2,1)} %refs_1_.13, bf16[256,896]{1,0:T(8,128)(2,1)S(1)} %add_convert_fusion.4.refs_2_), custom_call_target="tpu_custom_call" | custom-call | flops 1000 | bytes 1000 | tf_op jit(solution)/shard_map/pallas_call | solution.py:104
  39.1 6.9 %collective-permute-start.6 = (bf16[256,1024]{1,0:T(8,128)(2,1)}, bf16[256,1024]{1,0:T(8,128)(2,1)}, u32[]{:S(2)}, u32[]{:S(2)}) collective-permute-start(bf16[256,1024]{1,0:T(8,128)(2,1)} %shard_map.111), channel_id=1, source_target_pairs={{0,4},{12,8},{1,5},{13,9},{2,6},{14,10},{3,7},{15,11},{16,20},{28,... | collective-permute-start | bytes 1572872 | tf_op jit(solution)/shard_map/ppermute | solution.py:279
  46.0 1.4 add_convert_fusion.3.refs_2_
  47.4 4.8 %shard_map.112 = bf16[256,1024]{1,0:T(8,128)(2,1)S(1)} custom-call(bf16[256,2560]{1,0:T(8,128)(2,1)S(1)} %constant_dynamic-update-slice_fusion.refs_0_.refs_3_, bf16[2560,6144]{1,0:T(8,128)(2,1)} %refs_1_.13, bf16[256,1024]{1,0:T(8,128)(2,1)S(1)} %add_convert_fusion.3.refs_2_), custom_call_target="tpu_custom_call" | custom-call | flops 1000 | bytes 1000 | tf_op jit(solution)/shard_map/pallas_call | solution.py:104
  52.2 0.1 collective-permute-start.7
  52.3 2.4 %collective-permute-start.10 = (bf16[256,1024]{1,0:T(8,128)(2,1)S(1)}, bf16[256,1024]{1,0:T(8,128)(2,1)S(1)}, u32[]{:S(2)}, u32[]{:S(2)}) collective-permute-start(bf16[256,1024]{1,0:T(8,128)(2,1)S(1)} %shard_map.112), channel_id=1, source_target_pairs={{0,4},{12,8},{1,5},{13,9},{2,6},{14,10},{3,7},{15,11},{16,20},{28,... | collective-permute-start | bytes 1572872 | tf_op jit(solution)/shard_map/ppermute | solution.py:279
  54.8 2.2 %fusion.24.refs_1_ = bf16[256,768]{1,0:T(8,128)(2,1)} fusion(bf16[256,896]{1,0:T(8,128)(2,1)S(1)} %collective-permute-done.5, f32[768]{0:T(1024)S(1)} %get-tuple-element.50, bf16[256,896]{1,0:T(8,128)(2,1)S(1)} %add_convert_fusion.4.refs_2_, bf16[256,128]{1,0:T(8,128)(2,1)S(1)} %select_convert_fusion, bf16[128,6144]{1,0:T(8,128)(2,1)} %param.17), kind=kOutput, calls=%fused_computation.36 | convolution fusion | flops 53084160 | bytes 1444864 | tf_op jit(solution)/shard_map/dot_general | solution.py:41
  57.0 2.2 %add_convert_fusion.2.refs_2_ = bf16[256,1024]{1,0:T(8,128)(2,1)} fusion(bf16[256,1024]{1,0:T(8,128)(2,1)} %collective-permute-done.6, bf16[256,1024]{1,0:T(8,128)(2,1)} %shard_map.111), kind=kLoop, calls=%fused_computation.29 | loop fusion | flops 1048576 | bytes 1572864 | tf_op jit(solution)/shard_map/convert_element_type | solution.py:129
  59.2 1.4 collective-permute-start.8
  60.6 4.8 %shard_map.113 = bf16[256,1024]{1,0:T(8,128)(2,1)S(1)} custom-call(bf16[256,2560]{1,0:T(8,128)(2,1)S(1)} %constant_dynamic-update-slice_fusion.refs_0_.refs_3_, bf16[2560,6144]{1,0:T(8,128)(2,1)} %refs_1_.13, bf16[256,1024]{1,0:T(8,128)(2,1)} %add_convert_fusion.2.refs_2_), custom_call_target="tpu_custom_call" | custom-call | flops 1000 | bytes 1000 | tf_op jit(solution)/shard_map/pallas_call | solution.py:104
  65.4 0.1 collective-permute-start.11
  65.5 6.5 %collective-permute-start.12 = (bf16[256,1024]{1,0:T(8,128)(2,1)S(1)}, bf16[256,1024]{1,0:T(8,128)(2,1)}, u32[]{:S(2)}, u32[]{:S(2)}) collective-permute-start(bf16[256,1024]{1,0:T(8,128)(2,1)S(1)} %shard_map.113), channel_id=1, source_target_pairs={{0,4},{12,8},{1,5},{13,9},{2,6},{14,10},{3,7},{15,11},{16,20},{28,... | collective-permute-start | bytes 1572872 | tf_op jit(solution)/shard_map/ppermute | solution.py:279
  72.0 1.6 fusion.4.refs_2_
  73.6 1.3 collective-permute-start.9
  74.9 0.2 add_convert_fusion.1.refs_2_
  75.2 3.7 %shard_map.114 = bf16[256,768]{1,0:T(8,128)(2,1)S(1)} custom-call(bf16[256,2560]{1,0:T(8,128)(2,1)S(1)} %constant_dynamic-update-slice_fusion.refs_0_.refs_3_, bf16[2560,6144]{1,0:T(8,128)(2,1)} %refs_1_.13, bf16[256,1024]{1,0:T(8,128)(2,1)S(1)} %add_convert_fusion.1.refs_2_), custom_call_target="tpu_custom_call" | custom-call | flops 1000 | bytes 1000 | tf_op jit(solution)/shard_map/pallas_call | solution.py:104
  78.9 0.1 collective-permute-start.13
  79.0 6.9 %collective-permute-start.16 = (bf16[256,768]{1,0:T(8,128)(2,1)S(1)}, bf16[256,768]{1,0:T(8,128)(2,1)S(1)}, u32[]{:S(2)}, u32[]{:S(2)}) collective-permute-start(bf16[256,768]{1,0:T(8,128)(2,1)S(1)} %shard_map.114), channel_id=1, source_target_pairs={{0,4},{12,8},{1,5},{13,9},{2,6},{14,10},{3,7},{15,11},{16,20},{28,... | collective-permute-start | bytes 1179656 | tf_op jit(solution)/shard_map/ppermute | solution.py:279
  85.9 1.9 %fusion.9.refs_7_.refs_1_ = bf16[256,1024]{1,0:T(8,128)(2,1)S(1)} fusion(bf16[256,1024]{1,0:T(8,128)(2,1)} %collective-permute-done.11, bf16[256,1024]{1,0:T(8,128)(2,1)} %add_convert_fusion.2.refs_2_, f32[1024]{0:T(1024)S(1)} %bitcast.20, bf16[256,128]{1,0:T(8,128)(2,1)S(1)} %copy-done.5, bf16[128,6144]{1,0:T(8,128)(2,1)S(1)} %copy-done.11), kind=kOutput, calls=%fused_computation.16 | convolution fusion | flops 70778880 | bytes 1904640 | tf_op jit(solution)/shard_map/dot_general | solution.py:41
  87.9 0.1 collective-permute-done.9.refs_4_
  88.0 8.2 %shard_map.115 = (f32[256,2560]{1,0:T(8,128)S(1)}, f32[256,128]{1,0:T(8,128)S(1)}) custom-call(s32[1]{0:T(128)} %bitcast.refs_0_, bf16[256,768]{1,0:T(8,128)(2,1)} %fusion.24.refs_1_, bf16[256,1024]{1,0:T(8,128)(2,1)S(1)} %fusion.4.refs_2_, bf16[256,768]{1,0:T(8,128)(2,1)} %collective-permute-done.8.refs_3_, ...), custom_call_target="tpu_custom_call" | custom-call | flops 1000 | bytes 1000 | tf_op jit(solution)/shard_map/pallas_call | solution.py:222
  96.2 1.2 add_convert_fusion.refs_2_
  97.4 1.3 collective-permute-start.14
  98.7 3.1 %shard_map.116 = bf16[256,512]{1,0:T(8,128)(2,1)S(1)} custom-call(bf16[256,2560]{1,0:T(8,128)(2,1)S(1)} %constant_dynamic-update-slice_fusion.refs_0_.refs_3_, bf16[2560,6144]{1,0:T(8,128)(2,1)} %refs_1_.13, bf16[256,1024]{1,0:T(8,128)(2,1)S(1)} %add_convert_fusion.refs_2_), custom_call_target="tpu_custom_call" | custom-call | flops 1000 | bytes 1000 | tf_op jit(solution)/shard_map/pallas_call | solution.py:104
  101.9 0.6 fusion.14.refs_2_
  102.5 1.3 collective-permute-start.15
  103.8 6.2 %collective-permute-start.18 = (bf16[256,512]{1,0:T(8,128)(2,1)S(1)}, bf16[256,512]{1,0:T(8,128)(2,1)S(1)}, u32[]{:S(2)}, u32[]{:S(2)}) collective-permute-start(bf16[256,512]{1,0:T(8,128)(2,1)S(1)} %shard_map.116), channel_id=1, source_target_pairs={{0,4},{12,8},{1,5},{13,9},{2,6},{14,10},{3,7},{15,11},{16,20},{28,... | collective-permute-start | bytes 786440 | tf_op jit(solution)/shard_map/ppermute | solution.py:279
  110.0 0.1 add_convert_fusion.5
  110.2 0.6 fusion.19.refs_9_.refs_1_
  110.8 3.2 %collective-permute-done.14.refs_3_ = bf16[256,1024]{1,0:T(8,128)(2,1)S(1)} collective-permute-done((bf16[256,1024]{1,0:T(8,128)(2,1)S(1)}, bf16[256,1024]{1,0:T(8,128)(2,1)S(1)}, u32[]{:S(2)}, u32[]{:S(2)}) %collective-permute-start.14) | collective-permute-done | bytes 524320 | tf_op jit(solution)/shard_map/ppermute | solution.py:287
  114.0 8.0 %collective-permute-done.15.refs_4_ = bf16[256,1024]{1,0:T(8,128)(2,1)S(1)} collective-permute-done((bf16[256,1024]{1,0:T(8,128)(2,1)S(1)}, bf16[256,1024]{1,0:T(8,128)(2,1)S(1)}, u32[]{:S(2)}, u32[]{:S(2)}) %collective-permute-start.15) | collective-permute-done | bytes 524320 | tf_op jit(solution)/shard_map/ppermute | solution.py:287
  122.0 6.1 %shard_map.117 = (f32[256,2560]{1,0:T(8,128)S(1)}, f32[256,128]{1,0:T(8,128)S(1)}) custom-call(s32[1]{0:T(128)} %bitcast.refs_0_, bf16[256,1024]{1,0:T(8,128)(2,1)S(1)} %fusion.9.refs_7_.refs_1_, bf16[256,1024]{1,0:T(8,128)(2,1)S(1)} %fusion.14.refs_2_, bf16[256,1024]{1,0:T(8,128)(2,1)S(1)} %collective-permute-done.14.refs_3_, ...), custom_call_target="tpu_custom_call" | custom-call | flops 1000 | bytes 1000 | tf_op jit(solution)/shard_map/pallas_call | solution.py:222
  128.3 0.7 slice.116
  128.9 1.3 collective-permute-start.22
  130.2 0.5 fusion.29.refs_2_
  130.7 1.3 collective-permute-start.23
  132.1 0.4 fusion.36.refs_9_.refs_1_
  132.4 1.5 collective-permute-start.21
  134.0 20.0 %collective-permute-done.23.refs_4_ = bf16[256,768]{1,0:T(8,128)(2,1)S(1)} collective-permute-done((bf16[256,768]{1,0:T(8,128)(2,1)S(1)}, bf16[256,768]{1,0:T(8,128)(2,1)S(1)}, u32[]{:S(2)}, u32[]{:S(2)}) %collective-permute-start.23) | collective-permute-done | bytes 393248 | tf_op jit(solution)/shard_map/ppermute | solution.py:287
  154.0 5.7 %shard_map.118 = (f32[256,2560]{1,0:T(8,128)S(1)}, f32[256,128]{1,0:T(8,128)S(1)}) custom-call(s32[1]{0:T(128)} %bitcast.refs_0_, bf16[256,1024]{1,0:T(8,128)(2,1)S(1)} %fusion.19.refs_9_.refs_1_, bf16[256,768]{1,0:T(8,128)(2,1)S(1)} %fusion.29.refs_2_, bf16[256,1024]{1,0:T(8,128)(2,1)S(1)} %collective-permute-done.22.refs_3_, ...), custom_call_target="tpu_custom_call" | custom-call | flops 1000 | bytes 1000 | tf_op jit(solution)/shard_map/pallas_call | solution.py:222
  159.7 3.3 %shard_map.119 = (f32[256,2560]{1,0:T(8,128)S(1)}, f32[256,128]{1,0:T(8,128)S(1)}) custom-call(s32[1]{0:T(128)} %bitcast.refs_0_, bf16[256,512]{1,0:T(8,128)(2,1)S(1)} %fusion.36.refs_9_.refs_1_, bf16[256,512]{1,0:T(8,128)(2,1)S(1)} %collective-permute-done.21.refs_2_, bf16[6144,2560]{1,0:T(8,128)(2,1)} %refs_3_.1, bf16[6144,128]{1,0:T(8,128)(2,1)S(1)} %copy-done.1, ...), custom_call_target="tpu_custom_call" | custom-call | flops 1000 | bytes 1000 | tf_op jit(solution)/shard_map/pallas_call | solution.py:222
  163.0 0.2 constant_dynamic-update-slice_fusion.5
  163.2 0.1 convert.10
  163.5 0.1 fusion.60
  163.6 2.0 %collective-permute-done.24 = bf16[128,2688]{1,0:T(8,128)(2,1)S(1)} collective-permute-done((bf16[128,2688]{1,0:T(8,128)(2,1)S(1)}, bf16[128,2688]{1,0:T(8,128)(2,1)S(1)}, u32[]{:S(2)}, u32[]{:S(2)}) %collective-permute-start.24) | collective-permute-done | bytes 688160 | tf_op jit(solution)/shard_map/ppermute | solution.py:268
  165.7 0.1 maximum_add_fusion
  165.9 1.5 collective-permute-start.25
  167.4 8.6 %collective-permute-done.25 = bf16[64,2688]{1,0:T(8,128)(2,1)S(1)} collective-permute-done((bf16[64,2688]{1,0:T(8,128)(2,1)S(1)}, bf16[64,2688]{1,0:T(8,128)(2,1)S(1)}, u32[]{:S(2)}, u32[]{:S(2)}) %collective-permute-start.25) | collective-permute-done | bytes 344096 | tf_op jit(solution)/shard_map/ppermute | solution.py:268
  176.1 0.1 slice_add_fusion
  176.1 1.0 fusion.31
  (59 shorter events, 0.8 us)
Async XLA Ops:
  0.0 176.1 %copy-start = (bf16[128,2560]{1,0:T(8,128)(2,1)S(1)}, bf16[128,2560]{1,0:T(8,128)(2,1)}, u32[]{:S(2)}) copy-start(bf16[128,2560]{1,0:T(8,128)(2,1)} %param.21) | copy-start | bytes 1966084
  0.0 12.5 %copy-start.3 = (bf16[2560,128]{1,0:T(8,128)(2,1)S(1)}, bf16[2560,128]{1,0:T(8,128)(2,1)}, u32[]{:S(2)}) copy-start(bf16[2560,128]{1,0:T(8,128)(2,1)} %refs_2_.1) | copy-start | bytes 1966084
  0.0 10.9 %collective-permute-start.1 = (bf16[64,2560]{1,0:T(8,128)(2,1)}, bf16[64,2560]{1,0:T(8,128)(2,1)S(1)}, u32[]{:S(2)}, u32[]{:S(2)}) collective-permute-start(bf16[64,2560]{1,0:T(8,128)(2,1)} %param.11), channel_id=1, source_target_pairs={{0,2},{1,3},{2,0},{3,1},{4,6},{5,7},{6,4},{7,5},{8,10},{9,11},{10,... | collective-permute-start | bytes 983048 | tf_op jit(solution)/shard_map/ppermute | solution.py:268
  2.9 7.9 %collective-permute-start = (bf16[64,2560]{1,0:T(8,128)(2,1)}, bf16[64,2560]{1,0:T(8,128)(2,1)S(1)}, u32[]{:S(2)}, u32[]{:S(2)}) collective-permute-start(bf16[64,2560]{1,0:T(8,128)(2,1)} %param.11), channel_id=1, source_target_pairs={{0,1},{1,0},{2,3},{3,2},{4,5},{5,4},{6,7},{7,6},{8,9},{9,8},{10,11... | collective-permute-start | bytes 983048 | tf_op jit(solution)/shard_map/ppermute | solution.py:268
  10.9 1.6 collective-permute-start.2
  17.3 14.6 %collective-permute-start.3 = (bf16[256,896]{1,0:T(8,128)(2,1)S(1)}, bf16[256,896]{1,0:T(8,128)(2,1)}, u32[]{:S(2)}, u32[]{:S(2)}) collective-permute-start(bf16[256,896]{1,0:T(8,128)(2,1)S(1)} %shard_map.109.refs_2_), channel_id=1, source_target_pairs={{0,4},{12,8},{1,5},{13,9},{2,6},{14,10},{3,7},{15,11},{16,20},{28,... | collective-permute-start | bytes 1376264 | tf_op jit(solution)/shard_map/ppermute | solution.py:279
  21.9 6.9 %copy-start.6 = (f32[6144]{0:T(1024)S(1)}, f32[6144]{0:T(1024)}, u32[]{:S(2)}) copy-start(f32[6144]{0:T(1024)} %param.15) | copy-start | bytes 73732
  26.8 12.3 %copy-start.2 = (bf16[256,1024]{1,0:T(8,128)(2,1)}, bf16[256,1024]{1,0:T(8,128)(2,1)S(1)}, u32[]{:S(2)}) copy-start(bf16[256,1024]{1,0:T(8,128)(2,1)S(1)} %shard_map.110) | copy-start | bytes 1572868
  26.8 19.2 %collective-permute-start.4 = (bf16[256,1024]{1,0:T(8,128)(2,1)S(1)}, bf16[256,1024]{1,0:T(8,128)(2,1)}, u32[]{:S(2)}, u32[]{:S(2)}) collective-permute-start(bf16[256,1024]{1,0:T(8,128)(2,1)S(1)} %shard_map.110), channel_id=1, source_target_pairs={{0,4},{12,8},{1,5},{13,9},{2,6},{14,10},{3,7},{15,11},{16,20},{28,... | collective-permute-start | bytes 1572872 | tf_op jit(solution)/shard_map/ppermute | solution.py:279
  33.0 21.7 %collective-permute-start.5 = (bf16[256,896]{1,0:T(8,128)(2,1)S(1)}, bf16[256,896]{1,0:T(8,128)(2,1)S(1)}, u32[]{:S(2)}, u32[]{:S(2)}) collective-permute-start(bf16[256,896]{1,0:T(8,128)(2,1)S(1)} %add_convert_fusion.4.refs_2_), channel_id=1, source_target_pairs={{0,1},{1,0},{2,3},{3,2},{4,8},{5,9},{6,10},{7,11},{8,4},{9,5},{10,... | collective-permute-start | bytes 1376264 | tf_op jit(solution)/shard_map/ppermute | solution.py:282
  39.1 17.9 %collective-permute-start.6 = (bf16[256,1024]{1,0:T(8,128)(2,1)}, bf16[256,1024]{1,0:T(8,128)(2,1)}, u32[]{:S(2)}, u32[]{:S(2)}) collective-permute-start(bf16[256,1024]{1,0:T(8,128)(2,1)} %shard_map.111), channel_id=1, source_target_pairs={{0,4},{12,8},{1,5},{13,9},{2,6},{14,10},{3,7},{15,11},{16,20},{28,... | collective-permute-start | bytes 1572872 | tf_op jit(solution)/shard_map/ppermute | solution.py:279
  52.2 19.8 %collective-permute-start.7 = (bf16[256,1024]{1,0:T(8,128)(2,1)S(1)}, bf16[256,1024]{1,0:T(8,128)(2,1)S(1)}, u32[]{:S(2)}, u32[]{:S(2)}) collective-permute-start(bf16[256,1024]{1,0:T(8,128)(2,1)S(1)} %add_convert_fusion.3.refs_2_), channel_id=1, source_target_pairs={{0,1},{1,0},{2,3},{3,2},{4,8},{5,9},{6,10},{7,11},{8,4},{9,5},{10,... | collective-permute-start | bytes 1572872 | tf_op jit(solution)/shard_map/ppermute | solution.py:282
  52.3 22.6 %collective-permute-start.10 = (bf16[256,1024]{1,0:T(8,128)(2,1)S(1)}, bf16[256,1024]{1,0:T(8,128)(2,1)S(1)}, u32[]{:S(2)}, u32[]{:S(2)}) collective-permute-start(bf16[256,1024]{1,0:T(8,128)(2,1)S(1)} %shard_map.112), channel_id=1, source_target_pairs={{0,4},{12,8},{1,5},{13,9},{2,6},{14,10},{3,7},{15,11},{16,20},{28,... | collective-permute-start | bytes 1572872 | tf_op jit(solution)/shard_map/ppermute | solution.py:279
  54.8 17.3 %copy-start.4 = (bf16[256,128]{1,0:T(8,128)(2,1)}, bf16[256,128]{1,0:T(8,128)(2,1)S(1)}, u32[]{:S(2)}) copy-start(bf16[256,128]{1,0:T(8,128)(2,1)S(1)} %select_convert_fusion) | copy-start | bytes 196612
  59.2 12.8 %copy-start.10 = (f32[1,1024]{1,0:T(1,128)S(1)}, f32[1,1024]{1,0:T(1,128)}, u32[]{:S(2)}) copy-start(f32[1,1024]{1,0:T(1,128)} %get-tuple-element.62) | copy-start | bytes 12292
  59.2 28.7 %collective-permute-start.8 = (bf16[256,768]{1,0:T(8,128)(2,1)}, bf16[256,768]{1,0:T(8,128)(2,1)}, u32[]{:S(2)}, u32[]{:S(2)}) collective-permute-start(bf16[256,768]{1,0:T(8,128)(2,1)} %fusion.24.refs_1_), channel_id=1, source_target_pairs={{4,0},{8,12},{5,1},{9,13},{6,2},{10,14},{7,3},{11,15},{20,16},{24,... | collective-permute-start | bytes 1179656 | tf_op jit(solution)/shard_map/ppermute | solution.py:287
  65.4 13.5 %collective-permute-start.11 = (bf16[256,1024]{1,0:T(8,128)(2,1)}, bf16[256,1024]{1,0:T(8,128)(2,1)}, u32[]{:S(2)}, u32[]{:S(2)}) collective-permute-start(bf16[256,1024]{1,0:T(8,128)(2,1)} %add_convert_fusion.2.refs_2_), channel_id=1, source_target_pairs={{0,1},{1,0},{2,3},{3,2},{4,8},{5,9},{6,10},{7,11},{8,4},{9,5},{10,... | collective-permute-start | bytes 1572872 | tf_op jit(solution)/shard_map/ppermute | solution.py:282
  65.5 30.7 %collective-permute-start.12 = (bf16[256,1024]{1,0:T(8,128)(2,1)S(1)}, bf16[256,1024]{1,0:T(8,128)(2,1)}, u32[]{:S(2)}, u32[]{:S(2)}) collective-permute-start(bf16[256,1024]{1,0:T(8,128)(2,1)S(1)} %shard_map.113), channel_id=1, source_target_pairs={{0,4},{12,8},{1,5},{13,9},{2,6},{14,10},{3,7},{15,11},{16,20},{28,... | collective-permute-start | bytes 1572872 | tf_op jit(solution)/shard_map/ppermute | solution.py:279
  73.6 14.4 %collective-permute-start.9 = (bf16[256,1024]{1,0:T(8,128)(2,1)S(1)}, bf16[256,1024]{1,0:T(8,128)(2,1)}, u32[]{:S(2)}, u32[]{:S(2)}) collective-permute-start(bf16[256,1024]{1,0:T(8,128)(2,1)S(1)} %fusion.4.refs_2_), channel_id=1, source_target_pairs={{4,0},{8,12},{5,1},{9,13},{6,2},{10,14},{7,3},{11,15},{20,16},{24,... | collective-permute-start | bytes 1572872 | tf_op jit(solution)/shard_map/ppermute | solution.py:287
  75.1 10.8 %copy-start.5 = (bf16[256,128]{1,0:T(8,128)(2,1)S(1)}, bf16[256,128]{1,0:T(8,128)(2,1)}, u32[]{:S(2)}) copy-start(bf16[256,128]{1,0:T(8,128)(2,1)} %copy-done.4) | copy-start | bytes 196612
  75.1 10.7 %copy-start.9 = (f32[1,1024]{1,0:T(1,128)S(1)}, f32[1,1024]{1,0:T(1,128)}, u32[]{:S(2)}) copy-start(f32[1,1024]{1,0:T(1,128)} %get-tuple-element.61) | copy-start | bytes 12292
  75.1 10.7 %copy-start.11 = (bf16[128,6144]{1,0:T(8,128)(2,1)S(1)}, bf16[128,6144]{1,0:T(8,128)(2,1)}, u32[]{:S(2)}) copy-start(bf16[128,6144]{1,0:T(8,128)(2,1)} %param.17) | copy-start | bytes 4718596
  78.9 23.0 %collective-permute-start.13 = (bf16[256,1024]{1,0:T(8,128)(2,1)S(1)}, bf16[256,1024]{1,0:T(8,128)(2,1)S(1)}, u32[]{:S(2)}, u32[]{:S(2)}) collective-permute-start(bf16[256,1024]{1,0:T(8,128)(2,1)S(1)} %add_convert_fusion.1.refs_2_), channel_id=1, source_target_pairs={{0,1},{1,0},{2,3},{3,2},{4,8},{5,9},{6,10},{7,11},{8,4},{9,5},{10,... | collective-permute-start | bytes 1572872 | tf_op jit(solution)/shard_map/ppermute | solution.py:282
  79.0 31.0 %collective-permute-start.16 = (bf16[256,768]{1,0:T(8,128)(2,1)S(1)}, bf16[256,768]{1,0:T(8,128)(2,1)S(1)}, u32[]{:S(2)}, u32[]{:S(2)}) collective-permute-start(bf16[256,768]{1,0:T(8,128)(2,1)S(1)} %shard_map.114), channel_id=1, source_target_pairs={{0,4},{12,8},{1,5},{13,9},{2,6},{14,10},{3,7},{15,11},{16,20},{28,... | collective-permute-start | bytes 1179656 | tf_op jit(solution)/shard_map/ppermute | solution.py:279
  85.9 2.1 %copy-start.1 = (bf16[6144,128]{1,0:T(8,128)(2,1)S(1)}, bf16[6144,128]{1,0:T(8,128)(2,1)}, u32[]{:S(2)}) copy-start(bf16[6144,128]{1,0:T(8,128)(2,1)} %refs_4_.1) | copy-start | bytes 4718596
  97.4 4.5 %copy-start.8 = (f32[1,1024]{1,0:T(1,128)S(1)}, f32[1,1024]{1,0:T(1,128)}, u32[]{:S(2)}) copy-start(f32[1,1024]{1,0:T(1,128)} %get-tuple-element.60) | copy-start | bytes 12292
  97.4 16.6 %collective-permute-start.14 = (bf16[256,1024]{1,0:T(8,128)(2,1)S(1)}, bf16[256,1024]{1,0:T(8,128)(2,1)S(1)}, u32[]{:S(2)}, u32[]{:S(2)}) collective-permute-start(bf16[256,1024]{1,0:T(8,128)(2,1)S(1)} %fusion.9.refs_7_.refs_1_), channel_id=1, source_target_pairs={{4,0},{8,12},{5,1},{9,13},{6,2},{10,14},{7,3},{11,15},{20,16},{24,... | collective-permute-start | bytes 1572872 | tf_op jit(solution)/shard_map/ppermute | solution.py:287
  101.8 8.4 %collective-permute-start.17 = (bf16[256,1024]{1,0:T(8,128)(2,1)S(1)}, bf16[256,1024]{1,0:T(8,128)(2,1)S(1)}, u32[]{:S(2)}, u32[]{:S(2)}) collective-permute-start(bf16[256,1024]{1,0:T(8,128)(2,1)S(1)} %add_convert_fusion.refs_2_), channel_id=1, source_target_pairs={{0,1},{1,0},{2,3},{3,2},{4,8},{5,9},{6,10},{7,11},{8,4},{9,5},{10,... | collective-permute-start | bytes 1572872 | tf_op jit(solution)/shard_map/ppermute | solution.py:282
  102.5 19.5 %collective-permute-start.15 = (bf16[256,1024]{1,0:T(8,128)(2,1)S(1)}, bf16[256,1024]{1,0:T(8,128)(2,1)S(1)}, u32[]{:S(2)}, u32[]{:S(2)}) collective-permute-start(bf16[256,1024]{1,0:T(8,128)(2,1)S(1)} %fusion.14.refs_2_), channel_id=1, source_target_pairs={{4,0},{8,12},{5,1},{9,13},{6,2},{10,14},{7,3},{11,15},{20,16},{24,... | collective-permute-start | bytes 1572872 | tf_op jit(solution)/shard_map/ppermute | solution.py:287
  103.8 24.3 %collective-permute-start.18 = (bf16[256,512]{1,0:T(8,128)(2,1)S(1)}, bf16[256,512]{1,0:T(8,128)(2,1)S(1)}, u32[]{:S(2)}, u32[]{:S(2)}) collective-permute-start(bf16[256,512]{1,0:T(8,128)(2,1)S(1)} %shard_map.116), channel_id=1, source_target_pairs={{0,4},{12,8},{1,5},{13,9},{2,6},{14,10},{3,7},{15,11},{16,20},{28,... | collective-permute-start | bytes 786440 | tf_op jit(solution)/shard_map/ppermute | solution.py:279
  110.1 20.1 %collective-permute-start.19 = (bf16[256,768]{1,0:T(8,128)(2,1)S(1)}, bf16[256,768]{1,0:T(8,128)(2,1)S(1)}, u32[]{:S(2)}, u32[]{:S(2)}) collective-permute-start(bf16[256,768]{1,0:T(8,128)(2,1)S(1)} %add_convert_fusion.5), channel_id=1, source_target_pairs={{0,1},{1,0},{2,3},{3,2},{4,8},{5,9},{6,10},{7,11},{8,4},{9,5},{10,... | collective-permute-start | bytes 1179656 | tf_op jit(solution)/shard_map/ppermute | solution.py:282
  128.2 3.9 %collective-permute-start.20 = (bf16[256,512]{1,0:T(8,128)(2,1)S(1)}, bf16[256,512]{1,0:T(8,128)(2,1)S(1)}, u32[]{:S(2)}, u32[]{:S(2)}) collective-permute-start(bf16[256,512]{1,0:T(8,128)(2,1)S(1)} %add_convert_fusion.6), channel_id=1, source_target_pairs={{0,1},{1,0},{2,3},{3,2},{4,8},{5,9},{6,10},{7,11},{8,4},{9,5},{10,... | collective-permute-start | bytes 786440 | tf_op jit(solution)/shard_map/ppermute | solution.py:282
  128.9 25.0 %collective-permute-start.22 = (bf16[256,1024]{1,0:T(8,128)(2,1)S(1)}, bf16[256,1024]{1,0:T(8,128)(2,1)S(1)}, u32[]{:S(2)}, u32[]{:S(2)}) collective-permute-start(bf16[256,1024]{1,0:T(8,128)(2,1)S(1)} %fusion.19.refs_9_.refs_1_), channel_id=1, source_target_pairs={{4,0},{8,12},{5,1},{9,13},{6,2},{10,14},{7,3},{11,15},{20,16},{24,... | collective-permute-start | bytes 1572872 | tf_op jit(solution)/shard_map/ppermute | solution.py:287
  130.7 23.2 %collective-permute-start.23 = (bf16[256,768]{1,0:T(8,128)(2,1)S(1)}, bf16[256,768]{1,0:T(8,128)(2,1)S(1)}, u32[]{:S(2)}, u32[]{:S(2)}) collective-permute-start(bf16[256,768]{1,0:T(8,128)(2,1)S(1)} %fusion.29.refs_2_), channel_id=1, source_target_pairs={{4,0},{8,12},{5,1},{9,13},{6,2},{10,14},{7,3},{11,15},{20,16},{24,... | collective-permute-start | bytes 1179656 | tf_op jit(solution)/shard_map/ppermute | solution.py:287
  132.4 27.2 %collective-permute-start.21 = (bf16[256,512]{1,0:T(8,128)(2,1)S(1)}, bf16[256,512]{1,0:T(8,128)(2,1)S(1)}, u32[]{:S(2)}, u32[]{:S(2)}) collective-permute-start(bf16[256,512]{1,0:T(8,128)(2,1)S(1)} %fusion.36.refs_9_.refs_1_), channel_id=1, source_target_pairs={{4,0},{8,12},{5,1},{9,13},{6,2},{10,14},{7,3},{11,15},{20,16},{24,... | collective-permute-start | bytes 786440 | tf_op jit(solution)/shard_map/ppermute | solution.py:287
  163.5 2.2 %collective-permute-start.24 = (bf16[128,2688]{1,0:T(8,128)(2,1)S(1)}, bf16[128,2688]{1,0:T(8,128)(2,1)S(1)}, u32[]{:S(2)}, u32[]{:S(2)}) collective-permute-start(bf16[128,2688]{1,0:T(8,128)(2,1)S(1)} %pad_maximum_fusion), channel_id=1, source_target_pairs={{0,1},{1,0},{2,3},{3,2},{4,5},{5,4},{6,7},{7,6},{8,9},{9,8},{10,11... | collective-permute-start | bytes 2064392 | tf_op jit(solution)/shard_map/ppermute | solution.py:268
  165.8 10.3 %copy-start.7 = (f32[2560]{0:T(1024)S(1)}, f32[2560]{0:T(1024)}, u32[]{:S(2)}) copy-start(f32[2560]{0:T(1024)} %param.19) | copy-start | bytes 30724
  165.9 10.2 %collective-permute-start.25 = (bf16[64,2688]{1,0:T(8,128)(2,1)S(1)}, bf16[64,2688]{1,0:T(8,128)(2,1)S(1)}, u32[]{:S(2)}, u32[]{:S(2)}) collective-permute-start(bf16[64,2688]{1,0:T(8,128)(2,1)S(1)} %slice.160), channel_id=1, source_target_pairs={{0,2},{1,3},{2,0},{3,1},{4,6},{5,7},{6,4},{7,5},{8,10},{9,11},{10,... | collective-permute-start | bytes 1032200 | tf_op jit(solution)/shard_map/ppermute | solution.py:268

commit v5 on v4

--- a/solution.py
+++ b/solution.py
@@ -15,11 +15,13 @@
 AHEAD = 2
 SHARES = (6, 8, 8, 8, 8, 6, 4)
 PER_CALL = 2
+WINDOW = 3
+EARLY = 4
 F32 = jnp.float32
 BF16 = jnp.bfloat16
 ANY = pl.BlockSpec(memory_space=pl.ANY)
 COST = pl.CostEstimate(flops=1000, bytes_accessed=1000, transcendentals=0)
-PARAMS = pltpu.CompilerParams(vmem_limit_bytes=34 << 20)
+PARAMS = pltpu.CompilerParams(vmem_limit_bytes=18 << 20)
 
 
 def gelu_tanh(values):
@@ -56,73 +58,40 @@
     return [(lo * LANES, (hi - lo) * LANES) for lo, hi in zip(cuts, cuts[1:]) if hi > lo]
 
 
-def first_kernel(*refs, start, tiles, low):
-    x_hbm, w_hbm = refs[:2]
-    d_hbm = refs[2] if low else None
-    out_hbm, x_v, w_v, d_v, o_v, x_sem, w_sem, d_sem, o_sem = refs[-9:]
-    width = tiles[-1][0] + tiles[-1][1]
-    x_copy = pltpu.make_async_copy(x_hbm, x_v, x_sem)
-    w_copies = [
-        pltpu.make_async_copy(
-            w_hbm.at[:, pl.ds(start + at, size)], w_v.at[:, pl.ds(at, size)], w_sem.at[i]
-        )
-        for i, (at, size) in enumerate(tiles)
+def load_kernel(w_hbm, after_ref, *refs, spans):
+    outs, sem = refs[:-1], refs[-1]
+    copies = [
+        pltpu.make_async_copy(w_hbm.at[:, pl.ds(start, width)], out, sem.at[i])
+        for i, ((start, width), out) in enumerate(zip(spans, outs))
     ]
-    w_copies[0].start()
-    x_copy.start()
-    for copy in w_copies[1:]:
+    for copy in copies:
         copy.start()
-    sent = []
-
-    def finish(at, size, right, sem):
-        o_v[:, pl.ds(at, size)] = dot(x_v[...], right).astype(BF16)
-        copy = pltpu.make_async_copy(o_v.at[:, pl.ds(at, size)], out_hbm.at[:, pl.ds(at, size)], sem)
-        copy.start()
-        sent.append(copy)
-
-    if low:
-        d_copy = pltpu.make_async_copy(d_hbm, d_v, d_sem)
-        d_copy.start()
-    x_copy.wait()
-    for i, (at, size) in enumerate(tiles):
-        w_copies[i].wait()
-        finish(at, size, w_v[:, pl.ds(at, size)], o_sem.at[i])
-    if low:
-        d_copy.wait()
-        finish(width, LANES, d_v[...], o_sem.at[len(tiles)])
-    for copy in sent:
+    for copy in copies:
         copy.wait()
 
 
-def first_product(x, weight, down, span, after):
-    start, width = span
-    rows, depth = x.shape
-    low = down is not None
-    tiles = tiles_of(width, 256)
-    total = width + (LANES if low else 0)
-    operands = [x, weight] + ([down] if low else []) + [after]
+def load_chunks(weight, spans, after):
     return pl.pallas_call(
-        functools.partial(first_kernel, start=start, tiles=tiles, low=low),
-        in_specs=[ANY] * len(operands),
-        out_specs=ANY,
-        out_shape=jax.ShapeDtypeStruct((rows, total), BF16),
-        scratch_shapes=[
-            pltpu.VMEM((rows, depth), BF16),
-            pltpu.VMEM((depth, width), BF16),
-            pltpu.VMEM((depth if low else 16, LANES), BF16),
-            pltpu.VMEM((rows, total), BF16),
-            pltpu.SemaphoreType.DMA,
-            pltpu.SemaphoreType.DMA((len(tiles),)),
-            pltpu.SemaphoreType.DMA,
-            pltpu.SemaphoreType.DMA((len(tiles) + 1,)),
-        ],
-        compiler_params=PARAMS,
+        functools.partial(load_kernel, spans=spans),
+        in_specs=[ANY, ANY],
+        out_specs=[pl.BlockSpec(memory_space=pltpu.VMEM)] * len(spans),
+        out_shape=[pltpu.VMEM((weight.shape[0], width), BF16) for _, width in spans],
+        scratch_shapes=[pltpu.SemaphoreType.DMA((len(spans),))],
+        compiler_params=pltpu.CompilerParams(vmem_limit_bytes=1 << 20),
         cost_estimate=COST,
-    )(*operands)
+    )(pltpu.with_memory_space_constraint(weight, pltpu.HBM), after)
 
 
 def tie(value, after):
     return lax.optimization_barrier((value, after))[0]
+
+
+def first_product(x, part, down, after):
+    x = tie(x, after)
+    out = dot(x, part).astype(BF16)
+    if down is not None:
+        out = jnp.concatenate([out, dot(x, down).astype(BF16)], axis=1)
+    return out
 
 
 def add_rounded(a, b, after):
@@ -164,7 +133,7 @@
         for copy in copies:
             copy.wait()
 
-    for copy in w_copies[1:]:
+    for copy in w_copies[1:WINDOW]:
         copy.start()
     d_copy = pltpu.make_async_copy(d_hbm.at[pl.ds(start, depth), :], d_v, d_sem)
     d_copy.start()
@@ -198,6 +167,8 @@
         copy = pltpu.make_async_copy(acc_v.at[:, part], out_hbm.at[:, part], o_sem.at[i])
         copy.start()
         sent.append(copy)
+        if i + WINDOW < len(tiles):
+            w_copies[i + WINDOW].start()
     d_copy.wait()
     if first:
         low_v[...] = dot(state[...], d_v[...])
@@ -216,7 +187,7 @@
     widths = [h.shape[1] for h in own]
     depth = sum(widths)
     out_width = weight.shape[1]
-    tiles = tiles_of(out_width, 512)
+    tiles = tiles_of(out_width, 256)
     first = total is None
     operands = [*own, *come, weight, down] + ([] if first else [total, low_total]) + [after]
     return pl.pallas_call(
@@ -267,10 +238,10 @@
     def col_swap(value, flip):
         return lax.ppermute(value, "col", [(i, i ^ flip) for i in range(n_col)])
 
-    def gather_tokens(tokens):
+    def gather_tokens(tokens, loaded):
         shards = [tokens, col_swap(tokens, 1)]
         for step in range(1, chips):
-            far = col_swap(tokens, 2 * step)
+            far = tie(col_swap(tokens, 2 * step), loaded)
             shards += [far, col_swap(far, 1)]
         return jnp.concatenate(shards, axis=0)
 
@@ -322,7 +293,8 @@
             ],
             axis=0,
         )
-        gathered = gather_tokens(tokens)
+        loads = list(load_chunks(first_weight, spans[:EARLY], tokens))
+        gathered = gather_tokens(tokens, loads[-1])
         last = gathered
         partials, folded, sums, crossed, states, returned = {}, {}, {}, {}, {}, {}
         total, low_total, low_in = None, None, None
@@ -331,12 +303,15 @@
         def start_chunk(t):
             nonlocal last
             down = first_down_maps if t == 0 else None
-            last = first_product(gathered, first_weight, down, spans[t], last)
+            last = first_product(gathered, loads[t], down, last)
             partials[t] = last
             folded[t] = fold(last, 0)
 
         for t in range(min(AHEAD, count)):
             start_chunk(t)
+        if count > EARLY:
+            loads += load_chunks(first_weight, spans[EARLY:], last)
+            last = loads[-1]
         for t in range(count + 2):
             if t < count:
                 value = add_rounded(partials[t], folded[t], last)

time: 178 us -> 182 us (1.022)
  Pallas kernels: 54.6 us -> 43.2 us
  local copies, waits for them, and re-layouts: 2.84 us -> 13.7 us
  matrix products: 8.81 us -> 17.2 us
  other arithmetic: 7.64 us -> 1.69 us
  waiting for transfers between devices: 52.7 us -> 55.1 us
    pallas_call x7 -> x2, Pallas kernels: 31.3 us -> 11.3 us  [load_chunks(): pl.pallas_call(functools.partial(load_kernel, spans=spans), in_specs=[ANY...]
    unnamed x28 -> x40, local copies, waits for them, and re-layouts: 1.27 us -> 11.3 us
    pallas_call x4, Pallas kernels: 23.3 us -> 31.9 us  [second_product(): pl.pallas_call(functools.partial(second_kernel, count=len(own), widths=wi...]
    dot_general x8 -> x16, matrix products: 8.81 us -> 17.2 us  [dot(): return jnp.dot(left, right, preferred_element_type=F32)]
    ppermute x5, waiting for transfers between devices: 18.4 us -> 12.1 us  [col_swap(): return lax.ppermute(value, 'col', [(i, i ^ flip) for i in range(n_col)])]
    ppermute x7, waiting for transfers between devices: 3 us -> 9.15 us  [fold(): return lax.ppermute(value, 'row', pairs)]
    convert_element_type x7, other arithmetic: 6.32 us -> 1.04 us  [add_rounded(): return (tie(a, after).astype(F32) + b.astype(F32)).astype(BF16)]
    ppermute x7, waiting for transfers between devices: 31.3 us -> 33.8 us  [spread(): come = lax.ppermute(value, 'row', pairs)]
  transfers between devices with their start and end apart: 26 -> 26, of which waited for: 9 -> 9; matrix products, arithmetic and copies ran while one was open for 10% -> 11% of each run, Pallas kernels for 26% -> 21%
where the time goes in v5:
time: 182 us; the launch traced here: 181 us
  waiting for transfers between devices  55.1 us (30%)
  starting transfers between devices  49.3 us (27%)
  Pallas kernels  43.2 us (24%)
  matrix products  17.2 us (9%)
  local copies, waits for them, and re-layouts  13.7 us (8%)
    ppermute x7, starting transfers between devices, fold(): return lax.ppermute(value, 'row', pairs)  35.4 us
    ppermute x7, waiting for transfers between devices, spread(): come = lax.ppermute(value, 'row', pairs)  33.8 us
    pallas_call x4, Pallas kernels, second_product(): pl.pallas_call(functools.partial(second_kernel, count=len(own), widths=wi...  31.9 us
    dot_general x16, matrix products, dot(): return jnp.dot(left, right, preferred_element_type=F32)  17.2 us
    ppermute x5, waiting for transfers between devices, col_swap(): return lax.ppermute(value, 'col', [(i, i ^ flip) for i in range(n_col)])  12.1 us
    unnamed x40, local copies, waits for them, and re-layouts  11.3 us
    pallas_call x2, Pallas kernels, load_chunks(): pl.pallas_call(functools.partial(load_kernel, spans=spans), in_specs=[ANY...  11.3 us
    ppermute x7, waiting for transfers between devices, fold(): return lax.ppermute(value, 'row', pairs)  9.15 us
  transfers between devices with their start and end apart: 26, of which 9 were waited for; matrix products, arithmetic and copies ran while one was open for 11% of the time, Pallas kernels for 21%

profile of v5, /device:TPU:0, one launch (start us, length us, event | category | flops | bytes accessed | tf_op | source)
XLA Modules:
  0.0 181.0 jit_solution(5739350151669146712)
XLA Ops:
  0.0 0.5 collective-permute-start
  0.5 2.6 %collective-permute-start.1 = (bf16[64,2560]{1,0:T(8,128)(2,1)}, bf16[64,2560]{1,0:T(8,128)(2,1)}, u32[]{:S(2)}, u32[]{:S(2)}) collective-permute-start(bf16[64,2560]{1,0:T(8,128)(2,1)} %after_ref.1), channel_id=1, source_target_pairs={{0,2},{1,3},{2,0},{3,1},{4,6},{5,7},{6,4},{7,5},{8,10},{9,11},{10,... | collective-permute-start | bytes 983048 | tf_op jit(solution)/shard_map/ppermute | solution.py:239
  3.0 0.7 slice_reduce_fusion
  3.7 0.7 fusion.62
  4.5 1.0 copy-done.2
  5.5 6.8 %shard_map.109 = (bf16[2560,768]{1,0:T(8,128)(2,1)S(1)}, bf16[2560,1024]{1,0:T(8,128)(2,1)S(1)}, bf16[2560,1024]{1,0:T(8,128)(2,1)S(1)}, bf16[2560,1024]{1,0:T(8,128)(2,1)S(1)}) custom-call(bf16[2560,6144]{1,0:T(8,128)(2,1)} %w_hbm.3, bf16[64,2560]{1,0:T(8,128)(2,1)S(1)} %copy-done.2), custom_call_target="tpu_custom_call" | custom-call | flops 1000 | bytes 1000 | tf_op jit(solution)/shard_map/pallas_call | solution.py:74
  12.3 2.3 %copy-done.4 = bf16[2560,1024]{1,0:T(8,128)(2,1)} copy-done((bf16[2560,1024]{1,0:T(8,128)(2,1)}, bf16[2560,1024]{1,0:T(8,128)(2,1)S(1)}, u32[]{:S(2)}) %copy-start.4) | copy-done | bytes 5242904
  14.6 2.4 %copy-done.5 = bf16[2560,1024]{1,0:T(8,128)(2,1)} copy-done((bf16[2560,1024]{1,0:T(8,128)(2,1)}, bf16[2560,1024]{1,0:T(8,128)(2,1)S(1)}, u32[]{:S(2)}) %copy-start.5) | copy-done | bytes 5242904
  17.0 2.3 %copy-done.6 = bf16[2560,1024]{1,0:T(8,128)(2,1)} copy-done((bf16[2560,1024]{1,0:T(8,128)(2,1)}, bf16[2560,1024]{1,0:T(8,128)(2,1)S(1)}, u32[]{:S(2)}) %copy-start.6) | copy-done | bytes 5242904
  19.3 1.9 %copy-done.7 = bf16[2560,768]{1,0:T(8,128)(2,1)} copy-done((bf16[2560,768]{1,0:T(8,128)(2,1)}, bf16[2560,768]{1,0:T(8,128)(2,1)S(1)}, u32[]{:S(2)}) %copy-start.7) | copy-done | bytes 3932184
  21.4 0.2 collective-permute-start.2
  21.7 1.1 constant_dynamic-update-slice_fusion.1
  22.8 0.5 collective-permute-done.2
  23.4 0.5 convolution_convert_fusion.7
  23.9 1.2 convolution_convert_fusion.5
  25.2 3.5 %collective-permute-start.3 = (bf16[256,896]{1,0:T(8,128)(2,1)S(1)}, bf16[256,896]{1,0:T(8,128)(2,1)S(1)}, u32[]{:S(2)}, u32[]{:S(2)}) collective-permute-start(bf16[256,896]{1,0:T(8,128)(2,1)S(1)} %pad_maximum_fusion.1), channel_id=1, source_target_pairs={{0,4},{12,8},{1,5},{13,9},{2,6},{14,10},{3,7},{15,11},{16,20},{28,... | collective-permute-start | bytes 1376264 | tf_op jit(solution)/shard_map/ppermute | solution.py:250
  28.7 1.5 convolution_convert_fusion.3.after_ref
  30.2 4.5 %shard_map.110 = (bf16[2560,1024]{1,0:T(8,128)(2,1)S(1)}, bf16[2560,768]{1,0:T(8,128)(2,1)S(1)}, bf16[2560,512]{1,0:T(8,128)(2,1)S(1)}) custom-call(bf16[2560,6144]{1,0:T(8,128)(2,1)} %w_hbm.3, bf16[256,1024]{1,0:T(8,128)(2,1)S(1)} %convolution_convert_fusion.3.after_ref), custom_call_target="tpu_custom_call" | custom-call | flops 1000 | bytes 1000 | tf_op jit(solution)/shard_map/pallas_call | solution.py:74
  34.7 1.3 collective-permute-start.4
  36.1 3.4 %collective-permute-done.3 = bf16[256,896]{1,0:T(8,128)(2,1)S(1)} collective-permute-done((bf16[256,896]{1,0:T(8,128)(2,1)S(1)}, bf16[256,896]{1,0:T(8,128)(2,1)S(1)}, u32[]{:S(2)}, u32[]{:S(2)}) %collective-permute-start.3) | collective-permute-done | bytes 458784 | tf_op jit(solution)/shard_map/ppermute | solution.py:250
  39.7 4.2 %convolution_convert_fusion.2 = bf16[256,1024]{1,0:T(8,128)(2,1)S(1)} fusion(bf16[256,2560]{1,0:T(8,128)(2,1)S(1)} %constant_dynamic-update-slice_fusion, bf16[2560,1024]{1,0:T(8,128)(2,1)} %copy-done.5), kind=kOutput, calls=%fused_computation.7 | convolution fusion | flops 1342439424 | bytes 7077888 | tf_op jit(solution)/shard_map/dot_general | solution.py:43
  43.9 6.0 %collective-permute-start.6 = (bf16[256,1024]{1,0:T(8,128)(2,1)S(1)}, bf16[256,1024]{1,0:T(8,128)(2,1)S(1)}, u32[]{:S(2)}, u32[]{:S(2)}) collective-permute-start(bf16[256,1024]{1,0:T(8,128)(2,1)S(1)} %convolution_convert_fusion.2), channel_id=1, source_target_pairs={{0,4},{12,8},{1,5},{13,9},{2,6},{14,10},{3,7},{15,11},{16,20},{28,... | collective-permute-start | bytes 1572872 | tf_op jit(solution)/shard_map/ppermute | solution.py:250
  49.8 0.9 collective-permute-done.4
  50.7 0.2 add_convert_fusion.3
  51.0 1.5 convolution_convert_fusion.1
  52.6 6.0 %collective-permute-start.10 = (bf16[256,1024]{1,0:T(8,128)(2,1)S(1)}, bf16[256,1024]{1,0:T(8,128)(2,1)S(1)}, u32[]{:S(2)}, u32[]{:S(2)}) collective-permute-start(bf16[256,1024]{1,0:T(8,128)(2,1)S(1)} %convolution_convert_fusion.1), channel_id=1, source_target_pairs={{0,4},{12,8},{1,5},{13,9},{2,6},{14,10},{3,7},{15,11},{16,20},{28,... | collective-permute-start | bytes 1572872 | tf_op jit(solution)/shard_map/ppermute | solution.py:250
  58.6 0.5 fusion.24.refs_1_
  59.1 1.3 collective-permute-start.8
  60.4 1.8 collective-permute-done.6
  62.2 0.2 add_convert_fusion.2
  62.4 1.5 convolution_convert_fusion
  63.9 4.4 %collective-permute-start.12 = (bf16[256,1024]{1,0:T(8,128)(2,1)S(1)}, bf16[256,1024]{1,0:T(8,128)(2,1)S(1)}, u32[]{:S(2)}, u32[]{:S(2)}) collective-permute-start(bf16[256,1024]{1,0:T(8,128)(2,1)S(1)} %convolution_convert_fusion), channel_id=1, source_target_pairs={{0,4},{12,8},{1,5},{13,9},{2,6},{14,10},{3,7},{15,11},{16,20},{28,... | collective-permute-start | bytes 1572872 | tf_op jit(solution)/shard_map/ppermute | solution.py:250
  68.4 0.6 fusion.4.refs_2_
  69.0 1.3 collective-permute-start.9
  70.3 3.1 %collective-permute-done.10 = bf16[256,1024]{1,0:T(8,128)(2,1)S(1)} collective-permute-done((bf16[256,1024]{1,0:T(8,128)(2,1)S(1)}, bf16[256,1024]{1,0:T(8,128)(2,1)S(1)}, u32[]{:S(2)}, u32[]{:S(2)}) %collective-permute-start.10) | collective-permute-done | bytes 524320 | tf_op jit(solution)/shard_map/ppermute | solution.py:250
  73.4 0.2 add_convert_fusion.1
  73.7 1.2 convolution_convert_fusion.4
  74.9 9.6 %collective-permute-start.16 = (bf16[256,768]{1,0:T(8,128)(2,1)S(1)}, bf16[256,768]{1,0:T(8,128)(2,1)S(1)}, u32[]{:S(2)}, u32[]{:S(2)}) collective-permute-start(bf16[256,768]{1,0:T(8,128)(2,1)S(1)} %convolution_convert_fusion.4), channel_id=1, source_target_pairs={{0,4},{12,8},{1,5},{13,9},{2,6},{14,10},{3,7},{15,11},{16,20},{28,... | collective-permute-start | bytes 1179656 | tf_op jit(solution)/shard_map/ppermute | solution.py:250
  84.5 0.6 fusion.9.refs_7_.refs_1_
  85.2 1.3 collective-permute-start.14
  86.5 8.5 %shard_map.111 = (f32[256,2560]{1,0:T(8,128)S(1)}, f32[256,128]{1,0:T(8,128)S(1)}) custom-call(s32[1]{0:T(128)} %bitcast.refs_0_, bf16[256,768]{1,0:T(8,128)(2,1)S(1)} %fusion.24.refs_1_, bf16[256,1024]{1,0:T(8,128)(2,1)S(1)} %fusion.4.refs_2_, bf16[256,768]{1,0:T(8,128)(2,1)S(1)} %collective-permute-done.8.refs_3_, ...), custom_call_target="tpu_custom_call" | custom-call | flops 1000 | bytes 1000 | tf_op jit(solution)/shard_map/pallas_call | solution.py:193
  95.0 0.2 add_convert_fusion
  95.2 0.8 convolution_convert_fusion.6
  96.0 4.6 %collective-permute-start.18 = (bf16[256,512]{1,0:T(8,128)(2,1)S(1)}, bf16[256,512]{1,0:T(8,128)(2,1)S(1)}, u32[]{:S(2)}, u32[]{:S(2)}) collective-permute-start(bf16[256,512]{1,0:T(8,128)(2,1)S(1)} %convolution_convert_fusion.6), channel_id=1, source_target_pairs={{0,4},{12,8},{1,5},{13,9},{2,6},{14,10},{3,7},{15,11},{16,20},{28,... | collective-permute-start | bytes 786440 | tf_op jit(solution)/shard_map/ppermute | solution.py:250
  100.7 0.6 fusion.14.refs_2_
  101.3 1.3 collective-permute-start.15
  102.8 0.6 collective-permute-start.19
  103.3 0.6 fusion.19.refs_9_.refs_1_
  104.0 13.6 %collective-permute-done.15.refs_4_ = bf16[256,1024]{1,0:T(8,128)(2,1)S(1)} collective-permute-done((bf16[256,1024]{1,0:T(8,128)(2,1)S(1)}, bf16[256,1024]{1,0:T(8,128)(2,1)S(1)}, u32[]{:S(2)}, u32[]{:S(2)}) %collective-permute-start.15) | collective-permute-done | bytes 524320 | tf_op jit(solution)/shard_map/ppermute | solution.py:258
  117.5 9.2 %shard_map.112 = (f32[256,2560]{1,0:T(8,128)S(1)}, f32[256,128]{1,0:T(8,128)S(1)}) custom-call(s32[1]{0:T(128)} %bitcast.refs_0_, bf16[256,1024]{1,0:T(8,128)(2,1)S(1)} %fusion.9.refs_7_.refs_1_, bf16[256,1024]{1,0:T(8,128)(2,1)S(1)} %fusion.14.refs_2_, bf16[256,1024]{1,0:T(8,128)(2,1)S(1)} %collective-permute-done.14.refs_3_, ...), custom_call_target="tpu_custom_call" | custom-call | flops 1000 | bytes 1000 | tf_op jit(solution)/shard_map/pallas_call | solution.py:193
  126.9 0.7 slice.116
  127.6 1.3 collective-permute-start.22
  128.9 0.5 fusion.29.refs_2_
  129.4 1.3 collective-permute-start.23
  130.7 0.4 fusion.36.refs_9_.refs_1_
  131.1 1.3 collective-permute-start.21
  132.4 20.2 %collective-permute-done.23.refs_4_ = bf16[256,768]{1,0:T(8,128)(2,1)S(1)} collective-permute-done((bf16[256,768]{1,0:T(8,128)(2,1)S(1)}, bf16[256,768]{1,0:T(8,128)(2,1)S(1)}, u32[]{:S(2)}, u32[]{:S(2)}) %collective-permute-start.23) | collective-permute-done | bytes 393248 | tf_op jit(solution)/shard_map/ppermute | solution.py:258
  152.7 8.5 %shard_map.113 = (f32[256,2560]{1,0:T(8,128)S(1)}, f32[256,128]{1,0:T(8,128)S(1)}) custom-call(s32[1]{0:T(128)} %bitcast.refs_0_, bf16[256,1024]{1,0:T(8,128)(2,1)S(1)} %fusion.19.refs_9_.refs_1_, bf16[256,768]{1,0:T(8,128)(2,1)S(1)} %fusion.29.refs_2_, bf16[256,1024]{1,0:T(8,128)(2,1)S(1)} %collective-permute-done.22.refs_3_, ...), custom_call_target="tpu_custom_call" | custom-call | flops 1000 | bytes 1000 | tf_op jit(solution)/shard_map/pallas_call | solution.py:193
  161.2 5.8 %shard_map.114 = (f32[256,2560]{1,0:T(8,128)S(1)}, f32[256,128]{1,0:T(8,128)S(1)}) custom-call(s32[1]{0:T(128)} %bitcast.refs_0_, bf16[256,512]{1,0:T(8,128)(2,1)S(1)} %fusion.36.refs_9_.refs_1_, bf16[256,512]{1,0:T(8,128)(2,1)S(1)} %collective-permute-done.21.refs_2_, bf16[6144,2560]{1,0:T(8,128)(2,1)} %refs_3_.1, bf16[6144,128]{1,0:T(8,128)(2,1)S(1)} %copy-done.1, ...), custom_call_target="tpu_custom_call" | custom-call | flops 1000 | bytes 1000 | tf_op jit(solution)/shard_map/pallas_call | solution.py:193
  166.9 0.2 constant_dynamic-update-slice_fusion.5
  167.6 2.0 %collective-permute-done.24 = bf16[128,2688]{1,0:T(8,128)(2,1)S(1)} collective-permute-done((bf16[128,2688]{1,0:T(8,128)(2,1)S(1)}, bf16[128,2688]{1,0:T(8,128)(2,1)S(1)}, u32[]{:S(2)}, u32[]{:S(2)}) %collective-permute-start.24) | collective-permute-done | bytes 688160 | tf_op jit(solution)/shard_map/ppermute | solution.py:239
  169.8 0.6 collective-permute-start.25
  170.4 9.6 %collective-permute-done.25 = bf16[64,2688]{1,0:T(8,128)(2,1)S(1)} collective-permute-done((bf16[64,2688]{1,0:T(8,128)(2,1)S(1)}, bf16[64,2688]{1,0:T(8,128)(2,1)S(1)}, u32[]{:S(2)}, u32[]{:S(2)}) %collective-permute-start.25) | collective-permute-done | bytes 344096 | tf_op jit(solution)/shard_map/ppermute | solution.py:239
  180.1 1.0 fusion.31
  (77 shorter events, 1.9 us)
Async XLA Ops:
  0.0 180.0 %copy-start = (bf16[128,2560]{1,0:T(8,128)(2,1)S(1)}, bf16[128,2560]{1,0:T(8,128)(2,1)}, u32[]{:S(2)}) copy-start(bf16[128,2560]{1,0:T(8,128)(2,1)} %param.21) | copy-start | bytes 1966084
  0.0 21.7 %collective-permute-start = (bf16[64,2560]{1,0:T(8,128)(2,1)}, bf16[64,2560]{1,0:T(8,128)(2,1)S(1)}, u32[]{:S(2)}, u32[]{:S(2)}) collective-permute-start(bf16[64,2560]{1,0:T(8,128)(2,1)} %after_ref.1), channel_id=1, source_target_pairs={{0,1},{1,0},{2,3},{3,2},{4,5},{5,4},{6,7},{7,6},{8,9},{9,8},{10,11... | collective-permute-start | bytes 983048 | tf_op jit(solution)/shard_map/ppermute | solution.py:239
  0.5 21.0 %collective-permute-start.1 = (bf16[64,2560]{1,0:T(8,128)(2,1)}, bf16[64,2560]{1,0:T(8,128)(2,1)}, u32[]{:S(2)}, u32[]{:S(2)}) collective-permute-start(bf16[64,2560]{1,0:T(8,128)(2,1)} %after_ref.1), channel_id=1, source_target_pairs={{0,2},{1,3},{2,0},{3,1},{4,6},{5,7},{6,4},{7,5},{8,10},{9,11},{10,... | collective-permute-start | bytes 983048 | tf_op jit(solution)/shard_map/ppermute | solution.py:239
  4.5 1.0 copy-start.2
  5.5 15.7 %copy-start.11 = (s32[256]{0:T(256)S(1)}, s32[256]{0:T(256)}, u32[]{:S(2)}) copy-start(s32[256]{0:T(256)} %param.12) | copy-start | bytes 3076
  5.5 15.7 %copy-start.12 = (s32[4]{0:T(128)S(1)}, s32[4]{0:T(128)}, u32[]{:S(2)}) copy-start(s32[4]{0:T(128)} %param.13) | copy-start | bytes 52
  5.5 15.9 %copy-start.3 = (bf16[64,2560]{1,0:T(8,128)(2,1)S(1)}, bf16[64,2560]{1,0:T(8,128)(2,1)}, u32[]{:S(2)}) copy-start(bf16[64,2560]{1,0:T(8,128)(2,1)} %after_ref.1) | copy-start | bytes 983044
  12.3 2.3 %copy-start.4 = (bf16[2560,1024]{1,0:T(8,128)(2,1)}, bf16[2560,1024]{1,0:T(8,128)(2,1)S(1)}, u32[]{:S(2)}) copy-start(bf16[2560,1024]{1,0:T(8,128)(2,1)S(1)} %get-tuple-element.42) | copy-start | bytes 15728644
  14.6 2.4 %copy-start.5 = (bf16[2560,1024]{1,0:T(8,128)(2,1)}, bf16[2560,1024]{1,0:T(8,128)(2,1)S(1)}, u32[]{:S(2)}) copy-start(bf16[2560,1024]{1,0:T(8,128)(2,1)S(1)} %get-tuple-element.51) | copy-start | bytes 15728644
  17.0 2.3 %copy-start.6 = (bf16[2560,1024]{1,0:T(8,128)(2,1)}, bf16[2560,1024]{1,0:T(8,128)(2,1)S(1)}, u32[]{:S(2)}) copy-start(bf16[2560,1024]{1,0:T(8,128)(2,1)S(1)} %get-tuple-element.47) | copy-start | bytes 15728644
  19.3 1.9 %copy-start.7 = (bf16[2560,768]{1,0:T(8,128)(2,1)}, bf16[2560,768]{1,0:T(8,128)(2,1)S(1)}, u32[]{:S(2)}) copy-start(bf16[2560,768]{1,0:T(8,128)(2,1)S(1)} %get-tuple-element.45) | copy-start | bytes 11796484
  21.1 2.2 %copy-start.9 = (bf16[2560,128]{1,0:T(8,128)(2,1)S(1)}, bf16[2560,128]{1,0:T(8,128)(2,1)}, u32[]{:S(2)}) copy-start(bf16[2560,128]{1,0:T(8,128)(2,1)} %param.16) | copy-start | bytes 1966084
  21.4 1.9 %collective-permute-start.2 = (bf16[64,2560]{1,0:T(8,128)(2,1)}, bf16[64,2560]{1,0:T(8,128)(2,1)S(1)}, u32[]{:S(2)}, u32[]{:S(2)}) collective-permute-start(bf16[64,2560]{1,0:T(8,128)(2,1)} %collective-permute-done.1), channel_id=1, source_target_pairs={{0,1},{1,0},{2,3},{3,2},{4,5},{5,4},{6,7},{7,6},{8,9},{9,8},{10,11... | collective-permute-start | bytes 983048 | tf_op jit(solution)/shard_map/ppermute | solution.py:239
  21.7 2.3 %copy-start.8 = (bf16[2560,768]{1,0:T(8,128)(2,1)S(1)}, bf16[2560,768]{1,0:T(8,128)(2,1)}, u32[]{:S(2)}) copy-start(bf16[2560,768]{1,0:T(8,128)(2,1)} %copy-done.7) | copy-start | bytes 11796484
  23.4 5.3 %slice-start.2 = ((s8[5242880]{0:T(1024)(128)(4,1)}), s8[4194304]{0:T(1024)(128)(4,1)S(1)}, s32[]{:S(2)}) async-start(s8[5242880]{0:T(1024)(128)(4,1)} %bitcast.33), calls=%async_computation.2 | async-start | bytes 8388608
  23.9 4.8 %slice-start.3 = ((s8[5242880]{0:T(1024)(128)(4,1)}), s8[1048576]{0:T(1024)(128)(4,1)S(1)}, s32[]{:S(2)}) async-start(s8[5242880]{0:T(1024)(128)(4,1)} %bitcast.33), calls=%async_computation.3 | async-start | bytes 2097152
  25.2 14.3 %collective-permute-start.3 = (bf16[256,896]{1,0:T(8,128)(2,1)S(1)}, bf16[256,896]{1,0:T(8,128)(2,1)S(1)}, u32[]{:S(2)}, u32[]{:S(2)}) collective-permute-start(bf16[256,896]{1,0:T(8,128)(2,1)S(1)} %pad_maximum_fusion.1), channel_id=1, source_target_pairs={{0,4},{12,8},{1,5},{13,9},{2,6},{14,10},{3,7},{15,11},{16,20},{28,... | collective-permute-start | bytes 1376264 | tf_op jit(solution)/shard_map/ppermute | solution.py:250
  34.7 16.0 %collective-permute-start.4 = (bf16[256,1024]{1,0:T(8,128)(2,1)S(1)}, bf16[256,1024]{1,0:T(8,128)(2,1)S(1)}, u32[]{:S(2)}, u32[]{:S(2)}) collective-permute-start(bf16[256,1024]{1,0:T(8,128)(2,1)S(1)} %convolution_convert_fusion.3.after_ref), channel_id=1, source_target_pairs={{0,4},{12,8},{1,5},{13,9},{2,6},{14,10},{3,7},{15,11},{16,20},{28,... | collective-permute-start | bytes 1572872 | tf_op jit(solution)/shard_map/ppermute | solution.py:250
  39.6 18.9 %collective-permute-start.5 = (bf16[256,896]{1,0:T(8,128)(2,1)S(1)}, bf16[256,896]{1,0:T(8,128)(2,1)S(1)}, u32[]{:S(2)}, u32[]{:S(2)}) collective-permute-start(bf16[256,896]{1,0:T(8,128)(2,1)S(1)} %add_convert_fusion.4), channel_id=1, source_target_pairs={{0,1},{1,0},{2,3},{3,2},{4,8},{5,9},{6,10},{7,11},{8,4},{9,5},{10,... | collective-permute-start | bytes 1376264 | tf_op jit(solution)/shard_map/ppermute | solution.py:253
  39.7 11.3 %slice-start = ((s8[5242880]{0:T(1024)(128)(4,1)}), s8[4194304]{0:T(1024)(128)(4,1)S(1)}, s32[]{:S(2)}) async-start(s8[5242880]{0:T(1024)(128)(4,1)} %bitcast.31), calls=%async_computation | async-start | bytes 8388608
  39.7 11.3 %slice-start.1 = ((s8[5242880]{0:T(1024)(128)(4,1)}), s8[1048576]{0:T(1024)(128)(4,1)S(1)}, s32[]{:S(2)}) async-start(s8[5242880]{0:T(1024)(128)(4,1)} %bitcast.31), calls=%async_computation.1 | async-start | bytes 2097152
  43.9 18.3 %collective-permute-start.6 = (bf16[256,1024]{1,0:T(8,128)(2,1)S(1)}, bf16[256,1024]{1,0:T(8,128)(2,1)S(1)}, u32[]{:S(2)}, u32[]{:S(2)}) collective-permute-start(bf16[256,1024]{1,0:T(8,128)(2,1)S(1)} %convolution_convert_fusion.2), channel_id=1, source_target_pairs={{0,4},{12,8},{1,5},{13,9},{2,6},{14,10},{3,7},{15,11},{16,20},{28,... | collective-permute-start | bytes 1572872 | tf_op jit(solution)/shard_map/ppermute | solution.py:250
  50.9 7.7 %copy-start.13 = (bf16[128,6144]{1,0:T(8,128)(2,1)S(1)}, bf16[128,6144]{1,0:T(8,128)(2,1)}, u32[]{:S(2)}) copy-start(bf16[128,6144]{1,0:T(8,128)(2,1)} %param.17) | copy-start | bytes 4718596
  50.9 17.5 %collective-permute-start.7 = (bf16[256,1024]{1,0:T(8,128)(2,1)S(1)}, bf16[256,1024]{1,0:T(8,128)(2,1)S(1)}, u32[]{:S(2)}, u32[]{:S(2)}) collective-permute-start(bf16[256,1024]{1,0:T(8,128)(2,1)S(1)} %add_convert_fusion.3), channel_id=1, source_target_pairs={{0,1},{1,0},{2,3},{3,2},{4,8},{5,9},{6,10},{7,11},{8,4},{9,5},{10,... | collective-permute-start | bytes 1572872 | tf_op jit(solution)/shard_map/ppermute | solution.py:253
  52.6 20.8 %collective-permute-start.10 = (bf16[256,1024]{1,0:T(8,128)(2,1)S(1)}, bf16[256,1024]{1,0:T(8,128)(2,1)S(1)}, u32[]{:S(2)}, u32[]{:S(2)}) collective-permute-start(bf16[256,1024]{1,0:T(8,128)(2,1)S(1)} %convolution_convert_fusion.1), channel_id=1, source_target_pairs={{0,4},{12,8},{1,5},{13,9},{2,6},{14,10},{3,7},{15,11},{16,20},{28,... | collective-permute-start | bytes 1572872 | tf_op jit(solution)/shard_map/ppermute | solution.py:250
  59.1 26.1 %collective-permute-start.8 = (bf16[256,768]{1,0:T(8,128)(2,1)S(1)}, bf16[256,768]{1,0:T(8,128)(2,1)S(1)}, u32[]{:S(2)}, u32[]{:S(2)}) collective-permute-start(bf16[256,768]{1,0:T(8,128)(2,1)S(1)} %fusion.24.refs_1_), channel_id=1, source_target_pairs={{4,0},{8,12},{5,1},{9,13},{6,2},{10,14},{7,3},{11,15},{20,16},{24,... | collective-permute-start | bytes 1179656 | tf_op jit(solution)/shard_map/ppermute | solution.py:258
  63.9 31.1 %collective-permute-start.12 = (bf16[256,1024]{1,0:T(8,128)(2,1)S(1)}, bf16[256,1024]{1,0:T(8,128)(2,1)S(1)}, u32[]{:S(2)}, u32[]{:S(2)}) collective-permute-start(bf16[256,1024]{1,0:T(8,128)(2,1)S(1)} %convolution_convert_fusion), channel_id=1, source_target_pairs={{0,4},{12,8},{1,5},{13,9},{2,6},{14,10},{3,7},{15,11},{16,20},{28,... | collective-permute-start | bytes 1572872 | tf_op jit(solution)/shard_map/ppermute | solution.py:250
  68.3 6.5 %collective-permute-start.11 = (bf16[256,1024]{1,0:T(8,128)(2,1)S(1)}, bf16[256,1024]{1,0:T(8,128)(2,1)S(1)}, u32[]{:S(2)}, u32[]{:S(2)}) collective-permute-start(bf16[256,1024]{1,0:T(8,128)(2,1)S(1)} %add_convert_fusion.2), channel_id=1, source_target_pairs={{0,1},{1,0},{2,3},{3,2},{4,8},{5,9},{6,10},{7,11},{8,4},{9,5},{10,... | collective-permute-start | bytes 1572872 | tf_op jit(solution)/shard_map/ppermute | solution.py:253
  69.0 17.4 %collective-permute-start.9 = (bf16[256,1024]{1,0:T(8,128)(2,1)S(1)}, bf16[256,1024]{1,0:T(8,128)(2,1)S(1)}, u32[]{:S(2)}, u32[]{:S(2)}) collective-permute-start(bf16[256,1024]{1,0:T(8,128)(2,1)S(1)} %fusion.4.refs_2_), channel_id=1, source_target_pairs={{4,0},{8,12},{5,1},{9,13},{6,2},{10,14},{7,3},{11,15},{20,16},{24,... | collective-permute-start | bytes 1572872 | tf_op jit(solution)/shard_map/ppermute | solution.py:258
  73.6 27.1 %collective-permute-start.13 = (bf16[256,1024]{1,0:T(8,128)(2,1)S(1)}, bf16[256,1024]{1,0:T(8,128)(2,1)S(1)}, u32[]{:S(2)}, u32[]{:S(2)}) collective-permute-start(bf16[256,1024]{1,0:T(8,128)(2,1)S(1)} %add_convert_fusion.1), channel_id=1, source_target_pairs={{0,1},{1,0},{2,3},{3,2},{4,8},{5,9},{6,10},{7,11},{8,4},{9,5},{10,... | collective-permute-start | bytes 1572872 | tf_op jit(solution)/shard_map/ppermute | solution.py:253
  74.9 27.8 %collective-permute-start.16 = (bf16[256,768]{1,0:T(8,128)(2,1)S(1)}, bf16[256,768]{1,0:T(8,128)(2,1)S(1)}, u32[]{:S(2)}, u32[]{:S(2)}) collective-permute-start(bf16[256,768]{1,0:T(8,128)(2,1)S(1)} %convolution_convert_fusion.4), channel_id=1, source_target_pairs={{0,4},{12,8},{1,5},{13,9},{2,6},{14,10},{3,7},{15,11},{16,20},{28,... | collective-permute-start | bytes 1179656 | tf_op jit(solution)/shard_map/ppermute | solution.py:250
  84.5 2.0 %copy-start.1 = (bf16[6144,128]{1,0:T(8,128)(2,1)S(1)}, bf16[6144,128]{1,0:T(8,128)(2,1)}, u32[]{:S(2)}) copy-start(bf16[6144,128]{1,0:T(8,128)(2,1)} %refs_4_.1) | copy-start | bytes 4718596
  85.2 18.8 %collective-permute-start.14 = (bf16[256,1024]{1,0:T(8,128)(2,1)S(1)}, bf16[256,1024]{1,0:T(8,128)(2,1)S(1)}, u32[]{:S(2)}, u32[]{:S(2)}) collective-permute-start(bf16[256,1024]{1,0:T(8,128)(2,1)S(1)} %fusion.9.refs_7_.refs_1_), channel_id=1, source_target_pairs={{4,0},{8,12},{5,1},{9,13},{6,2},{10,14},{7,3},{11,15},{20,16},{24,... | collective-permute-start | bytes 1572872 | tf_op jit(solution)/shard_map/ppermute | solution.py:258
  96.0 30.8 %collective-permute-start.18 = (bf16[256,512]{1,0:T(8,128)(2,1)S(1)}, bf16[256,512]{1,0:T(8,128)(2,1)S(1)}, u32[]{:S(2)}, u32[]{:S(2)}) collective-permute-start(bf16[256,512]{1,0:T(8,128)(2,1)S(1)} %convolution_convert_fusion.6), channel_id=1, source_target_pairs={{0,4},{12,8},{1,5},{13,9},{2,6},{14,10},{3,7},{15,11},{16,20},{28,... | collective-permute-start | bytes 786440 | tf_op jit(solution)/shard_map/ppermute | solution.py:250
  100.6 2.7 %collective-permute-start.17 = (bf16[256,1024]{1,0:T(8,128)(2,1)S(1)}, bf16[256,1024]{1,0:T(8,128)(2,1)S(1)}, u32[]{:S(2)}, u32[]{:S(2)}) collective-permute-start(bf16[256,1024]{1,0:T(8,128)(2,1)S(1)} %add_convert_fusion), channel_id=1, source_target_pairs={{0,1},{1,0},{2,3},{3,2},{4,8},{5,9},{6,10},{7,11},{8,4},{9,5},{10,... | collective-permute-start | bytes 1572872 | tf_op jit(solution)/shard_map/ppermute | solution.py:253
  101.3 16.2 %collective-permute-start.15 = (bf16[256,1024]{1,0:T(8,128)(2,1)S(1)}, bf16[256,1024]{1,0:T(8,128)(2,1)S(1)}, u32[]{:S(2)}, u32[]{:S(2)}) collective-permute-start(bf16[256,1024]{1,0:T(8,128)(2,1)S(1)} %fusion.14.refs_2_), channel_id=1, source_target_pairs={{4,0},{8,12},{5,1},{9,13},{6,2},{10,14},{7,3},{11,15},{20,16},{24,... | collective-permute-start | bytes 1572872 | tf_op jit(solution)/shard_map/ppermute | solution.py:258
  102.8 26.2 %collective-permute-start.19 = (bf16[256,768]{1,0:T(8,128)(2,1)S(1)}, bf16[256,768]{1,0:T(8,128)(2,1)S(1)}, u32[]{:S(2)}, u32[]{:S(2)}) collective-permute-start(bf16[256,768]{1,0:T(8,128)(2,1)S(1)} %add_convert_fusion.5), channel_id=1, source_target_pairs={{0,1},{1,0},{2,3},{3,2},{4,8},{5,9},{6,10},{7,11},{8,4},{9,5},{10,... | collective-permute-start | bytes 1179656 | tf_op jit(solution)/shard_map/ppermute | solution.py:253
  126.9 3.9 %collective-permute-start.20 = (bf16[256,512]{1,0:T(8,128)(2,1)S(1)}, bf16[256,512]{1,0:T(8,128)(2,1)S(1)}, u32[]{:S(2)}, u32[]{:S(2)}) collective-permute-start(bf16[256,512]{1,0:T(8,128)(2,1)S(1)} %add_convert_fusion.6), channel_id=1, source_target_pairs={{0,1},{1,0},{2,3},{3,2},{4,8},{5,9},{6,10},{7,11},{8,4},{9,5},{10,... | collective-permute-start | bytes 786440 | tf_op jit(solution)/shard_map/ppermute | solution.py:253
  127.6 25.0 %collective-permute-start.22 = (bf16[256,1024]{1,0:T(8,128)(2,1)S(1)}, bf16[256,1024]{1,0:T(8,128)(2,1)S(1)}, u32[]{:S(2)}, u32[]{:S(2)}) collective-permute-start(bf16[256,1024]{1,0:T(8,128)(2,1)S(1)} %fusion.19.refs_9_.refs_1_), channel_id=1, source_target_pairs={{4,0},{8,12},{5,1},{9,13},{6,2},{10,14},{7,3},{11,15},{20,16},{24,... | collective-permute-start | bytes 1572872 | tf_op jit(solution)/shard_map/ppermute | solution.py:258
  129.4 23.2 %collective-permute-start.23 = (bf16[256,768]{1,0:T(8,128)(2,1)S(1)}, bf16[256,768]{1,0:T(8,128)(2,1)S(1)}, u32[]{:S(2)}, u32[]{:S(2)}) collective-permute-start(bf16[256,768]{1,0:T(8,128)(2,1)S(1)} %fusion.29.refs_2_), channel_id=1, source_target_pairs={{4,0},{8,12},{5,1},{9,13},{6,2},{10,14},{7,3},{11,15},{20,16},{24,... | collective-permute-start | bytes 1179656 | tf_op jit(solution)/shard_map/ppermute | solution.py:258
  131.1 30.0 %collective-permute-start.21 = (bf16[256,512]{1,0:T(8,128)(2,1)S(1)}, bf16[256,512]{1,0:T(8,128)(2,1)S(1)}, u32[]{:S(2)}, u32[]{:S(2)}) collective-permute-start(bf16[256,512]{1,0:T(8,128)(2,1)S(1)} %fusion.36.refs_9_.refs_1_), channel_id=1, source_target_pairs={{4,0},{8,12},{5,1},{9,13},{6,2},{10,14},{7,3},{11,15},{20,16},{24,... | collective-permute-start | bytes 786440 | tf_op jit(solution)/shard_map/ppermute | solution.py:258
  167.4 2.2 %collective-permute-start.24 = (bf16[128,2688]{1,0:T(8,128)(2,1)S(1)}, bf16[128,2688]{1,0:T(8,128)(2,1)S(1)}, u32[]{:S(2)}, u32[]{:S(2)}) collective-permute-start(bf16[128,2688]{1,0:T(8,128)(2,1)S(1)} %pad_maximum_fusion), channel_id=1, source_target_pairs={{0,1},{1,0},{2,3},{3,2},{4,5},{5,4},{6,7},{7,6},{8,9},{9,8},{10,11... | collective-permute-start | bytes 2064392 | tf_op jit(solution)/shard_map/ppermute | solution.py:239
  169.7 10.3 %copy-start.10 = (f32[2560]{0:T(1024)S(1)}, f32[2560]{0:T(1024)}, u32[]{:S(2)}) copy-start(f32[2560]{0:T(1024)} %param.19) | copy-start | bytes 30724
  169.8 10.2 %collective-permute-start.25 = (bf16[64,2688]{1,0:T(8,128)(2,1)S(1)}, bf16[64,2688]{1,0:T(8,128)(2,1)S(1)}, u32[]{:S(2)}, u32[]{:S(2)}) collective-permute-start(bf16[64,2688]{1,0:T(8,128)(2,1)S(1)} %slice.160), channel_id=1, source_target_pairs={{0,2},{1,3},{2,0},{3,1},{4,6},{5,7},{6,4},{7,5},{8,10},{9,11},{10,... | collective-permute-start | bytes 1032200 | tf_op jit(solution)/shard_map/ppermute | solution.py:239

commit v6 on v1

v6 whole, which is shorter than its diff:
```python
import jax
import jax.numpy as jnp
from jax import lax
from jax.sharding import PartitionSpec as P

ADAPTER_RANK = 16
ADAPTER_COUNT = 8
JOBS = 4
LANES = 128
CHUNKS = 12
LAG = 3
GROUP = 3
F32 = jnp.float32
BF16 = jnp.bfloat16


def gelu_tanh(values):
    return (
        0.5
        * values
        * (1.0 + jnp.tanh(0.7978845608 * (values + 0.044715 * values * values * values)))
    )


def token_mask(token_job_index, job_adapter_index):
    one_hot = token_job_index[:, None] == jnp.arange(JOBS, dtype=jnp.int32)[None, :]
    chosen = jnp.sum(jnp.where(one_hot, job_adapter_index[None, :], 0), axis=1)
    slot_ids = jnp.arange(ADAPTER_COUNT * ADAPTER_RANK, dtype=jnp.int32) // ADAPTER_RANK
    return slot_ids[None, :] == chosen[:, None]


def dot(left, right):
    return jnp.dot(left, right, preferred_element_type=F32)


def tie(value, after):
    return lax.optimization_barrier((value, after))[0]


def chunk_spans(hidden):
    units = hidden // LANES
    count = max(n for n in range(1, CHUNKS + 1) if units % n == 0)
    width = hidden // count
    return [(start, width) for start in range(0, hidden, width)]


def activate(summed, low_in, first_up_maps, first_bias, span):
    start, width = span
    part = slice(start, start + width)
    before = summed + first_bias[None, part] + dot(low_in, first_up_maps[:, part])
    return gelu_tanh(before).astype(BF16)


def hidden_plain(tokens, mask, first_weight, first_bias, first_down_maps, first_up_maps):
    width = first_weight.shape[1]
    joined = jnp.concatenate([dot(tokens, first_weight), dot(tokens, first_down_maps)], axis=1)
    summed = lax.psum_scatter(
        joined.astype(BF16), "row", scatter_dimension=0, tiled=True
    ).astype(F32)
    rows = summed.shape[0]
    own_mask = lax.dynamic_slice_in_dim(mask, lax.axis_index("row") * rows, rows, 0)
    low_in = jnp.where(own_mask, summed[:, width:], 0.0).astype(BF16)
    states = activate(summed[:, :width], low_in, first_up_maps, first_bias, (0, width))
    return lax.all_gather(states, "row", axis=0, tiled=True)


def make_local(n_group, n_row, n_col):
    chips = n_col // 2

    def place_of(group, row, col):
        return (group * n_row + row) * n_col + col

    cross_pairs = []
    for group in range(n_group):
        for row in range(n_row):
            for col in range(n_col):
                if n_row == 4 and row in (1, 2):
                    other = place_of(group, 3 - row, col)
                else:
                    other = place_of(group, row, col ^ 1)
                cross_pairs.append((place_of(group, row, col), other))

    def col_swap(value, flip):
        return lax.ppermute(value, "col", [(i, i ^ flip) for i in range(n_col)])

    def end_swap(value):
        return lax.ppermute(value, "row", [(i, i ^ 1) for i in range(n_row)])

    def cross(value):
        return lax.ppermute(value, ("group", "row", "col"), cross_pairs)

    def gather_tokens(tokens):
        shards = [tokens, col_swap(tokens, 1)]
        for step in range(1, chips):
            far = col_swap(tokens, 2 * step)
            shards += [far, col_swap(far, 1)]
        return jnp.concatenate(shards, axis=0)

    def pipeline(
        gathered,
        mask,
        first_weight,
        first_bias,
        first_down_maps,
        first_up_maps,
        second_weight,
        second_down_maps,
    ):
        spans = chunk_spans(first_weight.shape[1])
        count = len(spans)
        place = lax.axis_index("row")
        is_end = (place == 0) | (place == 3)
        last = gathered
        partials, payloads, swaps, sums, crosses = {}, {}, {}, {}, {}
        total, low_total, low_in = None, None, None
        ready = []

        def start_chunk(t):
            nonlocal last
            start, width = spans[t]
            x = tie(gathered, last)
            value = dot(x, first_weight[:, start : start + width]).astype(BF16)
            if t == 0:
                value = jnp.concatenate([value, dot(x, first_down_maps).astype(BF16)], axis=1)
            partials[t] = value
            last = value

        def send(t, value):
            payloads[t] = value
            swaps[t] = end_swap(value)

        for t in range(min(LAG, count)):
            start_chunk(t)
            if t < LAG - 1:
                send(t, partials[t])
        for t in range(count + LAG):
            if t < count:
                ours = tie(partials[t], last).astype(F32)
                sums[t] = (ours + swaps[t].astype(F32)).astype(BF16)
                last = sums[t]
                crosses[t] = cross(sums[t])
            if t == 0:
                send(LAG - 1, partials[LAG - 1])
            if 0 <= t - 1 < count:
                k = t - 1
                width = spans[k][1]
                summed = tie(sums[k], last).astype(F32) + crosses[k].astype(F32)
                if k == 0:
                    low_in = jnp.where(mask, summed[:, width:], 0.0).astype(BF16)
                    summed = summed[:, :width]
                value = activate(summed, low_in, first_up_maps, first_bias, spans[k])
                if k + LAG < count:
                    value = jnp.where(is_end, partials[k + LAG], value)
                last = value
                send(k + LAG, value)
            if t + LAG < count:
                start_chunk(t + LAG)
            if t >= LAG:
                ready.append(t - LAG)
                if len(ready) == GROUP or t - LAG >= count - 1:
                    own = [payloads[k + LAG] for k in ready]
                    come = [swaps[k + LAG] for k in ready]
                    states = jnp.where(
                        is_end, jnp.concatenate(come, axis=1), jnp.concatenate(own, axis=1)
                    )
                    states = tie(states, last)
                    part = slice(spans[ready[0]][0], spans[ready[-1]][0] + spans[ready[-1]][1])
                    value = dot(states, second_weight[part])
                    low = dot(states, second_down_maps[part])
                    total = value if total is None else total + value
                    low_total = low if low_total is None else low_total + low
                    last = low_total
                    ready = []
        return total, low_total

    def local(
        tokens,
        token_job_index,
        job_adapter_index,
        first_weight,
        first_bias,
        first_down_maps,
        first_up_maps,
        second_weight,
        second_bias,
        second_down_maps,
        second_up_maps,
    ):
        rows = tokens.shape[0]
        out_width = second_weight.shape[1]
        mine = lax.axis_index("col")
        mask_all = token_mask(token_job_index, job_adapter_index)
        mask = jnp.concatenate(
            [
                lax.dynamic_slice_in_dim(mask_all, (mine ^ i) * rows, rows, 0)
                for i in range(n_col)
            ],
            axis=0,
        )
        gathered = gather_tokens(tokens)
        first = (first_weight, first_bias, first_down_maps, first_up_maps)
        if n_row == 4:
            total, low_total = pipeline(gathered, mask, *first, second_weight, second_down_maps)
        else:
            states = hidden_plain(gathered, mask, *first)
            total, low_total = dot(states, second_weight), dot(states, second_down_maps)
        outputs = jnp.concatenate([total, low_total], axis=1)
        blocks = [outputs[i * rows : (i + 1) * rows] for i in range(n_col)]
        ours = jnp.concatenate(blocks[0::2], axis=0)
        theirs = jnp.concatenate(blocks[1::2], axis=0).astype(BF16)
        ours = ours + col_swap(theirs, 1).astype(F32)
        result = ours[:rows]
        for step in range(1, chips):
            piece = ours[step * rows : (step + 1) * rows].astype(BF16)
            result = result + col_swap(piece, 2 * step).astype(F32)
        low_out = jnp.where(mask[:rows], result[:, out_width:], 0.0).astype(BF16)
        layer_output = result[:, :out_width] + second_bias[None, :] + dot(low_out, second_up_maps)
        return layer_output.astype(BF16)

    return local


def solution(mesh):
    shape = mesh.shape
    return jax.shard_map(
        make_local(shape["group"], shape["row"], shape["col"]),
        mesh=mesh,
        in_specs=(
            P(("group", "col"), "row"),
            P("group"),
            P("group"),
            P("row", "col"),
            P("col"),
            P("row", None),
            P(None, "col"),
            P("col", "row"),
            P("row"),
            P("col", None),
            P(None, "row"),
        ),
        out_specs=P(("group", "col"), "row"),
        check_vma=False,
    )
```

time: 260 us -> 156 us (0.60)
  waiting for transfers between devices: 156 us -> 33.1 us
  matrix products: 54.7 us -> 69.6 us
  other arithmetic: 2.33 us -> 5.93 us
    ppermute x24 -> x27, waiting for transfers between devices: 138 us -> 16.4 us  [the longest x15 16.3 us: end_swap(): return lax.ppermute(value, 'row', [(i, i ^ 1) for i in range(n_row)])]
    dot_general x34, matrix products: 54.7 us -> 69.6 us  [dot(): return jnp.dot(left, right, preferred_element_type=F32)]
    ppermute x24 -> x27, starting transfers between devices: 38.4 us -> 38.2 us  [the longest x15 37.1 us: end_swap(): return lax.ppermute(value, 'row', [(i, i ^ 1) for i in range(n_row)])]
  transfers between devices with their start and end apart: 29 -> 32, of which waited for: 14 -> 9; matrix products, arithmetic and copies ran while one was open for 13% -> 44% of each run, Pallas kernels for 0% -> 0%
where the time goes in v6:
time: 156 us; the launch traced here: 155 us
  matrix products  69.6 us (45%)
  starting transfers between devices  42.7 us (27%)
  waiting for transfers between devices  33.1 us (21%)
  other arithmetic  5.93 us (4%)
  local copies, waits for them, and re-layouts  2.9 us (2%)
    dot_general x34, matrix products, dot(): return jnp.dot(left, right, preferred_element_type=F32)  69.6 us
    ppermute x15, starting transfers between devices, end_swap(): return lax.ppermute(value, 'row', [(i, i ^ 1) for i in range(n_row)])  37.1 us
    ppermute x5, waiting for transfers between devices, col_swap(): return lax.ppermute(value, 'col', [(i, i ^ flip) for i in range(n_col)])  16.8 us
    ppermute x15, waiting for transfers between devices, end_swap(): return lax.ppermute(value, 'row', [(i, i ^ 1) for i in range(n_row)])  16.3 us
    ppermute x5, starting transfers between devices, col_swap(): return lax.ppermute(value, 'col', [(i, i ^ flip) for i in range(n_col)])  4.57 us
  transfers between devices with their start and end apart: 32, of which 9 were waited for; matrix products, arithmetic and copies ran while one was open for 44% of the time, Pallas kernels for 0%

profile of v6, /device:TPU:0, one launch (start us, length us, event | category | flops | bytes accessed | tf_op | source)
XLA Modules:
  0.0 155.1 jit_solution(16273088871110508601)
XLA Ops:
  0.0 2.9 %collective-permute-start.1 = (bf16[64,2560]{1,0:T(8,128)(2,1)}, bf16[64,2560]{1,0:T(8,128)(2,1)S(1)}, u32[]{:S(2)}, u32[]{:S(2)}) collective-permute-start(bf16[64,2560]{1,0:T(8,128)(2,1)} %param.11), channel_id=1, source_target_pairs={{0,2},{1,3},{2,0},{3,1},{4,6},{5,7},{6,4},{7,5},{8,10},{9,11},{10,... | collective-permute-start | bytes 983048 | tf_op jit(solution)/shard_map/ppermute | solution.py:84
  2.9 1.4 fusion.214
  4.4 0.8 select_reduce_fusion
  5.3 1.0 constant_dynamic-update-slice_fusion.3
  6.3 4.5 %collective-permute-done.1 = bf16[64,2560]{1,0:T(8,128)(2,1)S(1)} collective-permute-done((bf16[64,2560]{1,0:T(8,128)(2,1)}, bf16[64,2560]{1,0:T(8,128)(2,1)S(1)}, u32[]{:S(2)}, u32[]{:S(2)}) %collective-permute-start.1) | collective-permute-done | bytes 327712 | tf_op jit(solution)/shard_map/ppermute | solution.py:84
  10.9 1.6 %collective-permute-done.2 = bf16[64,2560]{1,0:T(8,128)(2,1)S(1)} collective-permute-done((bf16[64,2560]{1,0:T(8,128)(2,1)S(1)}, bf16[64,2560]{1,0:T(8,128)(2,1)S(1)}, u32[]{:S(2)}, u32[]{:S(2)}) %collective-permute-start.2) | collective-permute-done | bytes 327712 | tf_op jit(solution)/shard_map/ppermute | solution.py:84
  12.5 2.6 %fusion.42 = bf16[256,512]{1,0:T(8,128)(2,1)S(1)} fusion(bf16[256,2560]{1,0:T(8,128)(2,1)S(1)} %constant_dynamic-update-slice_fusion, bf16[2560,6144]{1,0:T(8,128)(2,1)} %param.14), kind=kOutput, calls=%fused_computation.42 | convolution fusion | flops 671219712 | bytes 4194304 | tf_op jit(solution)/shard_map/dot_general | solution.py:33
  15.2 0.5 convolution_convert_fusion
  15.7 1.9 %collective-permute-start.3 = (bf16[256,640]{1,0:T(8,128)(2,1)S(1)}, bf16[256,640]{1,0:T(8,128)(2,1)S(1)}, u32[]{:S(2)}, u32[]{:S(2)}) collective-permute-start(bf16[256,640]{1,0:T(8,128)(2,1)S(1)} %pad_maximum_fusion.2), channel_id=1, source_target_pairs={{0,4},{4,0},{8,12},{12,8},{1,5},{5,1},{9,13},{13,9},{2,6},{6,2},{1... | collective-permute-start | bytes 983048 | tf_op jit(solution)/shard_map/ppermute | solution.py:87
  17.6 2.6 %fusion.45 = bf16[256,512]{1,0:T(8,128)(2,1)S(1)} fusion(bf16[256,2560]{1,0:T(8,128)(2,1)S(1)} %constant_dynamic-update-slice_fusion, bf16[2560,6144]{1,0:T(8,128)(2,1)} %param.14), kind=kOutput, calls=%fused_computation.43 | convolution fusion | flops 671219712 | bytes 4194304 | tf_op jit(solution)/shard_map/dot_general | solution.py:33
  20.5 2.6 %fusion.48 = bf16[256,512]{1,0:T(8,128)(2,1)S(1)} fusion(bf16[256,2560]{1,0:T(8,128)(2,1)S(1)} %constant_dynamic-update-slice_fusion, bf16[2560,6144]{1,0:T(8,128)(2,1)} %param.14), kind=kOutput, calls=%fused_computation.44 | convolution fusion | flops 671219712 | bytes 4194304 | tf_op jit(solution)/shard_map/dot_general | solution.py:33
  23.1 1.9 %collective-permute-start.7 = (bf16[256,512]{1,0:T(8,128)(2,1)S(1)}, bf16[256,512]{1,0:T(8,128)(2,1)S(1)}, u32[]{:S(2)}, u32[]{:S(2)}) collective-permute-start(bf16[256,512]{1,0:T(8,128)(2,1)S(1)} %fusion.48), channel_id=1, source_target_pairs={{0,4},{4,0},{8,12},{12,8},{1,5},{5,1},{9,13},{13,9},{2,6},{6,2},{1... | collective-permute-start | bytes 786440 | tf_op jit(solution)/shard_map/ppermute | solution.py:87
  24.9 1.4 collective-permute-done.3
  26.5 2.6 %fusion.51 = bf16[256,512]{1,0:T(8,128)(2,1)S(1)} fusion(bf16[256,2560]{1,0:T(8,128)(2,1)S(1)} %constant_dynamic-update-slice_fusion, bf16[2560,6144]{1,0:T(8,128)(2,1)} %param.14), kind=kOutput, calls=%fused_computation.45 | convolution fusion | flops 671219712 | bytes 4194304 | tf_op jit(solution)/shard_map/dot_general | solution.py:33
  29.1 2.9 %collective-permute-done.4 = bf16[256,512]{1,0:T(8,128)(2,1)S(1)} collective-permute-done((bf16[256,512]{1,0:T(8,128)(2,1)S(1)}, bf16[256,512]{1,0:T(8,128)(2,1)S(1)}, u32[]{:S(2)}, u32[]{:S(2)}) %collective-permute-start.4) | collective-permute-done | bytes 262176 | tf_op jit(solution)/shard_map/ppermute | solution.py:87
  32.2 1.3 fusion.156
  33.5 5.7 %collective-permute-start.6 = (bf16[256,512]{1,0:T(8,128)(2,1)S(1)}, bf16[256,512]{1,0:T(8,128)(2,1)S(1)}, u32[]{:S(2)}, u32[]{:S(2)}) collective-permute-start(bf16[256,512]{1,0:T(8,128)(2,1)S(1)} %fusion.156), channel_id=1, source_target_pairs={{0,4},{4,0},{8,12},{12,8},{1,5},{5,1},{9,13},{13,9},{2,6},{6,2},{1... | collective-permute-start | bytes 786440 | tf_op jit(solution)/shard_map/ppermute | solution.py:87
  39.3 2.6 %fusion.54 = bf16[256,512]{1,0:T(8,128)(2,1)S(1)} fusion(bf16[256,2560]{1,0:T(8,128)(2,1)S(1)} %constant_dynamic-update-slice_fusion, bf16[2560,6144]{1,0:T(8,128)(2,1)} %param.14), kind=kOutput, calls=%fused_computation.46 | convolution fusion | flops 671219712 | bytes 4194304 | tf_op jit(solution)/shard_map/dot_general | solution.py:33
  42.0 1.3 fusion.155
  43.4 1.6 %collective-permute-start.9 = (bf16[256,512]{1,0:T(8,128)(2,1)S(1)}, bf16[256,512]{1,0:T(8,128)(2,1)S(1)}, u32[]{:S(2)}, u32[]{:S(2)}) collective-permute-start(bf16[256,512]{1,0:T(8,128)(2,1)S(1)} %fusion.155), channel_id=1, source_target_pairs={{0,4},{4,0},{8,12},{12,8},{1,5},{5,1},{9,13},{13,9},{2,6},{6,2},{1... | collective-permute-start | bytes 786440 | tf_op jit(solution)/shard_map/ppermute | solution.py:87
  45.0 2.6 %fusion.57 = bf16[256,512]{1,0:T(8,128)(2,1)S(1)} fusion(bf16[256,2560]{1,0:T(8,128)(2,1)S(1)} %constant_dynamic-update-slice_fusion, bf16[2560,6144]{1,0:T(8,128)(2,1)} %param.14), kind=kOutput, calls=%fused_computation.47 | convolution fusion | flops 671219712 | bytes 4194304 | tf_op jit(solution)/shard_map/dot_general | solution.py:33
  47.7 1.3 fusion.154
  49.0 0.8 collective-permute-start.11
  49.8 2.6 %fusion.60 = bf16[256,512]{1,0:T(8,128)(2,1)S(1)} fusion(bf16[256,2560]{1,0:T(8,128)(2,1)S(1)} %constant_dynamic-update-slice_fusion, bf16[2560,6144]{1,0:T(8,128)(2,1)} %param.14), kind=kOutput, calls=%fused_computation.48 | convolution fusion | flops 671219712 | bytes 4194304 | tf_op jit(solution)/shard_map/dot_general | solution.py:33
  52.6 0.4 collective-permute-start.13
  53.0 2.0 %fusion.153 = bf16[256,512]{1,0:T(8,128)(2,1)} fusion(bf16[256,512]{1,0:T(8,128)(2,1)S(1)} %fusion.60, bf16[256,512]{1,0:T(8,128)(2,1)S(1)} %collective-permute-done.12, bf16[256,512]{1,0:T(8,128)(2,1)S(1)} %add_convert_fusion.9, f32[512]{0:T(512)S(1)} %get-tuple-element.100, pred[]{:T(512)S(6)} %or.3, bf16[256,128]{1,0:T(8,128)(2,1)S(1)} %fusion.157, ...), kind=kOutput, calls=%fused_computation.168 | convolution fusion | flops 35520512 | bytes 1247233 | tf_op jit(solution)/shard_map/dot_general | solution.py:33
  55.1 6.5 %collective-permute-start.14 = (bf16[256,512]{1,0:T(8,128)(2,1)}, bf16[256,512]{1,0:T(8,128)(2,1)S(1)}, u32[]{:S(2)}, u32[]{:S(2)}) collective-permute-start(bf16[256,512]{1,0:T(8,128)(2,1)} %fusion.153), channel_id=1, source_target_pairs={{0,4},{4,0},{8,12},{12,8},{1,5},{5,1},{9,13},{13,9},{2,6},{6,2},{1... | collective-permute-start | bytes 786440 | tf_op jit(solution)/shard_map/ppermute | solution.py:87
  61.5 2.6 %fusion.63 = bf16[256,512]{1,0:T(8,128)(2,1)S(1)} fusion(bf16[256,2560]{1,0:T(8,128)(2,1)S(1)} %constant_dynamic-update-slice_fusion, bf16[2560,6144]{1,0:T(8,128)(2,1)} %param.14), kind=kOutput, calls=%fused_computation.49 | convolution fusion | flops 671219712 | bytes 4194304 | tf_op jit(solution)/shard_map/dot_general | solution.py:33
  64.2 0.8 add_convert_fusion.7
  65.0 2.0 %fusion.152 = bf16[256,512]{1,0:T(8,128)(2,1)} fusion(bf16[256,512]{1,0:T(8,128)(2,1)S(1)} %fusion.63, bf16[256,512]{1,0:T(8,128)(2,1)S(1)} %collective-permute-done.13, bf16[256,512]{1,0:T(8,128)(2,1)S(1)} %add_convert_fusion.8, f32[512]{0:T(512)S(1)} %get-tuple-element.99, pred[]{:T(512)S(6)} %or.3, bf16[256,128]{1,0:T(8,128)(2,1)S(1)} %fusion.157, ...), kind=kOutput, calls=%fused_computation.167 | convolution fusion | flops 35520512 | bytes 1247233 | tf_op jit(solution)/shard_map/dot_general | solution.py:33
  67.0 1.2 collective-permute-start.15
  68.2 3.3 %fusion.66 = bf16[256,512]{1,0:T(8,128)(2,1)} fusion(bf16[256,2560]{1,0:T(8,128)(2,1)S(1)} %constant_dynamic-update-slice_fusion, bf16[2560,6144]{1,0:T(8,128)(2,1)} %param.14), kind=kOutput, calls=%fused_computation.50 | convolution fusion | flops 671219712 | bytes 4194304 | tf_op jit(solution)/shard_map/dot_general | solution.py:33
  71.7 1.4 fusion.146
  73.2 1.0 add_convert_fusion.6
  74.3 1.6 %fusion.151 = bf16[256,512]{1,0:T(8,128)(2,1)S(1)} fusion(bf16[256,512]{1,0:T(8,128)(2,1)} %fusion.66, bf16[256,512]{1,0:T(8,128)(2,1)} %collective-permute-done.16, bf16[256,512]{1,0:T(8,128)(2,1)} %add_convert_fusion.7, f32[512]{0:T(512)} %get-tuple-element.98, pred[]{:T(512)S(6)} %or.3, bf16[256,128]{1,0:T(8,128)(2,1)} %copy-done.7, ...), kind=kOutput, calls=%fused_computation.166 | convolution fusion | flops 35520512 | bytes 1247233 | tf_op jit(solution)/shard_map/dot_general | solution.py:33
  76.0 2.0 %collective-permute-start.17 = (bf16[256,512]{1,0:T(8,128)(2,1)S(1)}, bf16[256,512]{1,0:T(8,128)(2,1)S(1)}, u32[]{:S(2)}, u32[]{:S(2)}) collective-permute-start(bf16[256,512]{1,0:T(8,128)(2,1)S(1)} %fusion.151), channel_id=1, source_target_pairs={{0,4},{4,0},{8,12},{12,8},{1,5},{5,1},{9,13},{13,9},{2,6},{6,2},{1... | collective-permute-start | bytes 786440 | tf_op jit(solution)/shard_map/ppermute | solution.py:87
  78.0 2.6 %fusion.69 = bf16[256,512]{1,0:T(8,128)(2,1)S(1)} fusion(bf16[256,2560]{1,0:T(8,128)(2,1)S(1)} %constant_dynamic-update-slice_fusion, bf16[2560,6144]{1,0:T(8,128)(2,1)} %param.14), kind=kOutput, calls=%fused_computation.51 | convolution fusion | flops 671219712 | bytes 4194304 | tf_op jit(solution)/shard_map/dot_general | solution.py:33
  80.7 0.4 fusion.150
  81.2 2.9 %collective-permute-start.20 = (bf16[256,512]{1,0:T(8,128)(2,1)S(1)}, bf16[256,512]{1,0:T(8,128)(2,1)S(1)}, u32[]{:S(2)}, u32[]{:S(2)}) collective-permute-start(bf16[256,512]{1,0:T(8,128)(2,1)S(1)} %fusion.150), channel_id=1, source_target_pairs={{0,4},{4,0},{8,12},{12,8},{1,5},{5,1},{9,13},{13,9},{2,6},{6,2},{1... | collective-permute-start | bytes 786440 | tf_op jit(solution)/shard_map/ppermute | solution.py:87
  84.0 2.6 %fusion.72 = bf16[256,512]{1,0:T(8,128)(2,1)S(1)} fusion(bf16[256,2560]{1,0:T(8,128)(2,1)S(1)} %constant_dynamic-update-slice_fusion, bf16[2560,6144]{1,0:T(8,128)(2,1)} %param.14), kind=kOutput, calls=%fused_computation.52 | convolution fusion | flops 671219712 | bytes 4194304 | tf_op jit(solution)/shard_map/dot_general | solution.py:33
  86.8 0.4 fusion.149
  87.2 3.0 %collective-permute-start.21 = (bf16[256,512]{1,0:T(8,128)(2,1)S(1)}, bf16[256,512]{1,0:T(8,128)(2,1)S(1)}, u32[]{:S(2)}, u32[]{:S(2)}) collective-permute-start(bf16[256,512]{1,0:T(8,128)(2,1)S(1)} %fusion.149), channel_id=1, source_target_pairs={{0,4},{4,0},{8,12},{12,8},{1,5},{5,1},{9,13},{13,9},{2,6},{6,2},{1... | collective-permute-start | bytes 786440 | tf_op jit(solution)/shard_map/ppermute | solution.py:87
  90.2 2.6 %fusion.75 = bf16[256,512]{1,0:T(8,128)(2,1)S(1)} fusion(bf16[256,2560]{1,0:T(8,128)(2,1)S(1)} %constant_dynamic-update-slice_fusion, bf16[2560,6144]{1,0:T(8,128)(2,1)} %param.14), kind=kOutput, calls=%fused_computation.53 | convolution fusion | flops 671219712 | bytes 4194304 | tf_op jit(solution)/shard_map/dot_general | solution.py:33
  92.8 1.4 maximum_select_fusion.1
  94.2 5.5 %fusion.4 = f32[256,2560]{1,0:T(8,128)S(1)} fusion(bf16[256,1536]{1,0:T(8,128)(2,1)S(1)} %maximum_select_fusion.1, bf16[6144,2560]{1,0:T(8,128)(2,1)} %param.18), kind=kOutput, calls=%fused_computation.4 | convolution fusion | flops 2013265920 | bytes 11272192 | tf_op jit(solution)/shard_map/dot_general | solution.py:33
  99.7 5.6 %fusion.8 = f32[256,2560]{1,0:T(8,128)S(1)} fusion(f32[256,2560]{1,0:T(8,128)S(1)} %fusion.4, bf16[256,1536]{1,0:T(8,128)(2,1)S(1)} %maximum_select_fusion, bf16[6144,2560]{1,0:T(8,128)(2,1)} %param.18), kind=kOutput, calls=%fused_computation.11 | convolution fusion | flops 2013921280 | bytes 13893632 | tf_op jit(solution)/shard_map/dot_general | solution.py:33
  105.4 0.4 convolution_add_fusion.2
  106.0 0.4 fusion.148
  106.4 0.8 collective-permute-start.23
  107.4 0.4 fusion.131
  107.8 7.3 %collective-permute-done.23 = bf16[256,512]{1,0:T(8,128)(2,1)S(1)} collective-permute-done((bf16[256,512]{1,0:T(8,128)(2,1)S(1)}, bf16[256,512]{1,0:T(8,128)(2,1)S(1)}, u32[]{:S(2)}, u32[]{:S(2)}) %collective-permute-start.23) | collective-permute-done | bytes 262176 | tf_op jit(solution)/shard_map/ppermute | solution.py:87
  115.2 1.3 collective-permute-start.26
  116.5 0.4 fusion.136
  116.9 4.3 %collective-permute-start.27 = (bf16[256,512]{1,0:T(8,128)(2,1)S(1)}, bf16[256,512]{1,0:T(8,128)(2,1)S(1)}, u32[]{:S(2)}, u32[]{:S(2)}) collective-permute-start(bf16[256,512]{1,0:T(8,128)(2,1)S(1)} %fusion.136), channel_id=1, source_target_pairs={{0,4},{4,0},{8,12},{12,8},{1,5},{5,1},{9,13},{13,9},{2,6},{6,2},{1... | collective-permute-start | bytes 786440 | tf_op jit(solution)/shard_map/ppermute | solution.py:87
  121.4 0.4 convolution_add_fusion.1
  121.8 0.4 fusion.141
  122.1 2.9 %collective-permute-start.29 = (bf16[256,512]{1,0:T(8,128)(2,1)S(1)}, bf16[256,512]{1,0:T(8,128)(2,1)S(1)}, u32[]{:S(2)}, u32[]{:S(2)}) collective-permute-start(bf16[256,512]{1,0:T(8,128)(2,1)S(1)} %fusion.141), channel_id=1, source_target_pairs={{0,4},{4,0},{8,12},{12,8},{1,5},{5,1},{9,13},{13,9},{2,6},{6,2},{1... | collective-permute-start | bytes 786440 | tf_op jit(solution)/shard_map/ppermute | solution.py:87
  125.0 5.5 %fusion.11 = f32[256,2560]{1,0:T(8,128)S(1)} fusion(f32[256,2560]{1,0:T(8,128)S(1)} %fusion.8, bf16[256,1536]{1,0:T(8,128)(2,1)S(1)} %maximum_select_fusion.2, bf16[6144,2560]{1,0:T(8,128)(2,1)} %param.18), kind=kOutput, calls=%fused_computation.12 | convolution fusion | flops 2013921280 | bytes 13893632 | tf_op jit(solution)/shard_map/dot_general | solution.py:33
  130.6 4.6 %collective-permute-done.29 = bf16[256,512]{1,0:T(8,128)(2,1)S(1)} collective-permute-done((bf16[256,512]{1,0:T(8,128)(2,1)S(1)}, bf16[256,512]{1,0:T(8,128)(2,1)S(1)}, u32[]{:S(2)}, u32[]{:S(2)}) %collective-permute-start.29) | collective-permute-done | bytes 262176 | tf_op jit(solution)/shard_map/ppermute | solution.py:87
  135.7 5.5 %fusion.14 = f32[256,2560]{1,0:T(8,128)S(1)} fusion(f32[256,2560]{1,0:T(8,128)S(1)} %fusion.11, bf16[256,1536]{1,0:T(8,128)(2,1)S(1)} %maximum_select_fusion.3, bf16[6144,2560]{1,0:T(8,128)(2,1)} %param.18), kind=kOutput, calls=%fused_computation.13 | convolution fusion | flops 2013921280 | bytes 13893632 | tf_op jit(solution)/shard_map/dot_general | solution.py:33
  141.7 2.0 %collective-permute-done.30 = bf16[128,2688]{1,0:T(8,128)(2,1)S(1)} collective-permute-done((bf16[128,2688]{1,0:T(8,128)(2,1)S(1)}, bf16[128,2688]{1,0:T(8,128)(2,1)S(1)}, u32[]{:S(2)}, u32[]{:S(2)}) %collective-permute-start.30) | collective-permute-done | bytes 688160 | tf_op jit(solution)/shard_map/ppermute | solution.py:84
  143.9 1.6 %collective-permute-start.31 = (bf16[64,2688]{1,0:T(8,128)(2,1)S(1)}, bf16[64,2688]{1,0:T(8,128)(2,1)S(1)}, u32[]{:S(2)}, u32[]{:S(2)}) collective-permute-start(bf16[64,2688]{1,0:T(8,128)(2,1)S(1)} %slice.384), channel_id=1, source_target_pairs={{0,2},{1,3},{2,0},{3,1},{4,6},{5,7},{6,4},{7,5},{8,10},{9,11},{10,... | collective-permute-start | bytes 1032200 | tf_op jit(solution)/shard_map/ppermute | solution.py:84
  145.4 8.6 %collective-permute-done.31 = bf16[64,2688]{1,0:T(8,128)(2,1)S(1)} collective-permute-done((bf16[64,2688]{1,0:T(8,128)(2,1)S(1)}, bf16[64,2688]{1,0:T(8,128)(2,1)S(1)}, u32[]{:S(2)}, u32[]{:S(2)}) %collective-permute-start.31) | collective-permute-done | bytes 344096 | tf_op jit(solution)/shard_map/ppermute | solution.py:84
  154.1 1.0 fusion.81
  (100 shorter events, 3.9 us)
Async XLA Ops:
  0.0 154.1 %copy-start = (bf16[128,2560]{1,0:T(8,128)(2,1)S(1)}, bf16[128,2560]{1,0:T(8,128)(2,1)}, u32[]{:S(2)}) copy-start(bf16[128,2560]{1,0:T(8,128)(2,1)} %param.21) | copy-start | bytes 1966084
  0.0 10.9 %collective-permute-start.1 = (bf16[64,2560]{1,0:T(8,128)(2,1)}, bf16[64,2560]{1,0:T(8,128)(2,1)S(1)}, u32[]{:S(2)}, u32[]{:S(2)}) collective-permute-start(bf16[64,2560]{1,0:T(8,128)(2,1)} %param.11), channel_id=1, source_target_pairs={{0,2},{1,3},{2,0},{3,1},{4,6},{5,7},{6,4},{7,5},{8,10},{9,11},{10,... | collective-permute-start | bytes 983048 | tf_op jit(solution)/shard_map/ppermute | solution.py:84
  2.9 7.9 %collective-permute-start = (bf16[64,2560]{1,0:T(8,128)(2,1)}, bf16[64,2560]{1,0:T(8,128)(2,1)S(1)}, u32[]{:S(2)}, u32[]{:S(2)}) collective-permute-start(bf16[64,2560]{1,0:T(8,128)(2,1)} %param.11), channel_id=1, source_target_pairs={{0,1},{1,0},{2,3},{3,2},{4,5},{5,4},{6,7},{7,6},{8,9},{9,8},{10,11... | collective-permute-start | bytes 983048 | tf_op jit(solution)/shard_map/ppermute | solution.py:84
  10.9 1.6 %collective-permute-start.2 = (bf16[64,2560]{1,0:T(8,128)(2,1)S(1)}, bf16[64,2560]{1,0:T(8,128)(2,1)S(1)}, u32[]{:S(2)}, u32[]{:S(2)}) collective-permute-start(bf16[64,2560]{1,0:T(8,128)(2,1)S(1)} %collective-permute-done.1), channel_id=1, source_target_pairs={{0,1},{1,0},{2,3},{3,2},{4,5},{5,4},{6,7},{7,6},{8,9},{9,8},{10,11... | collective-permute-start | bytes 983048 | tf_op jit(solution)/shard_map/ppermute | solution.py:84
  12.5 2.7 %copy-start.2 = (bf16[2560,128]{1,0:T(8,128)(2,1)S(1)}, bf16[2560,128]{1,0:T(8,128)(2,1)}, u32[]{:S(2)}) copy-start(bf16[2560,128]{1,0:T(8,128)(2,1)} %param.16) | copy-start | bytes 1966084
  15.7 10.6 %collective-permute-start.3 = (bf16[256,640]{1,0:T(8,128)(2,1)S(1)}, bf16[256,640]{1,0:T(8,128)(2,1)S(1)}, u32[]{:S(2)}, u32[]{:S(2)}) collective-permute-start(bf16[256,640]{1,0:T(8,128)(2,1)S(1)} %pad_maximum_fusion.2), channel_id=1, source_target_pairs={{0,4},{4,0},{8,12},{12,8},{1,5},{5,1},{9,13},{13,9},{2,6},{6,2},{1... | collective-permute-start | bytes 983048 | tf_op jit(solution)/shard_map/ppermute | solution.py:87
  20.2 11.7 %collective-permute-start.4 = (bf16[256,512]{1,0:T(8,128)(2,1)S(1)}, bf16[256,512]{1,0:T(8,128)(2,1)S(1)}, u32[]{:S(2)}, u32[]{:S(2)}) collective-permute-start(bf16[256,512]{1,0:T(8,128)(2,1)S(1)} %fusion.45), channel_id=1, source_target_pairs={{0,4},{4,0},{8,12},{12,8},{1,5},{5,1},{9,13},{13,9},{2,6},{6,2},{1... | collective-permute-start | bytes 786440 | tf_op jit(solution)/shard_map/ppermute | solution.py:87
  23.1 18.8 %collective-permute-start.7 = (bf16[256,512]{1,0:T(8,128)(2,1)S(1)}, bf16[256,512]{1,0:T(8,128)(2,1)S(1)}, u32[]{:S(2)}, u32[]{:S(2)}) collective-permute-start(bf16[256,512]{1,0:T(8,128)(2,1)S(1)} %fusion.48), channel_id=1, source_target_pairs={{0,4},{4,0},{8,12},{12,8},{1,5},{5,1},{9,13},{13,9},{2,6},{6,2},{1... | collective-permute-start | bytes 786440 | tf_op jit(solution)/shard_map/ppermute | solution.py:87
  26.4 5.7 %collective-permute-start.5 = (bf16[256,640]{1,0:T(8,128)(2,1)S(1)}, bf16[256,640]{1,0:T(8,128)(2,1)S(1)}, u32[]{:S(2)}, u32[]{:S(2)}) collective-permute-start(bf16[256,640]{1,0:T(8,128)(2,1)S(1)} %add_convert_fusion), channel_id=1, source_target_pairs={{0,1},{1,0},{2,3},{3,2},{4,8},{5,9},{6,10},{7,11},{8,4},{9,5},{10,... | collective-permute-start | bytes 983048 | tf_op jit(solution)/shard_map/ppermute | solution.py:90
  32.0 10.0 %collective-permute-start.8 = (bf16[256,512]{1,0:T(8,128)(2,1)S(1)}, bf16[256,512]{1,0:T(8,128)(2,1)S(1)}, u32[]{:S(2)}, u32[]{:S(2)}) collective-permute-start(bf16[256,512]{1,0:T(8,128)(2,1)S(1)} %add_convert_fusion.11), channel_id=1, source_target_pairs={{0,1},{1,0},{2,3},{3,2},{4,8},{5,9},{6,10},{7,11},{8,4},{9,5},{10,... | collective-permute-start | bytes 786440 | tf_op jit(solution)/shard_map/ppermute | solution.py:90
  32.2 32.7 %copy-start.7 = (bf16[256,128]{1,0:T(8,128)(2,1)}, bf16[256,128]{1,0:T(8,128)(2,1)S(1)}, u32[]{:S(2)}) copy-start(bf16[256,128]{1,0:T(8,128)(2,1)S(1)} %fusion.157) | copy-start | bytes 196612
  33.5 14.0 %collective-permute-start.6 = (bf16[256,512]{1,0:T(8,128)(2,1)S(1)}, bf16[256,512]{1,0:T(8,128)(2,1)S(1)}, u32[]{:S(2)}, u32[]{:S(2)}) collective-permute-start(bf16[256,512]{1,0:T(8,128)(2,1)S(1)} %fusion.156), channel_id=1, source_target_pairs={{0,4},{4,0},{8,12},{12,8},{1,5},{5,1},{9,13},{13,9},{2,6},{6,2},{1... | collective-permute-start | bytes 786440 | tf_op jit(solution)/shard_map/ppermute | solution.py:87
  41.9 5.7 %collective-permute-start.10 = (bf16[256,512]{1,0:T(8,128)(2,1)S(1)}, bf16[256,512]{1,0:T(8,128)(2,1)S(1)}, u32[]{:S(2)}, u32[]{:S(2)}) collective-permute-start(bf16[256,512]{1,0:T(8,128)(2,1)S(1)} %add_convert_fusion.10), channel_id=1, source_target_pairs={{0,1},{1,0},{2,3},{3,2},{4,8},{5,9},{6,10},{7,11},{8,4},{9,5},{10,... | collective-permute-start | bytes 786440 | tf_op jit(solution)/shard_map/ppermute | solution.py:90
  43.4 9.2 %collective-permute-start.9 = (bf16[256,512]{1,0:T(8,128)(2,1)S(1)}, bf16[256,512]{1,0:T(8,128)(2,1)S(1)}, u32[]{:S(2)}, u32[]{:S(2)}) collective-permute-start(bf16[256,512]{1,0:T(8,128)(2,1)S(1)} %fusion.155), channel_id=1, source_target_pairs={{0,4},{4,0},{8,12},{12,8},{1,5},{5,1},{9,13},{13,9},{2,6},{6,2},{1... | collective-permute-start | bytes 786440 | tf_op jit(solution)/shard_map/ppermute | solution.py:87
  49.0 15.2 %collective-permute-start.11 = (bf16[256,512]{1,0:T(8,128)(2,1)S(1)}, bf16[256,512]{1,0:T(8,128)(2,1)S(1)}, u32[]{:S(2)}, u32[]{:S(2)}) collective-permute-start(bf16[256,512]{1,0:T(8,128)(2,1)S(1)} %fusion.154), channel_id=1, source_target_pairs={{0,4},{4,0},{8,12},{12,8},{1,5},{5,1},{9,13},{13,9},{2,6},{6,2},{1... | collective-permute-start | bytes 786440 | tf_op jit(solution)/shard_map/ppermute | solution.py:87
  49.8 3.3 %collective-permute-start.12 = (bf16[256,512]{1,0:T(8,128)(2,1)S(1)}, bf16[256,512]{1,0:T(8,128)(2,1)S(1)}, u32[]{:S(2)}, u32[]{:S(2)}) collective-permute-start(bf16[256,512]{1,0:T(8,128)(2,1)S(1)} %add_convert_fusion.9), channel_id=1, source_target_pairs={{0,1},{1,0},{2,3},{3,2},{4,8},{5,9},{6,10},{7,11},{8,4},{9,5},{10,... | collective-permute-start | bytes 786440 | tf_op jit(solution)/shard_map/ppermute | solution.py:90
  52.4 11.8 %copy-start.3 = (bf16[256,512]{1,0:T(8,128)(2,1)}, bf16[256,512]{1,0:T(8,128)(2,1)S(1)}, u32[]{:S(2)}) copy-start(bf16[256,512]{1,0:T(8,128)(2,1)S(1)} %fusion.60) | copy-start | bytes 786436
  52.6 12.4 %collective-permute-start.13 = (bf16[256,512]{1,0:T(8,128)(2,1)S(1)}, bf16[256,512]{1,0:T(8,128)(2,1)S(1)}, u32[]{:S(2)}, u32[]{:S(2)}) collective-permute-start(bf16[256,512]{1,0:T(8,128)(2,1)S(1)} %add_convert_fusion.8), channel_id=1, source_target_pairs={{0,1},{1,0},{2,3},{3,2},{4,8},{5,9},{6,10},{7,11},{8,4},{9,5},{10,... | collective-permute-start | bytes 786440 | tf_op jit(solution)/shard_map/ppermute | solution.py:90
  55.1 18.1 %collective-permute-start.14 = (bf16[256,512]{1,0:T(8,128)(2,1)}, bf16[256,512]{1,0:T(8,128)(2,1)S(1)}, u32[]{:S(2)}, u32[]{:S(2)}) collective-permute-start(bf16[256,512]{1,0:T(8,128)(2,1)} %fusion.153), channel_id=1, source_target_pairs={{0,4},{4,0},{8,12},{12,8},{1,5},{5,1},{9,13},{13,9},{2,6},{6,2},{1... | collective-permute-start | bytes 786440 | tf_op jit(solution)/shard_map/ppermute | solution.py:87
  64.1 4.1 %copy-start.4 = (bf16[256,512]{1,0:T(8,128)(2,1)}, bf16[256,512]{1,0:T(8,128)(2,1)S(1)}, u32[]{:S(2)}) copy-start(bf16[256,512]{1,0:T(8,128)(2,1)S(1)} %fusion.63) | copy-start | bytes 786436
  65.0 9.3 %collective-permute-start.16 = (bf16[256,512]{1,0:T(8,128)(2,1)}, bf16[256,512]{1,0:T(8,128)(2,1)}, u32[]{:S(2)}, u32[]{:S(2)}) collective-permute-start(bf16[256,512]{1,0:T(8,128)(2,1)} %add_convert_fusion.7), channel_id=1, source_target_pairs={{0,1},{1,0},{2,3},{3,2},{4,8},{5,9},{6,10},{7,11},{8,4},{9,5},{10,... | collective-permute-start | bytes 786440 | tf_op jit(solution)/shard_map/ppermute | solution.py:90
  67.0 13.5 %collective-permute-start.15 = (bf16[256,512]{1,0:T(8,128)(2,1)}, bf16[256,512]{1,0:T(8,128)(2,1)S(1)}, u32[]{:S(2)}, u32[]{:S(2)}) collective-permute-start(bf16[256,512]{1,0:T(8,128)(2,1)} %fusion.152), channel_id=1, source_target_pairs={{0,4},{4,0},{8,12},{12,8},{1,5},{5,1},{9,13},{13,9},{2,6},{6,2},{1... | collective-permute-start | bytes 786440 | tf_op jit(solution)/shard_map/ppermute | solution.py:87
  74.2 6.5 %collective-permute-start.18 = (bf16[256,512]{1,0:T(8,128)(2,1)S(1)}, bf16[256,512]{1,0:T(8,128)(2,1)S(1)}, u32[]{:S(2)}, u32[]{:S(2)}) collective-permute-start(bf16[256,512]{1,0:T(8,128)(2,1)S(1)} %add_convert_fusion.6), channel_id=1, source_target_pairs={{0,1},{1,0},{2,3},{3,2},{4,8},{5,9},{6,10},{7,11},{8,4},{9,5},{10,... | collective-permute-start | bytes 786440 | tf_op jit(solution)/shard_map/ppermute | solution.py:90
  75.9 4.6 %copy-start.5 = (bf16[256,512]{1,0:T(8,128)(2,1)S(1)}, bf16[256,512]{1,0:T(8,128)(2,1)}, u32[]{:S(2)}) copy-start(bf16[256,512]{1,0:T(8,128)(2,1)} %copy-done.4) | copy-start | bytes 786436
  75.9 4.8 %copy-start.8 = (bf16[256,128]{1,0:T(8,128)(2,1)S(1)}, bf16[256,128]{1,0:T(8,128)(2,1)}, u32[]{:S(2)}) copy-start(bf16[256,128]{1,0:T(8,128)(2,1)} %copy-done.7) | copy-start | bytes 196612
  75.9 4.8 %copy-start.13 = (f32[512]{0:T(512)S(1)}, f32[512]{0:T(512)}, u32[]{:S(2)}) copy-start(f32[512]{0:T(512)} %get-tuple-element.97) | copy-start | bytes 6148
  75.9 4.8 %copy-start.14 = (bf16[128,6144]{1,0:T(8,128)(2,1)S(1)}, bf16[128,6144]{1,0:T(8,128)(2,1)}, u32[]{:S(2)}) copy-start(bf16[128,6144]{1,0:T(8,128)(2,1)} %param.17) | copy-start | bytes 4718596
  76.0 10.7 %collective-permute-start.17 = (bf16[256,512]{1,0:T(8,128)(2,1)S(1)}, bf16[256,512]{1,0:T(8,128)(2,1)S(1)}, u32[]{:S(2)}, u32[]{:S(2)}) collective-permute-start(bf16[256,512]{1,0:T(8,128)(2,1)S(1)} %fusion.151), channel_id=1, source_target_pairs={{0,4},{4,0},{8,12},{12,8},{1,5},{5,1},{9,13},{13,9},{2,6},{6,2},{1... | collective-permute-start | bytes 786440 | tf_op jit(solution)/shard_map/ppermute | solution.py:87
  80.6 6.2 %collective-permute-start.19 = (bf16[256,512]{1,0:T(8,128)(2,1)S(1)}, bf16[256,512]{1,0:T(8,128)(2,1)S(1)}, u32[]{:S(2)}, u32[]{:S(2)}) collective-permute-start(bf16[256,512]{1,0:T(8,128)(2,1)S(1)} %add_convert_fusion.5), channel_id=1, source_target_pairs={{0,1},{1,0},{2,3},{3,2},{4,8},{5,9},{6,10},{7,11},{8,4},{9,5},{10,... | collective-permute-start | bytes 786440 | tf_op jit(solution)/shard_map/ppermute | solution.py:90
  81.2 5.5 %copy-start.6 = (bf16[256,512]{1,0:T(8,128)(2,1)S(1)}, bf16[256,512]{1,0:T(8,128)(2,1)}, u32[]{:S(2)}) copy-start(bf16[256,512]{1,0:T(8,128)(2,1)} %fusion.66) | copy-start | bytes 786436
  81.2 5.6 %copy-start.12 = (f32[512]{0:T(512)S(1)}, f32[512]{0:T(512)}, u32[]{:S(2)}) copy-start(f32[512]{0:T(512)} %get-tuple-element.96) | copy-start | bytes 6148
  81.2 24.5 %collective-permute-start.20 = (bf16[256,512]{1,0:T(8,128)(2,1)S(1)}, bf16[256,512]{1,0:T(8,128)(2,1)S(1)}, u32[]{:S(2)}, u32[]{:S(2)}) collective-permute-start(bf16[256,512]{1,0:T(8,128)(2,1)S(1)} %fusion.150), channel_id=1, source_target_pairs={{0,4},{4,0},{8,12},{12,8},{1,5},{5,1},{9,13},{13,9},{2,6},{6,2},{1... | collective-permute-start | bytes 786440 | tf_op jit(solution)/shard_map/ppermute | solution.py:87
  86.7 19.2 %collective-permute-start.22 = (bf16[256,512]{1,0:T(8,128)(2,1)S(1)}, bf16[256,512]{1,0:T(8,128)(2,1)S(1)}, u32[]{:S(2)}, u32[]{:S(2)}) collective-permute-start(bf16[256,512]{1,0:T(8,128)(2,1)S(1)} %add_convert_fusion.4), channel_id=1, source_target_pairs={{0,1},{1,0},{2,3},{3,2},{4,8},{5,9},{6,10},{7,11},{8,4},{9,5},{10,... | collective-permute-start | bytes 786440 | tf_op jit(solution)/shard_map/ppermute | solution.py:90
  87.2 20.0 %collective-permute-start.21 = (bf16[256,512]{1,0:T(8,128)(2,1)S(1)}, bf16[256,512]{1,0:T(8,128)(2,1)S(1)}, u32[]{:S(2)}, u32[]{:S(2)}) collective-permute-start(bf16[256,512]{1,0:T(8,128)(2,1)S(1)} %fusion.149), channel_id=1, source_target_pairs={{0,4},{4,0},{8,12},{12,8},{1,5},{5,1},{9,13},{13,9},{2,6},{6,2},{1... | collective-permute-start | bytes 786440 | tf_op jit(solution)/shard_map/ppermute | solution.py:87
  99.7 5.6 %copy-start.1 = (bf16[6144,128]{1,0:T(8,128)(2,1)S(1)}, bf16[6144,128]{1,0:T(8,128)(2,1)}, u32[]{:S(2)}) copy-start(bf16[6144,128]{1,0:T(8,128)(2,1)} %param.20) | copy-start | bytes 4718596
  105.3 0.7 copy-start.11
  105.8 1.6 %copy-start.10 = (f32[512]{0:T(512)S(1)}, f32[512]{0:T(512)}, u32[]{:S(2)}) copy-start(f32[512]{0:T(512)} %get-tuple-element.94) | copy-start | bytes 6148
  105.8 1.6 %collective-permute-start.24 = (bf16[256,512]{1,0:T(8,128)(2,1)S(1)}, bf16[256,512]{1,0:T(8,128)(2,1)S(1)}, u32[]{:S(2)}, u32[]{:S(2)}) collective-permute-start(bf16[256,512]{1,0:T(8,128)(2,1)S(1)} %add_convert_fusion.3), channel_id=1, source_target_pairs={{0,1},{1,0},{2,3},{3,2},{4,8},{5,9},{6,10},{7,11},{8,4},{9,5},{10,... | collective-permute-start | bytes 786440 | tf_op jit(solution)/shard_map/ppermute | solution.py:90
  106.4 8.7 %collective-permute-start.23 = (bf16[256,512]{1,0:T(8,128)(2,1)S(1)}, bf16[256,512]{1,0:T(8,128)(2,1)S(1)}, u32[]{:S(2)}, u32[]{:S(2)}) collective-permute-start(bf16[256,512]{1,0:T(8,128)(2,1)S(1)} %fusion.148), channel_id=1, source_target_pairs={{0,4},{4,0},{8,12},{12,8},{1,5},{5,1},{9,13},{13,9},{2,6},{6,2},{1... | collective-permute-start | bytes 786440 | tf_op jit(solution)/shard_map/ppermute | solution.py:87
  107.3 9.2 %collective-permute-start.25 = (bf16[256,512]{1,0:T(8,128)(2,1)S(1)}, bf16[256,512]{1,0:T(8,128)(2,1)S(1)}, u32[]{:S(2)}, u32[]{:S(2)}) collective-permute-start(bf16[256,512]{1,0:T(8,128)(2,1)S(1)} %add_convert_fusion.2), channel_id=1, source_target_pairs={{0,1},{1,0},{2,3},{3,2},{4,8},{5,9},{6,10},{7,11},{8,4},{9,5},{10,... | collective-permute-start | bytes 786440 | tf_op jit(solution)/shard_map/ppermute | solution.py:90
  115.1 6.6 %collective-permute-start.28 = (bf16[256,512]{1,0:T(8,128)(2,1)S(1)}, bf16[256,512]{1,0:T(8,128)(2,1)S(1)}, u32[]{:S(2)}, u32[]{:S(2)}) collective-permute-start(bf16[256,512]{1,0:T(8,128)(2,1)S(1)} %add_convert_fusion.1), channel_id=1, source_target_pairs={{0,1},{1,0},{2,3},{3,2},{4,8},{5,9},{6,10},{7,11},{8,4},{9,5},{10,... | collective-permute-start | bytes 786440 | tf_op jit(solution)/shard_map/ppermute | solution.py:90
  115.2 15.3 %collective-permute-start.26 = (bf16[256,512]{1,0:T(8,128)(2,1)S(1)}, bf16[256,512]{1,0:T(8,128)(2,1)S(1)}, u32[]{:S(2)}, u32[]{:S(2)}) collective-permute-start(bf16[256,512]{1,0:T(8,128)(2,1)S(1)} %fusion.131), channel_id=1, source_target_pairs={{0,4},{4,0},{8,12},{12,8},{1,5},{5,1},{9,13},{13,9},{2,6},{6,2},{1... | collective-permute-start | bytes 786440 | tf_op jit(solution)/shard_map/ppermute | solution.py:87
  116.9 13.7 %collective-permute-start.27 = (bf16[256,512]{1,0:T(8,128)(2,1)S(1)}, bf16[256,512]{1,0:T(8,128)(2,1)S(1)}, u32[]{:S(2)}, u32[]{:S(2)}) collective-permute-start(bf16[256,512]{1,0:T(8,128)(2,1)S(1)} %fusion.136), channel_id=1, source_target_pairs={{0,4},{4,0},{8,12},{12,8},{1,5},{5,1},{9,13},{13,9},{2,6},{6,2},{1... | collective-permute-start | bytes 786440 | tf_op jit(solution)/shard_map/ppermute | solution.py:87
  122.1 13.1 %collective-permute-start.29 = (bf16[256,512]{1,0:T(8,128)(2,1)S(1)}, bf16[256,512]{1,0:T(8,128)(2,1)S(1)}, u32[]{:S(2)}, u32[]{:S(2)}) collective-permute-start(bf16[256,512]{1,0:T(8,128)(2,1)S(1)} %fusion.141), channel_id=1, source_target_pairs={{0,4},{4,0},{8,12},{12,8},{1,5},{5,1},{9,13},{13,9},{2,6},{6,2},{1... | collective-permute-start | bytes 786440 | tf_op jit(solution)/shard_map/ppermute | solution.py:87
  141.5 2.2 %collective-permute-start.30 = (bf16[128,2688]{1,0:T(8,128)(2,1)S(1)}, bf16[128,2688]{1,0:T(8,128)(2,1)S(1)}, u32[]{:S(2)}, u32[]{:S(2)}) collective-permute-start(bf16[128,2688]{1,0:T(8,128)(2,1)S(1)} %pad_maximum_fusion.1), channel_id=1, source_target_pairs={{0,1},{1,0},{2,3},{3,2},{4,5},{5,4},{6,7},{7,6},{8,9},{9,8},{10,11... | collective-permute-start | bytes 2064392 | tf_op jit(solution)/shard_map/ppermute | solution.py:84
  143.8 10.3 %copy-start.9 = (f32[2560]{0:T(1024)S(1)}, f32[2560]{0:T(1024)}, u32[]{:S(2)}) copy-start(f32[2560]{0:T(1024)} %param.19) | copy-start | bytes 30724
  143.9 10.2 %collective-permute-start.31 = (bf16[64,2688]{1,0:T(8,128)(2,1)S(1)}, bf16[64,2688]{1,0:T(8,128)(2,1)S(1)}, u32[]{:S(2)}, u32[]{:S(2)}) collective-permute-start(bf16[64,2688]{1,0:T(8,128)(2,1)S(1)} %slice.384), channel_id=1, source_target_pairs={{0,2},{1,3},{2,0},{3,1},{4,6},{5,7},{6,4},{7,5},{8,10},{9,11},{10,... | collective-permute-start | bytes 1032200 | tf_op jit(solution)/shard_map/ppermute | solution.py:84

commit v7 on v6

v7 whole, which is shorter than its diff:
```python
import jax
import jax.numpy as jnp
from jax import lax
from jax.sharding import PartitionSpec as P

ADAPTER_RANK = 16
ADAPTER_COUNT = 8
JOBS = 4
LANES = 128
UNITS = 12
LAG = 3
F32 = jnp.float32
BF16 = jnp.bfloat16


def gelu_tanh(values):
    return (
        0.5
        * values
        * (1.0 + jnp.tanh(0.7978845608 * (values + 0.044715 * values * values * values)))
    )


def token_mask(token_job_index, job_adapter_index):
    one_hot = token_job_index[:, None] == jnp.arange(JOBS, dtype=jnp.int32)[None, :]
    chosen = jnp.sum(jnp.where(one_hot, job_adapter_index[None, :], 0), axis=1)
    slot_ids = jnp.arange(ADAPTER_COUNT * ADAPTER_RANK, dtype=jnp.int32) // ADAPTER_RANK
    return slot_ids[None, :] == chosen[:, None]


def dot(left, right):
    return jnp.dot(left, right, preferred_element_type=F32)


def tie(value, after):
    return lax.optimization_barrier((value, after))[0]


def activate(summed, low_in, first_up_maps, first_bias, part):
    before = summed + first_bias[None, part] + dot(low_in, first_up_maps[:, part])
    return gelu_tanh(before).astype(BF16)


def hidden_plain(tokens, mask, first_weight, first_bias, first_down_maps, first_up_maps):
    width = first_weight.shape[1]
    joined = jnp.concatenate([dot(tokens, first_weight), dot(tokens, first_down_maps)], axis=1)
    summed = lax.psum_scatter(
        joined.astype(BF16), "row", scatter_dimension=0, tiled=True
    ).astype(F32)
    rows = summed.shape[0]
    own_mask = lax.dynamic_slice_in_dim(mask, lax.axis_index("row") * rows, rows, 0)
    low_in = jnp.where(own_mask, summed[:, width:], 0.0).astype(BF16)
    states = activate(summed[:, :width], low_in, first_up_maps, first_bias, slice(0, width))
    return lax.all_gather(states, "row", axis=0, tiled=True)


def make_local(n_group, n_row, n_col):
    chips = n_col // 2

    def place_of(group, row, col):
        return (group * n_row + row) * n_col + col

    cross_pairs = []
    for group in range(n_group):
        for row in range(n_row):
            for col in range(n_col):
                if n_row == 4 and row in (1, 2):
                    other = place_of(group, 3 - row, col)
                else:
                    other = place_of(group, row, col ^ 1)
                cross_pairs.append((place_of(group, row, col), other))

    def col_swap(value, flip):
        return lax.ppermute(value, "col", [(i, i ^ flip) for i in range(n_col)])

    def end_swap(value):
        return lax.ppermute(value, "row", [(i, i ^ 1) for i in range(n_row)])

    def cross(value):
        return lax.ppermute(value, ("group", "row", "col"), cross_pairs)

    def gather_tokens(tokens):
        shards = [tokens, col_swap(tokens, 1)]
        for step in range(1, chips):
            far = col_swap(tokens, 2 * step)
            shards += [far, col_swap(far, 1)]
        return jnp.concatenate(shards, axis=0)

    def pipeline(
        tokens,
        mask,
        first_weight,
        first_bias,
        first_down_maps,
        first_up_maps,
        second_weight,
        second_down_maps,
    ):
        rows = tokens.shape[0]
        near = 2 * rows
        width = first_weight.shape[1] // UNITS
        wide = 2 * width
        fold = width // LANES
        place = lax.axis_index("row")
        is_end = (place == 0) | (place == 3)
        last = tokens
        partials, payloads, swaps, sums, crosses = {}, {}, {}, {}, {}
        total, low_total = None, None
        low_in = {}

        def halves(value):
            return jnp.concatenate([value[:, :width], value[:, width:]], axis=0)

        def unfold(value):
            return jnp.concatenate([value[:near], value[near : 2 * near]], axis=1)

        def columns(unit):
            if unit < 4:
                start, size = (unit % 2) * wide, wide
            elif unit < 8:
                start, size = unit * width, width
            else:
                start, size = 8 * width + (unit % 2) * wide, wide
            return slice(start, start + size)

        def own_chip(unit):
            return unit in (0, 1, 10, 11)

        def multiply(left, right):
            nonlocal last
            value = dot(tie(left, last), right).astype(BF16)
            last = value
            return value

        def first_half(unit, x):
            nonlocal last
            value = halves(multiply(x, first_weight[:, columns(unit)]))
            if unit in (0, 2):
                low = dot(x, first_down_maps).astype(BF16)
                low = jnp.concatenate(jnp.split(low, fold, axis=0), axis=1)
                value = jnp.concatenate([value, low], axis=0)
            partials[unit] = value
            last = value

        def first_pair(unit, x):
            value = multiply(x, first_weight[:, unit * width : (unit + 2) * width])
            partials[unit], partials[unit + 1] = value[:, :width], value[:, width:]

        def first_late(unit, x):
            value = multiply(x, first_weight[:, columns(unit)])
            partials[unit + 2], partials[unit] = halves(value[:near]), halves(value[near:])

        def send(t, value):
            payloads[t] = value
            swaps[t] = end_swap(value)

        def state(unit):
            return jnp.where(is_end, swaps[unit + LAG], payloads[unit + LAG])

        def second(states, part):
            nonlocal last
            states = tie(states, last)
            value = dot(states, second_weight[part])
            low = dot(states, second_down_maps[part])
            last = low
            return jnp.concatenate([value, low], axis=1)

        gathered_near = jnp.concatenate([tokens, col_swap(tokens, 1)], axis=0)
        far = col_swap(tokens, 2)
        first_half(0, gathered_near)
        send(0, partials[0])
        first_half(1, gathered_near)
        send(1, partials[1])
        gathered_far = None
        outputs = {}
        for t in range(UNITS + LAG):
            if t < UNITS:
                ours = tie(partials[t], last).astype(F32)
                sums[t] = (ours + swaps[t].astype(F32)).astype(BF16)
                last = sums[t]
                crosses[t] = cross(sums[t])
            if t == 0:
                gathered_far = jnp.concatenate([far, col_swap(far, 1)], axis=0)
                first_half(2, gathered_far)
                send(2, partials[2])
                first_half(3, gathered_far)
                gathered = jnp.concatenate([gathered_near, gathered_far], axis=0)
            k = t - 1
            if 0 <= k < UNITS:
                summed = tie(sums[k], last).astype(F32) + crosses[k].astype(F32)
                if k in (0, 2):
                    low = jnp.concatenate(jnp.split(summed[2 * near :], fold, axis=1), axis=0)
                    own_mask = mask[:near] if k == 0 else mask[near:]
                    low_in[k] = jnp.where(own_mask, low, 0.0).astype(BF16)
                if 4 <= k < 8:
                    low = jnp.concatenate([low_in[0], low_in[2]], axis=0)
                    value = activate(summed, low, first_up_maps, first_bias, columns(k))
                else:
                    low = low_in[0] if own_chip(k) else low_in[2]
                    value = activate(unfold(summed), low, first_up_maps, first_bias, columns(k))
                    value = halves(value)
                if k + LAG < UNITS:
                    value = jnp.where(is_end, partials[k + LAG], value)
                last = value
                send(k + LAG, value)
            if t in (1, 2):
                first_pair(2 * t + 2, gathered)
            elif t in (4, 5):
                first_late(t + 4, gathered)
            elif t == 6:
                top = jnp.concatenate([unfold(state(0)), unfold(state(1))], axis=1)
                bottom = jnp.concatenate([unfold(state(2)), unfold(state(3))], axis=1)
                total = second(jnp.concatenate([top, bottom], axis=0), slice(0, 4 * width))
            elif t == 10:
                states = jnp.concatenate([state(u) for u in range(4, 8)], axis=1)
                total = total + second(states, slice(4 * width, 8 * width))
                outputs["near"], outputs["far"] = total[:near], total[near:]
            elif t >= 11:
                unit = t - LAG
                name = "near" if own_chip(unit) else "far"
                outputs[name] = outputs[name] + second(unfold(state(unit)), columns(unit))
                if t == 12:
                    done = outputs["far"]
                    across = done[:rows] + col_swap(done[rows:].astype(BF16), 1).astype(F32)
                    across = across.astype(BF16)
                    last = across
                    across = col_swap(across, 2)
        done = outputs["near"]
        return done[:rows] + col_swap(done[rows:].astype(BF16), 1).astype(F32) + across.astype(F32)

    def plain(tokens, mask, second_weight, second_down_maps, *first):
        rows = tokens.shape[0]
        states = hidden_plain(gather_tokens(tokens), mask, *first)
        outputs = jnp.concatenate([dot(states, second_weight), dot(states, second_down_maps)], axis=1)
        blocks = [outputs[i * rows : (i + 1) * rows] for i in range(n_col)]
        ours = jnp.concatenate(blocks[0::2], axis=0)
        theirs = jnp.concatenate(blocks[1::2], axis=0).astype(BF16)
        ours = ours + col_swap(theirs, 1).astype(F32)
        result = ours[:rows]
        for step in range(1, chips):
            piece = ours[step * rows : (step + 1) * rows].astype(BF16)
            result = result + col_swap(piece, 2 * step).astype(F32)
        return result

    def local(
        tokens,
        token_job_index,
        job_adapter_index,
        first_weight,
        first_bias,
        first_down_maps,
        first_up_maps,
        second_weight,
        second_bias,
        second_down_maps,
        second_up_maps,
    ):
        rows = tokens.shape[0]
        out_width = second_weight.shape[1]
        mine = lax.axis_index("col")
        mask_all = token_mask(token_job_index, job_adapter_index)
        mask = jnp.concatenate(
            [
                lax.dynamic_slice_in_dim(mask_all, (mine ^ i) * rows, rows, 0)
                for i in range(n_col)
            ],
            axis=0,
        )
        first = (first_weight, first_bias, first_down_maps, first_up_maps)
        even = first_weight.shape[1] % (UNITS * LANES) == 0
        if n_row == 4 and n_col == 4 and even:
            result = pipeline(tokens, mask, *first, second_weight, second_down_maps)
        else:
            result = plain(tokens, mask, second_weight, second_down_maps, *first)
        low_out = jnp.where(mask[:rows], result[:, out_width:], 0.0).astype(BF16)
        layer_output = result[:, :out_width] + second_bias[None, :] + dot(low_out, second_up_maps)
        return layer_output.astype(BF16)

    return local


def solution(mesh):
    shape = mesh.shape
    return jax.shard_map(
        make_local(shape["group"], shape["row"], shape["col"]),
        mesh=mesh,
        in_specs=(
            P(("group", "col"), "row"),
            P("group"),
            P("group"),
            P("row", "col"),
            P("col"),
            P("row", None),
            P(None, "col"),
            P("col", "row"),
            P("row"),
            P("col", None),
            P(None, "row"),
        ),
        out_specs=P(("group", "col"), "row"),
        check_vma=False,
    )
```

time: 156 us -> 166 us (1.064)
  other arithmetic: 5.93 us -> 21 us
  waiting for transfers between devices: 33.1 us -> 23.3 us
  local copies, waits for them, and re-layouts: 2.9 us -> 11.7 us
  starting transfers between devices: 42.7 us -> 37.5 us
    ppermute x5 -> x6, waiting for transfers between devices: 16.8 us -> 8.08 us  [col_swap(): return lax.ppermute(value, 'col', [(i, i ^ flip) for i in range(n_col)])]
    ppermute x15, starting transfers between devices: 37.1 us -> 32.5 us  [end_swap(): return lax.ppermute(value, 'row', [(i, i ^ 1) for i in range(n_row)])]
    dot_general x1 -> x4, local copies, waits for them, and re-layouts: 0.09 us -> 4.05 us  [dot(): return jnp.dot(left, right, preferred_element_type=F32)]
    add x2 -> x4, other arithmetic: 0.17 us -> 3.64 us  [the longest x1 2.97 us: pipeline(): total = total + second(states, slice(4 * width, 8 * width))]
    concatenate x3 -> x17, other arithmetic: 0.17 us -> 3.47 us  [the longest x9 2.4 us: halves(): return jnp.concatenate([value[:, :width], value[:, width:]], axis=0)]
    unnamed x33 -> x71, local copies, waits for them, and re-layouts: 1.23 us -> 3.9 us
    add x1 -> x8, other arithmetic: 0.07 us -> 2.62 us  [pipeline(): summed = tie(sums[k], last).astype(F32) + crosses[k].astype(F32)]
    select_n x4 -> x13, other arithmetic: 1.96 us -> 4.47 us  [the longest x11 4.33 us: state(): return jnp.where(is_end, swaps[unit + LAG], payloads[unit + LAG])]
  transfers between devices with their start and end apart: 32 -> 33, of which waited for: 9 -> 6; matrix products, arithmetic and copies ran while one was open for 44% -> 53% of each run, Pallas kernels for 0% -> 0%
where the time goes in v7:
time: 166 us; the launch traced here: 165 us
  matrix products  70.2 us (42%)
  starting transfers between devices  37.5 us (23%)
  waiting for transfers between devices  23.3 us (14%)
  other arithmetic  21 us (13%)
  local copies, waits for them, and re-layouts  11.7 us (7%)
    dot_general x35, matrix products, dot(): return jnp.dot(left, right, preferred_element_type=F32)  70.2 us
    ppermute x15, starting transfers between devices, end_swap(): return lax.ppermute(value, 'row', [(i, i ^ 1) for i in range(n_row)])  32.5 us
    ppermute x15, waiting for transfers between devices, end_swap(): return lax.ppermute(value, 'row', [(i, i ^ 1) for i in range(n_row)])  15.2 us
    ppermute x6, waiting for transfers between devices, col_swap(): return lax.ppermute(value, 'col', [(i, i ^ flip) for i in range(n_col)])  8.08 us
    convert_element_type x12, other arithmetic, pipeline(): sums[t] = (ours + swaps[t].astype(F32)).astype(BF16)  4.84 us
    select_n x11, other arithmetic, state(): return jnp.where(is_end, swaps[unit + LAG], payloads[unit + LAG])  4.33 us
    dot_general x4, local copies, waits for them, and re-layouts, dot(): return jnp.dot(left, right, preferred_element_type=F32)  4.05 us
    unnamed x71, local copies, waits for them, and re-layouts  3.9 us
  transfers between devices with their start and end apart: 33, of which 6 were waited for; matrix products, arithmetic and copies ran while one was open for 53% of the time, Pallas kernels for 0%

profile of v7, /device:TPU:0, one launch (start us, length us, event | category | flops | bytes accessed | tf_op | source)
XLA Modules:
  0.0 165.1 jit_solution(15347717644323147612)
XLA Ops:
  0.5 2.6 %collective-permute-start = (bf16[64,2560]{1,0:T(8,128)(2,1)}, bf16[64,2560]{1,0:T(8,128)(2,1)S(1)}, u32[]{:S(2)}, u32[]{:S(2)}) collective-permute-start(bf16[64,2560]{1,0:T(8,128)(2,1)} %param.11), channel_id=1, source_target_pairs={{0,2},{1,3},{2,0},{3,1},{4,6},{5,7},{6,4},{7,5},{8,10},{9,11},{10,... | collective-permute-start | bytes 983048 | tf_op jit(solution)/shard_map/ppermute | solution.py:74
  3.8 1.4 fusion.204
  5.1 0.8 select_reduce_fusion
  6.1 1.0 constant_dynamic-update-slice_fusion.7
  7.5 3.5 %fusion.42 = bf16[128,1024]{1,0:T(8,128)(2,1)S(1)} fusion(bf16[128,2560]{1,0:T(8,128)(2,1)S(1)} %get-tuple-element.44, bf16[2560,6144]{1,0:T(8,128)(2,1)} %param.14), kind=kOutput, calls=%fused_computation.45 | convolution fusion | flops 671219712 | bytes 6160384 | tf_op jit(solution)/shard_map/dot_general | solution.py:32
  11.1 1.6 collective-permute-start.3
  12.7 4.1 %fusion.48 = bf16[128,1024]{1,0:T(8,128)(2,1)S(1)} fusion(bf16[128,2560]{1,0:T(8,128)(2,1)S(1)} %get-tuple-element.44, bf16[2560,6144]{1,0:T(8,128)(2,1)} %param.14), kind=kOutput, calls=%fused_computation.47 | convolution fusion | flops 671219712 | bytes 6160384 | tf_op jit(solution)/shard_map/dot_general | solution.py:32
  17.4 3.6 %collective-permute-done.3 = bf16[288,512]{1,0:T(8,128)(2,1)S(1)} collective-permute-done((bf16[288,512]{1,0:T(8,128)(2,1)S(1)}, bf16[288,512]{1,0:T(8,128)(2,1)S(1)}, u32[]{:S(2)}, u32[]{:S(2)}) %collective-permute-start.3) | collective-permute-done | bytes 294944 | tf_op jit(solution)/shard_map/ppermute | solution.py:77
  21.6 3.3 %fusion.45 = bf16[128,1024]{1,0:T(8,128)(2,1)S(1)} fusion(bf16[128,2560]{1,0:T(8,128)(2,1)S(1)} %get-tuple-element.47, bf16[2560,6144]{1,0:T(8,128)(2,1)} %param.14), kind=kOutput, calls=%fused_computation.46 | convolution fusion | flops 671219712 | bytes 6160384 | tf_op jit(solution)/shard_map/dot_general | solution.py:32
  25.0 0.9 fusion.51
  26.6 3.1 %collective-permute-start.7 = (bf16[288,512]{1,0:T(8,128)(2,1)S(1)}, bf16[288,512]{1,0:T(8,128)(2,1)S(1)}, u32[]{:S(2)}, u32[]{:S(2)}) collective-permute-start(bf16[288,512]{1,0:T(8,128)(2,1)S(1)} %maximum_maximum_fusion.2), channel_id=1, source_target_pairs={{0,4},{4,0},{8,12},{12,8},{1,5},{5,1},{9,13},{13,9},{2,6},{6,2},{1... | collective-permute-start | bytes 884744 | tf_op jit(solution)/shard_map/ppermute | solution.py:77
  31.0 1.5 fusion.30
  32.5 5.1 %collective-permute-done.7 = bf16[288,512]{1,0:T(8,128)(2,1)S(1)} collective-permute-done((bf16[288,512]{1,0:T(8,128)(2,1)S(1)}, bf16[288,512]{1,0:T(8,128)(2,1)S(1)}, u32[]{:S(2)}, u32[]{:S(2)}) %collective-permute-start.7) | collective-permute-done | bytes 294944 | tf_op jit(solution)/shard_map/ppermute | solution.py:77
  38.4 3.6 %collective-permute-start.9 = (bf16[256,512]{1,0:T(8,128)(2,1)S(1)}, bf16[256,512]{1,0:T(8,128)(2,1)S(1)}, u32[]{:S(2)}, u32[]{:S(2)}) collective-permute-start(bf16[256,512]{1,0:T(8,128)(2,1)S(1)} %get-tuple-element.113), channel_id=1, source_target_pairs={{0,4},{4,0},{8,12},{12,8},{1,5},{5,1},{9,13},{13,9},{2,6},{6,2},{1... | collective-permute-start | bytes 786440 | tf_op jit(solution)/shard_map/ppermute | solution.py:77
  42.1 1.5 fusion.33
  43.8 3.4 %collective-permute-done.9 = bf16[256,512]{1,0:T(8,128)(2,1)S(1)} collective-permute-done((bf16[256,512]{1,0:T(8,128)(2,1)S(1)}, bf16[256,512]{1,0:T(8,128)(2,1)S(1)}, u32[]{:S(2)}, u32[]{:S(2)}) %collective-permute-start.9) | collective-permute-done | bytes 262176 | tf_op jit(solution)/shard_map/ppermute | solution.py:77
  47.9 1.3 collective-permute-start.11
  50.0 3.2 %collective-permute-start.13 = (bf16[256,512]{1,0:T(8,128)(2,1)S(1)}, bf16[256,512]{1,0:T(8,128)(2,1)S(1)}, u32[]{:S(2)}, u32[]{:S(2)}) collective-permute-start(bf16[256,512]{1,0:T(8,128)(2,1)S(1)} %get-tuple-element.110), channel_id=1, source_target_pairs={{0,4},{4,0},{8,12},{12,8},{1,5},{5,1},{9,13},{13,9},{2,6},{6,2},{1... | collective-permute-start | bytes 786440 | tf_op jit(solution)/shard_map/ppermute | solution.py:77
  53.2 1.5 fusion.36
  55.6 1.1 fusion.125
  56.8 4.4 %collective-permute-start.16 = (bf16[256,512]{1,0:T(8,128)(2,1)}, bf16[256,512]{1,0:T(8,128)(2,1)S(1)}, u32[]{:S(2)}, u32[]{:S(2)}) collective-permute-start(bf16[256,512]{1,0:T(8,128)(2,1)} %fusion.125), channel_id=1, source_target_pairs={{0,4},{4,0},{8,12},{12,8},{1,5},{5,1},{9,13},{13,9},{2,6},{6,2},{1... | collective-permute-start | bytes 786440 | tf_op jit(solution)/shard_map/ppermute | solution.py:77
  61.1 1.5 fusion.39
  62.6 0.8 fusion.174
  64.2 0.8 add_convert_fusion.7
  65.2 1.1 fusion.124
  66.4 1.7 %collective-permute-start.17 = (bf16[256,512]{1,0:T(8,128)(2,1)}, bf16[256,512]{1,0:T(8,128)(2,1)}, u32[]{:S(2)}, u32[]{:S(2)}) collective-permute-start(bf16[256,512]{1,0:T(8,128)(2,1)} %fusion.124), channel_id=1, source_target_pairs={{0,4},{4,0},{8,12},{12,8},{1,5},{5,1},{9,13},{13,9},{2,6},{6,2},{1... | collective-permute-start | bytes 786440 | tf_op jit(solution)/shard_map/ppermute | solution.py:77
  68.1 8.3 %fusion.2 = f32[256,2560]{1,0:T(8,128)} fusion(bf16[256,2048]{1,0:T(8,128)(2,1)S(1)} %maximum_maximum_fusion, bf16[6144,2560]{1,0:T(8,128)(2,1)} %param.18), kind=kOutput, calls=%fused_computation.2 | convolution fusion | flops 2684354560 | bytes 14155776 | tf_op jit(solution)/shard_map/dot_general | solution.py:32
  76.4 1.1 fusion.120
  77.6 1.7 %copy.18 = f32[256,128]{1,0:T(8,128)} copy(f32[256,128]{0,1:T(8,128)} %fusion.120) | data formatting | bytes 262144 | tf_op jit(solution)/shard_map/dot_general | solution.py:32
  79.5 1.6 fusion.123
  81.1 1.6 collective-permute-start.19
  82.7 1.0 add_convert_fusion.5
  83.9 1.3 fusion.122
  85.2 5.2 %collective-permute-start.21 = (bf16[256,512]{1,0:T(8,128)(2,1)S(1)}, bf16[256,512]{1,0:T(8,128)(2,1)S(1)}, u32[]{:S(2)}, u32[]{:S(2)}) collective-permute-start(bf16[256,512]{1,0:T(8,128)(2,1)S(1)} %fusion.122), channel_id=1, source_target_pairs={{0,4},{4,0},{8,12},{12,8},{1,5},{5,1},{9,13},{13,9},{2,6},{6,2},{1... | collective-permute-start | bytes 786440 | tf_op jit(solution)/shard_map/ppermute | solution.py:77
  90.4 1.0 broadcast_select_fusion.6
  91.8 1.3 fusion.102
  93.1 0.8 pad_maximum_fusion.6
  94.0 3.0 %collective-permute-start.24 = (bf16[256,512]{1,0:T(8,128)(2,1)}, bf16[256,512]{1,0:T(8,128)(2,1)}, u32[]{:S(2)}, u32[]{:S(2)}) collective-permute-start(bf16[256,512]{1,0:T(8,128)(2,1)} %get-tuple-element.140), channel_id=1, source_target_pairs={{0,4},{4,0},{8,12},{12,8},{1,5},{5,1},{9,13},{13,9},{2,6},{6,2},{1... | collective-permute-start | bytes 786440 | tf_op jit(solution)/shard_map/ppermute | solution.py:77
  96.9 0.8 add_convert_fusion.3
  98.0 1.3 fusion.107
  101.3 8.4 %fusion = f32[256,2560]{1,0:T(8,128)} fusion(bf16[256,2048]{1,0:T(8,128)(2,1)S(1)} %pad_maximum_fusion, bf16[6144,2560]{1,0:T(8,128)(2,1)} %param.18), kind=kOutput, calls=%fused_computation | convolution fusion | flops 2684354560 | bytes 14155776 | tf_op jit(solution)/shard_map/dot_general | solution.py:32
  109.7 1.5 collective-permute-start.27
  111.9 3.0 %maximum_add_fusion = f32[256,2688]{1,0:T(8,128)S(1)} fusion(f32[256,128]{1,0:T(8,128)S(1)} %copy-done.12, f32[256,2560]{1,0:T(8,128)} %fusion.2, f32[256,128]{1,0:T(8,128)} %copy.19, f32[256,2560]{1,0:T(8,128)} %fusion), kind=kLoop, calls=%fused_computation.28 | loop fusion | flops 2064384 | bytes 8257536 | tf_op jit(solution)/shard_map/add | solution.py:216
  114.9 1.7 %add_convert_fusion.2 = bf16[256,512]{1,0:T(8,128)(2,1)} fusion(bf16[256,512]{1,0:T(8,128)(2,1)} %collective-permute-done.24, bf16[256,512]{1,0:T(8,128)(2,1)S(1)} %copy-done.10), kind=kLoop, calls=%fused_computation.148 | loop fusion | flops 524288 | bytes 786432 | tf_op jit(solution)/shard_map/convert_element_type | solution.py:179
  116.6 1.0 broadcast_select_fusion.2
  117.7 1.1 convert_add_fusion.3
  118.8 1.3 fusion.112
  122.8 1.8 %fusion.132 = f32[128,128]{0,1:T(8,128)} fusion(bf16[128,1024]{1,0:T(8,128)(2,1)S(1)} %pad_maximum_fusion.10, bf16[6144,128]{1,0:T(8,128)(2,1)} %param.20), kind=kOutput, calls=%fused_computation.208 | convolution fusion | flops 33554432 | bytes 589824 | tf_op jit(solution)/shard_map/dot_general | solution.py:32
  124.7 1.6 copy.20
  126.3 3.5 %fusion.18 = f32[128,2560]{1,0:T(8,128)S(1)} fusion(bf16[128,1024]{1,0:T(8,128)(2,1)} %copy-done.11, bf16[6144,2560]{1,0:T(8,128)(2,1)} %param.18), kind=kOutput, calls=%fused_computation.18 | convolution fusion | flops 671088640 | bytes 6815744 | tf_op jit(solution)/shard_map/dot_general | solution.py:32
  129.8 1.0 broadcast_select_fusion.1
  130.9 1.1 convert_add_fusion.2
  132.0 1.3 fusion.117
  134.0 1.2 fusion.128
  135.1 3.6 %fusion.14 = f32[128,2560]{1,0:T(8,128)S(1)} fusion(bf16[128,1024]{1,0:T(8,128)(2,1)S(1)} %pad_maximum_fusion.11, bf16[6144,2560]{1,0:T(8,128)(2,1)} %param.18), kind=kOutput, calls=%fused_computation.14 | convolution fusion | flops 671088640 | bytes 6815744 | tf_op jit(solution)/shard_map/dot_general | solution.py:32
  139.2 2.4 %collective-permute-done.30 = bf16[256,512]{1,0:T(8,128)(2,1)S(1)} collective-permute-done((bf16[256,512]{1,0:T(8,128)(2,1)S(1)}, bf16[256,512]{1,0:T(8,128)(2,1)S(1)}, u32[]{:S(2)}, u32[]{:S(2)}) %collective-permute-start.30) | collective-permute-done | bytes 262176 | tf_op jit(solution)/shard_map/ppermute | solution.py:77
  141.6 1.1 broadcast_select_fusion
  143.5 0.8 fusion.55
  144.3 1.2 fusion.130
  145.5 4.4 %fusion.16 = f32[128,2560]{1,0:T(8,128)} fusion(bf16[128,1024]{1,0:T(8,128)(2,1)S(1)} %pad_maximum_fusion.9, bf16[6144,2560]{1,0:T(8,128)(2,1)} %param.18), kind=kOutput, calls=%fused_computation.16 | convolution fusion | flops 671088640 | bytes 6815744 | tf_op jit(solution)/shard_map/dot_general | solution.py:32
  150.1 1.2 fusion.126
  151.3 3.5 %fusion.12 = f32[128,2560]{1,0:T(8,128)S(1)} fusion(bf16[128,1024]{1,0:T(8,128)(2,1)} %pad_maximum_fusion.13, bf16[6144,2560]{1,0:T(8,128)(2,1)} %param.18), kind=kOutput, calls=%fused_computation.12 | convolution fusion | flops 671088640 | bytes 6815744 | tf_op jit(solution)/shard_map/dot_general | solution.py:32
  155.9 8.1 %collective-permute-done.32 = bf16[64,2688]{1,0:T(8,128)(2,1)S(1)} collective-permute-done((bf16[64,2688]{1,0:T(8,128)(2,1)S(1)}, bf16[64,2688]{1,0:T(8,128)(2,1)S(1)}, u32[]{:S(2)}, u32[]{:S(2)}) %collective-permute-start.32) | collective-permute-done | bytes 344096 | tf_op jit(solution)/shard_map/ppermute | solution.py:74
  164.1 1.0 fusion.57
  (214 shorter events, 18.3 us)
Async XLA Ops:
  0.0 164.1 %copy-start = (bf16[128,2560]{1,0:T(8,128)(2,1)S(1)}, bf16[128,2560]{1,0:T(8,128)(2,1)}, u32[]{:S(2)}) copy-start(bf16[128,2560]{1,0:T(8,128)(2,1)} %param.21) | copy-start | bytes 1966084
  0.0 7.2 %copy-start.2 = (bf16[2560,128]{1,0:T(8,128)(2,1)S(1)}, bf16[2560,128]{1,0:T(8,128)(2,1)}, u32[]{:S(2)}) copy-start(bf16[2560,128]{1,0:T(8,128)(2,1)} %param.16) | copy-start | bytes 1966084
  0.0 7.1 %collective-permute-start.2 = (bf16[64,2560]{1,0:T(8,128)(2,1)}, bf16[64,2560]{1,0:T(8,128)(2,1)S(1)}, u32[]{:S(2)}, u32[]{:S(2)}) collective-permute-start(bf16[64,2560]{1,0:T(8,128)(2,1)} %param.11), channel_id=1, source_target_pairs={{0,1},{1,0},{2,3},{3,2},{4,5},{5,4},{6,7},{7,6},{8,9},{9,8},{10,11... | collective-permute-start | bytes 983048 | tf_op jit(solution)/shard_map/ppermute | solution.py:74
  0.5 16.9 %collective-permute-start = (bf16[64,2560]{1,0:T(8,128)(2,1)}, bf16[64,2560]{1,0:T(8,128)(2,1)S(1)}, u32[]{:S(2)}, u32[]{:S(2)}) collective-permute-start(bf16[64,2560]{1,0:T(8,128)(2,1)} %param.11), channel_id=1, source_target_pairs={{0,2},{1,3},{2,0},{3,1},{4,6},{5,7},{6,4},{7,5},{8,10},{9,11},{10,... | collective-permute-start | bytes 983048 | tf_op jit(solution)/shard_map/ppermute | solution.py:74
  7.2 17.8 %copy-start.32 = (bf16[2560,6144]{1,0:T(8,128)(2,1)S(1)}, bf16[2560,6144]{1,0:T(8,128)(2,1)}, u32[]{:S(2)}) copy-start(bf16[2560,6144]{1,0:T(8,128)(2,1)} %param.14) | copy-start | bytes 94371840
  11.1 9.9 %collective-permute-start.3 = (bf16[288,512]{1,0:T(8,128)(2,1)S(1)}, bf16[288,512]{1,0:T(8,128)(2,1)S(1)}, u32[]{:S(2)}, u32[]{:S(2)}) collective-permute-start(bf16[288,512]{1,0:T(8,128)(2,1)S(1)} %maximum_maximum_fusion.1), channel_id=1, source_target_pairs={{0,4},{4,0},{8,12},{12,8},{1,5},{5,1},{9,13},{13,9},{2,6},{6,2},{1... | collective-permute-start | bytes 884744 | tf_op jit(solution)/shard_map/ppermute | solution.py:77
  16.9 9.1 %collective-permute-start.4 = (bf16[256,512]{1,0:T(8,128)(2,1)S(1)}, bf16[256,512]{1,0:T(8,128)(2,1)S(1)}, u32[]{:S(2)}, u32[]{:S(2)}) collective-permute-start(bf16[256,512]{1,0:T(8,128)(2,1)S(1)} %pad_maximum_fusion.1), channel_id=1, source_target_pairs={{0,4},{4,0},{8,12},{12,8},{1,5},{5,1},{9,13},{13,9},{2,6},{6,2},{1... | collective-permute-start | bytes 786440 | tf_op jit(solution)/shard_map/ppermute | solution.py:77
  17.4 3.8 %collective-permute-start.1 = (bf16[64,2560]{1,0:T(8,128)(2,1)S(1)}, bf16[64,2560]{1,0:T(8,128)(2,1)S(1)}, u32[]{:S(2)}, u32[]{:S(2)}) collective-permute-start(bf16[64,2560]{1,0:T(8,128)(2,1)S(1)} %collective-permute-done), channel_id=1, source_target_pairs={{0,1},{1,0},{2,3},{3,2},{4,5},{5,4},{6,7},{7,6},{8,9},{9,8},{10,11... | collective-permute-start | bytes 983048 | tf_op jit(solution)/shard_map/ppermute | solution.py:74
  21.1 8.6 %collective-permute-start.5 = (bf16[288,512]{1,0:T(8,128)(2,1)S(1)}, bf16[288,512]{1,0:T(8,128)(2,1)S(1)}, u32[]{:S(2)}, u32[]{:S(2)}) collective-permute-start(bf16[288,512]{1,0:T(8,128)(2,1)S(1)} %add_convert_fusion.1), channel_id=1, source_target_pairs={{0,1},{1,0},{2,3},{3,2},{4,8},{5,9},{6,10},{7,11},{8,4},{9,5},{10,... | collective-permute-start | bytes 884744 | tf_op jit(solution)/shard_map/ppermute | solution.py:80
  25.9 4.0 %copy-start.33 = (bf16[128,6144]{1,0:T(8,128)(2,1)S(1)}, bf16[128,6144]{1,0:T(8,128)(2,1)}, u32[]{:S(2)}) copy-start(bf16[128,6144]{1,0:T(8,128)(2,1)} %param.17) | copy-start | bytes 4718596
  26.1 11.7 %collective-permute-start.8 = (bf16[256,512]{1,0:T(8,128)(2,1)S(1)}, bf16[256,512]{1,0:T(8,128)(2,1)S(1)}, u32[]{:S(2)}, u32[]{:S(2)}) collective-permute-start(bf16[256,512]{1,0:T(8,128)(2,1)S(1)} %add_convert_fusion.11), channel_id=1, source_target_pairs={{0,1},{1,0},{2,3},{3,2},{4,8},{5,9},{6,10},{7,11},{8,4},{9,5},{10,... | collective-permute-start | bytes 786440 | tf_op jit(solution)/shard_map/ppermute | solution.py:80
  26.6 11.0 %collective-permute-start.7 = (bf16[288,512]{1,0:T(8,128)(2,1)S(1)}, bf16[288,512]{1,0:T(8,128)(2,1)S(1)}, u32[]{:S(2)}, u32[]{:S(2)}) collective-permute-start(bf16[288,512]{1,0:T(8,128)(2,1)S(1)} %maximum_maximum_fusion.2), channel_id=1, source_target_pairs={{0,4},{4,0},{8,12},{12,8},{1,5},{5,1},{9,13},{13,9},{2,6},{6,2},{1... | collective-permute-start | bytes 884744 | tf_op jit(solution)/shard_map/ppermute | solution.py:77
  29.9 35.3 %copy-start.23 = (bf16[128,128]{1,0:T(8,128)(2,1)}, bf16[128,128]{1,0:T(8,128)(2,1)S(1)}, u32[]{:S(2)}) copy-start(bf16[128,128]{1,0:T(8,128)(2,1)S(1)} %fusion.150) | copy-start | bytes 98308
  30.4 13.2 %collective-permute-start.6 = (bf16[256,512]{1,0:T(8,128)(2,1)S(1)}, bf16[256,512]{1,0:T(8,128)(2,1)S(1)}, u32[]{:S(2)}, u32[]{:S(2)}) collective-permute-start(bf16[256,512]{1,0:T(8,128)(2,1)S(1)} %maximum_select_fusion), channel_id=1, source_target_pairs={{0,4},{4,0},{8,12},{12,8},{1,5},{5,1},{9,13},{13,9},{2,6},{6,2},{1... | collective-permute-start | bytes 786440 | tf_op jit(solution)/shard_map/ppermute | solution.py:77
  37.7 9.5 %collective-permute-start.10 = (bf16[288,512]{1,0:T(8,128)(2,1)S(1)}, bf16[288,512]{1,0:T(8,128)(2,1)S(1)}, u32[]{:S(2)}, u32[]{:S(2)}) collective-permute-start(bf16[288,512]{1,0:T(8,128)(2,1)S(1)} %add_convert_fusion), channel_id=1, source_target_pairs={{0,1},{1,0},{2,3},{3,2},{4,8},{5,9},{6,10},{7,11},{8,4},{9,5},{10,... | collective-permute-start | bytes 884744 | tf_op jit(solution)/shard_map/ppermute | solution.py:80
  38.4 8.8 %collective-permute-start.9 = (bf16[256,512]{1,0:T(8,128)(2,1)S(1)}, bf16[256,512]{1,0:T(8,128)(2,1)S(1)}, u32[]{:S(2)}, u32[]{:S(2)}) collective-permute-start(bf16[256,512]{1,0:T(8,128)(2,1)S(1)} %get-tuple-element.113), channel_id=1, source_target_pairs={{0,4},{4,0},{8,12},{12,8},{1,5},{5,1},{9,13},{13,9},{2,6},{6,2},{1... | collective-permute-start | bytes 786440 | tf_op jit(solution)/shard_map/ppermute | solution.py:77
  43.7 5.7 %collective-permute-start.12 = (bf16[256,512]{1,0:T(8,128)(2,1)S(1)}, bf16[256,512]{1,0:T(8,128)(2,1)S(1)}, u32[]{:S(2)}, u32[]{:S(2)}) collective-permute-start(bf16[256,512]{1,0:T(8,128)(2,1)S(1)} %add_convert_fusion.10), channel_id=1, source_target_pairs={{0,1},{1,0},{2,3},{3,2},{4,8},{5,9},{6,10},{7,11},{8,4},{9,5},{10,... | collective-permute-start | bytes 786440 | tf_op jit(solution)/shard_map/ppermute | solution.py:80
  47.4 17.8 %copy-start.27 = (bf16[128,128]{1,0:T(8,128)(2,1)}, bf16[128,128]{1,0:T(8,128)(2,1)S(1)}, u32[]{:S(2)}) copy-start(bf16[128,128]{1,0:T(8,128)(2,1)S(1)} %fusion.151) | copy-start | bytes 98308
  47.9 7.6 %collective-permute-start.11 = (bf16[256,512]{1,0:T(8,128)(2,1)S(1)}, bf16[256,512]{1,0:T(8,128)(2,1)S(1)}, u32[]{:S(2)}, u32[]{:S(2)}) collective-permute-start(bf16[256,512]{1,0:T(8,128)(2,1)S(1)} %maximum_select_fusion.2), channel_id=1, source_target_pairs={{0,4},{4,0},{8,12},{12,8},{1,5},{5,1},{9,13},{13,9},{2,6},{6,2},{1... | collective-permute-start | bytes 786440 | tf_op jit(solution)/shard_map/ppermute | solution.py:77
  49.3 6.4 %collective-permute-start.14 = (bf16[256,512]{1,0:T(8,128)(2,1)S(1)}, bf16[256,512]{1,0:T(8,128)(2,1)S(1)}, u32[]{:S(2)}, u32[]{:S(2)}) collective-permute-start(bf16[256,512]{1,0:T(8,128)(2,1)S(1)} %add_convert_fusion.9), channel_id=1, source_target_pairs={{0,1},{1,0},{2,3},{3,2},{4,8},{5,9},{6,10},{7,11},{8,4},{9,5},{10,... | collective-permute-start | bytes 786440 | tf_op jit(solution)/shard_map/ppermute | solution.py:80
  50.0 14.2 %collective-permute-start.13 = (bf16[256,512]{1,0:T(8,128)(2,1)S(1)}, bf16[256,512]{1,0:T(8,128)(2,1)S(1)}, u32[]{:S(2)}, u32[]{:S(2)}) collective-permute-start(bf16[256,512]{1,0:T(8,128)(2,1)S(1)} %get-tuple-element.110), channel_id=1, source_target_pairs={{0,4},{4,0},{8,12},{12,8},{1,5},{5,1},{9,13},{13,9},{2,6},{6,2},{1... | collective-permute-start | bytes 786440 | tf_op jit(solution)/shard_map/ppermute | solution.py:77
  54.7 2.0 %copy-start.13 = (bf16[128,512]{1,0:T(8,128)(2,1)}, bf16[128,512]{1,0:T(8,128)(2,1)S(1)}, u32[]{:S(2)}) copy-start(bf16[128,512]{1,0:T(8,128)(2,1)S(1)} %get-tuple-element.105) | copy-start | bytes 393220
  54.7 2.0 %copy-start.15 = (bf16[128,512]{1,0:T(8,128)(2,1)}, bf16[128,512]{1,0:T(8,128)(2,1)S(1)}, u32[]{:S(2)}) copy-start(bf16[128,512]{1,0:T(8,128)(2,1)S(1)} %get-tuple-element.106) | copy-start | bytes 393220
  55.5 9.7 %collective-permute-start.15 = (bf16[256,512]{1,0:T(8,128)(2,1)S(1)}, bf16[256,512]{1,0:T(8,128)(2,1)S(1)}, u32[]{:S(2)}, u32[]{:S(2)}) collective-permute-start(bf16[256,512]{1,0:T(8,128)(2,1)S(1)} %add_convert_fusion.8), channel_id=1, source_target_pairs={{0,1},{1,0},{2,3},{3,2},{4,8},{5,9},{6,10},{7,11},{8,4},{9,5},{10,... | collective-permute-start | bytes 786440 | tf_op jit(solution)/shard_map/ppermute | solution.py:80
  56.8 22.5 %collective-permute-start.16 = (bf16[256,512]{1,0:T(8,128)(2,1)}, bf16[256,512]{1,0:T(8,128)(2,1)S(1)}, u32[]{:S(2)}, u32[]{:S(2)}) collective-permute-start(bf16[256,512]{1,0:T(8,128)(2,1)} %fusion.125), channel_id=1, source_target_pairs={{0,4},{4,0},{8,12},{12,8},{1,5},{5,1},{9,13},{13,9},{2,6},{6,2},{1... | collective-permute-start | bytes 786440 | tf_op jit(solution)/shard_map/ppermute | solution.py:77
  63.4 0.7 copy-start.18
  64.1 1.1 copy-start.31
  65.0 14.5 %collective-permute-start.18 = (bf16[256,512]{1,0:T(8,128)(2,1)}, bf16[256,512]{1,0:T(8,128)(2,1)}, u32[]{:S(2)}, u32[]{:S(2)}) collective-permute-start(bf16[256,512]{1,0:T(8,128)(2,1)} %add_convert_fusion.7), channel_id=1, source_target_pairs={{0,1},{1,0},{2,3},{3,2},{4,8},{5,9},{6,10},{7,11},{8,4},{9,5},{10,... | collective-permute-start | bytes 786440 | tf_op jit(solution)/shard_map/ppermute | solution.py:80
  66.4 10.1 %copy-start.1 = (bf16[6144,128]{1,0:T(8,128)(2,1)S(1)}, bf16[6144,128]{1,0:T(8,128)(2,1)}, u32[]{:S(2)}) copy-start(bf16[6144,128]{1,0:T(8,128)(2,1)} %param.20) | copy-start | bytes 4718596
  66.4 16.3 %collective-permute-start.17 = (bf16[256,512]{1,0:T(8,128)(2,1)}, bf16[256,512]{1,0:T(8,128)(2,1)}, u32[]{:S(2)}, u32[]{:S(2)}) collective-permute-start(bf16[256,512]{1,0:T(8,128)(2,1)} %fusion.124), channel_id=1, source_target_pairs={{0,4},{4,0},{8,12},{12,8},{1,5},{5,1},{9,13},{13,9},{2,6},{6,2},{1... | collective-permute-start | bytes 786440 | tf_op jit(solution)/shard_map/ppermute | solution.py:77
  79.3 4.5 %copy-start.14 = (bf16[128,512]{1,0:T(8,128)(2,1)S(1)}, bf16[128,512]{1,0:T(8,128)(2,1)}, u32[]{:S(2)}) copy-start(bf16[128,512]{1,0:T(8,128)(2,1)} %copy-done.13) | copy-start | bytes 393220
  79.3 4.5 %copy-start.16 = (bf16[128,512]{1,0:T(8,128)(2,1)S(1)}, bf16[128,512]{1,0:T(8,128)(2,1)}, u32[]{:S(2)}) copy-start(bf16[128,512]{1,0:T(8,128)(2,1)} %copy-done.15) | copy-start | bytes 393220
  79.3 4.5 %copy-start.24 = (bf16[128,128]{1,0:T(8,128)(2,1)S(1)}, bf16[128,128]{1,0:T(8,128)(2,1)}, u32[]{:S(2)}) copy-start(bf16[128,128]{1,0:T(8,128)(2,1)} %copy-done.23) | copy-start | bytes 98308
  79.3 4.5 %copy-start.28 = (bf16[128,128]{1,0:T(8,128)(2,1)S(1)}, bf16[128,128]{1,0:T(8,128)(2,1)}, u32[]{:S(2)}) copy-start(bf16[128,128]{1,0:T(8,128)(2,1)} %copy-done.27) | copy-start | bytes 98308
  79.3 4.5 %copy-start.30 = (f32[512]{0:T(512)S(1)}, f32[512]{0:T(512)}, u32[]{:S(2)}) copy-start(f32[512]{0:T(512)} %get-tuple-element.185) | copy-start | bytes 6148
  79.4 4.5 %collective-permute-start.20 = (bf16[256,512]{1,0:T(8,128)(2,1)S(1)}, bf16[256,512]{1,0:T(8,128)(2,1)S(1)}, u32[]{:S(2)}, u32[]{:S(2)}) collective-permute-start(bf16[256,512]{1,0:T(8,128)(2,1)S(1)} %add_convert_fusion.6), channel_id=1, source_target_pairs={{0,1},{1,0},{2,3},{3,2},{4,8},{5,9},{6,10},{7,11},{8,4},{9,5},{10,... | collective-permute-start | bytes 786440 | tf_op jit(solution)/shard_map/ppermute | solution.py:80
  81.1 10.3 %collective-permute-start.19 = (bf16[256,512]{1,0:T(8,128)(2,1)S(1)}, bf16[256,512]{1,0:T(8,128)(2,1)S(1)}, u32[]{:S(2)}, u32[]{:S(2)}) collective-permute-start(bf16[256,512]{1,0:T(8,128)(2,1)S(1)} %fusion.123), channel_id=1, source_target_pairs={{0,4},{4,0},{8,12},{12,8},{1,5},{5,1},{9,13},{13,9},{2,6},{6,2},{1... | collective-permute-start | bytes 786440 | tf_op jit(solution)/shard_map/ppermute | solution.py:77
  83.7 7.9 %collective-permute-start.22 = (bf16[256,512]{1,0:T(8,128)(2,1)S(1)}, bf16[256,512]{1,0:T(8,128)(2,1)S(1)}, u32[]{:S(2)}, u32[]{:S(2)}) collective-permute-start(bf16[256,512]{1,0:T(8,128)(2,1)S(1)} %add_convert_fusion.5), channel_id=1, source_target_pairs={{0,1},{1,0},{2,3},{3,2},{4,8},{5,9},{6,10},{7,11},{8,4},{9,5},{10,... | collective-permute-start | bytes 786440 | tf_op jit(solution)/shard_map/ppermute | solution.py:80
  85.2 11.8 %collective-permute-start.21 = (bf16[256,512]{1,0:T(8,128)(2,1)S(1)}, bf16[256,512]{1,0:T(8,128)(2,1)S(1)}, u32[]{:S(2)}, u32[]{:S(2)}) collective-permute-start(bf16[256,512]{1,0:T(8,128)(2,1)S(1)} %fusion.122), channel_id=1, source_target_pairs={{0,4},{4,0},{8,12},{12,8},{1,5},{5,1},{9,13},{13,9},{2,6},{6,2},{1... | collective-permute-start | bytes 786440 | tf_op jit(solution)/shard_map/ppermute | solution.py:77
  91.5 6.4 %collective-permute-start.23 = (bf16[256,512]{1,0:T(8,128)(2,1)S(1)}, bf16[256,512]{1,0:T(8,128)(2,1)S(1)}, u32[]{:S(2)}, u32[]{:S(2)}) collective-permute-start(bf16[256,512]{1,0:T(8,128)(2,1)S(1)} %add_convert_fusion.4), channel_id=1, source_target_pairs={{0,1},{1,0},{2,3},{3,2},{4,8},{5,9},{6,10},{7,11},{8,4},{9,5},{10,... | collective-permute-start | bytes 786440 | tf_op jit(solution)/shard_map/ppermute | solution.py:80
  91.6 1.5 copy-start.19
  91.6 1.5 copy-start.20
  94.0 20.9 %collective-permute-start.24 = (bf16[256,512]{1,0:T(8,128)(2,1)}, bf16[256,512]{1,0:T(8,128)(2,1)}, u32[]{:S(2)}, u32[]{:S(2)}) collective-permute-start(bf16[256,512]{1,0:T(8,128)(2,1)} %get-tuple-element.140), channel_id=1, source_target_pairs={{0,4},{4,0},{8,12},{12,8},{1,5},{5,1},{9,13},{13,9},{2,6},{6,2},{1... | collective-permute-start | bytes 786440 | tf_op jit(solution)/shard_map/ppermute | solution.py:77
  97.7 19.9 %collective-permute-start.25 = (bf16[256,512]{1,0:T(8,128)(2,1)}, bf16[256,512]{1,0:T(8,128)(2,1)}, u32[]{:S(2)}, u32[]{:S(2)}) collective-permute-start(bf16[256,512]{1,0:T(8,128)(2,1)} %add_convert_fusion.3), channel_id=1, source_target_pairs={{0,1},{1,0},{2,3},{3,2},{4,8},{5,9},{6,10},{7,11},{8,4},{9,5},{10,... | collective-permute-start | bytes 786440 | tf_op jit(solution)/shard_map/ppermute | solution.py:80
  99.4 0.7 copy-start.8
  101.3 10.6 %copy-start.12 = (f32[256,128]{1,0:T(8,128)S(1)}, f32[256,128]{1,0:T(8,128)}, u32[]{:S(2)}) copy-start(f32[256,128]{1,0:T(8,128)} %copy.18) | copy-start | bytes 393220
  109.7 20.0 %collective-permute-start.27 = (bf16[256,512]{1,0:T(8,128)(2,1)}, bf16[256,512]{1,0:T(8,128)(2,1)}, u32[]{:S(2)}, u32[]{:S(2)}) collective-permute-start(bf16[256,512]{1,0:T(8,128)(2,1)} %pad_maximum_fusion.7), channel_id=1, source_target_pairs={{0,4},{4,0},{8,12},{12,8},{1,5},{5,1},{9,13},{13,9},{2,6},{6,2},{1... | collective-permute-start | bytes 786440 | tf_op jit(solution)/shard_map/ppermute | solution.py:77
  111.9 3.0 %copy-start.10 = (bf16[256,512]{1,0:T(8,128)(2,1)S(1)}, bf16[256,512]{1,0:T(8,128)(2,1)}, u32[]{:S(2)}) copy-start(bf16[256,512]{1,0:T(8,128)(2,1)} %get-tuple-element.74) | copy-start | bytes 786436
  114.9 3.9 %copy-start.25 = (bf16[128,128]{1,0:T(8,128)(2,1)S(1)}, bf16[128,128]{1,0:T(8,128)(2,1)}, u32[]{:S(2)}) copy-start(bf16[128,128]{1,0:T(8,128)(2,1)} %copy-done.23) | copy-start | bytes 98308
  116.6 14.2 %collective-permute-start.28 = (bf16[256,512]{1,0:T(8,128)(2,1)}, bf16[256,512]{1,0:T(8,128)(2,1)}, u32[]{:S(2)}, u32[]{:S(2)}) collective-permute-start(bf16[256,512]{1,0:T(8,128)(2,1)} %add_convert_fusion.2), channel_id=1, source_target_pairs={{0,1},{1,0},{2,3},{3,2},{4,8},{5,9},{6,10},{7,11},{8,4},{9,5},{10,... | collective-permute-start | bytes 786440 | tf_op jit(solution)/shard_map/ppermute | solution.py:80
  121.5 17.7 %collective-permute-start.26 = (bf16[256,512]{1,0:T(8,128)(2,1)}, bf16[256,512]{1,0:T(8,128)(2,1)}, u32[]{:S(2)}, u32[]{:S(2)}) collective-permute-start(bf16[256,512]{1,0:T(8,128)(2,1)} %pad_maximum_fusion.8), channel_id=1, source_target_pairs={{0,4},{4,0},{8,12},{12,8},{1,5},{5,1},{9,13},{13,9},{2,6},{6,2},{1... | collective-permute-start | bytes 786440 | tf_op jit(solution)/shard_map/ppermute | solution.py:77
  122.1 0.7 copy-start.11
  126.2 3.5 %copy-start.7 = (bf16[128,512]{1,0:T(8,128)(2,1)S(1)}, bf16[128,512]{1,0:T(8,128)(2,1)}, u32[]{:S(2)}) copy-start(bf16[128,512]{1,0:T(8,128)(2,1)} %copy-done.6) | copy-start | bytes 393220
  126.3 3.5 %copy-start.9 = (bf16[128,512]{1,0:T(8,128)(2,1)S(1)}, bf16[128,512]{1,0:T(8,128)(2,1)}, u32[]{:S(2)}) copy-start(bf16[128,512]{1,0:T(8,128)(2,1)} %copy-done.8) | copy-start | bytes 393220
  129.7 2.3 %copy-start.26 = (bf16[128,128]{1,0:T(8,128)(2,1)S(1)}, bf16[128,128]{1,0:T(8,128)(2,1)}, u32[]{:S(2)}) copy-start(bf16[128,128]{1,0:T(8,128)(2,1)} %copy-done.23) | copy-start | bytes 98308
  133.4 8.2 %collective-permute-start.30 = (bf16[256,512]{1,0:T(8,128)(2,1)S(1)}, bf16[256,512]{1,0:T(8,128)(2,1)S(1)}, u32[]{:S(2)}, u32[]{:S(2)}) collective-permute-start(bf16[256,512]{1,0:T(8,128)(2,1)S(1)} %pad_maximum_fusion.12), channel_id=1, source_target_pairs={{0,4},{4,0},{8,12},{12,8},{1,5},{5,1},{9,13},{13,9},{2,6},{6,2},{1... | collective-permute-start | bytes 786440 | tf_op jit(solution)/shard_map/ppermute | solution.py:77
  135.1 3.6 %copy-start.22 = (f32[128,128]{1,0:T(8,128)S(1)}, f32[128,128]{1,0:T(8,128)}, u32[]{:S(2)}) copy-start(f32[128,128]{1,0:T(8,128)} %copy.20) | copy-start | bytes 196612
  138.7 2.9 %copy-start.5 = (bf16[128,512]{1,0:T(8,128)(2,1)S(1)}, bf16[128,512]{1,0:T(8,128)(2,1)}, u32[]{:S(2)}) copy-start(bf16[128,512]{1,0:T(8,128)(2,1)} %copy-done.4) | copy-start | bytes 393220
  139.1 4.4 %collective-permute-start.29 = (bf16[64,2688]{1,0:T(8,128)(2,1)S(1)}, bf16[64,2688]{1,0:T(8,128)(2,1)S(1)}, u32[]{:S(2)}, u32[]{:S(2)}) collective-permute-start(bf16[64,2688]{1,0:T(8,128)(2,1)S(1)} %slice.660), channel_id=1, source_target_pairs={{0,1},{1,0},{2,3},{3,2},{4,5},{5,4},{6,7},{7,6},{8,9},{9,8},{10,11... | collective-permute-start | bytes 1032200 | tf_op jit(solution)/shard_map/ppermute | solution.py:74
  151.3 3.6 %copy-start.21 = (bf16[64,2688]{1,0:T(8,128)(2,1)S(1)}, bf16[64,2688]{1,0:T(8,128)(2,1)}, u32[]{:S(2)}) copy-start(bf16[64,2688]{1,0:T(8,128)(2,1)} %fusion.55) | copy-start | bytes 1032196
  151.3 4.2 %copy-start.3 = (f32[128,2560]{1,0:T(8,128)S(1)}, f32[128,2560]{1,0:T(8,128)}, u32[]{:S(2)}) copy-start(f32[128,2560]{1,0:T(8,128)} %fusion.16) | copy-start | bytes 3932164
  154.9 9.1 %collective-permute-start.32 = (bf16[64,2688]{1,0:T(8,128)(2,1)S(1)}, bf16[64,2688]{1,0:T(8,128)(2,1)S(1)}, u32[]{:S(2)}, u32[]{:S(2)}) collective-permute-start(bf16[64,2688]{1,0:T(8,128)(2,1)S(1)} %copy-done.21), channel_id=1, source_target_pairs={{0,2},{1,3},{2,0},{3,1},{4,6},{5,7},{6,4},{7,5},{8,10},{9,11},{10,... | collective-permute-start | bytes 1032200 | tf_op jit(solution)/shard_map/ppermute | solution.py:74
  155.8 8.3 %copy-start.29 = (f32[2560]{0:T(1024)S(1)}, f32[2560]{0:T(1024)}, u32[]{:S(2)}) copy-start(f32[2560]{0:T(1024)} %param.19) | copy-start | bytes 30724
  155.8 8.2 %collective-permute-start.31 = (bf16[64,2688]{1,0:T(8,128)(2,1)S(1)}, bf16[64,2688]{1,0:T(8,128)(2,1)S(1)}, u32[]{:S(2)}, u32[]{:S(2)}) collective-permute-start(bf16[64,2688]{1,0:T(8,128)(2,1)S(1)} %slice.659), channel_id=1, source_target_pairs={{0,1},{1,0},{2,3},{3,2},{4,5},{5,4},{6,7},{7,6},{8,9},{9,8},{10,11... | collective-permute-start | bytes 1032200 | tf_op jit(solution)/shard_map/ppermute | solution.py:74
  (3 other events, 1.9 us)

commit v8 on v7

--- a/solution.py
+++ b/solution.py
@@ -1,6 +1,10 @@
+import functools
+
 import jax
 import jax.numpy as jnp
 from jax import lax
+from jax.experimental import pallas as pl
+from jax.experimental.pallas import tpu as pltpu
 from jax.sharding import PartitionSpec as P
 
 ADAPTER_RANK = 16
@@ -34,6 +38,24 @@
 
 def tie(value, after):
     return lax.optimization_barrier((value, after))[0]
+
+
+def load_kernel(w_hbm, after_ref, out, sem, *, start):
+    copy = pltpu.make_async_copy(w_hbm.at[:, pl.ds(start, out.shape[1])], out, sem)
+    copy.start()
+    copy.wait()
+
+
+def load_columns(weight, start, width, after):
+    return pl.pallas_call(
+        functools.partial(load_kernel, start=start),
+        in_specs=[pl.BlockSpec(memory_space=pl.ANY)] * 2,
+        out_specs=pl.BlockSpec(memory_space=pltpu.VMEM),
+        out_shape=pltpu.VMEM((weight.shape[0], width), BF16),
+        scratch_shapes=[pltpu.SemaphoreType.DMA],
+        compiler_params=pltpu.CompilerParams(vmem_limit_bytes=1 << 20),
+        cost_estimate=pl.CostEstimate(flops=0, bytes_accessed=1000, transcendentals=0),
+    )(pltpu.with_memory_space_constraint(weight, pltpu.HBM), after)
 
 
 def activate(summed, low_in, first_up_maps, first_bias, part):
@@ -88,7 +110,7 @@
 
     def pipeline(
         tokens,
-        mask,
+        mask_of,
         first_weight,
         first_bias,
         first_down_maps,
@@ -126,15 +148,22 @@
         def own_chip(unit):
             return unit in (0, 1, 10, 11)
 
-        def multiply(left, right):
+        def load(block):
             nonlocal last
+            loads[block] = load_columns(first_weight, block * 4 * width, 4 * width, last)
+            last = loads[block]
+
+        def multiply(left, part):
+            nonlocal last
+            block, start = divmod(part.start, 4 * width)
+            right = loads[block][:, start : start + part.stop - part.start]
             value = dot(tie(left, last), right).astype(BF16)
             last = value
             return value
 
         def first_half(unit, x):
             nonlocal last
-            value = halves(multiply(x, first_weight[:, columns(unit)]))
+            value = halves(multiply(x, columns(unit)))
             if unit in (0, 2):
                 low = dot(x, first_down_maps).astype(BF16)
                 low = jnp.concatenate(jnp.split(low, fold, axis=0), axis=1)
@@ -143,11 +172,11 @@
             last = value
 
         def first_pair(unit, x):
-            value = multiply(x, first_weight[:, unit * width : (unit + 2) * width])
+            value = multiply(x, slice(unit * width, (unit + 2) * width))
             partials[unit], partials[unit + 1] = value[:, :width], value[:, width:]
 
         def first_late(unit, x):
-            value = multiply(x, first_weight[:, columns(unit)])
+            value = multiply(x, columns(unit))
             partials[unit + 2], partials[unit] = halves(value[:near]), halves(value[near:])
 
         def send(t, value):
@@ -160,17 +189,22 @@
         def second(states, part):
             nonlocal last
             states = tie(states, last)
+            low = dot(states, second_down_maps[part])
             value = dot(states, second_weight[part])
-            low = dot(states, second_down_maps[part])
-            last = low
+            last = value[:8, :LANES]
             return jnp.concatenate([value, low], axis=1)
 
-        gathered_near = jnp.concatenate([tokens, col_swap(tokens, 1)], axis=0)
         far = col_swap(tokens, 2)
+        loads = {}
+        load(0)
+        gathered_near = jnp.concatenate([tokens, tie(col_swap(tokens, 1), last)], axis=0)
         first_half(0, gathered_near)
         send(0, partials[0])
         first_half(1, gathered_near)
         send(1, partials[1])
+        mask = mask_of(last)
+        first_bias = tie(first_bias, last)
+        load(1)
         gathered_far = None
         outputs = {}
         for t in range(UNITS + LAG):
@@ -203,11 +237,13 @@
                     value = jnp.where(is_end, partials[k + LAG], value)
                 last = value
                 send(k + LAG, value)
+            if t == 0:
+                load(2)
             if t in (1, 2):
                 first_pair(2 * t + 2, gathered)
             elif t in (4, 5):
                 first_late(t + 4, gathered)
-            elif t == 6:
+            elif t == 9:
                 top = jnp.concatenate([unfold(state(0)), unfold(state(1))], axis=1)
                 bottom = jnp.concatenate([unfold(state(2)), unfold(state(3))], axis=1)
                 total = second(jnp.concatenate([top, bottom], axis=0), slice(0, 4 * width))
@@ -226,7 +262,8 @@
                     last = across
                     across = col_swap(across, 2)
         done = outputs["near"]
-        return done[:rows] + col_swap(done[rows:].astype(BF16), 1).astype(F32) + across.astype(F32)
+        done = done[:rows] + col_swap(done[rows:].astype(BF16), 1).astype(F32)
+        return done + across.astype(F32), mask
 
     def plain(tokens, mask, second_weight, second_down_maps, *first):
         rows = tokens.shape[0]
@@ -258,19 +295,23 @@
         rows = tokens.shape[0]
         out_width = second_weight.shape[1]
         mine = lax.axis_index("col")
-        mask_all = token_mask(token_job_index, job_adapter_index)
-        mask = jnp.concatenate(
-            [
-                lax.dynamic_slice_in_dim(mask_all, (mine ^ i) * rows, rows, 0)
-                for i in range(n_col)
-            ],
-            axis=0,
-        )
+
+        def mask_of(after):
+            mask_all = token_mask(tie(token_job_index, after), job_adapter_index)
+            return jnp.concatenate(
+                [
+                    lax.dynamic_slice_in_dim(mask_all, (mine ^ i) * rows, rows, 0)
+                    for i in range(n_col)
+                ],
+                axis=0,
+            )
+
         first = (first_weight, first_bias, first_down_maps, first_up_maps)
         even = first_weight.shape[1] % (UNITS * LANES) == 0
         if n_row == 4 and n_col == 4 and even:
-            result = pipeline(tokens, mask, *first, second_weight, second_down_maps)
+            result, mask = pipeline(tokens, mask_of, *first, second_weight, second_down_maps)
         else:
+            mask = mask_of(tokens)
             result = plain(tokens, mask, second_weight, second_down_maps, *first)
         low_out = jnp.where(mask[:rows], result[:, out_width:], 0.0).astype(BF16)
         layer_output = result[:, :out_width] + second_bias[None, :] + dot(low_out, second_up_maps)

time: 166 us -> 144 us (0.87)
  matrix products: 70.2 us -> 45.2 us
  other arithmetic: 21 us -> 4.08 us
  Pallas kernels: 0 us -> 12.1 us
  waiting for transfers between devices: 23.3 us -> 31.7 us
  local copies, waits for them, and re-layouts: 11.7 us -> 7.35 us
  starting transfers between devices: 37.5 us -> 41.8 us
    dot_general x35, matrix products: 70.2 us -> 45.2 us  [dot(): return jnp.dot(left, right, preferred_element_type=F32)]
    pallas_call x0 -> x3, Pallas kernels: none -> 12.1 us  [load_columns(): pl.pallas_call(functools.partial(load_kernel, start=start), in_specs=[pl....]
    ppermute x15, waiting for transfers between devices: 15.2 us -> 24.5 us  [end_swap(): return lax.ppermute(value, 'row', [(i, i ^ 1) for i in range(n_row)])]
    ppermute x15, starting transfers between devices: 32.5 us -> 37 us  [end_swap(): return lax.ppermute(value, 'row', [(i, i ^ 1) for i in range(n_row)])]
    dot_general x4 -> x0, local copies, waits for them, and re-layouts: 4.05 us -> none  [dot(): return jnp.dot(left, right, preferred_element_type=F32)]
    convert_element_type x12, other arithmetic: 4.84 us -> 0.82 us  [pipeline(): sums[t] = (ours + swaps[t].astype(F32)).astype(BF16)]
    select_n x11 -> x12, other arithmetic: 4.33 us -> 0.47 us  [state(): return jnp.where(is_end, swaps[unit + LAG], payloads[unit + LAG])]
    add x1, other arithmetic: 2.97 us -> 0.32 us  [pipeline(): total = total + second(states, slice(4 * width, 8 * width))]
  transfers between devices with their start and end apart: 33 -> 33, of which waited for: 6 -> 11; matrix products, arithmetic and copies ran while one was open for 53% -> 32% of each run, Pallas kernels for 0% -> 8%
where the time goes in v8:
time: 144 us
  matrix products  45.2 us (31%)
  starting transfers between devices  41.8 us (29%)
  waiting for transfers between devices  31.7 us (22%)
  Pallas kernels  12.1 us (8%)
  local copies, waits for them, and re-layouts  7.35 us (5%)
  other arithmetic  4.08 us (3%)
    dot_general x35, matrix products, dot(): return jnp.dot(left, right, preferred_element_type=F32)  45.2 us
    ppermute x15, starting transfers between devices, end_swap(): return lax.ppermute(value, 'row', [(i, i ^ 1) for i in range(n_row)])  37 us
    ppermute x15, waiting for transfers between devices, end_swap(): return lax.ppermute(value, 'row', [(i, i ^ 1) for i in range(n_row)])  24.5 us
    pallas_call x3, Pallas kernels, load_columns(): pl.pallas_call(functools.partial(load_kernel, start=start), in_specs=[pl....  12.1 us
    ppermute x6, waiting for transfers between devices, col_swap(): return lax.ppermute(value, 'col', [(i, i ^ flip) for i in range(n_col)])  7.16 us
    unnamed x27, local copies, waits for them, and re-layouts  6.4 us
    ppermute x6, starting transfers between devices, col_swap(): return lax.ppermute(value, 'col', [(i, i ^ flip) for i in range(n_col)])  3.8 us
  transfers between devices with their start and end apart: 33, of which 11 were waited for; matrix products, arithmetic and copies ran while one was open for 32% of the time, Pallas kernels for 8%

profile of v8, /device:TPU:0, one launch (start us, length us, event | category | flops | bytes accessed | tf_op | source)
XLA Modules:
  0.0 143.6 jit_solution(5901871422616200038)
XLA Ops:
  0.0 0.5 collective-permute-start.2
  0.5 2.6 %collective-permute-start = (bf16[64,2560]{1,0:T(8,128)(2,1)}, bf16[64,2560]{1,0:T(8,128)(2,1)S(1)}, u32[]{:S(2)}, u32[]{:S(2)}) collective-permute-start(bf16[64,2560]{1,0:T(8,128)(2,1)} %after_ref.1), channel_id=1, source_target_pairs={{0,2},{1,3},{2,0},{3,1},{4,6},{5,7},{6,4},{7,5},{8,10},{9,11},{10,... | collective-permute-start | bytes 983048 | tf_op jit(solution)/shard_map/ppermute | solution.py:96
  3.0 1.0 copy-done.3
  4.0 4.1 %shard_map.109 = bf16[2560,2048]{1,0:T(8,128)(2,1)S(1)} custom-call(bf16[2560,6144]{1,0:T(8,128)(2,1)} %w_hbm.5, bf16[64,2560]{1,0:T(8,128)(2,1)S(1)} %copy-done.3), custom_call_target="tpu_custom_call" | custom-call | bytes 1000 | tf_op jit(solution)/shard_map/pallas_call | solution.py:50
  8.1 4.0 %copy-done.1 = bf16[2560,2048]{1,0:T(8,128)(2,1)} copy-done((bf16[2560,2048]{1,0:T(8,128)(2,1)}, bf16[2560,2048]{1,0:T(8,128)(2,1)S(1)}, u32[]{:S(2)}) %copy-start.1) | copy-done | bytes 10485784
  12.2 0.3 convolution_convert_fusion.1
  12.6 3.5 %fusion.42 = bf16[128,1024]{1,0:T(8,128)(2,1)S(1)} fusion(bf16[128,2560]{1,0:T(8,128)(2,1)S(1)} %get-tuple-element.44, bf16[2560,2048]{1,0:T(8,128)(2,1)} %copy-done.1), kind=kOutput, calls=%fused_computation.45 | convolution fusion | flops 671219712 | bytes 6160384 | tf_op jit(solution)/shard_map/dot_general | solution.py:36
  16.1 1.6 %collective-permute-start.3 = (bf16[288,512]{1,0:T(8,128)(2,1)S(1)}, bf16[288,512]{1,0:T(8,128)(2,1)S(1)}, u32[]{:S(2)}, u32[]{:S(2)}) collective-permute-start(bf16[288,512]{1,0:T(8,128)(2,1)S(1)} %maximum_maximum_fusion.1), channel_id=1, source_target_pairs={{0,4},{4,0},{8,12},{12,8},{1,5},{5,1},{9,13},{13,9},{2,6},{6,2},{1... | collective-permute-start | bytes 884744 | tf_op jit(solution)/shard_map/ppermute | solution.py:99
  17.8 0.9 fusion.48
  18.8 4.0 %shard_map.110 = bf16[2560,2048]{1,0:T(8,128)(2,1)S(1)} custom-call(bf16[2560,6144]{1,0:T(8,128)(2,1)} %w_hbm.5, bf16[256,512]{1,0:T(8,128)(2,1)S(1)} %pad_maximum_fusion.1.after_ref), custom_call_target="tpu_custom_call" | custom-call | bytes 1000 | tf_op jit(solution)/shard_map/pallas_call | solution.py:50
  22.8 1.5 %collective-permute-start.4 = (bf16[256,512]{1,0:T(8,128)(2,1)S(1)}, bf16[256,512]{1,0:T(8,128)(2,1)S(1)}, u32[]{:S(2)}, u32[]{:S(2)}) collective-permute-start(bf16[256,512]{1,0:T(8,128)(2,1)S(1)} %pad_maximum_fusion.1.after_ref), channel_id=1, source_target_pairs={{0,4},{4,0},{8,12},{12,8},{1,5},{5,1},{9,13},{13,9},{2,6},{6,2},{1... | collective-permute-start | bytes 786440 | tf_op jit(solution)/shard_map/ppermute | solution.py:99
  24.8 0.5 collective-permute-done.3
  25.5 0.8 collective-permute-done.1
  26.3 0.3 convolution_convert_fusion
  26.7 0.9 fusion.45
  27.7 0.9 fusion.51
  28.7 4.0 %shard_map.111 = bf16[2560,2048]{1,0:T(8,128)(2,1)S(1)} custom-call(bf16[2560,6144]{1,0:T(8,128)(2,1)} %w_hbm.5, bf16[256,512]{1,0:T(8,128)(2,1)S(1)} %pad_maximum_fusion.2.after_ref), custom_call_target="tpu_custom_call" | custom-call | bytes 1000 | tf_op jit(solution)/shard_map/pallas_call | solution.py:50
  33.0 3.0 %collective-permute-start.7 = (bf16[288,512]{1,0:T(8,128)(2,1)S(1)}, bf16[288,512]{1,0:T(8,128)(2,1)S(1)}, u32[]{:S(2)}, u32[]{:S(2)}) collective-permute-start(bf16[288,512]{1,0:T(8,128)(2,1)S(1)} %maximum_maximum_fusion.2), channel_id=1, source_target_pairs={{0,4},{4,0},{8,12},{12,8},{1,5},{5,1},{9,13},{13,9},{2,6},{6,2},{1... | collective-permute-start | bytes 884744 | tf_op jit(solution)/shard_map/ppermute | solution.py:99
  36.1 0.3 fusion.62
  36.6 0.3 collective-permute-start.6
  36.9 1.6 %fusion.30 = bf16[256,1024]{1,0:T(8,128)(2,1)S(1)} fusion(bf16[256,2560]{1,0:T(8,128)(2,1)S(1)} %get-tuple-element.63, bf16[2560,2048]{1,0:T(8,128)(2,1)S(1)} %shard_map.110), kind=kOutput, calls=%fused_computation.33 | convolution fusion | flops 1342439424 | bytes 7077888 | tf_op jit(solution)/shard_map/dot_general | solution.py:36
  38.5 5.2 %collective-permute-done.7 = bf16[288,512]{1,0:T(8,128)(2,1)S(1)} collective-permute-done((bf16[288,512]{1,0:T(8,128)(2,1)S(1)}, bf16[288,512]{1,0:T(8,128)(2,1)S(1)}, u32[]{:S(2)}, u32[]{:S(2)}) %collective-permute-start.7) | collective-permute-done | bytes 294944 | tf_op jit(solution)/shard_map/ppermute | solution.py:99
  44.1 0.4 fusion.67
  44.6 3.4 %collective-permute-start.9 = (bf16[256,512]{1,0:T(8,128)(2,1)S(1)}, bf16[256,512]{1,0:T(8,128)(2,1)S(1)}, u32[]{:S(2)}, u32[]{:S(2)}) collective-permute-start(bf16[256,512]{1,0:T(8,128)(2,1)S(1)} %get-tuple-element.111), channel_id=1, source_target_pairs={{0,4},{4,0},{8,12},{12,8},{1,5},{5,1},{9,13},{13,9},{2,6},{6,2},{1... | collective-permute-start | bytes 786440 | tf_op jit(solution)/shard_map/ppermute | solution.py:99
  47.9 1.6 %fusion.33 = bf16[256,1024]{1,0:T(8,128)(2,1)S(1)} fusion(bf16[256,2560]{1,0:T(8,128)(2,1)S(1)} %get-tuple-element.63, bf16[2560,2048]{1,0:T(8,128)(2,1)S(1)} %shard_map.110), kind=kOutput, calls=%fused_computation.34 | convolution fusion | flops 1342439424 | bytes 7077888 | tf_op jit(solution)/shard_map/dot_general | solution.py:36
  49.8 4.4 %collective-permute-done.9 = bf16[256,512]{1,0:T(8,128)(2,1)S(1)} collective-permute-done((bf16[256,512]{1,0:T(8,128)(2,1)S(1)}, bf16[256,512]{1,0:T(8,128)(2,1)S(1)}, u32[]{:S(2)}, u32[]{:S(2)}) %collective-permute-start.9) | collective-permute-done | bytes 262176 | tf_op jit(solution)/shard_map/ppermute | solution.py:99
  54.5 0.3 fusion.72
  55.0 1.8 %collective-permute-start.11 = (bf16[256,512]{1,0:T(8,128)(2,1)S(1)}, bf16[256,512]{1,0:T(8,128)(2,1)S(1)}, u32[]{:S(2)}, u32[]{:S(2)}) collective-permute-start(bf16[256,512]{1,0:T(8,128)(2,1)S(1)} %maximum_select_fusion.2), channel_id=1, source_target_pairs={{0,4},{4,0},{8,12},{12,8},{1,5},{5,1},{9,13},{13,9},{2,6},{6,2},{1... | collective-permute-start | bytes 786440 | tf_op jit(solution)/shard_map/ppermute | solution.py:99
  57.0 0.4 fusion.77
  57.5 1.6 %collective-permute-start.13 = (bf16[256,512]{1,0:T(8,128)(2,1)S(1)}, bf16[256,512]{1,0:T(8,128)(2,1)S(1)}, u32[]{:S(2)}, u32[]{:S(2)}) collective-permute-start(bf16[256,512]{1,0:T(8,128)(2,1)S(1)} %get-tuple-element.108), channel_id=1, source_target_pairs={{0,4},{4,0},{8,12},{12,8},{1,5},{5,1},{9,13},{13,9},{2,6},{6,2},{1... | collective-permute-start | bytes 786440 | tf_op jit(solution)/shard_map/ppermute | solution.py:99
  59.1 1.6 %fusion.36 = bf16[256,1024]{1,0:T(8,128)(2,1)S(1)} fusion(bf16[256,2560]{1,0:T(8,128)(2,1)S(1)} %get-tuple-element.63, bf16[2560,2048]{1,0:T(8,128)(2,1)S(1)} %shard_map.111), kind=kOutput, calls=%fused_computation.35 | convolution fusion | flops 1342439424 | bytes 7077888 | tf_op jit(solution)/shard_map/dot_general | solution.py:36
  60.9 3.2 %collective-permute-done.11 = bf16[256,512]{1,0:T(8,128)(2,1)S(1)} collective-permute-done((bf16[256,512]{1,0:T(8,128)(2,1)S(1)}, bf16[256,512]{1,0:T(8,128)(2,1)S(1)}, u32[]{:S(2)}, u32[]{:S(2)}) %collective-permute-start.11) | collective-permute-done | bytes 262176 | tf_op jit(solution)/shard_map/ppermute | solution.py:99
  64.3 0.4 fusion.125
  64.7 2.8 %collective-permute-start.16 = (bf16[256,512]{1,0:T(8,128)(2,1)S(1)}, bf16[256,512]{1,0:T(8,128)(2,1)S(1)}, u32[]{:S(2)}, u32[]{:S(2)}) collective-permute-start(bf16[256,512]{1,0:T(8,128)(2,1)S(1)} %fusion.125), channel_id=1, source_target_pairs={{0,4},{4,0},{8,12},{12,8},{1,5},{5,1},{9,13},{13,9},{2,6},{6,2},{1... | collective-permute-start | bytes 786440 | tf_op jit(solution)/shard_map/ppermute | solution.py:99
  67.5 1.6 %fusion.39 = bf16[256,1024]{1,0:T(8,128)(2,1)S(1)} fusion(bf16[256,2560]{1,0:T(8,128)(2,1)S(1)} %get-tuple-element.63, bf16[2560,2048]{1,0:T(8,128)(2,1)S(1)} %shard_map.111), kind=kOutput, calls=%fused_computation.36 | convolution fusion | flops 1342439424 | bytes 7077888 | tf_op jit(solution)/shard_map/dot_general | solution.py:36
  69.6 0.4 fusion.124
  70.1 3.6 %collective-permute-start.18 = (bf16[256,512]{1,0:T(8,128)(2,1)S(1)}, bf16[256,512]{1,0:T(8,128)(2,1)S(1)}, u32[]{:S(2)}, u32[]{:S(2)}) collective-permute-start(bf16[256,512]{1,0:T(8,128)(2,1)S(1)} %fusion.124), channel_id=1, source_target_pairs={{0,4},{4,0},{8,12},{12,8},{1,5},{5,1},{9,13},{13,9},{2,6},{6,2},{1... | collective-permute-start | bytes 786440 | tf_op jit(solution)/shard_map/ppermute | solution.py:99
  73.7 0.6 collective-permute-done.16
  74.5 0.4 fusion.123
  74.9 5.5 %collective-permute-start.20 = (bf16[256,512]{1,0:T(8,128)(2,1)S(1)}, bf16[256,512]{1,0:T(8,128)(2,1)S(1)}, u32[]{:S(2)}, u32[]{:S(2)}) collective-permute-start(bf16[256,512]{1,0:T(8,128)(2,1)S(1)} %fusion.123), channel_id=1, source_target_pairs={{0,4},{4,0},{8,12},{12,8},{1,5},{5,1},{9,13},{13,9},{2,6},{6,2},{1... | collective-permute-start | bytes 786440 | tf_op jit(solution)/shard_map/ppermute | solution.py:99
  80.6 0.4 fusion.122
  81.0 5.6 %collective-permute-start.22 = (bf16[256,512]{1,0:T(8,128)(2,1)S(1)}, bf16[256,512]{1,0:T(8,128)(2,1)S(1)}, u32[]{:S(2)}, u32[]{:S(2)}) collective-permute-start(bf16[256,512]{1,0:T(8,128)(2,1)S(1)} %fusion.122), channel_id=1, source_target_pairs={{0,4},{4,0},{8,12},{12,8},{1,5},{5,1},{9,13},{13,9},{2,6},{6,2},{1... | collective-permute-start | bytes 786440 | tf_op jit(solution)/shard_map/ppermute | solution.py:99
  86.8 4.1 %collective-permute-done.22 = bf16[256,512]{1,0:T(8,128)(2,1)S(1)} collective-permute-done((bf16[256,512]{1,0:T(8,128)(2,1)S(1)}, bf16[256,512]{1,0:T(8,128)(2,1)S(1)}, u32[]{:S(2)}, u32[]{:S(2)}) %collective-permute-start.22) | collective-permute-done | bytes 262176 | tf_op jit(solution)/shard_map/ppermute | solution.py:99
  91.2 0.3 fusion.102
  91.7 2.1 %collective-permute-start.24 = (bf16[256,512]{1,0:T(8,128)(2,1)S(1)}, bf16[256,512]{1,0:T(8,128)(2,1)S(1)}, u32[]{:S(2)}, u32[]{:S(2)}) collective-permute-start(bf16[256,512]{1,0:T(8,128)(2,1)S(1)} %get-tuple-element.138), channel_id=1, source_target_pairs={{0,4},{4,0},{8,12},{12,8},{1,5},{5,1},{9,13},{13,9},{2,6},{6,2},{1... | collective-permute-start | bytes 786440 | tf_op jit(solution)/shard_map/ppermute | solution.py:99
  93.8 5.6 %fusion.2 = f32[256,2560]{1,0:T(8,128)S(1)} fusion(bf16[256,2048]{1,0:T(8,128)(2,1)S(1)} %maximum_maximum_fusion, bf16[6144,2560]{1,0:T(8,128)(2,1)} %param.18), kind=kOutput, calls=%fused_computation.2 | convolution fusion | flops 2684354560 | bytes 14155776 | tf_op jit(solution)/shard_map/dot_general | solution.py:36
  99.6 1.2 copy-done.6
  100.8 0.4 fusion.120
  101.4 0.3 fusion.107
  101.8 0.4 fusion.118
  102.2 5.6 %fusion = f32[256,2560]{1,0:T(8,128)S(1)} fusion(bf16[256,2048]{1,0:T(8,128)(2,1)S(1)} %pad_maximum_fusion, bf16[6144,2560]{1,0:T(8,128)(2,1)} %param.18), kind=kOutput, calls=%fused_computation | convolution fusion | flops 2684354560 | bytes 14155776 | tf_op jit(solution)/shard_map/dot_general | solution.py:36
  107.9 0.3 maximum_add_fusion
  108.6 0.4 fusion.112
  109.0 4.0 %collective-permute-start.26 = (bf16[256,512]{1,0:T(8,128)(2,1)S(1)}, bf16[256,512]{1,0:T(8,128)(2,1)S(1)}, u32[]{:S(2)}, u32[]{:S(2)}) collective-permute-start(bf16[256,512]{1,0:T(8,128)(2,1)S(1)} %pad_maximum_fusion.8), channel_id=1, source_target_pairs={{0,4},{4,0},{8,12},{12,8},{1,5},{5,1},{9,13},{13,9},{2,6},{6,2},{1... | collective-permute-start | bytes 786440 | tf_op jit(solution)/shard_map/ppermute | solution.py:99
  113.1 3.3 %fusion.26 = f32[128,2560]{1,0:T(8,128)S(1)} fusion(bf16[128,1024]{1,0:T(8,128)(2,1)S(1)} %pad_maximum_fusion.10, bf16[6144,2560]{1,0:T(8,128)(2,1)} %param.18), kind=kOutput, calls=%fused_computation.26 | convolution fusion | flops 671088640 | bytes 6815744 | tf_op jit(solution)/shard_map/dot_general | solution.py:36
  116.7 0.4 collective-permute-done.27
  117.4 0.3 fusion.117
  118.0 3.3 %fusion.22 = f32[128,2560]{1,0:T(8,128)S(1)} fusion(bf16[128,1024]{1,0:T(8,128)(2,1)S(1)} %pad_maximum_fusion.11, bf16[6144,2560]{1,0:T(8,128)(2,1)} %param.18), kind=kOutput, calls=%fused_computation.22 | convolution fusion | flops 671088640 | bytes 6815744 | tf_op jit(solution)/shard_map/dot_general | solution.py:36
  122.0 5.8 %collective-permute-done.30 = bf16[256,512]{1,0:T(8,128)(2,1)S(1)} collective-permute-done((bf16[256,512]{1,0:T(8,128)(2,1)S(1)}, bf16[256,512]{1,0:T(8,128)(2,1)S(1)}, u32[]{:S(2)}, u32[]{:S(2)}) %collective-permute-start.30) | collective-permute-done | bytes 262176 | tf_op jit(solution)/shard_map/ppermute | solution.py:99
  128.1 3.3 %fusion.20 = f32[128,2560]{1,0:T(8,128)S(1)} fusion(bf16[128,1024]{1,0:T(8,128)(2,1)S(1)} %pad_maximum_fusion.13, bf16[6144,2560]{1,0:T(8,128)(2,1)} %param.18), kind=kOutput, calls=%fused_computation.20 | convolution fusion | flops 671088640 | bytes 6815744 | tf_op jit(solution)/shard_map/dot_general | solution.py:36
  131.8 3.3 %fusion.24 = f32[128,2560]{1,0:T(8,128)S(1)} fusion(bf16[128,1024]{1,0:T(8,128)(2,1)S(1)} %pad_maximum_fusion.9, bf16[6144,2560]{1,0:T(8,128)(2,1)} %param.18), kind=kOutput, calls=%fused_computation.24 | convolution fusion | flops 671088640 | bytes 6815744 | tf_op jit(solution)/shard_map/dot_general | solution.py:36
  135.2 0.6 collective-permute-start.32
  136.2 6.3 %collective-permute-done.32 = bf16[64,2688]{1,0:T(8,128)(2,1)S(1)} collective-permute-done((bf16[64,2688]{1,0:T(8,128)(2,1)S(1)}, bf16[64,2688]{1,0:T(8,128)(2,1)S(1)}, u32[]{:S(2)}, u32[]{:S(2)}) %collective-permute-start.32) | collective-permute-done | bytes 344096 | tf_op jit(solution)/shard_map/ppermute | solution.py:96
  142.6 1.0 fusion.57
  (170 shorter events, 7.3 us)
Async XLA Ops:
  0.0 142.6 %copy-start = (bf16[128,2560]{1,0:T(8,128)(2,1)S(1)}, bf16[128,2560]{1,0:T(8,128)(2,1)}, u32[]{:S(2)}) copy-start(bf16[128,2560]{1,0:T(8,128)(2,1)} %param.21) | copy-start | bytes 1966084
  0.0 12.2 %collective-permute-start.2 = (bf16[64,2560]{1,0:T(8,128)(2,1)}, bf16[64,2560]{1,0:T(8,128)(2,1)S(1)}, u32[]{:S(2)}, u32[]{:S(2)}) collective-permute-start(bf16[64,2560]{1,0:T(8,128)(2,1)} %after_ref.1), channel_id=1, source_target_pairs={{0,1},{1,0},{2,3},{3,2},{4,5},{5,4},{6,7},{7,6},{8,9},{9,8},{10,11... | collective-permute-start | bytes 983048 | tf_op jit(solution)/shard_map/ppermute | solution.py:96
  0.5 24.1 %collective-permute-start = (bf16[64,2560]{1,0:T(8,128)(2,1)}, bf16[64,2560]{1,0:T(8,128)(2,1)S(1)}, u32[]{:S(2)}, u32[]{:S(2)}) collective-permute-start(bf16[64,2560]{1,0:T(8,128)(2,1)} %after_ref.1), channel_id=1, source_target_pairs={{0,2},{1,3},{2,0},{3,1},{4,6},{5,7},{6,4},{7,5},{8,10},{9,11},{10,... | collective-permute-start | bytes 983048 | tf_op jit(solution)/shard_map/ppermute | solution.py:96
  3.0 1.0 copy-start.3
  4.0 8.1 %copy-start.4 = (bf16[64,2560]{1,0:T(8,128)(2,1)S(1)}, bf16[64,2560]{1,0:T(8,128)(2,1)}, u32[]{:S(2)}) copy-start(bf16[64,2560]{1,0:T(8,128)(2,1)} %after_ref.1) | copy-start | bytes 983044
  4.0 8.2 %copy-start.5 = (bf16[2560,128]{1,0:T(8,128)(2,1)S(1)}, bf16[2560,128]{1,0:T(8,128)(2,1)}, u32[]{:S(2)}) copy-start(bf16[2560,128]{1,0:T(8,128)(2,1)} %param.16) | copy-start | bytes 1966084
  8.1 4.0 %copy-start.1 = (bf16[2560,2048]{1,0:T(8,128)(2,1)}, bf16[2560,2048]{1,0:T(8,128)(2,1)S(1)}, u32[]{:S(2)}) copy-start(bf16[2560,2048]{1,0:T(8,128)(2,1)S(1)} %shard_map.109) | copy-start | bytes 31457284
  12.2 5.6 %copy-start.2 = (bf16[2560,2048]{1,0:T(8,128)(2,1)S(1)}, bf16[2560,2048]{1,0:T(8,128)(2,1)}, u32[]{:S(2)}) copy-start(bf16[2560,2048]{1,0:T(8,128)(2,1)} %copy-done.1) | copy-start | bytes 31457284
  16.1 9.1 %collective-permute-start.3 = (bf16[288,512]{1,0:T(8,128)(2,1)S(1)}, bf16[288,512]{1,0:T(8,128)(2,1)S(1)}, u32[]{:S(2)}, u32[]{:S(2)}) collective-permute-start(bf16[288,512]{1,0:T(8,128)(2,1)S(1)} %maximum_maximum_fusion.1), channel_id=1, source_target_pairs={{0,4},{4,0},{8,12},{12,8},{1,5},{5,1},{9,13},{13,9},{2,6},{6,2},{1... | collective-permute-start | bytes 884744 | tf_op jit(solution)/shard_map/ppermute | solution.py:99
  18.8 5.6 %copy-start.7 = (f32[6144]{0:T(1024)S(1)}, f32[6144]{0:T(1024)}, u32[]{:S(2)}) copy-start(f32[6144]{0:T(1024)} %param.15) | copy-start | bytes 73732
  18.8 5.6 %copy-start.9 = (s32[256]{0:T(256)S(1)}, s32[256]{0:T(256)}, u32[]{:S(2)}) copy-start(s32[256]{0:T(256)} %param.12) | copy-start | bytes 3076
  18.8 5.6 %copy-start.10 = (s32[4]{0:T(128)S(1)}, s32[4]{0:T(128)}, u32[]{:S(2)}) copy-start(s32[4]{0:T(128)} %param.13) | copy-start | bytes 52
  22.8 9.9 %collective-permute-start.4 = (bf16[256,512]{1,0:T(8,128)(2,1)S(1)}, bf16[256,512]{1,0:T(8,128)(2,1)S(1)}, u32[]{:S(2)}, u32[]{:S(2)}) collective-permute-start(bf16[256,512]{1,0:T(8,128)(2,1)S(1)} %pad_maximum_fusion.1.after_ref), channel_id=1, source_target_pairs={{0,4},{4,0},{8,12},{12,8},{1,5},{5,1},{9,13},{13,9},{2,6},{6,2},{1... | collective-permute-start | bytes 786440 | tf_op jit(solution)/shard_map/ppermute | solution.py:99
  24.6 1.7 %collective-permute-start.1 = (bf16[64,2560]{1,0:T(8,128)(2,1)S(1)}, bf16[64,2560]{1,0:T(8,128)(2,1)S(1)}, u32[]{:S(2)}, u32[]{:S(2)}) collective-permute-start(bf16[64,2560]{1,0:T(8,128)(2,1)S(1)} %collective-permute-done), channel_id=1, source_target_pairs={{0,1},{1,0},{2,3},{3,2},{4,5},{5,4},{6,7},{7,6},{8,9},{9,8},{10,11... | collective-permute-start | bytes 983048 | tf_op jit(solution)/shard_map/ppermute | solution.py:96
  25.4 10.6 %collective-permute-start.5 = (bf16[288,512]{1,0:T(8,128)(2,1)S(1)}, bf16[288,512]{1,0:T(8,128)(2,1)S(1)}, u32[]{:S(2)}, u32[]{:S(2)}) collective-permute-start(bf16[288,512]{1,0:T(8,128)(2,1)S(1)} %add_convert_fusion.1), channel_id=1, source_target_pairs={{0,1},{1,0},{2,3},{3,2},{4,8},{5,9},{6,10},{7,11},{8,4},{9,5},{10,... | collective-permute-start | bytes 884744 | tf_op jit(solution)/shard_map/ppermute | solution.py:102
  32.7 3.5 %copy-start.11 = (bf16[128,6144]{1,0:T(8,128)(2,1)S(1)}, bf16[128,6144]{1,0:T(8,128)(2,1)}, u32[]{:S(2)}) copy-start(bf16[128,6144]{1,0:T(8,128)(2,1)} %param.17) | copy-start | bytes 4718596
  32.8 11.2 %collective-permute-start.8 = (bf16[256,512]{1,0:T(8,128)(2,1)S(1)}, bf16[256,512]{1,0:T(8,128)(2,1)S(1)}, u32[]{:S(2)}, u32[]{:S(2)}) collective-permute-start(bf16[256,512]{1,0:T(8,128)(2,1)S(1)} %add_convert_fusion.11), channel_id=1, source_target_pairs={{0,1},{1,0},{2,3},{3,2},{4,8},{5,9},{6,10},{7,11},{8,4},{9,5},{10,... | collective-permute-start | bytes 786440 | tf_op jit(solution)/shard_map/ppermute | solution.py:102
  33.0 10.8 %collective-permute-start.7 = (bf16[288,512]{1,0:T(8,128)(2,1)S(1)}, bf16[288,512]{1,0:T(8,128)(2,1)S(1)}, u32[]{:S(2)}, u32[]{:S(2)}) collective-permute-start(bf16[288,512]{1,0:T(8,128)(2,1)S(1)} %maximum_maximum_fusion.2), channel_id=1, source_target_pairs={{0,4},{4,0},{8,12},{12,8},{1,5},{5,1},{9,13},{13,9},{2,6},{6,2},{1... | collective-permute-start | bytes 884744 | tf_op jit(solution)/shard_map/ppermute | solution.py:99
  36.6 13.0 %collective-permute-start.6 = (bf16[256,512]{1,0:T(8,128)(2,1)S(1)}, bf16[256,512]{1,0:T(8,128)(2,1)S(1)}, u32[]{:S(2)}, u32[]{:S(2)}) collective-permute-start(bf16[256,512]{1,0:T(8,128)(2,1)S(1)} %maximum_select_fusion), channel_id=1, source_target_pairs={{0,4},{4,0},{8,12},{12,8},{1,5},{5,1},{9,13},{13,9},{2,6},{6,2},{1... | collective-permute-start | bytes 786440 | tf_op jit(solution)/shard_map/ppermute | solution.py:99
  43.9 10.4 %collective-permute-start.10 = (bf16[288,512]{1,0:T(8,128)(2,1)S(1)}, bf16[288,512]{1,0:T(8,128)(2,1)S(1)}, u32[]{:S(2)}, u32[]{:S(2)}) collective-permute-start(bf16[288,512]{1,0:T(8,128)(2,1)S(1)} %add_convert_fusion), channel_id=1, source_target_pairs={{0,1},{1,0},{2,3},{3,2},{4,8},{5,9},{6,10},{7,11},{8,4},{9,5},{10,... | collective-permute-start | bytes 884744 | tf_op jit(solution)/shard_map/ppermute | solution.py:102
  44.6 9.7 %collective-permute-start.9 = (bf16[256,512]{1,0:T(8,128)(2,1)S(1)}, bf16[256,512]{1,0:T(8,128)(2,1)S(1)}, u32[]{:S(2)}, u32[]{:S(2)}) collective-permute-start(bf16[256,512]{1,0:T(8,128)(2,1)S(1)} %get-tuple-element.111), channel_id=1, source_target_pairs={{0,4},{4,0},{8,12},{12,8},{1,5},{5,1},{9,13},{13,9},{2,6},{6,2},{1... | collective-permute-start | bytes 786440 | tf_op jit(solution)/shard_map/ppermute | solution.py:99
  49.7 7.3 %collective-permute-start.12 = (bf16[256,512]{1,0:T(8,128)(2,1)S(1)}, bf16[256,512]{1,0:T(8,128)(2,1)S(1)}, u32[]{:S(2)}, u32[]{:S(2)}) collective-permute-start(bf16[256,512]{1,0:T(8,128)(2,1)S(1)} %add_convert_fusion.10), channel_id=1, source_target_pairs={{0,1},{1,0},{2,3},{3,2},{4,8},{5,9},{6,10},{7,11},{8,4},{9,5},{10,... | collective-permute-start | bytes 786440 | tf_op jit(solution)/shard_map/ppermute | solution.py:102
  55.0 9.1 %collective-permute-start.11 = (bf16[256,512]{1,0:T(8,128)(2,1)S(1)}, bf16[256,512]{1,0:T(8,128)(2,1)S(1)}, u32[]{:S(2)}, u32[]{:S(2)}) collective-permute-start(bf16[256,512]{1,0:T(8,128)(2,1)S(1)} %maximum_select_fusion.2), channel_id=1, source_target_pairs={{0,4},{4,0},{8,12},{12,8},{1,5},{5,1},{9,13},{13,9},{2,6},{6,2},{1... | collective-permute-start | bytes 786440 | tf_op jit(solution)/shard_map/ppermute | solution.py:99
  56.8 7.4 %collective-permute-start.14 = (bf16[256,512]{1,0:T(8,128)(2,1)S(1)}, bf16[256,512]{1,0:T(8,128)(2,1)S(1)}, u32[]{:S(2)}, u32[]{:S(2)}) collective-permute-start(bf16[256,512]{1,0:T(8,128)(2,1)S(1)} %add_convert_fusion.9), channel_id=1, source_target_pairs={{0,1},{1,0},{2,3},{3,2},{4,8},{5,9},{6,10},{7,11},{8,4},{9,5},{10,... | collective-permute-start | bytes 786440 | tf_op jit(solution)/shard_map/ppermute | solution.py:102
  57.5 11.7 %collective-permute-start.13 = (bf16[256,512]{1,0:T(8,128)(2,1)S(1)}, bf16[256,512]{1,0:T(8,128)(2,1)S(1)}, u32[]{:S(2)}, u32[]{:S(2)}) collective-permute-start(bf16[256,512]{1,0:T(8,128)(2,1)S(1)} %get-tuple-element.108), channel_id=1, source_target_pairs={{0,4},{4,0},{8,12},{12,8},{1,5},{5,1},{9,13},{13,9},{2,6},{6,2},{1... | collective-permute-start | bytes 786440 | tf_op jit(solution)/shard_map/ppermute | solution.py:99
  64.2 5.5 %collective-permute-start.15 = (bf16[256,512]{1,0:T(8,128)(2,1)S(1)}, bf16[256,512]{1,0:T(8,128)(2,1)S(1)}, u32[]{:S(2)}, u32[]{:S(2)}) collective-permute-start(bf16[256,512]{1,0:T(8,128)(2,1)S(1)} %add_convert_fusion.8), channel_id=1, source_target_pairs={{0,1},{1,0},{2,3},{3,2},{4,8},{5,9},{6,10},{7,11},{8,4},{9,5},{10,... | collective-permute-start | bytes 786440 | tf_op jit(solution)/shard_map/ppermute | solution.py:102
  64.7 9.6 %collective-permute-start.16 = (bf16[256,512]{1,0:T(8,128)(2,1)S(1)}, bf16[256,512]{1,0:T(8,128)(2,1)S(1)}, u32[]{:S(2)}, u32[]{:S(2)}) collective-permute-start(bf16[256,512]{1,0:T(8,128)(2,1)S(1)} %fusion.125), channel_id=1, source_target_pairs={{0,4},{4,0},{8,12},{12,8},{1,5},{5,1},{9,13},{13,9},{2,6},{6,2},{1... | collective-permute-start | bytes 786440 | tf_op jit(solution)/shard_map/ppermute | solution.py:99
  69.4 5.0 %collective-permute-start.17 = (bf16[256,512]{1,0:T(8,128)(2,1)S(1)}, bf16[256,512]{1,0:T(8,128)(2,1)S(1)}, u32[]{:S(2)}, u32[]{:S(2)}) collective-permute-start(bf16[256,512]{1,0:T(8,128)(2,1)S(1)} %add_convert_fusion.7), channel_id=1, source_target_pairs={{0,1},{1,0},{2,3},{3,2},{4,8},{5,9},{6,10},{7,11},{8,4},{9,5},{10,... | collective-permute-start | bytes 786440 | tf_op jit(solution)/shard_map/ppermute | solution.py:102
  70.1 10.4 %collective-permute-start.18 = (bf16[256,512]{1,0:T(8,128)(2,1)S(1)}, bf16[256,512]{1,0:T(8,128)(2,1)S(1)}, u32[]{:S(2)}, u32[]{:S(2)}) collective-permute-start(bf16[256,512]{1,0:T(8,128)(2,1)S(1)} %fusion.124), channel_id=1, source_target_pairs={{0,4},{4,0},{8,12},{12,8},{1,5},{5,1},{9,13},{13,9},{2,6},{6,2},{1... | collective-permute-start | bytes 786440 | tf_op jit(solution)/shard_map/ppermute | solution.py:99
  74.3 6.3 %collective-permute-start.19 = (bf16[256,512]{1,0:T(8,128)(2,1)S(1)}, bf16[256,512]{1,0:T(8,128)(2,1)S(1)}, u32[]{:S(2)}, u32[]{:S(2)}) collective-permute-start(bf16[256,512]{1,0:T(8,128)(2,1)S(1)} %add_convert_fusion.6), channel_id=1, source_target_pairs={{0,1},{1,0},{2,3},{3,2},{4,8},{5,9},{6,10},{7,11},{8,4},{9,5},{10,... | collective-permute-start | bytes 786440 | tf_op jit(solution)/shard_map/ppermute | solution.py:102
  74.9 11.8 %collective-permute-start.20 = (bf16[256,512]{1,0:T(8,128)(2,1)S(1)}, bf16[256,512]{1,0:T(8,128)(2,1)S(1)}, u32[]{:S(2)}, u32[]{:S(2)}) collective-permute-start(bf16[256,512]{1,0:T(8,128)(2,1)S(1)} %fusion.123), channel_id=1, source_target_pairs={{0,4},{4,0},{8,12},{12,8},{1,5},{5,1},{9,13},{13,9},{2,6},{6,2},{1... | collective-permute-start | bytes 786440 | tf_op jit(solution)/shard_map/ppermute | solution.py:99
  80.5 10.6 %collective-permute-start.21 = (bf16[256,512]{1,0:T(8,128)(2,1)S(1)}, bf16[256,512]{1,0:T(8,128)(2,1)S(1)}, u32[]{:S(2)}, u32[]{:S(2)}) collective-permute-start(bf16[256,512]{1,0:T(8,128)(2,1)S(1)} %add_convert_fusion.5), channel_id=1, source_target_pairs={{0,1},{1,0},{2,3},{3,2},{4,8},{5,9},{6,10},{7,11},{8,4},{9,5},{10,... | collective-permute-start | bytes 786440 | tf_op jit(solution)/shard_map/ppermute | solution.py:102
  81.0 9.9 %collective-permute-start.22 = (bf16[256,512]{1,0:T(8,128)(2,1)S(1)}, bf16[256,512]{1,0:T(8,128)(2,1)S(1)}, u32[]{:S(2)}, u32[]{:S(2)}) collective-permute-start(bf16[256,512]{1,0:T(8,128)(2,1)S(1)} %fusion.122), channel_id=1, source_target_pairs={{0,4},{4,0},{8,12},{12,8},{1,5},{5,1},{9,13},{13,9},{2,6},{6,2},{1... | collective-permute-start | bytes 786440 | tf_op jit(solution)/shard_map/ppermute | solution.py:99
  86.7 14.5 %collective-permute-start.23 = (bf16[256,512]{1,0:T(8,128)(2,1)S(1)}, bf16[256,512]{1,0:T(8,128)(2,1)S(1)}, u32[]{:S(2)}, u32[]{:S(2)}) collective-permute-start(bf16[256,512]{1,0:T(8,128)(2,1)S(1)} %add_convert_fusion.4), channel_id=1, source_target_pairs={{0,1},{1,0},{2,3},{3,2},{4,8},{5,9},{6,10},{7,11},{8,4},{9,5},{10,... | collective-permute-start | bytes 786440 | tf_op jit(solution)/shard_map/ppermute | solution.py:102
  91.0 17.4 %collective-permute-start.25 = (bf16[256,512]{1,0:T(8,128)(2,1)S(1)}, bf16[256,512]{1,0:T(8,128)(2,1)S(1)}, u32[]{:S(2)}, u32[]{:S(2)}) collective-permute-start(bf16[256,512]{1,0:T(8,128)(2,1)S(1)} %add_convert_fusion.3), channel_id=1, source_target_pairs={{0,1},{1,0},{2,3},{3,2},{4,8},{5,9},{6,10},{7,11},{8,4},{9,5},{10,... | collective-permute-start | bytes 786440 | tf_op jit(solution)/shard_map/ppermute | solution.py:102
  91.7 16.6 %collective-permute-start.24 = (bf16[256,512]{1,0:T(8,128)(2,1)S(1)}, bf16[256,512]{1,0:T(8,128)(2,1)S(1)}, u32[]{:S(2)}, u32[]{:S(2)}) collective-permute-start(bf16[256,512]{1,0:T(8,128)(2,1)S(1)} %get-tuple-element.138), channel_id=1, source_target_pairs={{0,4},{4,0},{8,12},{12,8},{1,5},{5,1},{9,13},{13,9},{2,6},{6,2},{1... | collective-permute-start | bytes 786440 | tf_op jit(solution)/shard_map/ppermute | solution.py:99
  99.4 1.4 copy-start.6
  107.8 9.3 %collective-permute-start.27 = (bf16[256,512]{1,0:T(8,128)(2,1)S(1)}, bf16[256,512]{1,0:T(8,128)(2,1)S(1)}, u32[]{:S(2)}, u32[]{:S(2)}) collective-permute-start(bf16[256,512]{1,0:T(8,128)(2,1)S(1)} %pad_maximum_fusion.7), channel_id=1, source_target_pairs={{0,4},{4,0},{8,12},{12,8},{1,5},{5,1},{9,13},{13,9},{2,6},{6,2},{1... | collective-permute-start | bytes 786440 | tf_op jit(solution)/shard_map/ppermute | solution.py:99
  108.3 8.9 %collective-permute-start.28 = (bf16[256,512]{1,0:T(8,128)(2,1)S(1)}, bf16[256,512]{1,0:T(8,128)(2,1)S(1)}, u32[]{:S(2)}, u32[]{:S(2)}) collective-permute-start(bf16[256,512]{1,0:T(8,128)(2,1)S(1)} %add_convert_fusion.2), channel_id=1, source_target_pairs={{0,1},{1,0},{2,3},{3,2},{4,8},{5,9},{6,10},{7,11},{8,4},{9,5},{10,... | collective-permute-start | bytes 786440 | tf_op jit(solution)/shard_map/ppermute | solution.py:102
  109.0 12.9 %collective-permute-start.26 = (bf16[256,512]{1,0:T(8,128)(2,1)S(1)}, bf16[256,512]{1,0:T(8,128)(2,1)S(1)}, u32[]{:S(2)}, u32[]{:S(2)}) collective-permute-start(bf16[256,512]{1,0:T(8,128)(2,1)S(1)} %pad_maximum_fusion.8), channel_id=1, source_target_pairs={{0,4},{4,0},{8,12},{12,8},{1,5},{5,1},{9,13},{13,9},{2,6},{6,2},{1... | collective-permute-start | bytes 786440 | tf_op jit(solution)/shard_map/ppermute | solution.py:99
  121.4 6.4 %collective-permute-start.30 = (bf16[256,512]{1,0:T(8,128)(2,1)S(1)}, bf16[256,512]{1,0:T(8,128)(2,1)S(1)}, u32[]{:S(2)}, u32[]{:S(2)}) collective-permute-start(bf16[256,512]{1,0:T(8,128)(2,1)S(1)} %pad_maximum_fusion.12), channel_id=1, source_target_pairs={{0,4},{4,0},{8,12},{12,8},{1,5},{5,1},{9,13},{13,9},{2,6},{6,2},{1... | collective-permute-start | bytes 786440 | tf_op jit(solution)/shard_map/ppermute | solution.py:99
  121.8 9.7 %collective-permute-start.29 = (bf16[64,2688]{1,0:T(8,128)(2,1)S(1)}, bf16[64,2688]{1,0:T(8,128)(2,1)S(1)}, u32[]{:S(2)}, u32[]{:S(2)}) collective-permute-start(bf16[64,2688]{1,0:T(8,128)(2,1)S(1)} %slice.670), channel_id=1, source_target_pairs={{0,1},{1,0},{2,3},{3,2},{4,5},{5,4},{6,7},{7,6},{8,9},{9,8},{10,11... | collective-permute-start | bytes 1032200 | tf_op jit(solution)/shard_map/ppermute | solution.py:96
  135.2 7.3 %collective-permute-start.32 = (bf16[64,2688]{1,0:T(8,128)(2,1)S(1)}, bf16[64,2688]{1,0:T(8,128)(2,1)S(1)}, u32[]{:S(2)}, u32[]{:S(2)}) collective-permute-start(bf16[64,2688]{1,0:T(8,128)(2,1)S(1)} %fusion.55), channel_id=1, source_target_pairs={{0,2},{1,3},{2,0},{3,1},{4,6},{5,7},{6,4},{7,5},{8,10},{9,11},{10,... | collective-permute-start | bytes 1032200 | tf_op jit(solution)/shard_map/ppermute | solution.py:96
  136.0 6.6 %copy-start.8 = (f32[2560]{0:T(1024)S(1)}, f32[2560]{0:T(1024)}, u32[]{:S(2)}) copy-start(f32[2560]{0:T(1024)} %param.19) | copy-start | bytes 30724
  136.1 6.4 %collective-permute-start.31 = (bf16[64,2688]{1,0:T(8,128)(2,1)S(1)}, bf16[64,2688]{1,0:T(8,128)(2,1)S(1)}, u32[]{:S(2)}, u32[]{:S(2)}) collective-permute-start(bf16[64,2688]{1,0:T(8,128)(2,1)S(1)} %slice.669), channel_id=1, source_target_pairs={{0,1},{1,0},{2,3},{3,2},{4,5},{5,4},{6,7},{7,6},{8,9},{9,8},{10,11... | collective-permute-start | bytes 1032200 | tf_op jit(solution)/shard_map/ppermute | solution.py:96

commit v9 on v8

--- a/solution.py
+++ b/solution.py
@@ -40,18 +40,19 @@
     return lax.optimization_barrier((value, after))[0]
 
 
-def load_kernel(w_hbm, after_ref, out, sem, *, start):
-    copy = pltpu.make_async_copy(w_hbm.at[:, pl.ds(start, out.shape[1])], out, sem)
+def load_kernel(w_hbm, after_ref, out, sem, *, part):
+    copy = pltpu.make_async_copy(w_hbm.at[part], out, sem)
     copy.start()
     copy.wait()
 
 
-def load_columns(weight, start, width, after):
+def load_part(weight, part, after):
+    shape = tuple(p.size for p in part)
     return pl.pallas_call(
-        functools.partial(load_kernel, start=start),
+        functools.partial(load_kernel, part=part),
         in_specs=[pl.BlockSpec(memory_space=pl.ANY)] * 2,
         out_specs=pl.BlockSpec(memory_space=pltpu.VMEM),
-        out_shape=pltpu.VMEM((weight.shape[0], width), BF16),
+        out_shape=pltpu.VMEM(shape, BF16),
         scratch_shapes=[pltpu.SemaphoreType.DMA],
         compiler_params=pltpu.CompilerParams(vmem_limit_bytes=1 << 20),
         cost_estimate=pl.CostEstimate(flops=0, bytes_accessed=1000, transcendentals=0),
@@ -110,6 +111,7 @@
 
     def pipeline(
         tokens,
+        mine,
         mask_of,
         first_weight,
         first_bias,
@@ -150,20 +152,25 @@
 
         def load(block):
             nonlocal last
-            loads[block] = load_columns(first_weight, block * 4 * width, 4 * width, last)
+            part = (pl.ds(0, first_weight.shape[0]), pl.ds(block * wide, wide))
+            loads[block] = load_part(first_weight, part, last[:16, :LANES])
             last = loads[block]
 
-        def multiply(left, part):
-            nonlocal last
-            block, start = divmod(part.start, 4 * width)
-            right = loads[block][:, start : start + part.stop - part.start]
-            value = dot(tie(left, last), right).astype(BF16)
+        def load_second(block):
+            nonlocal last
+            part = (pl.ds(block * wide, wide), pl.ds(0, second_weight.shape[1]))
+            second_loads[block] = load_part(second_weight, part, last[:16, :LANES])
+            last = second_loads[block]
+
+        def multiply(x, block):
+            nonlocal last
+            value = dot(tie(x, last), loads[block]).astype(BF16)
             last = value
             return value
 
         def first_half(unit, x):
             nonlocal last
-            value = halves(multiply(x, columns(unit)))
+            value = halves(multiply(x, unit % 2))
             if unit in (0, 2):
                 low = dot(x, first_down_maps).astype(BF16)
                 low = jnp.concatenate(jnp.split(low, fold, axis=0), axis=1)
@@ -172,11 +179,11 @@
             last = value
 
         def first_pair(unit, x):
-            value = multiply(x, slice(unit * width, (unit + 2) * width))
+            value = multiply(x, unit // 2)
             partials[unit], partials[unit + 1] = value[:, :width], value[:, width:]
 
         def first_late(unit, x):
-            value = multiply(x, columns(unit))
+            value = multiply(x, unit - 4)
             partials[unit + 2], partials[unit] = halves(value[:near]), halves(value[near:])
 
         def send(t, value):
@@ -186,27 +193,34 @@
         def state(unit):
             return jnp.where(is_end, swaps[unit + LAG], payloads[unit + LAG])
 
-        def second(states, part):
+        def second(name, states, block):
             nonlocal last
             states = tie(states, last)
+            part = slice(block * wide, (block + 1) * wide)
             low = dot(states, second_down_maps[part])
-            value = dot(states, second_weight[part])
+            value = dot(states, second_loads[block] if block in second_loads else second_weight[part])
             last = value[:8, :LANES]
-            return jnp.concatenate([value, low], axis=1)
+            if name in outputs:
+                value, low = outputs[name][0] + value, outputs[name][1] + low
+            outputs[name] = (value, low)
+
+        def core_sum(name):
+            joined = jnp.concatenate(outputs[name], axis=1)
+            return joined[:rows] + col_swap(joined[rows:].astype(BF16), 1).astype(F32)
 
         far = col_swap(tokens, 2)
-        loads = {}
+        loads, second_loads, outputs = {}, {}, {}
+        last, is_end, mine = lax.optimization_barrier((tokens[:16, :LANES], is_end, mine))
         load(0)
         gathered_near = jnp.concatenate([tokens, tie(col_swap(tokens, 1), last)], axis=0)
         first_half(0, gathered_near)
         send(0, partials[0])
+        load(1)
         first_half(1, gathered_near)
         send(1, partials[1])
-        mask = mask_of(last)
+        mask = mask_of(mine, last)
         first_bias = tie(first_bias, last)
-        load(1)
-        gathered_far = None
-        outputs = {}
+        load(2)
         for t in range(UNITS + LAG):
             if t < UNITS:
                 ours = tie(partials[t], last).astype(F32)
@@ -237,33 +251,33 @@
                     value = jnp.where(is_end, partials[k + LAG], value)
                 last = value
                 send(k + LAG, value)
-            if t == 0:
-                load(2)
+            if t < 3:
+                load(t + 3)
             if t in (1, 2):
                 first_pair(2 * t + 2, gathered)
-            elif t in (4, 5):
-                first_late(t + 4, gathered)
-            elif t == 9:
-                top = jnp.concatenate([unfold(state(0)), unfold(state(1))], axis=1)
-                bottom = jnp.concatenate([unfold(state(2)), unfold(state(3))], axis=1)
-                total = second(jnp.concatenate([top, bottom], axis=0), slice(0, 4 * width))
-            elif t == 10:
-                states = jnp.concatenate([state(u) for u in range(4, 8)], axis=1)
-                total = total + second(states, slice(4 * width, 8 * width))
-                outputs["near"], outputs["far"] = total[:near], total[near:]
+            elif t == 3:
+                first_late(8, gathered)
+                first_late(9, gathered)
+            elif t in (5, 6):
+                top, bottom = unfold(state(t - 5)), unfold(state(t - 3))
+                second("all", jnp.concatenate([top, bottom], axis=0), t - 5)
+            elif t in (7, 9):
+                load_second((t + 1) // 2)
+            elif t in (8, 10):
+                states = jnp.concatenate([state(t - 4), state(t - 3)], axis=1)
+                second("all", states, t // 2 - 2)
             elif t >= 11:
                 unit = t - LAG
-                name = "near" if own_chip(unit) else "far"
-                outputs[name] = outputs[name] + second(unfold(state(unit)), columns(unit))
+                if t == 11:
+                    value, low = outputs["all"]
+                    outputs["near"] = (value[:near], low[:near])
+                    outputs["far"] = (value[near:], low[near:])
+                second("near" if own_chip(unit) else "far", unfold(state(unit)), 4 + unit % 2)
                 if t == 12:
-                    done = outputs["far"]
-                    across = done[:rows] + col_swap(done[rows:].astype(BF16), 1).astype(F32)
-                    across = across.astype(BF16)
+                    across = core_sum("far").astype(BF16)
                     last = across
                     across = col_swap(across, 2)
-        done = outputs["near"]
-        done = done[:rows] + col_swap(done[rows:].astype(BF16), 1).astype(F32)
-        return done + across.astype(F32), mask
+        return core_sum("near") + across.astype(F32), mask
 
     def plain(tokens, mask, second_weight, second_down_maps, *first):
         rows = tokens.shape[0]
@@ -296,22 +310,20 @@
         out_width = second_weight.shape[1]
         mine = lax.axis_index("col")
 
-        def mask_of(after):
-            mask_all = token_mask(tie(token_job_index, after), job_adapter_index)
-            return jnp.concatenate(
-                [
-                    lax.dynamic_slice_in_dim(mask_all, (mine ^ i) * rows, rows, 0)
-                    for i in range(n_col)
-                ],
-                axis=0,
-            )
+        def mask_of(mine, after):
+            index = tie(token_job_index, after)
+            for bit in range(n_col.bit_length() - 1):
+                pairs = index.reshape(-1, 2, rows << bit)
+                turned = jnp.concatenate([pairs[:, 1:], pairs[:, :1]], axis=1)
+                index = jnp.where((mine >> bit) & 1 == 1, turned, pairs).reshape(-1)
+            return token_mask(index, job_adapter_index)
 
         first = (first_weight, first_bias, first_down_maps, first_up_maps)
         even = first_weight.shape[1] % (UNITS * LANES) == 0
         if n_row == 4 and n_col == 4 and even:
-            result, mask = pipeline(tokens, mask_of, *first, second_weight, second_down_maps)
+            result, mask = pipeline(tokens, mine, mask_of, *first, second_weight, second_down_maps)
         else:
-            mask = mask_of(tokens)
+            mask = mask_of(mine, tokens)
             result = plain(tokens, mask, second_weight, second_down_maps, *first)
         low_out = jnp.where(mask[:rows], result[:, out_width:], 0.0).astype(BF16)
         layer_output = result[:, :out_width] + second_bias[None, :] + dot(low_out, second_up_maps)

time: 144 us -> 141 us (0.979)
  Pallas kernels: 12.1 us -> 20.2 us
  matrix products: 45.2 us -> 37.7 us
  starting transfers between devices: 41.8 us -> 38.3 us
    pallas_call x3 -> x8, Pallas kernels: 12.1 us -> 20.2 us  [load_part(): pl.pallas_call(functools.partial(load_kernel, part=part), in_specs=[pl.Bl...]
    dot_general x35 -> x39, matrix products: 45.2 us -> 37.7 us  [dot(): return jnp.dot(left, right, preferred_element_type=F32)]
    ppermute x15, starting transfers between devices: 37 us -> 33.2 us  [end_swap(): return lax.ppermute(value, 'row', [(i, i ^ 1) for i in range(n_row)])]
    ppermute x6, waiting for transfers between devices: 7.16 us -> 9.88 us  [col_swap(): return lax.ppermute(value, 'col', [(i, i ^ flip) for i in range(n_col)])]
    unnamed x27 -> x37, local copies, waits for them, and re-layouts: 6.4 us -> 4.27 us
    ppermute x15, waiting for transfers between devices: 24.5 us -> 22.9 us  [end_swap(): return lax.ppermute(value, 'row', [(i, i ^ 1) for i in range(n_row)])]
  transfers between devices with their start and end apart: 33 -> 33, of which waited for: 11 -> 8; matrix products, arithmetic and copies ran while one was open for 32% -> 28% of each run, Pallas kernels for 8% -> 14%
where the time goes in v9:
time: 141 us; the launch traced here: 140 us
  starting transfers between devices  38.3 us (27%)
  matrix products  37.7 us (27%)
  waiting for transfers between devices  32.8 us (23%)
  Pallas kernels  20.2 us (14%)
  local copies, waits for them, and re-layouts  6.1 us (4%)
  other arithmetic  3.47 us (2%)
  between operations  1.57 us (1%)
    dot_general x39, matrix products, dot(): return jnp.dot(left, right, preferred_element_type=F32)  37.7 us
    ppermute x15, starting transfers between devices, end_swap(): return lax.ppermute(value, 'row', [(i, i ^ 1) for i in range(n_row)])  33.2 us
    ppermute x15, waiting for transfers between devices, end_swap(): return lax.ppermute(value, 'row', [(i, i ^ 1) for i in range(n_row)])  22.9 us
    pallas_call x8, Pallas kernels, load_part(): pl.pallas_call(functools.partial(load_kernel, part=part), in_specs=[pl.Bl...  20.2 us
    ppermute x6, waiting for transfers between devices, col_swap(): return lax.ppermute(value, 'col', [(i, i ^ flip) for i in range(n_col)])  9.88 us
    unnamed x37, local copies, waits for them, and re-layouts  4.27 us
    ppermute x6, starting transfers between devices, col_swap(): return lax.ppermute(value, 'col', [(i, i ^ flip) for i in range(n_col)])  3.76 us
  transfers between devices with their start and end apart: 33, of which 8 were waited for; matrix products, arithmetic and copies ran while one was open for 28% of the time, Pallas kernels for 14%

profile of v9, /device:TPU:0, one launch (start us, length us, event | category | flops | bytes accessed | tf_op | source)
XLA Modules:
  0.0 140.0 jit_solution(16689660307739509834)
XLA Ops:
  0.0 2.9 %collective-permute-start = (bf16[64,2560]{1,0:T(8,128)(2,1)}, bf16[64,2560]{1,0:T(8,128)(2,1)S(1)}, u32[]{:S(2)}, u32[]{:S(2)}) collective-permute-start(bf16[64,2560]{1,0:T(8,128)(2,1)} %param.11), channel_id=1, source_target_pairs={{0,2},{1,3},{2,0},{3,1},{4,6},{5,7},{6,4},{7,5},{8,10},{9,11},{10,... | collective-permute-start | bytes 983048 | tf_op jit(solution)/shard_map/ppermute | solution.py:97
  2.9 0.7 slice.400.after_ref
  3.7 2.5 %shard_map.109 = bf16[2560,1024]{1,0:T(8,128)(2,1)S(1)} custom-call(bf16[2560,6144]{1,0:T(8,128)(2,1)} %w_hbm.13, bf16[16,128]{1,0:T(8,128)(2,1)S(1)} %slice.400.after_ref), custom_call_target="tpu_custom_call" | custom-call | bytes 1000 | tf_op jit(solution)/shard_map/pallas_call | solution.py:51
  6.4 1.2 copy-done.6
  7.6 0.9 convolution_convert_fusion.7
  8.5 0.4 copy-done.1
  9.0 2.5 %shard_map.110 = bf16[2560,1024]{1,0:T(8,128)(2,1)S(1)} custom-call(bf16[2560,6144]{1,0:T(8,128)(2,1)} %w_hbm.13, bf16[16,128]{1,0:T(8,128)(2,1)S(1)} %slice.521.after_ref), custom_call_target="tpu_custom_call" | custom-call | bytes 1000 | tf_op jit(solution)/shard_map/pallas_call | solution.py:51
  11.5 0.9 convolution_convert_fusion.6
  12.4 1.4 copy-done.2
  14.2 1.6 %collective-permute-start.4 = (bf16[256,512]{1,0:T(8,128)(2,1)S(1)}, bf16[256,512]{1,0:T(8,128)(2,1)S(1)}, u32[]{:S(2)}, u32[]{:S(2)}) collective-permute-start(bf16[256,512]{1,0:T(8,128)(2,1)S(1)} %pad_maximum_fusion.5), channel_id=1, source_target_pairs={{0,4},{4,0},{8,12},{12,8},{1,5},{5,1},{9,13},{13,9},{2,6},{6,2},{1... | collective-permute-start | bytes 786440 | tf_op jit(solution)/shard_map/ppermute | solution.py:100
  16.1 0.5 collective-permute-start.3
  17.1 2.7 %shard_map.111 = bf16[2560,1024]{1,0:T(8,128)(2,1)S(1)} custom-call(bf16[2560,6144]{1,0:T(8,128)(2,1)} %w_hbm.13, bf16[16,128]{1,0:T(8,128)(2,1)S(1)} %slice.522.after_ref), custom_call_target="tpu_custom_call" | custom-call | bytes 1000 | tf_op jit(solution)/shard_map/pallas_call | solution.py:51
  19.7 9.4 %collective-permute-done.3 = bf16[288,512]{1,0:T(8,128)(2,1)S(1)} collective-permute-done((bf16[288,512]{1,0:T(8,128)(2,1)S(1)}, bf16[288,512]{1,0:T(8,128)(2,1)S(1)}, u32[]{:S(2)}, u32[]{:S(2)}) %collective-permute-start.3) | collective-permute-done | bytes 294944 | tf_op jit(solution)/shard_map/ppermute | solution.py:100
  29.8 0.9 convolution_convert_fusion.5
  30.8 3.2 %collective-permute-start.7 = (bf16[288,512]{1,0:T(8,128)(2,1)S(1)}, bf16[288,512]{1,0:T(8,128)(2,1)S(1)}, u32[]{:S(2)}, u32[]{:S(2)}) collective-permute-start(bf16[288,512]{1,0:T(8,128)(2,1)S(1)} %maximum_maximum_fusion.3), channel_id=1, source_target_pairs={{0,4},{4,0},{8,12},{12,8},{1,5},{5,1},{9,13},{13,9},{2,6},{6,2},{1... | collective-permute-start | bytes 884744 | tf_op jit(solution)/shard_map/ppermute | solution.py:100
  34.0 0.9 convolution_convert_fusion.4
  34.9 2.5 %shard_map.112 = bf16[2560,1024]{1,0:T(8,128)(2,1)S(1)} custom-call(bf16[2560,6144]{1,0:T(8,128)(2,1)} %w_hbm.13, bf16[16,128]{1,0:T(8,128)(2,1)S(1)} %slice.529.after_ref), custom_call_target="tpu_custom_call" | custom-call | bytes 1000 | tf_op jit(solution)/shard_map/pallas_call | solution.py:51
  37.8 1.1 copy-done.12
  39.3 0.9 collective-permute-start.6
  40.2 2.5 %shard_map.113 = bf16[2560,1024]{1,0:T(8,128)(2,1)S(1)} custom-call(bf16[2560,6144]{1,0:T(8,128)(2,1)} %w_hbm.13, bf16[16,128]{1,0:T(8,128)(2,1)S(1)} %slice.539.after_ref), custom_call_target="tpu_custom_call" | custom-call | bytes 1000 | tf_op jit(solution)/shard_map/pallas_call | solution.py:51
  42.7 1.5 %convolution_convert_fusion.3 = bf16[256,1024]{1,0:T(8,128)(2,1)S(1)} fusion(bf16[256,2560]{1,0:T(8,128)(2,1)S(1)} %get-tuple-element.65, bf16[2560,1024]{1,0:T(8,128)(2,1)S(1)} %shard_map.111), kind=kOutput, calls=%fused_computation.22 | convolution fusion | flops 1342439424 | bytes 7077888 | tf_op jit(solution)/shard_map/dot_general | solution.py:36
  44.5 0.3 fusion.36
  45.0 1.6 %collective-permute-start.11 = (bf16[256,512]{1,0:T(8,128)(2,1)S(1)}, bf16[256,512]{1,0:T(8,128)(2,1)S(1)}, u32[]{:S(2)}, u32[]{:S(2)}) collective-permute-start(bf16[256,512]{1,0:T(8,128)(2,1)S(1)} %maximum_select_fusion.1), channel_id=1, source_target_pairs={{0,4},{4,0},{8,12},{12,8},{1,5},{5,1},{9,13},{13,9},{2,6},{6,2},{1... | collective-permute-start | bytes 786440 | tf_op jit(solution)/shard_map/ppermute | solution.py:100
  46.5 2.5 %shard_map.114 = bf16[2560,1024]{1,0:T(8,128)(2,1)S(1)} custom-call(bf16[2560,6144]{1,0:T(8,128)(2,1)} %w_hbm.13, bf16[16,128]{1,0:T(8,128)(2,1)S(1)} %slice.546.after_ref), custom_call_target="tpu_custom_call" | custom-call | bytes 1000 | tf_op jit(solution)/shard_map/pallas_call | solution.py:51
  49.0 1.5 %convolution_convert_fusion.2 = bf16[256,1024]{1,0:T(8,128)(2,1)S(1)} fusion(bf16[256,2560]{1,0:T(8,128)(2,1)S(1)} %get-tuple-element.65, bf16[2560,1024]{1,0:T(8,128)(2,1)S(1)} %shard_map.112), kind=kOutput, calls=%fused_computation.21 | convolution fusion | flops 1342439424 | bytes 7077888 | tf_op jit(solution)/shard_map/dot_general | solution.py:36
  50.6 0.6 collective-permute-start.12
  51.3 1.4 collective-permute-done.11
  52.9 0.3 fusion.41
  53.4 3.4 %collective-permute-start.10 = (bf16[256,512]{1,0:T(8,128)(2,1)S(1)}, bf16[256,512]{1,0:T(8,128)(2,1)S(1)}, u32[]{:S(2)}, u32[]{:S(2)}) collective-permute-start(bf16[256,512]{1,0:T(8,128)(2,1)S(1)} %get-tuple-element.119), channel_id=1, source_target_pairs={{0,4},{4,0},{8,12},{12,8},{1,5},{5,1},{9,13},{13,9},{2,6},{6,2},{1... | collective-permute-start | bytes 786440 | tf_op jit(solution)/shard_map/ppermute | solution.py:100
  56.8 1.5 %convolution_convert_fusion.1 = bf16[256,1024]{1,0:T(8,128)(2,1)S(1)} fusion(bf16[256,2560]{1,0:T(8,128)(2,1)S(1)} %get-tuple-element.65, bf16[2560,1024]{1,0:T(8,128)(2,1)S(1)} %shard_map.113), kind=kOutput, calls=%fused_computation.20 | convolution fusion | flops 1342439424 | bytes 7077888 | tf_op jit(solution)/shard_map/dot_general | solution.py:36
  58.4 1.5 %convolution_convert_fusion = bf16[256,1024]{1,0:T(8,128)(2,1)S(1)} fusion(bf16[256,2560]{1,0:T(8,128)(2,1)S(1)} %get-tuple-element.65, bf16[2560,1024]{1,0:T(8,128)(2,1)S(1)} %shard_map.114), kind=kOutput, calls=%fused_computation.19 | convolution fusion | flops 1342439424 | bytes 7077888 | tf_op jit(solution)/shard_map/dot_general | solution.py:36
  60.5 0.4 fusion.46
  61.0 2.5 %collective-permute-start.14 = (bf16[256,512]{1,0:T(8,128)(2,1)S(1)}, bf16[256,512]{1,0:T(8,128)(2,1)S(1)}, u32[]{:S(2)}, u32[]{:S(2)}) collective-permute-start(bf16[256,512]{1,0:T(8,128)(2,1)S(1)} %get-tuple-element.114), channel_id=1, source_target_pairs={{0,4},{4,0},{8,12},{12,8},{1,5},{5,1},{9,13},{13,9},{2,6},{6,2},{1... | collective-permute-start | bytes 786440 | tf_op jit(solution)/shard_map/ppermute | solution.py:100
  63.8 0.4 fusion.90
  64.2 3.7 %collective-permute-start.16 = (bf16[256,512]{1,0:T(8,128)(2,1)S(1)}, bf16[256,512]{1,0:T(8,128)(2,1)S(1)}, u32[]{:S(2)}, u32[]{:S(2)}) collective-permute-start(bf16[256,512]{1,0:T(8,128)(2,1)S(1)} %fusion.90), channel_id=1, source_target_pairs={{0,4},{4,0},{8,12},{12,8},{1,5},{5,1},{9,13},{13,9},{2,6},{6,2},{1... | collective-permute-start | bytes 786440 | tf_op jit(solution)/shard_map/ppermute | solution.py:100
  68.3 2.4 %collective-permute-done.14 = bf16[256,512]{1,0:T(8,128)(2,1)S(1)} collective-permute-done((bf16[256,512]{1,0:T(8,128)(2,1)S(1)}, bf16[256,512]{1,0:T(8,128)(2,1)S(1)}, u32[]{:S(2)}, u32[]{:S(2)}) %collective-permute-start.14) | collective-permute-done | bytes 262176 | tf_op jit(solution)/shard_map/ppermute | solution.py:100
  71.0 4.4 %collective-permute-done.16 = bf16[256,512]{1,0:T(8,128)(2,1)S(1)} collective-permute-done((bf16[256,512]{1,0:T(8,128)(2,1)S(1)}, bf16[256,512]{1,0:T(8,128)(2,1)S(1)}, u32[]{:S(2)}, u32[]{:S(2)}) %collective-permute-start.16) | collective-permute-done | bytes 262176 | tf_op jit(solution)/shard_map/ppermute | solution.py:100
  75.6 0.4 fusion.89
  76.0 2.8 %collective-permute-start.17 = (bf16[256,512]{1,0:T(8,128)(2,1)S(1)}, bf16[256,512]{1,0:T(8,128)(2,1)S(1)}, u32[]{:S(2)}, u32[]{:S(2)}) collective-permute-start(bf16[256,512]{1,0:T(8,128)(2,1)S(1)} %fusion.89), channel_id=1, source_target_pairs={{0,4},{4,0},{8,12},{12,8},{1,5},{5,1},{9,13},{13,9},{2,6},{6,2},{1... | collective-permute-start | bytes 786440 | tf_op jit(solution)/shard_map/ppermute | solution.py:100
  78.8 4.0 %fusion.4 = f32[256,2560]{1,0:T(8,128)S(1)} fusion(bf16[256,1024]{1,0:T(8,128)(2,1)S(1)} %maximum_maximum_fusion.1, bf16[6144,2560]{1,0:T(8,128)(2,1)} %w_hbm.15), kind=kOutput, calls=%fused_computation.4 | convolution fusion | flops 1342177280 | bytes 8388608 | tf_op jit(solution)/shard_map/dot_general | solution.py:36
  82.8 4.0 %fusion.8 = f32[256,2560]{1,0:T(8,128)S(1)} fusion(f32[256,2560]{1,0:T(8,128)S(1)} %fusion.4, bf16[256,1024]{1,0:T(8,128)(2,1)S(1)} %maximum_maximum_fusion, bf16[6144,2560]{1,0:T(8,128)(2,1)} %w_hbm.15), kind=kOutput, calls=%fused_computation.8 | convolution fusion | flops 1342832640 | bytes 11010048 | tf_op jit(solution)/shard_map/dot_general | solution.py:36
  87.1 0.4 fusion.88
  87.6 2.5 %shard_map.115 = bf16[1024,2560]{1,0:T(8,128)(2,1)S(1)} custom-call(bf16[6144,2560]{1,0:T(8,128)(2,1)} %w_hbm.15, bf16[16,128]{1,0:T(8,128)(2,1)S(1)} %slice.570.after_ref), custom_call_target="tpu_custom_call" | custom-call | bytes 1000 | tf_op jit(solution)/shard_map/pallas_call | solution.py:51
  90.3 0.4 fusion.87
  90.7 2.1 %collective-permute-start.21 = (bf16[256,512]{1,0:T(8,128)(2,1)S(1)}, bf16[256,512]{1,0:T(8,128)(2,1)S(1)}, u32[]{:S(2)}, u32[]{:S(2)}) collective-permute-start(bf16[256,512]{1,0:T(8,128)(2,1)S(1)} %fusion.87), channel_id=1, source_target_pairs={{0,4},{4,0},{8,12},{12,8},{1,5},{5,1},{9,13},{13,9},{2,6},{6,2},{1... | collective-permute-start | bytes 786440 | tf_op jit(solution)/shard_map/ppermute | solution.py:100
  92.9 4.0 %fusion.11 = f32[256,2560]{1,0:T(8,128)S(1)} fusion(f32[256,2560]{1,0:T(8,128)S(1)} %fusion.8, bf16[256,1024]{1,0:T(8,128)(2,1)S(1)} %pad_maximum_fusion.2, bf16[6144,2560]{1,0:T(8,128)(2,1)} %w_hbm.15), kind=kOutput, calls=%fused_computation.9 | convolution fusion | flops 1342832640 | bytes 11010048 | tf_op jit(solution)/shard_map/dot_general | solution.py:36
  97.5 0.3 fusion.71
  98.0 2.1 %collective-permute-start.24 = (bf16[256,512]{1,0:T(8,128)(2,1)S(1)}, bf16[256,512]{1,0:T(8,128)(2,1)S(1)}, u32[]{:S(2)}, u32[]{:S(2)}) collective-permute-start(bf16[256,512]{1,0:T(8,128)(2,1)S(1)} %get-tuple-element.154), channel_id=1, source_target_pairs={{0,4},{4,0},{8,12},{12,8},{1,5},{5,1},{9,13},{13,9},{2,6},{6,2},{1... | collective-permute-start | bytes 786440 | tf_op jit(solution)/shard_map/ppermute | solution.py:100
  100.1 2.5 %shard_map.116 = bf16[1024,2560]{1,0:T(8,128)(2,1)S(1)} custom-call(bf16[6144,2560]{1,0:T(8,128)(2,1)} %w_hbm.15, bf16[16,128]{1,0:T(8,128)(2,1)S(1)} %slice.577.after_ref), custom_call_target="tpu_custom_call" | custom-call | bytes 1000 | tf_op jit(solution)/shard_map/pallas_call | solution.py:51
  103.4 3.0 %collective-permute-start.27 = (bf16[256,512]{1,0:T(8,128)(2,1)S(1)}, bf16[256,512]{1,0:T(8,128)(2,1)S(1)}, u32[]{:S(2)}, u32[]{:S(2)}) collective-permute-start(bf16[256,512]{1,0:T(8,128)(2,1)S(1)} %pad_maximum_fusion.10), channel_id=1, source_target_pairs={{0,4},{4,0},{8,12},{12,8},{1,5},{5,1},{9,13},{13,9},{2,6},{6,2},{1... | collective-permute-start | bytes 786440 | tf_op jit(solution)/shard_map/ppermute | solution.py:100
  106.4 4.0 %fusion.14 = f32[256,2560]{1,0:T(8,128)S(1)} fusion(f32[256,2560]{1,0:T(8,128)S(1)} %fusion.11, bf16[256,1024]{1,0:T(8,128)(2,1)S(1)} %pad_maximum_fusion.3, bf16[6144,2560]{1,0:T(8,128)(2,1)} %w_hbm.15), kind=kOutput, calls=%fused_computation.10 | convolution fusion | flops 1342832640 | bytes 11010048 | tf_op jit(solution)/shard_map/dot_general | solution.py:36
  111.1 0.3 fusion.81
  111.5 1.8 %collective-permute-start.26 = (bf16[256,512]{1,0:T(8,128)(2,1)S(1)}, bf16[256,512]{1,0:T(8,128)(2,1)S(1)}, u32[]{:S(2)}, u32[]{:S(2)}) collective-permute-start(bf16[256,512]{1,0:T(8,128)(2,1)S(1)} %pad_maximum_fusion.11), channel_id=1, source_target_pairs={{0,4},{4,0},{8,12},{12,8},{1,5},{5,1},{9,13},{13,9},{2,6},{6,2},{1... | collective-permute-start | bytes 786440 | tf_op jit(solution)/shard_map/ppermute | solution.py:100
  113.3 0.9 convolution_add_fusion.3
  115.1 4.0 %collective-permute-start.30 = (bf16[256,512]{1,0:T(8,128)(2,1)S(1)}, bf16[256,512]{1,0:T(8,128)(2,1)S(1)}, u32[]{:S(2)}, u32[]{:S(2)}) collective-permute-start(bf16[256,512]{1,0:T(8,128)(2,1)S(1)} %pad_maximum_fusion.15), channel_id=1, source_target_pairs={{0,4},{4,0},{8,12},{12,8},{1,5},{5,1},{9,13},{13,9},{2,6},{6,2},{1... | collective-permute-start | bytes 786440 | tf_op jit(solution)/shard_map/ppermute | solution.py:100
  119.1 0.4 convolution_add_fusion.17
  119.5 0.9 convolution_add_fusion.2
  120.8 5.1 %collective-permute-done.30 = bf16[256,512]{1,0:T(8,128)(2,1)S(1)} collective-permute-done((bf16[256,512]{1,0:T(8,128)(2,1)S(1)}, bf16[256,512]{1,0:T(8,128)(2,1)S(1)}, u32[]{:S(2)}, u32[]{:S(2)}) %collective-permute-start.30) | collective-permute-done | bytes 262176 | tf_op jit(solution)/shard_map/ppermute | solution.py:100
  126.1 0.9 convolution_add_fusion.1
  127.2 0.9 convolution_add_fusion
  128.5 0.6 collective-permute-start.32
  129.1 1.0 collective-permute-done.31
  130.1 8.8 %collective-permute-done.32 = bf16[64,2688]{1,0:T(8,128)(2,1)S(1)} collective-permute-done((bf16[64,2688]{1,0:T(8,128)(2,1)S(1)}, bf16[64,2688]{1,0:T(8,128)(2,1)S(1)}, u32[]{:S(2)}, u32[]{:S(2)}) %collective-permute-start.32) | collective-permute-done | bytes 344096 | tf_op jit(solution)/shard_map/ppermute | solution.py:97
  139.1 1.0 fusion.26
  (203 shorter events, 9.5 us)
Async XLA Ops:
  0.0 139.1 %copy-start = (bf16[128,2560]{1,0:T(8,128)(2,1)S(1)}, bf16[128,2560]{1,0:T(8,128)(2,1)}, u32[]{:S(2)}) copy-start(bf16[128,2560]{1,0:T(8,128)(2,1)} %param.21) | copy-start | bytes 1966084
  0.0 16.7 %collective-permute-start = (bf16[64,2560]{1,0:T(8,128)(2,1)}, bf16[64,2560]{1,0:T(8,128)(2,1)S(1)}, u32[]{:S(2)}, u32[]{:S(2)}) collective-permute-start(bf16[64,2560]{1,0:T(8,128)(2,1)} %param.11), channel_id=1, source_target_pairs={{0,2},{1,3},{2,0},{3,1},{4,6},{5,7},{6,4},{7,5},{8,10},{9,11},{10,... | collective-permute-start | bytes 983048 | tf_op jit(solution)/shard_map/ppermute | solution.py:97
  2.9 3.3 %collective-permute-start.2 = (bf16[64,2560]{1,0:T(8,128)(2,1)}, bf16[64,2560]{1,0:T(8,128)(2,1)S(1)}, u32[]{:S(2)}, u32[]{:S(2)}) collective-permute-start(bf16[64,2560]{1,0:T(8,128)(2,1)} %param.11), channel_id=1, source_target_pairs={{0,1},{1,0},{2,3},{3,2},{4,5},{5,4},{6,7},{7,6},{8,9},{9,8},{10,11... | collective-permute-start | bytes 983048 | tf_op jit(solution)/shard_map/ppermute | solution.py:97
  3.7 2.6 %copy-start.5 = (bf16[64,2560]{1,0:T(8,128)(2,1)S(1)}, bf16[64,2560]{1,0:T(8,128)(2,1)}, u32[]{:S(2)}) copy-start(bf16[64,2560]{1,0:T(8,128)(2,1)} %param.11) | copy-start | bytes 983044
  6.2 2.7 %copy-start.1 = (bf16[2560,1024]{1,0:T(8,128)(2,1)}, bf16[2560,1024]{1,0:T(8,128)(2,1)S(1)}, u32[]{:S(2)}) copy-start(bf16[2560,1024]{1,0:T(8,128)(2,1)S(1)} %shard_map.109) | copy-start | bytes 15728644
  6.4 1.2 copy-start.6
  11.5 2.3 %copy-start.2 = (bf16[2560,1024]{1,0:T(8,128)(2,1)}, bf16[2560,1024]{1,0:T(8,128)(2,1)S(1)}, u32[]{:S(2)}) copy-start(bf16[2560,1024]{1,0:T(8,128)(2,1)S(1)} %shard_map.110) | copy-start | bytes 15728644
  11.5 2.4 %copy-start.10 = (s32[256]{0:T(256)S(1)}, s32[256]{0:T(256)}, u32[]{:S(2)}) copy-start(s32[256]{0:T(256)} %param.12) | copy-start | bytes 3076
  11.5 4.2 %copy-start.4 = (bf16[2560,128]{1,0:T(8,128)(2,1)S(1)}, bf16[2560,128]{1,0:T(8,128)(2,1)}, u32[]{:S(2)}) copy-start(bf16[2560,128]{1,0:T(8,128)(2,1)} %param.16) | copy-start | bytes 1966084
  13.8 2.8 %copy-start.8 = (f32[6144]{0:T(1024)S(1)}, f32[6144]{0:T(1024)}, u32[]{:S(2)}) copy-start(f32[6144]{0:T(1024)} %param.15) | copy-start | bytes 73732
  13.9 3.0 %copy-start.11 = (s32[4]{0:T(128)S(1)}, s32[4]{0:T(128)}, u32[]{:S(2)}) copy-start(s32[4]{0:T(128)} %param.13) | copy-start | bytes 52
  14.1 2.6 %copy-start.7 = (bf16[256,2560]{1,0:T(8,128)(2,1)S(1)}, bf16[256,2560]{1,0:T(8,128)(2,1)}, u32[]{:S(2)}) copy-start(bf16[256,2560]{1,0:T(8,128)(2,1)} %copy-done.6) | copy-start | bytes 3932164
  14.2 23.3 %collective-permute-start.4 = (bf16[256,512]{1,0:T(8,128)(2,1)S(1)}, bf16[256,512]{1,0:T(8,128)(2,1)S(1)}, u32[]{:S(2)}, u32[]{:S(2)}) collective-permute-start(bf16[256,512]{1,0:T(8,128)(2,1)S(1)} %pad_maximum_fusion.5), channel_id=1, source_target_pairs={{0,4},{4,0},{8,12},{12,8},{1,5},{5,1},{9,13},{13,9},{2,6},{6,2},{1... | collective-permute-start | bytes 786440 | tf_op jit(solution)/shard_map/ppermute | solution.py:100
  16.1 13.1 %collective-permute-start.3 = (bf16[288,512]{1,0:T(8,128)(2,1)S(1)}, bf16[288,512]{1,0:T(8,128)(2,1)S(1)}, u32[]{:S(2)}, u32[]{:S(2)}) collective-permute-start(bf16[288,512]{1,0:T(8,128)(2,1)S(1)} %maximum_maximum_fusion.2), channel_id=1, source_target_pairs={{0,4},{4,0},{8,12},{12,8},{1,5},{5,1},{9,13},{13,9},{2,6},{6,2},{1... | collective-permute-start | bytes 884744 | tf_op jit(solution)/shard_map/ppermute | solution.py:100
  16.7 12.6 %collective-permute-start.1 = (bf16[64,2560]{1,0:T(8,128)(2,1)S(1)}, bf16[64,2560]{1,0:T(8,128)(2,1)S(1)}, u32[]{:S(2)}, u32[]{:S(2)}) collective-permute-start(bf16[64,2560]{1,0:T(8,128)(2,1)S(1)} %collective-permute-done), channel_id=1, source_target_pairs={{0,1},{1,0},{2,3},{3,2},{4,5},{5,4},{6,7},{7,6},{8,9},{9,8},{10,11... | collective-permute-start | bytes 983048 | tf_op jit(solution)/shard_map/ppermute | solution.py:97
  16.8 17.2 %slice-start.2 = ((s8[5242880]{0:T(1024)(128)(4,1)}), s8[4194304]{0:T(1024)(128)(4,1)S(1)}, s32[]{:S(2)}) async-start(s8[5242880]{0:T(1024)(128)(4,1)} %bitcast.57), calls=%async_computation.2 | async-start | bytes 8388608
  17.0 12.7 %slice-start = ((s8[5242880]{0:T(1024)(128)(4,1)}), s8[4194304]{0:T(1024)(128)(4,1)S(1)}, s32[]{:S(2)}) async-start(s8[5242880]{0:T(1024)(128)(4,1)} %bitcast.55), calls=%async_computation | async-start | bytes 8388608
  17.1 12.7 %slice-start.1 = ((s8[5242880]{0:T(1024)(128)(4,1)}), s8[1048576]{0:T(1024)(128)(4,1)S(1)}, s32[]{:S(2)}) async-start(s8[5242880]{0:T(1024)(128)(4,1)} %bitcast.55), calls=%async_computation.1 | async-start | bytes 2097152
  17.1 16.9 %slice-start.3 = ((s8[5242880]{0:T(1024)(128)(4,1)}), s8[1048576]{0:T(1024)(128)(4,1)S(1)}, s32[]{:S(2)}) async-start(s8[5242880]{0:T(1024)(128)(4,1)} %bitcast.57), calls=%async_computation.3 | async-start | bytes 2097152
  29.2 8.3 %collective-permute-start.5 = (bf16[288,512]{1,0:T(8,128)(2,1)S(1)}, bf16[288,512]{1,0:T(8,128)(2,1)S(1)}, u32[]{:S(2)}, u32[]{:S(2)}) collective-permute-start(bf16[288,512]{1,0:T(8,128)(2,1)S(1)} %add_convert_fusion.1), channel_id=1, source_target_pairs={{0,1},{1,0},{2,3},{3,2},{4,8},{5,9},{6,10},{7,11},{8,4},{9,5},{10,... | collective-permute-start | bytes 884744 | tf_op jit(solution)/shard_map/ppermute | solution.py:103
  30.8 13.5 %collective-permute-start.7 = (bf16[288,512]{1,0:T(8,128)(2,1)S(1)}, bf16[288,512]{1,0:T(8,128)(2,1)S(1)}, u32[]{:S(2)}, u32[]{:S(2)}) collective-permute-start(bf16[288,512]{1,0:T(8,128)(2,1)S(1)} %maximum_maximum_fusion.3), channel_id=1, source_target_pairs={{0,4},{4,0},{8,12},{12,8},{1,5},{5,1},{9,13},{13,9},{2,6},{6,2},{1... | collective-permute-start | bytes 884744 | tf_op jit(solution)/shard_map/ppermute | solution.py:100
  37.4 1.4 %copy-start.12 = (bf16[128,6144]{1,0:T(8,128)(2,1)S(1)}, bf16[128,6144]{1,0:T(8,128)(2,1)}, u32[]{:S(2)}) copy-start(bf16[128,6144]{1,0:T(8,128)(2,1)} %param.17) | copy-start | bytes 4718596
  37.5 6.8 %collective-permute-start.8 = (bf16[256,512]{1,0:T(8,128)(2,1)S(1)}, bf16[256,512]{1,0:T(8,128)(2,1)S(1)}, u32[]{:S(2)}, u32[]{:S(2)}) collective-permute-start(bf16[256,512]{1,0:T(8,128)(2,1)S(1)} %add_convert_fusion.11), channel_id=1, source_target_pairs={{0,1},{1,0},{2,3},{3,2},{4,8},{5,9},{6,10},{7,11},{8,4},{9,5},{10,... | collective-permute-start | bytes 786440 | tf_op jit(solution)/shard_map/ppermute | solution.py:103
  39.3 11.2 %collective-permute-start.6 = (bf16[256,512]{1,0:T(8,128)(2,1)S(1)}, bf16[256,512]{1,0:T(8,128)(2,1)S(1)}, u32[]{:S(2)}, u32[]{:S(2)}) collective-permute-start(bf16[256,512]{1,0:T(8,128)(2,1)S(1)} %get-tuple-element.162), channel_id=1, source_target_pairs={{0,4},{4,0},{8,12},{12,8},{1,5},{5,1},{9,13},{13,9},{2,6},{6,2},{1... | collective-permute-start | bytes 786440 | tf_op jit(solution)/shard_map/ppermute | solution.py:100
  45.0 7.7 %collective-permute-start.11 = (bf16[256,512]{1,0:T(8,128)(2,1)S(1)}, bf16[256,512]{1,0:T(8,128)(2,1)S(1)}, u32[]{:S(2)}, u32[]{:S(2)}) collective-permute-start(bf16[256,512]{1,0:T(8,128)(2,1)S(1)} %maximum_select_fusion.1), channel_id=1, source_target_pairs={{0,4},{4,0},{8,12},{12,8},{1,5},{5,1},{9,13},{13,9},{2,6},{6,2},{1... | collective-permute-start | bytes 786440 | tf_op jit(solution)/shard_map/ppermute | solution.py:100
  46.5 6.2 %collective-permute-start.9 = (bf16[288,512]{1,0:T(8,128)(2,1)S(1)}, bf16[288,512]{1,0:T(8,128)(2,1)S(1)}, u32[]{:S(2)}, u32[]{:S(2)}) collective-permute-start(bf16[288,512]{1,0:T(8,128)(2,1)S(1)} %add_convert_fusion), channel_id=1, source_target_pairs={{0,1},{1,0},{2,3},{3,2},{4,8},{5,9},{6,10},{7,11},{8,4},{9,5},{10,... | collective-permute-start | bytes 884744 | tf_op jit(solution)/shard_map/ppermute | solution.py:103
  50.6 9.7 %collective-permute-start.12 = (bf16[256,512]{1,0:T(8,128)(2,1)S(1)}, bf16[256,512]{1,0:T(8,128)(2,1)S(1)}, u32[]{:S(2)}, u32[]{:S(2)}) collective-permute-start(bf16[256,512]{1,0:T(8,128)(2,1)S(1)} %add_convert_fusion.10), channel_id=1, source_target_pairs={{0,1},{1,0},{2,3},{3,2},{4,8},{5,9},{6,10},{7,11},{8,4},{9,5},{10,... | collective-permute-start | bytes 786440 | tf_op jit(solution)/shard_map/ppermute | solution.py:103
  53.4 10.2 %collective-permute-start.10 = (bf16[256,512]{1,0:T(8,128)(2,1)S(1)}, bf16[256,512]{1,0:T(8,128)(2,1)S(1)}, u32[]{:S(2)}, u32[]{:S(2)}) collective-permute-start(bf16[256,512]{1,0:T(8,128)(2,1)S(1)} %get-tuple-element.119), channel_id=1, source_target_pairs={{0,4},{4,0},{8,12},{12,8},{1,5},{5,1},{9,13},{13,9},{2,6},{6,2},{1... | collective-permute-start | bytes 786440 | tf_op jit(solution)/shard_map/ppermute | solution.py:100
  60.2 3.6 %collective-permute-start.13 = (bf16[256,512]{1,0:T(8,128)(2,1)S(1)}, bf16[256,512]{1,0:T(8,128)(2,1)S(1)}, u32[]{:S(2)}, u32[]{:S(2)}) collective-permute-start(bf16[256,512]{1,0:T(8,128)(2,1)S(1)} %add_convert_fusion.9), channel_id=1, source_target_pairs={{0,1},{1,0},{2,3},{3,2},{4,8},{5,9},{6,10},{7,11},{8,4},{9,5},{10,... | collective-permute-start | bytes 786440 | tf_op jit(solution)/shard_map/ppermute | solution.py:103
  61.0 9.7 %collective-permute-start.14 = (bf16[256,512]{1,0:T(8,128)(2,1)S(1)}, bf16[256,512]{1,0:T(8,128)(2,1)S(1)}, u32[]{:S(2)}, u32[]{:S(2)}) collective-permute-start(bf16[256,512]{1,0:T(8,128)(2,1)S(1)} %get-tuple-element.114), channel_id=1, source_target_pairs={{0,4},{4,0},{8,12},{12,8},{1,5},{5,1},{9,13},{13,9},{2,6},{6,2},{1... | collective-permute-start | bytes 786440 | tf_op jit(solution)/shard_map/ppermute | solution.py:100
  63.6 11.9 %collective-permute-start.15 = (bf16[256,512]{1,0:T(8,128)(2,1)S(1)}, bf16[256,512]{1,0:T(8,128)(2,1)S(1)}, u32[]{:S(2)}, u32[]{:S(2)}) collective-permute-start(bf16[256,512]{1,0:T(8,128)(2,1)S(1)} %add_convert_fusion.8), channel_id=1, source_target_pairs={{0,1},{1,0},{2,3},{3,2},{4,8},{5,9},{6,10},{7,11},{8,4},{9,5},{10,... | collective-permute-start | bytes 786440 | tf_op jit(solution)/shard_map/ppermute | solution.py:103
  63.8 4.2 %copy-start.3 = (bf16[6144,128]{1,0:T(8,128)(2,1)S(1)}, bf16[6144,128]{1,0:T(8,128)(2,1)}, u32[]{:S(2)}) copy-start(bf16[6144,128]{1,0:T(8,128)(2,1)} %param.20) | copy-start | bytes 4718596
  64.2 11.2 %collective-permute-start.16 = (bf16[256,512]{1,0:T(8,128)(2,1)S(1)}, bf16[256,512]{1,0:T(8,128)(2,1)S(1)}, u32[]{:S(2)}, u32[]{:S(2)}) collective-permute-start(bf16[256,512]{1,0:T(8,128)(2,1)S(1)} %fusion.90), channel_id=1, source_target_pairs={{0,4},{4,0},{8,12},{12,8},{1,5},{5,1},{9,13},{13,9},{2,6},{6,2},{1... | collective-permute-start | bytes 786440 | tf_op jit(solution)/shard_map/ppermute | solution.py:100
  70.8 16.4 %collective-permute-start.18 = (bf16[256,512]{1,0:T(8,128)(2,1)S(1)}, bf16[256,512]{1,0:T(8,128)(2,1)S(1)}, u32[]{:S(2)}, u32[]{:S(2)}) collective-permute-start(bf16[256,512]{1,0:T(8,128)(2,1)S(1)} %add_convert_fusion.7), channel_id=1, source_target_pairs={{0,1},{1,0},{2,3},{3,2},{4,8},{5,9},{6,10},{7,11},{8,4},{9,5},{10,... | collective-permute-start | bytes 786440 | tf_op jit(solution)/shard_map/ppermute | solution.py:103
  75.5 14.9 %collective-permute-start.19 = (bf16[256,512]{1,0:T(8,128)(2,1)S(1)}, bf16[256,512]{1,0:T(8,128)(2,1)S(1)}, u32[]{:S(2)}, u32[]{:S(2)}) collective-permute-start(bf16[256,512]{1,0:T(8,128)(2,1)S(1)} %add_convert_fusion.6), channel_id=1, source_target_pairs={{0,1},{1,0},{2,3},{3,2},{4,8},{5,9},{6,10},{7,11},{8,4},{9,5},{10,... | collective-permute-start | bytes 786440 | tf_op jit(solution)/shard_map/ppermute | solution.py:103
  76.0 14.2 %collective-permute-start.17 = (bf16[256,512]{1,0:T(8,128)(2,1)S(1)}, bf16[256,512]{1,0:T(8,128)(2,1)S(1)}, u32[]{:S(2)}, u32[]{:S(2)}) collective-permute-start(bf16[256,512]{1,0:T(8,128)(2,1)S(1)} %fusion.89), channel_id=1, source_target_pairs={{0,4},{4,0},{8,12},{12,8},{1,5},{5,1},{9,13},{13,9},{2,6},{6,2},{1... | collective-permute-start | bytes 786440 | tf_op jit(solution)/shard_map/ppermute | solution.py:100
  87.6 9.6 %collective-permute-start.20 = (bf16[256,512]{1,0:T(8,128)(2,1)S(1)}, bf16[256,512]{1,0:T(8,128)(2,1)S(1)}, u32[]{:S(2)}, u32[]{:S(2)}) collective-permute-start(bf16[256,512]{1,0:T(8,128)(2,1)S(1)} %fusion.88), channel_id=1, source_target_pairs={{0,4},{4,0},{8,12},{12,8},{1,5},{5,1},{9,13},{13,9},{2,6},{6,2},{1... | collective-permute-start | bytes 786440 | tf_op jit(solution)/shard_map/ppermute | solution.py:100
  90.2 7.2 %collective-permute-start.22 = (bf16[256,512]{1,0:T(8,128)(2,1)S(1)}, bf16[256,512]{1,0:T(8,128)(2,1)S(1)}, u32[]{:S(2)}, u32[]{:S(2)}) collective-permute-start(bf16[256,512]{1,0:T(8,128)(2,1)S(1)} %add_convert_fusion.5), channel_id=1, source_target_pairs={{0,1},{1,0},{2,3},{3,2},{4,8},{5,9},{6,10},{7,11},{8,4},{9,5},{10,... | collective-permute-start | bytes 786440 | tf_op jit(solution)/shard_map/ppermute | solution.py:103
  90.7 11.9 %collective-permute-start.21 = (bf16[256,512]{1,0:T(8,128)(2,1)S(1)}, bf16[256,512]{1,0:T(8,128)(2,1)S(1)}, u32[]{:S(2)}, u32[]{:S(2)}) collective-permute-start(bf16[256,512]{1,0:T(8,128)(2,1)S(1)} %fusion.87), channel_id=1, source_target_pairs={{0,4},{4,0},{8,12},{12,8},{1,5},{5,1},{9,13},{13,9},{2,6},{6,2},{1... | collective-permute-start | bytes 786440 | tf_op jit(solution)/shard_map/ppermute | solution.py:100
  97.3 5.6 %collective-permute-start.23 = (bf16[256,512]{1,0:T(8,128)(2,1)S(1)}, bf16[256,512]{1,0:T(8,128)(2,1)S(1)}, u32[]{:S(2)}, u32[]{:S(2)}) collective-permute-start(bf16[256,512]{1,0:T(8,128)(2,1)S(1)} %add_convert_fusion.4), channel_id=1, source_target_pairs={{0,1},{1,0},{2,3},{3,2},{4,8},{5,9},{6,10},{7,11},{8,4},{9,5},{10,... | collective-permute-start | bytes 786440 | tf_op jit(solution)/shard_map/ppermute | solution.py:103
  98.0 12.7 %collective-permute-start.24 = (bf16[256,512]{1,0:T(8,128)(2,1)S(1)}, bf16[256,512]{1,0:T(8,128)(2,1)S(1)}, u32[]{:S(2)}, u32[]{:S(2)}) collective-permute-start(bf16[256,512]{1,0:T(8,128)(2,1)S(1)} %get-tuple-element.154), channel_id=1, source_target_pairs={{0,4},{4,0},{8,12},{12,8},{1,5},{5,1},{9,13},{13,9},{2,6},{6,2},{1... | collective-permute-start | bytes 786440 | tf_op jit(solution)/shard_map/ppermute | solution.py:100
  102.7 8.3 %collective-permute-start.25 = (bf16[256,512]{1,0:T(8,128)(2,1)S(1)}, bf16[256,512]{1,0:T(8,128)(2,1)S(1)}, u32[]{:S(2)}, u32[]{:S(2)}) collective-permute-start(bf16[256,512]{1,0:T(8,128)(2,1)S(1)} %add_convert_fusion.3), channel_id=1, source_target_pairs={{0,1},{1,0},{2,3},{3,2},{4,8},{5,9},{6,10},{7,11},{8,4},{9,5},{10,... | collective-permute-start | bytes 786440 | tf_op jit(solution)/shard_map/ppermute | solution.py:103
  103.4 11.0 %collective-permute-start.27 = (bf16[256,512]{1,0:T(8,128)(2,1)S(1)}, bf16[256,512]{1,0:T(8,128)(2,1)S(1)}, u32[]{:S(2)}, u32[]{:S(2)}) collective-permute-start(bf16[256,512]{1,0:T(8,128)(2,1)S(1)} %pad_maximum_fusion.10), channel_id=1, source_target_pairs={{0,4},{4,0},{8,12},{12,8},{1,5},{5,1},{9,13},{13,9},{2,6},{6,2},{1... | collective-permute-start | bytes 786440 | tf_op jit(solution)/shard_map/ppermute | solution.py:100
  110.8 3.8 %collective-permute-start.28 = (bf16[256,512]{1,0:T(8,128)(2,1)S(1)}, bf16[256,512]{1,0:T(8,128)(2,1)S(1)}, u32[]{:S(2)}, u32[]{:S(2)}) collective-permute-start(bf16[256,512]{1,0:T(8,128)(2,1)S(1)} %add_convert_fusion.2), channel_id=1, source_target_pairs={{0,1},{1,0},{2,3},{3,2},{4,8},{5,9},{6,10},{7,11},{8,4},{9,5},{10,... | collective-permute-start | bytes 786440 | tf_op jit(solution)/shard_map/ppermute | solution.py:103
  111.5 9.2 %collective-permute-start.26 = (bf16[256,512]{1,0:T(8,128)(2,1)S(1)}, bf16[256,512]{1,0:T(8,128)(2,1)S(1)}, u32[]{:S(2)}, u32[]{:S(2)}) collective-permute-start(bf16[256,512]{1,0:T(8,128)(2,1)S(1)} %pad_maximum_fusion.11), channel_id=1, source_target_pairs={{0,4},{4,0},{8,12},{12,8},{1,5},{5,1},{9,13},{13,9},{2,6},{6,2},{1... | collective-permute-start | bytes 786440 | tf_op jit(solution)/shard_map/ppermute | solution.py:100
  115.1 10.8 %collective-permute-start.30 = (bf16[256,512]{1,0:T(8,128)(2,1)S(1)}, bf16[256,512]{1,0:T(8,128)(2,1)S(1)}, u32[]{:S(2)}, u32[]{:S(2)}) collective-permute-start(bf16[256,512]{1,0:T(8,128)(2,1)S(1)} %pad_maximum_fusion.15), channel_id=1, source_target_pairs={{0,4},{4,0},{8,12},{12,8},{1,5},{5,1},{9,13},{13,9},{2,6},{6,2},{1... | collective-permute-start | bytes 786440 | tf_op jit(solution)/shard_map/ppermute | solution.py:100
  120.5 5.5 %collective-permute-start.29 = (bf16[64,2688]{1,0:T(8,128)(2,1)S(1)}, bf16[64,2688]{1,0:T(8,128)(2,1)S(1)}, u32[]{:S(2)}, u32[]{:S(2)}) collective-permute-start(bf16[64,2688]{1,0:T(8,128)(2,1)S(1)} %fusion.24), channel_id=1, source_target_pairs={{0,1},{1,0},{2,3},{3,2},{4,5},{5,4},{6,7},{7,6},{8,9},{9,8},{10,11... | collective-permute-start | bytes 1032200 | tf_op jit(solution)/shard_map/ppermute | solution.py:97
  128.4 10.7 %copy-start.9 = (f32[2560]{0:T(1024)S(1)}, f32[2560]{0:T(1024)}, u32[]{:S(2)}) copy-start(f32[2560]{0:T(1024)} %param.19) | copy-start | bytes 30724
  128.4 1.7 %collective-permute-start.31 = (bf16[64,2688]{1,0:T(8,128)(2,1)S(1)}, bf16[64,2688]{1,0:T(8,128)(2,1)S(1)}, u32[]{:S(2)}, u32[]{:S(2)}) collective-permute-start(bf16[64,2688]{1,0:T(8,128)(2,1)S(1)} %fusion.23), channel_id=1, source_target_pairs={{0,1},{1,0},{2,3},{3,2},{4,5},{5,4},{6,7},{7,6},{8,9},{9,8},{10,11... | collective-permute-start | bytes 1032200 | tf_op jit(solution)/shard_map/ppermute | solution.py:97
  128.5 10.5 %collective-permute-start.32 = (bf16[64,2688]{1,0:T(8,128)(2,1)S(1)}, bf16[64,2688]{1,0:T(8,128)(2,1)S(1)}, u32[]{:S(2)}, u32[]{:S(2)}) collective-permute-start(bf16[64,2688]{1,0:T(8,128)(2,1)S(1)} %fusion.22), channel_id=1, source_target_pairs={{0,2},{1,3},{2,0},{3,1},{4,6},{5,7},{6,4},{7,5},{8,10},{9,11},{10,... | collective-permute-start | bytes 1032200 | tf_op jit(solution)/shard_map/ppermute | solution.py:97

commit v10 on v9

--- a/solution.py
+++ b/solution.py
@@ -111,6 +111,7 @@
 
     def pipeline(
         tokens,
+        jobs,
         mine,
         mask_of,
         first_weight,
@@ -138,29 +139,20 @@
         def unfold(value):
             return jnp.concatenate([value[:near], value[near : 2 * near]], axis=1)
 
+        def block_of(unit):
+            return unit % 3 if unit < 6 else 3 + unit % 3
+
+        def is_near(unit):
+            return unit < 3 or unit >= 9
+
         def columns(unit):
-            if unit < 4:
-                start, size = (unit % 2) * wide, wide
-            elif unit < 8:
-                start, size = unit * width, width
-            else:
-                start, size = 8 * width + (unit % 2) * wide, wide
-            return slice(start, start + size)
-
-        def own_chip(unit):
-            return unit in (0, 1, 10, 11)
+            return slice(block_of(unit) * wide, (block_of(unit) + 1) * wide)
 
         def load(block):
             nonlocal last
             part = (pl.ds(0, first_weight.shape[0]), pl.ds(block * wide, wide))
-            loads[block] = load_part(first_weight, part, last[:16, :LANES])
+            loads[block] = load_part(first_weight, part, last)
             last = loads[block]
-
-        def load_second(block):
-            nonlocal last
-            part = (pl.ds(block * wide, wide), pl.ds(0, second_weight.shape[1]))
-            second_loads[block] = load_part(second_weight, part, last[:16, :LANES])
-            last = second_loads[block]
 
         def multiply(x, block):
             nonlocal last
@@ -170,21 +162,17 @@
 
         def first_half(unit, x):
             nonlocal last
-            value = halves(multiply(x, unit % 2))
-            if unit in (0, 2):
+            value = halves(multiply(x, block_of(unit)))
+            if unit in (0, 3):
                 low = dot(x, first_down_maps).astype(BF16)
                 low = jnp.concatenate(jnp.split(low, fold, axis=0), axis=1)
                 value = jnp.concatenate([value, low], axis=0)
             partials[unit] = value
             last = value
 
-        def first_pair(unit, x):
-            value = multiply(x, unit // 2)
-            partials[unit], partials[unit + 1] = value[:, :width], value[:, width:]
-
         def first_late(unit, x):
-            value = multiply(x, unit - 4)
-            partials[unit + 2], partials[unit] = halves(value[:near]), halves(value[near:])
+            value = multiply(x, block_of(unit))
+            partials[unit + 3], partials[unit] = halves(value[:near]), halves(value[near:])
 
         def send(t, value):
             payloads[t] = value
@@ -198,29 +186,29 @@
             states = tie(states, last)
             part = slice(block * wide, (block + 1) * wide)
             low = dot(states, second_down_maps[part])
-            value = dot(states, second_loads[block] if block in second_loads else second_weight[part])
-            last = value[:8, :LANES]
+            value = dot(states, second_weight[part])
             if name in outputs:
                 value, low = outputs[name][0] + value, outputs[name][1] + low
+            value = lax.optimization_barrier(value)
+            last = value[:8, :LANES]
             outputs[name] = (value, low)
 
-        def core_sum(name):
+        def core_parts(name):
             joined = jnp.concatenate(outputs[name], axis=1)
-            return joined[:rows] + col_swap(joined[rows:].astype(BF16), 1).astype(F32)
+            return joined[:rows], joined[rows:].astype(BF16)
 
         far = col_swap(tokens, 2)
-        loads, second_loads, outputs = {}, {}, {}
-        last, is_end, mine = lax.optimization_barrier((tokens[:16, :LANES], is_end, mine))
+        loads, outputs = {}, {}
+        last, is_end, mine = lax.optimization_barrier((jobs, is_end, mine))
         load(0)
         gathered_near = jnp.concatenate([tokens, tie(col_swap(tokens, 1), last)], axis=0)
-        first_half(0, gathered_near)
-        send(0, partials[0])
-        load(1)
-        first_half(1, gathered_near)
-        send(1, partials[1])
+        for unit in range(3):
+            if unit > 0:
+                load(unit)
+            first_half(unit, gathered_near)
+            send(unit, partials[unit])
         mask = mask_of(mine, last)
         first_bias = tie(first_bias, last)
-        load(2)
         for t in range(UNITS + LAG):
             if t < UNITS:
                 ours = tie(partials[t], last).astype(F32)
@@ -229,55 +217,48 @@
                 crosses[t] = cross(sums[t])
             if t == 0:
                 gathered_far = jnp.concatenate([far, col_swap(far, 1)], axis=0)
-                first_half(2, gathered_far)
-                send(2, partials[2])
-                first_half(3, gathered_far)
                 gathered = jnp.concatenate([gathered_near, gathered_far], axis=0)
+                for unit in range(3, 6):
+                    first_half(unit, gathered_far)
             k = t - 1
             if 0 <= k < UNITS:
                 summed = tie(sums[k], last).astype(F32) + crosses[k].astype(F32)
-                if k in (0, 2):
+                if k in (0, 3):
                     low = jnp.concatenate(jnp.split(summed[2 * near :], fold, axis=1), axis=0)
                     own_mask = mask[:near] if k == 0 else mask[near:]
-                    low_in[k] = jnp.where(own_mask, low, 0.0).astype(BF16)
-                if 4 <= k < 8:
-                    low = jnp.concatenate([low_in[0], low_in[2]], axis=0)
-                    value = activate(summed, low, first_up_maps, first_bias, columns(k))
-                else:
-                    low = low_in[0] if own_chip(k) else low_in[2]
-                    value = activate(unfold(summed), low, first_up_maps, first_bias, columns(k))
-                    value = halves(value)
+                    low_in[is_near(k)] = jnp.where(own_mask, low, 0.0).astype(BF16)
+                low = low_in[is_near(k)]
+                value = activate(unfold(summed), low, first_up_maps, first_bias, columns(k))
+                value = halves(value)
+                if k + LAG == 3:
+                    value = jnp.concatenate([value, jnp.zeros_like(value[: near // fold])], axis=0)
                 if k + LAG < UNITS:
                     value = jnp.where(is_end, partials[k + LAG], value)
                 last = value
                 send(k + LAG, value)
-            if t < 3:
-                load(t + 3)
-            if t in (1, 2):
-                first_pair(2 * t + 2, gathered)
-            elif t == 3:
-                first_late(8, gathered)
-                first_late(9, gathered)
-            elif t in (5, 6):
-                top, bottom = unfold(state(t - 5)), unfold(state(t - 3))
-                second("all", jnp.concatenate([top, bottom], axis=0), t - 5)
-            elif t in (7, 9):
-                load_second((t + 1) // 2)
-            elif t in (8, 10):
-                states = jnp.concatenate([state(t - 4), state(t - 3)], axis=1)
-                second("all", states, t // 2 - 2)
-            elif t >= 11:
+            if t in (1, 2, 3):
+                load(t + 2)
+                first_late(t + 5, gathered)
+            elif t in (6, 7, 8):
+                top, bottom = unfold(state(t - 6)), unfold(state(t - 3))
+                second("all", jnp.concatenate([top, bottom], axis=0), t - 6)
+            elif t >= 9:
                 unit = t - LAG
-                if t == 11:
+                if t == 9:
                     value, low = outputs["all"]
                     outputs["near"] = (value[:near], low[:near])
                     outputs["far"] = (value[near:], low[near:])
-                second("near" if own_chip(unit) else "far", unfold(state(unit)), 4 + unit % 2)
-                if t == 12:
-                    across = core_sum("far").astype(BF16)
+                if t == 13:
+                    last = across
+                second("near" if is_near(unit) else "far", unfold(state(unit)), block_of(unit))
+                if t == 11:
+                    ours, theirs = core_parts("far")
+                    across = (ours + col_swap(theirs, 1).astype(F32)).astype(BF16)
                     last = across
                     across = col_swap(across, 2)
-        return core_sum("near") + across.astype(F32), mask
+        ours, theirs = core_parts("near")
+        come = col_swap(theirs, 1)
+        return ours + come.astype(F32) + across.astype(F32), mask
 
     def plain(tokens, mask, second_weight, second_down_maps, *first):
         rows = tokens.shape[0]
@@ -311,17 +292,18 @@
         mine = lax.axis_index("col")
 
         def mask_of(mine, after):
-            index = tie(token_job_index, after)
+            mask = token_mask(tie(token_job_index, after), job_adapter_index).astype(jnp.int32)
             for bit in range(n_col.bit_length() - 1):
-                pairs = index.reshape(-1, 2, rows << bit)
-                turned = jnp.concatenate([pairs[:, 1:], pairs[:, :1]], axis=1)
-                index = jnp.where((mine >> bit) & 1 == 1, turned, pairs).reshape(-1)
-            return token_mask(index, job_adapter_index)
+                size = rows << bit
+                blocks = [mask[i : i + size] for i in range(0, mask.shape[0], size)]
+                turned = jnp.concatenate([blocks[i ^ 1] for i in range(len(blocks))], axis=0)
+                mask = jnp.where((mine >> bit) & 1 == 1, turned, mask)
+            return mask == 1
 
         first = (first_weight, first_bias, first_down_maps, first_up_maps)
         even = first_weight.shape[1] % (UNITS * LANES) == 0
         if n_row == 4 and n_col == 4 and even:
-            result, mask = pipeline(tokens, mine, mask_of, *first, second_weight, second_down_maps)
+            result, mask = pipeline(tokens, job_adapter_index, mine, mask_of, *first, second_weight, second_down_maps)
         else:
             mask = mask_of(mine, tokens)
             result = plain(tokens, mask, second_weight, second_down_maps, *first)

time: 141 us -> 135 us (0.957)
  Pallas kernels: 20.2 us -> 15.2 us
  other arithmetic: 3.47 us -> 7.78 us
  matrix products: 37.7 us -> 35.2 us
  starting transfers between devices: 38.3 us -> 35.9 us
    ppermute x15, waiting for transfers between devices: 22.9 us -> 30.6 us  [end_swap(): return lax.ppermute(value, 'row', [(i, i ^ 1) for i in range(n_row)])]
    ppermute x6, waiting for transfers between devices: 9.88 us -> 2.54 us  [col_swap(): return lax.ppermute(value, 'col', [(i, i ^ flip) for i in range(n_col)])]
    pallas_call x8 -> x6, Pallas kernels: 20.2 us -> 15.2 us  [load_part(): pl.pallas_call(functools.partial(load_kernel, part=part), in_specs=[pl.Bl...]
    ppermute x15, starting transfers between devices: 33.2 us -> 30.7 us  [end_swap(): return lax.ppermute(value, 'row', [(i, i ^ 1) for i in range(n_row)])]
    dot_general x39 -> x42, matrix products: 37.7 us -> 35.2 us  [dot(): return jnp.dot(left, right, preferred_element_type=F32)]
    select_n x12 -> x11, other arithmetic: 0.46 us -> 2.41 us  [state(): return jnp.where(is_end, swaps[unit + LAG], payloads[unit + LAG])]
    unnamed x37 -> x55, local copies, waits for them, and re-layouts: 4.27 us -> 3.33 us
  transfers between devices with their start and end apart: 33 -> 33, of which waited for: 8 -> 11; matrix products, arithmetic and copies ran while one was open for 28% -> 31% of each run, Pallas kernels for 14% -> 11%
where the time goes in v10:
time: 135 us; the launch traced here: 134 us
  starting transfers between devices  35.9 us (27%)
  matrix products  35.2 us (26%)
  waiting for transfers between devices  33.2 us (25%)
  Pallas kernels  15.2 us (11%)
  other arithmetic  7.78 us (6%)
  local copies, waits for them, and re-layouts  5.3 us (4%)
  between operations  1.79 us (1%)
    dot_general x42, matrix products, dot(): return jnp.dot(left, right, preferred_element_type=F32)  35.2 us
    ppermute x15, starting transfers between devices, end_swap(): return lax.ppermute(value, 'row', [(i, i ^ 1) for i in range(n_row)])  30.7 us
    ppermute x15, waiting for transfers between devices, end_swap(): return lax.ppermute(value, 'row', [(i, i ^ 1) for i in range(n_row)])  30.6 us
    pallas_call x6, Pallas kernels, load_part(): pl.pallas_call(functools.partial(load_kernel, part=part), in_specs=[pl.Bl...  15.2 us
    ppermute x6, starting transfers between devices, col_swap(): return lax.ppermute(value, 'col', [(i, i ^ flip) for i in range(n_col)])  3.75 us
    unnamed x55, local copies, waits for them, and re-layouts  3.33 us
  transfers between devices with their start and end apart: 33, of which 11 were waited for; matrix products, arithmetic and copies ran while one was open for 31% of the time, Pallas kernels for 11%

profile of v10, /device:TPU:0, one launch (start us, length us, event | category | flops | bytes accessed | tf_op | source)
XLA Modules:
  0.0 134.3 jit_solution(6311086487804700998)
XLA Ops:
  0.0 2.9 %collective-permute-start = (bf16[64,2560]{1,0:T(8,128)(2,1)}, bf16[64,2560]{1,0:T(8,128)(2,1)S(1)}, u32[]{:S(2)}, u32[]{:S(2)}) collective-permute-start(bf16[64,2560]{1,0:T(8,128)(2,1)} %param.11), channel_id=1, source_target_pairs={{0,2},{1,3},{2,0},{3,1},{4,6},{5,7},{6,4},{7,5},{8,10},{9,11},{10,... | collective-permute-start | bytes 983048 | tf_op jit(solution)/shard_map/ppermute | solution.py:97
  3.0 0.6 copy-done.1
  3.6 2.5 %shard_map.109 = bf16[2560,1024]{1,0:T(8,128)(2,1)S(1)} custom-call(bf16[2560,6144]{1,0:T(8,128)(2,1)} %w_hbm.11, s32[4]{0:T(128)S(1)} %copy-done.1), custom_call_target="tpu_custom_call" | custom-call | bytes 1000 | tf_op jit(solution)/shard_map/pallas_call | solution.py:51
  6.3 1.0 copy-done.4
  7.6 0.9 convolution_convert_fusion.8
  8.6 1.6 %collective-permute-start.3 = (bf16[288,512]{1,0:T(8,128)(2,1)S(1)}, bf16[288,512]{1,0:T(8,128)(2,1)S(1)}, u32[]{:S(2)}, u32[]{:S(2)}) collective-permute-start(bf16[288,512]{1,0:T(8,128)(2,1)S(1)} %maximum_maximum_fusion.3.after_ref), channel_id=1, source_target_pairs={{0,4},{4,0},{8,12},{12,8},{1,5},{5,1},{9,13},{13,9},{2,6},{6,2},{1... | collective-permute-start | bytes 884744 | tf_op jit(solution)/shard_map/ppermute | solution.py:100
  10.3 2.5 %shard_map.110 = bf16[2560,1024]{1,0:T(8,128)(2,1)S(1)} custom-call(bf16[2560,6144]{1,0:T(8,128)(2,1)} %w_hbm.11, bf16[288,512]{1,0:T(8,128)(2,1)S(1)} %maximum_maximum_fusion.3.after_ref), custom_call_target="tpu_custom_call" | custom-call | bytes 1000 | tf_op jit(solution)/shard_map/pallas_call | solution.py:51
  12.8 0.9 convolution_convert_fusion.7
  14.3 2.5 %shard_map.111 = bf16[2560,1024]{1,0:T(8,128)(2,1)S(1)} custom-call(bf16[2560,6144]{1,0:T(8,128)(2,1)} %w_hbm.11, bf16[256,512]{1,0:T(8,128)(2,1)S(1)} %pad_maximum_fusion.2.after_ref), custom_call_target="tpu_custom_call" | custom-call | bytes 1000 | tf_op jit(solution)/shard_map/pallas_call | solution.py:51
  16.8 0.9 convolution_convert_fusion.6
  17.8 1.6 %collective-permute-start.7 = (bf16[256,512]{1,0:T(8,128)(2,1)S(1)}, bf16[256,512]{1,0:T(8,128)(2,1)S(1)}, u32[]{:S(2)}, u32[]{:S(2)}) collective-permute-start(bf16[256,512]{1,0:T(8,128)(2,1)S(1)} %pad_maximum_fusion.3), channel_id=1, source_target_pairs={{0,4},{4,0},{8,12},{12,8},{1,5},{5,1},{9,13},{13,9},{2,6},{6,2},{1... | collective-permute-start | bytes 786440 | tf_op jit(solution)/shard_map/ppermute | solution.py:100
  20.7 0.9 collective-permute-done.1
  21.9 0.8 convolution_convert_fusion.5
  22.9 0.8 convolution_convert_fusion.4
  23.8 0.8 convolution_convert_fusion.3
  25.2 0.9 copy-done.16
  26.6 5.3 %collective-permute-start.6 = (bf16[288,512]{1,0:T(8,128)(2,1)S(1)}, bf16[288,512]{1,0:T(8,128)(2,1)S(1)}, u32[]{:S(2)}, u32[]{:S(2)}) collective-permute-start(bf16[288,512]{1,0:T(8,128)(2,1)S(1)} %maximum_select_fusion.after_ref), channel_id=1, source_target_pairs={{0,4},{4,0},{8,12},{12,8},{1,5},{5,1},{9,13},{13,9},{2,6},{6,2},{1... | collective-permute-start | bytes 884744 | tf_op jit(solution)/shard_map/ppermute | solution.py:100
  32.0 2.5 %shard_map.112 = bf16[2560,1024]{1,0:T(8,128)(2,1)S(1)} custom-call(bf16[2560,6144]{1,0:T(8,128)(2,1)} %w_hbm.11, bf16[288,512]{1,0:T(8,128)(2,1)S(1)} %maximum_select_fusion.after_ref), custom_call_target="tpu_custom_call" | custom-call | bytes 1000 | tf_op jit(solution)/shard_map/pallas_call | solution.py:51
  34.5 1.5 %convolution_convert_fusion.2 = bf16[256,1024]{1,0:T(8,128)(2,1)S(1)} fusion(bf16[256,2560]{1,0:T(8,128)(2,1)S(1)} %get-tuple-element.68, bf16[2560,1024]{1,0:T(8,128)(2,1)S(1)} %shard_map.112), kind=kOutput, calls=%fused_computation.31 | convolution fusion | flops 1342439424 | bytes 7077888 | tf_op jit(solution)/shard_map/dot_general | solution.py:36
  36.8 2.0 %collective-permute-start.10 = (bf16[256,512]{1,0:T(8,128)(2,1)S(1)}, bf16[256,512]{1,0:T(8,128)(2,1)S(1)}, u32[]{:S(2)}, u32[]{:S(2)}) collective-permute-start(bf16[256,512]{1,0:T(8,128)(2,1)S(1)} %maximum_select_fusion.1.after_ref), channel_id=1, source_target_pairs={{0,4},{4,0},{8,12},{12,8},{1,5},{5,1},{9,13},{13,9},{2,6},{6,2},{1... | collective-permute-start | bytes 786440 | tf_op jit(solution)/shard_map/ppermute | solution.py:100
  38.8 2.5 %shard_map.113 = bf16[2560,1024]{1,0:T(8,128)(2,1)S(1)} custom-call(bf16[2560,6144]{1,0:T(8,128)(2,1)} %w_hbm.11, bf16[256,512]{1,0:T(8,128)(2,1)S(1)} %maximum_select_fusion.1.after_ref), custom_call_target="tpu_custom_call" | custom-call | bytes 1000 | tf_op jit(solution)/shard_map/pallas_call | solution.py:51
  41.3 1.5 %convolution_convert_fusion.1 = bf16[256,1024]{1,0:T(8,128)(2,1)S(1)} fusion(bf16[256,2560]{1,0:T(8,128)(2,1)S(1)} %get-tuple-element.68, bf16[2560,1024]{1,0:T(8,128)(2,1)S(1)} %shard_map.113), kind=kOutput, calls=%fused_computation.30 | convolution fusion | flops 1342439424 | bytes 7077888 | tf_op jit(solution)/shard_map/dot_general | solution.py:36
  42.9 2.6 %collective-permute-done.10 = bf16[256,512]{1,0:T(8,128)(2,1)S(1)} collective-permute-done((bf16[256,512]{1,0:T(8,128)(2,1)S(1)}, bf16[256,512]{1,0:T(8,128)(2,1)S(1)}, u32[]{:S(2)}, u32[]{:S(2)}) %collective-permute-start.10) | collective-permute-done | bytes 262176 | tf_op jit(solution)/shard_map/ppermute | solution.py:100
  46.3 2.3 %collective-permute-start.13 = (bf16[256,512]{1,0:T(8,128)(2,1)S(1)}, bf16[256,512]{1,0:T(8,128)(2,1)S(1)}, u32[]{:S(2)}, u32[]{:S(2)}) collective-permute-start(bf16[256,512]{1,0:T(8,128)(2,1)S(1)} %maximum_select_fusion.2.after_ref), channel_id=1, source_target_pairs={{0,4},{4,0},{8,12},{12,8},{1,5},{5,1},{9,13},{13,9},{2,6},{6,2},{1... | collective-permute-start | bytes 786440 | tf_op jit(solution)/shard_map/ppermute | solution.py:100
  48.6 2.6 %shard_map.114 = bf16[2560,1024]{1,0:T(8,128)(2,1)S(1)} custom-call(bf16[2560,6144]{1,0:T(8,128)(2,1)} %w_hbm.11, bf16[256,512]{1,0:T(8,128)(2,1)S(1)} %maximum_select_fusion.2.after_ref), custom_call_target="tpu_custom_call" | custom-call | bytes 1000 | tf_op jit(solution)/shard_map/pallas_call | solution.py:51
  51.3 1.7 %convolution_convert_fusion = bf16[256,1024]{1,0:T(8,128)(2,1)S(1)} fusion(bf16[256,2560]{1,0:T(8,128)(2,1)S(1)} %get-tuple-element.68, bf16[2560,1024]{1,0:T(8,128)(2,1)S(1)} %shard_map.114), kind=kOutput, calls=%fused_computation.29 | convolution fusion | flops 1342439424 | bytes 7077888 | tf_op jit(solution)/shard_map/dot_general | solution.py:36
  53.3 0.8 fusion.149
  54.0 1.1 collective-permute-done.13
  56.0 2.2 %collective-permute-start.12 = (bf16[256,512]{1,0:T(8,128)(2,1)S(1)}, bf16[256,512]{1,0:T(8,128)(2,1)S(1)}, u32[]{:S(2)}, u32[]{:S(2)}) collective-permute-start(bf16[256,512]{1,0:T(8,128)(2,1)S(1)} %get-tuple-element.192), channel_id=1, source_target_pairs={{0,4},{4,0},{8,12},{12,8},{1,5},{5,1},{9,13},{13,9},{2,6},{6,2},{1... | collective-permute-start | bytes 786440 | tf_op jit(solution)/shard_map/ppermute | solution.py:100
  58.8 4.3 %collective-permute-start.16 = (bf16[256,512]{1,0:T(8,128)(2,1)S(1)}, bf16[256,512]{1,0:T(8,128)(2,1)S(1)}, u32[]{:S(2)}, u32[]{:S(2)}) collective-permute-start(bf16[256,512]{1,0:T(8,128)(2,1)S(1)} %get-tuple-element.188), channel_id=1, source_target_pairs={{0,4},{4,0},{8,12},{12,8},{1,5},{5,1},{9,13},{13,9},{2,6},{6,2},{1... | collective-permute-start | bytes 786440 | tf_op jit(solution)/shard_map/ppermute | solution.py:100
  63.1 2.2 %collective-permute-done.12 = bf16[256,512]{1,0:T(8,128)(2,1)S(1)} collective-permute-done((bf16[256,512]{1,0:T(8,128)(2,1)S(1)}, bf16[256,512]{1,0:T(8,128)(2,1)S(1)}, u32[]{:S(2)}, u32[]{:S(2)}) %collective-permute-start.12) | collective-permute-done | bytes 262176 | tf_op jit(solution)/shard_map/ppermute | solution.py:100
  66.1 4.3 %collective-permute-done.16 = bf16[256,512]{1,0:T(8,128)(2,1)S(1)} collective-permute-done((bf16[256,512]{1,0:T(8,128)(2,1)S(1)}, bf16[256,512]{1,0:T(8,128)(2,1)S(1)}, u32[]{:S(2)}, u32[]{:S(2)}) %collective-permute-start.16) | collective-permute-done | bytes 262176 | tf_op jit(solution)/shard_map/ppermute | solution.py:100
  70.6 2.3 %collective-permute-start.18 = (bf16[256,512]{1,0:T(8,128)(2,1)S(1)}, bf16[256,512]{1,0:T(8,128)(2,1)S(1)}, u32[]{:S(2)}, u32[]{:S(2)}) collective-permute-start(bf16[256,512]{1,0:T(8,128)(2,1)S(1)} %get-tuple-element.180), channel_id=1, source_target_pairs={{0,4},{4,0},{8,12},{12,8},{1,5},{5,1},{9,13},{13,9},{2,6},{6,2},{1... | collective-permute-start | bytes 786440 | tf_op jit(solution)/shard_map/ppermute | solution.py:100
  72.9 1.9 %fusion.112 = f32[256,128]{1,0:T(8,128)} fusion(bf16[256,1024]{1,0:T(8,128)(2,1)S(1)} %maximum_maximum_fusion, bf16[6144,128]{1,0:T(8,128)(2,1)} %param.20), kind=kOutput, calls=%fused_computation.217 | convolution fusion | flops 67108864 | bytes 917504 | tf_op jit(solution)/shard_map/dot_general | solution.py:36
  74.8 1.5 %fusion.4 = f32[256,2560]{1,0:T(8,128)S(1)} fusion(bf16[256,1024]{1,0:T(8,128)(2,1)S(1)} %maximum_maximum_fusion, bf16[6144,2560]{1,0:T(8,128)(2,1)S(1)} %bitcast.54), kind=kOutput, calls=%fused_computation.4 | convolution fusion | flops 1342177280 | bytes 8388608 | tf_op jit(solution)/shard_map/dot_general | solution.py:36
  76.5 2.8 %collective-permute-done.18 = bf16[256,512]{1,0:T(8,128)(2,1)S(1)} collective-permute-done((bf16[256,512]{1,0:T(8,128)(2,1)S(1)}, bf16[256,512]{1,0:T(8,128)(2,1)S(1)}, u32[]{:S(2)}, u32[]{:S(2)}) %collective-permute-start.18) | collective-permute-done | bytes 262176 | tf_op jit(solution)/shard_map/ppermute | solution.py:100
  79.6 1.3 fusion.84
  81.0 2.3 %collective-permute-start.20 = (bf16[256,512]{1,0:T(8,128)(2,1)S(1)}, bf16[256,512]{1,0:T(8,128)(2,1)S(1)}, u32[]{:S(2)}, u32[]{:S(2)}) collective-permute-start(bf16[256,512]{1,0:T(8,128)(2,1)S(1)} %get-tuple-element.184), channel_id=1, source_target_pairs={{0,4},{4,0},{8,12},{12,8},{1,5},{5,1},{9,13},{13,9},{2,6},{6,2},{1... | collective-permute-start | bytes 786440 | tf_op jit(solution)/shard_map/ppermute | solution.py:100
  83.5 1.3 fusion.89
  84.8 0.8 pad_maximum_fusion.10
  86.1 1.5 %fusion.18 = f32[256,2560]{1,0:T(8,128)S(1)} fusion(f32[256,2560]{1,0:T(8,128)S(1)} %fusion.4, bf16[256,1024]{1,0:T(8,128)(2,1)S(1)} %maximum_maximum_fusion.1, bf16[6144,2560]{1,0:T(8,128)(2,1)S(1)} %bitcast.54), kind=kOutput, calls=%fused_computation.18 | convolution fusion | flops 1342832640 | bytes 11010048 | tf_op jit(solution)/shard_map/dot_general | solution.py:36
  87.6 1.5 %fusion.21 = f32[256,2560]{1,0:T(8,128)S(1)} fusion(f32[256,2560]{1,0:T(8,128)S(1)} %fusion.18, bf16[256,1024]{1,0:T(8,128)(2,1)S(1)} %maximum_maximum_fusion.2, bf16[6144,2560]{1,0:T(8,128)(2,1)S(1)} %bitcast.54), kind=kOutput, calls=%fused_computation.19 | convolution fusion | flops 1342832640 | bytes 11010048 | tf_op jit(solution)/shard_map/dot_general | solution.py:36
  89.2 1.3 convolution_add_fusion.13
  90.4 1.3 convolution_add_fusion.12
  91.9 3.5 %collective-permute-done.21 = bf16[256,512]{1,0:T(8,128)(2,1)S(1)} collective-permute-done((bf16[256,512]{1,0:T(8,128)(2,1)}, bf16[256,512]{1,0:T(8,128)(2,1)S(1)}, u32[]{:S(2)}, u32[]{:S(2)}) %collective-permute-start.21) | collective-permute-done | bytes 262176 | tf_op jit(solution)/shard_map/ppermute | solution.py:100
  95.7 1.1 convert_add_fusion.4
  97.8 2.2 %collective-permute-start.25 = (bf16[256,512]{1,0:T(8,128)(2,1)S(1)}, bf16[256,512]{1,0:T(8,128)(2,1)S(1)}, u32[]{:S(2)}, u32[]{:S(2)}) collective-permute-start(bf16[256,512]{1,0:T(8,128)(2,1)S(1)} %get-tuple-element.168), channel_id=1, source_target_pairs={{0,4},{4,0},{8,12},{12,8},{1,5},{5,1},{9,13},{13,9},{2,6},{6,2},{1... | collective-permute-start | bytes 786440 | tf_op jit(solution)/shard_map/ppermute | solution.py:100
  100.3 0.9 fusion.24
  101.2 5.2 %collective-permute-done.25 = bf16[256,512]{1,0:T(8,128)(2,1)S(1)} collective-permute-done((bf16[256,512]{1,0:T(8,128)(2,1)S(1)}, bf16[256,512]{1,0:T(8,128)(2,1)S(1)}, u32[]{:S(2)}, u32[]{:S(2)}) %collective-permute-start.25) | collective-permute-done | bytes 262176 | tf_op jit(solution)/shard_map/ppermute | solution.py:100
  107.2 2.3 %collective-permute-start.23 = (bf16[256,512]{1,0:T(8,128)(2,1)S(1)}, bf16[256,512]{1,0:T(8,128)(2,1)}, u32[]{:S(2)}, u32[]{:S(2)}) collective-permute-start(bf16[256,512]{1,0:T(8,128)(2,1)S(1)} %pad_maximum_fusion.11), channel_id=1, source_target_pairs={{0,4},{4,0},{8,12},{12,8},{1,5},{5,1},{9,13},{13,9},{2,6},{6,2},{1... | collective-permute-start | bytes 786440 | tf_op jit(solution)/shard_map/ppermute | solution.py:100
  110.4 1.1 fusion.30
  111.8 0.9 fusion.36
  112.8 3.9 %collective-permute-done.23 = bf16[256,512]{1,0:T(8,128)(2,1)} collective-permute-done((bf16[256,512]{1,0:T(8,128)(2,1)S(1)}, bf16[256,512]{1,0:T(8,128)(2,1)}, u32[]{:S(2)}, u32[]{:S(2)}) %collective-permute-start.23) | collective-permute-done | bytes 262176 | tf_op jit(solution)/shard_map/ppermute | solution.py:100
  116.7 1.0 broadcast_select_fusion.6
  117.8 0.6 collective-permute-start.30
  118.6 1.3 fusion.109
  119.9 1.3 collective-permute-start.31
  121.2 0.9 fusion.27
  122.3 4.9 %collective-permute-done.31 = bf16[256,512]{1,0:T(8,128)(2,1)S(1)} collective-permute-done((bf16[256,512]{1,0:T(8,128)(2,1)S(1)}, bf16[256,512]{1,0:T(8,128)(2,1)S(1)}, u32[]{:S(2)}, u32[]{:S(2)}) %collective-permute-start.31) | collective-permute-done | bytes 262176 | tf_op jit(solution)/shard_map/ppermute | solution.py:100
  127.2 1.1 broadcast_select_fusion.1
  128.6 0.9 fusion.6
  129.5 0.9 fusion.33
  130.9 1.6 %collective-permute-done.32 = bf16[64,2688]{1,0:T(8,128)(2,1)S(1)} collective-permute-done((bf16[64,2688]{1,0:T(8,128)(2,1)S(1)}, bf16[64,2688]{1,0:T(8,128)(2,1)S(1)}, u32[]{:S(2)}, u32[]{:S(2)}) %collective-permute-start.32) | collective-permute-done | bytes 344096 | tf_op jit(solution)/shard_map/ppermute | solution.py:97
  132.7 1.6 %fusion.49 = bf16[64,2560]{1,0:T(8,128)(2,1)} fusion(f32[64,2688]{1,0:T(8,128)S(1)} %fusion.42, f32[2560]{0:T(1024)S(1)} %copy-done.14, bf16[128,2560]{1,0:T(8,128)(2,1)S(1)} %copy-done, pred[256,128]{1,0:T(32,128)(4,1)} %copy-done.10), kind=kOutput, calls=%fused_computation.84 | convolution fusion | flops 42450944 | bytes 1689600 | tf_op jit(solution)/shard_map/dot_general | solution.py:36
  (235 shorter events, 13.7 us)
Async XLA Ops:
  0.0 132.6 %copy-start = (bf16[128,2560]{1,0:T(8,128)(2,1)S(1)}, bf16[128,2560]{1,0:T(8,128)(2,1)}, u32[]{:S(2)}) copy-start(bf16[128,2560]{1,0:T(8,128)(2,1)} %param.21) | copy-start | bytes 1966084
  0.0 19.8 %collective-permute-start = (bf16[64,2560]{1,0:T(8,128)(2,1)}, bf16[64,2560]{1,0:T(8,128)(2,1)S(1)}, u32[]{:S(2)}, u32[]{:S(2)}) collective-permute-start(bf16[64,2560]{1,0:T(8,128)(2,1)} %param.11), channel_id=1, source_target_pairs={{0,2},{1,3},{2,0},{3,1},{4,6},{5,7},{6,4},{7,5},{8,10},{9,11},{10,... | collective-permute-start | bytes 983048 | tf_op jit(solution)/shard_map/ppermute | solution.py:97
  2.9 3.3 %collective-permute-start.2 = (bf16[64,2560]{1,0:T(8,128)(2,1)}, bf16[64,2560]{1,0:T(8,128)(2,1)S(1)}, u32[]{:S(2)}, u32[]{:S(2)}) collective-permute-start(bf16[64,2560]{1,0:T(8,128)(2,1)} %param.11), channel_id=1, source_target_pairs={{0,1},{1,0},{2,3},{3,2},{4,5},{5,4},{6,7},{7,6},{8,9},{9,8},{10,11... | collective-permute-start | bytes 983048 | tf_op jit(solution)/shard_map/ppermute | solution.py:97
  3.0 0.7 copy-start.1
  3.6 2.6 %copy-start.9 = (bf16[64,2560]{1,0:T(8,128)(2,1)S(1)}, bf16[64,2560]{1,0:T(8,128)(2,1)}, u32[]{:S(2)}) copy-start(bf16[64,2560]{1,0:T(8,128)(2,1)} %param.11) | copy-start | bytes 983044
  6.2 1.1 copy-start.4
  8.6 11.4 %collective-permute-start.3 = (bf16[288,512]{1,0:T(8,128)(2,1)S(1)}, bf16[288,512]{1,0:T(8,128)(2,1)S(1)}, u32[]{:S(2)}, u32[]{:S(2)}) collective-permute-start(bf16[288,512]{1,0:T(8,128)(2,1)S(1)} %maximum_maximum_fusion.3.after_ref), channel_id=1, source_target_pairs={{0,4},{4,0},{8,12},{12,8},{1,5},{5,1},{9,13},{13,9},{2,6},{6,2},{1... | collective-permute-start | bytes 884744 | tf_op jit(solution)/shard_map/ppermute | solution.py:100
  13.8 10.9 %collective-permute-start.4 = (bf16[256,512]{1,0:T(8,128)(2,1)S(1)}, bf16[256,512]{1,0:T(8,128)(2,1)S(1)}, u32[]{:S(2)}, u32[]{:S(2)}) collective-permute-start(bf16[256,512]{1,0:T(8,128)(2,1)S(1)} %pad_maximum_fusion.2.after_ref), channel_id=1, source_target_pairs={{0,4},{4,0},{8,12},{12,8},{1,5},{5,1},{9,13},{13,9},{2,6},{6,2},{1... | collective-permute-start | bytes 786440 | tf_op jit(solution)/shard_map/ppermute | solution.py:100
  16.8 2.7 %copy-start.2 = (s32[4]{0:T(128)S(1)}, s32[4]{0:T(128)}, u32[]{:S(2)}) copy-start(s32[4]{0:T(128)} %after_ref) | copy-start | bytes 52
  16.8 2.7 %copy-start.15 = (s32[256]{0:T(256)S(1)}, s32[256]{0:T(256)}, u32[]{:S(2)}) copy-start(s32[256]{0:T(256)} %param.12) | copy-start | bytes 3076
  17.7 2.2 %copy-start.13 = (f32[6144]{0:T(1024)S(1)}, f32[6144]{0:T(1024)}, u32[]{:S(2)}) copy-start(f32[6144]{0:T(1024)} %param.15) | copy-start | bytes 73732
  17.8 18.2 %collective-permute-start.7 = (bf16[256,512]{1,0:T(8,128)(2,1)S(1)}, bf16[256,512]{1,0:T(8,128)(2,1)S(1)}, u32[]{:S(2)}, u32[]{:S(2)}) collective-permute-start(bf16[256,512]{1,0:T(8,128)(2,1)S(1)} %pad_maximum_fusion.3), channel_id=1, source_target_pairs={{0,4},{4,0},{8,12},{12,8},{1,5},{5,1},{9,13},{13,9},{2,6},{6,2},{1... | collective-permute-start | bytes 786440 | tf_op jit(solution)/shard_map/ppermute | solution.py:100
  19.8 35.5 %copy-start.10 = (pred[256,128]{1,0:T(32,128)(4,1)}, pred[256,128]{1,0:T(32,128)(4,1)S(1)}, u32[]{:S(2)}) copy-start(pred[256,128]{1,0:T(32,128)(4,1)S(1)} %fusion.133) | copy-start | bytes 98308
  19.8 1.7 %collective-permute-start.1 = (bf16[64,2560]{1,0:T(8,128)(2,1)S(1)}, bf16[64,2560]{1,0:T(8,128)(2,1)S(1)}, u32[]{:S(2)}, u32[]{:S(2)}) collective-permute-start(bf16[64,2560]{1,0:T(8,128)(2,1)S(1)} %collective-permute-done), channel_id=1, source_target_pairs={{0,1},{1,0},{2,3},{3,2},{4,5},{5,4},{6,7},{7,6},{8,9},{9,8},{10,11... | collective-permute-start | bytes 983048 | tf_op jit(solution)/shard_map/ppermute | solution.py:97
  20.1 4.9 %collective-permute-start.5 = (bf16[288,512]{1,0:T(8,128)(2,1)S(1)}, bf16[288,512]{1,0:T(8,128)(2,1)S(1)}, u32[]{:S(2)}, u32[]{:S(2)}) collective-permute-start(bf16[288,512]{1,0:T(8,128)(2,1)S(1)} %add_convert_fusion.1), channel_id=1, source_target_pairs={{0,1},{1,0},{2,3},{3,2},{4,8},{5,9},{6,10},{7,11},{8,4},{9,5},{10,... | collective-permute-start | bytes 884744 | tf_op jit(solution)/shard_map/ppermute | solution.py:103
  24.7 1.4 %copy-start.16 = (bf16[128,6144]{1,0:T(8,128)(2,1)S(1)}, bf16[128,6144]{1,0:T(8,128)(2,1)}, u32[]{:S(2)}) copy-start(bf16[128,6144]{1,0:T(8,128)(2,1)} %param.17) | copy-start | bytes 4718596
  24.8 11.4 %collective-permute-start.8 = (bf16[256,512]{1,0:T(8,128)(2,1)S(1)}, bf16[256,512]{1,0:T(8,128)(2,1)S(1)}, u32[]{:S(2)}, u32[]{:S(2)}) collective-permute-start(bf16[256,512]{1,0:T(8,128)(2,1)S(1)} %add_convert_fusion.11), channel_id=1, source_target_pairs={{0,1},{1,0},{2,3},{3,2},{4,8},{5,9},{6,10},{7,11},{8,4},{9,5},{10,... | collective-permute-start | bytes 786440 | tf_op jit(solution)/shard_map/ppermute | solution.py:103
  25.1 20.7 %copy-start.11 = (bf16[128,128]{1,0:T(8,128)(2,1)}, bf16[128,128]{1,0:T(8,128)(2,1)S(1)}, u32[]{:S(2)}) copy-start(bf16[128,128]{1,0:T(8,128)(2,1)S(1)} %fusion.134) | copy-start | bytes 98308
  26.6 19.0 %collective-permute-start.6 = (bf16[288,512]{1,0:T(8,128)(2,1)S(1)}, bf16[288,512]{1,0:T(8,128)(2,1)S(1)}, u32[]{:S(2)}, u32[]{:S(2)}) collective-permute-start(bf16[288,512]{1,0:T(8,128)(2,1)S(1)} %maximum_select_fusion.after_ref), channel_id=1, source_target_pairs={{0,4},{4,0},{8,12},{12,8},{1,5},{5,1},{9,13},{13,9},{2,6},{6,2},{1... | collective-permute-start | bytes 884744 | tf_op jit(solution)/shard_map/ppermute | solution.py:100
  36.1 9.7 %collective-permute-start.9 = (bf16[256,512]{1,0:T(8,128)(2,1)S(1)}, bf16[256,512]{1,0:T(8,128)(2,1)S(1)}, u32[]{:S(2)}, u32[]{:S(2)}) collective-permute-start(bf16[256,512]{1,0:T(8,128)(2,1)S(1)} %add_convert_fusion.10), channel_id=1, source_target_pairs={{0,1},{1,0},{2,3},{3,2},{4,8},{5,9},{6,10},{7,11},{8,4},{9,5},{10,... | collective-permute-start | bytes 786440 | tf_op jit(solution)/shard_map/ppermute | solution.py:103
  36.8 8.8 %collective-permute-start.10 = (bf16[256,512]{1,0:T(8,128)(2,1)S(1)}, bf16[256,512]{1,0:T(8,128)(2,1)S(1)}, u32[]{:S(2)}, u32[]{:S(2)}) collective-permute-start(bf16[256,512]{1,0:T(8,128)(2,1)S(1)} %maximum_select_fusion.1.after_ref), channel_id=1, source_target_pairs={{0,4},{4,0},{8,12},{12,8},{1,5},{5,1},{9,13},{13,9},{2,6},{6,2},{1... | collective-permute-start | bytes 786440 | tf_op jit(solution)/shard_map/ppermute | solution.py:100
  45.7 9.5 %collective-permute-start.11 = (bf16[288,512]{1,0:T(8,128)(2,1)S(1)}, bf16[288,512]{1,0:T(8,128)(2,1)S(1)}, u32[]{:S(2)}, u32[]{:S(2)}) collective-permute-start(bf16[288,512]{1,0:T(8,128)(2,1)S(1)} %add_convert_fusion), channel_id=1, source_target_pairs={{0,1},{1,0},{2,3},{3,2},{4,8},{5,9},{6,10},{7,11},{8,4},{9,5},{10,... | collective-permute-start | bytes 884744 | tf_op jit(solution)/shard_map/ppermute | solution.py:103
  46.3 8.8 %collective-permute-start.13 = (bf16[256,512]{1,0:T(8,128)(2,1)S(1)}, bf16[256,512]{1,0:T(8,128)(2,1)S(1)}, u32[]{:S(2)}, u32[]{:S(2)}) collective-permute-start(bf16[256,512]{1,0:T(8,128)(2,1)S(1)} %maximum_select_fusion.2.after_ref), channel_id=1, source_target_pairs={{0,4},{4,0},{8,12},{12,8},{1,5},{5,1},{9,13},{13,9},{2,6},{6,2},{1... | collective-permute-start | bytes 786440 | tf_op jit(solution)/shard_map/ppermute | solution.py:100
  48.6 26.1 %slice-start = ((s8[31457280]{0:T(1024)(128)(4,1)}), s8[4194304]{0:T(1024)(128)(4,1)S(1)}, s32[]{:S(2)}) async-start(s8[31457280]{0:T(1024)(128)(4,1)} %bitcast.53), calls=%async_computation | async-start | bytes 8388608
  48.6 26.1 %slice-start.1 = ((s8[31457280]{0:T(1024)(128)(4,1)}), s8[4194304]{0:T(1024)(128)(4,1)S(1)}, s32[]{:S(2)}) async-start(s8[31457280]{0:T(1024)(128)(4,1)} %bitcast.53), calls=%async_computation.1 | async-start | bytes 8388608
  48.6 26.1 %slice-start.2 = ((s8[31457280]{0:T(1024)(128)(4,1)}), s8[4194304]{0:T(1024)(128)(4,1)S(1)}, s32[]{:S(2)}) async-start(s8[31457280]{0:T(1024)(128)(4,1)} %bitcast.53), calls=%async_computation.2 | async-start | bytes 8388608
  48.6 26.1 %slice-start.3 = ((s8[31457280]{0:T(1024)(128)(4,1)}), s8[4194304]{0:T(1024)(128)(4,1)S(1)}, s32[]{:S(2)}) async-start(s8[31457280]{0:T(1024)(128)(4,1)} %bitcast.53), calls=%async_computation.3 | async-start | bytes 8388608
  51.3 23.5 %slice-start.4 = ((s8[31457280]{0:T(1024)(128)(4,1)}), s8[4194304]{0:T(1024)(128)(4,1)S(1)}, s32[]{:S(2)}) async-start(s8[31457280]{0:T(1024)(128)(4,1)} %bitcast.53), calls=%async_computation.4 | async-start | bytes 8388608
  51.3 23.5 %slice-start.5 = ((s8[31457280]{0:T(1024)(128)(4,1)}), s8[4194304]{0:T(1024)(128)(4,1)S(1)}, s32[]{:S(2)}) async-start(s8[31457280]{0:T(1024)(128)(4,1)} %bitcast.53), calls=%async_computation.5 | async-start | bytes 8388608
  53.2 5.0 %collective-permute-start.14 = (bf16[256,512]{1,0:T(8,128)(2,1)S(1)}, bf16[256,512]{1,0:T(8,128)(2,1)S(1)}, u32[]{:S(2)}, u32[]{:S(2)}) collective-permute-start(bf16[256,512]{1,0:T(8,128)(2,1)S(1)} %add_convert_fusion.9), channel_id=1, source_target_pairs={{0,1},{1,0},{2,3},{3,2},{4,8},{5,9},{6,10},{7,11},{8,4},{9,5},{10,... | collective-permute-start | bytes 786440 | tf_op jit(solution)/shard_map/ppermute | solution.py:103
  55.7 19.1 %slice-start.6 = ((s8[31457280]{0:T(1024)(128)(4,1)}), s8[4194304]{0:T(1024)(128)(4,1)S(1)}, s32[]{:S(2)}) async-start(s8[31457280]{0:T(1024)(128)(4,1)} %bitcast.53), calls=%async_computation.6 | async-start | bytes 8388608
  55.9 9.6 %collective-permute-start.15 = (bf16[256,512]{1,0:T(8,128)(2,1)S(1)}, bf16[256,512]{1,0:T(8,128)(2,1)S(1)}, u32[]{:S(2)}, u32[]{:S(2)}) collective-permute-start(bf16[256,512]{1,0:T(8,128)(2,1)S(1)} %add_convert_fusion.8), channel_id=1, source_target_pairs={{0,1},{1,0},{2,3},{3,2},{4,8},{5,9},{6,10},{7,11},{8,4},{9,5},{10,... | collective-permute-start | bytes 786440 | tf_op jit(solution)/shard_map/ppermute | solution.py:103
  56.0 9.3 %collective-permute-start.12 = (bf16[256,512]{1,0:T(8,128)(2,1)S(1)}, bf16[256,512]{1,0:T(8,128)(2,1)S(1)}, u32[]{:S(2)}, u32[]{:S(2)}) collective-permute-start(bf16[256,512]{1,0:T(8,128)(2,1)S(1)} %get-tuple-element.192), channel_id=1, source_target_pairs={{0,4},{4,0},{8,12},{12,8},{1,5},{5,1},{9,13},{13,9},{2,6},{6,2},{1... | collective-permute-start | bytes 786440 | tf_op jit(solution)/shard_map/ppermute | solution.py:100
  58.8 11.5 %collective-permute-start.16 = (bf16[256,512]{1,0:T(8,128)(2,1)S(1)}, bf16[256,512]{1,0:T(8,128)(2,1)S(1)}, u32[]{:S(2)}, u32[]{:S(2)}) collective-permute-start(bf16[256,512]{1,0:T(8,128)(2,1)S(1)} %get-tuple-element.188), channel_id=1, source_target_pairs={{0,4},{4,0},{8,12},{12,8},{1,5},{5,1},{9,13},{13,9},{2,6},{6,2},{1... | collective-permute-start | bytes 786440 | tf_op jit(solution)/shard_map/ppermute | solution.py:100
  65.4 9.4 %slice-start.7 = ((s8[31457280]{0:T(1024)(128)(4,1)}), s8[2097152]{0:T(1024)(128)(4,1)S(1)}, s32[]{:S(2)}) async-start(s8[31457280]{0:T(1024)(128)(4,1)} %bitcast.53), calls=%async_computation.7 | async-start | bytes 4194304
  65.4 14.1 %collective-permute-start.17 = (bf16[256,512]{1,0:T(8,128)(2,1)S(1)}, bf16[256,512]{1,0:T(8,128)(2,1)S(1)}, u32[]{:S(2)}, u32[]{:S(2)}) collective-permute-start(bf16[256,512]{1,0:T(8,128)(2,1)S(1)} %add_convert_fusion.7), channel_id=1, source_target_pairs={{0,1},{1,0},{2,3},{3,2},{4,8},{5,9},{6,10},{7,11},{8,4},{9,5},{10,... | collective-permute-start | bytes 786440 | tf_op jit(solution)/shard_map/ppermute | solution.py:103
  70.4 13.0 %collective-permute-start.19 = (bf16[256,512]{1,0:T(8,128)(2,1)S(1)}, bf16[256,512]{1,0:T(8,128)(2,1)S(1)}, u32[]{:S(2)}, u32[]{:S(2)}) collective-permute-start(bf16[256,512]{1,0:T(8,128)(2,1)S(1)} %add_convert_fusion.6), channel_id=1, source_target_pairs={{0,1},{1,0},{2,3},{3,2},{4,8},{5,9},{6,10},{7,11},{8,4},{9,5},{10,... | collective-permute-start | bytes 786440 | tf_op jit(solution)/shard_map/ppermute | solution.py:103
  70.6 8.8 %collective-permute-start.18 = (bf16[256,512]{1,0:T(8,128)(2,1)S(1)}, bf16[256,512]{1,0:T(8,128)(2,1)S(1)}, u32[]{:S(2)}, u32[]{:S(2)}) collective-permute-start(bf16[256,512]{1,0:T(8,128)(2,1)S(1)} %get-tuple-element.180), channel_id=1, source_target_pairs={{0,4},{4,0},{8,12},{12,8},{1,5},{5,1},{9,13},{13,9},{2,6},{6,2},{1... | collective-permute-start | bytes 786440 | tf_op jit(solution)/shard_map/ppermute | solution.py:100
  79.4 16.3 %collective-permute-start.24 = (bf16[256,512]{1,0:T(8,128)(2,1)S(1)}, bf16[256,512]{1,0:T(8,128)(2,1)}, u32[]{:S(2)}, u32[]{:S(2)}) collective-permute-start(bf16[256,512]{1,0:T(8,128)(2,1)S(1)} %add_convert_fusion.5), channel_id=1, source_target_pairs={{0,1},{1,0},{2,3},{3,2},{4,8},{5,9},{6,10},{7,11},{8,4},{9,5},{10,... | collective-permute-start | bytes 786440 | tf_op jit(solution)/shard_map/ppermute | solution.py:103
  81.0 2.5 %copy-start.5 = (bf16[256,512]{1,0:T(8,128)(2,1)}, bf16[256,512]{1,0:T(8,128)(2,1)S(1)}, u32[]{:S(2)}) copy-start(bf16[256,512]{1,0:T(8,128)(2,1)S(1)} %get-tuple-element.184) | copy-start | bytes 786436
  81.0 10.7 %collective-permute-start.20 = (bf16[256,512]{1,0:T(8,128)(2,1)S(1)}, bf16[256,512]{1,0:T(8,128)(2,1)S(1)}, u32[]{:S(2)}, u32[]{:S(2)}) collective-permute-start(bf16[256,512]{1,0:T(8,128)(2,1)S(1)} %get-tuple-element.184), channel_id=1, source_target_pairs={{0,4},{4,0},{8,12},{12,8},{1,5},{5,1},{9,13},{13,9},{2,6},{6,2},{1... | collective-permute-start | bytes 786440 | tf_op jit(solution)/shard_map/ppermute | solution.py:100
  85.6 9.8 %collective-permute-start.21 = (bf16[256,512]{1,0:T(8,128)(2,1)}, bf16[256,512]{1,0:T(8,128)(2,1)S(1)}, u32[]{:S(2)}, u32[]{:S(2)}) collective-permute-start(bf16[256,512]{1,0:T(8,128)(2,1)} %get-tuple-element.176), channel_id=1, source_target_pairs={{0,4},{4,0},{8,12},{12,8},{1,5},{5,1},{9,13},{13,9},{2,6},{6,2},{1... | collective-permute-start | bytes 786440 | tf_op jit(solution)/shard_map/ppermute | solution.py:100
  90.4 5.1 %copy-start.6 = (bf16[256,512]{1,0:T(8,128)(2,1)S(1)}, bf16[256,512]{1,0:T(8,128)(2,1)}, u32[]{:S(2)}) copy-start(bf16[256,512]{1,0:T(8,128)(2,1)} %copy-done.5) | copy-start | bytes 786436
  91.8 14.8 %collective-permute-start.22 = (bf16[256,512]{1,0:T(8,128)(2,1)S(1)}, bf16[256,512]{1,0:T(8,128)(2,1)S(1)}, u32[]{:S(2)}, u32[]{:S(2)}) collective-permute-start(bf16[256,512]{1,0:T(8,128)(2,1)S(1)} %add_convert_fusion.4), channel_id=1, source_target_pairs={{0,1},{1,0},{2,3},{3,2},{4,8},{5,9},{6,10},{7,11},{8,4},{9,5},{10,... | collective-permute-start | bytes 786440 | tf_op jit(solution)/shard_map/ppermute | solution.py:103
  95.5 1.5 %copy-start.17 = (bf16[128,6144]{1,0:T(8,128)(2,1)S(1)}, bf16[128,6144]{1,0:T(8,128)(2,1)}, u32[]{:S(2)}) copy-start(bf16[128,6144]{1,0:T(8,128)(2,1)} %param.17) | copy-start | bytes 4718596
  95.5 14.0 %collective-permute-start.26 = (bf16[256,512]{1,0:T(8,128)(2,1)S(1)}, bf16[256,512]{1,0:T(8,128)(2,1)S(1)}, u32[]{:S(2)}, u32[]{:S(2)}) collective-permute-start(bf16[256,512]{1,0:T(8,128)(2,1)S(1)} %add_convert_fusion.3), channel_id=1, source_target_pairs={{0,1},{1,0},{2,3},{3,2},{4,8},{5,9},{6,10},{7,11},{8,4},{9,5},{10,... | collective-permute-start | bytes 786440 | tf_op jit(solution)/shard_map/ppermute | solution.py:103
  96.8 1.0 copy-start.7
  96.8 1.0 copy-start.8
  97.3 2.7 %copy-start.3 = (bf16[6144,128]{1,0:T(8,128)(2,1)S(1)}, bf16[6144,128]{1,0:T(8,128)(2,1)}, u32[]{:S(2)}) copy-start(bf16[6144,128]{1,0:T(8,128)(2,1)} %param.20) | copy-start | bytes 4718596
  97.8 8.7 %collective-permute-start.25 = (bf16[256,512]{1,0:T(8,128)(2,1)S(1)}, bf16[256,512]{1,0:T(8,128)(2,1)S(1)}, u32[]{:S(2)}, u32[]{:S(2)}) collective-permute-start(bf16[256,512]{1,0:T(8,128)(2,1)S(1)} %get-tuple-element.168), channel_id=1, source_target_pairs={{0,4},{4,0},{8,12},{12,8},{1,5},{5,1},{9,13},{13,9},{2,6},{6,2},{1... | collective-permute-start | bytes 786440 | tf_op jit(solution)/shard_map/ppermute | solution.py:100
  101.2 5.5 %copy-start.12 = (bf16[128,128]{1,0:T(8,128)(2,1)S(1)}, bf16[128,128]{1,0:T(8,128)(2,1)}, u32[]{:S(2)}) copy-start(bf16[128,128]{1,0:T(8,128)(2,1)} %copy-done.11) | copy-start | bytes 98308
  106.6 11.9 %collective-permute-start.28 = (bf16[256,512]{1,0:T(8,128)(2,1)S(1)}, bf16[256,512]{1,0:T(8,128)(2,1)S(1)}, u32[]{:S(2)}, u32[]{:S(2)}) collective-permute-start(bf16[256,512]{1,0:T(8,128)(2,1)S(1)} %add_convert_fusion.2), channel_id=1, source_target_pairs={{0,1},{1,0},{2,3},{3,2},{4,8},{5,9},{6,10},{7,11},{8,4},{9,5},{10,... | collective-permute-start | bytes 786440 | tf_op jit(solution)/shard_map/ppermute | solution.py:103
  107.2 9.5 %collective-permute-start.23 = (bf16[256,512]{1,0:T(8,128)(2,1)S(1)}, bf16[256,512]{1,0:T(8,128)(2,1)}, u32[]{:S(2)}, u32[]{:S(2)}) collective-permute-start(bf16[256,512]{1,0:T(8,128)(2,1)S(1)} %pad_maximum_fusion.11), channel_id=1, source_target_pairs={{0,4},{4,0},{8,12},{12,8},{1,5},{5,1},{9,13},{13,9},{2,6},{6,2},{1... | collective-permute-start | bytes 786440 | tf_op jit(solution)/shard_map/ppermute | solution.py:100
  110.1 12.2 %collective-permute-start.29 = (bf16[256,512]{1,0:T(8,128)(2,1)S(1)}, bf16[256,512]{1,0:T(8,128)(2,1)}, u32[]{:S(2)}, u32[]{:S(2)}) collective-permute-start(bf16[256,512]{1,0:T(8,128)(2,1)S(1)} %pad_maximum_fusion.17), channel_id=1, source_target_pairs={{0,4},{4,0},{8,12},{12,8},{1,5},{5,1},{9,13},{13,9},{2,6},{6,2},{1... | collective-permute-start | bytes 786440 | tf_op jit(solution)/shard_map/ppermute | solution.py:100
  112.7 5.0 %collective-permute-start.27 = (bf16[64,2688]{1,0:T(8,128)(2,1)S(1)}, bf16[64,2688]{1,0:T(8,128)(2,1)S(1)}, u32[]{:S(2)}, u32[]{:S(2)}) collective-permute-start(bf16[64,2688]{1,0:T(8,128)(2,1)S(1)} %fusion.47), channel_id=1, source_target_pairs={{0,1},{1,0},{2,3},{3,2},{4,5},{5,4},{6,7},{7,6},{8,9},{9,8},{10,11... | collective-permute-start | bytes 1032200 | tf_op jit(solution)/shard_map/ppermute | solution.py:97
  117.8 11.6 %collective-permute-start.30 = (bf16[64,2688]{1,0:T(8,128)(2,1)S(1)}, bf16[64,2688]{1,0:T(8,128)(2,1)S(1)}, u32[]{:S(2)}, u32[]{:S(2)}) collective-permute-start(bf16[64,2688]{1,0:T(8,128)(2,1)S(1)} %fusion.45), channel_id=1, source_target_pairs={{0,2},{1,3},{2,0},{3,1},{4,6},{5,7},{6,4},{7,5},{8,10},{9,11},{10,... | collective-permute-start | bytes 1032200 | tf_op jit(solution)/shard_map/ppermute | solution.py:97
  119.9 7.3 %collective-permute-start.31 = (bf16[256,512]{1,0:T(8,128)(2,1)S(1)}, bf16[256,512]{1,0:T(8,128)(2,1)S(1)}, u32[]{:S(2)}, u32[]{:S(2)}) collective-permute-start(bf16[256,512]{1,0:T(8,128)(2,1)S(1)} %pad_maximum_fusion.18), channel_id=1, source_target_pairs={{0,4},{4,0},{8,12},{12,8},{1,5},{5,1},{9,13},{13,9},{2,6},{6,2},{1... | collective-permute-start | bytes 786440 | tf_op jit(solution)/shard_map/ppermute | solution.py:100
  130.8 1.9 %copy-start.14 = (f32[2560]{0:T(1024)S(1)}, f32[2560]{0:T(1024)}, u32[]{:S(2)}) copy-start(f32[2560]{0:T(1024)} %param.19) | copy-start | bytes 30724
  130.8 1.7 %collective-permute-start.32 = (bf16[64,2688]{1,0:T(8,128)(2,1)S(1)}, bf16[64,2688]{1,0:T(8,128)(2,1)S(1)}, u32[]{:S(2)}, u32[]{:S(2)}) collective-permute-start(bf16[64,2688]{1,0:T(8,128)(2,1)S(1)} %fusion.46), channel_id=1, source_target_pairs={{0,1},{1,0},{2,3},{3,2},{4,5},{5,4},{6,7},{7,6},{8,9},{9,8},{10,11... | collective-permute-start | bytes 1032200 | tf_op jit(solution)/shard_map/ppermute | solution.py:97

commit v11 on v10

--- a/solution.py
+++ b/solution.py
@@ -12,7 +12,7 @@
 JOBS = 4
 LANES = 128
 UNITS = 12
-LAG = 3
+LAG = 4
 F32 = jnp.float32
 BF16 = jnp.bfloat16
 
@@ -125,7 +125,8 @@
         near = 2 * rows
         width = first_weight.shape[1] // UNITS
         wide = 2 * width
-        fold = width // LANES
+        early = UNITS // 4
+        fold = max(n for n in range(1, width // LANES + 1) if near % n == 0)
         place = lax.axis_index("row")
         is_end = (place == 0) | (place == 3)
         last = tokens
@@ -140,10 +141,10 @@
             return jnp.concatenate([value[:near], value[near : 2 * near]], axis=1)
 
         def block_of(unit):
-            return unit % 3 if unit < 6 else 3 + unit % 3
+            return unit % early + (early if unit >= 2 * early else 0)
 
         def is_near(unit):
-            return unit < 3 or unit >= 9
+            return unit < early or unit >= 3 * early
 
         def columns(unit):
             return slice(block_of(unit) * wide, (block_of(unit) + 1) * wide)
@@ -163,23 +164,25 @@
         def first_half(unit, x):
             nonlocal last
             value = halves(multiply(x, block_of(unit)))
-            if unit in (0, 3):
+            if unit in (0, early):
                 low = dot(x, first_down_maps).astype(BF16)
                 low = jnp.concatenate(jnp.split(low, fold, axis=0), axis=1)
+                low = jnp.pad(low, ((0, 0), (0, width - fold * LANES)))
                 value = jnp.concatenate([value, low], axis=0)
             partials[unit] = value
             last = value
 
         def first_late(unit, x):
             value = multiply(x, block_of(unit))
-            partials[unit + 3], partials[unit] = halves(value[:near]), halves(value[near:])
+            partials[unit + early], partials[unit] = halves(value[:near]), halves(value[near:])
 
         def send(t, value):
             payloads[t] = value
             swaps[t] = end_swap(value)
 
         def state(unit):
-            return jnp.where(is_end, swaps[unit + LAG], payloads[unit + LAG])
+            come = tie(swaps[unit + LAG], last)
+            return jnp.where(is_end, come, payloads[unit + LAG])
 
         def second(name, states, block):
             nonlocal last
@@ -202,7 +205,7 @@
         last, is_end, mine = lax.optimization_barrier((jobs, is_end, mine))
         load(0)
         gathered_near = jnp.concatenate([tokens, tie(col_swap(tokens, 1), last)], axis=0)
-        for unit in range(3):
+        for unit in range(early):
             if unit > 0:
                 load(unit)
             first_half(unit, gathered_near)
@@ -218,43 +221,45 @@
             if t == 0:
                 gathered_far = jnp.concatenate([far, col_swap(far, 1)], axis=0)
                 gathered = jnp.concatenate([gathered_near, gathered_far], axis=0)
-                for unit in range(3, 6):
-                    first_half(unit, gathered_far)
+            if t < early:
+                first_half(early + t, gathered_far)
+                if early + t < LAG:
+                    send(early + t, partials[early + t])
             k = t - 1
             if 0 <= k < UNITS:
                 summed = tie(sums[k], last).astype(F32) + crosses[k].astype(F32)
-                if k in (0, 3):
-                    low = jnp.concatenate(jnp.split(summed[2 * near :], fold, axis=1), axis=0)
+                if k in (0, early):
+                    low = jnp.split(summed[2 * near :, : fold * LANES], fold, axis=1)
+                    low = jnp.concatenate(low, axis=0)
                     own_mask = mask[:near] if k == 0 else mask[near:]
                     low_in[is_near(k)] = jnp.where(own_mask, low, 0.0).astype(BF16)
                 low = low_in[is_near(k)]
                 value = activate(unfold(summed), low, first_up_maps, first_bias, columns(k))
                 value = halves(value)
-                if k + LAG == 3:
+                if k + LAG == early:
                     value = jnp.concatenate([value, jnp.zeros_like(value[: near // fold])], axis=0)
                 if k + LAG < UNITS:
                     value = jnp.where(is_end, partials[k + LAG], value)
                 last = value
                 send(k + LAG, value)
-            if t in (1, 2, 3):
-                load(t + 2)
-                first_late(t + 5, gathered)
-            elif t in (6, 7, 8):
-                top, bottom = unfold(state(t - 6)), unfold(state(t - 3))
-                second("all", jnp.concatenate([top, bottom], axis=0), t - 6)
-            elif t >= 9:
-                unit = t - LAG
-                if t == 9:
+            unit = t - LAG
+            if 1 <= t <= early:
+                load(early + t - 1)
+                first_late(2 * early + t - 1, gathered)
+            if early <= unit < 2 * early:
+                top, bottom = unfold(state(unit - early)), unfold(state(unit))
+                second("all", jnp.concatenate([top, bottom], axis=0), unit - early)
+            elif unit >= 2 * early:
+                if unit == 2 * early:
                     value, low = outputs["all"]
                     outputs["near"] = (value[:near], low[:near])
                     outputs["far"] = (value[near:], low[near:])
-                if t == 13:
+                if unit == UNITS - 1:
                     last = across
                 second("near" if is_near(unit) else "far", unfold(state(unit)), block_of(unit))
-                if t == 11:
+                if unit == 3 * early - 1:
                     ours, theirs = core_parts("far")
                     across = (ours + col_swap(theirs, 1).astype(F32)).astype(BF16)
-                    last = across
                     across = col_swap(across, 2)
         ours, theirs = core_parts("near")
         come = col_swap(theirs, 1)

time: 135 us -> 129 us (0.956)
  waiting for transfers between devices: 33.2 us -> 14.1 us
  starting transfers between devices: 35.9 us -> 43.6 us
  other arithmetic: 7.78 us -> 12.7 us
    ppermute x15 -> x16, waiting for transfers between devices: 30.6 us -> 2.85 us  [end_swap(): return lax.ppermute(value, 'row', [(i, i ^ 1) for i in range(n_row)])]
    ppermute x6, waiting for transfers between devices: 2.54 us -> 11.2 us  [col_swap(): return lax.ppermute(value, 'col', [(i, i ^ flip) for i in range(n_col)])]
    ppermute x15 -> x16, starting transfers between devices: 30.7 us -> 37.6 us  [end_swap(): return lax.ppermute(value, 'row', [(i, i ^ 1) for i in range(n_row)])]
    add x12, other arithmetic: 1.87 us -> 4.07 us  [pipeline(): summed = tie(sums[k], last).astype(F32) + crosses[k].astype(F32)]
    concatenate x13 -> x14, other arithmetic: 1.27 us -> 2.84 us  [halves(): return jnp.concatenate([value[:, :width], value[:, width:]], axis=0)]
    convert_element_type x12, other arithmetic: 0.82 us -> 2.26 us  [pipeline(): sums[t] = (ours + swaps[t].astype(F32)).astype(BF16)]
    unnamed x55 -> x51, local copies, waits for them, and re-layouts: 3.33 us -> 3.71 us
  transfers between devices with their start and end apart: 33 -> 34, of which waited for: 11 -> 6; matrix products, arithmetic and copies ran while one was open for 31% -> 36% of each run, Pallas kernels for 11% -> 12%
where the time goes in v11:
time: 129 us; the launch traced here: 128 us
  starting transfers between devices  43.6 us (34%)
  matrix products  36 us (28%)
  Pallas kernels  15.2 us (12%)
  waiting for transfers between devices  14.1 us (11%)
  other arithmetic  12.7 us (10%)
  local copies, waits for them, and re-layouts  4.95 us (4%)
  between operations  1.73 us (1%)
    ppermute x16, starting transfers between devices, end_swap(): return lax.ppermute(value, 'row', [(i, i ^ 1) for i in range(n_row)])  37.6 us
    dot_general x42, matrix products, dot(): return jnp.dot(left, right, preferred_element_type=F32)  36 us
    pallas_call x6, Pallas kernels, load_part(): pl.pallas_call(functools.partial(load_kernel, part=part), in_specs=[pl.Bl...  15.2 us
    ppermute x6, waiting for transfers between devices, col_swap(): return lax.ppermute(value, 'col', [(i, i ^ flip) for i in range(n_col)])  11.2 us
    add x12, other arithmetic, pipeline(): summed = tie(sums[k], last).astype(F32) + crosses[k].astype(F32)  4.07 us
    ppermute x6, starting transfers between devices, col_swap(): return lax.ppermute(value, 'col', [(i, i ^ flip) for i in range(n_col)])  3.76 us
    unnamed x51, local copies, waits for them, and re-layouts  3.71 us
    ppermute x16, waiting for transfers between devices, end_swap(): return lax.ppermute(value, 'row', [(i, i ^ 1) for i in range(n_row)])  2.85 us
  transfers between devices with their start and end apart: 34, of which 6 were waited for; matrix products, arithmetic and copies ran while one was open for 36% of the time, Pallas kernels for 12%

profile of v11, /device:TPU:0, one launch (start us, length us, event | category | flops | bytes accessed | tf_op | source)
XLA Modules:
  0.0 128.1 jit_solution(13732540374538096565)
XLA Ops:
  0.0 2.9 %collective-permute-start = (bf16[64,2560]{1,0:T(8,128)(2,1)}, bf16[64,2560]{1,0:T(8,128)(2,1)S(1)}, u32[]{:S(2)}, u32[]{:S(2)}) collective-permute-start(bf16[64,2560]{1,0:T(8,128)(2,1)} %param.11), channel_id=1, source_target_pairs={{0,2},{1,3},{2,0},{3,1},{4,6},{5,7},{6,4},{7,5},{8,10},{9,11},{10,... | collective-permute-start | bytes 983048 | tf_op jit(solution)/shard_map/ppermute | solution.py:97
  3.6 2.5 %shard_map.109 = bf16[2560,1024]{1,0:T(8,128)(2,1)S(1)} custom-call(bf16[2560,6144]{1,0:T(8,128)(2,1)} %w_hbm.11, s32[4]{0:T(128)S(1)} %copy-done.1), custom_call_target="tpu_custom_call" | custom-call | bytes 1000 | tf_op jit(solution)/shard_map/pallas_call | solution.py:51
  6.3 1.0 copy-done.4
  7.6 0.9 convolution_convert_fusion.8
  8.5 1.6 %collective-permute-start.3 = (bf16[288,512]{1,0:T(8,128)(2,1)S(1)}, bf16[288,512]{1,0:T(8,128)(2,1)S(1)}, u32[]{:S(2)}, u32[]{:S(2)}) collective-permute-start(bf16[288,512]{1,0:T(8,128)(2,1)S(1)} %maximum_maximum_fusion.3.after_ref), channel_id=1, source_target_pairs={{0,4},{4,0},{8,12},{12,8},{1,5},{5,1},{9,13},{13,9},{2,6},{6,2},{1... | collective-permute-start | bytes 884744 | tf_op jit(solution)/shard_map/ppermute | solution.py:100
  10.2 2.5 %shard_map.110 = bf16[2560,1024]{1,0:T(8,128)(2,1)S(1)} custom-call(bf16[2560,6144]{1,0:T(8,128)(2,1)} %w_hbm.11, bf16[288,512]{1,0:T(8,128)(2,1)S(1)} %maximum_maximum_fusion.3.after_ref), custom_call_target="tpu_custom_call" | custom-call | bytes 1000 | tf_op jit(solution)/shard_map/pallas_call | solution.py:51
  12.7 0.8 convolution_convert_fusion.7
  14.1 2.5 %shard_map.111 = bf16[2560,1024]{1,0:T(8,128)(2,1)S(1)} custom-call(bf16[2560,6144]{1,0:T(8,128)(2,1)} %w_hbm.11, bf16[256,512]{1,0:T(8,128)(2,1)S(1)} %pad_maximum_fusion.2.after_ref), custom_call_target="tpu_custom_call" | custom-call | bytes 1000 | tf_op jit(solution)/shard_map/pallas_call | solution.py:51
  16.6 0.9 convolution_convert_fusion.6
  17.5 1.6 %collective-permute-start.7 = (bf16[256,512]{1,0:T(8,128)(2,1)S(1)}, bf16[256,512]{1,0:T(8,128)(2,1)S(1)}, u32[]{:S(2)}, u32[]{:S(2)}) collective-permute-start(bf16[256,512]{1,0:T(8,128)(2,1)S(1)} %pad_maximum_fusion.3), channel_id=1, source_target_pairs={{0,4},{4,0},{8,12},{12,8},{1,5},{5,1},{9,13},{13,9},{2,6},{6,2},{1... | collective-permute-start | bytes 786440 | tf_op jit(solution)/shard_map/ppermute | solution.py:100
  20.4 0.9 collective-permute-done.1
  21.6 0.9 convolution_convert_fusion.5
  22.6 1.4 %collective-permute-done.4 = bf16[256,512]{1,0:T(8,128)(2,1)S(1)} collective-permute-done((bf16[256,512]{1,0:T(8,128)(2,1)S(1)}, bf16[256,512]{1,0:T(8,128)(2,1)S(1)}, u32[]{:S(2)}, u32[]{:S(2)}) %collective-permute-start.4) | collective-permute-done | bytes 262176 | tf_op jit(solution)/shard_map/ppermute | solution.py:100
  24.1 3.1 %collective-permute-start.9 = (bf16[288,512]{1,0:T(8,128)(2,1)S(1)}, bf16[288,512]{1,0:T(8,128)(2,1)S(1)}, u32[]{:S(2)}, u32[]{:S(2)}) collective-permute-start(bf16[288,512]{1,0:T(8,128)(2,1)S(1)} %maximum_maximum_fusion.4), channel_id=1, source_target_pairs={{0,4},{4,0},{8,12},{12,8},{1,5},{5,1},{9,13},{13,9},{2,6},{6,2},{1... | collective-permute-start | bytes 884744 | tf_op jit(solution)/shard_map/ppermute | solution.py:100
  27.3 0.8 convolution_convert_fusion.4
  28.4 1.2 copy-done.15
  30.0 1.6 %collective-permute-start.6 = (bf16[256,512]{1,0:T(8,128)(2,1)S(1)}, bf16[256,512]{1,0:T(8,128)(2,1)S(1)}, u32[]{:S(2)}, u32[]{:S(2)}) collective-permute-start(bf16[256,512]{1,0:T(8,128)(2,1)S(1)} %maximum_select_fusion.after_ref), channel_id=1, source_target_pairs={{0,4},{4,0},{8,12},{12,8},{1,5},{5,1},{9,13},{13,9},{2,6},{6,2},{1... | collective-permute-start | bytes 786440 | tf_op jit(solution)/shard_map/ppermute | solution.py:100
  31.6 2.5 %shard_map.112 = bf16[2560,1024]{1,0:T(8,128)(2,1)S(1)} custom-call(bf16[2560,6144]{1,0:T(8,128)(2,1)} %w_hbm.11, bf16[256,512]{1,0:T(8,128)(2,1)S(1)} %maximum_select_fusion.after_ref), custom_call_target="tpu_custom_call" | custom-call | bytes 1000 | tf_op jit(solution)/shard_map/pallas_call | solution.py:51
  34.1 1.5 %convolution_convert_fusion.2 = bf16[256,1024]{1,0:T(8,128)(2,1)S(1)} fusion(bf16[256,2560]{1,0:T(8,128)(2,1)S(1)} %get-tuple-element.81, bf16[2560,1024]{1,0:T(8,128)(2,1)S(1)} %shard_map.112), kind=kOutput, calls=%fused_computation.32 | convolution fusion | flops 1342439424 | bytes 7077888 | tf_op jit(solution)/shard_map/dot_general | solution.py:36
  35.8 0.9 convolution_convert_fusion.3
  37.3 2.0 %collective-permute-start.12 = (bf16[256,512]{1,0:T(8,128)(2,1)S(1)}, bf16[256,512]{1,0:T(8,128)(2,1)S(1)}, u32[]{:S(2)}, u32[]{:S(2)}) collective-permute-start(bf16[256,512]{1,0:T(8,128)(2,1)S(1)} %maximum_select_fusion.1.after_ref), channel_id=1, source_target_pairs={{0,4},{4,0},{8,12},{12,8},{1,5},{5,1},{9,13},{13,9},{2,6},{6,2},{1... | collective-permute-start | bytes 786440 | tf_op jit(solution)/shard_map/ppermute | solution.py:100
  39.3 2.5 %shard_map.113 = bf16[2560,1024]{1,0:T(8,128)(2,1)S(1)} custom-call(bf16[2560,6144]{1,0:T(8,128)(2,1)} %w_hbm.11, bf16[256,512]{1,0:T(8,128)(2,1)S(1)} %maximum_select_fusion.1.after_ref), custom_call_target="tpu_custom_call" | custom-call | bytes 1000 | tf_op jit(solution)/shard_map/pallas_call | solution.py:51
  41.8 1.5 %convolution_convert_fusion.1 = bf16[256,1024]{1,0:T(8,128)(2,1)S(1)} fusion(bf16[256,2560]{1,0:T(8,128)(2,1)S(1)} %get-tuple-element.81, bf16[2560,1024]{1,0:T(8,128)(2,1)S(1)} %shard_map.113), kind=kOutput, calls=%fused_computation.31 | convolution fusion | flops 1342439424 | bytes 7077888 | tf_op jit(solution)/shard_map/dot_general | solution.py:36
  44.2 2.1 %collective-permute-start.14 = (bf16[256,512]{1,0:T(8,128)(2,1)S(1)}, bf16[256,512]{1,0:T(8,128)(2,1)S(1)}, u32[]{:S(2)}, u32[]{:S(2)}) collective-permute-start(bf16[256,512]{1,0:T(8,128)(2,1)S(1)} %get-tuple-element.218.after_ref), channel_id=1, source_target_pairs={{0,4},{4,0},{8,12},{12,8},{1,5},{5,1},{9,13},{13,9},{2,6},{6,2},{1... | collective-permute-start | bytes 786440 | tf_op jit(solution)/shard_map/ppermute | solution.py:100
  46.3 2.6 %shard_map.114 = bf16[2560,1024]{1,0:T(8,128)(2,1)S(1)} custom-call(bf16[2560,6144]{1,0:T(8,128)(2,1)} %w_hbm.11, bf16[256,512]{1,0:T(8,128)(2,1)S(1)} %get-tuple-element.218.after_ref), custom_call_target="tpu_custom_call" | custom-call | bytes 1000 | tf_op jit(solution)/shard_map/pallas_call | solution.py:51
  49.0 1.7 %convolution_convert_fusion = bf16[256,1024]{1,0:T(8,128)(2,1)S(1)} fusion(bf16[256,2560]{1,0:T(8,128)(2,1)S(1)} %get-tuple-element.81, bf16[2560,1024]{1,0:T(8,128)(2,1)S(1)} %shard_map.114), kind=kOutput, calls=%fused_computation.30 | convolution fusion | flops 1342439424 | bytes 7077888 | tf_op jit(solution)/shard_map/dot_general | solution.py:36
  52.2 3.8 %collective-permute-start.16 = (bf16[256,512]{1,0:T(8,128)(2,1)S(1)}, bf16[256,512]{1,0:T(8,128)(2,1)S(1)}, u32[]{:S(2)}, u32[]{:S(2)}) collective-permute-start(bf16[256,512]{1,0:T(8,128)(2,1)S(1)} %get-tuple-element.210), channel_id=1, source_target_pairs={{0,4},{4,0},{8,12},{12,8},{1,5},{5,1},{9,13},{13,9},{2,6},{6,2},{1... | collective-permute-start | bytes 786440 | tf_op jit(solution)/shard_map/ppermute | solution.py:100
  56.7 4.8 %collective-permute-start.18 = (bf16[256,512]{1,0:T(8,128)(2,1)S(1)}, bf16[256,512]{1,0:T(8,128)(2,1)S(1)}, u32[]{:S(2)}, u32[]{:S(2)}) collective-permute-start(bf16[256,512]{1,0:T(8,128)(2,1)S(1)} %get-tuple-element.196), channel_id=1, source_target_pairs={{0,4},{4,0},{8,12},{12,8},{1,5},{5,1},{9,13},{13,9},{2,6},{6,2},{1... | collective-permute-start | bytes 786440 | tf_op jit(solution)/shard_map/ppermute | solution.py:100
  62.3 4.9 %collective-permute-start.20 = (bf16[256,512]{1,0:T(8,128)(2,1)S(1)}, bf16[256,512]{1,0:T(8,128)(2,1)S(1)}, u32[]{:S(2)}, u32[]{:S(2)}) collective-permute-start(bf16[256,512]{1,0:T(8,128)(2,1)S(1)} %get-tuple-element.212), channel_id=1, source_target_pairs={{0,4},{4,0},{8,12},{12,8},{1,5},{5,1},{9,13},{13,9},{2,6},{6,2},{1... | collective-permute-start | bytes 786440 | tf_op jit(solution)/shard_map/ppermute | solution.py:100
  67.7 0.8 pad_maximum_fusion.6
  68.5 4.1 %collective-permute-start.22 = (bf16[256,512]{1,0:T(8,128)(2,1)}, bf16[256,512]{1,0:T(8,128)(2,1)S(1)}, u32[]{:S(2)}, u32[]{:S(2)}) collective-permute-start(bf16[256,512]{1,0:T(8,128)(2,1)} %get-tuple-element.206), channel_id=1, source_target_pairs={{0,4},{4,0},{8,12},{12,8},{1,5},{5,1},{9,13},{13,9},{2,6},{6,2},{1... | collective-permute-start | bytes 786440 | tf_op jit(solution)/shard_map/ppermute | solution.py:100
  73.6 1.2 fusion.114
  74.9 1.5 %fusion.4 = f32[256,2560]{1,0:T(8,128)S(1)} fusion(bf16[256,1024]{1,0:T(8,128)(2,1)S(1)} %maximum_maximum_fusion, bf16[6144,2560]{1,0:T(8,128)(2,1)S(1)} %bitcast.54), kind=kOutput, calls=%fused_computation.4 | convolution fusion | flops 1342177280 | bytes 8388608 | tf_op jit(solution)/shard_map/dot_general | solution.py:36
  78.2 0.9 pad_maximum_fusion.11
  79.1 1.5 %collective-permute-start.25 = (bf16[256,512]{1,0:T(8,128)(2,1)}, bf16[256,512]{1,0:T(8,128)(2,1)S(1)}, u32[]{:S(2)}, u32[]{:S(2)}) collective-permute-start(bf16[256,512]{1,0:T(8,128)(2,1)} %get-tuple-element.182), channel_id=1, source_target_pairs={{0,4},{4,0},{8,12},{12,8},{1,5},{5,1},{9,13},{13,9},{2,6},{6,2},{1... | collective-permute-start | bytes 786440 | tf_op jit(solution)/shard_map/ppermute | solution.py:100
  80.8 1.5 %fusion.18 = f32[256,2560]{1,0:T(8,128)S(1)} fusion(f32[256,2560]{1,0:T(8,128)S(1)} %fusion.4, bf16[256,1024]{1,0:T(8,128)(2,1)S(1)} %maximum_maximum_fusion.1, bf16[6144,2560]{1,0:T(8,128)(2,1)S(1)} %bitcast.54), kind=kOutput, calls=%fused_computation.18 | convolution fusion | flops 1342832640 | bytes 11010048 | tf_op jit(solution)/shard_map/dot_general | solution.py:36
  82.3 1.9 %convolution_add_fusion.13 = f32[256,128]{1,0:T(8,128)} fusion(f32[256,128]{1,0:T(8,128)S(1)} %fusion.114, bf16[256,1024]{1,0:T(8,128)(2,1)S(1)} %maximum_maximum_fusion.1, bf16[6144,128]{1,0:T(8,128)(2,1)} %param.20), kind=kOutput, calls=%fused_computation.52 | convolution fusion | flops 67141632 | bytes 1048576 | tf_op jit(solution)/shard_map/dot_general | solution.py:36
  84.4 1.1 convert_add_fusion.5
  85.6 1.3 %fusion.96 = bf16[128,1024]{1,0:T(8,128)(2,1)S(1)} fusion(bf16[128,128]{1,0:T(8,128)(2,1)S(1)} %fusion.136, f32[128,512]{1,0:T(8,128)S(1)} %get-tuple-element.132, f32[128,512]{1,0:T(8,128)S(1)} %get-tuple-element.131, f32[1024]{0:T(1024)S(1)} %get-tuple-element.253, bf16[128,6144]{1,0:T(8,128)(2,1)} %param.17), kind=kOutput, calls=%fused_computation.134 | convolution fusion | flops 35127296 | bytes 1085440 | tf_op jit(solution)/shard_map/dot_general | solution.py:36
  87.7 1.3 collective-permute-start.27
  89.2 1.5 %fusion.21 = f32[256,2560]{1,0:T(8,128)S(1)} fusion(f32[256,2560]{1,0:T(8,128)S(1)} %fusion.18, bf16[256,1024]{1,0:T(8,128)(2,1)S(1)} %maximum_maximum_fusion.2, bf16[6144,2560]{1,0:T(8,128)(2,1)S(1)} %bitcast.54), kind=kOutput, calls=%fused_computation.19 | convolution fusion | flops 1342832640 | bytes 11010048 | tf_op jit(solution)/shard_map/dot_general | solution.py:36
  90.7 1.2 convolution_add_fusion.12
  92.1 1.1 convert_add_fusion.4
  93.3 1.3 %fusion.101 = bf16[128,1024]{1,0:T(8,128)(2,1)S(1)} fusion(bf16[128,128]{1,0:T(8,128)(2,1)S(1)} %fusion.135, f32[128,512]{1,0:T(8,128)S(1)} %get-tuple-element.140, f32[128,512]{1,0:T(8,128)S(1)} %get-tuple-element.139, f32[1024]{0:T(1024)S(1)} %get-tuple-element.255, bf16[128,6144]{1,0:T(8,128)(2,1)} %param.17), kind=kOutput, calls=%fused_computation.139 | convolution fusion | flops 35127296 | bytes 1085440 | tf_op jit(solution)/shard_map/dot_general | solution.py:36
  94.6 1.6 %collective-permute-start.24 = (bf16[256,512]{1,0:T(8,128)(2,1)S(1)}, bf16[256,512]{1,0:T(8,128)(2,1)S(1)}, u32[]{:S(2)}, u32[]{:S(2)}) collective-permute-start(bf16[256,512]{1,0:T(8,128)(2,1)S(1)} %pad_maximum_fusion.13), channel_id=1, source_target_pairs={{0,4},{4,0},{8,12},{12,8},{1,5},{5,1},{9,13},{13,9},{2,6},{6,2},{1... | collective-permute-start | bytes 786440 | tf_op jit(solution)/shard_map/ppermute | solution.py:100
  96.3 0.9 fusion.24
  97.2 1.2 convolution_add_fusion.19
  98.4 1.0 convert_add_fusion.3
  99.5 1.3 %fusion.106 = bf16[128,1024]{1,0:T(8,128)(2,1)S(1)} fusion(bf16[128,128]{1,0:T(8,128)(2,1)S(1)} %fusion.135, f32[128,512]{1,0:T(8,128)S(1)} %get-tuple-element.130, f32[128,512]{1,0:T(8,128)S(1)} %get-tuple-element.129, f32[1024]{0:T(1024)S(1)} %get-tuple-element.254, bf16[128,6144]{1,0:T(8,128)(2,1)} %param.17), kind=kOutput, calls=%fused_computation.144 | convolution fusion | flops 35127296 | bytes 1085440 | tf_op jit(solution)/shard_map/dot_general | solution.py:36
  100.8 1.5 %collective-permute-start.29 = (bf16[256,512]{1,0:T(8,128)(2,1)S(1)}, bf16[256,512]{1,0:T(8,128)(2,1)S(1)}, u32[]{:S(2)}, u32[]{:S(2)}) collective-permute-start(bf16[256,512]{1,0:T(8,128)(2,1)S(1)} %pad_maximum_fusion.15), channel_id=1, source_target_pairs={{0,4},{4,0},{8,12},{12,8},{1,5},{5,1},{9,13},{13,9},{2,6},{6,2},{1... | collective-permute-start | bytes 786440 | tf_op jit(solution)/shard_map/ppermute | solution.py:100
  102.4 0.9 fusion.30
  104.6 1.3 %fusion.111 = bf16[128,1024]{1,0:T(8,128)(2,1)S(1)} fusion(bf16[128,128]{1,0:T(8,128)(2,1)S(1)} %copy-done.11, f32[128,512]{1,0:T(8,128)S(1)} %get-tuple-element.128, f32[128,512]{1,0:T(8,128)S(1)} %get-tuple-element.127, f32[1024]{0:T(1024)S(1)} %get-tuple-element.253, bf16[128,6144]{1,0:T(8,128)(2,1)} %param.17), kind=kOutput, calls=%fused_computation.149 | convolution fusion | flops 35127296 | bytes 1085440 | tf_op jit(solution)/shard_map/dot_general | solution.py:36
  106.0 1.6 %collective-permute-start.30 = (bf16[256,512]{1,0:T(8,128)(2,1)S(1)}, bf16[256,512]{1,0:T(8,128)(2,1)}, u32[]{:S(2)}, u32[]{:S(2)}) collective-permute-start(bf16[256,512]{1,0:T(8,128)(2,1)S(1)} %pad_maximum_fusion.17), channel_id=1, source_target_pairs={{0,4},{4,0},{8,12},{12,8},{1,5},{5,1},{9,13},{13,9},{2,6},{6,2},{1... | collective-permute-start | bytes 786440 | tf_op jit(solution)/shard_map/ppermute | solution.py:100
  107.5 1.0 broadcast_select_fusion.3
  108.6 0.9 fusion.36
  110.0 1.6 %collective-permute-done.31 = bf16[64,2688]{1,0:T(8,128)(2,1)S(1)} collective-permute-done((bf16[64,2688]{1,0:T(8,128)(2,1)S(1)}, bf16[64,2688]{1,0:T(8,128)(2,1)S(1)}, u32[]{:S(2)}, u32[]{:S(2)}) %collective-permute-start.31) | collective-permute-done | bytes 344096 | tf_op jit(solution)/shard_map/ppermute | solution.py:97
  112.3 0.9 fusion.27
  113.4 1.4 %collective-permute-done.30 = bf16[256,512]{1,0:T(8,128)(2,1)} collective-permute-done((bf16[256,512]{1,0:T(8,128)(2,1)S(1)}, bf16[256,512]{1,0:T(8,128)(2,1)}, u32[]{:S(2)}, u32[]{:S(2)}) %collective-permute-start.30) | collective-permute-done | bytes 262176 | tf_op jit(solution)/shard_map/ppermute | solution.py:100
  114.7 7.1 %collective-permute-done.32 = bf16[64,2688]{1,0:T(8,128)(2,1)S(1)} collective-permute-done((bf16[64,2688]{1,0:T(8,128)(2,1)S(1)}, bf16[64,2688]{1,0:T(8,128)(2,1)S(1)}, u32[]{:S(2)}, u32[]{:S(2)}) %collective-permute-start.32) | collective-permute-done | bytes 344096 | tf_op jit(solution)/shard_map/ppermute | solution.py:97
  121.8 1.1 broadcast_select_fusion
  123.0 0.9 fusion.33
  124.3 0.9 fusion.39
  125.4 1.6 %collective-permute-done.33 = bf16[64,2688]{1,0:T(8,128)(2,1)S(1)} collective-permute-done((bf16[64,2688]{1,0:T(8,128)(2,1)S(1)}, bf16[64,2688]{1,0:T(8,128)(2,1)S(1)}, u32[]{:S(2)}, u32[]{:S(2)}) %collective-permute-start.33) | collective-permute-done | bytes 344096 | tf_op jit(solution)/shard_map/ppermute | solution.py:97
  127.2 1.0 fusion.51
  (230 shorter events, 16.6 us)
Async XLA Ops:
  0.0 127.2 %copy-start = (bf16[128,2560]{1,0:T(8,128)(2,1)S(1)}, bf16[128,2560]{1,0:T(8,128)(2,1)}, u32[]{:S(2)}) copy-start(bf16[128,2560]{1,0:T(8,128)(2,1)} %param.21) | copy-start | bytes 1966084
  0.0 19.6 %collective-permute-start = (bf16[64,2560]{1,0:T(8,128)(2,1)}, bf16[64,2560]{1,0:T(8,128)(2,1)S(1)}, u32[]{:S(2)}, u32[]{:S(2)}) collective-permute-start(bf16[64,2560]{1,0:T(8,128)(2,1)} %param.11), channel_id=1, source_target_pairs={{0,2},{1,3},{2,0},{3,1},{4,6},{5,7},{6,4},{7,5},{8,10},{9,11},{10,... | collective-permute-start | bytes 983048 | tf_op jit(solution)/shard_map/ppermute | solution.py:97
  2.9 3.3 %collective-permute-start.2 = (bf16[64,2560]{1,0:T(8,128)(2,1)}, bf16[64,2560]{1,0:T(8,128)(2,1)S(1)}, u32[]{:S(2)}, u32[]{:S(2)}) collective-permute-start(bf16[64,2560]{1,0:T(8,128)(2,1)} %param.11), channel_id=1, source_target_pairs={{0,1},{1,0},{2,3},{3,2},{4,5},{5,4},{6,7},{7,6},{8,9},{9,8},{10,11... | collective-permute-start | bytes 983048 | tf_op jit(solution)/shard_map/ppermute | solution.py:97
  2.9 0.7 copy-start.1
  3.6 2.6 %copy-start.9 = (bf16[64,2560]{1,0:T(8,128)(2,1)S(1)}, bf16[64,2560]{1,0:T(8,128)(2,1)}, u32[]{:S(2)}) copy-start(bf16[64,2560]{1,0:T(8,128)(2,1)} %param.11) | copy-start | bytes 983044
  6.2 1.1 copy-start.4
  8.5 11.2 %collective-permute-start.3 = (bf16[288,512]{1,0:T(8,128)(2,1)S(1)}, bf16[288,512]{1,0:T(8,128)(2,1)S(1)}, u32[]{:S(2)}, u32[]{:S(2)}) collective-permute-start(bf16[288,512]{1,0:T(8,128)(2,1)S(1)} %maximum_maximum_fusion.3.after_ref), channel_id=1, source_target_pairs={{0,4},{4,0},{8,12},{12,8},{1,5},{5,1},{9,13},{13,9},{2,6},{6,2},{1... | collective-permute-start | bytes 884744 | tf_op jit(solution)/shard_map/ppermute | solution.py:100
  13.6 10.4 %collective-permute-start.4 = (bf16[256,512]{1,0:T(8,128)(2,1)S(1)}, bf16[256,512]{1,0:T(8,128)(2,1)S(1)}, u32[]{:S(2)}, u32[]{:S(2)}) collective-permute-start(bf16[256,512]{1,0:T(8,128)(2,1)S(1)} %pad_maximum_fusion.2.after_ref), channel_id=1, source_target_pairs={{0,4},{4,0},{8,12},{12,8},{1,5},{5,1},{9,13},{13,9},{2,6},{6,2},{1... | collective-permute-start | bytes 786440 | tf_op jit(solution)/shard_map/ppermute | solution.py:100
  16.6 2.6 %copy-start.2 = (s32[4]{0:T(128)S(1)}, s32[4]{0:T(128)}, u32[]{:S(2)}) copy-start(s32[4]{0:T(128)} %after_ref) | copy-start | bytes 52
  16.6 2.6 %copy-start.14 = (s32[256]{0:T(256)S(1)}, s32[256]{0:T(256)}, u32[]{:S(2)}) copy-start(s32[256]{0:T(256)} %param.12) | copy-start | bytes 3076
  17.5 2.2 %copy-start.12 = (f32[6144]{0:T(1024)S(1)}, f32[6144]{0:T(1024)}, u32[]{:S(2)}) copy-start(f32[6144]{0:T(1024)} %param.15) | copy-start | bytes 73732
  17.5 18.1 %collective-permute-start.7 = (bf16[256,512]{1,0:T(8,128)(2,1)S(1)}, bf16[256,512]{1,0:T(8,128)(2,1)S(1)}, u32[]{:S(2)}, u32[]{:S(2)}) collective-permute-start(bf16[256,512]{1,0:T(8,128)(2,1)S(1)} %pad_maximum_fusion.3), channel_id=1, source_target_pairs={{0,4},{4,0},{8,12},{12,8},{1,5},{5,1},{9,13},{13,9},{2,6},{6,2},{1... | collective-permute-start | bytes 786440 | tf_op jit(solution)/shard_map/ppermute | solution.py:100
  19.6 1.7 %collective-permute-start.1 = (bf16[64,2560]{1,0:T(8,128)(2,1)S(1)}, bf16[64,2560]{1,0:T(8,128)(2,1)S(1)}, u32[]{:S(2)}, u32[]{:S(2)}) collective-permute-start(bf16[64,2560]{1,0:T(8,128)(2,1)S(1)} %collective-permute-done), channel_id=1, source_target_pairs={{0,1},{1,0},{2,3},{3,2},{4,5},{5,4},{6,7},{7,6},{8,9},{9,8},{10,11... | collective-permute-start | bytes 983048 | tf_op jit(solution)/shard_map/ppermute | solution.py:97
  19.8 8.4 %collective-permute-start.5 = (bf16[288,512]{1,0:T(8,128)(2,1)S(1)}, bf16[288,512]{1,0:T(8,128)(2,1)S(1)}, u32[]{:S(2)}, u32[]{:S(2)}) collective-permute-start(bf16[288,512]{1,0:T(8,128)(2,1)S(1)} %add_convert_fusion.1), channel_id=1, source_target_pairs={{0,1},{1,0},{2,3},{3,2},{4,8},{5,9},{6,10},{7,11},{8,4},{9,5},{10,... | collective-permute-start | bytes 884744 | tf_op jit(solution)/shard_map/ppermute | solution.py:103
  24.1 12.7 %collective-permute-start.8 = (bf16[256,512]{1,0:T(8,128)(2,1)S(1)}, bf16[256,512]{1,0:T(8,128)(2,1)S(1)}, u32[]{:S(2)}, u32[]{:S(2)}) collective-permute-start(bf16[256,512]{1,0:T(8,128)(2,1)S(1)} %add_convert_fusion.11), channel_id=1, source_target_pairs={{0,1},{1,0},{2,3},{3,2},{4,8},{5,9},{6,10},{7,11},{8,4},{9,5},{10,... | collective-permute-start | bytes 786440 | tf_op jit(solution)/shard_map/ppermute | solution.py:103
  24.1 19.3 %collective-permute-start.9 = (bf16[288,512]{1,0:T(8,128)(2,1)S(1)}, bf16[288,512]{1,0:T(8,128)(2,1)S(1)}, u32[]{:S(2)}, u32[]{:S(2)}) collective-permute-start(bf16[288,512]{1,0:T(8,128)(2,1)S(1)} %maximum_maximum_fusion.4), channel_id=1, source_target_pairs={{0,4},{4,0},{8,12},{12,8},{1,5},{5,1},{9,13},{13,9},{2,6},{6,2},{1... | collective-permute-start | bytes 884744 | tf_op jit(solution)/shard_map/ppermute | solution.py:100
  28.2 1.4 %copy-start.15 = (bf16[128,6144]{1,0:T(8,128)(2,1)S(1)}, bf16[128,6144]{1,0:T(8,128)(2,1)}, u32[]{:S(2)}) copy-start(bf16[128,6144]{1,0:T(8,128)(2,1)} %param.17) | copy-start | bytes 4718596
  28.4 71.1 %copy-start.10 = (bf16[128,128]{1,0:T(8,128)(2,1)}, bf16[128,128]{1,0:T(8,128)(2,1)S(1)}, u32[]{:S(2)}) copy-start(bf16[128,128]{1,0:T(8,128)(2,1)S(1)} %fusion.135) | copy-start | bytes 98308
  30.0 20.6 %collective-permute-start.6 = (bf16[256,512]{1,0:T(8,128)(2,1)S(1)}, bf16[256,512]{1,0:T(8,128)(2,1)S(1)}, u32[]{:S(2)}, u32[]{:S(2)}) collective-permute-start(bf16[256,512]{1,0:T(8,128)(2,1)S(1)} %maximum_select_fusion.after_ref), channel_id=1, source_target_pairs={{0,4},{4,0},{8,12},{12,8},{1,5},{5,1},{9,13},{13,9},{2,6},{6,2},{1... | collective-permute-start | bytes 786440 | tf_op jit(solution)/shard_map/ppermute | solution.py:100
  35.7 7.9 %collective-permute-start.10 = (bf16[256,512]{1,0:T(8,128)(2,1)S(1)}, bf16[256,512]{1,0:T(8,128)(2,1)S(1)}, u32[]{:S(2)}, u32[]{:S(2)}) collective-permute-start(bf16[256,512]{1,0:T(8,128)(2,1)S(1)} %add_convert_fusion.10), channel_id=1, source_target_pairs={{0,1},{1,0},{2,3},{3,2},{4,8},{5,9},{6,10},{7,11},{8,4},{9,5},{10,... | collective-permute-start | bytes 786440 | tf_op jit(solution)/shard_map/ppermute | solution.py:103
  37.3 14.2 %collective-permute-start.12 = (bf16[256,512]{1,0:T(8,128)(2,1)S(1)}, bf16[256,512]{1,0:T(8,128)(2,1)S(1)}, u32[]{:S(2)}, u32[]{:S(2)}) collective-permute-start(bf16[256,512]{1,0:T(8,128)(2,1)S(1)} %maximum_select_fusion.1.after_ref), channel_id=1, source_target_pairs={{0,4},{4,0},{8,12},{12,8},{1,5},{5,1},{9,13},{13,9},{2,6},{6,2},{1... | collective-permute-start | bytes 786440 | tf_op jit(solution)/shard_map/ppermute | solution.py:100
  43.5 7.4 %collective-permute-start.11 = (bf16[288,512]{1,0:T(8,128)(2,1)S(1)}, bf16[288,512]{1,0:T(8,128)(2,1)S(1)}, u32[]{:S(2)}, u32[]{:S(2)}) collective-permute-start(bf16[288,512]{1,0:T(8,128)(2,1)S(1)} %add_convert_fusion), channel_id=1, source_target_pairs={{0,1},{1,0},{2,3},{3,2},{4,8},{5,9},{6,10},{7,11},{8,4},{9,5},{10,... | collective-permute-start | bytes 884744 | tf_op jit(solution)/shard_map/ppermute | solution.py:103
  44.2 12.4 %collective-permute-start.14 = (bf16[256,512]{1,0:T(8,128)(2,1)S(1)}, bf16[256,512]{1,0:T(8,128)(2,1)S(1)}, u32[]{:S(2)}, u32[]{:S(2)}) collective-permute-start(bf16[256,512]{1,0:T(8,128)(2,1)S(1)} %get-tuple-element.218.after_ref), channel_id=1, source_target_pairs={{0,4},{4,0},{8,12},{12,8},{1,5},{5,1},{9,13},{13,9},{2,6},{6,2},{1... | collective-permute-start | bytes 786440 | tf_op jit(solution)/shard_map/ppermute | solution.py:100
  46.3 28.5 %slice-start = ((s8[31457280]{0:T(1024)(128)(4,1)}), s8[4194304]{0:T(1024)(128)(4,1)S(1)}, s32[]{:S(2)}) async-start(s8[31457280]{0:T(1024)(128)(4,1)} %bitcast.53), calls=%async_computation | async-start | bytes 8388608
  46.3 28.5 %slice-start.1 = ((s8[31457280]{0:T(1024)(128)(4,1)}), s8[4194304]{0:T(1024)(128)(4,1)S(1)}, s32[]{:S(2)}) async-start(s8[31457280]{0:T(1024)(128)(4,1)} %bitcast.53), calls=%async_computation.1 | async-start | bytes 8388608
  46.3 28.6 %slice-start.2 = ((s8[31457280]{0:T(1024)(128)(4,1)}), s8[4194304]{0:T(1024)(128)(4,1)S(1)}, s32[]{:S(2)}) async-start(s8[31457280]{0:T(1024)(128)(4,1)} %bitcast.53), calls=%async_computation.2 | async-start | bytes 8388608
  46.3 28.6 %slice-start.3 = ((s8[31457280]{0:T(1024)(128)(4,1)}), s8[4194304]{0:T(1024)(128)(4,1)S(1)}, s32[]{:S(2)}) async-start(s8[31457280]{0:T(1024)(128)(4,1)} %bitcast.53), calls=%async_computation.3 | async-start | bytes 8388608
  48.9 25.9 %slice-start.4 = ((s8[31457280]{0:T(1024)(128)(4,1)}), s8[4194304]{0:T(1024)(128)(4,1)S(1)}, s32[]{:S(2)}) async-start(s8[31457280]{0:T(1024)(128)(4,1)} %bitcast.53), calls=%async_computation.4 | async-start | bytes 8388608
  50.8 5.2 %collective-permute-start.13 = (bf16[256,512]{1,0:T(8,128)(2,1)S(1)}, bf16[256,512]{1,0:T(8,128)(2,1)S(1)}, u32[]{:S(2)}, u32[]{:S(2)}) collective-permute-start(bf16[256,512]{1,0:T(8,128)(2,1)S(1)} %add_convert_fusion.9), channel_id=1, source_target_pairs={{0,1},{1,0},{2,3},{3,2},{4,8},{5,9},{6,10},{7,11},{8,4},{9,5},{10,... | collective-permute-start | bytes 786440 | tf_op jit(solution)/shard_map/ppermute | solution.py:103
  51.0 23.9 %slice-start.5 = ((s8[31457280]{0:T(1024)(128)(4,1)}), s8[4194304]{0:T(1024)(128)(4,1)S(1)}, s32[]{:S(2)}) async-start(s8[31457280]{0:T(1024)(128)(4,1)} %bitcast.53), calls=%async_computation.5 | async-start | bytes 8388608
  51.6 9.9 %collective-permute-start.15 = (bf16[256,512]{1,0:T(8,128)(2,1)S(1)}, bf16[256,512]{1,0:T(8,128)(2,1)S(1)}, u32[]{:S(2)}, u32[]{:S(2)}) collective-permute-start(bf16[256,512]{1,0:T(8,128)(2,1)S(1)} %add_convert_fusion.8), channel_id=1, source_target_pairs={{0,1},{1,0},{2,3},{3,2},{4,8},{5,9},{6,10},{7,11},{8,4},{9,5},{10,... | collective-permute-start | bytes 786440 | tf_op jit(solution)/shard_map/ppermute | solution.py:103
  52.2 10.0 %collective-permute-start.16 = (bf16[256,512]{1,0:T(8,128)(2,1)S(1)}, bf16[256,512]{1,0:T(8,128)(2,1)S(1)}, u32[]{:S(2)}, u32[]{:S(2)}) collective-permute-start(bf16[256,512]{1,0:T(8,128)(2,1)S(1)} %get-tuple-element.210), channel_id=1, source_target_pairs={{0,4},{4,0},{8,12},{12,8},{1,5},{5,1},{9,13},{13,9},{2,6},{6,2},{1... | collective-permute-start | bytes 786440 | tf_op jit(solution)/shard_map/ppermute | solution.py:100
  56.5 18.4 %slice-start.6 = ((s8[31457280]{0:T(1024)(128)(4,1)}), s8[4194304]{0:T(1024)(128)(4,1)S(1)}, s32[]{:S(2)}) async-start(s8[31457280]{0:T(1024)(128)(4,1)} %bitcast.53), calls=%async_computation.6 | async-start | bytes 8388608
  56.7 10.5 %collective-permute-start.17 = (bf16[256,512]{1,0:T(8,128)(2,1)S(1)}, bf16[256,512]{1,0:T(8,128)(2,1)S(1)}, u32[]{:S(2)}, u32[]{:S(2)}) collective-permute-start(bf16[256,512]{1,0:T(8,128)(2,1)S(1)} %add_convert_fusion.7), channel_id=1, source_target_pairs={{0,1},{1,0},{2,3},{3,2},{4,8},{5,9},{6,10},{7,11},{8,4},{9,5},{10,... | collective-permute-start | bytes 786440 | tf_op jit(solution)/shard_map/ppermute | solution.py:103
  56.7 16.0 %collective-permute-start.18 = (bf16[256,512]{1,0:T(8,128)(2,1)S(1)}, bf16[256,512]{1,0:T(8,128)(2,1)S(1)}, u32[]{:S(2)}, u32[]{:S(2)}) collective-permute-start(bf16[256,512]{1,0:T(8,128)(2,1)S(1)} %get-tuple-element.196), channel_id=1, source_target_pairs={{0,4},{4,0},{8,12},{12,8},{1,5},{5,1},{9,13},{13,9},{2,6},{6,2},{1... | collective-permute-start | bytes 786440 | tf_op jit(solution)/shard_map/ppermute | solution.py:100
  62.1 5.5 %copy-start.6 = (bf16[256,512]{1,0:T(8,128)(2,1)}, bf16[256,512]{1,0:T(8,128)(2,1)S(1)}, u32[]{:S(2)}) copy-start(bf16[256,512]{1,0:T(8,128)(2,1)S(1)} %get-tuple-element.212) | copy-start | bytes 786436
  62.2 15.5 %collective-permute-start.19 = (bf16[256,512]{1,0:T(8,128)(2,1)S(1)}, bf16[256,512]{1,0:T(8,128)(2,1)S(1)}, u32[]{:S(2)}, u32[]{:S(2)}) collective-permute-start(bf16[256,512]{1,0:T(8,128)(2,1)S(1)} %add_convert_fusion.6), channel_id=1, source_target_pairs={{0,1},{1,0},{2,3},{3,2},{4,8},{5,9},{6,10},{7,11},{8,4},{9,5},{10,... | collective-permute-start | bytes 786440 | tf_op jit(solution)/shard_map/ppermute | solution.py:103
  62.3 14.1 %collective-permute-start.20 = (bf16[256,512]{1,0:T(8,128)(2,1)S(1)}, bf16[256,512]{1,0:T(8,128)(2,1)S(1)}, u32[]{:S(2)}, u32[]{:S(2)}) collective-permute-start(bf16[256,512]{1,0:T(8,128)(2,1)S(1)} %get-tuple-element.212), channel_id=1, source_target_pairs={{0,4},{4,0},{8,12},{12,8},{1,5},{5,1},{9,13},{13,9},{2,6},{6,2},{1... | collective-permute-start | bytes 786440 | tf_op jit(solution)/shard_map/ppermute | solution.py:100
  67.2 7.6 %slice-start.7 = ((s8[31457280]{0:T(1024)(128)(4,1)}), s8[2097152]{0:T(1024)(128)(4,1)S(1)}, s32[]{:S(2)}) async-start(s8[31457280]{0:T(1024)(128)(4,1)} %bitcast.53), calls=%async_computation.7 | async-start | bytes 4194304
  68.5 15.7 %collective-permute-start.22 = (bf16[256,512]{1,0:T(8,128)(2,1)}, bf16[256,512]{1,0:T(8,128)(2,1)S(1)}, u32[]{:S(2)}, u32[]{:S(2)}) collective-permute-start(bf16[256,512]{1,0:T(8,128)(2,1)} %get-tuple-element.206), channel_id=1, source_target_pairs={{0,4},{4,0},{8,12},{12,8},{1,5},{5,1},{9,13},{13,9},{2,6},{6,2},{1... | collective-permute-start | bytes 786440 | tf_op jit(solution)/shard_map/ppermute | solution.py:100
  73.6 10.8 %collective-permute-start.21 = (bf16[256,512]{1,0:T(8,128)(2,1)}, bf16[256,512]{1,0:T(8,128)(2,1)}, u32[]{:S(2)}, u32[]{:S(2)}) collective-permute-start(bf16[256,512]{1,0:T(8,128)(2,1)} %add_convert_fusion.5), channel_id=1, source_target_pairs={{0,1},{1,0},{2,3},{3,2},{4,8},{5,9},{6,10},{7,11},{8,4},{9,5},{10,... | collective-permute-start | bytes 786440 | tf_op jit(solution)/shard_map/ppermute | solution.py:103
  77.2 14.9 %collective-permute-start.23 = (bf16[256,512]{1,0:T(8,128)(2,1)}, bf16[256,512]{1,0:T(8,128)(2,1)}, u32[]{:S(2)}, u32[]{:S(2)}) collective-permute-start(bf16[256,512]{1,0:T(8,128)(2,1)} %add_convert_fusion.4), channel_id=1, source_target_pairs={{0,1},{1,0},{2,3},{3,2},{4,8},{5,9},{6,10},{7,11},{8,4},{9,5},{10,... | collective-permute-start | bytes 786440 | tf_op jit(solution)/shard_map/ppermute | solution.py:103
  79.1 12.9 %collective-permute-start.25 = (bf16[256,512]{1,0:T(8,128)(2,1)}, bf16[256,512]{1,0:T(8,128)(2,1)S(1)}, u32[]{:S(2)}, u32[]{:S(2)}) collective-permute-start(bf16[256,512]{1,0:T(8,128)(2,1)} %get-tuple-element.182), channel_id=1, source_target_pairs={{0,4},{4,0},{8,12},{12,8},{1,5},{5,1},{9,13},{13,9},{2,6},{6,2},{1... | collective-permute-start | bytes 786440 | tf_op jit(solution)/shard_map/ppermute | solution.py:100
  84.3 14.1 %collective-permute-start.26 = (bf16[256,512]{1,0:T(8,128)(2,1)S(1)}, bf16[256,512]{1,0:T(8,128)(2,1)}, u32[]{:S(2)}, u32[]{:S(2)}) collective-permute-start(bf16[256,512]{1,0:T(8,128)(2,1)S(1)} %add_convert_fusion.3), channel_id=1, source_target_pairs={{0,1},{1,0},{2,3},{3,2},{4,8},{5,9},{6,10},{7,11},{8,4},{9,5},{10,... | collective-permute-start | bytes 786440 | tf_op jit(solution)/shard_map/ppermute | solution.py:103
  85.5 3.4 %copy-start.7 = (bf16[256,512]{1,0:T(8,128)(2,1)S(1)}, bf16[256,512]{1,0:T(8,128)(2,1)}, u32[]{:S(2)}) copy-start(bf16[256,512]{1,0:T(8,128)(2,1)} %copy-done.6) | copy-start | bytes 786436
  87.7 19.9 %collective-permute-start.27 = (bf16[256,512]{1,0:T(8,128)(2,1)}, bf16[256,512]{1,0:T(8,128)(2,1)}, u32[]{:S(2)}, u32[]{:S(2)}) collective-permute-start(bf16[256,512]{1,0:T(8,128)(2,1)} %pad_maximum_fusion.12), channel_id=1, source_target_pairs={{0,4},{4,0},{8,12},{12,8},{1,5},{5,1},{9,13},{13,9},{2,6},{6,2},{1... | collective-permute-start | bytes 786440 | tf_op jit(solution)/shard_map/ppermute | solution.py:100
  89.1 1.5 %copy-start.8 = (f32[256,128]{1,0:T(8,128)S(1)}, f32[256,128]{1,0:T(8,128)}, u32[]{:S(2)}) copy-start(f32[256,128]{1,0:T(8,128)} %convolution_add_fusion.13) | copy-start | bytes 393220
  89.2 2.8 %copy-start.5 = (bf16[256,512]{1,0:T(8,128)(2,1)S(1)}, bf16[256,512]{1,0:T(8,128)(2,1)}, u32[]{:S(2)}) copy-start(bf16[256,512]{1,0:T(8,128)(2,1)} %get-tuple-element.181) | copy-start | bytes 786436
  92.0 12.0 %collective-permute-start.28 = (bf16[256,512]{1,0:T(8,128)(2,1)S(1)}, bf16[256,512]{1,0:T(8,128)(2,1)S(1)}, u32[]{:S(2)}, u32[]{:S(2)}) collective-permute-start(bf16[256,512]{1,0:T(8,128)(2,1)S(1)} %add_convert_fusion.2), channel_id=1, source_target_pairs={{0,1},{1,0},{2,3},{3,2},{4,8},{5,9},{6,10},{7,11},{8,4},{9,5},{10,... | collective-permute-start | bytes 786440 | tf_op jit(solution)/shard_map/ppermute | solution.py:103
  94.6 15.1 %collective-permute-start.24 = (bf16[256,512]{1,0:T(8,128)(2,1)S(1)}, bf16[256,512]{1,0:T(8,128)(2,1)S(1)}, u32[]{:S(2)}, u32[]{:S(2)}) collective-permute-start(bf16[256,512]{1,0:T(8,128)(2,1)S(1)} %pad_maximum_fusion.13), channel_id=1, source_target_pairs={{0,4},{4,0},{8,12},{12,8},{1,5},{5,1},{9,13},{13,9},{2,6},{6,2},{1... | collective-permute-start | bytes 786440 | tf_op jit(solution)/shard_map/ppermute | solution.py:100
  100.8 12.5 %collective-permute-start.29 = (bf16[256,512]{1,0:T(8,128)(2,1)S(1)}, bf16[256,512]{1,0:T(8,128)(2,1)S(1)}, u32[]{:S(2)}, u32[]{:S(2)}) collective-permute-start(bf16[256,512]{1,0:T(8,128)(2,1)S(1)} %pad_maximum_fusion.15), channel_id=1, source_target_pairs={{0,4},{4,0},{8,12},{12,8},{1,5},{5,1},{9,13},{13,9},{2,6},{6,2},{1... | collective-permute-start | bytes 786440 | tf_op jit(solution)/shard_map/ppermute | solution.py:100
  102.4 1.4 %copy-start.3 = (bf16[6144,128]{1,0:T(8,128)(2,1)S(1)}, bf16[6144,128]{1,0:T(8,128)(2,1)}, u32[]{:S(2)}) copy-start(bf16[6144,128]{1,0:T(8,128)(2,1)} %param.20) | copy-start | bytes 4718596
  103.8 0.8 copy-start.11
  106.0 8.8 %collective-permute-start.30 = (bf16[256,512]{1,0:T(8,128)(2,1)S(1)}, bf16[256,512]{1,0:T(8,128)(2,1)}, u32[]{:S(2)}, u32[]{:S(2)}) collective-permute-start(bf16[256,512]{1,0:T(8,128)(2,1)S(1)} %pad_maximum_fusion.17), channel_id=1, source_target_pairs={{0,4},{4,0},{8,12},{12,8},{1,5},{5,1},{9,13},{13,9},{2,6},{6,2},{1... | collective-permute-start | bytes 786440 | tf_op jit(solution)/shard_map/ppermute | solution.py:100
  109.8 1.7 %collective-permute-start.31 = (bf16[64,2688]{1,0:T(8,128)(2,1)S(1)}, bf16[64,2688]{1,0:T(8,128)(2,1)S(1)}, u32[]{:S(2)}, u32[]{:S(2)}) collective-permute-start(bf16[64,2688]{1,0:T(8,128)(2,1)S(1)} %fusion.49), channel_id=1, source_target_pairs={{0,1},{1,0},{2,3},{3,2},{4,5},{5,4},{6,7},{7,6},{8,9},{9,8},{10,11... | collective-permute-start | bytes 1032200 | tf_op jit(solution)/shard_map/ppermute | solution.py:97
  111.6 10.2 %collective-permute-start.32 = (bf16[64,2688]{1,0:T(8,128)(2,1)S(1)}, bf16[64,2688]{1,0:T(8,128)(2,1)S(1)}, u32[]{:S(2)}, u32[]{:S(2)}) collective-permute-start(bf16[64,2688]{1,0:T(8,128)(2,1)S(1)} %fusion.47), channel_id=1, source_target_pairs={{0,2},{1,3},{2,0},{3,1},{4,6},{5,7},{6,4},{7,5},{8,10},{9,11},{10,... | collective-permute-start | bytes 1032200 | tf_op jit(solution)/shard_map/ppermute | solution.py:97
  125.3 1.8 %copy-start.13 = (f32[2560]{0:T(1024)S(1)}, f32[2560]{0:T(1024)}, u32[]{:S(2)}) copy-start(f32[2560]{0:T(1024)} %param.19) | copy-start | bytes 30724
  125.3 1.7 %collective-permute-start.33 = (bf16[64,2688]{1,0:T(8,128)(2,1)S(1)}, bf16[64,2688]{1,0:T(8,128)(2,1)S(1)}, u32[]{:S(2)}, u32[]{:S(2)}) collective-permute-start(bf16[64,2688]{1,0:T(8,128)(2,1)S(1)} %fusion.48), channel_id=1, source_target_pairs={{0,1},{1,0},{2,3},{3,2},{4,5},{5,4},{6,7},{7,6},{8,9},{9,8},{10,11... | collective-permute-start | bytes 1032200 | tf_op jit(solution)/shard_map/ppermute | solution.py:97

commit v12 on v11

--- a/solution.py
+++ b/solution.py
@@ -155,6 +155,12 @@
             loads[block] = load_part(first_weight, part, last)
             last = loads[block]
 
+        def load_second(block):
+            nonlocal last
+            part = (pl.ds(block * wide, wide), pl.ds(0, second_weight.shape[1]))
+            second_loads[block] = load_part(second_weight, part, last)
+            last = second_loads[block]
+
         def multiply(x, block):
             nonlocal last
             value = dot(tie(x, last), loads[block]).astype(BF16)
@@ -189,7 +195,7 @@
             states = tie(states, last)
             part = slice(block * wide, (block + 1) * wide)
             low = dot(states, second_down_maps[part])
-            value = dot(states, second_weight[part])
+            value = dot(states, second_loads[block])
             if name in outputs:
                 value, low = outputs[name][0] + value, outputs[name][1] + low
             value = lax.optimization_barrier(value)
@@ -200,8 +206,7 @@
             joined = jnp.concatenate(outputs[name], axis=1)
             return joined[:rows], joined[rows:].astype(BF16)
 
-        far = col_swap(tokens, 2)
-        loads, outputs = {}, {}
+        loads, second_loads, outputs = {}, {}, {}
         last, is_end, mine = lax.optimization_barrier((jobs, is_end, mine))
         load(0)
         gathered_near = jnp.concatenate([tokens, tie(col_swap(tokens, 1), last)], axis=0)
@@ -210,6 +215,8 @@
                 load(unit)
             first_half(unit, gathered_near)
             send(unit, partials[unit])
+            if unit == 0:
+                far = col_swap(tie(tokens, last), 2)
         mask = mask_of(mine, last)
         first_bias = tie(first_bias, last)
         for t in range(UNITS + LAG):
@@ -220,7 +227,6 @@
                 crosses[t] = cross(sums[t])
             if t == 0:
                 gathered_far = jnp.concatenate([far, col_swap(far, 1)], axis=0)
-                gathered = jnp.concatenate([gathered_near, gathered_far], axis=0)
             if t < early:
                 first_half(early + t, gathered_far)
                 if early + t < LAG:
@@ -243,6 +249,11 @@
                 last = value
                 send(k + LAG, value)
             unit = t - LAG
+            if t == 1:
+                whole = tie((gathered_near, gathered_far), last)
+                gathered = jnp.concatenate(whole, axis=0)
+            if LAG <= t < LAG + 2 * early:
+                load_second(t - LAG)
             if 1 <= t <= early:
                 load(early + t - 1)
                 first_late(2 * early + t - 1, gathered)

time: 129 us -> 135 us (1.047)
  Pallas kernels: 15.2 us -> 30 us
  waiting for transfers between devices: 14.1 us -> 23.3 us
  other arithmetic: 12.7 us -> 3.9 us
  matrix products: 36 us -> 28 us
  local copies, waits for them, and re-layouts: 4.95 us -> 3.35 us
    pallas_call x6 -> x12, Pallas kernels: 15.2 us -> 30 us  [load_part(): pl.pallas_call(functools.partial(load_kernel, part=part), in_specs=[pl.Bl...]
    dot_general x42, matrix products: 36 us -> 28 us  [dot(): return jnp.dot(left, right, preferred_element_type=F32)]
    ppermute x16, waiting for transfers between devices: 2.85 us -> 8.57 us  [end_swap(): return lax.ppermute(value, 'row', [(i, i ^ 1) for i in range(n_row)])]
    ppermute x6, waiting for transfers between devices: 11.2 us -> 14.7 us  [col_swap(): return lax.ppermute(value, 'col', [(i, i ^ flip) for i in range(n_col)])]
    add x12, other arithmetic: 4.07 us -> 0.84 us  [pipeline(): summed = tie(sums[k], last).astype(F32) + crosses[k].astype(F32)]
    concatenate x14, other arithmetic: 2.84 us -> 0.61 us  [halves(): return jnp.concatenate([value[:, :width], value[:, width:]], axis=0)]
    select_n x11, other arithmetic: 2.43 us -> 0.51 us  [state(): return jnp.where(is_end, come, payloads[unit + LAG])]
    unnamed x51 -> x23, local copies, waits for them, and re-layouts: 3.71 us -> 2.06 us
  transfers between devices with their start and end apart: 34 -> 34, of which waited for: 6 -> 8; matrix products, arithmetic and copies ran while one was open for 36% -> 21% of each run, Pallas kernels for 12% -> 22%
where the time goes in v12:
time: 135 us; the launch traced here: 134 us
  starting transfers between devices  43.8 us (32%)
  Pallas kernels  30 us (22%)
  matrix products  28 us (21%)
  waiting for transfers between devices  23.3 us (17%)
  other arithmetic  3.9 us (3%)
  local copies, waits for them, and re-layouts  3.35 us (2%)
  between operations  1.6 us (1%)
    ppermute x16, starting transfers between devices, end_swap(): return lax.ppermute(value, 'row', [(i, i ^ 1) for i in range(n_row)])  37.4 us
    pallas_call x12, Pallas kernels, load_part(): pl.pallas_call(functools.partial(load_kernel, part=part), in_specs=[pl.Bl...  30 us
    dot_general x42, matrix products, dot(): return jnp.dot(left, right, preferred_element_type=F32)  28 us
    ppermute x6, waiting for transfers between devices, col_swap(): return lax.ppermute(value, 'col', [(i, i ^ flip) for i in range(n_col)])  14.7 us
    ppermute x16, waiting for transfers between devices, end_swap(): return lax.ppermute(value, 'row', [(i, i ^ 1) for i in range(n_row)])  8.57 us
    ppermute x6, starting transfers between devices, col_swap(): return lax.ppermute(value, 'col', [(i, i ^ flip) for i in range(n_col)])  4.14 us
  transfers between devices with their start and end apart: 34, of which 8 were waited for; matrix products, arithmetic and copies ran while one was open for 21% of the time, Pallas kernels for 22%

profile of v12, /device:TPU:0, one launch (start us, length us, event | category | flops | bytes accessed | tf_op | source)
XLA Modules:
  0.0 134.0 jit_solution(14465153671564514935)
XLA Ops:
  0.0 0.5 collective-permute-start
  0.5 0.7 copy-done.1
  1.1 2.6 %shard_map.109 = bf16[2560,1024]{1,0:T(8,128)(2,1)S(1)} custom-call(bf16[2560,6144]{1,0:T(8,128)(2,1)} %w_hbm.17, s32[4]{0:T(128)S(1)} %copy-done.1), custom_call_target="tpu_custom_call" | custom-call | bytes 1000 | tf_op jit(solution)/shard_map/pallas_call | solution.py:51
  4.2 0.9 convolution_convert_fusion.8
  5.1 2.7 %collective-permute-start.3 = (bf16[288,512]{1,0:T(8,128)(2,1)S(1)}, bf16[288,512]{1,0:T(8,128)(2,1)S(1)}, u32[]{:S(2)}, u32[]{:S(2)}) collective-permute-start(bf16[288,512]{1,0:T(8,128)(2,1)S(1)} %maximum_maximum_fusion.3.after_ref), channel_id=1, source_target_pairs={{0,4},{4,0},{8,12},{12,8},{1,5},{5,1},{9,13},{13,9},{2,6},{6,2},{1... | collective-permute-start | bytes 884744 | tf_op jit(solution)/shard_map/ppermute | solution.py:100
  7.9 2.5 %shard_map.110 = bf16[2560,1024]{1,0:T(8,128)(2,1)S(1)} custom-call(bf16[2560,6144]{1,0:T(8,128)(2,1)} %w_hbm.17, bf16[288,512]{1,0:T(8,128)(2,1)S(1)} %maximum_maximum_fusion.3.after_ref), custom_call_target="tpu_custom_call" | custom-call | bytes 1000 | tf_op jit(solution)/shard_map/pallas_call | solution.py:51
  10.4 0.9 convolution_convert_fusion.7
  11.3 2.5 %shard_map.111 = bf16[2560,1024]{1,0:T(8,128)(2,1)S(1)} custom-call(bf16[2560,6144]{1,0:T(8,128)(2,1)} %w_hbm.17, bf16[256,512]{1,0:T(8,128)(2,1)S(1)} %pad_maximum_fusion.2.after_ref), custom_call_target="tpu_custom_call" | custom-call | bytes 1000 | tf_op jit(solution)/shard_map/pallas_call | solution.py:51
  13.9 0.8 convolution_convert_fusion.6
  14.8 2.0 %collective-permute-start.1 = (bf16[64,2560]{1,0:T(8,128)(2,1)S(1)}, bf16[64,2560]{1,0:T(8,128)(2,1)S(1)}, u32[]{:S(2)}, u32[]{:S(2)}) collective-permute-start(bf16[64,2560]{1,0:T(8,128)(2,1)S(1)} %copy-done.5), channel_id=1, source_target_pairs={{0,2},{1,3},{2,0},{3,1},{4,6},{5,7},{6,4},{7,5},{8,10},{9,11},{10,... | collective-permute-start | bytes 983048 | tf_op jit(solution)/shard_map/ppermute | solution.py:97
  16.8 1.6 %collective-permute-start.7 = (bf16[256,512]{1,0:T(8,128)(2,1)S(1)}, bf16[256,512]{1,0:T(8,128)(2,1)S(1)}, u32[]{:S(2)}, u32[]{:S(2)}) collective-permute-start(bf16[256,512]{1,0:T(8,128)(2,1)S(1)} %pad_maximum_fusion.3), channel_id=1, source_target_pairs={{0,4},{4,0},{8,12},{12,8},{1,5},{5,1},{9,13},{13,9},{2,6},{6,2},{1... | collective-permute-start | bytes 786440 | tf_op jit(solution)/shard_map/ppermute | solution.py:100
  19.0 5.6 %collective-permute-done.1 = bf16[64,2560]{1,0:T(8,128)(2,1)S(1)} collective-permute-done((bf16[64,2560]{1,0:T(8,128)(2,1)S(1)}, bf16[64,2560]{1,0:T(8,128)(2,1)S(1)}, u32[]{:S(2)}, u32[]{:S(2)}) %collective-permute-start.1) | collective-permute-done | bytes 327712 | tf_op jit(solution)/shard_map/ppermute | solution.py:97
  24.6 1.6 %collective-permute-done.2 = bf16[64,2560]{1,0:T(8,128)(2,1)S(1)} collective-permute-done((bf16[64,2560]{1,0:T(8,128)(2,1)S(1)}, bf16[64,2560]{1,0:T(8,128)(2,1)S(1)}, u32[]{:S(2)}, u32[]{:S(2)}) %collective-permute-start.2) | collective-permute-done | bytes 327712 | tf_op jit(solution)/shard_map/ppermute | solution.py:97
  26.6 0.8 convolution_convert_fusion.5
  27.6 0.8 convolution_convert_fusion.4
  28.7 1.2 copy-done.9
  30.4 2.5 %shard_map.112 = bf16[2560,1024]{1,0:T(8,128)(2,1)S(1)} custom-call(bf16[2560,6144]{1,0:T(8,128)(2,1)} %w_hbm.17, bf16[256,512]{1,0:T(8,128)(2,1)S(1)} %maximum_select_fusion.after_ref), custom_call_target="tpu_custom_call" | custom-call | bytes 1000 | tf_op jit(solution)/shard_map/pallas_call | solution.py:51
  32.9 1.8 %collective-permute-start.9 = (bf16[288,512]{1,0:T(8,128)(2,1)S(1)}, bf16[288,512]{1,0:T(8,128)(2,1)S(1)}, u32[]{:S(2)}, u32[]{:S(2)}) collective-permute-start(bf16[288,512]{1,0:T(8,128)(2,1)S(1)} %maximum_maximum_fusion.4), channel_id=1, source_target_pairs={{0,4},{4,0},{8,12},{12,8},{1,5},{5,1},{9,13},{13,9},{2,6},{6,2},{1... | collective-permute-start | bytes 884744 | tf_op jit(solution)/shard_map/ppermute | solution.py:100
  34.7 3.2 %collective-permute-start.6 = (bf16[256,512]{1,0:T(8,128)(2,1)S(1)}, bf16[256,512]{1,0:T(8,128)(2,1)S(1)}, u32[]{:S(2)}, u32[]{:S(2)}) collective-permute-start(bf16[256,512]{1,0:T(8,128)(2,1)S(1)} %maximum_select_fusion.after_ref), channel_id=1, source_target_pairs={{0,4},{4,0},{8,12},{12,8},{1,5},{5,1},{9,13},{13,9},{2,6},{6,2},{1... | collective-permute-start | bytes 786440 | tf_op jit(solution)/shard_map/ppermute | solution.py:100
  37.9 1.5 %convolution_convert_fusion.2 = bf16[256,1024]{1,0:T(8,128)(2,1)S(1)} fusion(bf16[256,2560]{1,0:T(8,128)(2,1)S(1)} %constant_dynamic-update-slice_fusion.4, bf16[2560,1024]{1,0:T(8,128)(2,1)S(1)} %shard_map.112), kind=kOutput, calls=%fused_computation.14 | convolution fusion | flops 1342439424 | bytes 7077888 | tf_op jit(solution)/shard_map/dot_general | solution.py:36
  39.6 0.9 convolution_convert_fusion.3
  41.2 2.5 %shard_map.113 = bf16[2560,1024]{1,0:T(8,128)(2,1)S(1)} custom-call(bf16[2560,6144]{1,0:T(8,128)(2,1)} %w_hbm.17, bf16[256,512]{1,0:T(8,128)(2,1)S(1)} %maximum_select_fusion.1.after_ref), custom_call_target="tpu_custom_call" | custom-call | bytes 1000 | tf_op jit(solution)/shard_map/pallas_call | solution.py:51
  43.7 4.4 %collective-permute-start.12 = (bf16[256,512]{1,0:T(8,128)(2,1)S(1)}, bf16[256,512]{1,0:T(8,128)(2,1)S(1)}, u32[]{:S(2)}, u32[]{:S(2)}) collective-permute-start(bf16[256,512]{1,0:T(8,128)(2,1)S(1)} %maximum_select_fusion.1.after_ref), channel_id=1, source_target_pairs={{0,4},{4,0},{8,12},{12,8},{1,5},{5,1},{9,13},{13,9},{2,6},{6,2},{1... | collective-permute-start | bytes 786440 | tf_op jit(solution)/shard_map/ppermute | solution.py:100
  48.1 1.5 %convolution_convert_fusion.1 = bf16[256,1024]{1,0:T(8,128)(2,1)S(1)} fusion(bf16[256,2560]{1,0:T(8,128)(2,1)S(1)} %constant_dynamic-update-slice_fusion.4, bf16[2560,1024]{1,0:T(8,128)(2,1)S(1)} %shard_map.113), kind=kOutput, calls=%fused_computation.13 | convolution fusion | flops 1342439424 | bytes 7077888 | tf_op jit(solution)/shard_map/dot_general | solution.py:36
  50.4 2.5 %shard_map.114 = bf16[2560,1024]{1,0:T(8,128)(2,1)S(1)} custom-call(bf16[2560,6144]{1,0:T(8,128)(2,1)} %w_hbm.17, bf16[256,512]{1,0:T(8,128)(2,1)S(1)} %get-tuple-element.216.after_ref), custom_call_target="tpu_custom_call" | custom-call | bytes 1000 | tf_op jit(solution)/shard_map/pallas_call | solution.py:51
  52.9 2.1 %collective-permute-start.14 = (bf16[256,512]{1,0:T(8,128)(2,1)S(1)}, bf16[256,512]{1,0:T(8,128)(2,1)S(1)}, u32[]{:S(2)}, u32[]{:S(2)}) collective-permute-start(bf16[256,512]{1,0:T(8,128)(2,1)S(1)} %get-tuple-element.216.after_ref), channel_id=1, source_target_pairs={{0,4},{4,0},{8,12},{12,8},{1,5},{5,1},{9,13},{13,9},{2,6},{6,2},{1... | collective-permute-start | bytes 786440 | tf_op jit(solution)/shard_map/ppermute | solution.py:100
  55.1 1.7 %convolution_convert_fusion = bf16[256,1024]{1,0:T(8,128)(2,1)S(1)} fusion(bf16[256,2560]{1,0:T(8,128)(2,1)S(1)} %constant_dynamic-update-slice_fusion.4, bf16[2560,1024]{1,0:T(8,128)(2,1)S(1)} %shard_map.114), kind=kOutput, calls=%fused_computation.12 | convolution fusion | flops 1342439424 | bytes 7077888 | tf_op jit(solution)/shard_map/dot_general | solution.py:36
  57.6 2.5 %shard_map.115 = bf16[1024,2560]{1,0:T(8,128)(2,1)S(1)} custom-call(bf16[6144,2560]{1,0:T(8,128)(2,1)} %w_hbm.23, bf16[256,512]{1,0:T(8,128)(2,1)S(1)} %get-tuple-element.208.after_ref), custom_call_target="tpu_custom_call" | custom-call | bytes 1000 | tf_op jit(solution)/shard_map/pallas_call | solution.py:51
  60.2 0.6 collective-permute-start.15
  61.4 2.5 %shard_map.116 = bf16[1024,2560]{1,0:T(8,128)(2,1)S(1)} custom-call(bf16[6144,2560]{1,0:T(8,128)(2,1)} %w_hbm.23, bf16[256,512]{1,0:T(8,128)(2,1)S(1)} %get-tuple-element.194.after_ref), custom_call_target="tpu_custom_call" | custom-call | bytes 1000 | tf_op jit(solution)/shard_map/pallas_call | solution.py:51
  64.0 7.3 %collective-permute-start.16 = (bf16[256,512]{1,0:T(8,128)(2,1)S(1)}, bf16[256,512]{1,0:T(8,128)(2,1)S(1)}, u32[]{:S(2)}, u32[]{:S(2)}) collective-permute-start(bf16[256,512]{1,0:T(8,128)(2,1)S(1)} %get-tuple-element.208.after_ref), channel_id=1, source_target_pairs={{0,4},{4,0},{8,12},{12,8},{1,5},{5,1},{9,13},{13,9},{2,6},{6,2},{1... | collective-permute-start | bytes 786440 | tf_op jit(solution)/shard_map/ppermute | solution.py:100
  72.0 2.1 %collective-permute-start.20 = (bf16[256,512]{1,0:T(8,128)(2,1)S(1)}, bf16[256,512]{1,0:T(8,128)(2,1)S(1)}, u32[]{:S(2)}, u32[]{:S(2)}) collective-permute-start(bf16[256,512]{1,0:T(8,128)(2,1)S(1)} %get-tuple-element.210.after_ref), channel_id=1, source_target_pairs={{0,4},{4,0},{8,12},{12,8},{1,5},{5,1},{9,13},{13,9},{2,6},{6,2},{1... | collective-permute-start | bytes 786440 | tf_op jit(solution)/shard_map/ppermute | solution.py:100
  74.0 2.5 %shard_map.117 = bf16[1024,2560]{1,0:T(8,128)(2,1)S(1)} custom-call(bf16[6144,2560]{1,0:T(8,128)(2,1)} %w_hbm.23, bf16[256,512]{1,0:T(8,128)(2,1)S(1)} %get-tuple-element.210.after_ref), custom_call_target="tpu_custom_call" | custom-call | bytes 1000 | tf_op jit(solution)/shard_map/pallas_call | solution.py:51
  76.5 2.0 %collective-permute-done.16 = bf16[256,512]{1,0:T(8,128)(2,1)S(1)} collective-permute-done((bf16[256,512]{1,0:T(8,128)(2,1)S(1)}, bf16[256,512]{1,0:T(8,128)(2,1)S(1)}, u32[]{:S(2)}, u32[]{:S(2)}) %collective-permute-start.16) | collective-permute-done | bytes 262176 | tf_op jit(solution)/shard_map/ppermute | solution.py:100
  78.8 0.3 fusion.44
  79.2 2.1 %collective-permute-start.22 = (bf16[256,512]{1,0:T(8,128)(2,1)S(1)}, bf16[256,512]{1,0:T(8,128)(2,1)S(1)}, u32[]{:S(2)}, u32[]{:S(2)}) collective-permute-start(bf16[256,512]{1,0:T(8,128)(2,1)S(1)} %get-tuple-element.204.after_ref), channel_id=1, source_target_pairs={{0,4},{4,0},{8,12},{12,8},{1,5},{5,1},{9,13},{13,9},{2,6},{6,2},{1... | collective-permute-start | bytes 786440 | tf_op jit(solution)/shard_map/ppermute | solution.py:100
  81.3 2.5 %shard_map.118 = bf16[1024,2560]{1,0:T(8,128)(2,1)S(1)} custom-call(bf16[6144,2560]{1,0:T(8,128)(2,1)} %w_hbm.23, bf16[256,512]{1,0:T(8,128)(2,1)S(1)} %get-tuple-element.204.after_ref), custom_call_target="tpu_custom_call" | custom-call | bytes 1000 | tf_op jit(solution)/shard_map/pallas_call | solution.py:51
  84.1 1.5 %fusion.154 = f32[256,2560]{1,0:T(8,128)S(1)} fusion(bf16[256,1024]{1,0:T(8,128)(2,1)S(1)} %maximum_maximum_fusion, bf16[1024,2560]{1,0:T(8,128)(2,1)S(1)} %shard_map.115), kind=kOutput, calls=%fused_computation.308 | convolution fusion | flops 1342177280 | bytes 8388608 | tf_op jit(solution)/shard_map/dot_general | solution.py:36
  85.7 0.6 collective-permute-start.21
  86.6 3.2 %collective-permute-done.20 = bf16[256,512]{1,0:T(8,128)(2,1)S(1)} collective-permute-done((bf16[256,512]{1,0:T(8,128)(2,1)S(1)}, bf16[256,512]{1,0:T(8,128)(2,1)S(1)}, u32[]{:S(2)}, u32[]{:S(2)}) %collective-permute-start.20) | collective-permute-done | bytes 262176 | tf_op jit(solution)/shard_map/ppermute | solution.py:100
  90.5 2.5 %shard_map.119 = bf16[1024,2560]{1,0:T(8,128)(2,1)S(1)} custom-call(bf16[6144,2560]{1,0:T(8,128)(2,1)} %w_hbm.23, bf16[256,512]{1,0:T(8,128)(2,1)S(1)} %get-tuple-element.180.after_ref), custom_call_target="tpu_custom_call" | custom-call | bytes 1000 | tf_op jit(solution)/shard_map/pallas_call | solution.py:51
  93.0 2.1 %collective-permute-start.25 = (bf16[256,512]{1,0:T(8,128)(2,1)S(1)}, bf16[256,512]{1,0:T(8,128)(2,1)S(1)}, u32[]{:S(2)}, u32[]{:S(2)}) collective-permute-start(bf16[256,512]{1,0:T(8,128)(2,1)S(1)} %get-tuple-element.180.after_ref), channel_id=1, source_target_pairs={{0,4},{4,0},{8,12},{12,8},{1,5},{5,1},{9,13},{13,9},{2,6},{6,2},{1... | collective-permute-start | bytes 786440 | tf_op jit(solution)/shard_map/ppermute | solution.py:100
  95.7 2.5 %shard_map.120 = bf16[1024,2560]{1,0:T(8,128)(2,1)S(1)} custom-call(bf16[6144,2560]{1,0:T(8,128)(2,1)} %w_hbm.23, bf16[256,512]{1,0:T(8,128)(2,1)S(1)} %pad_maximum_fusion.12.after_ref), custom_call_target="tpu_custom_call" | custom-call | bytes 1000 | tf_op jit(solution)/shard_map/pallas_call | solution.py:51
  98.2 0.8 collective-permute-start.27
  99.2 1.5 %convolution_add_fusion.1 = f32[256,2560]{1,0:T(8,128)S(1)} fusion(f32[256,2560]{1,0:T(8,128)S(1)} %fusion.154, bf16[256,1024]{1,0:T(8,128)(2,1)S(1)} %maximum_maximum_fusion.1, bf16[1024,2560]{1,0:T(8,128)(2,1)S(1)} %shard_map.116), kind=kOutput, calls=%fused_computation.1 | convolution fusion | flops 1342832640 | bytes 11010048 | tf_op jit(solution)/shard_map/dot_general | solution.py:36
  101.1 1.5 %convolution_add_fusion = f32[256,2560]{1,0:T(8,128)S(1)} fusion(f32[256,2560]{1,0:T(8,128)S(1)} %convolution_add_fusion.1, bf16[256,1024]{1,0:T(8,128)(2,1)S(1)} %maximum_maximum_fusion.2, bf16[1024,2560]{1,0:T(8,128)(2,1)S(1)} %shard_map.117), kind=kOutput, calls=%fused_computation | convolution fusion | flops 1342832640 | bytes 11010048 | tf_op jit(solution)/shard_map/dot_general | solution.py:36
  103.3 0.6 collective-permute-start.28
  104.4 2.9 %collective-permute-start.24 = (bf16[256,512]{1,0:T(8,128)(2,1)S(1)}, bf16[256,512]{1,0:T(8,128)(2,1)S(1)}, u32[]{:S(2)}, u32[]{:S(2)}) collective-permute-start(bf16[256,512]{1,0:T(8,128)(2,1)S(1)} %pad_maximum_fusion.13), channel_id=1, source_target_pairs={{0,4},{4,0},{8,12},{12,8},{1,5},{5,1},{9,13},{13,9},{2,6},{6,2},{1... | collective-permute-start | bytes 786440 | tf_op jit(solution)/shard_map/ppermute | solution.py:100
  107.4 0.9 convolution_add_fusion.7
  108.4 0.4 fusion.64
  108.8 3.4 %collective-permute-start.29 = (bf16[256,512]{1,0:T(8,128)(2,1)S(1)}, bf16[256,512]{1,0:T(8,128)(2,1)S(1)}, u32[]{:S(2)}, u32[]{:S(2)}) collective-permute-start(bf16[256,512]{1,0:T(8,128)(2,1)S(1)} %pad_maximum_fusion.15), channel_id=1, source_target_pairs={{0,4},{4,0},{8,12},{12,8},{1,5},{5,1},{9,13},{13,9},{2,6},{6,2},{1... | collective-permute-start | bytes 786440 | tf_op jit(solution)/shard_map/ppermute | solution.py:100
  112.2 0.9 convolution_add_fusion.6
  113.8 0.5 fusion.69
  114.3 0.8 collective-permute-start.30
  115.3 0.9 convolution_add_fusion.5
  116.7 1.6 %collective-permute-done.31 = bf16[64,2688]{1,0:T(8,128)(2,1)S(1)} collective-permute-done((bf16[64,2688]{1,0:T(8,128)(2,1)S(1)}, bf16[64,2688]{1,0:T(8,128)(2,1)S(1)}, u32[]{:S(2)}, u32[]{:S(2)}) %collective-permute-start.31) | collective-permute-done | bytes 344096 | tf_op jit(solution)/shard_map/ppermute | solution.py:97
  118.3 1.6 %collective-permute-start.32 = (bf16[64,2688]{1,0:T(8,128)(2,1)S(1)}, bf16[64,2688]{1,0:T(8,128)(2,1)S(1)}, u32[]{:S(2)}, u32[]{:S(2)}) collective-permute-start(bf16[64,2688]{1,0:T(8,128)(2,1)S(1)} %fusion.5), channel_id=1, source_target_pairs={{0,2},{1,3},{2,0},{3,1},{4,6},{5,7},{6,4},{7,5},{8,10},{9,11},{10,... | collective-permute-start | bytes 1032200 | tf_op jit(solution)/shard_map/ppermute | solution.py:97
  119.9 0.9 convolution_add_fusion.4
  121.0 3.3 %collective-permute-done.30 = bf16[256,512]{1,0:T(8,128)(2,1)S(1)} collective-permute-done((bf16[256,512]{1,0:T(8,128)(2,1)S(1)}, bf16[256,512]{1,0:T(8,128)(2,1)S(1)}, u32[]{:S(2)}, u32[]{:S(2)}) %collective-permute-start.30) | collective-permute-done | bytes 262176 | tf_op jit(solution)/shard_map/ppermute | solution.py:100
  124.3 4.2 %collective-permute-done.32 = bf16[64,2688]{1,0:T(8,128)(2,1)S(1)} collective-permute-done((bf16[64,2688]{1,0:T(8,128)(2,1)S(1)}, bf16[64,2688]{1,0:T(8,128)(2,1)S(1)}, u32[]{:S(2)}, u32[]{:S(2)}) %collective-permute-start.32) | collective-permute-done | bytes 344096 | tf_op jit(solution)/shard_map/ppermute | solution.py:97
  128.7 0.9 convolution_add_fusion.3
  129.7 0.9 convolution_add_fusion.2
  131.2 1.6 %collective-permute-done.33 = bf16[64,2688]{1,0:T(8,128)(2,1)S(1)} collective-permute-done((bf16[64,2688]{1,0:T(8,128)(2,1)S(1)}, bf16[64,2688]{1,0:T(8,128)(2,1)S(1)}, u32[]{:S(2)}, u32[]{:S(2)}) %collective-permute-start.33) | collective-permute-done | bytes 344096 | tf_op jit(solution)/shard_map/ppermute | solution.py:97
  133.0 1.0 fusion.9
  (209 shorter events, 12.3 us)
Async XLA Ops:
  0.0 133.0 %copy-start = (bf16[128,2560]{1,0:T(8,128)(2,1)S(1)}, bf16[128,2560]{1,0:T(8,128)(2,1)}, u32[]{:S(2)}) copy-start(bf16[128,2560]{1,0:T(8,128)(2,1)} %param.21) | copy-start | bytes 1966084
  0.0 3.7 %collective-permute-start = (bf16[64,2560]{1,0:T(8,128)(2,1)}, bf16[64,2560]{1,0:T(8,128)(2,1)S(1)}, u32[]{:S(2)}, u32[]{:S(2)}) collective-permute-start(bf16[64,2560]{1,0:T(8,128)(2,1)} %param.11), channel_id=1, source_target_pairs={{0,1},{1,0},{2,3},{3,2},{4,5},{5,4},{6,7},{7,6},{8,9},{9,8},{10,11... | collective-permute-start | bytes 983048 | tf_op jit(solution)/shard_map/ppermute | solution.py:97
  0.5 0.7 copy-start.1
  1.1 2.6 %copy-start.5 = (bf16[64,2560]{1,0:T(8,128)(2,1)S(1)}, bf16[64,2560]{1,0:T(8,128)(2,1)}, u32[]{:S(2)}) copy-start(bf16[64,2560]{1,0:T(8,128)(2,1)} %param.11) | copy-start | bytes 983044
  1.1 2.8 %copy-start.4 = (bf16[2560,128]{1,0:T(8,128)(2,1)S(1)}, bf16[2560,128]{1,0:T(8,128)(2,1)}, u32[]{:S(2)}) copy-start(bf16[2560,128]{1,0:T(8,128)(2,1)} %param.16) | copy-start | bytes 1966084
  5.1 13.7 %collective-permute-start.3 = (bf16[288,512]{1,0:T(8,128)(2,1)S(1)}, bf16[288,512]{1,0:T(8,128)(2,1)S(1)}, u32[]{:S(2)}, u32[]{:S(2)}) collective-permute-start(bf16[288,512]{1,0:T(8,128)(2,1)S(1)} %maximum_maximum_fusion.3.after_ref), channel_id=1, source_target_pairs={{0,4},{4,0},{8,12},{12,8},{1,5},{5,1},{9,13},{13,9},{2,6},{6,2},{1... | collective-permute-start | bytes 884744 | tf_op jit(solution)/shard_map/ppermute | solution.py:100
  13.8 4.7 %copy-start.2 = (s32[4]{0:T(128)S(1)}, s32[4]{0:T(128)}, u32[]{:S(2)}) copy-start(s32[4]{0:T(128)} %after_ref) | copy-start | bytes 52
  13.8 4.7 %copy-start.8 = (s32[256]{0:T(256)S(1)}, s32[256]{0:T(256)}, u32[]{:S(2)}) copy-start(s32[256]{0:T(256)} %param.12) | copy-start | bytes 3076
  13.8 13.7 %collective-permute-start.4 = (bf16[256,512]{1,0:T(8,128)(2,1)S(1)}, bf16[256,512]{1,0:T(8,128)(2,1)S(1)}, u32[]{:S(2)}, u32[]{:S(2)}) collective-permute-start(bf16[256,512]{1,0:T(8,128)(2,1)S(1)} %pad_maximum_fusion.2.after_ref), channel_id=1, source_target_pairs={{0,4},{4,0},{8,12},{12,8},{1,5},{5,1},{9,13},{13,9},{2,6},{6,2},{1... | collective-permute-start | bytes 786440 | tf_op jit(solution)/shard_map/ppermute | solution.py:100
  14.7 4.1 %copy-start.6 = (f32[6144]{0:T(1024)S(1)}, f32[6144]{0:T(1024)}, u32[]{:S(2)}) copy-start(f32[6144]{0:T(1024)} %param.15) | copy-start | bytes 73732
  14.8 9.8 %collective-permute-start.1 = (bf16[64,2560]{1,0:T(8,128)(2,1)S(1)}, bf16[64,2560]{1,0:T(8,128)(2,1)S(1)}, u32[]{:S(2)}, u32[]{:S(2)}) collective-permute-start(bf16[64,2560]{1,0:T(8,128)(2,1)S(1)} %copy-done.5), channel_id=1, source_target_pairs={{0,2},{1,3},{2,0},{3,1},{4,6},{5,7},{6,4},{7,5},{8,10},{9,11},{10,... | collective-permute-start | bytes 983048 | tf_op jit(solution)/shard_map/ppermute | solution.py:97
  16.8 22.7 %collective-permute-start.7 = (bf16[256,512]{1,0:T(8,128)(2,1)S(1)}, bf16[256,512]{1,0:T(8,128)(2,1)S(1)}, u32[]{:S(2)}, u32[]{:S(2)}) collective-permute-start(bf16[256,512]{1,0:T(8,128)(2,1)S(1)} %pad_maximum_fusion.3), channel_id=1, source_target_pairs={{0,4},{4,0},{8,12},{12,8},{1,5},{5,1},{9,13},{13,9},{2,6},{6,2},{1... | collective-permute-start | bytes 786440 | tf_op jit(solution)/shard_map/ppermute | solution.py:100
  18.9 9.6 %collective-permute-start.5 = (bf16[288,512]{1,0:T(8,128)(2,1)S(1)}, bf16[288,512]{1,0:T(8,128)(2,1)S(1)}, u32[]{:S(2)}, u32[]{:S(2)}) collective-permute-start(bf16[288,512]{1,0:T(8,128)(2,1)S(1)} %add_convert_fusion.1), channel_id=1, source_target_pairs={{0,1},{1,0},{2,3},{3,2},{4,8},{5,9},{6,10},{7,11},{8,4},{9,5},{10,... | collective-permute-start | bytes 884744 | tf_op jit(solution)/shard_map/ppermute | solution.py:103
  24.6 1.6 %collective-permute-start.2 = (bf16[64,2560]{1,0:T(8,128)(2,1)S(1)}, bf16[64,2560]{1,0:T(8,128)(2,1)S(1)}, u32[]{:S(2)}, u32[]{:S(2)}) collective-permute-start(bf16[64,2560]{1,0:T(8,128)(2,1)S(1)} %collective-permute-done.1), channel_id=1, source_target_pairs={{0,1},{1,0},{2,3},{3,2},{4,5},{5,4},{6,7},{7,6},{8,9},{9,8},{10,11... | collective-permute-start | bytes 983048 | tf_op jit(solution)/shard_map/ppermute | solution.py:97
  28.5 1.4 %copy-start.9 = (bf16[128,6144]{1,0:T(8,128)(2,1)S(1)}, bf16[128,6144]{1,0:T(8,128)(2,1)}, u32[]{:S(2)}) copy-start(bf16[128,6144]{1,0:T(8,128)(2,1)} %param.17) | copy-start | bytes 4718596
  32.9 16.8 %collective-permute-start.9 = (bf16[288,512]{1,0:T(8,128)(2,1)S(1)}, bf16[288,512]{1,0:T(8,128)(2,1)S(1)}, u32[]{:S(2)}, u32[]{:S(2)}) collective-permute-start(bf16[288,512]{1,0:T(8,128)(2,1)S(1)} %maximum_maximum_fusion.4), channel_id=1, source_target_pairs={{0,4},{4,0},{8,12},{12,8},{1,5},{5,1},{9,13},{13,9},{2,6},{6,2},{1... | collective-permute-start | bytes 884744 | tf_op jit(solution)/shard_map/ppermute | solution.py:100
  34.7 5.9 %collective-permute-start.8 = (bf16[256,512]{1,0:T(8,128)(2,1)S(1)}, bf16[256,512]{1,0:T(8,128)(2,1)S(1)}, u32[]{:S(2)}, u32[]{:S(2)}) collective-permute-start(bf16[256,512]{1,0:T(8,128)(2,1)S(1)} %add_convert_fusion.11), channel_id=1, source_target_pairs={{0,1},{1,0},{2,3},{3,2},{4,8},{5,9},{6,10},{7,11},{8,4},{9,5},{10,... | collective-permute-start | bytes 786440 | tf_op jit(solution)/shard_map/ppermute | solution.py:103
  34.7 22.1 %collective-permute-start.6 = (bf16[256,512]{1,0:T(8,128)(2,1)S(1)}, bf16[256,512]{1,0:T(8,128)(2,1)S(1)}, u32[]{:S(2)}, u32[]{:S(2)}) collective-permute-start(bf16[256,512]{1,0:T(8,128)(2,1)S(1)} %maximum_select_fusion.after_ref), channel_id=1, source_target_pairs={{0,4},{4,0},{8,12},{12,8},{1,5},{5,1},{9,13},{13,9},{2,6},{6,2},{1... | collective-permute-start | bytes 786440 | tf_op jit(solution)/shard_map/ppermute | solution.py:100
  39.5 10.3 %collective-permute-start.10 = (bf16[256,512]{1,0:T(8,128)(2,1)S(1)}, bf16[256,512]{1,0:T(8,128)(2,1)S(1)}, u32[]{:S(2)}, u32[]{:S(2)}) collective-permute-start(bf16[256,512]{1,0:T(8,128)(2,1)S(1)} %add_convert_fusion.10), channel_id=1, source_target_pairs={{0,1},{1,0},{2,3},{3,2},{4,8},{5,9},{6,10},{7,11},{8,4},{9,5},{10,... | collective-permute-start | bytes 786440 | tf_op jit(solution)/shard_map/ppermute | solution.py:103
  43.7 16.5 %collective-permute-start.12 = (bf16[256,512]{1,0:T(8,128)(2,1)S(1)}, bf16[256,512]{1,0:T(8,128)(2,1)S(1)}, u32[]{:S(2)}, u32[]{:S(2)}) collective-permute-start(bf16[256,512]{1,0:T(8,128)(2,1)S(1)} %maximum_select_fusion.1.after_ref), channel_id=1, source_target_pairs={{0,4},{4,0},{8,12},{12,8},{1,5},{5,1},{9,13},{13,9},{2,6},{6,2},{1... | collective-permute-start | bytes 786440 | tf_op jit(solution)/shard_map/ppermute | solution.py:100
  49.8 7.2 %collective-permute-start.11 = (bf16[288,512]{1,0:T(8,128)(2,1)S(1)}, bf16[288,512]{1,0:T(8,128)(2,1)S(1)}, u32[]{:S(2)}, u32[]{:S(2)}) collective-permute-start(bf16[288,512]{1,0:T(8,128)(2,1)S(1)} %add_convert_fusion), channel_id=1, source_target_pairs={{0,1},{1,0},{2,3},{3,2},{4,8},{5,9},{6,10},{7,11},{8,4},{9,5},{10,... | collective-permute-start | bytes 884744 | tf_op jit(solution)/shard_map/ppermute | solution.py:103
  52.9 10.9 %collective-permute-start.14 = (bf16[256,512]{1,0:T(8,128)(2,1)S(1)}, bf16[256,512]{1,0:T(8,128)(2,1)S(1)}, u32[]{:S(2)}, u32[]{:S(2)}) collective-permute-start(bf16[256,512]{1,0:T(8,128)(2,1)S(1)} %get-tuple-element.216.after_ref), channel_id=1, source_target_pairs={{0,4},{4,0},{8,12},{12,8},{1,5},{5,1},{9,13},{13,9},{2,6},{6,2},{1... | collective-permute-start | bytes 786440 | tf_op jit(solution)/shard_map/ppermute | solution.py:100
  56.9 3.9 %collective-permute-start.13 = (bf16[256,512]{1,0:T(8,128)(2,1)S(1)}, bf16[256,512]{1,0:T(8,128)(2,1)S(1)}, u32[]{:S(2)}, u32[]{:S(2)}) collective-permute-start(bf16[256,512]{1,0:T(8,128)(2,1)S(1)} %add_convert_fusion.9), channel_id=1, source_target_pairs={{0,1},{1,0},{2,3},{3,2},{4,8},{5,9},{6,10},{7,11},{8,4},{9,5},{10,... | collective-permute-start | bytes 786440 | tf_op jit(solution)/shard_map/ppermute | solution.py:103
  60.2 11.2 %collective-permute-start.15 = (bf16[256,512]{1,0:T(8,128)(2,1)S(1)}, bf16[256,512]{1,0:T(8,128)(2,1)S(1)}, u32[]{:S(2)}, u32[]{:S(2)}) collective-permute-start(bf16[256,512]{1,0:T(8,128)(2,1)S(1)} %add_convert_fusion.8), channel_id=1, source_target_pairs={{0,1},{1,0},{2,3},{3,2},{4,8},{5,9},{6,10},{7,11},{8,4},{9,5},{10,... | collective-permute-start | bytes 786440 | tf_op jit(solution)/shard_map/ppermute | solution.py:103
  64.0 14.7 %collective-permute-start.17 = (bf16[256,512]{1,0:T(8,128)(2,1)S(1)}, bf16[256,512]{1,0:T(8,128)(2,1)S(1)}, u32[]{:S(2)}, u32[]{:S(2)}) collective-permute-start(bf16[256,512]{1,0:T(8,128)(2,1)S(1)} %add_convert_fusion.7), channel_id=1, source_target_pairs={{0,1},{1,0},{2,3},{3,2},{4,8},{5,9},{6,10},{7,11},{8,4},{9,5},{10,... | collective-permute-start | bytes 786440 | tf_op jit(solution)/shard_map/ppermute | solution.py:103
  64.0 14.5 %collective-permute-start.16 = (bf16[256,512]{1,0:T(8,128)(2,1)S(1)}, bf16[256,512]{1,0:T(8,128)(2,1)S(1)}, u32[]{:S(2)}, u32[]{:S(2)}) collective-permute-start(bf16[256,512]{1,0:T(8,128)(2,1)S(1)} %get-tuple-element.208.after_ref), channel_id=1, source_target_pairs={{0,4},{4,0},{8,12},{12,8},{1,5},{5,1},{9,13},{13,9},{2,6},{6,2},{1... | collective-permute-start | bytes 786440 | tf_op jit(solution)/shard_map/ppermute | solution.py:100
  71.3 14.3 %collective-permute-start.18 = (bf16[256,512]{1,0:T(8,128)(2,1)S(1)}, bf16[256,512]{1,0:T(8,128)(2,1)S(1)}, u32[]{:S(2)}, u32[]{:S(2)}) collective-permute-start(bf16[256,512]{1,0:T(8,128)(2,1)S(1)} %get-tuple-element.194.after_ref), channel_id=1, source_target_pairs={{0,4},{4,0},{8,12},{12,8},{1,5},{5,1},{9,13},{13,9},{2,6},{6,2},{1... | collective-permute-start | bytes 786440 | tf_op jit(solution)/shard_map/ppermute | solution.py:100
  72.0 17.8 %collective-permute-start.20 = (bf16[256,512]{1,0:T(8,128)(2,1)S(1)}, bf16[256,512]{1,0:T(8,128)(2,1)S(1)}, u32[]{:S(2)}, u32[]{:S(2)}) collective-permute-start(bf16[256,512]{1,0:T(8,128)(2,1)S(1)} %get-tuple-element.210.after_ref), channel_id=1, source_target_pairs={{0,4},{4,0},{8,12},{12,8},{1,5},{5,1},{9,13},{13,9},{2,6},{6,2},{1... | collective-permute-start | bytes 786440 | tf_op jit(solution)/shard_map/ppermute | solution.py:100
  79.2 21.7 %collective-permute-start.22 = (bf16[256,512]{1,0:T(8,128)(2,1)S(1)}, bf16[256,512]{1,0:T(8,128)(2,1)S(1)}, u32[]{:S(2)}, u32[]{:S(2)}) collective-permute-start(bf16[256,512]{1,0:T(8,128)(2,1)S(1)} %get-tuple-element.204.after_ref), channel_id=1, source_target_pairs={{0,4},{4,0},{8,12},{12,8},{1,5},{5,1},{9,13},{13,9},{2,6},{6,2},{1... | collective-permute-start | bytes 786440 | tf_op jit(solution)/shard_map/ppermute | solution.py:100
  83.8 6.1 %collective-permute-start.19 = (bf16[256,512]{1,0:T(8,128)(2,1)S(1)}, bf16[256,512]{1,0:T(8,128)(2,1)S(1)}, u32[]{:S(2)}, u32[]{:S(2)}) collective-permute-start(bf16[256,512]{1,0:T(8,128)(2,1)S(1)} %add_convert_fusion.6), channel_id=1, source_target_pairs={{0,1},{1,0},{2,3},{3,2},{4,8},{5,9},{6,10},{7,11},{8,4},{9,5},{10,... | collective-permute-start | bytes 786440 | tf_op jit(solution)/shard_map/ppermute | solution.py:103
  84.1 2.2 %copy-start.3 = (bf16[6144,128]{1,0:T(8,128)(2,1)S(1)}, bf16[6144,128]{1,0:T(8,128)(2,1)}, u32[]{:S(2)}) copy-start(bf16[6144,128]{1,0:T(8,128)(2,1)} %param.20) | copy-start | bytes 4718596
  85.7 9.5 %collective-permute-start.21 = (bf16[256,512]{1,0:T(8,128)(2,1)S(1)}, bf16[256,512]{1,0:T(8,128)(2,1)S(1)}, u32[]{:S(2)}, u32[]{:S(2)}) collective-permute-start(bf16[256,512]{1,0:T(8,128)(2,1)S(1)} %add_convert_fusion.5), channel_id=1, source_target_pairs={{0,1},{1,0},{2,3},{3,2},{4,8},{5,9},{6,10},{7,11},{8,4},{9,5},{10,... | collective-permute-start | bytes 786440 | tf_op jit(solution)/shard_map/ppermute | solution.py:103
  89.9 14.0 %collective-permute-start.23 = (bf16[256,512]{1,0:T(8,128)(2,1)S(1)}, bf16[256,512]{1,0:T(8,128)(2,1)S(1)}, u32[]{:S(2)}, u32[]{:S(2)}) collective-permute-start(bf16[256,512]{1,0:T(8,128)(2,1)S(1)} %add_convert_fusion.4), channel_id=1, source_target_pairs={{0,1},{1,0},{2,3},{3,2},{4,8},{5,9},{6,10},{7,11},{8,4},{9,5},{10,... | collective-permute-start | bytes 786440 | tf_op jit(solution)/shard_map/ppermute | solution.py:103
  93.0 10.1 %collective-permute-start.25 = (bf16[256,512]{1,0:T(8,128)(2,1)S(1)}, bf16[256,512]{1,0:T(8,128)(2,1)S(1)}, u32[]{:S(2)}, u32[]{:S(2)}) collective-permute-start(bf16[256,512]{1,0:T(8,128)(2,1)S(1)} %get-tuple-element.180.after_ref), channel_id=1, source_target_pairs={{0,4},{4,0},{8,12},{12,8},{1,5},{5,1},{9,13},{13,9},{2,6},{6,2},{1... | collective-permute-start | bytes 786440 | tf_op jit(solution)/shard_map/ppermute | solution.py:100
  98.2 16.9 %collective-permute-start.27 = (bf16[256,512]{1,0:T(8,128)(2,1)S(1)}, bf16[256,512]{1,0:T(8,128)(2,1)S(1)}, u32[]{:S(2)}, u32[]{:S(2)}) collective-permute-start(bf16[256,512]{1,0:T(8,128)(2,1)S(1)} %pad_maximum_fusion.12.after_ref), channel_id=1, source_target_pairs={{0,4},{4,0},{8,12},{12,8},{1,5},{5,1},{9,13},{13,9},{2,6},{6,2},{1... | collective-permute-start | bytes 786440 | tf_op jit(solution)/shard_map/ppermute | solution.py:100
  101.0 7.3 %collective-permute-start.26 = (bf16[256,512]{1,0:T(8,128)(2,1)S(1)}, bf16[256,512]{1,0:T(8,128)(2,1)S(1)}, u32[]{:S(2)}, u32[]{:S(2)}) collective-permute-start(bf16[256,512]{1,0:T(8,128)(2,1)S(1)} %add_convert_fusion.3), channel_id=1, source_target_pairs={{0,1},{1,0},{2,3},{3,2},{4,8},{5,9},{6,10},{7,11},{8,4},{9,5},{10,... | collective-permute-start | bytes 786440 | tf_op jit(solution)/shard_map/ppermute | solution.py:103
  103.3 10.4 %collective-permute-start.28 = (bf16[256,512]{1,0:T(8,128)(2,1)S(1)}, bf16[256,512]{1,0:T(8,128)(2,1)S(1)}, u32[]{:S(2)}, u32[]{:S(2)}) collective-permute-start(bf16[256,512]{1,0:T(8,128)(2,1)S(1)} %add_convert_fusion.2), channel_id=1, source_target_pairs={{0,1},{1,0},{2,3},{3,2},{4,8},{5,9},{6,10},{7,11},{8,4},{9,5},{10,... | collective-permute-start | bytes 786440 | tf_op jit(solution)/shard_map/ppermute | solution.py:103
  104.4 11.8 %collective-permute-start.24 = (bf16[256,512]{1,0:T(8,128)(2,1)S(1)}, bf16[256,512]{1,0:T(8,128)(2,1)S(1)}, u32[]{:S(2)}, u32[]{:S(2)}) collective-permute-start(bf16[256,512]{1,0:T(8,128)(2,1)S(1)} %pad_maximum_fusion.13), channel_id=1, source_target_pairs={{0,4},{4,0},{8,12},{12,8},{1,5},{5,1},{9,13},{13,9},{2,6},{6,2},{1... | collective-permute-start | bytes 786440 | tf_op jit(solution)/shard_map/ppermute | solution.py:100
  108.8 12.0 %collective-permute-start.29 = (bf16[256,512]{1,0:T(8,128)(2,1)S(1)}, bf16[256,512]{1,0:T(8,128)(2,1)S(1)}, u32[]{:S(2)}, u32[]{:S(2)}) collective-permute-start(bf16[256,512]{1,0:T(8,128)(2,1)S(1)} %pad_maximum_fusion.15), channel_id=1, source_target_pairs={{0,4},{4,0},{8,12},{12,8},{1,5},{5,1},{9,13},{13,9},{2,6},{6,2},{1... | collective-permute-start | bytes 786440 | tf_op jit(solution)/shard_map/ppermute | solution.py:100
  114.3 9.9 %collective-permute-start.30 = (bf16[256,512]{1,0:T(8,128)(2,1)S(1)}, bf16[256,512]{1,0:T(8,128)(2,1)S(1)}, u32[]{:S(2)}, u32[]{:S(2)}) collective-permute-start(bf16[256,512]{1,0:T(8,128)(2,1)S(1)} %pad_maximum_fusion.17), channel_id=1, source_target_pairs={{0,4},{4,0},{8,12},{12,8},{1,5},{5,1},{9,13},{13,9},{2,6},{6,2},{1... | collective-permute-start | bytes 786440 | tf_op jit(solution)/shard_map/ppermute | solution.py:100
  116.6 1.7 %collective-permute-start.31 = (bf16[64,2688]{1,0:T(8,128)(2,1)S(1)}, bf16[64,2688]{1,0:T(8,128)(2,1)S(1)}, u32[]{:S(2)}, u32[]{:S(2)}) collective-permute-start(bf16[64,2688]{1,0:T(8,128)(2,1)S(1)} %fusion.7), channel_id=1, source_target_pairs={{0,1},{1,0},{2,3},{3,2},{4,5},{5,4},{6,7},{7,6},{8,9},{9,8},{10,11... | collective-permute-start | bytes 1032200 | tf_op jit(solution)/shard_map/ppermute | solution.py:97
  118.3 10.2 %collective-permute-start.32 = (bf16[64,2688]{1,0:T(8,128)(2,1)S(1)}, bf16[64,2688]{1,0:T(8,128)(2,1)S(1)}, u32[]{:S(2)}, u32[]{:S(2)}) collective-permute-start(bf16[64,2688]{1,0:T(8,128)(2,1)S(1)} %fusion.5), channel_id=1, source_target_pairs={{0,2},{1,3},{2,0},{3,1},{4,6},{5,7},{6,4},{7,5},{8,10},{9,11},{10,... | collective-permute-start | bytes 1032200 | tf_op jit(solution)/shard_map/ppermute | solution.py:97
  131.1 1.9 %copy-start.7 = (f32[2560]{0:T(1024)S(1)}, f32[2560]{0:T(1024)}, u32[]{:S(2)}) copy-start(f32[2560]{0:T(1024)} %param.19) | copy-start | bytes 30724
  131.2 1.7 %collective-permute-start.33 = (bf16[64,2688]{1,0:T(8,128)(2,1)S(1)}, bf16[64,2688]{1,0:T(8,128)(2,1)S(1)}, u32[]{:S(2)}, u32[]{:S(2)}) collective-permute-start(bf16[64,2688]{1,0:T(8,128)(2,1)S(1)} %fusion.6), channel_id=1, source_target_pairs={{0,1},{1,0},{2,3},{3,2},{4,5},{5,4},{6,7},{7,6},{8,9},{9,8},{10,11... | collective-permute-start | bytes 1032200 | tf_op jit(solution)/shard_map/ppermute | solution.py:97

commit v13 on v11

--- a/solution.py
+++ b/solution.py
@@ -220,7 +220,6 @@
                 crosses[t] = cross(sums[t])
             if t == 0:
                 gathered_far = jnp.concatenate([far, col_swap(far, 1)], axis=0)
-                gathered = jnp.concatenate([gathered_near, gathered_far], axis=0)
             if t < early:
                 first_half(early + t, gathered_far)
                 if early + t < LAG:
@@ -243,17 +242,16 @@
                 last = value
                 send(k + LAG, value)
             unit = t - LAG
+            if t == 1:
+                whole = tie((gathered_near, gathered_far), last)
+                gathered = jnp.concatenate(whole, axis=0)
             if 1 <= t <= early:
                 load(early + t - 1)
                 first_late(2 * early + t - 1, gathered)
             if early <= unit < 2 * early:
-                top, bottom = unfold(state(unit - early)), unfold(state(unit))
-                second("all", jnp.concatenate([top, bottom], axis=0), unit - early)
+                second("near", unfold(state(unit - early)), unit - early)
+                second("far", unfold(state(unit)), unit - early)
             elif unit >= 2 * early:
-                if unit == 2 * early:
-                    value, low = outputs["all"]
-                    outputs["near"] = (value[:near], low[:near])
-                    outputs["far"] = (value[near:], low[near:])
                 if unit == UNITS - 1:
                     last = across
                 second("near" if is_near(unit) else "far", unfold(state(unit)), block_of(unit))

time: 129 us -> 124 us (0.961)
  other arithmetic: 12.7 us -> 10.1 us
  matrix products: 36 us -> 34.5 us
  local copies, waits for them, and re-layouts: 4.95 us -> 3.66 us
    unnamed x51 -> x47, local copies, waits for them, and re-layouts: 3.71 us -> 2.15 us
    dot_general x42 -> x48, matrix products: 36 us -> 34.5 us  [dot(): return jnp.dot(left, right, preferred_element_type=F32)]
    convert_element_type x12, other arithmetic: 2.26 us -> 0.85 us  [pipeline(): sums[t] = (ours + swaps[t].astype(F32)).astype(BF16)]
  transfers between devices with their start and end apart: 34 -> 34, of which waited for: 6 -> 6; matrix products, arithmetic and copies ran while one was open for 36% -> 35% of each run, Pallas kernels for 12% -> 12%
where the time goes in v13:
time: 124 us; the launch traced here: 123 us
  starting transfers between devices  43.9 us (35%)
  matrix products  34.5 us (28%)
  Pallas kernels  15.2 us (12%)
  waiting for transfers between devices  14.1 us (11%)
  other arithmetic  10.1 us (8%)
  local copies, waits for them, and re-layouts  3.66 us (3%)
  between operations  1.83 us (1%)
    ppermute x16, starting transfers between devices, end_swap(): return lax.ppermute(value, 'row', [(i, i ^ 1) for i in range(n_row)])  38.3 us
    dot_general x48, matrix products, dot(): return jnp.dot(left, right, preferred_element_type=F32)  34.5 us
    pallas_call x6, Pallas kernels, load_part(): pl.pallas_call(functools.partial(load_kernel, part=part), in_specs=[pl.Bl...  15.2 us
    ppermute x6, waiting for transfers between devices, col_swap(): return lax.ppermute(value, 'col', [(i, i ^ flip) for i in range(n_col)])  11.1 us
    add x12, other arithmetic, pipeline(): summed = tie(sums[k], last).astype(F32) + crosses[k].astype(F32)  4.65 us
    ppermute x6, starting transfers between devices, col_swap(): return lax.ppermute(value, 'col', [(i, i ^ flip) for i in range(n_col)])  3.76 us
    ppermute x16, waiting for transfers between devices, end_swap(): return lax.ppermute(value, 'row', [(i, i ^ 1) for i in range(n_row)])  2.93 us
  transfers between devices with their start and end apart: 34, of which 6 were waited for; matrix products, arithmetic and copies ran while one was open for 35% of the time, Pallas kernels for 12%

profile of v13, /device:TPU:0, one launch (start us, length us, event | category | flops | bytes accessed | tf_op | source)
XLA Modules:
  0.0 123.2 jit_solution(13931882489059010533)
XLA Ops:
  0.0 2.9 %collective-permute-start = (bf16[64,2560]{1,0:T(8,128)(2,1)}, bf16[64,2560]{1,0:T(8,128)(2,1)S(1)}, u32[]{:S(2)}, u32[]{:S(2)}) collective-permute-start(bf16[64,2560]{1,0:T(8,128)(2,1)} %param.11), channel_id=1, source_target_pairs={{0,2},{1,3},{2,0},{3,1},{4,6},{5,7},{6,4},{7,5},{8,10},{9,11},{10,... | collective-permute-start | bytes 983048 | tf_op jit(solution)/shard_map/ppermute | solution.py:97
  3.0 0.7 copy-done.1
  3.6 2.6 %shard_map.109 = bf16[2560,1024]{1,0:T(8,128)(2,1)S(1)} custom-call(bf16[2560,6144]{1,0:T(8,128)(2,1)} %w_hbm.11, s32[4]{0:T(128)S(1)} %copy-done.1), custom_call_target="tpu_custom_call" | custom-call | bytes 1000 | tf_op jit(solution)/shard_map/pallas_call | solution.py:51
  6.7 0.8 convolution_convert_fusion.8
  7.6 1.6 %collective-permute-start.3 = (bf16[288,512]{1,0:T(8,128)(2,1)S(1)}, bf16[288,512]{1,0:T(8,128)(2,1)S(1)}, u32[]{:S(2)}, u32[]{:S(2)}) collective-permute-start(bf16[288,512]{1,0:T(8,128)(2,1)S(1)} %maximum_maximum_fusion.after_ref), channel_id=1, source_target_pairs={{0,4},{4,0},{8,12},{12,8},{1,5},{5,1},{9,13},{13,9},{2,6},{6,2},{1... | collective-permute-start | bytes 884744 | tf_op jit(solution)/shard_map/ppermute | solution.py:100
  9.3 2.5 %shard_map.110 = bf16[2560,1024]{1,0:T(8,128)(2,1)S(1)} custom-call(bf16[2560,6144]{1,0:T(8,128)(2,1)} %w_hbm.11, bf16[288,512]{1,0:T(8,128)(2,1)S(1)} %maximum_maximum_fusion.after_ref), custom_call_target="tpu_custom_call" | custom-call | bytes 1000 | tf_op jit(solution)/shard_map/pallas_call | solution.py:51
  11.8 0.8 convolution_convert_fusion.7
  13.2 2.5 %shard_map.111 = bf16[2560,1024]{1,0:T(8,128)(2,1)S(1)} custom-call(bf16[2560,6144]{1,0:T(8,128)(2,1)} %w_hbm.11, bf16[256,512]{1,0:T(8,128)(2,1)S(1)} %pad_maximum_fusion.2.after_ref), custom_call_target="tpu_custom_call" | custom-call | bytes 1000 | tf_op jit(solution)/shard_map/pallas_call | solution.py:51
  15.7 0.9 convolution_convert_fusion.6
  16.6 1.6 %collective-permute-start.7 = (bf16[256,512]{1,0:T(8,128)(2,1)S(1)}, bf16[256,512]{1,0:T(8,128)(2,1)S(1)}, u32[]{:S(2)}, u32[]{:S(2)}) collective-permute-start(bf16[256,512]{1,0:T(8,128)(2,1)S(1)} %pad_maximum_fusion.3), channel_id=1, source_target_pairs={{0,4},{4,0},{8,12},{12,8},{1,5},{5,1},{9,13},{13,9},{2,6},{6,2},{1... | collective-permute-start | bytes 786440 | tf_op jit(solution)/shard_map/ppermute | solution.py:100
  19.5 0.9 collective-permute-done.1
  20.7 0.9 convolution_convert_fusion.5
  21.7 1.4 %collective-permute-done.4 = bf16[256,512]{1,0:T(8,128)(2,1)S(1)} collective-permute-done((bf16[256,512]{1,0:T(8,128)(2,1)S(1)}, bf16[256,512]{1,0:T(8,128)(2,1)S(1)}, u32[]{:S(2)}, u32[]{:S(2)}) %collective-permute-start.4) | collective-permute-done | bytes 262176 | tf_op jit(solution)/shard_map/ppermute | solution.py:100
  23.3 3.1 %collective-permute-start.9 = (bf16[288,512]{1,0:T(8,128)(2,1)S(1)}, bf16[288,512]{1,0:T(8,128)(2,1)S(1)}, u32[]{:S(2)}, u32[]{:S(2)}) collective-permute-start(bf16[288,512]{1,0:T(8,128)(2,1)S(1)} %maximum_maximum_fusion.1), channel_id=1, source_target_pairs={{0,4},{4,0},{8,12},{12,8},{1,5},{5,1},{9,13},{13,9},{2,6},{6,2},{1... | collective-permute-start | bytes 884744 | tf_op jit(solution)/shard_map/ppermute | solution.py:100
  26.4 0.9 convolution_convert_fusion.4
  27.5 1.2 copy-done.13
  29.2 1.5 %collective-permute-start.6 = (bf16[256,512]{1,0:T(8,128)(2,1)S(1)}, bf16[256,512]{1,0:T(8,128)(2,1)S(1)}, u32[]{:S(2)}, u32[]{:S(2)}) collective-permute-start(bf16[256,512]{1,0:T(8,128)(2,1)S(1)} %maximum_select_fusion.after_ref), channel_id=1, source_target_pairs={{0,4},{4,0},{8,12},{12,8},{1,5},{5,1},{9,13},{13,9},{2,6},{6,2},{1... | collective-permute-start | bytes 786440 | tf_op jit(solution)/shard_map/ppermute | solution.py:100
  30.7 2.5 %shard_map.112 = bf16[2560,1024]{1,0:T(8,128)(2,1)S(1)} custom-call(bf16[2560,6144]{1,0:T(8,128)(2,1)} %w_hbm.11, bf16[256,512]{1,0:T(8,128)(2,1)S(1)} %maximum_select_fusion.after_ref), custom_call_target="tpu_custom_call" | custom-call | bytes 1000 | tf_op jit(solution)/shard_map/pallas_call | solution.py:51
  33.3 1.5 %convolution_convert_fusion.2 = bf16[256,1024]{1,0:T(8,128)(2,1)S(1)} fusion(bf16[256,2560]{1,0:T(8,128)(2,1)S(1)} %constant_dynamic-update-slice_fusion.4, bf16[2560,1024]{1,0:T(8,128)(2,1)S(1)} %shard_map.112), kind=kOutput, calls=%fused_computation.40 | convolution fusion | flops 1342439424 | bytes 7077888 | tf_op jit(solution)/shard_map/dot_general | solution.py:36
  35.0 0.9 convolution_convert_fusion.3
  36.5 2.0 %collective-permute-start.12 = (bf16[256,512]{1,0:T(8,128)(2,1)S(1)}, bf16[256,512]{1,0:T(8,128)(2,1)S(1)}, u32[]{:S(2)}, u32[]{:S(2)}) collective-permute-start(bf16[256,512]{1,0:T(8,128)(2,1)S(1)} %maximum_select_fusion.1.after_ref), channel_id=1, source_target_pairs={{0,4},{4,0},{8,12},{12,8},{1,5},{5,1},{9,13},{13,9},{2,6},{6,2},{1... | collective-permute-start | bytes 786440 | tf_op jit(solution)/shard_map/ppermute | solution.py:100
  38.5 2.5 %shard_map.113 = bf16[2560,1024]{1,0:T(8,128)(2,1)S(1)} custom-call(bf16[2560,6144]{1,0:T(8,128)(2,1)} %w_hbm.11, bf16[256,512]{1,0:T(8,128)(2,1)S(1)} %maximum_select_fusion.1.after_ref), custom_call_target="tpu_custom_call" | custom-call | bytes 1000 | tf_op jit(solution)/shard_map/pallas_call | solution.py:51
  41.0 1.5 %convolution_convert_fusion.1 = bf16[256,1024]{1,0:T(8,128)(2,1)S(1)} fusion(bf16[256,2560]{1,0:T(8,128)(2,1)S(1)} %constant_dynamic-update-slice_fusion.4, bf16[2560,1024]{1,0:T(8,128)(2,1)S(1)} %shard_map.113), kind=kOutput, calls=%fused_computation.39 | convolution fusion | flops 1342439424 | bytes 7077888 | tf_op jit(solution)/shard_map/dot_general | solution.py:36
  43.4 2.1 %collective-permute-start.14 = (bf16[256,512]{1,0:T(8,128)(2,1)S(1)}, bf16[256,512]{1,0:T(8,128)(2,1)S(1)}, u32[]{:S(2)}, u32[]{:S(2)}) collective-permute-start(bf16[256,512]{1,0:T(8,128)(2,1)S(1)} %get-tuple-element.222.after_ref), channel_id=1, source_target_pairs={{0,4},{4,0},{8,12},{12,8},{1,5},{5,1},{9,13},{13,9},{2,6},{6,2},{1... | collective-permute-start | bytes 786440 | tf_op jit(solution)/shard_map/ppermute | solution.py:100
  45.5 2.6 %shard_map.114 = bf16[2560,1024]{1,0:T(8,128)(2,1)S(1)} custom-call(bf16[2560,6144]{1,0:T(8,128)(2,1)} %w_hbm.11, bf16[256,512]{1,0:T(8,128)(2,1)S(1)} %get-tuple-element.222.after_ref), custom_call_target="tpu_custom_call" | custom-call | bytes 1000 | tf_op jit(solution)/shard_map/pallas_call | solution.py:51
  48.2 1.7 %convolution_convert_fusion = bf16[256,1024]{1,0:T(8,128)(2,1)S(1)} fusion(bf16[256,2560]{1,0:T(8,128)(2,1)S(1)} %constant_dynamic-update-slice_fusion.4, bf16[2560,1024]{1,0:T(8,128)(2,1)S(1)} %shard_map.114), kind=kOutput, calls=%fused_computation.38 | convolution fusion | flops 1342439424 | bytes 7077888 | tf_op jit(solution)/shard_map/dot_general | solution.py:36
  51.4 3.7 %collective-permute-start.16 = (bf16[256,512]{1,0:T(8,128)(2,1)S(1)}, bf16[256,512]{1,0:T(8,128)(2,1)S(1)}, u32[]{:S(2)}, u32[]{:S(2)}) collective-permute-start(bf16[256,512]{1,0:T(8,128)(2,1)S(1)} %get-tuple-element.216), channel_id=1, source_target_pairs={{0,4},{4,0},{8,12},{12,8},{1,5},{5,1},{9,13},{13,9},{2,6},{6,2},{1... | collective-permute-start | bytes 786440 | tf_op jit(solution)/shard_map/ppermute | solution.py:100
  55.9 4.8 %collective-permute-start.18 = (bf16[256,512]{1,0:T(8,128)(2,1)S(1)}, bf16[256,512]{1,0:T(8,128)(2,1)S(1)}, u32[]{:S(2)}, u32[]{:S(2)}) collective-permute-start(bf16[256,512]{1,0:T(8,128)(2,1)S(1)} %get-tuple-element.208), channel_id=1, source_target_pairs={{0,4},{4,0},{8,12},{12,8},{1,5},{5,1},{9,13},{13,9},{2,6},{6,2},{1... | collective-permute-start | bytes 786440 | tf_op jit(solution)/shard_map/ppermute | solution.py:100
  61.5 4.9 %collective-permute-start.20 = (bf16[256,512]{1,0:T(8,128)(2,1)S(1)}, bf16[256,512]{1,0:T(8,128)(2,1)S(1)}, u32[]{:S(2)}, u32[]{:S(2)}) collective-permute-start(bf16[256,512]{1,0:T(8,128)(2,1)S(1)} %get-tuple-element.202), channel_id=1, source_target_pairs={{0,4},{4,0},{8,12},{12,8},{1,5},{5,1},{9,13},{13,9},{2,6},{6,2},{1... | collective-permute-start | bytes 786440 | tf_op jit(solution)/shard_map/ppermute | solution.py:100
  66.6 1.3 %fusion.98 = bf16[128,1024]{1,0:T(8,128)(2,1)S(1)} fusion(bf16[128,128]{1,0:T(8,128)(2,1)S(1)} %fusion.152, f32[128,512]{1,0:T(8,128)S(1)} %get-tuple-element.156, f32[128,512]{1,0:T(8,128)S(1)} %get-tuple-element.155, f32[1024]{0:T(1024)S(1)} %get-tuple-element.257, bf16[128,6144]{1,0:T(8,128)(2,1)} %param.17), kind=kOutput, calls=%fused_computation.134 | convolution fusion | flops 35127296 | bytes 1085440 | tf_op jit(solution)/shard_map/dot_general | solution.py:36
  68.0 4.1 %collective-permute-start.22 = (bf16[256,512]{1,0:T(8,128)(2,1)S(1)}, bf16[256,512]{1,0:T(8,128)(2,1)S(1)}, u32[]{:S(2)}, u32[]{:S(2)}) collective-permute-start(bf16[256,512]{1,0:T(8,128)(2,1)S(1)} %get-tuple-element.196), channel_id=1, source_target_pairs={{0,4},{4,0},{8,12},{12,8},{1,5},{5,1},{9,13},{13,9},{2,6},{6,2},{1... | collective-permute-start | bytes 786440 | tf_op jit(solution)/shard_map/ppermute | solution.py:100
  72.5 0.9 fusion.22
  73.5 0.9 fusion.20
  74.9 1.3 %fusion.103 = bf16[128,1024]{1,0:T(8,128)(2,1)S(1)} fusion(bf16[128,128]{1,0:T(8,128)(2,1)S(1)} %fusion.152, f32[128,512]{1,0:T(8,128)S(1)} %get-tuple-element.150, f32[128,512]{1,0:T(8,128)S(1)} %get-tuple-element.149, f32[1024]{0:T(1024)S(1)} %get-tuple-element.256, bf16[128,6144]{1,0:T(8,128)(2,1)} %param.17), kind=kOutput, calls=%fused_computation.139 | convolution fusion | flops 35127296 | bytes 1085440 | tf_op jit(solution)/shard_map/dot_general | solution.py:36
  76.2 0.8 pad_maximum_fusion.12
  77.0 1.8 %collective-permute-start.25 = (bf16[256,512]{1,0:T(8,128)(2,1)}, bf16[256,512]{1,0:T(8,128)(2,1)S(1)}, u32[]{:S(2)}, u32[]{:S(2)}) collective-permute-start(bf16[256,512]{1,0:T(8,128)(2,1)} %get-tuple-element.184), channel_id=1, source_target_pairs={{0,4},{4,0},{8,12},{12,8},{1,5},{5,1},{9,13},{13,9},{2,6},{6,2},{1... | collective-permute-start | bytes 786440 | tf_op jit(solution)/shard_map/ppermute | solution.py:100
  78.9 0.9 fusion.24
  79.9 0.9 fusion.27
  81.4 1.0 convert_add_fusion.5
  82.4 1.3 %fusion.108 = bf16[128,1024]{1,0:T(8,128)(2,1)S(1)} fusion(bf16[128,128]{1,0:T(8,128)(2,1)S(1)} %fusion.152, f32[128,512]{1,0:T(8,128)S(1)} %get-tuple-element.144, f32[128,512]{1,0:T(8,128)S(1)} %get-tuple-element.143, f32[1024]{0:T(1024)S(1)} %get-tuple-element.255, bf16[128,6144]{1,0:T(8,128)(2,1)} %param.17), kind=kOutput, calls=%fused_computation.144 | convolution fusion | flops 35127296 | bytes 1085440 | tf_op jit(solution)/shard_map/dot_general | solution.py:36
  83.8 0.7 pad_maximum_fusion.14
  84.5 1.3 %collective-permute-start.27 = (bf16[256,512]{1,0:T(8,128)(2,1)}, bf16[256,512]{1,0:T(8,128)(2,1)}, u32[]{:S(2)}, u32[]{:S(2)}) collective-permute-start(bf16[256,512]{1,0:T(8,128)(2,1)} %pad_maximum_fusion.14), channel_id=1, source_target_pairs={{0,4},{4,0},{8,12},{12,8},{1,5},{5,1},{9,13},{13,9},{2,6},{6,2},{1... | collective-permute-start | bytes 786440 | tf_op jit(solution)/shard_map/ppermute | solution.py:100
  85.9 0.9 fusion.30
  86.9 0.9 fusion.33
  88.4 1.0 convert_add_fusion.4
  89.5 1.3 %fusion.113 = bf16[128,1024]{1,0:T(8,128)(2,1)S(1)} fusion(bf16[128,128]{1,0:T(8,128)(2,1)S(1)} %copy-done.9, f32[128,512]{1,0:T(8,128)S(1)} %get-tuple-element.142, f32[128,512]{1,0:T(8,128)S(1)} %get-tuple-element.141, f32[1024]{0:T(1024)S(1)} %get-tuple-element.257, bf16[128,6144]{1,0:T(8,128)(2,1)} %param.17), kind=kOutput, calls=%fused_computation.149 | convolution fusion | flops 35127296 | bytes 1085440 | tf_op jit(solution)/shard_map/dot_general | solution.py:36
  90.9 2.1 %collective-permute-start.24 = (bf16[256,512]{1,0:T(8,128)(2,1)S(1)}, bf16[256,512]{1,0:T(8,128)(2,1)S(1)}, u32[]{:S(2)}, u32[]{:S(2)}) collective-permute-start(bf16[256,512]{1,0:T(8,128)(2,1)S(1)} %pad_maximum_fusion.16), channel_id=1, source_target_pairs={{0,4},{4,0},{8,12},{12,8},{1,5},{5,1},{9,13},{13,9},{2,6},{6,2},{1... | collective-permute-start | bytes 786440 | tf_op jit(solution)/shard_map/ppermute | solution.py:100
  93.1 0.9 fusion.36
  94.2 1.0 convert_add_fusion.3
  95.5 1.3 %fusion.118 = bf16[128,1024]{1,0:T(8,128)(2,1)S(1)} fusion(bf16[128,128]{1,0:T(8,128)(2,1)S(1)} %copy-done.9, f32[128,512]{1,0:T(8,128)S(1)} %get-tuple-element.140, f32[128,512]{1,0:T(8,128)S(1)} %get-tuple-element.139, f32[1024]{0:T(1024)S(1)} %get-tuple-element.256, bf16[128,6144]{1,0:T(8,128)(2,1)} %param.17), kind=kOutput, calls=%fused_computation.154 | convolution fusion | flops 35127296 | bytes 1085440 | tf_op jit(solution)/shard_map/dot_general | solution.py:36
  97.0 0.9 fusion.42
  98.2 1.0 convert_add_fusion.2
  99.2 1.3 %fusion.123 = bf16[128,1024]{1,0:T(8,128)(2,1)S(1)} fusion(bf16[128,128]{1,0:T(8,128)(2,1)S(1)} %copy-done.9, f32[128,512]{1,0:T(8,128)S(1)} %get-tuple-element.138, f32[128,512]{1,0:T(8,128)S(1)} %get-tuple-element.137, f32[1024]{0:T(1024)S(1)} %get-tuple-element.255, bf16[128,6144]{1,0:T(8,128)(2,1)} %param.17), kind=kOutput, calls=%fused_computation.159 | convolution fusion | flops 35127296 | bytes 1085440 | tf_op jit(solution)/shard_map/dot_general | solution.py:36
  100.6 3.0 %collective-permute-start.30 = (bf16[256,512]{1,0:T(8,128)(2,1)S(1)}, bf16[256,512]{1,0:T(8,128)(2,1)S(1)}, u32[]{:S(2)}, u32[]{:S(2)}) collective-permute-start(bf16[256,512]{1,0:T(8,128)(2,1)S(1)} %pad_maximum_fusion.23), channel_id=1, source_target_pairs={{0,4},{4,0},{8,12},{12,8},{1,5},{5,1},{9,13},{13,9},{2,6},{6,2},{1... | collective-permute-start | bytes 786440 | tf_op jit(solution)/shard_map/ppermute | solution.py:100
  103.6 1.0 broadcast_select_fusion.3
  104.7 0.9 fusion.48
  106.1 1.6 %collective-permute-done.31 = bf16[64,2688]{1,0:T(8,128)(2,1)S(1)} collective-permute-done((bf16[64,2688]{1,0:T(8,128)(2,1)S(1)}, bf16[64,2688]{1,0:T(8,128)(2,1)S(1)}, u32[]{:S(2)}, u32[]{:S(2)}) %collective-permute-start.31) | collective-permute-done | bytes 344096 | tf_op jit(solution)/shard_map/ppermute | solution.py:97
  108.3 0.9 fusion.39
  109.4 1.4 %collective-permute-done.30 = bf16[256,512]{1,0:T(8,128)(2,1)S(1)} collective-permute-done((bf16[256,512]{1,0:T(8,128)(2,1)S(1)}, bf16[256,512]{1,0:T(8,128)(2,1)S(1)}, u32[]{:S(2)}, u32[]{:S(2)}) %collective-permute-start.30) | collective-permute-done | bytes 262176 | tf_op jit(solution)/shard_map/ppermute | solution.py:100
  110.9 7.0 %collective-permute-done.32 = bf16[64,2688]{1,0:T(8,128)(2,1)S(1)} collective-permute-done((bf16[64,2688]{1,0:T(8,128)(2,1)S(1)}, bf16[64,2688]{1,0:T(8,128)(2,1)S(1)}, u32[]{:S(2)}, u32[]{:S(2)}) %collective-permute-start.32) | collective-permute-done | bytes 344096 | tf_op jit(solution)/shard_map/ppermute | solution.py:97
  118.1 0.9 fusion.45
  119.5 0.9 fusion.51
  120.5 1.6 %collective-permute-done.33 = bf16[64,2688]{1,0:T(8,128)(2,1)S(1)} collective-permute-done((bf16[64,2688]{1,0:T(8,128)(2,1)S(1)}, bf16[64,2688]{1,0:T(8,128)(2,1)S(1)}, u32[]{:S(2)}, u32[]{:S(2)}) %collective-permute-start.33) | collective-permute-done | bytes 344096 | tf_op jit(solution)/shard_map/ppermute | solution.py:97
  122.2 1.0 fusion.63
  (237 shorter events, 13.9 us)
Async XLA Ops:
  0.0 122.2 %copy-start = (bf16[128,2560]{1,0:T(8,128)(2,1)S(1)}, bf16[128,2560]{1,0:T(8,128)(2,1)}, u32[]{:S(2)}) copy-start(bf16[128,2560]{1,0:T(8,128)(2,1)} %param.21) | copy-start | bytes 1966084
  0.0 18.7 %collective-permute-start = (bf16[64,2560]{1,0:T(8,128)(2,1)}, bf16[64,2560]{1,0:T(8,128)(2,1)S(1)}, u32[]{:S(2)}, u32[]{:S(2)}) collective-permute-start(bf16[64,2560]{1,0:T(8,128)(2,1)} %param.11), channel_id=1, source_target_pairs={{0,2},{1,3},{2,0},{3,1},{4,6},{5,7},{6,4},{7,5},{8,10},{9,11},{10,... | collective-permute-start | bytes 983048 | tf_op jit(solution)/shard_map/ppermute | solution.py:97
  2.9 3.3 %collective-permute-start.2 = (bf16[64,2560]{1,0:T(8,128)(2,1)}, bf16[64,2560]{1,0:T(8,128)(2,1)S(1)}, u32[]{:S(2)}, u32[]{:S(2)}) collective-permute-start(bf16[64,2560]{1,0:T(8,128)(2,1)} %param.11), channel_id=1, source_target_pairs={{0,1},{1,0},{2,3},{3,2},{4,5},{5,4},{6,7},{7,6},{8,9},{9,8},{10,11... | collective-permute-start | bytes 983048 | tf_op jit(solution)/shard_map/ppermute | solution.py:97
  2.9 0.7 copy-start.1
  3.6 2.6 %copy-start.7 = (bf16[64,2560]{1,0:T(8,128)(2,1)S(1)}, bf16[64,2560]{1,0:T(8,128)(2,1)}, u32[]{:S(2)}) copy-start(bf16[64,2560]{1,0:T(8,128)(2,1)} %param.11) | copy-start | bytes 983044
  3.6 2.8 %copy-start.4 = (bf16[2560,128]{1,0:T(8,128)(2,1)S(1)}, bf16[2560,128]{1,0:T(8,128)(2,1)}, u32[]{:S(2)}) copy-start(bf16[2560,128]{1,0:T(8,128)(2,1)} %param.16) | copy-start | bytes 1966084
  7.6 11.2 %collective-permute-start.3 = (bf16[288,512]{1,0:T(8,128)(2,1)S(1)}, bf16[288,512]{1,0:T(8,128)(2,1)S(1)}, u32[]{:S(2)}, u32[]{:S(2)}) collective-permute-start(bf16[288,512]{1,0:T(8,128)(2,1)S(1)} %maximum_maximum_fusion.after_ref), channel_id=1, source_target_pairs={{0,4},{4,0},{8,12},{12,8},{1,5},{5,1},{9,13},{13,9},{2,6},{6,2},{1... | collective-permute-start | bytes 884744 | tf_op jit(solution)/shard_map/ppermute | solution.py:100
  12.7 10.4 %collective-permute-start.4 = (bf16[256,512]{1,0:T(8,128)(2,1)S(1)}, bf16[256,512]{1,0:T(8,128)(2,1)S(1)}, u32[]{:S(2)}, u32[]{:S(2)}) collective-permute-start(bf16[256,512]{1,0:T(8,128)(2,1)S(1)} %pad_maximum_fusion.2.after_ref), channel_id=1, source_target_pairs={{0,4},{4,0},{8,12},{12,8},{1,5},{5,1},{9,13},{13,9},{2,6},{6,2},{1... | collective-permute-start | bytes 786440 | tf_op jit(solution)/shard_map/ppermute | solution.py:100
  15.7 2.6 %copy-start.2 = (s32[4]{0:T(128)S(1)}, s32[4]{0:T(128)}, u32[]{:S(2)}) copy-start(s32[4]{0:T(128)} %after_ref) | copy-start | bytes 52
  15.7 2.6 %copy-start.12 = (s32[256]{0:T(256)S(1)}, s32[256]{0:T(256)}, u32[]{:S(2)}) copy-start(s32[256]{0:T(256)} %param.12) | copy-start | bytes 3076
  16.6 2.2 %copy-start.10 = (f32[6144]{0:T(1024)S(1)}, f32[6144]{0:T(1024)}, u32[]{:S(2)}) copy-start(f32[6144]{0:T(1024)} %param.15) | copy-start | bytes 73732
  16.6 18.2 %collective-permute-start.7 = (bf16[256,512]{1,0:T(8,128)(2,1)S(1)}, bf16[256,512]{1,0:T(8,128)(2,1)S(1)}, u32[]{:S(2)}, u32[]{:S(2)}) collective-permute-start(bf16[256,512]{1,0:T(8,128)(2,1)S(1)} %pad_maximum_fusion.3), channel_id=1, source_target_pairs={{0,4},{4,0},{8,12},{12,8},{1,5},{5,1},{9,13},{13,9},{2,6},{6,2},{1... | collective-permute-start | bytes 786440 | tf_op jit(solution)/shard_map/ppermute | solution.py:100
  18.7 1.7 %collective-permute-start.1 = (bf16[64,2560]{1,0:T(8,128)(2,1)S(1)}, bf16[64,2560]{1,0:T(8,128)(2,1)S(1)}, u32[]{:S(2)}, u32[]{:S(2)}) collective-permute-start(bf16[64,2560]{1,0:T(8,128)(2,1)S(1)} %collective-permute-done), channel_id=1, source_target_pairs={{0,1},{1,0},{2,3},{3,2},{4,5},{5,4},{6,7},{7,6},{8,9},{9,8},{10,11... | collective-permute-start | bytes 983048 | tf_op jit(solution)/shard_map/ppermute | solution.py:97
  18.9 8.4 %collective-permute-start.5 = (bf16[288,512]{1,0:T(8,128)(2,1)S(1)}, bf16[288,512]{1,0:T(8,128)(2,1)S(1)}, u32[]{:S(2)}, u32[]{:S(2)}) collective-permute-start(bf16[288,512]{1,0:T(8,128)(2,1)S(1)} %add_convert_fusion.1), channel_id=1, source_target_pairs={{0,1},{1,0},{2,3},{3,2},{4,8},{5,9},{6,10},{7,11},{8,4},{9,5},{10,... | collective-permute-start | bytes 884744 | tf_op jit(solution)/shard_map/ppermute | solution.py:103
  23.2 12.7 %collective-permute-start.8 = (bf16[256,512]{1,0:T(8,128)(2,1)S(1)}, bf16[256,512]{1,0:T(8,128)(2,1)S(1)}, u32[]{:S(2)}, u32[]{:S(2)}) collective-permute-start(bf16[256,512]{1,0:T(8,128)(2,1)S(1)} %add_convert_fusion.11), channel_id=1, source_target_pairs={{0,1},{1,0},{2,3},{3,2},{4,8},{5,9},{6,10},{7,11},{8,4},{9,5},{10,... | collective-permute-start | bytes 786440 | tf_op jit(solution)/shard_map/ppermute | solution.py:103
  23.3 19.4 %collective-permute-start.9 = (bf16[288,512]{1,0:T(8,128)(2,1)S(1)}, bf16[288,512]{1,0:T(8,128)(2,1)S(1)}, u32[]{:S(2)}, u32[]{:S(2)}) collective-permute-start(bf16[288,512]{1,0:T(8,128)(2,1)S(1)} %maximum_maximum_fusion.1), channel_id=1, source_target_pairs={{0,4},{4,0},{8,12},{12,8},{1,5},{5,1},{9,13},{13,9},{2,6},{6,2},{1... | collective-permute-start | bytes 884744 | tf_op jit(solution)/shard_map/ppermute | solution.py:100
  27.3 1.4 %copy-start.13 = (bf16[128,6144]{1,0:T(8,128)(2,1)S(1)}, bf16[128,6144]{1,0:T(8,128)(2,1)}, u32[]{:S(2)}) copy-start(bf16[128,6144]{1,0:T(8,128)(2,1)} %param.17) | copy-start | bytes 4718596
  27.5 15.4 %copy-start.8 = (bf16[128,128]{1,0:T(8,128)(2,1)}, bf16[128,128]{1,0:T(8,128)(2,1)S(1)}, u32[]{:S(2)}) copy-start(bf16[128,128]{1,0:T(8,128)(2,1)S(1)} %fusion.151) | copy-start | bytes 98308
  29.2 20.7 %collective-permute-start.6 = (bf16[256,512]{1,0:T(8,128)(2,1)S(1)}, bf16[256,512]{1,0:T(8,128)(2,1)S(1)}, u32[]{:S(2)}, u32[]{:S(2)}) collective-permute-start(bf16[256,512]{1,0:T(8,128)(2,1)S(1)} %maximum_select_fusion.after_ref), channel_id=1, source_target_pairs={{0,4},{4,0},{8,12},{12,8},{1,5},{5,1},{9,13},{13,9},{2,6},{6,2},{1... | collective-permute-start | bytes 786440 | tf_op jit(solution)/shard_map/ppermute | solution.py:100
  34.9 7.9 %collective-permute-start.10 = (bf16[256,512]{1,0:T(8,128)(2,1)S(1)}, bf16[256,512]{1,0:T(8,128)(2,1)S(1)}, u32[]{:S(2)}, u32[]{:S(2)}) collective-permute-start(bf16[256,512]{1,0:T(8,128)(2,1)S(1)} %add_convert_fusion.10), channel_id=1, source_target_pairs={{0,1},{1,0},{2,3},{3,2},{4,8},{5,9},{6,10},{7,11},{8,4},{9,5},{10,... | collective-permute-start | bytes 786440 | tf_op jit(solution)/shard_map/ppermute | solution.py:103
  36.5 14.3 %collective-permute-start.12 = (bf16[256,512]{1,0:T(8,128)(2,1)S(1)}, bf16[256,512]{1,0:T(8,128)(2,1)S(1)}, u32[]{:S(2)}, u32[]{:S(2)}) collective-permute-start(bf16[256,512]{1,0:T(8,128)(2,1)S(1)} %maximum_select_fusion.1.after_ref), channel_id=1, source_target_pairs={{0,4},{4,0},{8,12},{12,8},{1,5},{5,1},{9,13},{13,9},{2,6},{6,2},{1... | collective-permute-start | bytes 786440 | tf_op jit(solution)/shard_map/ppermute | solution.py:100
  42.7 7.4 %collective-permute-start.11 = (bf16[288,512]{1,0:T(8,128)(2,1)S(1)}, bf16[288,512]{1,0:T(8,128)(2,1)S(1)}, u32[]{:S(2)}, u32[]{:S(2)}) collective-permute-start(bf16[288,512]{1,0:T(8,128)(2,1)S(1)} %add_convert_fusion), channel_id=1, source_target_pairs={{0,1},{1,0},{2,3},{3,2},{4,8},{5,9},{6,10},{7,11},{8,4},{9,5},{10,... | collective-permute-start | bytes 884744 | tf_op jit(solution)/shard_map/ppermute | solution.py:103
  43.4 12.3 %collective-permute-start.14 = (bf16[256,512]{1,0:T(8,128)(2,1)S(1)}, bf16[256,512]{1,0:T(8,128)(2,1)S(1)}, u32[]{:S(2)}, u32[]{:S(2)}) collective-permute-start(bf16[256,512]{1,0:T(8,128)(2,1)S(1)} %get-tuple-element.222.after_ref), channel_id=1, source_target_pairs={{0,4},{4,0},{8,12},{12,8},{1,5},{5,1},{9,13},{13,9},{2,6},{6,2},{1... | collective-permute-start | bytes 786440 | tf_op jit(solution)/shard_map/ppermute | solution.py:100
  45.5 26.9 %slice-start = ((s8[31457280]{0:T(1024)(128)(4,1)}), s8[4194304]{0:T(1024)(128)(4,1)S(1)}, s32[]{:S(2)}) async-start(s8[31457280]{0:T(1024)(128)(4,1)} %bitcast.59), calls=%async_computation | async-start | bytes 8388608
  45.5 26.9 %slice-start.1 = ((s8[31457280]{0:T(1024)(128)(4,1)}), s8[4194304]{0:T(1024)(128)(4,1)S(1)}, s32[]{:S(2)}) async-start(s8[31457280]{0:T(1024)(128)(4,1)} %bitcast.59), calls=%async_computation.1 | async-start | bytes 8388608
  45.5 27.0 %slice-start.2 = ((s8[31457280]{0:T(1024)(128)(4,1)}), s8[4194304]{0:T(1024)(128)(4,1)S(1)}, s32[]{:S(2)}) async-start(s8[31457280]{0:T(1024)(128)(4,1)} %bitcast.59), calls=%async_computation.2 | async-start | bytes 8388608
  45.5 27.0 %slice-start.3 = ((s8[31457280]{0:T(1024)(128)(4,1)}), s8[4194304]{0:T(1024)(128)(4,1)S(1)}, s32[]{:S(2)}) async-start(s8[31457280]{0:T(1024)(128)(4,1)} %bitcast.59), calls=%async_computation.3 | async-start | bytes 8388608
  48.1 24.3 %slice-start.4 = ((s8[31457280]{0:T(1024)(128)(4,1)}), s8[4194304]{0:T(1024)(128)(4,1)S(1)}, s32[]{:S(2)}) async-start(s8[31457280]{0:T(1024)(128)(4,1)} %bitcast.59), calls=%async_computation.4 | async-start | bytes 8388608
  50.0 22.5 %slice-start.5 = ((s8[31457280]{0:T(1024)(128)(4,1)}), s8[4194304]{0:T(1024)(128)(4,1)S(1)}, s32[]{:S(2)}) async-start(s8[31457280]{0:T(1024)(128)(4,1)} %bitcast.59), calls=%async_computation.5 | async-start | bytes 8388608
  50.0 5.1 %collective-permute-start.13 = (bf16[256,512]{1,0:T(8,128)(2,1)S(1)}, bf16[256,512]{1,0:T(8,128)(2,1)S(1)}, u32[]{:S(2)}, u32[]{:S(2)}) collective-permute-start(bf16[256,512]{1,0:T(8,128)(2,1)S(1)} %add_convert_fusion.9), channel_id=1, source_target_pairs={{0,1},{1,0},{2,3},{3,2},{4,8},{5,9},{6,10},{7,11},{8,4},{9,5},{10,... | collective-permute-start | bytes 786440 | tf_op jit(solution)/shard_map/ppermute | solution.py:103
  50.8 9.9 %collective-permute-start.15 = (bf16[256,512]{1,0:T(8,128)(2,1)S(1)}, bf16[256,512]{1,0:T(8,128)(2,1)S(1)}, u32[]{:S(2)}, u32[]{:S(2)}) collective-permute-start(bf16[256,512]{1,0:T(8,128)(2,1)S(1)} %add_convert_fusion.8), channel_id=1, source_target_pairs={{0,1},{1,0},{2,3},{3,2},{4,8},{5,9},{6,10},{7,11},{8,4},{9,5},{10,... | collective-permute-start | bytes 786440 | tf_op jit(solution)/shard_map/ppermute | solution.py:103
  51.4 9.9 %collective-permute-start.16 = (bf16[256,512]{1,0:T(8,128)(2,1)S(1)}, bf16[256,512]{1,0:T(8,128)(2,1)S(1)}, u32[]{:S(2)}, u32[]{:S(2)}) collective-permute-start(bf16[256,512]{1,0:T(8,128)(2,1)S(1)} %get-tuple-element.216), channel_id=1, source_target_pairs={{0,4},{4,0},{8,12},{12,8},{1,5},{5,1},{9,13},{13,9},{2,6},{6,2},{1... | collective-permute-start | bytes 786440 | tf_op jit(solution)/shard_map/ppermute | solution.py:100
  55.2 17.2 %slice-start.6 = ((s8[31457280]{0:T(1024)(128)(4,1)}), s8[4194304]{0:T(1024)(128)(4,1)S(1)}, s32[]{:S(2)}) async-start(s8[31457280]{0:T(1024)(128)(4,1)} %bitcast.59), calls=%async_computation.6 | async-start | bytes 8388608
  55.8 10.7 %collective-permute-start.17 = (bf16[256,512]{1,0:T(8,128)(2,1)S(1)}, bf16[256,512]{1,0:T(8,128)(2,1)S(1)}, u32[]{:S(2)}, u32[]{:S(2)}) collective-permute-start(bf16[256,512]{1,0:T(8,128)(2,1)S(1)} %add_convert_fusion.7), channel_id=1, source_target_pairs={{0,1},{1,0},{2,3},{3,2},{4,8},{5,9},{6,10},{7,11},{8,4},{9,5},{10,... | collective-permute-start | bytes 786440 | tf_op jit(solution)/shard_map/ppermute | solution.py:103
  55.9 10.4 %collective-permute-start.18 = (bf16[256,512]{1,0:T(8,128)(2,1)S(1)}, bf16[256,512]{1,0:T(8,128)(2,1)S(1)}, u32[]{:S(2)}, u32[]{:S(2)}) collective-permute-start(bf16[256,512]{1,0:T(8,128)(2,1)S(1)} %get-tuple-element.208), channel_id=1, source_target_pairs={{0,4},{4,0},{8,12},{12,8},{1,5},{5,1},{9,13},{13,9},{2,6},{6,2},{1... | collective-permute-start | bytes 786440 | tf_op jit(solution)/shard_map/ppermute | solution.py:100
  61.3 5.3 %copy-start.5 = (bf16[256,512]{1,0:T(8,128)(2,1)}, bf16[256,512]{1,0:T(8,128)(2,1)S(1)}, u32[]{:S(2)}) copy-start(bf16[256,512]{1,0:T(8,128)(2,1)S(1)} %get-tuple-element.202) | copy-start | bytes 786436
  61.3 11.2 %slice-start.7 = ((s8[31457280]{0:T(1024)(128)(4,1)}), s8[2097152]{0:T(1024)(128)(4,1)S(1)}, s32[]{:S(2)}) async-start(s8[31457280]{0:T(1024)(128)(4,1)} %bitcast.59), calls=%async_computation.7 | async-start | bytes 4194304
  61.4 13.3 %collective-permute-start.19 = (bf16[256,512]{1,0:T(8,128)(2,1)S(1)}, bf16[256,512]{1,0:T(8,128)(2,1)S(1)}, u32[]{:S(2)}, u32[]{:S(2)}) collective-permute-start(bf16[256,512]{1,0:T(8,128)(2,1)S(1)} %add_convert_fusion.6), channel_id=1, source_target_pairs={{0,1},{1,0},{2,3},{3,2},{4,8},{5,9},{6,10},{7,11},{8,4},{9,5},{10,... | collective-permute-start | bytes 786440 | tf_op jit(solution)/shard_map/ppermute | solution.py:103
  61.5 13.1 %collective-permute-start.20 = (bf16[256,512]{1,0:T(8,128)(2,1)S(1)}, bf16[256,512]{1,0:T(8,128)(2,1)S(1)}, u32[]{:S(2)}, u32[]{:S(2)}) collective-permute-start(bf16[256,512]{1,0:T(8,128)(2,1)S(1)} %get-tuple-element.202), channel_id=1, source_target_pairs={{0,4},{4,0},{8,12},{12,8},{1,5},{5,1},{9,13},{13,9},{2,6},{6,2},{1... | collective-permute-start | bytes 786440 | tf_op jit(solution)/shard_map/ppermute | solution.py:100
  66.4 15.0 %collective-permute-start.21 = (bf16[256,512]{1,0:T(8,128)(2,1)S(1)}, bf16[256,512]{1,0:T(8,128)(2,1)}, u32[]{:S(2)}, u32[]{:S(2)}) collective-permute-start(bf16[256,512]{1,0:T(8,128)(2,1)S(1)} %add_convert_fusion.5), channel_id=1, source_target_pairs={{0,1},{1,0},{2,3},{3,2},{4,8},{5,9},{6,10},{7,11},{8,4},{9,5},{10,... | collective-permute-start | bytes 786440 | tf_op jit(solution)/shard_map/ppermute | solution.py:103
  67.9 4.2 %copy-start.3 = (bf16[6144,128]{1,0:T(8,128)(2,1)S(1)}, bf16[6144,128]{1,0:T(8,128)(2,1)}, u32[]{:S(2)}) copy-start(bf16[6144,128]{1,0:T(8,128)(2,1)} %param.20) | copy-start | bytes 4718596
  68.0 13.1 %collective-permute-start.22 = (bf16[256,512]{1,0:T(8,128)(2,1)S(1)}, bf16[256,512]{1,0:T(8,128)(2,1)S(1)}, u32[]{:S(2)}, u32[]{:S(2)}) collective-permute-start(bf16[256,512]{1,0:T(8,128)(2,1)S(1)} %get-tuple-element.196), channel_id=1, source_target_pairs={{0,4},{4,0},{8,12},{12,8},{1,5},{5,1},{9,13},{13,9},{2,6},{6,2},{1... | collective-permute-start | bytes 786440 | tf_op jit(solution)/shard_map/ppermute | solution.py:100
  74.6 13.8 %collective-permute-start.23 = (bf16[256,512]{1,0:T(8,128)(2,1)S(1)}, bf16[256,512]{1,0:T(8,128)(2,1)}, u32[]{:S(2)}, u32[]{:S(2)}) collective-permute-start(bf16[256,512]{1,0:T(8,128)(2,1)S(1)} %add_convert_fusion.4), channel_id=1, source_target_pairs={{0,1},{1,0},{2,3},{3,2},{4,8},{5,9},{6,10},{7,11},{8,4},{9,5},{10,... | collective-permute-start | bytes 786440 | tf_op jit(solution)/shard_map/ppermute | solution.py:103
  77.0 11.3 %collective-permute-start.25 = (bf16[256,512]{1,0:T(8,128)(2,1)}, bf16[256,512]{1,0:T(8,128)(2,1)S(1)}, u32[]{:S(2)}, u32[]{:S(2)}) collective-permute-start(bf16[256,512]{1,0:T(8,128)(2,1)} %get-tuple-element.184), channel_id=1, source_target_pairs={{0,4},{4,0},{8,12},{12,8},{1,5},{5,1},{9,13},{13,9},{2,6},{6,2},{1... | collective-permute-start | bytes 786440 | tf_op jit(solution)/shard_map/ppermute | solution.py:100
  81.3 12.9 %collective-permute-start.26 = (bf16[256,512]{1,0:T(8,128)(2,1)S(1)}, bf16[256,512]{1,0:T(8,128)(2,1)}, u32[]{:S(2)}, u32[]{:S(2)}) collective-permute-start(bf16[256,512]{1,0:T(8,128)(2,1)S(1)} %add_convert_fusion.3), channel_id=1, source_target_pairs={{0,1},{1,0},{2,3},{3,2},{4,8},{5,9},{6,10},{7,11},{8,4},{9,5},{10,... | collective-permute-start | bytes 786440 | tf_op jit(solution)/shard_map/ppermute | solution.py:103
  84.5 19.1 %collective-permute-start.27 = (bf16[256,512]{1,0:T(8,128)(2,1)}, bf16[256,512]{1,0:T(8,128)(2,1)}, u32[]{:S(2)}, u32[]{:S(2)}) collective-permute-start(bf16[256,512]{1,0:T(8,128)(2,1)} %pad_maximum_fusion.14), channel_id=1, source_target_pairs={{0,4},{4,0},{8,12},{12,8},{1,5},{5,1},{9,13},{13,9},{2,6},{6,2},{1... | collective-permute-start | bytes 786440 | tf_op jit(solution)/shard_map/ppermute | solution.py:100
  85.9 1.0 copy-start.6
  88.2 1.3 %copy-start.9 = (bf16[128,128]{1,0:T(8,128)(2,1)S(1)}, bf16[128,128]{1,0:T(8,128)(2,1)}, u32[]{:S(2)}) copy-start(bf16[128,128]{1,0:T(8,128)(2,1)} %copy-done.8) | copy-start | bytes 98308
  88.3 9.8 %collective-permute-start.28 = (bf16[256,512]{1,0:T(8,128)(2,1)S(1)}, bf16[256,512]{1,0:T(8,128)(2,1)}, u32[]{:S(2)}, u32[]{:S(2)}) collective-permute-start(bf16[256,512]{1,0:T(8,128)(2,1)S(1)} %add_convert_fusion.2), channel_id=1, source_target_pairs={{0,1},{1,0},{2,3},{3,2},{4,8},{5,9},{6,10},{7,11},{8,4},{9,5},{10,... | collective-permute-start | bytes 786440 | tf_op jit(solution)/shard_map/ppermute | solution.py:103
  90.9 14.9 %collective-permute-start.24 = (bf16[256,512]{1,0:T(8,128)(2,1)S(1)}, bf16[256,512]{1,0:T(8,128)(2,1)S(1)}, u32[]{:S(2)}, u32[]{:S(2)}) collective-permute-start(bf16[256,512]{1,0:T(8,128)(2,1)S(1)} %pad_maximum_fusion.16), channel_id=1, source_target_pairs={{0,4},{4,0},{8,12},{12,8},{1,5},{5,1},{9,13},{13,9},{2,6},{6,2},{1... | collective-permute-start | bytes 786440 | tf_op jit(solution)/shard_map/ppermute | solution.py:100
  96.9 12.6 %collective-permute-start.29 = (bf16[256,512]{1,0:T(8,128)(2,1)S(1)}, bf16[256,512]{1,0:T(8,128)(2,1)S(1)}, u32[]{:S(2)}, u32[]{:S(2)}) collective-permute-start(bf16[256,512]{1,0:T(8,128)(2,1)S(1)} %pad_maximum_fusion.21), channel_id=1, source_target_pairs={{0,4},{4,0},{8,12},{12,8},{1,5},{5,1},{9,13},{13,9},{2,6},{6,2},{1... | collective-permute-start | bytes 786440 | tf_op jit(solution)/shard_map/ppermute | solution.py:100
  100.6 10.3 %collective-permute-start.30 = (bf16[256,512]{1,0:T(8,128)(2,1)S(1)}, bf16[256,512]{1,0:T(8,128)(2,1)S(1)}, u32[]{:S(2)}, u32[]{:S(2)}) collective-permute-start(bf16[256,512]{1,0:T(8,128)(2,1)S(1)} %pad_maximum_fusion.23), channel_id=1, source_target_pairs={{0,4},{4,0},{8,12},{12,8},{1,5},{5,1},{9,13},{13,9},{2,6},{6,2},{1... | collective-permute-start | bytes 786440 | tf_op jit(solution)/shard_map/ppermute | solution.py:100
  105.9 1.7 %collective-permute-start.31 = (bf16[64,2688]{1,0:T(8,128)(2,1)S(1)}, bf16[64,2688]{1,0:T(8,128)(2,1)S(1)}, u32[]{:S(2)}, u32[]{:S(2)}) collective-permute-start(bf16[64,2688]{1,0:T(8,128)(2,1)S(1)} %fusion.61), channel_id=1, source_target_pairs={{0,1},{1,0},{2,3},{3,2},{4,5},{5,4},{6,7},{7,6},{8,9},{9,8},{10,11... | collective-permute-start | bytes 1032200 | tf_op jit(solution)/shard_map/ppermute | solution.py:97
  107.7 10.2 %collective-permute-start.32 = (bf16[64,2688]{1,0:T(8,128)(2,1)S(1)}, bf16[64,2688]{1,0:T(8,128)(2,1)S(1)}, u32[]{:S(2)}, u32[]{:S(2)}) collective-permute-start(bf16[64,2688]{1,0:T(8,128)(2,1)S(1)} %fusion.59), channel_id=1, source_target_pairs={{0,2},{1,3},{2,0},{3,1},{4,6},{5,7},{6,4},{7,5},{8,10},{9,11},{10,... | collective-permute-start | bytes 1032200 | tf_op jit(solution)/shard_map/ppermute | solution.py:97
  120.4 1.9 %copy-start.11 = (f32[2560]{0:T(1024)S(1)}, f32[2560]{0:T(1024)}, u32[]{:S(2)}) copy-start(f32[2560]{0:T(1024)} %param.19) | copy-start | bytes 30724
  120.4 1.7 %collective-permute-start.33 = (bf16[64,2688]{1,0:T(8,128)(2,1)S(1)}, bf16[64,2688]{1,0:T(8,128)(2,1)S(1)}, u32[]{:S(2)}, u32[]{:S(2)}) collective-permute-start(bf16[64,2688]{1,0:T(8,128)(2,1)S(1)} %fusion.60), channel_id=1, source_target_pairs={{0,1},{1,0},{2,3},{3,2},{4,5},{5,4},{6,7},{7,6},{8,9},{9,8},{10,11... | collective-permute-start | bytes 1032200 | tf_op jit(solution)/shard_map/ppermute | solution.py:97

commit v14 on v13

--- a/solution.py
+++ b/solution.py
@@ -155,6 +155,12 @@
             loads[block] = load_part(first_weight, part, last)
             last = loads[block]
 
+        def load_second(pair):
+            nonlocal last
+            part = (pl.ds(pair * 2 * wide, 2 * wide), pl.ds(0, second_weight.shape[1]))
+            second_loads[pair] = load_part(second_weight, part, last)
+            last = second_loads[pair]
+
         def multiply(x, block):
             nonlocal last
             value = dot(tie(x, last), loads[block]).astype(BF16)
@@ -189,7 +195,8 @@
             states = tie(states, last)
             part = slice(block * wide, (block + 1) * wide)
             low = dot(states, second_down_maps[part])
-            value = dot(states, second_weight[part])
+            start = block % 2 * wide
+            value = dot(states, second_loads[block // 2][start : start + wide])
             if name in outputs:
                 value, low = outputs[name][0] + value, outputs[name][1] + low
             value = lax.optimization_barrier(value)
@@ -201,7 +208,7 @@
             return joined[:rows], joined[rows:].astype(BF16)
 
         far = col_swap(tokens, 2)
-        loads, outputs = {}, {}
+        loads, second_loads, outputs = {}, {}, {}
         last, is_end, mine = lax.optimization_barrier((jobs, is_end, mine))
         load(0)
         gathered_near = jnp.concatenate([tokens, tie(col_swap(tokens, 1), last)], axis=0)
@@ -224,6 +231,11 @@
                 first_half(early + t, gathered_far)
                 if early + t < LAG:
                     send(early + t, partials[early + t])
+            unit = t - LAG
+            if unit == 3 * early - 1:
+                second("far", unfold(state(unit)), block_of(unit))
+                ours, theirs = core_parts("far")
+                come = col_swap(theirs, 1)
             k = t - 1
             if 0 <= k < UNITS:
                 summed = tie(sums[k], last).astype(F32) + crosses[k].astype(F32)
@@ -245,20 +257,21 @@
             if t == 1:
                 whole = tie((gathered_near, gathered_far), last)
                 gathered = jnp.concatenate(whole, axis=0)
+            if t >= LAG and (t - LAG) % 2 == 0 and t - LAG < 2 * early:
+                load_second((t - LAG) // 2)
             if 1 <= t <= early:
                 load(early + t - 1)
                 first_late(2 * early + t - 1, gathered)
             if early <= unit < 2 * early:
                 second("near", unfold(state(unit - early)), unit - early)
                 second("far", unfold(state(unit)), unit - early)
+            elif unit == 3 * early - 1:
+                across = (ours + come.astype(F32)).astype(BF16)
+                across = col_swap(across, 2)
             elif unit >= 2 * early:
                 if unit == UNITS - 1:
                     last = across
                 second("near" if is_near(unit) else "far", unfold(state(unit)), block_of(unit))
-                if unit == 3 * early - 1:
-                    ours, theirs = core_parts("far")
-                    across = (ours + col_swap(theirs, 1).astype(F32)).astype(BF16)
-                    across = col_swap(across, 2)
         ours, theirs = core_parts("near")
         come = col_swap(theirs, 1)
         return ours + come.astype(F32) + across.astype(F32), mask

time: 124 us -> 122 us (0.984)
  Pallas kernels: 15.2 us -> 27 us
  other arithmetic: 10.1 us -> 3.81 us
  matrix products: 34.5 us -> 29.5 us
  waiting for transfers between devices: 14.1 us -> 11.8 us
  starting transfers between devices: 43.9 us -> 42.5 us
    pallas_call x6 -> x9, Pallas kernels: 15.2 us -> 27 us  [load_part(): pl.pallas_call(functools.partial(load_kernel, part=part), in_specs=[pl.Bl...]
    ppermute x6, waiting for transfers between devices: 11.1 us -> 3.65 us  [col_swap(): return lax.ppermute(value, 'col', [(i, i ^ flip) for i in range(n_col)])]
    ppermute x16, waiting for transfers between devices: 2.93 us -> 8.15 us  [end_swap(): return lax.ppermute(value, 'row', [(i, i ^ 1) for i in range(n_row)])]
    dot_general x48, matrix products: 34.5 us -> 29.5 us  [dot(): return jnp.dot(left, right, preferred_element_type=F32)]
    add x12, other arithmetic: 4.65 us -> 0.83 us  [pipeline(): summed = tie(sums[k], last).astype(F32) + crosses[k].astype(F32)]
    ppermute x16, starting transfers between devices: 38.3 us -> 35.9 us  [end_swap(): return lax.ppermute(value, 'row', [(i, i ^ 1) for i in range(n_row)])]
    concatenate x14, other arithmetic: 2.01 us -> 0.59 us  [halves(): return jnp.concatenate([value[:, :width], value[:, width:]], axis=0)]
    unnamed x47 -> x25, local copies, waits for them, and re-layouts: 2.15 us -> 3.42 us
  transfers between devices with their start and end apart: 34 -> 34, of which waited for: 6 -> 6; matrix products, arithmetic and copies ran while one was open for 35% -> 26% of each run, Pallas kernels for 12% -> 22%
where the time goes in v14:
time: 122 us; the launch traced here: 121 us
  starting transfers between devices  42.5 us (35%)
  matrix products  29.5 us (24%)
  Pallas kernels  27 us (22%)
  waiting for transfers between devices  11.8 us (10%)
  local copies, waits for them, and re-layouts  4.7 us (4%)
  other arithmetic  3.81 us (3%)
  between operations  1.71 us (1%)
    ppermute x16, starting transfers between devices, end_swap(): return lax.ppermute(value, 'row', [(i, i ^ 1) for i in range(n_row)])  35.9 us
    dot_general x48, matrix products, dot(): return jnp.dot(left, right, preferred_element_type=F32)  29.5 us
    pallas_call x9, Pallas kernels, load_part(): pl.pallas_call(functools.partial(load_kernel, part=part), in_specs=[pl.Bl...  27 us
    ppermute x16, waiting for transfers between devices, end_swap(): return lax.ppermute(value, 'row', [(i, i ^ 1) for i in range(n_row)])  8.15 us
    ppermute x6, starting transfers between devices, col_swap(): return lax.ppermute(value, 'col', [(i, i ^ flip) for i in range(n_col)])  3.77 us
    ppermute x6, waiting for transfers between devices, col_swap(): return lax.ppermute(value, 'col', [(i, i ^ flip) for i in range(n_col)])  3.65 us
    unnamed x25, local copies, waits for them, and re-layouts  3.42 us
    ppermute x12, starting transfers between devices, cross(): return lax.ppermute(value, ('group', 'row', 'col'), cross_pairs)  2.8 us
  transfers between devices with their start and end apart: 34, of which 6 were waited for; matrix products, arithmetic and copies ran while one was open for 26% of the time, Pallas kernels for 22%

profile of v14, /device:TPU:0, one launch (start us, length us, event | category | flops | bytes accessed | tf_op | source)
XLA Modules:
  0.0 121.1 jit_solution(14395107705561072203)
XLA Ops:
  0.0 2.9 %collective-permute-start = (bf16[64,2560]{1,0:T(8,128)(2,1)}, bf16[64,2560]{1,0:T(8,128)(2,1)S(1)}, u32[]{:S(2)}, u32[]{:S(2)}) collective-permute-start(bf16[64,2560]{1,0:T(8,128)(2,1)} %param.11), channel_id=1, source_target_pairs={{0,2},{1,3},{2,0},{3,1},{4,6},{5,7},{6,4},{7,5},{8,10},{9,11},{10,... | collective-permute-start | bytes 983048 | tf_op jit(solution)/shard_map/ppermute | solution.py:97
  3.0 0.7 copy-done.1
  3.6 2.6 %shard_map.109 = bf16[2560,1024]{1,0:T(8,128)(2,1)S(1)} custom-call(bf16[2560,6144]{1,0:T(8,128)(2,1)} %w_hbm.14, s32[4]{0:T(128)S(1)} %copy-done.1), custom_call_target="tpu_custom_call" | custom-call | bytes 1000 | tf_op jit(solution)/shard_map/pallas_call | solution.py:51
  6.7 0.8 convolution_convert_fusion.8
  7.6 1.6 %collective-permute-start.3 = (bf16[288,512]{1,0:T(8,128)(2,1)S(1)}, bf16[288,512]{1,0:T(8,128)(2,1)S(1)}, u32[]{:S(2)}, u32[]{:S(2)}) collective-permute-start(bf16[288,512]{1,0:T(8,128)(2,1)S(1)} %maximum_maximum_fusion.after_ref), channel_id=1, source_target_pairs={{0,4},{4,0},{8,12},{12,8},{1,5},{5,1},{9,13},{13,9},{2,6},{6,2},{1... | collective-permute-start | bytes 884744 | tf_op jit(solution)/shard_map/ppermute | solution.py:100
  9.3 2.5 %shard_map.110 = bf16[2560,1024]{1,0:T(8,128)(2,1)S(1)} custom-call(bf16[2560,6144]{1,0:T(8,128)(2,1)} %w_hbm.14, bf16[288,512]{1,0:T(8,128)(2,1)S(1)} %maximum_maximum_fusion.after_ref), custom_call_target="tpu_custom_call" | custom-call | bytes 1000 | tf_op jit(solution)/shard_map/pallas_call | solution.py:51
  11.8 0.8 convolution_convert_fusion.7
  12.7 0.5 collective-permute-start.4
  13.2 2.5 %shard_map.111 = bf16[2560,1024]{1,0:T(8,128)(2,1)S(1)} custom-call(bf16[2560,6144]{1,0:T(8,128)(2,1)} %w_hbm.14, bf16[256,512]{1,0:T(8,128)(2,1)S(1)} %pad_maximum_fusion.2.after_ref), custom_call_target="tpu_custom_call" | custom-call | bytes 1000 | tf_op jit(solution)/shard_map/pallas_call | solution.py:51
  15.7 0.9 convolution_convert_fusion.6
  16.7 1.6 %collective-permute-start.7 = (bf16[256,512]{1,0:T(8,128)(2,1)S(1)}, bf16[256,512]{1,0:T(8,128)(2,1)S(1)}, u32[]{:S(2)}, u32[]{:S(2)}) collective-permute-start(bf16[256,512]{1,0:T(8,128)(2,1)S(1)} %pad_maximum_fusion.3), channel_id=1, source_target_pairs={{0,4},{4,0},{8,12},{12,8},{1,5},{5,1},{9,13},{13,9},{2,6},{6,2},{1... | collective-permute-start | bytes 786440 | tf_op jit(solution)/shard_map/ppermute | solution.py:100
  18.9 0.6 collective-permute-start.5
  19.5 0.9 collective-permute-done.1
  20.7 0.9 convolution_convert_fusion.5
  21.7 1.4 %collective-permute-done.4 = bf16[256,512]{1,0:T(8,128)(2,1)S(1)} collective-permute-done((bf16[256,512]{1,0:T(8,128)(2,1)S(1)}, bf16[256,512]{1,0:T(8,128)(2,1)S(1)}, u32[]{:S(2)}, u32[]{:S(2)}) %collective-permute-start.4) | collective-permute-done | bytes 262176 | tf_op jit(solution)/shard_map/ppermute | solution.py:100
  23.3 3.1 %collective-permute-start.9 = (bf16[288,512]{1,0:T(8,128)(2,1)S(1)}, bf16[288,512]{1,0:T(8,128)(2,1)S(1)}, u32[]{:S(2)}, u32[]{:S(2)}) collective-permute-start(bf16[288,512]{1,0:T(8,128)(2,1)S(1)} %maximum_maximum_fusion.1), channel_id=1, source_target_pairs={{0,4},{4,0},{8,12},{12,8},{1,5},{5,1},{9,13},{13,9},{2,6},{6,2},{1... | collective-permute-start | bytes 884744 | tf_op jit(solution)/shard_map/ppermute | solution.py:100
  26.4 0.9 convolution_convert_fusion.4
  27.6 1.2 copy-done.9
  29.2 1.5 %collective-permute-start.6 = (bf16[256,512]{1,0:T(8,128)(2,1)S(1)}, bf16[256,512]{1,0:T(8,128)(2,1)S(1)}, u32[]{:S(2)}, u32[]{:S(2)}) collective-permute-start(bf16[256,512]{1,0:T(8,128)(2,1)S(1)} %maximum_select_fusion.after_ref), channel_id=1, source_target_pairs={{0,4},{4,0},{8,12},{12,8},{1,5},{5,1},{9,13},{13,9},{2,6},{6,2},{1... | collective-permute-start | bytes 786440 | tf_op jit(solution)/shard_map/ppermute | solution.py:100
  30.7 2.5 %shard_map.112 = bf16[2560,1024]{1,0:T(8,128)(2,1)S(1)} custom-call(bf16[2560,6144]{1,0:T(8,128)(2,1)} %w_hbm.14, bf16[256,512]{1,0:T(8,128)(2,1)S(1)} %maximum_select_fusion.after_ref), custom_call_target="tpu_custom_call" | custom-call | bytes 1000 | tf_op jit(solution)/shard_map/pallas_call | solution.py:51
  33.3 1.6 %convolution_convert_fusion.2 = bf16[256,1024]{1,0:T(8,128)(2,1)S(1)} fusion(bf16[256,2560]{1,0:T(8,128)(2,1)S(1)} %constant_dynamic-update-slice_fusion.4, bf16[2560,1024]{1,0:T(8,128)(2,1)S(1)} %shard_map.112), kind=kOutput, calls=%fused_computation.40 | convolution fusion | flops 1342439424 | bytes 7077888 | tf_op jit(solution)/shard_map/dot_general | solution.py:36
  35.1 0.9 convolution_convert_fusion.3
  36.7 2.0 %collective-permute-start.12 = (bf16[256,512]{1,0:T(8,128)(2,1)S(1)}, bf16[256,512]{1,0:T(8,128)(2,1)S(1)}, u32[]{:S(2)}, u32[]{:S(2)}) collective-permute-start(bf16[256,512]{1,0:T(8,128)(2,1)S(1)} %maximum_select_fusion.1.after_ref), channel_id=1, source_target_pairs={{0,4},{4,0},{8,12},{12,8},{1,5},{5,1},{9,13},{13,9},{2,6},{6,2},{1... | collective-permute-start | bytes 786440 | tf_op jit(solution)/shard_map/ppermute | solution.py:100
  38.7 2.5 %shard_map.113 = bf16[2560,1024]{1,0:T(8,128)(2,1)S(1)} custom-call(bf16[2560,6144]{1,0:T(8,128)(2,1)} %w_hbm.14, bf16[256,512]{1,0:T(8,128)(2,1)S(1)} %maximum_select_fusion.1.after_ref), custom_call_target="tpu_custom_call" | custom-call | bytes 1000 | tf_op jit(solution)/shard_map/pallas_call | solution.py:51
  41.2 1.6 %convolution_convert_fusion.1 = bf16[256,1024]{1,0:T(8,128)(2,1)S(1)} fusion(bf16[256,2560]{1,0:T(8,128)(2,1)S(1)} %constant_dynamic-update-slice_fusion.4, bf16[2560,1024]{1,0:T(8,128)(2,1)S(1)} %shard_map.113), kind=kOutput, calls=%fused_computation.39 | convolution fusion | flops 1342439424 | bytes 7077888 | tf_op jit(solution)/shard_map/dot_general | solution.py:36
  43.7 2.0 %collective-permute-start.14 = (bf16[256,512]{1,0:T(8,128)(2,1)S(1)}, bf16[256,512]{1,0:T(8,128)(2,1)S(1)}, u32[]{:S(2)}, u32[]{:S(2)}) collective-permute-start(bf16[256,512]{1,0:T(8,128)(2,1)S(1)} %get-tuple-element.222.after_ref), channel_id=1, source_target_pairs={{0,4},{4,0},{8,12},{12,8},{1,5},{5,1},{9,13},{13,9},{2,6},{6,2},{1... | collective-permute-start | bytes 786440 | tf_op jit(solution)/shard_map/ppermute | solution.py:100
  45.8 2.5 %shard_map.114 = bf16[2560,1024]{1,0:T(8,128)(2,1)S(1)} custom-call(bf16[2560,6144]{1,0:T(8,128)(2,1)} %w_hbm.14, bf16[256,512]{1,0:T(8,128)(2,1)S(1)} %get-tuple-element.222.after_ref), custom_call_target="tpu_custom_call" | custom-call | bytes 1000 | tf_op jit(solution)/shard_map/pallas_call | solution.py:51
  48.3 1.8 %convolution_convert_fusion = bf16[256,1024]{1,0:T(8,128)(2,1)S(1)} fusion(bf16[256,2560]{1,0:T(8,128)(2,1)S(1)} %constant_dynamic-update-slice_fusion.4, bf16[2560,1024]{1,0:T(8,128)(2,1)S(1)} %shard_map.114), kind=kOutput, calls=%fused_computation.38 | convolution fusion | flops 1342439424 | bytes 7077888 | tf_op jit(solution)/shard_map/dot_general | solution.py:36
  50.9 2.3 %collective-permute-start.16 = (bf16[256,512]{1,0:T(8,128)(2,1)S(1)}, bf16[256,512]{1,0:T(8,128)(2,1)S(1)}, u32[]{:S(2)}, u32[]{:S(2)}) collective-permute-start(bf16[256,512]{1,0:T(8,128)(2,1)S(1)} %get-tuple-element.216.after_ref), channel_id=1, source_target_pairs={{0,4},{4,0},{8,12},{12,8},{1,5},{5,1},{9,13},{13,9},{2,6},{6,2},{1... | collective-permute-start | bytes 786440 | tf_op jit(solution)/shard_map/ppermute | solution.py:100
  53.2 4.0 %shard_map.115 = bf16[2048,2560]{1,0:T(8,128)(2,1)S(1)} custom-call(bf16[6144,2560]{1,0:T(8,128)(2,1)} %w_hbm.17, bf16[256,512]{1,0:T(8,128)(2,1)S(1)} %get-tuple-element.216.after_ref), custom_call_target="tpu_custom_call" | custom-call | bytes 1000 | tf_op jit(solution)/shard_map/pallas_call | solution.py:51
  58.0 0.6 collective-permute-start.17
  58.6 2.0 %collective-permute-start.18 = (bf16[256,512]{1,0:T(8,128)(2,1)S(1)}, bf16[256,512]{1,0:T(8,128)(2,1)S(1)}, u32[]{:S(2)}, u32[]{:S(2)}) collective-permute-start(bf16[256,512]{1,0:T(8,128)(2,1)S(1)} %get-tuple-element.208), channel_id=1, source_target_pairs={{0,4},{4,0},{8,12},{12,8},{1,5},{5,1},{9,13},{13,9},{2,6},{6,2},{1... | collective-permute-start | bytes 786440 | tf_op jit(solution)/shard_map/ppermute | solution.py:100
  61.2 6.2 %collective-permute-start.20 = (bf16[256,512]{1,0:T(8,128)(2,1)S(1)}, bf16[256,512]{1,0:T(8,128)(2,1)S(1)}, u32[]{:S(2)}, u32[]{:S(2)}) collective-permute-start(bf16[256,512]{1,0:T(8,128)(2,1)S(1)} %get-tuple-element.202.after_ref), channel_id=1, source_target_pairs={{0,4},{4,0},{8,12},{12,8},{1,5},{5,1},{9,13},{13,9},{2,6},{6,2},{1... | collective-permute-start | bytes 786440 | tf_op jit(solution)/shard_map/ppermute | solution.py:100
  67.3 4.0 %shard_map.116 = bf16[2048,2560]{1,0:T(8,128)(2,1)S(1)} custom-call(bf16[6144,2560]{1,0:T(8,128)(2,1)} %w_hbm.17, bf16[256,512]{1,0:T(8,128)(2,1)S(1)} %get-tuple-element.202.after_ref), custom_call_target="tpu_custom_call" | custom-call | bytes 1000 | tf_op jit(solution)/shard_map/pallas_call | solution.py:51
  71.6 0.6 collective-permute-start.21
  72.7 1.7 %collective-permute-start.22 = (bf16[256,512]{1,0:T(8,128)(2,1)S(1)}, bf16[256,512]{1,0:T(8,128)(2,1)S(1)}, u32[]{:S(2)}, u32[]{:S(2)}) collective-permute-start(bf16[256,512]{1,0:T(8,128)(2,1)S(1)} %get-tuple-element.196), channel_id=1, source_target_pairs={{0,4},{4,0},{8,12},{12,8},{1,5},{5,1},{9,13},{13,9},{2,6},{6,2},{1... | collective-permute-start | bytes 786440 | tf_op jit(solution)/shard_map/ppermute | solution.py:100
  74.5 0.9 fusion.22
  75.4 0.9 fusion.20
  76.3 0.5 copy-done.3
  77.9 3.2 %collective-permute-start.25 = (bf16[256,512]{1,0:T(8,128)(2,1)S(1)}, bf16[256,512]{1,0:T(8,128)(2,1)S(1)}, u32[]{:S(2)}, u32[]{:S(2)}) collective-permute-start(bf16[256,512]{1,0:T(8,128)(2,1)S(1)} %get-tuple-element.192.after_ref), channel_id=1, source_target_pairs={{0,4},{4,0},{8,12},{12,8},{1,5},{5,1},{9,13},{13,9},{2,6},{6,2},{1... | collective-permute-start | bytes 786440 | tf_op jit(solution)/shard_map/ppermute | solution.py:100
  81.1 4.0 %shard_map.117 = bf16[2048,2560]{1,0:T(8,128)(2,1)S(1)} custom-call(bf16[6144,2560]{1,0:T(8,128)(2,1)} %w_hbm.17, bf16[256,512]{1,0:T(8,128)(2,1)S(1)} %get-tuple-element.192.after_ref), custom_call_target="tpu_custom_call" | custom-call | bytes 1000 | tf_op jit(solution)/shard_map/pallas_call | solution.py:51
  85.3 0.9 fusion.24
  86.3 0.9 fusion.27
  87.8 0.8 copy-done.10
  89.0 0.9 collective-permute-start.30
  90.2 0.9 fusion.30
  91.2 0.9 fusion.33
  92.6 0.6 collective-permute-start.26
  93.7 2.7 %collective-permute-start.24 = (bf16[256,512]{1,0:T(8,128)(2,1)S(1)}, bf16[256,512]{1,0:T(8,128)(2,1)S(1)}, u32[]{:S(2)}, u32[]{:S(2)}) collective-permute-start(bf16[256,512]{1,0:T(8,128)(2,1)S(1)} %pad_maximum_fusion.16), channel_id=1, source_target_pairs={{0,4},{4,0},{8,12},{12,8},{1,5},{5,1},{9,13},{13,9},{2,6},{6,2},{1... | collective-permute-start | bytes 786440 | tf_op jit(solution)/shard_map/ppermute | solution.py:100
  96.5 0.9 fusion.39
  97.7 0.6 fusion.123
  98.4 2.9 %collective-permute-start.28 = (bf16[256,512]{1,0:T(8,128)(2,1)S(1)}, bf16[256,512]{1,0:T(8,128)(2,1)S(1)}, u32[]{:S(2)}, u32[]{:S(2)}) collective-permute-start(bf16[256,512]{1,0:T(8,128)(2,1)S(1)} %pad_maximum_fusion.19), channel_id=1, source_target_pairs={{0,4},{4,0},{8,12},{12,8},{1,5},{5,1},{9,13},{13,9},{2,6},{6,2},{1... | collective-permute-start | bytes 786440 | tf_op jit(solution)/shard_map/ppermute | solution.py:100
  101.4 0.9 fusion.45
  102.6 0.9 fusion.48
  104.4 1.6 %collective-permute-start.29 = (bf16[256,512]{1,0:T(8,128)(2,1)S(1)}, bf16[256,512]{1,0:T(8,128)(2,1)S(1)}, u32[]{:S(2)}, u32[]{:S(2)}) collective-permute-start(bf16[256,512]{1,0:T(8,128)(2,1)S(1)} %pad_maximum_fusion.17), channel_id=1, source_target_pairs={{0,4},{4,0},{8,12},{12,8},{1,5},{5,1},{9,13},{13,9},{2,6},{6,2},{1... | collective-permute-start | bytes 786440 | tf_op jit(solution)/shard_map/ppermute | solution.py:100
  106.2 0.6 collective-permute-start.32
  106.8 0.9 fusion.36
  107.9 1.5 %collective-permute-done.28 = bf16[256,512]{1,0:T(8,128)(2,1)S(1)} collective-permute-done((bf16[256,512]{1,0:T(8,128)(2,1)S(1)}, bf16[256,512]{1,0:T(8,128)(2,1)S(1)}, u32[]{:S(2)}, u32[]{:S(2)}) %collective-permute-start.28) | collective-permute-done | bytes 262176 | tf_op jit(solution)/shard_map/ppermute | solution.py:100
  109.4 5.2 %collective-permute-done.29 = bf16[256,512]{1,0:T(8,128)(2,1)S(1)} collective-permute-done((bf16[256,512]{1,0:T(8,128)(2,1)S(1)}, bf16[256,512]{1,0:T(8,128)(2,1)S(1)}, u32[]{:S(2)}, u32[]{:S(2)}) %collective-permute-start.29) | collective-permute-done | bytes 262176 | tf_op jit(solution)/shard_map/ppermute | solution.py:100
  114.6 1.1 collective-permute-done.32
  116.0 0.9 fusion.42
  117.3 0.9 fusion.51
  118.3 1.6 %collective-permute-done.33 = bf16[64,2688]{1,0:T(8,128)(2,1)S(1)} collective-permute-done((bf16[64,2688]{1,0:T(8,128)(2,1)S(1)}, bf16[64,2688]{1,0:T(8,128)(2,1)S(1)}, u32[]{:S(2)}, u32[]{:S(2)}) %collective-permute-start.33) | collective-permute-done | bytes 344096 | tf_op jit(solution)/shard_map/ppermute | solution.py:97
  120.1 1.0 fusion.63
  (217 shorter events, 13.2 us)
Async XLA Ops:
  0.0 120.1 %copy-start = (bf16[128,2560]{1,0:T(8,128)(2,1)S(1)}, bf16[128,2560]{1,0:T(8,128)(2,1)}, u32[]{:S(2)}) copy-start(bf16[128,2560]{1,0:T(8,128)(2,1)} %param.21) | copy-start | bytes 1966084
  0.0 18.7 %collective-permute-start = (bf16[64,2560]{1,0:T(8,128)(2,1)}, bf16[64,2560]{1,0:T(8,128)(2,1)S(1)}, u32[]{:S(2)}, u32[]{:S(2)}) collective-permute-start(bf16[64,2560]{1,0:T(8,128)(2,1)} %param.11), channel_id=1, source_target_pairs={{0,2},{1,3},{2,0},{3,1},{4,6},{5,7},{6,4},{7,5},{8,10},{9,11},{10,... | collective-permute-start | bytes 983048 | tf_op jit(solution)/shard_map/ppermute | solution.py:97
  2.9 3.3 %collective-permute-start.2 = (bf16[64,2560]{1,0:T(8,128)(2,1)}, bf16[64,2560]{1,0:T(8,128)(2,1)S(1)}, u32[]{:S(2)}, u32[]{:S(2)}) collective-permute-start(bf16[64,2560]{1,0:T(8,128)(2,1)} %param.11), channel_id=1, source_target_pairs={{0,1},{1,0},{2,3},{3,2},{4,5},{5,4},{6,7},{7,6},{8,9},{9,8},{10,11... | collective-permute-start | bytes 983048 | tf_op jit(solution)/shard_map/ppermute | solution.py:97
  2.9 0.7 copy-start.1
  3.6 2.6 %copy-start.5 = (bf16[64,2560]{1,0:T(8,128)(2,1)S(1)}, bf16[64,2560]{1,0:T(8,128)(2,1)}, u32[]{:S(2)}) copy-start(bf16[64,2560]{1,0:T(8,128)(2,1)} %param.11) | copy-start | bytes 983044
  3.6 2.8 %copy-start.4 = (bf16[2560,128]{1,0:T(8,128)(2,1)S(1)}, bf16[2560,128]{1,0:T(8,128)(2,1)}, u32[]{:S(2)}) copy-start(bf16[2560,128]{1,0:T(8,128)(2,1)} %param.16) | copy-start | bytes 1966084
  7.6 11.2 %collective-permute-start.3 = (bf16[288,512]{1,0:T(8,128)(2,1)S(1)}, bf16[288,512]{1,0:T(8,128)(2,1)S(1)}, u32[]{:S(2)}, u32[]{:S(2)}) collective-permute-start(bf16[288,512]{1,0:T(8,128)(2,1)S(1)} %maximum_maximum_fusion.after_ref), channel_id=1, source_target_pairs={{0,4},{4,0},{8,12},{12,8},{1,5},{5,1},{9,13},{13,9},{2,6},{6,2},{1... | collective-permute-start | bytes 884744 | tf_op jit(solution)/shard_map/ppermute | solution.py:100
  12.7 10.4 %collective-permute-start.4 = (bf16[256,512]{1,0:T(8,128)(2,1)S(1)}, bf16[256,512]{1,0:T(8,128)(2,1)S(1)}, u32[]{:S(2)}, u32[]{:S(2)}) collective-permute-start(bf16[256,512]{1,0:T(8,128)(2,1)S(1)} %pad_maximum_fusion.2.after_ref), channel_id=1, source_target_pairs={{0,4},{4,0},{8,12},{12,8},{1,5},{5,1},{9,13},{13,9},{2,6},{6,2},{1... | collective-permute-start | bytes 786440 | tf_op jit(solution)/shard_map/ppermute | solution.py:100
  15.7 2.6 %copy-start.2 = (s32[4]{0:T(128)S(1)}, s32[4]{0:T(128)}, u32[]{:S(2)}) copy-start(s32[4]{0:T(128)} %after_ref) | copy-start | bytes 52
  15.7 2.6 %copy-start.8 = (s32[256]{0:T(256)S(1)}, s32[256]{0:T(256)}, u32[]{:S(2)}) copy-start(s32[256]{0:T(256)} %param.12) | copy-start | bytes 3076
  16.6 2.2 %copy-start.6 = (f32[6144]{0:T(1024)S(1)}, f32[6144]{0:T(1024)}, u32[]{:S(2)}) copy-start(f32[6144]{0:T(1024)} %param.15) | copy-start | bytes 73732
  16.7 18.3 %collective-permute-start.7 = (bf16[256,512]{1,0:T(8,128)(2,1)S(1)}, bf16[256,512]{1,0:T(8,128)(2,1)S(1)}, u32[]{:S(2)}, u32[]{:S(2)}) collective-permute-start(bf16[256,512]{1,0:T(8,128)(2,1)S(1)} %pad_maximum_fusion.3), channel_id=1, source_target_pairs={{0,4},{4,0},{8,12},{12,8},{1,5},{5,1},{9,13},{13,9},{2,6},{6,2},{1... | collective-permute-start | bytes 786440 | tf_op jit(solution)/shard_map/ppermute | solution.py:100
  18.7 1.7 %collective-permute-start.1 = (bf16[64,2560]{1,0:T(8,128)(2,1)S(1)}, bf16[64,2560]{1,0:T(8,128)(2,1)S(1)}, u32[]{:S(2)}, u32[]{:S(2)}) collective-permute-start(bf16[64,2560]{1,0:T(8,128)(2,1)S(1)} %collective-permute-done), channel_id=1, source_target_pairs={{0,1},{1,0},{2,3},{3,2},{4,5},{5,4},{6,7},{7,6},{8,9},{9,8},{10,11... | collective-permute-start | bytes 983048 | tf_op jit(solution)/shard_map/ppermute | solution.py:97
  18.9 8.5 %collective-permute-start.5 = (bf16[288,512]{1,0:T(8,128)(2,1)S(1)}, bf16[288,512]{1,0:T(8,128)(2,1)S(1)}, u32[]{:S(2)}, u32[]{:S(2)}) collective-permute-start(bf16[288,512]{1,0:T(8,128)(2,1)S(1)} %add_convert_fusion.1), channel_id=1, source_target_pairs={{0,1},{1,0},{2,3},{3,2},{4,8},{5,9},{6,10},{7,11},{8,4},{9,5},{10,... | collective-permute-start | bytes 884744 | tf_op jit(solution)/shard_map/ppermute | solution.py:103
  23.2 12.9 %collective-permute-start.8 = (bf16[256,512]{1,0:T(8,128)(2,1)S(1)}, bf16[256,512]{1,0:T(8,128)(2,1)S(1)}, u32[]{:S(2)}, u32[]{:S(2)}) collective-permute-start(bf16[256,512]{1,0:T(8,128)(2,1)S(1)} %add_convert_fusion.11), channel_id=1, source_target_pairs={{0,1},{1,0},{2,3},{3,2},{4,8},{5,9},{6,10},{7,11},{8,4},{9,5},{10,... | collective-permute-start | bytes 786440 | tf_op jit(solution)/shard_map/ppermute | solution.py:103
  23.3 19.7 %collective-permute-start.9 = (bf16[288,512]{1,0:T(8,128)(2,1)S(1)}, bf16[288,512]{1,0:T(8,128)(2,1)S(1)}, u32[]{:S(2)}, u32[]{:S(2)}) collective-permute-start(bf16[288,512]{1,0:T(8,128)(2,1)S(1)} %maximum_maximum_fusion.1), channel_id=1, source_target_pairs={{0,4},{4,0},{8,12},{12,8},{1,5},{5,1},{9,13},{13,9},{2,6},{6,2},{1... | collective-permute-start | bytes 884744 | tf_op jit(solution)/shard_map/ppermute | solution.py:100
  27.4 1.4 %copy-start.9 = (bf16[128,6144]{1,0:T(8,128)(2,1)S(1)}, bf16[128,6144]{1,0:T(8,128)(2,1)}, u32[]{:S(2)}) copy-start(bf16[128,6144]{1,0:T(8,128)(2,1)} %param.17) | copy-start | bytes 4718596
  29.2 20.8 %collective-permute-start.6 = (bf16[256,512]{1,0:T(8,128)(2,1)S(1)}, bf16[256,512]{1,0:T(8,128)(2,1)S(1)}, u32[]{:S(2)}, u32[]{:S(2)}) collective-permute-start(bf16[256,512]{1,0:T(8,128)(2,1)S(1)} %maximum_select_fusion.after_ref), channel_id=1, source_target_pairs={{0,4},{4,0},{8,12},{12,8},{1,5},{5,1},{9,13},{13,9},{2,6},{6,2},{1... | collective-permute-start | bytes 786440 | tf_op jit(solution)/shard_map/ppermute | solution.py:100
  35.0 8.1 %collective-permute-start.10 = (bf16[256,512]{1,0:T(8,128)(2,1)S(1)}, bf16[256,512]{1,0:T(8,128)(2,1)S(1)}, u32[]{:S(2)}, u32[]{:S(2)}) collective-permute-start(bf16[256,512]{1,0:T(8,128)(2,1)S(1)} %add_convert_fusion.10), channel_id=1, source_target_pairs={{0,1},{1,0},{2,3},{3,2},{4,8},{5,9},{6,10},{7,11},{8,4},{9,5},{10,... | collective-permute-start | bytes 786440 | tf_op jit(solution)/shard_map/ppermute | solution.py:103
  36.7 20.5 %collective-permute-start.12 = (bf16[256,512]{1,0:T(8,128)(2,1)S(1)}, bf16[256,512]{1,0:T(8,128)(2,1)S(1)}, u32[]{:S(2)}, u32[]{:S(2)}) collective-permute-start(bf16[256,512]{1,0:T(8,128)(2,1)S(1)} %maximum_select_fusion.1.after_ref), channel_id=1, source_target_pairs={{0,4},{4,0},{8,12},{12,8},{1,5},{5,1},{9,13},{13,9},{2,6},{6,2},{1... | collective-permute-start | bytes 786440 | tf_op jit(solution)/shard_map/ppermute | solution.py:100
  43.0 7.3 %collective-permute-start.11 = (bf16[288,512]{1,0:T(8,128)(2,1)S(1)}, bf16[288,512]{1,0:T(8,128)(2,1)S(1)}, u32[]{:S(2)}, u32[]{:S(2)}) collective-permute-start(bf16[288,512]{1,0:T(8,128)(2,1)S(1)} %add_convert_fusion), channel_id=1, source_target_pairs={{0,1},{1,0},{2,3},{3,2},{4,8},{5,9},{6,10},{7,11},{8,4},{9,5},{10,... | collective-permute-start | bytes 884744 | tf_op jit(solution)/shard_map/ppermute | solution.py:103
  43.7 14.2 %collective-permute-start.14 = (bf16[256,512]{1,0:T(8,128)(2,1)S(1)}, bf16[256,512]{1,0:T(8,128)(2,1)S(1)}, u32[]{:S(2)}, u32[]{:S(2)}) collective-permute-start(bf16[256,512]{1,0:T(8,128)(2,1)S(1)} %get-tuple-element.222.after_ref), channel_id=1, source_target_pairs={{0,4},{4,0},{8,12},{12,8},{1,5},{5,1},{9,13},{13,9},{2,6},{6,2},{1... | collective-permute-start | bytes 786440 | tf_op jit(solution)/shard_map/ppermute | solution.py:100
  50.2 7.2 %collective-permute-start.13 = (bf16[256,512]{1,0:T(8,128)(2,1)S(1)}, bf16[256,512]{1,0:T(8,128)(2,1)S(1)}, u32[]{:S(2)}, u32[]{:S(2)}) collective-permute-start(bf16[256,512]{1,0:T(8,128)(2,1)S(1)} %add_convert_fusion.9), channel_id=1, source_target_pairs={{0,1},{1,0},{2,3},{3,2},{4,8},{5,9},{6,10},{7,11},{8,4},{9,5},{10,... | collective-permute-start | bytes 786440 | tf_op jit(solution)/shard_map/ppermute | solution.py:103
  50.9 20.4 %collective-permute-start.16 = (bf16[256,512]{1,0:T(8,128)(2,1)S(1)}, bf16[256,512]{1,0:T(8,128)(2,1)S(1)}, u32[]{:S(2)}, u32[]{:S(2)}) collective-permute-start(bf16[256,512]{1,0:T(8,128)(2,1)S(1)} %get-tuple-element.216.after_ref), channel_id=1, source_target_pairs={{0,4},{4,0},{8,12},{12,8},{1,5},{5,1},{9,13},{13,9},{2,6},{6,2},{1... | collective-permute-start | bytes 786440 | tf_op jit(solution)/shard_map/ppermute | solution.py:100
  57.3 3.3 %collective-permute-start.15 = (bf16[256,512]{1,0:T(8,128)(2,1)S(1)}, bf16[256,512]{1,0:T(8,128)(2,1)S(1)}, u32[]{:S(2)}, u32[]{:S(2)}) collective-permute-start(bf16[256,512]{1,0:T(8,128)(2,1)S(1)} %add_convert_fusion.8), channel_id=1, source_target_pairs={{0,1},{1,0},{2,3},{3,2},{4,8},{5,9},{6,10},{7,11},{8,4},{9,5},{10,... | collective-permute-start | bytes 786440 | tf_op jit(solution)/shard_map/ppermute | solution.py:103
  58.0 14.1 %collective-permute-start.17 = (bf16[256,512]{1,0:T(8,128)(2,1)S(1)}, bf16[256,512]{1,0:T(8,128)(2,1)S(1)}, u32[]{:S(2)}, u32[]{:S(2)}) collective-permute-start(bf16[256,512]{1,0:T(8,128)(2,1)S(1)} %add_convert_fusion.7), channel_id=1, source_target_pairs={{0,1},{1,0},{2,3},{3,2},{4,8},{5,9},{6,10},{7,11},{8,4},{9,5},{10,... | collective-permute-start | bytes 786440 | tf_op jit(solution)/shard_map/ppermute | solution.py:103
  58.6 12.9 %collective-permute-start.18 = (bf16[256,512]{1,0:T(8,128)(2,1)S(1)}, bf16[256,512]{1,0:T(8,128)(2,1)S(1)}, u32[]{:S(2)}, u32[]{:S(2)}) collective-permute-start(bf16[256,512]{1,0:T(8,128)(2,1)S(1)} %get-tuple-element.208), channel_id=1, source_target_pairs={{0,4},{4,0},{8,12},{12,8},{1,5},{5,1},{9,13},{13,9},{2,6},{6,2},{1... | collective-permute-start | bytes 786440 | tf_op jit(solution)/shard_map/ppermute | solution.py:100
  61.2 23.9 %collective-permute-start.20 = (bf16[256,512]{1,0:T(8,128)(2,1)S(1)}, bf16[256,512]{1,0:T(8,128)(2,1)S(1)}, u32[]{:S(2)}, u32[]{:S(2)}) collective-permute-start(bf16[256,512]{1,0:T(8,128)(2,1)S(1)} %get-tuple-element.202.after_ref), channel_id=1, source_target_pairs={{0,4},{4,0},{8,12},{12,8},{1,5},{5,1},{9,13},{13,9},{2,6},{6,2},{1... | collective-permute-start | bytes 786440 | tf_op jit(solution)/shard_map/ppermute | solution.py:100
  71.4 5.9 %collective-permute-start.19 = (bf16[256,512]{1,0:T(8,128)(2,1)S(1)}, bf16[256,512]{1,0:T(8,128)(2,1)S(1)}, u32[]{:S(2)}, u32[]{:S(2)}) collective-permute-start(bf16[256,512]{1,0:T(8,128)(2,1)S(1)} %add_convert_fusion.6), channel_id=1, source_target_pairs={{0,1},{1,0},{2,3},{3,2},{4,8},{5,9},{6,10},{7,11},{8,4},{9,5},{10,... | collective-permute-start | bytes 786440 | tf_op jit(solution)/shard_map/ppermute | solution.py:103
  71.6 16.1 %collective-permute-start.21 = (bf16[256,512]{1,0:T(8,128)(2,1)S(1)}, bf16[256,512]{1,0:T(8,128)(2,1)S(1)}, u32[]{:S(2)}, u32[]{:S(2)}) collective-permute-start(bf16[256,512]{1,0:T(8,128)(2,1)S(1)} %add_convert_fusion.5), channel_id=1, source_target_pairs={{0,1},{1,0},{2,3},{3,2},{4,8},{5,9},{6,10},{7,11},{8,4},{9,5},{10,... | collective-permute-start | bytes 786440 | tf_op jit(solution)/shard_map/ppermute | solution.py:103
  72.7 17.3 %collective-permute-start.22 = (bf16[256,512]{1,0:T(8,128)(2,1)S(1)}, bf16[256,512]{1,0:T(8,128)(2,1)S(1)}, u32[]{:S(2)}, u32[]{:S(2)}) collective-permute-start(bf16[256,512]{1,0:T(8,128)(2,1)S(1)} %get-tuple-element.196), channel_id=1, source_target_pairs={{0,4},{4,0},{8,12},{12,8},{1,5},{5,1},{9,13},{13,9},{2,6},{6,2},{1... | collective-permute-start | bytes 786440 | tf_op jit(solution)/shard_map/ppermute | solution.py:100
  75.4 1.4 %copy-start.3 = (bf16[6144,128]{1,0:T(8,128)(2,1)S(1)}, bf16[6144,128]{1,0:T(8,128)(2,1)}, u32[]{:S(2)}) copy-start(bf16[6144,128]{1,0:T(8,128)(2,1)} %param.20) | copy-start | bytes 4718596
  77.9 14.6 %collective-permute-start.25 = (bf16[256,512]{1,0:T(8,128)(2,1)S(1)}, bf16[256,512]{1,0:T(8,128)(2,1)S(1)}, u32[]{:S(2)}, u32[]{:S(2)}) collective-permute-start(bf16[256,512]{1,0:T(8,128)(2,1)S(1)} %get-tuple-element.192.after_ref), channel_id=1, source_target_pairs={{0,4},{4,0},{8,12},{12,8},{1,5},{5,1},{9,13},{13,9},{2,6},{6,2},{1... | collective-permute-start | bytes 786440 | tf_op jit(solution)/shard_map/ppermute | solution.py:100
  85.2 8.0 %collective-permute-start.23 = (bf16[256,512]{1,0:T(8,128)(2,1)S(1)}, bf16[256,512]{1,0:T(8,128)(2,1)S(1)}, u32[]{:S(2)}, u32[]{:S(2)}) collective-permute-start(bf16[256,512]{1,0:T(8,128)(2,1)S(1)} %add_convert_fusion.4), channel_id=1, source_target_pairs={{0,1},{1,0},{2,3},{3,2},{4,8},{5,9},{6,10},{7,11},{8,4},{9,5},{10,... | collective-permute-start | bytes 786440 | tf_op jit(solution)/shard_map/ppermute | solution.py:103
  87.2 1.4 %copy-start.10 = (bf16[128,6144]{1,0:T(8,128)(2,1)S(1)}, bf16[128,6144]{1,0:T(8,128)(2,1)}, u32[]{:S(2)}) copy-start(bf16[128,6144]{1,0:T(8,128)(2,1)} %param.17) | copy-start | bytes 4718596
  89.0 13.5 %collective-permute-start.30 = (bf16[256,512]{1,0:T(8,128)(2,1)S(1)}, bf16[256,512]{1,0:T(8,128)(2,1)S(1)}, u32[]{:S(2)}, u32[]{:S(2)}) collective-permute-start(bf16[256,512]{1,0:T(8,128)(2,1)S(1)} %pad_maximum_fusion.14), channel_id=1, source_target_pairs={{0,4},{4,0},{8,12},{12,8},{1,5},{5,1},{9,13},{13,9},{2,6},{6,2},{1... | collective-permute-start | bytes 786440 | tf_op jit(solution)/shard_map/ppermute | solution.py:100
  90.1 7.5 %collective-permute-start.27 = (bf16[256,512]{1,0:T(8,128)(2,1)S(1)}, bf16[256,512]{1,0:T(8,128)(2,1)S(1)}, u32[]{:S(2)}, u32[]{:S(2)}) collective-permute-start(bf16[256,512]{1,0:T(8,128)(2,1)S(1)} %add_convert_fusion.3), channel_id=1, source_target_pairs={{0,1},{1,0},{2,3},{3,2},{4,8},{5,9},{6,10},{7,11},{8,4},{9,5},{10,... | collective-permute-start | bytes 786440 | tf_op jit(solution)/shard_map/ppermute | solution.py:103
  92.6 11.3 %collective-permute-start.26 = (bf16[256,512]{1,0:T(8,128)(2,1)S(1)}, bf16[256,512]{1,0:T(8,128)(2,1)S(1)}, u32[]{:S(2)}, u32[]{:S(2)}) collective-permute-start(bf16[256,512]{1,0:T(8,128)(2,1)S(1)} %add_convert_fusion.2), channel_id=1, source_target_pairs={{0,1},{1,0},{2,3},{3,2},{4,8},{5,9},{6,10},{7,11},{8,4},{9,5},{10,... | collective-permute-start | bytes 786440 | tf_op jit(solution)/shard_map/ppermute | solution.py:103
  93.7 12.3 %collective-permute-start.24 = (bf16[256,512]{1,0:T(8,128)(2,1)S(1)}, bf16[256,512]{1,0:T(8,128)(2,1)S(1)}, u32[]{:S(2)}, u32[]{:S(2)}) collective-permute-start(bf16[256,512]{1,0:T(8,128)(2,1)S(1)} %pad_maximum_fusion.16), channel_id=1, source_target_pairs={{0,4},{4,0},{8,12},{12,8},{1,5},{5,1},{9,13},{13,9},{2,6},{6,2},{1... | collective-permute-start | bytes 786440 | tf_op jit(solution)/shard_map/ppermute | solution.py:100
  98.4 11.0 %collective-permute-start.28 = (bf16[256,512]{1,0:T(8,128)(2,1)S(1)}, bf16[256,512]{1,0:T(8,128)(2,1)S(1)}, u32[]{:S(2)}, u32[]{:S(2)}) collective-permute-start(bf16[256,512]{1,0:T(8,128)(2,1)S(1)} %pad_maximum_fusion.19), channel_id=1, source_target_pairs={{0,4},{4,0},{8,12},{12,8},{1,5},{5,1},{9,13},{13,9},{2,6},{6,2},{1... | collective-permute-start | bytes 786440 | tf_op jit(solution)/shard_map/ppermute | solution.py:100
  103.8 2.3 %collective-permute-start.31 = (bf16[64,2688]{1,0:T(8,128)(2,1)S(1)}, bf16[64,2688]{1,0:T(8,128)(2,1)S(1)}, u32[]{:S(2)}, u32[]{:S(2)}) collective-permute-start(bf16[64,2688]{1,0:T(8,128)(2,1)S(1)} %fusion.61), channel_id=1, source_target_pairs={{0,1},{1,0},{2,3},{3,2},{4,5},{5,4},{6,7},{7,6},{8,9},{9,8},{10,11... | collective-permute-start | bytes 1032200 | tf_op jit(solution)/shard_map/ppermute | solution.py:97
  104.4 10.2 %collective-permute-start.29 = (bf16[256,512]{1,0:T(8,128)(2,1)S(1)}, bf16[256,512]{1,0:T(8,128)(2,1)S(1)}, u32[]{:S(2)}, u32[]{:S(2)}) collective-permute-start(bf16[256,512]{1,0:T(8,128)(2,1)S(1)} %pad_maximum_fusion.17), channel_id=1, source_target_pairs={{0,4},{4,0},{8,12},{12,8},{1,5},{5,1},{9,13},{13,9},{2,6},{6,2},{1... | collective-permute-start | bytes 786440 | tf_op jit(solution)/shard_map/ppermute | solution.py:100
  106.2 9.6 %collective-permute-start.32 = (bf16[64,2688]{1,0:T(8,128)(2,1)S(1)}, bf16[64,2688]{1,0:T(8,128)(2,1)S(1)}, u32[]{:S(2)}, u32[]{:S(2)}) collective-permute-start(bf16[64,2688]{1,0:T(8,128)(2,1)S(1)} %fusion.59), channel_id=1, source_target_pairs={{0,2},{1,3},{2,0},{3,1},{4,6},{5,7},{6,4},{7,5},{8,10},{9,11},{10,... | collective-permute-start | bytes 1032200 | tf_op jit(solution)/shard_map/ppermute | solution.py:97
  118.2 1.8 %copy-start.7 = (f32[2560]{0:T(1024)S(1)}, f32[2560]{0:T(1024)}, u32[]{:S(2)}) copy-start(f32[2560]{0:T(1024)} %param.19) | copy-start | bytes 30724
  118.3 1.7 %collective-permute-start.33 = (bf16[64,2688]{1,0:T(8,128)(2,1)S(1)}, bf16[64,2688]{1,0:T(8,128)(2,1)S(1)}, u32[]{:S(2)}, u32[]{:S(2)}) collective-permute-start(bf16[64,2688]{1,0:T(8,128)(2,1)S(1)} %fusion.60), channel_id=1, source_target_pairs={{0,1},{1,0},{2,3},{3,2},{4,5},{5,4},{6,7},{7,6},{8,9},{9,8},{10,11... | collective-permute-start | bytes 1032200 | tf_op jit(solution)/shard_map/ppermute | solution.py:97

commit v15 on v14

--- a/solution.py
+++ b/solution.py
@@ -11,8 +11,8 @@
 ADAPTER_COUNT = 8
 JOBS = 4
 LANES = 128
-UNITS = 12
-LAG = 4
+UNITS = 8
+LAG = 3
 F32 = jnp.float32
 BF16 = jnp.bfloat16
 
@@ -155,11 +155,11 @@
             loads[block] = load_part(first_weight, part, last)
             last = loads[block]
 
-        def load_second(pair):
-            nonlocal last
-            part = (pl.ds(pair * 2 * wide, 2 * wide), pl.ds(0, second_weight.shape[1]))
-            second_loads[pair] = load_part(second_weight, part, last)
-            last = second_loads[pair]
+        def load_second(block):
+            nonlocal last
+            part = (pl.ds(block * wide, wide), pl.ds(0, second_weight.shape[1]))
+            second_loads[block] = load_part(second_weight, part, last)
+            last = second_loads[block]
 
         def multiply(x, block):
             nonlocal last
@@ -195,8 +195,7 @@
             states = tie(states, last)
             part = slice(block * wide, (block + 1) * wide)
             low = dot(states, second_down_maps[part])
-            start = block % 2 * wide
-            value = dot(states, second_loads[block // 2][start : start + wide])
+            value = dot(states, second_loads[block])
             if name in outputs:
                 value, low = outputs[name][0] + value, outputs[name][1] + low
             value = lax.optimization_barrier(value)
@@ -219,18 +218,19 @@
             send(unit, partials[unit])
         mask = mask_of(mine, last)
         first_bias = tie(first_bias, last)
+        def far_half(unit):
+            first_half(unit, gathered_far)
+            if unit < LAG:
+                send(unit, partials[unit])
+
+        gathered_far = jnp.concatenate([far, col_swap(far, 1)], axis=0)
+        far_half(early)
         for t in range(UNITS + LAG):
             if t < UNITS:
                 ours = tie(partials[t], last).astype(F32)
                 sums[t] = (ours + swaps[t].astype(F32)).astype(BF16)
                 last = sums[t]
                 crosses[t] = cross(sums[t])
-            if t == 0:
-                gathered_far = jnp.concatenate([far, col_swap(far, 1)], axis=0)
-            if t < early:
-                first_half(early + t, gathered_far)
-                if early + t < LAG:
-                    send(early + t, partials[early + t])
             unit = t - LAG
             if unit == 3 * early - 1:
                 second("far", unfold(state(unit)), block_of(unit))
@@ -253,12 +253,13 @@
                     value = jnp.where(is_end, partials[k + LAG], value)
                 last = value
                 send(k + LAG, value)
-            unit = t - LAG
+            if t + 1 < early:
+                far_half(early + t + 1)
             if t == 1:
                 whole = tie((gathered_near, gathered_far), last)
                 gathered = jnp.concatenate(whole, axis=0)
-            if t >= LAG and (t - LAG) % 2 == 0 and t - LAG < 2 * early:
-                load_second((t - LAG) // 2)
+            if LAG <= t < LAG + 2 * early:
+                load_second(t - LAG)
             if 1 <= t <= early:
                 load(early + t - 1)
                 first_late(2 * early + t - 1, gathered)

time: 122 us -> 118 us (0.967)
  waiting for transfers between devices: 11.8 us -> 23.8 us
  starting transfers between devices: 42.5 us -> 32.7 us
  matrix products: 29.5 us -> 26.1 us
  local copies, waits for them, and re-layouts: 4.7 us -> 3.44 us
    ppermute x16 -> x11, waiting for transfers between devices: 8.15 us -> 20.7 us  [end_swap(): return lax.ppermute(value, 'row', [(i, i ^ 1) for i in range(n_row)])]
    ppermute x16 -> x11, starting transfers between devices: 35.9 us -> 28.1 us  [end_swap(): return lax.ppermute(value, 'row', [(i, i ^ 1) for i in range(n_row)])]
    dot_general x48 -> x33, matrix products: 29.5 us -> 26.1 us  [dot(): return jnp.dot(left, right, preferred_element_type=F32)]
    ppermute x12 -> x8, starting transfers between devices: 2.8 us -> 0.57 us  [cross(): return lax.ppermute(value, ('group', 'row', 'col'), cross_pairs)]
    unnamed x25 -> x23, local copies, waits for them, and re-layouts: 3.42 us -> 2.2 us
    pallas_call x9 -> x8, Pallas kernels: 27 us -> 26 us  [load_part(): pl.pallas_call(functools.partial(load_kernel, part=part), in_specs=[pl.Bl...]
  transfers between devices with their start and end apart: 34 -> 25, of which waited for: 6 -> 8; matrix products, arithmetic and copies ran while one was open for 26% -> 23% of each run, Pallas kernels for 22% -> 22%
where the time goes in v15:
time: 118 us; the launch traced here: 117 us
  starting transfers between devices  32.7 us (28%)
  matrix products  26.1 us (22%)
  Pallas kernels  26 us (22%)
  waiting for transfers between devices  23.8 us (20%)
  other arithmetic  3.82 us (3%)
  local copies, waits for them, and re-layouts  3.44 us (3%)
  between operations  1.25 us (1%)
    ppermute x11, starting transfers between devices, end_swap(): return lax.ppermute(value, 'row', [(i, i ^ 1) for i in range(n_row)])  28.1 us
    dot_general x33, matrix products, dot(): return jnp.dot(left, right, preferred_element_type=F32)  26.1 us
    pallas_call x8, Pallas kernels, load_part(): pl.pallas_call(functools.partial(load_kernel, part=part), in_specs=[pl.Bl...  26 us
    ppermute x11, waiting for transfers between devices, end_swap(): return lax.ppermute(value, 'row', [(i, i ^ 1) for i in range(n_row)])  20.7 us
    ppermute x6, starting transfers between devices, col_swap(): return lax.ppermute(value, 'col', [(i, i ^ flip) for i in range(n_col)])  3.97 us
    ppermute x6, waiting for transfers between devices, col_swap(): return lax.ppermute(value, 'col', [(i, i ^ flip) for i in range(n_col)])  3.03 us
  transfers between devices with their start and end apart: 25, of which 8 were waited for; matrix products, arithmetic and copies ran while one was open for 23% of the time, Pallas kernels for 22%

profile of v15, /device:TPU:0, one launch (start us, length us, event | category | flops | bytes accessed | tf_op | source)
XLA Modules:
  0.0 117.1 jit_solution(2048034596888775038)
XLA Ops:
  0.0 2.9 %collective-permute-start = (bf16[64,2560]{1,0:T(8,128)(2,1)}, bf16[64,2560]{1,0:T(8,128)(2,1)S(1)}, u32[]{:S(2)}, u32[]{:S(2)}) collective-permute-start(bf16[64,2560]{1,0:T(8,128)(2,1)} %param.11), channel_id=1, source_target_pairs={{0,2},{1,3},{2,0},{3,1},{4,6},{5,7},{6,4},{7,5},{8,10},{9,11},{10,... | collective-permute-start | bytes 983048 | tf_op jit(solution)/shard_map/ppermute | solution.py:97
  3.0 0.7 copy-done.1
  3.6 3.3 %shard_map.109 = bf16[2560,1536]{1,0:T(8,128)(2,1)S(1)} custom-call(bf16[2560,6144]{1,0:T(8,128)(2,1)} %w_hbm.11, s32[4]{0:T(128)S(1)} %copy-done.1), custom_call_target="tpu_custom_call" | custom-call | bytes 1000 | tf_op jit(solution)/shard_map/pallas_call | solution.py:51
  7.0 0.3 convolution_convert_fusion.7
  7.4 1.2 %convolution_convert_fusion.5 = bf16[128,1536]{1,0:T(8,128)(2,1)S(1)} fusion(bf16[128,2560]{1,0:T(8,128)(2,1)S(1)} %constant_dynamic-update-slice_fusion.2, bf16[2560,1536]{1,0:T(8,128)(2,1)S(1)} %shard_map.109), kind=kOutput, calls=%fused_computation.19 | convolution fusion | flops 1006829568 | bytes 8912896 | tf_op jit(solution)/shard_map/dot_general | solution.py:36
  8.7 1.6 %collective-permute-start.3 = (bf16[288,768]{1,0:T(8,128)(2,1)S(1)}, bf16[288,768]{1,0:T(8,128)(2,1)S(1)}, u32[]{:S(2)}, u32[]{:S(2)}) collective-permute-start(bf16[288,768]{1,0:T(8,128)(2,1)S(1)} %pad_maximum_fusion.2.after_ref), channel_id=1, source_target_pairs={{0,4},{4,0},{8,12},{12,8},{1,5},{5,1},{9,13},{13,9},{2,6},{6,2},{1... | collective-permute-start | bytes 1327112 | tf_op jit(solution)/shard_map/ppermute | solution.py:100
  10.3 3.2 %shard_map.110 = bf16[2560,1536]{1,0:T(8,128)(2,1)S(1)} custom-call(bf16[2560,6144]{1,0:T(8,128)(2,1)} %w_hbm.11, bf16[288,768]{1,0:T(8,128)(2,1)S(1)} %pad_maximum_fusion.2.after_ref), custom_call_target="tpu_custom_call" | custom-call | bytes 1000 | tf_op jit(solution)/shard_map/pallas_call | solution.py:51
  13.6 1.2 %convolution_convert_fusion.4 = bf16[128,1536]{1,0:T(8,128)(2,1)S(1)} fusion(bf16[128,2560]{1,0:T(8,128)(2,1)S(1)} %constant_dynamic-update-slice_fusion.2, bf16[2560,1536]{1,0:T(8,128)(2,1)S(1)} %shard_map.110), kind=kOutput, calls=%fused_computation.18 | convolution fusion | flops 1006829568 | bytes 8912896 | tf_op jit(solution)/shard_map/dot_general | solution.py:36
  14.9 0.5 collective-permute-start.4
  15.9 0.3 collective-permute-start.1
  16.2 1.4 %collective-permute-done.1 = bf16[64,2560]{1,0:T(8,128)(2,1)S(1)} collective-permute-done((bf16[64,2560]{1,0:T(8,128)(2,1)S(1)}, bf16[64,2560]{1,0:T(8,128)(2,1)S(1)}, u32[]{:S(2)}, u32[]{:S(2)}) %collective-permute-start.1) | collective-permute-done | bytes 327712 | tf_op jit(solution)/shard_map/ppermute | solution.py:97
  17.6 0.3 convolution_convert_fusion.6
  17.9 1.2 %convolution_convert_fusion.3 = bf16[128,1536]{1,0:T(8,128)(2,1)S(1)} fusion(bf16[128,2560]{1,0:T(8,128)(2,1)S(1)} %constant_dynamic-update-slice_fusion, bf16[2560,1536]{1,0:T(8,128)(2,1)S(1)} %shard_map.109), kind=kOutput, calls=%fused_computation.17 | convolution fusion | flops 1006829568 | bytes 8912896 | tf_op jit(solution)/shard_map/dot_general | solution.py:36
  19.2 1.6 %collective-permute-start.7 = (bf16[288,768]{1,0:T(8,128)(2,1)S(1)}, bf16[288,768]{1,0:T(8,128)(2,1)S(1)}, u32[]{:S(2)}, u32[]{:S(2)}) collective-permute-start(bf16[288,768]{1,0:T(8,128)(2,1)S(1)} %pad_maximum_fusion.3), channel_id=1, source_target_pairs={{0,4},{4,0},{8,12},{12,8},{1,5},{5,1},{9,13},{13,9},{2,6},{6,2},{1... | collective-permute-start | bytes 1327112 | tf_op jit(solution)/shard_map/ppermute | solution.py:100
  20.8 0.9 collective-permute-done.3
  21.9 1.2 %convolution_convert_fusion.2 = bf16[128,1536]{1,0:T(8,128)(2,1)S(1)} fusion(bf16[128,2560]{1,0:T(8,128)(2,1)S(1)} %constant_dynamic-update-slice_fusion, bf16[2560,1536]{1,0:T(8,128)(2,1)S(1)} %shard_map.110), kind=kOutput, calls=%fused_computation.16 | convolution fusion | flops 1006829568 | bytes 8912896 | tf_op jit(solution)/shard_map/dot_general | solution.py:36
  23.2 7.0 %collective-permute-done.4 = bf16[256,768]{1,0:T(8,128)(2,1)S(1)} collective-permute-done((bf16[256,768]{1,0:T(8,128)(2,1)S(1)}, bf16[256,768]{1,0:T(8,128)(2,1)S(1)}, u32[]{:S(2)}, u32[]{:S(2)}) %collective-permute-start.4) | collective-permute-done | bytes 393248 | tf_op jit(solution)/shard_map/ppermute | solution.py:100
  30.5 1.1 copy-done.9
  31.6 0.4 fusion.4
  32.2 4.5 %collective-permute-start.6 = (bf16[256,768]{1,0:T(8,128)(2,1)S(1)}, bf16[256,768]{1,0:T(8,128)(2,1)S(1)}, u32[]{:S(2)}, u32[]{:S(2)}) collective-permute-start(bf16[256,768]{1,0:T(8,128)(2,1)S(1)} %maximum_select_fusion.after_ref), channel_id=1, source_target_pairs={{0,4},{4,0},{8,12},{12,8},{1,5},{5,1},{9,13},{13,9},{2,6},{6,2},{1... | collective-permute-start | bytes 1179656 | tf_op jit(solution)/shard_map/ppermute | solution.py:100
  36.7 3.2 %shard_map.111 = bf16[2560,1536]{1,0:T(8,128)(2,1)S(1)} custom-call(bf16[2560,6144]{1,0:T(8,128)(2,1)} %w_hbm.11, bf16[256,768]{1,0:T(8,128)(2,1)S(1)} %maximum_select_fusion.after_ref), custom_call_target="tpu_custom_call" | custom-call | bytes 1000 | tf_op jit(solution)/shard_map/pallas_call | solution.py:51
  40.1 2.2 %convolution_convert_fusion.1 = bf16[256,1536]{1,0:T(8,128)(2,1)S(1)} fusion(bf16[256,2560]{1,0:T(8,128)(2,1)S(1)} %constant_dynamic-update-slice_fusion.4, bf16[2560,1536]{1,0:T(8,128)(2,1)S(1)} %shard_map.111), kind=kOutput, calls=%fused_computation.7 | convolution fusion | flops 2013659136 | bytes 9961472 | tf_op jit(solution)/shard_map/dot_general | solution.py:36
  42.7 0.4 fusion.9
  43.3 1.6 %collective-permute-start.10 = (bf16[256,768]{1,0:T(8,128)(2,1)S(1)}, bf16[256,768]{1,0:T(8,128)(2,1)S(1)}, u32[]{:S(2)}, u32[]{:S(2)}) collective-permute-start(bf16[256,768]{1,0:T(8,128)(2,1)S(1)} %get-tuple-element.158.after_ref), channel_id=1, source_target_pairs={{0,4},{4,0},{8,12},{12,8},{1,5},{5,1},{9,13},{13,9},{2,6},{6,2},{1... | collective-permute-start | bytes 1179656 | tf_op jit(solution)/shard_map/ppermute | solution.py:100
  44.9 3.2 %shard_map.112 = bf16[2560,1536]{1,0:T(8,128)(2,1)S(1)} custom-call(bf16[2560,6144]{1,0:T(8,128)(2,1)} %w_hbm.11, bf16[256,768]{1,0:T(8,128)(2,1)S(1)} %get-tuple-element.158.after_ref), custom_call_target="tpu_custom_call" | custom-call | bytes 1000 | tf_op jit(solution)/shard_map/pallas_call | solution.py:51
  48.2 2.2 %convolution_convert_fusion = bf16[256,1536]{1,0:T(8,128)(2,1)S(1)} fusion(bf16[256,2560]{1,0:T(8,128)(2,1)S(1)} %constant_dynamic-update-slice_fusion.4, bf16[2560,1536]{1,0:T(8,128)(2,1)S(1)} %shard_map.112), kind=kOutput, calls=%fused_computation.6 | convolution fusion | flops 2013659136 | bytes 9961472 | tf_op jit(solution)/shard_map/dot_general | solution.py:36
  50.8 0.4 fusion.14
  51.4 2.2 %collective-permute-start.12 = (bf16[256,768]{1,0:T(8,128)(2,1)S(1)}, bf16[256,768]{1,0:T(8,128)(2,1)S(1)}, u32[]{:S(2)}, u32[]{:S(2)}) collective-permute-start(bf16[256,768]{1,0:T(8,128)(2,1)S(1)} %get-tuple-element.154.after_ref), channel_id=1, source_target_pairs={{0,4},{4,0},{8,12},{12,8},{1,5},{5,1},{9,13},{13,9},{2,6},{6,2},{1... | collective-permute-start | bytes 1179656 | tf_op jit(solution)/shard_map/ppermute | solution.py:100
  53.6 3.2 %shard_map.113 = bf16[1536,2560]{1,0:T(8,128)(2,1)S(1)} custom-call(bf16[6144,2560]{1,0:T(8,128)(2,1)} %w_hbm.15, bf16[256,768]{1,0:T(8,128)(2,1)S(1)} %get-tuple-element.154.after_ref), custom_call_target="tpu_custom_call" | custom-call | bytes 1000 | tf_op jit(solution)/shard_map/pallas_call | solution.py:51
  57.2 0.6 fusion.19
  58.0 6.0 %collective-permute-start.14 = (bf16[256,768]{1,0:T(8,128)(2,1)S(1)}, bf16[256,768]{1,0:T(8,128)(2,1)S(1)}, u32[]{:S(2)}, u32[]{:S(2)}) collective-permute-start(bf16[256,768]{1,0:T(8,128)(2,1)S(1)} %get-tuple-element.146.after_ref), channel_id=1, source_target_pairs={{0,4},{4,0},{8,12},{12,8},{1,5},{5,1},{9,13},{13,9},{2,6},{6,2},{1... | collective-permute-start | bytes 1179656 | tf_op jit(solution)/shard_map/ppermute | solution.py:100
  64.0 3.2 %shard_map.114 = bf16[1536,2560]{1,0:T(8,128)(2,1)S(1)} custom-call(bf16[6144,2560]{1,0:T(8,128)(2,1)} %w_hbm.15, bf16[256,768]{1,0:T(8,128)(2,1)S(1)} %get-tuple-element.146.after_ref), custom_call_target="tpu_custom_call" | custom-call | bytes 1000 | tf_op jit(solution)/shard_map/pallas_call | solution.py:51
  67.6 0.4 fusion.24
  68.2 4.1 %collective-permute-start.16 = (bf16[256,768]{1,0:T(8,128)(2,1)S(1)}, bf16[256,768]{1,0:T(8,128)(2,1)S(1)}, u32[]{:S(2)}, u32[]{:S(2)}) collective-permute-start(bf16[256,768]{1,0:T(8,128)(2,1)S(1)} %get-tuple-element.140.after_ref), channel_id=1, source_target_pairs={{0,4},{4,0},{8,12},{12,8},{1,5},{5,1},{9,13},{13,9},{2,6},{6,2},{1... | collective-permute-start | bytes 1179656 | tf_op jit(solution)/shard_map/ppermute | solution.py:100
  72.2 3.2 %shard_map.115 = bf16[1536,2560]{1,0:T(8,128)(2,1)S(1)} custom-call(bf16[6144,2560]{1,0:T(8,128)(2,1)} %w_hbm.15, bf16[256,768]{1,0:T(8,128)(2,1)S(1)} %get-tuple-element.140.after_ref), custom_call_target="tpu_custom_call" | custom-call | bytes 1000 | tf_op jit(solution)/shard_map/pallas_call | solution.py:51
  75.6 1.2 %fusion.129 = f32[128,2560]{1,0:T(8,128)S(1)} fusion(bf16[128,1536]{1,0:T(8,128)(2,1)S(1)} %pad_maximum_fusion.10, bf16[1536,2560]{1,0:T(8,128)(2,1)S(1)} %shard_map.113), kind=kOutput, calls=%fused_computation.244 | convolution fusion | flops 1006632960 | bytes 9568256 | tf_op jit(solution)/shard_map/dot_general | solution.py:36
  76.9 1.2 %fusion.130 = f32[128,2560]{1,0:T(8,128)S(1)} fusion(bf16[128,1536]{1,0:T(8,128)(2,1)S(1)} %pad_maximum_fusion.16, bf16[1536,2560]{1,0:T(8,128)(2,1)S(1)} %shard_map.113), kind=kOutput, calls=%fused_computation.245 | convolution fusion | flops 1006632960 | bytes 9568256 | tf_op jit(solution)/shard_map/dot_general | solution.py:36
  78.3 0.2 fusion.58
  78.8 2.6 %collective-permute-done.16 = bf16[256,768]{1,0:T(8,128)(2,1)S(1)} collective-permute-done((bf16[256,768]{1,0:T(8,128)(2,1)S(1)}, bf16[256,768]{1,0:T(8,128)(2,1)S(1)}, u32[]{:S(2)}, u32[]{:S(2)}) %collective-permute-start.16) | collective-permute-done | bytes 393248 | tf_op jit(solution)/shard_map/ppermute | solution.py:100
  81.7 0.5 fusion.29
  82.2 3.2 %collective-permute-start.21 = (bf16[256,768]{1,0:T(8,128)(2,1)S(1)}, bf16[256,768]{1,0:T(8,128)(2,1)S(1)}, u32[]{:S(2)}, u32[]{:S(2)}) collective-permute-start(bf16[256,768]{1,0:T(8,128)(2,1)S(1)} %pad_maximum_fusion.11.after_ref), channel_id=1, source_target_pairs={{0,4},{4,0},{8,12},{12,8},{1,5},{5,1},{9,13},{13,9},{2,6},{6,2},{1... | collective-permute-start | bytes 1179656 | tf_op jit(solution)/shard_map/ppermute | solution.py:100
  85.4 3.2 %shard_map.116 = bf16[1536,2560]{1,0:T(8,128)(2,1)S(1)} custom-call(bf16[6144,2560]{1,0:T(8,128)(2,1)} %w_hbm.15, bf16[256,768]{1,0:T(8,128)(2,1)S(1)} %pad_maximum_fusion.11.after_ref), custom_call_target="tpu_custom_call" | custom-call | bytes 1000 | tf_op jit(solution)/shard_map/pallas_call | solution.py:51
  88.8 1.2 %convolution_add_fusion.5 = f32[128,2560]{1,0:T(8,128)S(1)} fusion(f32[128,2560]{1,0:T(8,128)S(1)} %fusion.129, bf16[128,1536]{1,0:T(8,128)(2,1)S(1)} %pad_maximum_fusion.12, bf16[1536,2560]{1,0:T(8,128)(2,1)S(1)} %shard_map.114), kind=kOutput, calls=%fused_computation.5 | convolution fusion | flops 1006960640 | bytes 10878976 | tf_op jit(solution)/shard_map/dot_general | solution.py:36
  90.1 1.2 %convolution_add_fusion.3 = f32[128,2560]{1,0:T(8,128)S(1)} fusion(f32[128,2560]{1,0:T(8,128)S(1)} %fusion.130, bf16[128,1536]{1,0:T(8,128)(2,1)S(1)} %pad_maximum_fusion.17, bf16[1536,2560]{1,0:T(8,128)(2,1)S(1)} %shard_map.114), kind=kOutput, calls=%fused_computation.3 | convolution fusion | flops 1006960640 | bytes 10878976 | tf_op jit(solution)/shard_map/dot_general | solution.py:36
  91.3 0.3 convolution_add_fusion.19
  91.7 0.4 fusion.34
  92.5 1.2 %convolution_add_fusion.2 = f32[128,2560]{1,0:T(8,128)S(1)} fusion(f32[128,2560]{1,0:T(8,128)S(1)} %convolution_add_fusion.3, bf16[128,1536]{1,0:T(8,128)(2,1)S(1)} %pad_maximum_fusion.18, bf16[1536,2560]{1,0:T(8,128)(2,1)S(1)} %shard_map.115), kind=kOutput, calls=%fused_computation.2 | convolution fusion | flops 1006960640 | bytes 10878976 | tf_op jit(solution)/shard_map/dot_general | solution.py:36
  93.7 0.3 convolution_add_fusion.18
  94.1 0.2 collective-permute-done.21
  94.5 1.2 %convolution_add_fusion.1 = f32[128,2560]{1,0:T(8,128)S(1)} fusion(f32[128,2560]{1,0:T(8,128)S(1)} %convolution_add_fusion.2, bf16[128,1536]{1,0:T(8,128)(2,1)S(1)} %pad_maximum_fusion.19, bf16[1536,2560]{1,0:T(8,128)(2,1)S(1)} %shard_map.116), kind=kOutput, calls=%fused_computation.1 | convolution fusion | flops 1006960640 | bytes 10878976 | tf_op jit(solution)/shard_map/dot_general | solution.py:36
  95.7 0.3 convolution_add_fusion.17
  96.1 0.4 fusion.39
  96.6 2.8 %collective-permute-start.20 = (bf16[256,768]{1,0:T(8,128)(2,1)S(1)}, bf16[256,768]{1,0:T(8,128)(2,1)S(1)}, u32[]{:S(2)}, u32[]{:S(2)}) collective-permute-start(bf16[256,768]{1,0:T(8,128)(2,1)S(1)} %pad_maximum_fusion.14), channel_id=1, source_target_pairs={{0,4},{4,0},{8,12},{12,8},{1,5},{5,1},{9,13},{13,9},{2,6},{6,2},{1... | collective-permute-start | bytes 1179656 | tf_op jit(solution)/shard_map/ppermute | solution.py:100
  99.5 0.6 collective-permute-start.23
  100.1 0.2 fusion.56
  100.4 0.3 convolution_add_fusion.16
  100.6 3.0 %collective-permute-done.18 = bf16[256,768]{1,0:T(8,128)(2,1)S(1)} collective-permute-done((bf16[256,768]{1,0:T(8,128)(2,1)S(1)}, bf16[256,768]{1,0:T(8,128)(2,1)S(1)}, u32[]{:S(2)}, u32[]{:S(2)}) %collective-permute-start.18) | collective-permute-done | bytes 393248 | tf_op jit(solution)/shard_map/ppermute | solution.py:100
  103.6 7.1 %collective-permute-done.20 = bf16[256,768]{1,0:T(8,128)(2,1)S(1)} collective-permute-done((bf16[256,768]{1,0:T(8,128)(2,1)S(1)}, bf16[256,768]{1,0:T(8,128)(2,1)S(1)}, u32[]{:S(2)}, u32[]{:S(2)}) %collective-permute-start.20) | collective-permute-done | bytes 393248 | tf_op jit(solution)/shard_map/ppermute | solution.py:100
  111.2 1.2 %convolution_add_fusion.4 = f32[128,2560]{1,0:T(8,128)S(1)} fusion(f32[128,2560]{1,0:T(8,128)S(1)} %convolution_add_fusion.5, bf16[128,1536]{1,0:T(8,128)(2,1)S(1)} %pad_maximum_fusion.15, bf16[1536,2560]{1,0:T(8,128)(2,1)S(1)} %shard_map.115), kind=kOutput, calls=%fused_computation.4 | convolution fusion | flops 1006960640 | bytes 10878976 | tf_op jit(solution)/shard_map/dot_general | solution.py:36
  112.4 0.3 convolution_add_fusion.15
  112.7 0.3 convolution_add_fusion.14
  113.0 1.2 %convolution_add_fusion = f32[128,2560]{1,0:T(8,128)S(1)} fusion(f32[128,2560]{1,0:T(8,128)S(1)} %convolution_add_fusion.4, bf16[128,1536]{1,0:T(8,128)(2,1)S(1)} %pad_maximum_fusion.20, bf16[1536,2560]{1,0:T(8,128)(2,1)S(1)} %shard_map.116), kind=kOutput, calls=%fused_computation | convolution fusion | flops 1006960640 | bytes 10878976 | tf_op jit(solution)/shard_map/dot_general | solution.py:36
  114.4 1.6 %collective-permute-done.24 = bf16[64,2688]{1,0:T(8,128)(2,1)S(1)} collective-permute-done((bf16[64,2688]{1,0:T(8,128)(2,1)S(1)}, bf16[64,2688]{1,0:T(8,128)(2,1)S(1)}, u32[]{:S(2)}, u32[]{:S(2)}) %collective-permute-start.24) | collective-permute-done | bytes 344096 | tf_op jit(solution)/shard_map/ppermute | solution.py:97
  116.1 1.0 fusion.49
  (146 shorter events, 6.3 us)
Async XLA Ops:
  0.0 116.1 %copy-start = (bf16[128,2560]{1,0:T(8,128)(2,1)S(1)}, bf16[128,2560]{1,0:T(8,128)(2,1)}, u32[]{:S(2)}) copy-start(bf16[128,2560]{1,0:T(8,128)(2,1)} %param.21) | copy-start | bytes 1966084
  0.0 15.9 %collective-permute-start = (bf16[64,2560]{1,0:T(8,128)(2,1)}, bf16[64,2560]{1,0:T(8,128)(2,1)S(1)}, u32[]{:S(2)}, u32[]{:S(2)}) collective-permute-start(bf16[64,2560]{1,0:T(8,128)(2,1)} %param.11), channel_id=1, source_target_pairs={{0,2},{1,3},{2,0},{3,1},{4,6},{5,7},{6,4},{7,5},{8,10},{9,11},{10,... | collective-permute-start | bytes 983048 | tf_op jit(solution)/shard_map/ppermute | solution.py:97
  2.9 4.0 %collective-permute-start.2 = (bf16[64,2560]{1,0:T(8,128)(2,1)}, bf16[64,2560]{1,0:T(8,128)(2,1)S(1)}, u32[]{:S(2)}, u32[]{:S(2)}) collective-permute-start(bf16[64,2560]{1,0:T(8,128)(2,1)} %param.11), channel_id=1, source_target_pairs={{0,1},{1,0},{2,3},{3,2},{4,5},{5,4},{6,7},{7,6},{8,9},{9,8},{10,11... | collective-permute-start | bytes 983048 | tf_op jit(solution)/shard_map/ppermute | solution.py:97
  2.9 0.7 copy-start.1
  3.6 3.3 %copy-start.5 = (bf16[64,2560]{1,0:T(8,128)(2,1)S(1)}, bf16[64,2560]{1,0:T(8,128)(2,1)}, u32[]{:S(2)}) copy-start(bf16[64,2560]{1,0:T(8,128)(2,1)} %param.11) | copy-start | bytes 983044
  3.6 3.4 %copy-start.4 = (bf16[2560,128]{1,0:T(8,128)(2,1)S(1)}, bf16[2560,128]{1,0:T(8,128)(2,1)}, u32[]{:S(2)}) copy-start(bf16[2560,128]{1,0:T(8,128)(2,1)} %param.16) | copy-start | bytes 1966084
  8.7 13.0 %collective-permute-start.3 = (bf16[288,768]{1,0:T(8,128)(2,1)S(1)}, bf16[288,768]{1,0:T(8,128)(2,1)S(1)}, u32[]{:S(2)}, u32[]{:S(2)}) collective-permute-start(bf16[288,768]{1,0:T(8,128)(2,1)S(1)} %pad_maximum_fusion.2.after_ref), channel_id=1, source_target_pairs={{0,4},{4,0},{8,12},{12,8},{1,5},{5,1},{9,13},{13,9},{2,6},{6,2},{1... | collective-permute-start | bytes 1327112 | tf_op jit(solution)/shard_map/ppermute | solution.py:100
  14.8 0.7 copy-start.2
  14.8 0.7 copy-start.8
  14.8 1.0 copy-start.6
  14.9 15.3 %collective-permute-start.4 = (bf16[256,768]{1,0:T(8,128)(2,1)S(1)}, bf16[256,768]{1,0:T(8,128)(2,1)S(1)}, u32[]{:S(2)}, u32[]{:S(2)}) collective-permute-start(bf16[256,768]{1,0:T(8,128)(2,1)S(1)} %pad_maximum_fusion.4), channel_id=1, source_target_pairs={{0,4},{4,0},{8,12},{12,8},{1,5},{5,1},{9,13},{13,9},{2,6},{6,2},{1... | collective-permute-start | bytes 1179656 | tf_op jit(solution)/shard_map/ppermute | solution.py:100
  15.9 1.7 %collective-permute-start.1 = (bf16[64,2560]{1,0:T(8,128)(2,1)S(1)}, bf16[64,2560]{1,0:T(8,128)(2,1)S(1)}, u32[]{:S(2)}, u32[]{:S(2)}) collective-permute-start(bf16[64,2560]{1,0:T(8,128)(2,1)S(1)} %collective-permute-done), channel_id=1, source_target_pairs={{0,1},{1,0},{2,3},{3,2},{4,5},{5,4},{6,7},{7,6},{8,9},{9,8},{10,11... | collective-permute-start | bytes 983048 | tf_op jit(solution)/shard_map/ppermute | solution.py:97
  19.2 23.0 %collective-permute-start.7 = (bf16[288,768]{1,0:T(8,128)(2,1)S(1)}, bf16[288,768]{1,0:T(8,128)(2,1)S(1)}, u32[]{:S(2)}, u32[]{:S(2)}) collective-permute-start(bf16[288,768]{1,0:T(8,128)(2,1)S(1)} %pad_maximum_fusion.3), channel_id=1, source_target_pairs={{0,4},{4,0},{8,12},{12,8},{1,5},{5,1},{9,13},{13,9},{2,6},{6,2},{1... | collective-permute-start | bytes 1327112 | tf_op jit(solution)/shard_map/ppermute | solution.py:100
  21.8 8.5 %collective-permute-start.5 = (bf16[288,768]{1,0:T(8,128)(2,1)S(1)}, bf16[288,768]{1,0:T(8,128)(2,1)S(1)}, u32[]{:S(2)}, u32[]{:S(2)}) collective-permute-start(bf16[288,768]{1,0:T(8,128)(2,1)S(1)} %add_convert_fusion.1), channel_id=1, source_target_pairs={{0,1},{1,0},{2,3},{3,2},{4,8},{5,9},{6,10},{7,11},{8,4},{9,5},{10,... | collective-permute-start | bytes 1327112 | tf_op jit(solution)/shard_map/ppermute | solution.py:103
  30.2 1.4 %copy-start.9 = (bf16[128,6144]{1,0:T(8,128)(2,1)S(1)}, bf16[128,6144]{1,0:T(8,128)(2,1)}, u32[]{:S(2)}) copy-start(bf16[128,6144]{1,0:T(8,128)(2,1)} %param.17) | copy-start | bytes 4718596
  30.2 12.3 %collective-permute-start.8 = (bf16[256,768]{1,0:T(8,128)(2,1)S(1)}, bf16[256,768]{1,0:T(8,128)(2,1)S(1)}, u32[]{:S(2)}, u32[]{:S(2)}) collective-permute-start(bf16[256,768]{1,0:T(8,128)(2,1)S(1)} %add_convert_fusion.7), channel_id=1, source_target_pairs={{0,1},{1,0},{2,3},{3,2},{4,8},{5,9},{6,10},{7,11},{8,4},{9,5},{10,... | collective-permute-start | bytes 1179656 | tf_op jit(solution)/shard_map/ppermute | solution.py:103
  32.2 18.2 %collective-permute-start.6 = (bf16[256,768]{1,0:T(8,128)(2,1)S(1)}, bf16[256,768]{1,0:T(8,128)(2,1)S(1)}, u32[]{:S(2)}, u32[]{:S(2)}) collective-permute-start(bf16[256,768]{1,0:T(8,128)(2,1)S(1)} %maximum_select_fusion.after_ref), channel_id=1, source_target_pairs={{0,4},{4,0},{8,12},{12,8},{1,5},{5,1},{9,13},{13,9},{2,6},{6,2},{1... | collective-permute-start | bytes 1179656 | tf_op jit(solution)/shard_map/ppermute | solution.py:100
  42.4 8.2 %collective-permute-start.9 = (bf16[288,768]{1,0:T(8,128)(2,1)S(1)}, bf16[288,768]{1,0:T(8,128)(2,1)S(1)}, u32[]{:S(2)}, u32[]{:S(2)}) collective-permute-start(bf16[288,768]{1,0:T(8,128)(2,1)S(1)} %add_convert_fusion), channel_id=1, source_target_pairs={{0,1},{1,0},{2,3},{3,2},{4,8},{5,9},{6,10},{7,11},{8,4},{9,5},{10,... | collective-permute-start | bytes 1327112 | tf_op jit(solution)/shard_map/ppermute | solution.py:103
  43.3 13.6 %collective-permute-start.10 = (bf16[256,768]{1,0:T(8,128)(2,1)S(1)}, bf16[256,768]{1,0:T(8,128)(2,1)S(1)}, u32[]{:S(2)}, u32[]{:S(2)}) collective-permute-start(bf16[256,768]{1,0:T(8,128)(2,1)S(1)} %get-tuple-element.158.after_ref), channel_id=1, source_target_pairs={{0,4},{4,0},{8,12},{12,8},{1,5},{5,1},{9,13},{13,9},{2,6},{6,2},{1... | collective-permute-start | bytes 1179656 | tf_op jit(solution)/shard_map/ppermute | solution.py:100
  50.5 6.5 %collective-permute-start.11 = (bf16[256,768]{1,0:T(8,128)(2,1)S(1)}, bf16[256,768]{1,0:T(8,128)(2,1)S(1)}, u32[]{:S(2)}, u32[]{:S(2)}) collective-permute-start(bf16[256,768]{1,0:T(8,128)(2,1)S(1)} %add_convert_fusion.6), channel_id=1, source_target_pairs={{0,1},{1,0},{2,3},{3,2},{4,8},{5,9},{6,10},{7,11},{8,4},{9,5},{10,... | collective-permute-start | bytes 1179656 | tf_op jit(solution)/shard_map/ppermute | solution.py:103
  51.4 15.8 %collective-permute-start.12 = (bf16[256,768]{1,0:T(8,128)(2,1)S(1)}, bf16[256,768]{1,0:T(8,128)(2,1)S(1)}, u32[]{:S(2)}, u32[]{:S(2)}) collective-permute-start(bf16[256,768]{1,0:T(8,128)(2,1)S(1)} %get-tuple-element.154.after_ref), channel_id=1, source_target_pairs={{0,4},{4,0},{8,12},{12,8},{1,5},{5,1},{9,13},{13,9},{2,6},{6,2},{1... | collective-permute-start | bytes 1179656 | tf_op jit(solution)/shard_map/ppermute | solution.py:100
  57.0 10.4 %collective-permute-start.13 = (bf16[256,768]{1,0:T(8,128)(2,1)S(1)}, bf16[256,768]{1,0:T(8,128)(2,1)S(1)}, u32[]{:S(2)}, u32[]{:S(2)}) collective-permute-start(bf16[256,768]{1,0:T(8,128)(2,1)S(1)} %add_convert_fusion.5), channel_id=1, source_target_pairs={{0,1},{1,0},{2,3},{3,2},{4,8},{5,9},{6,10},{7,11},{8,4},{9,5},{10,... | collective-permute-start | bytes 1179656 | tf_op jit(solution)/shard_map/ppermute | solution.py:103
  58.0 20.6 %collective-permute-start.14 = (bf16[256,768]{1,0:T(8,128)(2,1)S(1)}, bf16[256,768]{1,0:T(8,128)(2,1)S(1)}, u32[]{:S(2)}, u32[]{:S(2)}) collective-permute-start(bf16[256,768]{1,0:T(8,128)(2,1)S(1)} %get-tuple-element.146.after_ref), channel_id=1, source_target_pairs={{0,4},{4,0},{8,12},{12,8},{1,5},{5,1},{9,13},{13,9},{2,6},{6,2},{1... | collective-permute-start | bytes 1179656 | tf_op jit(solution)/shard_map/ppermute | solution.py:100
  67.3 14.2 %collective-permute-start.15 = (bf16[256,768]{1,0:T(8,128)(2,1)S(1)}, bf16[256,768]{1,0:T(8,128)(2,1)S(1)}, u32[]{:S(2)}, u32[]{:S(2)}) collective-permute-start(bf16[256,768]{1,0:T(8,128)(2,1)S(1)} %add_convert_fusion.4), channel_id=1, source_target_pairs={{0,1},{1,0},{2,3},{3,2},{4,8},{5,9},{6,10},{7,11},{8,4},{9,5},{10,... | collective-permute-start | bytes 1179656 | tf_op jit(solution)/shard_map/ppermute | solution.py:103
  68.2 13.2 %collective-permute-start.16 = (bf16[256,768]{1,0:T(8,128)(2,1)S(1)}, bf16[256,768]{1,0:T(8,128)(2,1)S(1)}, u32[]{:S(2)}, u32[]{:S(2)}) collective-permute-start(bf16[256,768]{1,0:T(8,128)(2,1)S(1)} %get-tuple-element.140.after_ref), channel_id=1, source_target_pairs={{0,4},{4,0},{8,12},{12,8},{1,5},{5,1},{9,13},{13,9},{2,6},{6,2},{1... | collective-permute-start | bytes 1179656 | tf_op jit(solution)/shard_map/ppermute | solution.py:100
  76.9 1.4 %copy-start.3 = (bf16[6144,128]{1,0:T(8,128)(2,1)S(1)}, bf16[6144,128]{1,0:T(8,128)(2,1)}, u32[]{:S(2)}) copy-start(bf16[6144,128]{1,0:T(8,128)(2,1)} %param.20) | copy-start | bytes 4718596
  78.7 12.9 %collective-permute-start.17 = (bf16[256,768]{1,0:T(8,128)(2,1)S(1)}, bf16[256,768]{1,0:T(8,128)(2,1)S(1)}, u32[]{:S(2)}, u32[]{:S(2)}) collective-permute-start(bf16[256,768]{1,0:T(8,128)(2,1)S(1)} %add_convert_fusion.3), channel_id=1, source_target_pairs={{0,1},{1,0},{2,3},{3,2},{4,8},{5,9},{6,10},{7,11},{8,4},{9,5},{10,... | collective-permute-start | bytes 1179656 | tf_op jit(solution)/shard_map/ppermute | solution.py:103
  81.5 12.5 %collective-permute-start.19 = (bf16[256,768]{1,0:T(8,128)(2,1)S(1)}, bf16[256,768]{1,0:T(8,128)(2,1)S(1)}, u32[]{:S(2)}, u32[]{:S(2)}) collective-permute-start(bf16[256,768]{1,0:T(8,128)(2,1)S(1)} %add_convert_fusion.2), channel_id=1, source_target_pairs={{0,1},{1,0},{2,3},{3,2},{4,8},{5,9},{6,10},{7,11},{8,4},{9,5},{10,... | collective-permute-start | bytes 1179656 | tf_op jit(solution)/shard_map/ppermute | solution.py:103
  82.2 12.1 %collective-permute-start.21 = (bf16[256,768]{1,0:T(8,128)(2,1)S(1)}, bf16[256,768]{1,0:T(8,128)(2,1)S(1)}, u32[]{:S(2)}, u32[]{:S(2)}) collective-permute-start(bf16[256,768]{1,0:T(8,128)(2,1)S(1)} %pad_maximum_fusion.11.after_ref), channel_id=1, source_target_pairs={{0,4},{4,0},{8,12},{12,8},{1,5},{5,1},{9,13},{13,9},{2,6},{6,2},{1... | collective-permute-start | bytes 1179656 | tf_op jit(solution)/shard_map/ppermute | solution.py:100
  92.3 11.3 %collective-permute-start.18 = (bf16[256,768]{1,0:T(8,128)(2,1)S(1)}, bf16[256,768]{1,0:T(8,128)(2,1)S(1)}, u32[]{:S(2)}, u32[]{:S(2)}) collective-permute-start(bf16[256,768]{1,0:T(8,128)(2,1)S(1)} %pad_maximum_fusion.13), channel_id=1, source_target_pairs={{0,4},{4,0},{8,12},{12,8},{1,5},{5,1},{9,13},{13,9},{2,6},{6,2},{1... | collective-permute-start | bytes 1179656 | tf_op jit(solution)/shard_map/ppermute | solution.py:100
  96.0 3.4 %collective-permute-start.22 = (bf16[64,2688]{1,0:T(8,128)(2,1)S(1)}, bf16[64,2688]{1,0:T(8,128)(2,1)S(1)}, u32[]{:S(2)}, u32[]{:S(2)}) collective-permute-start(bf16[64,2688]{1,0:T(8,128)(2,1)S(1)} %fusion.47), channel_id=1, source_target_pairs={{0,1},{1,0},{2,3},{3,2},{4,5},{5,4},{6,7},{7,6},{8,9},{9,8},{10,11... | collective-permute-start | bytes 1032200 | tf_op jit(solution)/shard_map/ppermute | solution.py:97
  96.6 14.0 %collective-permute-start.20 = (bf16[256,768]{1,0:T(8,128)(2,1)S(1)}, bf16[256,768]{1,0:T(8,128)(2,1)S(1)}, u32[]{:S(2)}, u32[]{:S(2)}) collective-permute-start(bf16[256,768]{1,0:T(8,128)(2,1)S(1)} %pad_maximum_fusion.14), channel_id=1, source_target_pairs={{0,4},{4,0},{8,12},{12,8},{1,5},{5,1},{9,13},{13,9},{2,6},{6,2},{1... | collective-permute-start | bytes 1179656 | tf_op jit(solution)/shard_map/ppermute | solution.py:100
  99.5 11.1 %collective-permute-start.23 = (bf16[64,2688]{1,0:T(8,128)(2,1)S(1)}, bf16[64,2688]{1,0:T(8,128)(2,1)S(1)}, u32[]{:S(2)}, u32[]{:S(2)}) collective-permute-start(bf16[64,2688]{1,0:T(8,128)(2,1)S(1)} %fusion.45), channel_id=1, source_target_pairs={{0,2},{1,3},{2,0},{3,1},{4,6},{5,7},{6,4},{7,5},{8,10},{9,11},{10,... | collective-permute-start | bytes 1032200 | tf_op jit(solution)/shard_map/ppermute | solution.py:97
  114.3 1.9 %copy-start.7 = (f32[2560]{0:T(1024)S(1)}, f32[2560]{0:T(1024)}, u32[]{:S(2)}) copy-start(f32[2560]{0:T(1024)} %param.19) | copy-start | bytes 30724
  114.3 1.7 %collective-permute-start.24 = (bf16[64,2688]{1,0:T(8,128)(2,1)S(1)}, bf16[64,2688]{1,0:T(8,128)(2,1)S(1)}, u32[]{:S(2)}, u32[]{:S(2)}) collective-permute-start(bf16[64,2688]{1,0:T(8,128)(2,1)S(1)} %fusion.46), channel_id=1, source_target_pairs={{0,1},{1,0},{2,3},{3,2},{4,5},{5,4},{6,7},{7,6},{8,9},{9,8},{10,11... | collective-permute-start | bytes 1032200 | tf_op jit(solution)/shard_map/ppermute | solution.py:97

commit v16 on v15

--- a/solution.py
+++ b/solution.py
@@ -57,6 +57,10 @@
         compiler_params=pltpu.CompilerParams(vmem_limit_bytes=1 << 20),
         cost_estimate=pl.CostEstimate(flops=0, bytes_accessed=1000, transcendentals=0),
     )(pltpu.with_memory_space_constraint(weight, pltpu.HBM), after)
+
+
+def behind(value, row):
+    return value + 0.0 * row[:1, : value.shape[1]].astype(F32)
 
 
 def activate(summed, low_in, first_up_maps, first_bias, part):
@@ -228,6 +232,8 @@
         for t in range(UNITS + LAG):
             if t < UNITS:
                 ours = tie(partials[t], last).astype(F32)
+                if t > 0 and t - 1 + LAG - 1 in payloads:
+                    ours = behind(ours, payloads[t - 2 + LAG])
                 sums[t] = (ours + swaps[t].astype(F32)).astype(BF16)
                 last = sums[t]
                 crosses[t] = cross(sums[t])
@@ -244,6 +250,8 @@
                     low = jnp.concatenate(low, axis=0)
                     own_mask = mask[:near] if k == 0 else mask[near:]
                     low_in[is_near(k)] = jnp.where(own_mask, low, 0.0).astype(BF16)
+                if k == UNITS - 1:
+                    summed = behind(summed, outputs["far"][0])
                 low = low_in[is_near(k)]
                 value = activate(unfold(summed), low, first_up_maps, first_bias, columns(k))
                 value = halves(value)
@@ -270,9 +278,10 @@
                 across = (ours + come.astype(F32)).astype(BF16)
                 across = col_swap(across, 2)
             elif unit >= 2 * early:
+                states = unfold(state(unit))
                 if unit == UNITS - 1:
                     last = across
-                second("near" if is_near(unit) else "far", unfold(state(unit)), block_of(unit))
+                second("near" if is_near(unit) else "far", states, block_of(unit))
         ours, theirs = core_parts("near")
         come = col_swap(theirs, 1)
         return ours + come.astype(F32) + across.astype(F32), mask

time: 118 us -> 117 us (level)
  transfers between devices with their start and end apart: 25 -> 25, of which waited for: 8 -> 7; matrix products, arithmetic and copies ran while one was open for 23% -> 25% of each run, Pallas kernels for 22% -> 22%
where the time goes in v16:
time: 117 us; the launch traced here: 116 us
  starting transfers between devices  32 us (27%)
  Pallas kernels  26 us (22%)
  matrix products  26 us (22%)
  waiting for transfers between devices  23.3 us (20%)
  other arithmetic  3.94 us (3%)
  local copies, waits for them, and re-layouts  3.62 us (3%)
  between operations  1.31 us (1%)
    ppermute x11, starting transfers between devices, end_swap(): return lax.ppermute(value, 'row', [(i, i ^ 1) for i in range(n_row)])  27.3 us
    dot_general x33, matrix products, dot(): return jnp.dot(left, right, preferred_element_type=F32)  26 us
    pallas_call x8, Pallas kernels, load_part(): pl.pallas_call(functools.partial(load_kernel, part=part), in_specs=[pl.Bl...  26 us
    ppermute x11, waiting for transfers between devices, end_swap(): return lax.ppermute(value, 'row', [(i, i ^ 1) for i in range(n_row)])  20.3 us
    ppermute x6, starting transfers between devices, col_swap(): return lax.ppermute(value, 'col', [(i, i ^ flip) for i in range(n_col)])  4.18 us
    ppermute x6, waiting for transfers between devices, col_swap(): return lax.ppermute(value, 'col', [(i, i ^ flip) for i in range(n_col)])  3.03 us
  transfers between devices with their start and end apart: 25, of which 7 were waited for; matrix products, arithmetic and copies ran while one was open for 25% of the time, Pallas kernels for 22%

profile of v16, /device:TPU:0, one launch (start us, length us, event | category | flops | bytes accessed | tf_op | source)
XLA Modules:
  0.0 116.2 jit_solution(15840288286650100513)
XLA Ops:
  0.0 2.9 %collective-permute-start = (bf16[64,2560]{1,0:T(8,128)(2,1)}, bf16[64,2560]{1,0:T(8,128)(2,1)S(1)}, u32[]{:S(2)}, u32[]{:S(2)}) collective-permute-start(bf16[64,2560]{1,0:T(8,128)(2,1)} %param.11), channel_id=1, source_target_pairs={{0,2},{1,3},{2,0},{3,1},{4,6},{5,7},{6,4},{7,5},{8,10},{9,11},{10,... | collective-permute-start | bytes 983048 | tf_op jit(solution)/shard_map/ppermute | solution.py:101
  3.0 0.7 copy-done.1
  3.6 3.3 %shard_map.109 = bf16[2560,1536]{1,0:T(8,128)(2,1)S(1)} custom-call(bf16[2560,6144]{1,0:T(8,128)(2,1)} %w_hbm.11, s32[4]{0:T(128)S(1)} %copy-done.1), custom_call_target="tpu_custom_call" | custom-call | bytes 1000 | tf_op jit(solution)/shard_map/pallas_call | solution.py:51
  7.0 0.3 convolution_convert_fusion.7
  7.4 1.2 %convolution_convert_fusion.5 = bf16[128,1536]{1,0:T(8,128)(2,1)S(1)} fusion(bf16[128,2560]{1,0:T(8,128)(2,1)S(1)} %constant_dynamic-update-slice_fusion.2, bf16[2560,1536]{1,0:T(8,128)(2,1)S(1)} %shard_map.109), kind=kOutput, calls=%fused_computation.19 | convolution fusion | flops 1006829568 | bytes 8912896 | tf_op jit(solution)/shard_map/dot_general | solution.py:36
  8.7 1.6 %collective-permute-start.3 = (bf16[288,768]{1,0:T(8,128)(2,1)S(1)}, bf16[288,768]{1,0:T(8,128)(2,1)S(1)}, u32[]{:S(2)}, u32[]{:S(2)}) collective-permute-start(bf16[288,768]{1,0:T(8,128)(2,1)S(1)} %pad_maximum_fusion.2.after_ref), channel_id=1, source_target_pairs={{0,4},{4,0},{8,12},{12,8},{1,5},{5,1},{9,13},{13,9},{2,6},{6,2},{1... | collective-permute-start | bytes 1327112 | tf_op jit(solution)/shard_map/ppermute | solution.py:104
  10.3 3.2 %shard_map.110 = bf16[2560,1536]{1,0:T(8,128)(2,1)S(1)} custom-call(bf16[2560,6144]{1,0:T(8,128)(2,1)} %w_hbm.11, bf16[288,768]{1,0:T(8,128)(2,1)S(1)} %pad_maximum_fusion.2.after_ref), custom_call_target="tpu_custom_call" | custom-call | bytes 1000 | tf_op jit(solution)/shard_map/pallas_call | solution.py:51
  13.6 1.2 %convolution_convert_fusion.4 = bf16[128,1536]{1,0:T(8,128)(2,1)S(1)} fusion(bf16[128,2560]{1,0:T(8,128)(2,1)S(1)} %constant_dynamic-update-slice_fusion.2, bf16[2560,1536]{1,0:T(8,128)(2,1)S(1)} %shard_map.110), kind=kOutput, calls=%fused_computation.18 | convolution fusion | flops 1006829568 | bytes 8912896 | tf_op jit(solution)/shard_map/dot_general | solution.py:36
  14.9 0.5 collective-permute-start.4
  15.9 0.3 collective-permute-start.1
  16.2 1.4 %collective-permute-done.1 = bf16[64,2560]{1,0:T(8,128)(2,1)S(1)} collective-permute-done((bf16[64,2560]{1,0:T(8,128)(2,1)S(1)}, bf16[64,2560]{1,0:T(8,128)(2,1)S(1)}, u32[]{:S(2)}, u32[]{:S(2)}) %collective-permute-start.1) | collective-permute-done | bytes 327712 | tf_op jit(solution)/shard_map/ppermute | solution.py:101
  17.6 0.3 convolution_convert_fusion.6
  17.9 1.2 %convolution_convert_fusion.3 = bf16[128,1536]{1,0:T(8,128)(2,1)S(1)} fusion(bf16[128,2560]{1,0:T(8,128)(2,1)S(1)} %constant_dynamic-update-slice_fusion, bf16[2560,1536]{1,0:T(8,128)(2,1)S(1)} %shard_map.109), kind=kOutput, calls=%fused_computation.17 | convolution fusion | flops 1006829568 | bytes 8912896 | tf_op jit(solution)/shard_map/dot_general | solution.py:36
  19.2 1.6 %collective-permute-start.7 = (bf16[288,768]{1,0:T(8,128)(2,1)S(1)}, bf16[288,768]{1,0:T(8,128)(2,1)S(1)}, u32[]{:S(2)}, u32[]{:S(2)}) collective-permute-start(bf16[288,768]{1,0:T(8,128)(2,1)S(1)} %pad_maximum_fusion.3), channel_id=1, source_target_pairs={{0,4},{4,0},{8,12},{12,8},{1,5},{5,1},{9,13},{13,9},{2,6},{6,2},{1... | collective-permute-start | bytes 1327112 | tf_op jit(solution)/shard_map/ppermute | solution.py:104
  20.8 0.9 collective-permute-done.3
  21.9 1.2 %convolution_convert_fusion.2 = bf16[128,1536]{1,0:T(8,128)(2,1)S(1)} fusion(bf16[128,2560]{1,0:T(8,128)(2,1)S(1)} %constant_dynamic-update-slice_fusion, bf16[2560,1536]{1,0:T(8,128)(2,1)S(1)} %shard_map.110), kind=kOutput, calls=%fused_computation.16 | convolution fusion | flops 1006829568 | bytes 8912896 | tf_op jit(solution)/shard_map/dot_general | solution.py:36
  23.2 7.0 %collective-permute-done.4 = bf16[256,768]{1,0:T(8,128)(2,1)S(1)} collective-permute-done((bf16[256,768]{1,0:T(8,128)(2,1)S(1)}, bf16[256,768]{1,0:T(8,128)(2,1)S(1)}, u32[]{:S(2)}, u32[]{:S(2)}) %collective-permute-start.4) | collective-permute-done | bytes 393248 | tf_op jit(solution)/shard_map/ppermute | solution.py:104
  30.6 1.1 copy-done.9
  31.7 0.4 fusion.4
  32.3 4.4 %collective-permute-start.6 = (bf16[256,768]{1,0:T(8,128)(2,1)S(1)}, bf16[256,768]{1,0:T(8,128)(2,1)S(1)}, u32[]{:S(2)}, u32[]{:S(2)}) collective-permute-start(bf16[256,768]{1,0:T(8,128)(2,1)S(1)} %maximum_select_fusion.after_ref), channel_id=1, source_target_pairs={{0,4},{4,0},{8,12},{12,8},{1,5},{5,1},{9,13},{13,9},{2,6},{6,2},{1... | collective-permute-start | bytes 1179656 | tf_op jit(solution)/shard_map/ppermute | solution.py:104
  36.7 3.2 %shard_map.111 = bf16[2560,1536]{1,0:T(8,128)(2,1)S(1)} custom-call(bf16[2560,6144]{1,0:T(8,128)(2,1)} %w_hbm.11, bf16[256,768]{1,0:T(8,128)(2,1)S(1)} %maximum_select_fusion.after_ref), custom_call_target="tpu_custom_call" | custom-call | bytes 1000 | tf_op jit(solution)/shard_map/pallas_call | solution.py:51
  40.0 2.2 %convolution_convert_fusion.1 = bf16[256,1536]{1,0:T(8,128)(2,1)S(1)} fusion(bf16[256,2560]{1,0:T(8,128)(2,1)S(1)} %constant_dynamic-update-slice_fusion.4, bf16[2560,1536]{1,0:T(8,128)(2,1)S(1)} %shard_map.111), kind=kOutput, calls=%fused_computation.7 | convolution fusion | flops 2013659136 | bytes 9961472 | tf_op jit(solution)/shard_map/dot_general | solution.py:36
  42.7 0.4 fusion.9
  43.3 1.6 %collective-permute-start.10 = (bf16[256,768]{1,0:T(8,128)(2,1)S(1)}, bf16[256,768]{1,0:T(8,128)(2,1)S(1)}, u32[]{:S(2)}, u32[]{:S(2)}) collective-permute-start(bf16[256,768]{1,0:T(8,128)(2,1)S(1)} %get-tuple-element.156.after_ref), channel_id=1, source_target_pairs={{0,4},{4,0},{8,12},{12,8},{1,5},{5,1},{9,13},{13,9},{2,6},{6,2},{1... | collective-permute-start | bytes 1179656 | tf_op jit(solution)/shard_map/ppermute | solution.py:104
  45.0 3.2 %shard_map.112 = bf16[2560,1536]{1,0:T(8,128)(2,1)S(1)} custom-call(bf16[2560,6144]{1,0:T(8,128)(2,1)} %w_hbm.11, bf16[256,768]{1,0:T(8,128)(2,1)S(1)} %get-tuple-element.156.after_ref), custom_call_target="tpu_custom_call" | custom-call | bytes 1000 | tf_op jit(solution)/shard_map/pallas_call | solution.py:51
  48.2 2.2 %convolution_convert_fusion = bf16[256,1536]{1,0:T(8,128)(2,1)S(1)} fusion(bf16[256,2560]{1,0:T(8,128)(2,1)S(1)} %constant_dynamic-update-slice_fusion.4, bf16[2560,1536]{1,0:T(8,128)(2,1)S(1)} %shard_map.112), kind=kOutput, calls=%fused_computation.6 | convolution fusion | flops 2013659136 | bytes 9961472 | tf_op jit(solution)/shard_map/dot_general | solution.py:36
  50.9 0.4 fusion.14
  51.5 2.2 %collective-permute-start.12 = (bf16[256,768]{1,0:T(8,128)(2,1)S(1)}, bf16[256,768]{1,0:T(8,128)(2,1)S(1)}, u32[]{:S(2)}, u32[]{:S(2)}) collective-permute-start(bf16[256,768]{1,0:T(8,128)(2,1)S(1)} %get-tuple-element.152.after_ref), channel_id=1, source_target_pairs={{0,4},{4,0},{8,12},{12,8},{1,5},{5,1},{9,13},{13,9},{2,6},{6,2},{1... | collective-permute-start | bytes 1179656 | tf_op jit(solution)/shard_map/ppermute | solution.py:104
  53.7 3.2 %shard_map.113 = bf16[1536,2560]{1,0:T(8,128)(2,1)S(1)} custom-call(bf16[6144,2560]{1,0:T(8,128)(2,1)} %w_hbm.15, bf16[256,768]{1,0:T(8,128)(2,1)S(1)} %get-tuple-element.152.after_ref), custom_call_target="tpu_custom_call" | custom-call | bytes 1000 | tf_op jit(solution)/shard_map/pallas_call | solution.py:51
  57.2 0.2 fusion.117
  57.5 0.4 fusion.19
  58.1 6.0 %collective-permute-start.14 = (bf16[256,768]{1,0:T(8,128)(2,1)S(1)}, bf16[256,768]{1,0:T(8,128)(2,1)S(1)}, u32[]{:S(2)}, u32[]{:S(2)}) collective-permute-start(bf16[256,768]{1,0:T(8,128)(2,1)S(1)} %get-tuple-element.144.after_ref), channel_id=1, source_target_pairs={{0,4},{4,0},{8,12},{12,8},{1,5},{5,1},{9,13},{13,9},{2,6},{6,2},{1... | collective-permute-start | bytes 1179656 | tf_op jit(solution)/shard_map/ppermute | solution.py:104
  64.1 3.2 %shard_map.114 = bf16[1536,2560]{1,0:T(8,128)(2,1)S(1)} custom-call(bf16[6144,2560]{1,0:T(8,128)(2,1)} %w_hbm.15, bf16[256,768]{1,0:T(8,128)(2,1)S(1)} %get-tuple-element.144.after_ref), custom_call_target="tpu_custom_call" | custom-call | bytes 1000 | tf_op jit(solution)/shard_map/pallas_call | solution.py:51
  67.7 0.4 fusion.24
  68.3 4.0 %collective-permute-start.16 = (bf16[256,768]{1,0:T(8,128)(2,1)S(1)}, bf16[256,768]{1,0:T(8,128)(2,1)S(1)}, u32[]{:S(2)}, u32[]{:S(2)}) collective-permute-start(bf16[256,768]{1,0:T(8,128)(2,1)S(1)} %get-tuple-element.138.after_ref), channel_id=1, source_target_pairs={{0,4},{4,0},{8,12},{12,8},{1,5},{5,1},{9,13},{13,9},{2,6},{6,2},{1... | collective-permute-start | bytes 1179656 | tf_op jit(solution)/shard_map/ppermute | solution.py:104
  72.3 3.2 %shard_map.115 = bf16[1536,2560]{1,0:T(8,128)(2,1)S(1)} custom-call(bf16[6144,2560]{1,0:T(8,128)(2,1)} %w_hbm.15, bf16[256,768]{1,0:T(8,128)(2,1)S(1)} %get-tuple-element.138.after_ref), custom_call_target="tpu_custom_call" | custom-call | bytes 1000 | tf_op jit(solution)/shard_map/pallas_call | solution.py:51
  75.7 1.2 %fusion.144 = f32[128,2560]{1,0:T(8,128)S(1)} fusion(bf16[128,1536]{1,0:T(8,128)(2,1)S(1)} %pad_maximum_fusion.10, bf16[1536,2560]{1,0:T(8,128)(2,1)S(1)} %shard_map.113), kind=kOutput, calls=%fused_computation.267 | convolution fusion | flops 1006632960 | bytes 9568256 | tf_op jit(solution)/shard_map/dot_general | solution.py:36
  77.0 1.2 %fusion.145 = f32[128,2560]{1,0:T(8,128)S(1)} fusion(bf16[128,1536]{1,0:T(8,128)(2,1)S(1)} %pad_maximum_fusion.14, bf16[1536,2560]{1,0:T(8,128)(2,1)S(1)} %shard_map.113), kind=kOutput, calls=%fused_computation.268 | convolution fusion | flops 1006632960 | bytes 9568256 | tf_op jit(solution)/shard_map/dot_general | solution.py:36
  78.4 0.2 fusion.56
  78.7 0.3 fusion.58
  79.3 0.4 fusion.29
  79.8 1.5 %collective-permute-done.16 = bf16[256,768]{1,0:T(8,128)(2,1)S(1)} collective-permute-done((bf16[256,768]{1,0:T(8,128)(2,1)S(1)}, bf16[256,768]{1,0:T(8,128)(2,1)S(1)}, u32[]{:S(2)}, u32[]{:S(2)}) %collective-permute-start.16) | collective-permute-done | bytes 393248 | tf_op jit(solution)/shard_map/ppermute | solution.py:104
  81.6 3.2 %collective-permute-start.20 = (bf16[256,768]{1,0:T(8,128)(2,1)S(1)}, bf16[256,768]{1,0:T(8,128)(2,1)S(1)}, u32[]{:S(2)}, u32[]{:S(2)}) collective-permute-start(bf16[256,768]{1,0:T(8,128)(2,1)S(1)} %pad_maximum_fusion.11.after_ref), channel_id=1, source_target_pairs={{0,4},{4,0},{8,12},{12,8},{1,5},{5,1},{9,13},{13,9},{2,6},{6,2},{1... | collective-permute-start | bytes 1179656 | tf_op jit(solution)/shard_map/ppermute | solution.py:104
  84.8 3.2 %shard_map.116 = bf16[1536,2560]{1,0:T(8,128)(2,1)S(1)} custom-call(bf16[6144,2560]{1,0:T(8,128)(2,1)} %w_hbm.15, bf16[256,768]{1,0:T(8,128)(2,1)S(1)} %pad_maximum_fusion.11.after_ref), custom_call_target="tpu_custom_call" | custom-call | bytes 1000 | tf_op jit(solution)/shard_map/pallas_call | solution.py:51
  88.2 1.2 %convolution_add_fusion.5 = f32[128,2560]{1,0:T(8,128)S(1)} fusion(f32[128,2560]{1,0:T(8,128)S(1)} %fusion.144, bf16[128,1536]{1,0:T(8,128)(2,1)S(1)} %pad_maximum_fusion.12, bf16[1536,2560]{1,0:T(8,128)(2,1)S(1)} %shard_map.114), kind=kOutput, calls=%fused_computation.5 | convolution fusion | flops 1006960640 | bytes 10878976 | tf_op jit(solution)/shard_map/dot_general | solution.py:36
  89.5 1.2 %convolution_add_fusion.4 = f32[128,2560]{1,0:T(8,128)S(1)} fusion(f32[128,2560]{1,0:T(8,128)S(1)} %fusion.145, bf16[128,1536]{1,0:T(8,128)(2,1)S(1)} %pad_maximum_fusion.15, bf16[1536,2560]{1,0:T(8,128)(2,1)S(1)} %shard_map.114), kind=kOutput, calls=%fused_computation.4 | convolution fusion | flops 1006960640 | bytes 10878976 | tf_op jit(solution)/shard_map/dot_general | solution.py:36
  90.7 0.3 convolution_add_fusion.16
  91.0 0.3 convolution_add_fusion.19
  91.4 0.4 fusion.34
  92.1 1.2 %convolution_add_fusion.3 = f32[128,2560]{1,0:T(8,128)S(1)} fusion(f32[128,2560]{1,0:T(8,128)S(1)} %convolution_add_fusion.4, bf16[128,1536]{1,0:T(8,128)(2,1)S(1)} %pad_maximum_fusion.16, bf16[1536,2560]{1,0:T(8,128)(2,1)S(1)} %shard_map.115), kind=kOutput, calls=%fused_computation.3 | convolution fusion | flops 1006960640 | bytes 10878976 | tf_op jit(solution)/shard_map/dot_general | solution.py:36
  93.4 0.3 convolution_add_fusion.18
  93.8 1.2 %convolution_add_fusion.2 = f32[128,2560]{1,0:T(8,128)S(1)} fusion(f32[128,2560]{1,0:T(8,128)S(1)} %convolution_add_fusion.3, bf16[128,1536]{1,0:T(8,128)(2,1)S(1)} %pad_maximum_fusion.17, bf16[1536,2560]{1,0:T(8,128)(2,1)S(1)} %shard_map.116), kind=kOutput, calls=%fused_computation.2 | convolution fusion | flops 1006960640 | bytes 10878976 | tf_op jit(solution)/shard_map/dot_general | solution.py:36
  95.1 0.3 convolution_add_fusion.17
  95.7 0.4 fusion.39
  96.2 2.1 %collective-permute-start.21 = (bf16[256,768]{1,0:T(8,128)(2,1)S(1)}, bf16[256,768]{1,0:T(8,128)(2,1)S(1)}, u32[]{:S(2)}, u32[]{:S(2)}) collective-permute-start(bf16[256,768]{1,0:T(8,128)(2,1)S(1)} %pad_maximum_fusion.18), channel_id=1, source_target_pairs={{0,4},{4,0},{8,12},{12,8},{1,5},{5,1},{9,13},{13,9},{2,6},{6,2},{1... | collective-permute-start | bytes 1179656 | tf_op jit(solution)/shard_map/ppermute | solution.py:104
  98.4 0.8 collective-permute-start.23
  99.2 4.3 %collective-permute-done.18 = bf16[256,768]{1,0:T(8,128)(2,1)S(1)} collective-permute-done((bf16[256,768]{1,0:T(8,128)(2,1)S(1)}, bf16[256,768]{1,0:T(8,128)(2,1)S(1)}, u32[]{:S(2)}, u32[]{:S(2)}) %collective-permute-start.18) | collective-permute-done | bytes 393248 | tf_op jit(solution)/shard_map/ppermute | solution.py:104
  103.5 6.5 %collective-permute-done.21 = bf16[256,768]{1,0:T(8,128)(2,1)S(1)} collective-permute-done((bf16[256,768]{1,0:T(8,128)(2,1)S(1)}, bf16[256,768]{1,0:T(8,128)(2,1)S(1)}, u32[]{:S(2)}, u32[]{:S(2)}) %collective-permute-start.21) | collective-permute-done | bytes 393248 | tf_op jit(solution)/shard_map/ppermute | solution.py:104
  110.3 1.2 %convolution_add_fusion.1 = f32[128,2560]{1,0:T(8,128)S(1)} fusion(f32[128,2560]{1,0:T(8,128)S(1)} %convolution_add_fusion.5, bf16[128,1536]{1,0:T(8,128)(2,1)S(1)} %pad_maximum_fusion.19, bf16[1536,2560]{1,0:T(8,128)(2,1)S(1)} %shard_map.115), kind=kOutput, calls=%fused_computation.1 | convolution fusion | flops 1006960640 | bytes 10878976 | tf_op jit(solution)/shard_map/dot_general | solution.py:36
  111.6 0.3 convolution_add_fusion.15
  111.9 0.3 convolution_add_fusion.14
  112.1 1.2 %convolution_add_fusion = f32[128,2560]{1,0:T(8,128)S(1)} fusion(f32[128,2560]{1,0:T(8,128)S(1)} %convolution_add_fusion.1, bf16[128,1536]{1,0:T(8,128)(2,1)S(1)} %pad_maximum_fusion.20, bf16[1536,2560]{1,0:T(8,128)(2,1)S(1)} %shard_map.116), kind=kOutput, calls=%fused_computation | convolution fusion | flops 1006960640 | bytes 10878976 | tf_op jit(solution)/shard_map/dot_general | solution.py:36
  113.5 1.6 %collective-permute-done.24 = bf16[64,2688]{1,0:T(8,128)(2,1)S(1)} collective-permute-done((bf16[64,2688]{1,0:T(8,128)(2,1)S(1)}, bf16[64,2688]{1,0:T(8,128)(2,1)S(1)}, u32[]{:S(2)}, u32[]{:S(2)}) %collective-permute-start.24) | collective-permute-done | bytes 344096 | tf_op jit(solution)/shard_map/ppermute | solution.py:101
  115.2 1.0 fusion.49
  (154 shorter events, 6.4 us)
Async XLA Ops:
  0.0 115.2 %copy-start = (bf16[128,2560]{1,0:T(8,128)(2,1)S(1)}, bf16[128,2560]{1,0:T(8,128)(2,1)}, u32[]{:S(2)}) copy-start(bf16[128,2560]{1,0:T(8,128)(2,1)} %param.21) | copy-start | bytes 1966084
  0.0 15.9 %collective-permute-start = (bf16[64,2560]{1,0:T(8,128)(2,1)}, bf16[64,2560]{1,0:T(8,128)(2,1)S(1)}, u32[]{:S(2)}, u32[]{:S(2)}) collective-permute-start(bf16[64,2560]{1,0:T(8,128)(2,1)} %param.11), channel_id=1, source_target_pairs={{0,2},{1,3},{2,0},{3,1},{4,6},{5,7},{6,4},{7,5},{8,10},{9,11},{10,... | collective-permute-start | bytes 983048 | tf_op jit(solution)/shard_map/ppermute | solution.py:101
  2.9 4.0 %collective-permute-start.2 = (bf16[64,2560]{1,0:T(8,128)(2,1)}, bf16[64,2560]{1,0:T(8,128)(2,1)S(1)}, u32[]{:S(2)}, u32[]{:S(2)}) collective-permute-start(bf16[64,2560]{1,0:T(8,128)(2,1)} %param.11), channel_id=1, source_target_pairs={{0,1},{1,0},{2,3},{3,2},{4,5},{5,4},{6,7},{7,6},{8,9},{9,8},{10,11... | collective-permute-start | bytes 983048 | tf_op jit(solution)/shard_map/ppermute | solution.py:101
  2.9 0.7 copy-start.1
  3.6 3.3 %copy-start.5 = (bf16[64,2560]{1,0:T(8,128)(2,1)S(1)}, bf16[64,2560]{1,0:T(8,128)(2,1)}, u32[]{:S(2)}) copy-start(bf16[64,2560]{1,0:T(8,128)(2,1)} %param.11) | copy-start | bytes 983044
  3.6 3.4 %copy-start.4 = (bf16[2560,128]{1,0:T(8,128)(2,1)S(1)}, bf16[2560,128]{1,0:T(8,128)(2,1)}, u32[]{:S(2)}) copy-start(bf16[2560,128]{1,0:T(8,128)(2,1)} %param.16) | copy-start | bytes 1966084
  8.7 13.0 %collective-permute-start.3 = (bf16[288,768]{1,0:T(8,128)(2,1)S(1)}, bf16[288,768]{1,0:T(8,128)(2,1)S(1)}, u32[]{:S(2)}, u32[]{:S(2)}) collective-permute-start(bf16[288,768]{1,0:T(8,128)(2,1)S(1)} %pad_maximum_fusion.2.after_ref), channel_id=1, source_target_pairs={{0,4},{4,0},{8,12},{12,8},{1,5},{5,1},{9,13},{13,9},{2,6},{6,2},{1... | collective-permute-start | bytes 1327112 | tf_op jit(solution)/shard_map/ppermute | solution.py:104
  14.8 0.7 copy-start.2
  14.8 0.7 copy-start.8
  14.8 1.0 copy-start.6
  14.9 15.3 %collective-permute-start.4 = (bf16[256,768]{1,0:T(8,128)(2,1)S(1)}, bf16[256,768]{1,0:T(8,128)(2,1)S(1)}, u32[]{:S(2)}, u32[]{:S(2)}) collective-permute-start(bf16[256,768]{1,0:T(8,128)(2,1)S(1)} %pad_maximum_fusion.4), channel_id=1, source_target_pairs={{0,4},{4,0},{8,12},{12,8},{1,5},{5,1},{9,13},{13,9},{2,6},{6,2},{1... | collective-permute-start | bytes 1179656 | tf_op jit(solution)/shard_map/ppermute | solution.py:104
  15.9 1.7 %collective-permute-start.1 = (bf16[64,2560]{1,0:T(8,128)(2,1)S(1)}, bf16[64,2560]{1,0:T(8,128)(2,1)S(1)}, u32[]{:S(2)}, u32[]{:S(2)}) collective-permute-start(bf16[64,2560]{1,0:T(8,128)(2,1)S(1)} %collective-permute-done), channel_id=1, source_target_pairs={{0,1},{1,0},{2,3},{3,2},{4,5},{5,4},{6,7},{7,6},{8,9},{9,8},{10,11... | collective-permute-start | bytes 983048 | tf_op jit(solution)/shard_map/ppermute | solution.py:101
  19.2 23.0 %collective-permute-start.7 = (bf16[288,768]{1,0:T(8,128)(2,1)S(1)}, bf16[288,768]{1,0:T(8,128)(2,1)S(1)}, u32[]{:S(2)}, u32[]{:S(2)}) collective-permute-start(bf16[288,768]{1,0:T(8,128)(2,1)S(1)} %pad_maximum_fusion.3), channel_id=1, source_target_pairs={{0,4},{4,0},{8,12},{12,8},{1,5},{5,1},{9,13},{13,9},{2,6},{6,2},{1... | collective-permute-start | bytes 1327112 | tf_op jit(solution)/shard_map/ppermute | solution.py:104
  21.8 8.5 %collective-permute-start.5 = (bf16[288,768]{1,0:T(8,128)(2,1)S(1)}, bf16[288,768]{1,0:T(8,128)(2,1)S(1)}, u32[]{:S(2)}, u32[]{:S(2)}) collective-permute-start(bf16[288,768]{1,0:T(8,128)(2,1)S(1)} %add_convert_fusion.1), channel_id=1, source_target_pairs={{0,1},{1,0},{2,3},{3,2},{4,8},{5,9},{6,10},{7,11},{8,4},{9,5},{10,... | collective-permute-start | bytes 1327112 | tf_op jit(solution)/shard_map/ppermute | solution.py:107
  30.3 1.4 %copy-start.9 = (bf16[128,6144]{1,0:T(8,128)(2,1)S(1)}, bf16[128,6144]{1,0:T(8,128)(2,1)}, u32[]{:S(2)}) copy-start(bf16[128,6144]{1,0:T(8,128)(2,1)} %param.17) | copy-start | bytes 4718596
  30.3 12.3 %collective-permute-start.8 = (bf16[256,768]{1,0:T(8,128)(2,1)S(1)}, bf16[256,768]{1,0:T(8,128)(2,1)S(1)}, u32[]{:S(2)}, u32[]{:S(2)}) collective-permute-start(bf16[256,768]{1,0:T(8,128)(2,1)S(1)} %add_convert_fusion.7), channel_id=1, source_target_pairs={{0,1},{1,0},{2,3},{3,2},{4,8},{5,9},{6,10},{7,11},{8,4},{9,5},{10,... | collective-permute-start | bytes 1179656 | tf_op jit(solution)/shard_map/ppermute | solution.py:107
  32.3 18.2 %collective-permute-start.6 = (bf16[256,768]{1,0:T(8,128)(2,1)S(1)}, bf16[256,768]{1,0:T(8,128)(2,1)S(1)}, u32[]{:S(2)}, u32[]{:S(2)}) collective-permute-start(bf16[256,768]{1,0:T(8,128)(2,1)S(1)} %maximum_select_fusion.after_ref), channel_id=1, source_target_pairs={{0,4},{4,0},{8,12},{12,8},{1,5},{5,1},{9,13},{13,9},{2,6},{6,2},{1... | collective-permute-start | bytes 1179656 | tf_op jit(solution)/shard_map/ppermute | solution.py:104
  42.4 8.3 %collective-permute-start.9 = (bf16[288,768]{1,0:T(8,128)(2,1)S(1)}, bf16[288,768]{1,0:T(8,128)(2,1)S(1)}, u32[]{:S(2)}, u32[]{:S(2)}) collective-permute-start(bf16[288,768]{1,0:T(8,128)(2,1)S(1)} %add_convert_fusion), channel_id=1, source_target_pairs={{0,1},{1,0},{2,3},{3,2},{4,8},{5,9},{6,10},{7,11},{8,4},{9,5},{10,... | collective-permute-start | bytes 1327112 | tf_op jit(solution)/shard_map/ppermute | solution.py:107
  43.3 13.6 %collective-permute-start.10 = (bf16[256,768]{1,0:T(8,128)(2,1)S(1)}, bf16[256,768]{1,0:T(8,128)(2,1)S(1)}, u32[]{:S(2)}, u32[]{:S(2)}) collective-permute-start(bf16[256,768]{1,0:T(8,128)(2,1)S(1)} %get-tuple-element.156.after_ref), channel_id=1, source_target_pairs={{0,4},{4,0},{8,12},{12,8},{1,5},{5,1},{9,13},{13,9},{2,6},{6,2},{1... | collective-permute-start | bytes 1179656 | tf_op jit(solution)/shard_map/ppermute | solution.py:104
  50.6 6.5 %collective-permute-start.11 = (bf16[256,768]{1,0:T(8,128)(2,1)S(1)}, bf16[256,768]{1,0:T(8,128)(2,1)S(1)}, u32[]{:S(2)}, u32[]{:S(2)}) collective-permute-start(bf16[256,768]{1,0:T(8,128)(2,1)S(1)} %add_convert_fusion.6), channel_id=1, source_target_pairs={{0,1},{1,0},{2,3},{3,2},{4,8},{5,9},{6,10},{7,11},{8,4},{9,5},{10,... | collective-permute-start | bytes 1179656 | tf_op jit(solution)/shard_map/ppermute | solution.py:107
  51.5 15.8 %collective-permute-start.12 = (bf16[256,768]{1,0:T(8,128)(2,1)S(1)}, bf16[256,768]{1,0:T(8,128)(2,1)S(1)}, u32[]{:S(2)}, u32[]{:S(2)}) collective-permute-start(bf16[256,768]{1,0:T(8,128)(2,1)S(1)} %get-tuple-element.152.after_ref), channel_id=1, source_target_pairs={{0,4},{4,0},{8,12},{12,8},{1,5},{5,1},{9,13},{13,9},{2,6},{6,2},{1... | collective-permute-start | bytes 1179656 | tf_op jit(solution)/shard_map/ppermute | solution.py:104
  57.1 10.5 %collective-permute-start.13 = (bf16[256,768]{1,0:T(8,128)(2,1)S(1)}, bf16[256,768]{1,0:T(8,128)(2,1)S(1)}, u32[]{:S(2)}, u32[]{:S(2)}) collective-permute-start(bf16[256,768]{1,0:T(8,128)(2,1)S(1)} %add_convert_fusion.5), channel_id=1, source_target_pairs={{0,1},{1,0},{2,3},{3,2},{4,8},{5,9},{6,10},{7,11},{8,4},{9,5},{10,... | collective-permute-start | bytes 1179656 | tf_op jit(solution)/shard_map/ppermute | solution.py:107
  58.1 20.9 %collective-permute-start.14 = (bf16[256,768]{1,0:T(8,128)(2,1)S(1)}, bf16[256,768]{1,0:T(8,128)(2,1)S(1)}, u32[]{:S(2)}, u32[]{:S(2)}) collective-permute-start(bf16[256,768]{1,0:T(8,128)(2,1)S(1)} %get-tuple-element.144.after_ref), channel_id=1, source_target_pairs={{0,4},{4,0},{8,12},{12,8},{1,5},{5,1},{9,13},{13,9},{2,6},{6,2},{1... | collective-permute-start | bytes 1179656 | tf_op jit(solution)/shard_map/ppermute | solution.py:104
  67.5 11.7 %collective-permute-start.15 = (bf16[256,768]{1,0:T(8,128)(2,1)S(1)}, bf16[256,768]{1,0:T(8,128)(2,1)S(1)}, u32[]{:S(2)}, u32[]{:S(2)}) collective-permute-start(bf16[256,768]{1,0:T(8,128)(2,1)S(1)} %add_convert_fusion.4), channel_id=1, source_target_pairs={{0,1},{1,0},{2,3},{3,2},{4,8},{5,9},{6,10},{7,11},{8,4},{9,5},{10,... | collective-permute-start | bytes 1179656 | tf_op jit(solution)/shard_map/ppermute | solution.py:107
  68.3 13.1 %collective-permute-start.16 = (bf16[256,768]{1,0:T(8,128)(2,1)S(1)}, bf16[256,768]{1,0:T(8,128)(2,1)S(1)}, u32[]{:S(2)}, u32[]{:S(2)}) collective-permute-start(bf16[256,768]{1,0:T(8,128)(2,1)S(1)} %get-tuple-element.138.after_ref), channel_id=1, source_target_pairs={{0,4},{4,0},{8,12},{12,8},{1,5},{5,1},{9,13},{13,9},{2,6},{6,2},{1... | collective-permute-start | bytes 1179656 | tf_op jit(solution)/shard_map/ppermute | solution.py:104
  77.0 1.4 %copy-start.3 = (bf16[6144,128]{1,0:T(8,128)(2,1)S(1)}, bf16[6144,128]{1,0:T(8,128)(2,1)}, u32[]{:S(2)}) copy-start(bf16[6144,128]{1,0:T(8,128)(2,1)} %param.20) | copy-start | bytes 4718596
  79.1 12.1 %collective-permute-start.17 = (bf16[256,768]{1,0:T(8,128)(2,1)S(1)}, bf16[256,768]{1,0:T(8,128)(2,1)S(1)}, u32[]{:S(2)}, u32[]{:S(2)}) collective-permute-start(bf16[256,768]{1,0:T(8,128)(2,1)S(1)} %add_convert_fusion.3), channel_id=1, source_target_pairs={{0,1},{1,0},{2,3},{3,2},{4,8},{5,9},{6,10},{7,11},{8,4},{9,5},{10,... | collective-permute-start | bytes 1179656 | tf_op jit(solution)/shard_map/ppermute | solution.py:107
  81.5 13.9 %collective-permute-start.19 = (bf16[256,768]{1,0:T(8,128)(2,1)S(1)}, bf16[256,768]{1,0:T(8,128)(2,1)S(1)}, u32[]{:S(2)}, u32[]{:S(2)}) collective-permute-start(bf16[256,768]{1,0:T(8,128)(2,1)S(1)} %add_convert_fusion.2), channel_id=1, source_target_pairs={{0,1},{1,0},{2,3},{3,2},{4,8},{5,9},{6,10},{7,11},{8,4},{9,5},{10,... | collective-permute-start | bytes 1179656 | tf_op jit(solution)/shard_map/ppermute | solution.py:107
  81.6 12.0 %collective-permute-start.20 = (bf16[256,768]{1,0:T(8,128)(2,1)S(1)}, bf16[256,768]{1,0:T(8,128)(2,1)S(1)}, u32[]{:S(2)}, u32[]{:S(2)}) collective-permute-start(bf16[256,768]{1,0:T(8,128)(2,1)S(1)} %pad_maximum_fusion.11.after_ref), channel_id=1, source_target_pairs={{0,4},{4,0},{8,12},{12,8},{1,5},{5,1},{9,13},{13,9},{2,6},{6,2},{1... | collective-permute-start | bytes 1179656 | tf_op jit(solution)/shard_map/ppermute | solution.py:104
  91.9 11.6 %collective-permute-start.18 = (bf16[256,768]{1,0:T(8,128)(2,1)S(1)}, bf16[256,768]{1,0:T(8,128)(2,1)S(1)}, u32[]{:S(2)}, u32[]{:S(2)}) collective-permute-start(bf16[256,768]{1,0:T(8,128)(2,1)S(1)} %pad_maximum_fusion.13), channel_id=1, source_target_pairs={{0,4},{4,0},{8,12},{12,8},{1,5},{5,1},{9,13},{13,9},{2,6},{6,2},{1... | collective-permute-start | bytes 1179656 | tf_op jit(solution)/shard_map/ppermute | solution.py:104
  95.6 2.7 %collective-permute-start.22 = (bf16[64,2688]{1,0:T(8,128)(2,1)S(1)}, bf16[64,2688]{1,0:T(8,128)(2,1)S(1)}, u32[]{:S(2)}, u32[]{:S(2)}) collective-permute-start(bf16[64,2688]{1,0:T(8,128)(2,1)S(1)} %fusion.47), channel_id=1, source_target_pairs={{0,1},{1,0},{2,3},{3,2},{4,5},{5,4},{6,7},{7,6},{8,9},{9,8},{10,11... | collective-permute-start | bytes 1032200 | tf_op jit(solution)/shard_map/ppermute | solution.py:101
  96.2 13.8 %collective-permute-start.21 = (bf16[256,768]{1,0:T(8,128)(2,1)S(1)}, bf16[256,768]{1,0:T(8,128)(2,1)S(1)}, u32[]{:S(2)}, u32[]{:S(2)}) collective-permute-start(bf16[256,768]{1,0:T(8,128)(2,1)S(1)} %pad_maximum_fusion.18), channel_id=1, source_target_pairs={{0,4},{4,0},{8,12},{12,8},{1,5},{5,1},{9,13},{13,9},{2,6},{6,2},{1... | collective-permute-start | bytes 1179656 | tf_op jit(solution)/shard_map/ppermute | solution.py:104
  98.4 13.5 %collective-permute-start.23 = (bf16[64,2688]{1,0:T(8,128)(2,1)S(1)}, bf16[64,2688]{1,0:T(8,128)(2,1)S(1)}, u32[]{:S(2)}, u32[]{:S(2)}) collective-permute-start(bf16[64,2688]{1,0:T(8,128)(2,1)S(1)} %fusion.45), channel_id=1, source_target_pairs={{0,2},{1,3},{2,0},{3,1},{4,6},{5,7},{6,4},{7,5},{8,10},{9,11},{10,... | collective-permute-start | bytes 1032200 | tf_op jit(solution)/shard_map/ppermute | solution.py:101
  113.4 1.9 %copy-start.7 = (f32[2560]{0:T(1024)S(1)}, f32[2560]{0:T(1024)}, u32[]{:S(2)}) copy-start(f32[2560]{0:T(1024)} %param.19) | copy-start | bytes 30724
  113.4 1.7 %collective-permute-start.24 = (bf16[64,2688]{1,0:T(8,128)(2,1)S(1)}, bf16[64,2688]{1,0:T(8,128)(2,1)S(1)}, u32[]{:S(2)}, u32[]{:S(2)}) collective-permute-start(bf16[64,2688]{1,0:T(8,128)(2,1)S(1)} %fusion.46), channel_id=1, source_target_pairs={{0,1},{1,0},{2,3},{3,2},{4,5},{5,4},{6,7},{7,6},{8,9},{9,8},{10,11... | collective-permute-start | bytes 1032200 | tf_op jit(solution)/shard_map/ppermute | solution.py:101

commit v17 on v16

--- a/solution.py
+++ b/solution.py
@@ -266,14 +266,17 @@
             if t == 1:
                 whole = tie((gathered_near, gathered_far), last)
                 gathered = jnp.concatenate(whole, axis=0)
-            if LAG <= t < LAG + 2 * early:
-                load_second(t - LAG)
+            if t < early:
+                load(early + t)
             if 1 <= t <= early:
-                load(early + t - 1)
                 first_late(2 * early + t - 1, gathered)
+            if LAG - 1 <= t < LAG + early:
+                load_second(t - LAG + 1)
             if early <= unit < 2 * early:
                 second("near", unfold(state(unit - early)), unit - early)
                 second("far", unfold(state(unit)), unit - early)
+                if unit == early:
+                    load_second(2 * early - 1)
             elif unit == 3 * early - 1:
                 across = (ours + come.astype(F32)).astype(BF16)
                 across = col_swap(across, 2)

time: 117 us -> 117 us (level)
  waiting for transfers between devices: 23.3 us -> 19.7 us
  starting transfers between devices: 32 us -> 35.3 us
    ppermute x11, waiting for transfers between devices: 20.3 us -> 16.7 us  [end_swap(): return lax.ppermute(value, 'row', [(i, i ^ 1) for i in range(n_row)])]
    ppermute x11, starting transfers between devices: 27.3 us -> 30.5 us  [end_swap(): return lax.ppermute(value, 'row', [(i, i ^ 1) for i in range(n_row)])]
  transfers between devices with their start and end apart: 25 -> 25, of which waited for: 7 -> 8; matrix products, arithmetic and copies ran while one was open for 25% -> 25% of each run, Pallas kernels for 22% -> 22%
where the time goes in v17:
time: 117 us; the launch traced here: 116 us
  starting transfers between devices  35.3 us (30%)
  matrix products  26.4 us (23%)
  Pallas kernels  26 us (22%)
  waiting for transfers between devices  19.7 us (17%)
  other arithmetic  3.96 us (3%)
  local copies, waits for them, and re-layouts  3.61 us (3%)
  between operations  1.29 us (1%)
    ppermute x11, starting transfers between devices, end_swap(): return lax.ppermute(value, 'row', [(i, i ^ 1) for i in range(n_row)])  30.5 us
    dot_general x33, matrix products, dot(): return jnp.dot(left, right, preferred_element_type=F32)  26.4 us
    pallas_call x8, Pallas kernels, load_part(): pl.pallas_call(functools.partial(load_kernel, part=part), in_specs=[pl.Bl...  26 us
    ppermute x11, waiting for transfers between devices, end_swap(): return lax.ppermute(value, 'row', [(i, i ^ 1) for i in range(n_row)])  16.7 us
    ppermute x6, starting transfers between devices, col_swap(): return lax.ppermute(value, 'col', [(i, i ^ flip) for i in range(n_col)])  4.19 us
    ppermute x6, waiting for transfers between devices, col_swap(): return lax.ppermute(value, 'col', [(i, i ^ flip) for i in range(n_col)])  3.02 us
  transfers between devices with their start and end apart: 25, of which 8 were waited for; matrix products, arithmetic and copies ran while one was open for 25% of the time, Pallas kernels for 22%

profile of v17, /device:TPU:0, one launch (start us, length us, event | category | flops | bytes accessed | tf_op | source)
XLA Modules:
  0.0 116.4 jit_solution(6960451858621574519)
XLA Ops:
  0.0 2.9 %collective-permute-start = (bf16[64,2560]{1,0:T(8,128)(2,1)}, bf16[64,2560]{1,0:T(8,128)(2,1)S(1)}, u32[]{:S(2)}, u32[]{:S(2)}) collective-permute-start(bf16[64,2560]{1,0:T(8,128)(2,1)} %param.11), channel_id=1, source_target_pairs={{0,2},{1,3},{2,0},{3,1},{4,6},{5,7},{6,4},{7,5},{8,10},{9,11},{10,... | collective-permute-start | bytes 983048 | tf_op jit(solution)/shard_map/ppermute | solution.py:101
  3.0 0.7 copy-done.1
  3.6 3.3 %shard_map.109 = bf16[2560,1536]{1,0:T(8,128)(2,1)S(1)} custom-call(bf16[2560,6144]{1,0:T(8,128)(2,1)} %w_hbm.11, s32[4]{0:T(128)S(1)} %copy-done.1), custom_call_target="tpu_custom_call" | custom-call | bytes 1000 | tf_op jit(solution)/shard_map/pallas_call | solution.py:51
  7.0 0.3 convolution_convert_fusion.7
  7.4 1.2 %convolution_convert_fusion.5 = bf16[128,1536]{1,0:T(8,128)(2,1)S(1)} fusion(bf16[128,2560]{1,0:T(8,128)(2,1)S(1)} %constant_dynamic-update-slice_fusion.2, bf16[2560,1536]{1,0:T(8,128)(2,1)S(1)} %shard_map.109), kind=kOutput, calls=%fused_computation.19 | convolution fusion | flops 1006829568 | bytes 8912896 | tf_op jit(solution)/shard_map/dot_general | solution.py:36
  8.7 1.6 %collective-permute-start.3 = (bf16[288,768]{1,0:T(8,128)(2,1)S(1)}, bf16[288,768]{1,0:T(8,128)(2,1)S(1)}, u32[]{:S(2)}, u32[]{:S(2)}) collective-permute-start(bf16[288,768]{1,0:T(8,128)(2,1)S(1)} %pad_maximum_fusion.2.after_ref), channel_id=1, source_target_pairs={{0,4},{4,0},{8,12},{12,8},{1,5},{5,1},{9,13},{13,9},{2,6},{6,2},{1... | collective-permute-start | bytes 1327112 | tf_op jit(solution)/shard_map/ppermute | solution.py:104
  10.4 3.2 %shard_map.110 = bf16[2560,1536]{1,0:T(8,128)(2,1)S(1)} custom-call(bf16[2560,6144]{1,0:T(8,128)(2,1)} %w_hbm.11, bf16[288,768]{1,0:T(8,128)(2,1)S(1)} %pad_maximum_fusion.2.after_ref), custom_call_target="tpu_custom_call" | custom-call | bytes 1000 | tf_op jit(solution)/shard_map/pallas_call | solution.py:51
  13.6 1.2 %convolution_convert_fusion.4 = bf16[128,1536]{1,0:T(8,128)(2,1)S(1)} fusion(bf16[128,2560]{1,0:T(8,128)(2,1)S(1)} %constant_dynamic-update-slice_fusion.2, bf16[2560,1536]{1,0:T(8,128)(2,1)S(1)} %shard_map.110), kind=kOutput, calls=%fused_computation.18 | convolution fusion | flops 1006829568 | bytes 8912896 | tf_op jit(solution)/shard_map/dot_general | solution.py:36
  14.9 0.5 collective-permute-start.4
  15.9 0.3 collective-permute-start.1
  16.3 1.4 %collective-permute-done.1 = bf16[64,2560]{1,0:T(8,128)(2,1)S(1)} collective-permute-done((bf16[64,2560]{1,0:T(8,128)(2,1)S(1)}, bf16[64,2560]{1,0:T(8,128)(2,1)S(1)}, u32[]{:S(2)}, u32[]{:S(2)}) %collective-permute-start.1) | collective-permute-done | bytes 327712 | tf_op jit(solution)/shard_map/ppermute | solution.py:101
  17.7 0.3 convolution_convert_fusion.6
  18.0 1.2 %convolution_convert_fusion.3 = bf16[128,1536]{1,0:T(8,128)(2,1)S(1)} fusion(bf16[128,2560]{1,0:T(8,128)(2,1)S(1)} %constant_dynamic-update-slice_fusion, bf16[2560,1536]{1,0:T(8,128)(2,1)S(1)} %shard_map.109), kind=kOutput, calls=%fused_computation.17 | convolution fusion | flops 1006829568 | bytes 8912896 | tf_op jit(solution)/shard_map/dot_general | solution.py:36
  19.3 1.6 %collective-permute-start.7 = (bf16[288,768]{1,0:T(8,128)(2,1)S(1)}, bf16[288,768]{1,0:T(8,128)(2,1)S(1)}, u32[]{:S(2)}, u32[]{:S(2)}) collective-permute-start(bf16[288,768]{1,0:T(8,128)(2,1)S(1)} %pad_maximum_fusion.3), channel_id=1, source_target_pairs={{0,4},{4,0},{8,12},{12,8},{1,5},{5,1},{9,13},{13,9},{2,6},{6,2},{1... | collective-permute-start | bytes 1327112 | tf_op jit(solution)/shard_map/ppermute | solution.py:104
  20.9 0.8 collective-permute-done.3
  21.9 1.2 %convolution_convert_fusion.2 = bf16[128,1536]{1,0:T(8,128)(2,1)S(1)} fusion(bf16[128,2560]{1,0:T(8,128)(2,1)S(1)} %constant_dynamic-update-slice_fusion, bf16[2560,1536]{1,0:T(8,128)(2,1)S(1)} %shard_map.110), kind=kOutput, calls=%fused_computation.16 | convolution fusion | flops 1006829568 | bytes 8912896 | tf_op jit(solution)/shard_map/dot_general | solution.py:36
  23.2 3.2 %shard_map.111 = bf16[2560,1536]{1,0:T(8,128)(2,1)S(1)} custom-call(bf16[2560,6144]{1,0:T(8,128)(2,1)} %w_hbm.11, bf16[256,768]{1,0:T(8,128)(2,1)S(1)} %pad_maximum_fusion.5.after_ref), custom_call_target="tpu_custom_call" | custom-call | bytes 1000 | tf_op jit(solution)/shard_map/pallas_call | solution.py:51
  26.5 3.7 %collective-permute-done.4 = bf16[256,768]{1,0:T(8,128)(2,1)S(1)} collective-permute-done((bf16[256,768]{1,0:T(8,128)(2,1)S(1)}, bf16[256,768]{1,0:T(8,128)(2,1)S(1)}, u32[]{:S(2)}, u32[]{:S(2)}) %collective-permute-start.4) | collective-permute-done | bytes 393248 | tf_op jit(solution)/shard_map/ppermute | solution.py:104
  30.6 1.1 copy-done.9
  31.7 0.4 fusion.4
  32.3 4.5 %collective-permute-start.6 = (bf16[256,768]{1,0:T(8,128)(2,1)S(1)}, bf16[256,768]{1,0:T(8,128)(2,1)S(1)}, u32[]{:S(2)}, u32[]{:S(2)}) collective-permute-start(bf16[256,768]{1,0:T(8,128)(2,1)S(1)} %maximum_select_fusion.after_ref), channel_id=1, source_target_pairs={{0,4},{4,0},{8,12},{12,8},{1,5},{5,1},{9,13},{13,9},{2,6},{6,2},{1... | collective-permute-start | bytes 1179656 | tf_op jit(solution)/shard_map/ppermute | solution.py:104
  36.8 3.2 %shard_map.112 = bf16[2560,1536]{1,0:T(8,128)(2,1)S(1)} custom-call(bf16[2560,6144]{1,0:T(8,128)(2,1)} %w_hbm.11, bf16[256,768]{1,0:T(8,128)(2,1)S(1)} %maximum_select_fusion.after_ref), custom_call_target="tpu_custom_call" | custom-call | bytes 1000 | tf_op jit(solution)/shard_map/pallas_call | solution.py:51
  40.1 2.2 %convolution_convert_fusion.1 = bf16[256,1536]{1,0:T(8,128)(2,1)S(1)} fusion(bf16[256,2560]{1,0:T(8,128)(2,1)S(1)} %constant_dynamic-update-slice_fusion.4, bf16[2560,1536]{1,0:T(8,128)(2,1)S(1)} %shard_map.111), kind=kOutput, calls=%fused_computation.7 | convolution fusion | flops 2013659136 | bytes 9961472 | tf_op jit(solution)/shard_map/dot_general | solution.py:36
  42.8 0.4 fusion.9
  43.4 1.6 %collective-permute-start.10 = (bf16[256,768]{1,0:T(8,128)(2,1)S(1)}, bf16[256,768]{1,0:T(8,128)(2,1)S(1)}, u32[]{:S(2)}, u32[]{:S(2)}) collective-permute-start(bf16[256,768]{1,0:T(8,128)(2,1)S(1)} %get-tuple-element.158), channel_id=1, source_target_pairs={{0,4},{4,0},{8,12},{12,8},{1,5},{5,1},{9,13},{13,9},{2,6},{6,2},{1... | collective-permute-start | bytes 1179656 | tf_op jit(solution)/shard_map/ppermute | solution.py:104
  45.0 2.2 %convolution_convert_fusion.after_ref = bf16[256,1536]{1,0:T(8,128)(2,1)S(1)} fusion(bf16[256,2560]{1,0:T(8,128)(2,1)S(1)} %constant_dynamic-update-slice_fusion.4, bf16[2560,1536]{1,0:T(8,128)(2,1)S(1)} %shard_map.112), kind=kOutput, calls=%fused_computation.6 | convolution fusion | flops 2013659136 | bytes 9961472 | tf_op jit(solution)/shard_map/dot_general | solution.py:36
  47.2 3.2 %shard_map.113 = bf16[1536,2560]{1,0:T(8,128)(2,1)S(1)} custom-call(bf16[6144,2560]{1,0:T(8,128)(2,1)} %w_hbm.15, bf16[256,1536]{1,0:T(8,128)(2,1)S(1)} %convolution_convert_fusion.after_ref), custom_call_target="tpu_custom_call" | custom-call | bytes 1000 | tf_op jit(solution)/shard_map/pallas_call | solution.py:51
  51.0 0.4 fusion.14
  51.6 2.1 %collective-permute-start.12 = (bf16[256,768]{1,0:T(8,128)(2,1)S(1)}, bf16[256,768]{1,0:T(8,128)(2,1)S(1)}, u32[]{:S(2)}, u32[]{:S(2)}) collective-permute-start(bf16[256,768]{1,0:T(8,128)(2,1)S(1)} %get-tuple-element.154.after_ref), channel_id=1, source_target_pairs={{0,4},{4,0},{8,12},{12,8},{1,5},{5,1},{9,13},{13,9},{2,6},{6,2},{1... | collective-permute-start | bytes 1179656 | tf_op jit(solution)/shard_map/ppermute | solution.py:104
  53.7 3.2 %shard_map.114 = bf16[1536,2560]{1,0:T(8,128)(2,1)S(1)} custom-call(bf16[6144,2560]{1,0:T(8,128)(2,1)} %w_hbm.15, bf16[256,768]{1,0:T(8,128)(2,1)S(1)} %get-tuple-element.154.after_ref), custom_call_target="tpu_custom_call" | custom-call | bytes 1000 | tf_op jit(solution)/shard_map/pallas_call | solution.py:51
  57.6 0.4 fusion.19
  58.2 6.0 %collective-permute-start.14 = (bf16[256,768]{1,0:T(8,128)(2,1)S(1)}, bf16[256,768]{1,0:T(8,128)(2,1)S(1)}, u32[]{:S(2)}, u32[]{:S(2)}) collective-permute-start(bf16[256,768]{1,0:T(8,128)(2,1)S(1)} %get-tuple-element.146.after_ref), channel_id=1, source_target_pairs={{0,4},{4,0},{8,12},{12,8},{1,5},{5,1},{9,13},{13,9},{2,6},{6,2},{1... | collective-permute-start | bytes 1179656 | tf_op jit(solution)/shard_map/ppermute | solution.py:104
  64.1 3.2 %shard_map.115 = bf16[1536,2560]{1,0:T(8,128)(2,1)S(1)} custom-call(bf16[6144,2560]{1,0:T(8,128)(2,1)} %w_hbm.15, bf16[256,768]{1,0:T(8,128)(2,1)S(1)} %get-tuple-element.146.after_ref), custom_call_target="tpu_custom_call" | custom-call | bytes 1000 | tf_op jit(solution)/shard_map/pallas_call | solution.py:51
  67.8 0.4 fusion.24
  68.4 4.0 %collective-permute-start.16 = (bf16[256,768]{1,0:T(8,128)(2,1)S(1)}, bf16[256,768]{1,0:T(8,128)(2,1)S(1)}, u32[]{:S(2)}, u32[]{:S(2)}) collective-permute-start(bf16[256,768]{1,0:T(8,128)(2,1)S(1)} %get-tuple-element.138), channel_id=1, source_target_pairs={{0,4},{4,0},{8,12},{12,8},{1,5},{5,1},{9,13},{13,9},{2,6},{6,2},{1... | collective-permute-start | bytes 1179656 | tf_op jit(solution)/shard_map/ppermute | solution.py:104
  72.5 1.2 %fusion.144 = f32[128,2560]{1,0:T(8,128)S(1)} fusion(bf16[128,1536]{1,0:T(8,128)(2,1)S(1)} %pad_maximum_fusion.10, bf16[1536,2560]{1,0:T(8,128)(2,1)S(1)} %shard_map.113), kind=kOutput, calls=%fused_computation.267 | convolution fusion | flops 1006632960 | bytes 9568256 | tf_op jit(solution)/shard_map/dot_general | solution.py:36
  73.9 1.2 %fusion.145 = f32[128,2560]{1,0:T(8,128)S(1)} fusion(bf16[128,1536]{1,0:T(8,128)(2,1)S(1)} %pad_maximum_fusion.11, bf16[1536,2560]{1,0:T(8,128)(2,1)S(1)} %shard_map.113), kind=kOutput, calls=%fused_computation.268 | convolution fusion | flops 1006632960 | bytes 9568256 | tf_op jit(solution)/shard_map/dot_general | solution.py:36
  75.3 0.3 fusion.56
  75.5 0.3 fusion.58
  75.8 3.2 %shard_map.116 = bf16[1536,2560]{1,0:T(8,128)(2,1)S(1)} custom-call(bf16[6144,2560]{1,0:T(8,128)(2,1)} %w_hbm.15, f32[8,128]{1,0:T(8,128)S(1)} %slice.507.after_ref), custom_call_target="tpu_custom_call" | custom-call | bytes 1000 | tf_op jit(solution)/shard_map/pallas_call | solution.py:51
  79.5 0.4 fusion.29
  80.0 1.4 %collective-permute-done.16 = bf16[256,768]{1,0:T(8,128)(2,1)S(1)} collective-permute-done((bf16[256,768]{1,0:T(8,128)(2,1)S(1)}, bf16[256,768]{1,0:T(8,128)(2,1)S(1)}, u32[]{:S(2)}, u32[]{:S(2)}) %collective-permute-start.16) | collective-permute-done | bytes 393248 | tf_op jit(solution)/shard_map/ppermute | solution.py:104
  81.6 3.2 %collective-permute-start.20 = (bf16[256,768]{1,0:T(8,128)(2,1)S(1)}, bf16[256,768]{1,0:T(8,128)(2,1)S(1)}, u32[]{:S(2)}, u32[]{:S(2)}) collective-permute-start(bf16[256,768]{1,0:T(8,128)(2,1)S(1)} %pad_maximum_fusion.12), channel_id=1, source_target_pairs={{0,4},{4,0},{8,12},{12,8},{1,5},{5,1},{9,13},{13,9},{2,6},{6,2},{1... | collective-permute-start | bytes 1179656 | tf_op jit(solution)/shard_map/ppermute | solution.py:104
  85.0 1.3 %convolution_add_fusion.5 = f32[128,2560]{1,0:T(8,128)S(1)} fusion(f32[128,2560]{1,0:T(8,128)S(1)} %fusion.144, bf16[128,1536]{1,0:T(8,128)(2,1)S(1)} %pad_maximum_fusion.13, bf16[1536,2560]{1,0:T(8,128)(2,1)S(1)} %shard_map.114), kind=kOutput, calls=%fused_computation.5 | convolution fusion | flops 1006960640 | bytes 10878976 | tf_op jit(solution)/shard_map/dot_general | solution.py:36
  86.4 1.2 %convolution_add_fusion.4 = f32[128,2560]{1,0:T(8,128)S(1)} fusion(f32[128,2560]{1,0:T(8,128)S(1)} %fusion.145, bf16[128,1536]{1,0:T(8,128)(2,1)S(1)} %pad_maximum_fusion.15, bf16[1536,2560]{1,0:T(8,128)(2,1)S(1)} %shard_map.114), kind=kOutput, calls=%fused_computation.4 | convolution fusion | flops 1006960640 | bytes 10878976 | tf_op jit(solution)/shard_map/dot_general | solution.py:36
  87.9 0.3 convolution_add_fusion.19
  88.3 0.4 fusion.34
  88.8 3.3 %collective-permute-start.18 = (bf16[256,768]{1,0:T(8,128)(2,1)S(1)}, bf16[256,768]{1,0:T(8,128)(2,1)S(1)}, u32[]{:S(2)}, u32[]{:S(2)}) collective-permute-start(bf16[256,768]{1,0:T(8,128)(2,1)S(1)} %pad_maximum_fusion.14), channel_id=1, source_target_pairs={{0,4},{4,0},{8,12},{12,8},{1,5},{5,1},{9,13},{13,9},{2,6},{6,2},{1... | collective-permute-start | bytes 1179656 | tf_op jit(solution)/shard_map/ppermute | solution.py:104
  92.2 1.3 %convolution_add_fusion.3 = f32[128,2560]{1,0:T(8,128)S(1)} fusion(f32[128,2560]{1,0:T(8,128)S(1)} %convolution_add_fusion.4, bf16[128,1536]{1,0:T(8,128)(2,1)S(1)} %pad_maximum_fusion.16, bf16[1536,2560]{1,0:T(8,128)(2,1)S(1)} %shard_map.115), kind=kOutput, calls=%fused_computation.3 | convolution fusion | flops 1006960640 | bytes 10878976 | tf_op jit(solution)/shard_map/dot_general | solution.py:36
  93.5 0.3 convolution_add_fusion.18
  93.8 1.1 collective-permute-done.20
  95.1 1.3 %convolution_add_fusion.2 = f32[128,2560]{1,0:T(8,128)S(1)} fusion(f32[128,2560]{1,0:T(8,128)S(1)} %convolution_add_fusion.3, bf16[128,1536]{1,0:T(8,128)(2,1)S(1)} %pad_maximum_fusion.17, bf16[1536,2560]{1,0:T(8,128)(2,1)S(1)} %shard_map.116), kind=kOutput, calls=%fused_computation.2 | convolution fusion | flops 1006960640 | bytes 10878976 | tf_op jit(solution)/shard_map/dot_general | solution.py:36
  96.3 0.3 convolution_add_fusion.17
  96.9 0.4 fusion.39
  97.4 2.1 %collective-permute-start.21 = (bf16[256,768]{1,0:T(8,128)(2,1)S(1)}, bf16[256,768]{1,0:T(8,128)(2,1)S(1)}, u32[]{:S(2)}, u32[]{:S(2)}) collective-permute-start(bf16[256,768]{1,0:T(8,128)(2,1)S(1)} %pad_maximum_fusion.18), channel_id=1, source_target_pairs={{0,4},{4,0},{8,12},{12,8},{1,5},{5,1},{9,13},{13,9},{2,6},{6,2},{1... | collective-permute-start | bytes 1179656 | tf_op jit(solution)/shard_map/ppermute | solution.py:104
  99.6 0.8 collective-permute-start.23
  100.4 1.9 %collective-permute-done.18 = bf16[256,768]{1,0:T(8,128)(2,1)S(1)} collective-permute-done((bf16[256,768]{1,0:T(8,128)(2,1)S(1)}, bf16[256,768]{1,0:T(8,128)(2,1)S(1)}, u32[]{:S(2)}, u32[]{:S(2)}) %collective-permute-start.18) | collective-permute-done | bytes 393248 | tf_op jit(solution)/shard_map/ppermute | solution.py:104
  102.3 7.7 %collective-permute-done.21 = bf16[256,768]{1,0:T(8,128)(2,1)S(1)} collective-permute-done((bf16[256,768]{1,0:T(8,128)(2,1)S(1)}, bf16[256,768]{1,0:T(8,128)(2,1)S(1)}, u32[]{:S(2)}, u32[]{:S(2)}) %collective-permute-start.21) | collective-permute-done | bytes 393248 | tf_op jit(solution)/shard_map/ppermute | solution.py:104
  110.4 1.3 %convolution_add_fusion.1 = f32[128,2560]{1,0:T(8,128)S(1)} fusion(f32[128,2560]{1,0:T(8,128)S(1)} %convolution_add_fusion.5, bf16[128,1536]{1,0:T(8,128)(2,1)S(1)} %pad_maximum_fusion.19, bf16[1536,2560]{1,0:T(8,128)(2,1)S(1)} %shard_map.115), kind=kOutput, calls=%fused_computation.1 | convolution fusion | flops 1006960640 | bytes 10878976 | tf_op jit(solution)/shard_map/dot_general | solution.py:36
  111.7 0.3 convolution_add_fusion.15
  112.0 0.3 convolution_add_fusion.14
  112.2 1.3 %convolution_add_fusion = f32[128,2560]{1,0:T(8,128)S(1)} fusion(f32[128,2560]{1,0:T(8,128)S(1)} %convolution_add_fusion.1, bf16[128,1536]{1,0:T(8,128)(2,1)S(1)} %pad_maximum_fusion.20, bf16[1536,2560]{1,0:T(8,128)(2,1)S(1)} %shard_map.116), kind=kOutput, calls=%fused_computation | convolution fusion | flops 1006960640 | bytes 10878976 | tf_op jit(solution)/shard_map/dot_general | solution.py:36
  113.6 1.6 %collective-permute-done.24 = bf16[64,2688]{1,0:T(8,128)(2,1)S(1)} collective-permute-done((bf16[64,2688]{1,0:T(8,128)(2,1)S(1)}, bf16[64,2688]{1,0:T(8,128)(2,1)S(1)}, u32[]{:S(2)}, u32[]{:S(2)}) %collective-permute-start.24) | collective-permute-done | bytes 344096 | tf_op jit(solution)/shard_map/ppermute | solution.py:101
  115.4 1.0 fusion.49
  (155 shorter events, 6.8 us)
Async XLA Ops:
  0.0 115.4 %copy-start = (bf16[128,2560]{1,0:T(8,128)(2,1)S(1)}, bf16[128,2560]{1,0:T(8,128)(2,1)}, u32[]{:S(2)}) copy-start(bf16[128,2560]{1,0:T(8,128)(2,1)} %param.21) | copy-start | bytes 1966084
  0.0 15.9 %collective-permute-start = (bf16[64,2560]{1,0:T(8,128)(2,1)}, bf16[64,2560]{1,0:T(8,128)(2,1)S(1)}, u32[]{:S(2)}, u32[]{:S(2)}) collective-permute-start(bf16[64,2560]{1,0:T(8,128)(2,1)} %param.11), channel_id=1, source_target_pairs={{0,2},{1,3},{2,0},{3,1},{4,6},{5,7},{6,4},{7,5},{8,10},{9,11},{10,... | collective-permute-start | bytes 983048 | tf_op jit(solution)/shard_map/ppermute | solution.py:101
  2.9 4.0 %collective-permute-start.2 = (bf16[64,2560]{1,0:T(8,128)(2,1)}, bf16[64,2560]{1,0:T(8,128)(2,1)S(1)}, u32[]{:S(2)}, u32[]{:S(2)}) collective-permute-start(bf16[64,2560]{1,0:T(8,128)(2,1)} %param.11), channel_id=1, source_target_pairs={{0,1},{1,0},{2,3},{3,2},{4,5},{5,4},{6,7},{7,6},{8,9},{9,8},{10,11... | collective-permute-start | bytes 983048 | tf_op jit(solution)/shard_map/ppermute | solution.py:101
  2.9 0.7 copy-start.1
  3.6 3.3 %copy-start.5 = (bf16[64,2560]{1,0:T(8,128)(2,1)S(1)}, bf16[64,2560]{1,0:T(8,128)(2,1)}, u32[]{:S(2)}) copy-start(bf16[64,2560]{1,0:T(8,128)(2,1)} %param.11) | copy-start | bytes 983044
  3.6 3.4 %copy-start.4 = (bf16[2560,128]{1,0:T(8,128)(2,1)S(1)}, bf16[2560,128]{1,0:T(8,128)(2,1)}, u32[]{:S(2)}) copy-start(bf16[2560,128]{1,0:T(8,128)(2,1)} %param.16) | copy-start | bytes 1966084
  8.7 13.0 %collective-permute-start.3 = (bf16[288,768]{1,0:T(8,128)(2,1)S(1)}, bf16[288,768]{1,0:T(8,128)(2,1)S(1)}, u32[]{:S(2)}, u32[]{:S(2)}) collective-permute-start(bf16[288,768]{1,0:T(8,128)(2,1)S(1)} %pad_maximum_fusion.2.after_ref), channel_id=1, source_target_pairs={{0,4},{4,0},{8,12},{12,8},{1,5},{5,1},{9,13},{13,9},{2,6},{6,2},{1... | collective-permute-start | bytes 1327112 | tf_op jit(solution)/shard_map/ppermute | solution.py:104
  14.8 0.7 copy-start.2
  14.8 0.7 copy-start.8
  14.8 1.0 copy-start.6
  14.9 15.2 %collective-permute-start.4 = (bf16[256,768]{1,0:T(8,128)(2,1)S(1)}, bf16[256,768]{1,0:T(8,128)(2,1)S(1)}, u32[]{:S(2)}, u32[]{:S(2)}) collective-permute-start(bf16[256,768]{1,0:T(8,128)(2,1)S(1)} %pad_maximum_fusion.4), channel_id=1, source_target_pairs={{0,4},{4,0},{8,12},{12,8},{1,5},{5,1},{9,13},{13,9},{2,6},{6,2},{1... | collective-permute-start | bytes 1179656 | tf_op jit(solution)/shard_map/ppermute | solution.py:104
  15.9 1.7 %collective-permute-start.1 = (bf16[64,2560]{1,0:T(8,128)(2,1)S(1)}, bf16[64,2560]{1,0:T(8,128)(2,1)S(1)}, u32[]{:S(2)}, u32[]{:S(2)}) collective-permute-start(bf16[64,2560]{1,0:T(8,128)(2,1)S(1)} %collective-permute-done), channel_id=1, source_target_pairs={{0,1},{1,0},{2,3},{3,2},{4,5},{5,4},{6,7},{7,6},{8,9},{9,8},{10,11... | collective-permute-start | bytes 983048 | tf_op jit(solution)/shard_map/ppermute | solution.py:101
  19.3 23.0 %collective-permute-start.7 = (bf16[288,768]{1,0:T(8,128)(2,1)S(1)}, bf16[288,768]{1,0:T(8,128)(2,1)S(1)}, u32[]{:S(2)}, u32[]{:S(2)}) collective-permute-start(bf16[288,768]{1,0:T(8,128)(2,1)S(1)} %pad_maximum_fusion.3), channel_id=1, source_target_pairs={{0,4},{4,0},{8,12},{12,8},{1,5},{5,1},{9,13},{13,9},{2,6},{6,2},{1... | collective-permute-start | bytes 1327112 | tf_op jit(solution)/shard_map/ppermute | solution.py:104
  21.9 8.5 %collective-permute-start.5 = (bf16[288,768]{1,0:T(8,128)(2,1)S(1)}, bf16[288,768]{1,0:T(8,128)(2,1)S(1)}, u32[]{:S(2)}, u32[]{:S(2)}) collective-permute-start(bf16[288,768]{1,0:T(8,128)(2,1)S(1)} %add_convert_fusion.1), channel_id=1, source_target_pairs={{0,1},{1,0},{2,3},{3,2},{4,8},{5,9},{6,10},{7,11},{8,4},{9,5},{10,... | collective-permute-start | bytes 1327112 | tf_op jit(solution)/shard_map/ppermute | solution.py:107
  30.3 1.4 %copy-start.9 = (bf16[128,6144]{1,0:T(8,128)(2,1)S(1)}, bf16[128,6144]{1,0:T(8,128)(2,1)}, u32[]{:S(2)}) copy-start(bf16[128,6144]{1,0:T(8,128)(2,1)} %param.17) | copy-start | bytes 4718596
  30.3 12.3 %collective-permute-start.8 = (bf16[256,768]{1,0:T(8,128)(2,1)S(1)}, bf16[256,768]{1,0:T(8,128)(2,1)S(1)}, u32[]{:S(2)}, u32[]{:S(2)}) collective-permute-start(bf16[256,768]{1,0:T(8,128)(2,1)S(1)} %add_convert_fusion.7), channel_id=1, source_target_pairs={{0,1},{1,0},{2,3},{3,2},{4,8},{5,9},{6,10},{7,11},{8,4},{9,5},{10,... | collective-permute-start | bytes 1179656 | tf_op jit(solution)/shard_map/ppermute | solution.py:107
  32.3 18.3 %collective-permute-start.6 = (bf16[256,768]{1,0:T(8,128)(2,1)S(1)}, bf16[256,768]{1,0:T(8,128)(2,1)S(1)}, u32[]{:S(2)}, u32[]{:S(2)}) collective-permute-start(bf16[256,768]{1,0:T(8,128)(2,1)S(1)} %maximum_select_fusion.after_ref), channel_id=1, source_target_pairs={{0,4},{4,0},{8,12},{12,8},{1,5},{5,1},{9,13},{13,9},{2,6},{6,2},{1... | collective-permute-start | bytes 1179656 | tf_op jit(solution)/shard_map/ppermute | solution.py:104
  42.5 8.3 %collective-permute-start.9 = (bf16[288,768]{1,0:T(8,128)(2,1)S(1)}, bf16[288,768]{1,0:T(8,128)(2,1)S(1)}, u32[]{:S(2)}, u32[]{:S(2)}) collective-permute-start(bf16[288,768]{1,0:T(8,128)(2,1)S(1)} %add_convert_fusion), channel_id=1, source_target_pairs={{0,1},{1,0},{2,3},{3,2},{4,8},{5,9},{6,10},{7,11},{8,4},{9,5},{10,... | collective-permute-start | bytes 1327112 | tf_op jit(solution)/shard_map/ppermute | solution.py:107
  43.4 13.6 %collective-permute-start.10 = (bf16[256,768]{1,0:T(8,128)(2,1)S(1)}, bf16[256,768]{1,0:T(8,128)(2,1)S(1)}, u32[]{:S(2)}, u32[]{:S(2)}) collective-permute-start(bf16[256,768]{1,0:T(8,128)(2,1)S(1)} %get-tuple-element.158), channel_id=1, source_target_pairs={{0,4},{4,0},{8,12},{12,8},{1,5},{5,1},{9,13},{13,9},{2,6},{6,2},{1... | collective-permute-start | bytes 1179656 | tf_op jit(solution)/shard_map/ppermute | solution.py:104
  50.7 6.5 %collective-permute-start.11 = (bf16[256,768]{1,0:T(8,128)(2,1)S(1)}, bf16[256,768]{1,0:T(8,128)(2,1)S(1)}, u32[]{:S(2)}, u32[]{:S(2)}) collective-permute-start(bf16[256,768]{1,0:T(8,128)(2,1)S(1)} %add_convert_fusion.6), channel_id=1, source_target_pairs={{0,1},{1,0},{2,3},{3,2},{4,8},{5,9},{6,10},{7,11},{8,4},{9,5},{10,... | collective-permute-start | bytes 1179656 | tf_op jit(solution)/shard_map/ppermute | solution.py:107
  51.6 15.8 %collective-permute-start.12 = (bf16[256,768]{1,0:T(8,128)(2,1)S(1)}, bf16[256,768]{1,0:T(8,128)(2,1)S(1)}, u32[]{:S(2)}, u32[]{:S(2)}) collective-permute-start(bf16[256,768]{1,0:T(8,128)(2,1)S(1)} %get-tuple-element.154.after_ref), channel_id=1, source_target_pairs={{0,4},{4,0},{8,12},{12,8},{1,5},{5,1},{9,13},{13,9},{2,6},{6,2},{1... | collective-permute-start | bytes 1179656 | tf_op jit(solution)/shard_map/ppermute | solution.py:104
  57.1 10.5 %collective-permute-start.13 = (bf16[256,768]{1,0:T(8,128)(2,1)S(1)}, bf16[256,768]{1,0:T(8,128)(2,1)S(1)}, u32[]{:S(2)}, u32[]{:S(2)}) collective-permute-start(bf16[256,768]{1,0:T(8,128)(2,1)S(1)} %add_convert_fusion.5), channel_id=1, source_target_pairs={{0,1},{1,0},{2,3},{3,2},{4,8},{5,9},{6,10},{7,11},{8,4},{9,5},{10,... | collective-permute-start | bytes 1179656 | tf_op jit(solution)/shard_map/ppermute | solution.py:107
  58.2 20.9 %collective-permute-start.14 = (bf16[256,768]{1,0:T(8,128)(2,1)S(1)}, bf16[256,768]{1,0:T(8,128)(2,1)S(1)}, u32[]{:S(2)}, u32[]{:S(2)}) collective-permute-start(bf16[256,768]{1,0:T(8,128)(2,1)S(1)} %get-tuple-element.146.after_ref), channel_id=1, source_target_pairs={{0,4},{4,0},{8,12},{12,8},{1,5},{5,1},{9,13},{13,9},{2,6},{6,2},{1... | collective-permute-start | bytes 1179656 | tf_op jit(solution)/shard_map/ppermute | solution.py:104
  67.6 11.8 %collective-permute-start.15 = (bf16[256,768]{1,0:T(8,128)(2,1)S(1)}, bf16[256,768]{1,0:T(8,128)(2,1)S(1)}, u32[]{:S(2)}, u32[]{:S(2)}) collective-permute-start(bf16[256,768]{1,0:T(8,128)(2,1)S(1)} %add_convert_fusion.4), channel_id=1, source_target_pairs={{0,1},{1,0},{2,3},{3,2},{4,8},{5,9},{6,10},{7,11},{8,4},{9,5},{10,... | collective-permute-start | bytes 1179656 | tf_op jit(solution)/shard_map/ppermute | solution.py:107
  68.4 13.0 %collective-permute-start.16 = (bf16[256,768]{1,0:T(8,128)(2,1)S(1)}, bf16[256,768]{1,0:T(8,128)(2,1)S(1)}, u32[]{:S(2)}, u32[]{:S(2)}) collective-permute-start(bf16[256,768]{1,0:T(8,128)(2,1)S(1)} %get-tuple-element.138), channel_id=1, source_target_pairs={{0,4},{4,0},{8,12},{12,8},{1,5},{5,1},{9,13},{13,9},{2,6},{6,2},{1... | collective-permute-start | bytes 1179656 | tf_op jit(solution)/shard_map/ppermute | solution.py:104
  73.9 1.4 %copy-start.3 = (bf16[6144,128]{1,0:T(8,128)(2,1)S(1)}, bf16[6144,128]{1,0:T(8,128)(2,1)}, u32[]{:S(2)}) copy-start(bf16[6144,128]{1,0:T(8,128)(2,1)} %param.20) | copy-start | bytes 4718596
  79.2 8.9 %collective-permute-start.17 = (bf16[256,768]{1,0:T(8,128)(2,1)S(1)}, bf16[256,768]{1,0:T(8,128)(2,1)S(1)}, u32[]{:S(2)}, u32[]{:S(2)}) collective-permute-start(bf16[256,768]{1,0:T(8,128)(2,1)S(1)} %add_convert_fusion.3), channel_id=1, source_target_pairs={{0,1},{1,0},{2,3},{3,2},{4,8},{5,9},{6,10},{7,11},{8,4},{9,5},{10,... | collective-permute-start | bytes 1179656 | tf_op jit(solution)/shard_map/ppermute | solution.py:107
  81.5 15.1 %collective-permute-start.19 = (bf16[256,768]{1,0:T(8,128)(2,1)S(1)}, bf16[256,768]{1,0:T(8,128)(2,1)S(1)}, u32[]{:S(2)}, u32[]{:S(2)}) collective-permute-start(bf16[256,768]{1,0:T(8,128)(2,1)S(1)} %add_convert_fusion.2), channel_id=1, source_target_pairs={{0,1},{1,0},{2,3},{3,2},{4,8},{5,9},{6,10},{7,11},{8,4},{9,5},{10,... | collective-permute-start | bytes 1179656 | tf_op jit(solution)/shard_map/ppermute | solution.py:107
  81.6 13.2 %collective-permute-start.20 = (bf16[256,768]{1,0:T(8,128)(2,1)S(1)}, bf16[256,768]{1,0:T(8,128)(2,1)S(1)}, u32[]{:S(2)}, u32[]{:S(2)}) collective-permute-start(bf16[256,768]{1,0:T(8,128)(2,1)S(1)} %pad_maximum_fusion.12), channel_id=1, source_target_pairs={{0,4},{4,0},{8,12},{12,8},{1,5},{5,1},{9,13},{13,9},{2,6},{6,2},{1... | collective-permute-start | bytes 1179656 | tf_op jit(solution)/shard_map/ppermute | solution.py:104
  88.8 13.5 %collective-permute-start.18 = (bf16[256,768]{1,0:T(8,128)(2,1)S(1)}, bf16[256,768]{1,0:T(8,128)(2,1)S(1)}, u32[]{:S(2)}, u32[]{:S(2)}) collective-permute-start(bf16[256,768]{1,0:T(8,128)(2,1)S(1)} %pad_maximum_fusion.14), channel_id=1, source_target_pairs={{0,4},{4,0},{8,12},{12,8},{1,5},{5,1},{9,13},{13,9},{2,6},{6,2},{1... | collective-permute-start | bytes 1179656 | tf_op jit(solution)/shard_map/ppermute | solution.py:104
  96.8 2.7 %collective-permute-start.22 = (bf16[64,2688]{1,0:T(8,128)(2,1)S(1)}, bf16[64,2688]{1,0:T(8,128)(2,1)S(1)}, u32[]{:S(2)}, u32[]{:S(2)}) collective-permute-start(bf16[64,2688]{1,0:T(8,128)(2,1)S(1)} %fusion.47), channel_id=1, source_target_pairs={{0,1},{1,0},{2,3},{3,2},{4,5},{5,4},{6,7},{7,6},{8,9},{9,8},{10,11... | collective-permute-start | bytes 1032200 | tf_op jit(solution)/shard_map/ppermute | solution.py:101
  97.4 12.6 %collective-permute-start.21 = (bf16[256,768]{1,0:T(8,128)(2,1)S(1)}, bf16[256,768]{1,0:T(8,128)(2,1)S(1)}, u32[]{:S(2)}, u32[]{:S(2)}) collective-permute-start(bf16[256,768]{1,0:T(8,128)(2,1)S(1)} %pad_maximum_fusion.18), channel_id=1, source_target_pairs={{0,4},{4,0},{8,12},{12,8},{1,5},{5,1},{9,13},{13,9},{2,6},{6,2},{1... | collective-permute-start | bytes 1179656 | tf_op jit(solution)/shard_map/ppermute | solution.py:104
  99.6 12.4 %collective-permute-start.23 = (bf16[64,2688]{1,0:T(8,128)(2,1)S(1)}, bf16[64,2688]{1,0:T(8,128)(2,1)S(1)}, u32[]{:S(2)}, u32[]{:S(2)}) collective-permute-start(bf16[64,2688]{1,0:T(8,128)(2,1)S(1)} %fusion.45), channel_id=1, source_target_pairs={{0,2},{1,3},{2,0},{3,1},{4,6},{5,7},{6,4},{7,5},{8,10},{9,11},{10,... | collective-permute-start | bytes 1032200 | tf_op jit(solution)/shard_map/ppermute | solution.py:101
  113.5 1.8 %copy-start.7 = (f32[2560]{0:T(1024)S(1)}, f32[2560]{0:T(1024)}, u32[]{:S(2)}) copy-start(f32[2560]{0:T(1024)} %param.19) | copy-start | bytes 30724
  113.6 1.7 %collective-permute-start.24 = (bf16[64,2688]{1,0:T(8,128)(2,1)S(1)}, bf16[64,2688]{1,0:T(8,128)(2,1)S(1)}, u32[]{:S(2)}, u32[]{:S(2)}) collective-permute-start(bf16[64,2688]{1,0:T(8,128)(2,1)S(1)} %fusion.46), channel_id=1, source_target_pairs={{0,1},{1,0},{2,3},{3,2},{4,5},{5,4},{6,7},{7,6},{8,9},{9,8},{10,11... | collective-permute-start | bytes 1032200 | tf_op jit(solution)/shard_map/ppermute | solution.py:101

commit v18 on v16

--- a/solution.py
+++ b/solution.py
@@ -266,8 +266,10 @@
             if t == 1:
                 whole = tie((gathered_near, gathered_far), last)
                 gathered = jnp.concatenate(whole, axis=0)
-            if LAG <= t < LAG + 2 * early:
+            if LAG <= t < LAG + 2 * early - 1:
                 load_second(t - LAG)
+            elif t == UNITS - 1:
+                load_second(2 * early - 1)
             if 1 <= t <= early:
                 load(early + t - 1)
                 first_late(2 * early + t - 1, gathered)

time: 117 us -> 119 us (1.017)
  waiting for transfers between devices: 23.3 us -> 26.6 us
    ppermute x11, waiting for transfers between devices: 20.3 us -> 23.4 us  [end_swap(): return lax.ppermute(value, 'row', [(i, i ^ 1) for i in range(n_row)])]
  transfers between devices with their start and end apart: 25 -> 25, of which waited for: 7 -> 8; matrix products, arithmetic and copies ran while one was open for 25% -> 24% of each run, Pallas kernels for 22% -> 22%
where the time goes in v18:
time: 119 us
  starting transfers between devices  31.2 us (26%)
  waiting for transfers between devices  26.6 us (22%)
  matrix products  26.1 us (22%)
  Pallas kernels  26 us (22%)
  other arithmetic  3.88 us (3%)
  local copies, waits for them, and re-layouts  3.62 us (3%)
  between operations  1.3 us (1%)
    ppermute x11, starting transfers between devices, end_swap(): return lax.ppermute(value, 'row', [(i, i ^ 1) for i in range(n_row)])  26.6 us
    dot_general x33, matrix products, dot(): return jnp.dot(left, right, preferred_element_type=F32)  26.1 us
    pallas_call x8, Pallas kernels, load_part(): pl.pallas_call(functools.partial(load_kernel, part=part), in_specs=[pl.Bl...  26 us
    ppermute x11, waiting for transfers between devices, end_swap(): return lax.ppermute(value, 'row', [(i, i ^ 1) for i in range(n_row)])  23.4 us
    ppermute x6, starting transfers between devices, col_swap(): return lax.ppermute(value, 'col', [(i, i ^ flip) for i in range(n_col)])  3.99 us
    ppermute x6, waiting for transfers between devices, col_swap(): return lax.ppermute(value, 'col', [(i, i ^ flip) for i in range(n_col)])  3.23 us
  transfers between devices with their start and end apart: 25, of which 8 were waited for; matrix products, arithmetic and copies ran while one was open for 24% of the time, Pallas kernels for 22%

profile of v18, /device:TPU:0, one launch (start us, length us, event | category | flops | bytes accessed | tf_op | source)
XLA Modules:
  0.0 118.8 jit_solution(14033123694562132597)
XLA Ops:
  0.0 0.5 collective-permute-start.2
  0.5 2.6 %collective-permute-start = (bf16[64,2560]{1,0:T(8,128)(2,1)}, bf16[64,2560]{1,0:T(8,128)(2,1)S(1)}, u32[]{:S(2)}, u32[]{:S(2)}) collective-permute-start(bf16[64,2560]{1,0:T(8,128)(2,1)} %param.11), channel_id=1, source_target_pairs={{0,2},{1,3},{2,0},{3,1},{4,6},{5,7},{6,4},{7,5},{8,10},{9,11},{10,... | collective-permute-start | bytes 983048 | tf_op jit(solution)/shard_map/ppermute | solution.py:101
  3.0 0.7 copy-done.1
  3.7 3.3 %shard_map.109 = bf16[2560,1536]{1,0:T(8,128)(2,1)S(1)} custom-call(bf16[2560,6144]{1,0:T(8,128)(2,1)} %w_hbm.11, s32[4]{0:T(128)S(1)} %copy-done.1), custom_call_target="tpu_custom_call" | custom-call | bytes 1000 | tf_op jit(solution)/shard_map/pallas_call | solution.py:51
  7.1 0.3 convolution_convert_fusion.7
  7.5 1.2 convolution_convert_fusion.5
  8.7 1.6 %collective-permute-start.3 = (bf16[288,768]{1,0:T(8,128)(2,1)S(1)}, bf16[288,768]{1,0:T(8,128)(2,1)S(1)}, u32[]{:S(2)}, u32[]{:S(2)}) collective-permute-start(bf16[288,768]{1,0:T(8,128)(2,1)S(1)} %pad_maximum_fusion.2.after_ref), channel_id=1, source_target_pairs={{0,4},{4,0},{8,12},{12,8},{1,5},{5,1},{9,13},{13,9},{2,6},{6,2},{1... | collective-permute-start | bytes 1327112 | tf_op jit(solution)/shard_map/ppermute | solution.py:104
  10.4 3.2 %shard_map.110 = bf16[2560,1536]{1,0:T(8,128)(2,1)S(1)} custom-call(bf16[2560,6144]{1,0:T(8,128)(2,1)} %w_hbm.11, bf16[288,768]{1,0:T(8,128)(2,1)S(1)} %pad_maximum_fusion.2.after_ref), custom_call_target="tpu_custom_call" | custom-call | bytes 1000 | tf_op jit(solution)/shard_map/pallas_call | solution.py:51
  13.6 1.2 %convolution_convert_fusion.4 = bf16[128,1536]{1,0:T(8,128)(2,1)S(1)} fusion(bf16[128,2560]{1,0:T(8,128)(2,1)S(1)} %constant_dynamic-update-slice_fusion.2, bf16[2560,1536]{1,0:T(8,128)(2,1)S(1)} %shard_map.110), kind=kOutput, calls=%fused_computation.18 | convolution fusion | flops 1006829568 | bytes 8912896 | tf_op jit(solution)/shard_map/dot_general | solution.py:36
  14.9 0.5 collective-permute-start.4
  16.1 1.6 %collective-permute-done.1 = bf16[64,2560]{1,0:T(8,128)(2,1)S(1)} collective-permute-done((bf16[64,2560]{1,0:T(8,128)(2,1)S(1)}, bf16[64,2560]{1,0:T(8,128)(2,1)S(1)}, u32[]{:S(2)}, u32[]{:S(2)}) %collective-permute-start.1) | collective-permute-done | bytes 327712 | tf_op jit(solution)/shard_map/ppermute | solution.py:101
  17.7 0.3 convolution_convert_fusion.6
  18.0 1.2 %convolution_convert_fusion.3 = bf16[128,1536]{1,0:T(8,128)(2,1)S(1)} fusion(bf16[128,2560]{1,0:T(8,128)(2,1)S(1)} %constant_dynamic-update-slice_fusion, bf16[2560,1536]{1,0:T(8,128)(2,1)S(1)} %shard_map.109), kind=kOutput, calls=%fused_computation.17 | convolution fusion | flops 1006829568 | bytes 8912896 | tf_op jit(solution)/shard_map/dot_general | solution.py:36
  19.3 1.6 %collective-permute-start.7 = (bf16[288,768]{1,0:T(8,128)(2,1)S(1)}, bf16[288,768]{1,0:T(8,128)(2,1)S(1)}, u32[]{:S(2)}, u32[]{:S(2)}) collective-permute-start(bf16[288,768]{1,0:T(8,128)(2,1)S(1)} %pad_maximum_fusion.3), channel_id=1, source_target_pairs={{0,4},{4,0},{8,12},{12,8},{1,5},{5,1},{9,13},{13,9},{2,6},{6,2},{1... | collective-permute-start | bytes 1327112 | tf_op jit(solution)/shard_map/ppermute | solution.py:104
  20.9 0.9 collective-permute-done.3
  22.0 1.2 convolution_convert_fusion.2
  23.3 7.0 %collective-permute-done.4 = bf16[256,768]{1,0:T(8,128)(2,1)S(1)} collective-permute-done((bf16[256,768]{1,0:T(8,128)(2,1)S(1)}, bf16[256,768]{1,0:T(8,128)(2,1)S(1)}, u32[]{:S(2)}, u32[]{:S(2)}) %collective-permute-start.4) | collective-permute-done | bytes 393248 | tf_op jit(solution)/shard_map/ppermute | solution.py:104
  30.7 1.1 copy-done.9
  31.8 0.4 fusion.4
  32.4 4.1 %collective-permute-start.6 = (bf16[256,768]{1,0:T(8,128)(2,1)S(1)}, bf16[256,768]{1,0:T(8,128)(2,1)S(1)}, u32[]{:S(2)}, u32[]{:S(2)}) collective-permute-start(bf16[256,768]{1,0:T(8,128)(2,1)S(1)} %maximum_select_fusion.after_ref), channel_id=1, source_target_pairs={{0,4},{4,0},{8,12},{12,8},{1,5},{5,1},{9,13},{13,9},{2,6},{6,2},{1... | collective-permute-start | bytes 1179656 | tf_op jit(solution)/shard_map/ppermute | solution.py:104
  36.5 3.2 %shard_map.111 = bf16[2560,1536]{1,0:T(8,128)(2,1)S(1)} custom-call(bf16[2560,6144]{1,0:T(8,128)(2,1)} %w_hbm.11, bf16[256,768]{1,0:T(8,128)(2,1)S(1)} %maximum_select_fusion.after_ref), custom_call_target="tpu_custom_call" | custom-call | bytes 1000 | tf_op jit(solution)/shard_map/pallas_call | solution.py:51
  39.8 2.2 %convolution_convert_fusion.1 = bf16[256,1536]{1,0:T(8,128)(2,1)S(1)} fusion(bf16[256,2560]{1,0:T(8,128)(2,1)S(1)} %constant_dynamic-update-slice_fusion.4, bf16[2560,1536]{1,0:T(8,128)(2,1)S(1)} %shard_map.111), kind=kOutput, calls=%fused_computation.7 | convolution fusion | flops 2013659136 | bytes 9961472 | tf_op jit(solution)/shard_map/dot_general | solution.py:36
  42.5 0.4 fusion.9
  43.1 3.2 %shard_map.112 = bf16[2560,1536]{1,0:T(8,128)(2,1)S(1)} custom-call(bf16[2560,6144]{1,0:T(8,128)(2,1)} %w_hbm.11, bf16[256,768]{1,0:T(8,128)(2,1)S(1)} %get-tuple-element.156.after_ref), custom_call_target="tpu_custom_call" | custom-call | bytes 1000 | tf_op jit(solution)/shard_map/pallas_call | solution.py:51
  46.4 2.0 %collective-permute-start.10 = (bf16[256,768]{1,0:T(8,128)(2,1)S(1)}, bf16[256,768]{1,0:T(8,128)(2,1)S(1)}, u32[]{:S(2)}, u32[]{:S(2)}) collective-permute-start(bf16[256,768]{1,0:T(8,128)(2,1)S(1)} %get-tuple-element.156.after_ref), channel_id=1, source_target_pairs={{0,4},{4,0},{8,12},{12,8},{1,5},{5,1},{9,13},{13,9},{2,6},{6,2},{1... | collective-permute-start | bytes 1179656 | tf_op jit(solution)/shard_map/ppermute | solution.py:104
  48.3 2.2 %convolution_convert_fusion = bf16[256,1536]{1,0:T(8,128)(2,1)S(1)} fusion(bf16[256,2560]{1,0:T(8,128)(2,1)S(1)} %constant_dynamic-update-slice_fusion.4, bf16[2560,1536]{1,0:T(8,128)(2,1)S(1)} %shard_map.112), kind=kOutput, calls=%fused_computation.6 | convolution fusion | flops 2013659136 | bytes 9961472 | tf_op jit(solution)/shard_map/dot_general | solution.py:36
  51.1 0.4 fusion.14
  51.6 2.1 %collective-permute-start.12 = (bf16[256,768]{1,0:T(8,128)(2,1)S(1)}, bf16[256,768]{1,0:T(8,128)(2,1)S(1)}, u32[]{:S(2)}, u32[]{:S(2)}) collective-permute-start(bf16[256,768]{1,0:T(8,128)(2,1)S(1)} %get-tuple-element.152.after_ref), channel_id=1, source_target_pairs={{0,4},{4,0},{8,12},{12,8},{1,5},{5,1},{9,13},{13,9},{2,6},{6,2},{1... | collective-permute-start | bytes 1179656 | tf_op jit(solution)/shard_map/ppermute | solution.py:104
  53.7 3.2 %shard_map.113 = bf16[1536,2560]{1,0:T(8,128)(2,1)S(1)} custom-call(bf16[6144,2560]{1,0:T(8,128)(2,1)} %w_hbm.15, bf16[256,768]{1,0:T(8,128)(2,1)S(1)} %get-tuple-element.152.after_ref), custom_call_target="tpu_custom_call" | custom-call | bytes 1000 | tf_op jit(solution)/shard_map/pallas_call | solution.py:51
  57.0 1.3 %collective-permute-done.10 = bf16[256,768]{1,0:T(8,128)(2,1)S(1)} collective-permute-done((bf16[256,768]{1,0:T(8,128)(2,1)S(1)}, bf16[256,768]{1,0:T(8,128)(2,1)S(1)}, u32[]{:S(2)}, u32[]{:S(2)}) %collective-permute-start.10) | collective-permute-done | bytes 393248 | tf_op jit(solution)/shard_map/ppermute | solution.py:104
  58.9 0.4 fusion.19
  59.5 3.2 %shard_map.114 = bf16[1536,2560]{1,0:T(8,128)(2,1)S(1)} custom-call(bf16[6144,2560]{1,0:T(8,128)(2,1)} %w_hbm.15, bf16[256,768]{1,0:T(8,128)(2,1)S(1)} %get-tuple-element.144.after_ref), custom_call_target="tpu_custom_call" | custom-call | bytes 1000 | tf_op jit(solution)/shard_map/pallas_call | solution.py:51
  62.7 4.4 %collective-permute-start.14 = (bf16[256,768]{1,0:T(8,128)(2,1)S(1)}, bf16[256,768]{1,0:T(8,128)(2,1)S(1)}, u32[]{:S(2)}, u32[]{:S(2)}) collective-permute-start(bf16[256,768]{1,0:T(8,128)(2,1)S(1)} %get-tuple-element.144.after_ref), channel_id=1, source_target_pairs={{0,4},{4,0},{8,12},{12,8},{1,5},{5,1},{9,13},{13,9},{2,6},{6,2},{1... | collective-permute-start | bytes 1179656 | tf_op jit(solution)/shard_map/ppermute | solution.py:104
  67.5 0.4 fusion.24
  68.1 3.2 %shard_map.115 = bf16[1536,2560]{1,0:T(8,128)(2,1)S(1)} custom-call(bf16[6144,2560]{1,0:T(8,128)(2,1)} %w_hbm.15, bf16[256,768]{1,0:T(8,128)(2,1)S(1)} %get-tuple-element.138.after_ref), custom_call_target="tpu_custom_call" | custom-call | bytes 1000 | tf_op jit(solution)/shard_map/pallas_call | solution.py:51
  71.4 4.9 %collective-permute-start.16 = (bf16[256,768]{1,0:T(8,128)(2,1)S(1)}, bf16[256,768]{1,0:T(8,128)(2,1)S(1)}, u32[]{:S(2)}, u32[]{:S(2)}) collective-permute-start(bf16[256,768]{1,0:T(8,128)(2,1)S(1)} %get-tuple-element.138.after_ref), channel_id=1, source_target_pairs={{0,4},{4,0},{8,12},{12,8},{1,5},{5,1},{9,13},{13,9},{2,6},{6,2},{1... | collective-permute-start | bytes 1179656 | tf_op jit(solution)/shard_map/ppermute | solution.py:104
  76.4 1.2 %fusion.144 = f32[128,2560]{1,0:T(8,128)S(1)} fusion(bf16[128,1536]{1,0:T(8,128)(2,1)S(1)} %pad_maximum_fusion.10, bf16[1536,2560]{1,0:T(8,128)(2,1)S(1)} %shard_map.113), kind=kOutput, calls=%fused_computation.267 | convolution fusion | flops 1006632960 | bytes 9568256 | tf_op jit(solution)/shard_map/dot_general | solution.py:36
  77.7 1.2 %fusion.145 = f32[128,2560]{1,0:T(8,128)S(1)} fusion(bf16[128,1536]{1,0:T(8,128)(2,1)S(1)} %pad_maximum_fusion.14, bf16[1536,2560]{1,0:T(8,128)(2,1)S(1)} %shard_map.113), kind=kOutput, calls=%fused_computation.268 | convolution fusion | flops 1006632960 | bytes 9568256 | tf_op jit(solution)/shard_map/dot_general | solution.py:36
  79.4 0.2 fusion.56
  80.0 0.4 fusion.29
  80.5 3.3 %collective-permute-done.16 = bf16[256,768]{1,0:T(8,128)(2,1)S(1)} collective-permute-done((bf16[256,768]{1,0:T(8,128)(2,1)S(1)}, bf16[256,768]{1,0:T(8,128)(2,1)S(1)}, u32[]{:S(2)}, u32[]{:S(2)}) %collective-permute-start.16) | collective-permute-done | bytes 393248 | tf_op jit(solution)/shard_map/ppermute | solution.py:104
  84.1 3.3 %collective-permute-start.20 = (bf16[256,768]{1,0:T(8,128)(2,1)S(1)}, bf16[256,768]{1,0:T(8,128)(2,1)S(1)}, u32[]{:S(2)}, u32[]{:S(2)}) collective-permute-start(bf16[256,768]{1,0:T(8,128)(2,1)S(1)} %pad_maximum_fusion.11), channel_id=1, source_target_pairs={{0,4},{4,0},{8,12},{12,8},{1,5},{5,1},{9,13},{13,9},{2,6},{6,2},{1... | collective-permute-start | bytes 1179656 | tf_op jit(solution)/shard_map/ppermute | solution.py:104
  87.6 1.2 %convolution_add_fusion.5 = f32[128,2560]{1,0:T(8,128)S(1)} fusion(f32[128,2560]{1,0:T(8,128)S(1)} %fusion.144, bf16[128,1536]{1,0:T(8,128)(2,1)S(1)} %pad_maximum_fusion.12, bf16[1536,2560]{1,0:T(8,128)(2,1)S(1)} %shard_map.114), kind=kOutput, calls=%fused_computation.5 | convolution fusion | flops 1006960640 | bytes 10878976 | tf_op jit(solution)/shard_map/dot_general | solution.py:36
  88.9 1.2 %convolution_add_fusion.4 = f32[128,2560]{1,0:T(8,128)S(1)} fusion(f32[128,2560]{1,0:T(8,128)S(1)} %fusion.145, bf16[128,1536]{1,0:T(8,128)(2,1)S(1)} %pad_maximum_fusion.15, bf16[1536,2560]{1,0:T(8,128)(2,1)S(1)} %shard_map.114), kind=kOutput, calls=%fused_computation.4 | convolution fusion | flops 1006960640 | bytes 10878976 | tf_op jit(solution)/shard_map/dot_general | solution.py:36
  90.1 0.3 convolution_add_fusion.19
  90.3 0.3 convolution_add_fusion.16
  90.8 0.5 fusion.34
  91.3 3.2 %shard_map.116 = bf16[1536,2560]{1,0:T(8,128)(2,1)S(1)} custom-call(bf16[6144,2560]{1,0:T(8,128)(2,1)} %w_hbm.15, bf16[256,768]{1,0:T(8,128)(2,1)S(1)} %pad_maximum_fusion.13.after_ref), custom_call_target="tpu_custom_call" | custom-call | bytes 1000 | tf_op jit(solution)/shard_map/pallas_call | solution.py:51
  94.5 0.9 collective-permute-start.18
  95.6 1.2 %convolution_add_fusion.3 = f32[128,2560]{1,0:T(8,128)S(1)} fusion(f32[128,2560]{1,0:T(8,128)S(1)} %convolution_add_fusion.4, bf16[128,1536]{1,0:T(8,128)(2,1)S(1)} %pad_maximum_fusion.16, bf16[1536,2560]{1,0:T(8,128)(2,1)S(1)} %shard_map.115), kind=kOutput, calls=%fused_computation.3 | convolution fusion | flops 1006960640 | bytes 10878976 | tf_op jit(solution)/shard_map/dot_general | solution.py:36
  96.9 0.3 convolution_add_fusion.18
  97.3 1.2 %convolution_add_fusion.2 = f32[128,2560]{1,0:T(8,128)S(1)} fusion(f32[128,2560]{1,0:T(8,128)S(1)} %convolution_add_fusion.3, bf16[128,1536]{1,0:T(8,128)(2,1)S(1)} %pad_maximum_fusion.17, bf16[1536,2560]{1,0:T(8,128)(2,1)S(1)} %shard_map.116), kind=kOutput, calls=%fused_computation.2 | convolution fusion | flops 1006960640 | bytes 10878976 | tf_op jit(solution)/shard_map/dot_general | solution.py:36
  98.8 0.3 convolution_add_fusion.17
  99.2 0.4 fusion.39
  99.7 1.2 %collective-permute-start.21 = (bf16[256,768]{1,0:T(8,128)(2,1)S(1)}, bf16[256,768]{1,0:T(8,128)(2,1)S(1)}, u32[]{:S(2)}, u32[]{:S(2)}) collective-permute-start(bf16[256,768]{1,0:T(8,128)(2,1)S(1)} %pad_maximum_fusion.18), channel_id=1, source_target_pairs={{0,4},{4,0},{8,12},{12,8},{1,5},{5,1},{9,13},{13,9},{2,6},{6,2},{1... | collective-permute-start | bytes 1179656 | tf_op jit(solution)/shard_map/ppermute | solution.py:104
  100.9 4.4 %collective-permute-done.18 = bf16[256,768]{1,0:T(8,128)(2,1)S(1)} collective-permute-done((bf16[256,768]{1,0:T(8,128)(2,1)S(1)}, bf16[256,768]{1,0:T(8,128)(2,1)S(1)}, u32[]{:S(2)}, u32[]{:S(2)}) %collective-permute-start.18) | collective-permute-done | bytes 393248 | tf_op jit(solution)/shard_map/ppermute | solution.py:104
  105.4 0.8 collective-permute-start.23
  106.1 6.4 %collective-permute-done.21 = bf16[256,768]{1,0:T(8,128)(2,1)S(1)} collective-permute-done((bf16[256,768]{1,0:T(8,128)(2,1)S(1)}, bf16[256,768]{1,0:T(8,128)(2,1)S(1)}, u32[]{:S(2)}, u32[]{:S(2)}) %collective-permute-start.21) | collective-permute-done | bytes 393248 | tf_op jit(solution)/shard_map/ppermute | solution.py:104
  112.8 1.2 %convolution_add_fusion.1 = f32[128,2560]{1,0:T(8,128)S(1)} fusion(f32[128,2560]{1,0:T(8,128)S(1)} %convolution_add_fusion.5, bf16[128,1536]{1,0:T(8,128)(2,1)S(1)} %pad_maximum_fusion.19, bf16[1536,2560]{1,0:T(8,128)(2,1)S(1)} %shard_map.115), kind=kOutput, calls=%fused_computation.1 | convolution fusion | flops 1006960640 | bytes 10878976 | tf_op jit(solution)/shard_map/dot_general | solution.py:36
  114.1 0.3 convolution_add_fusion.15
  114.4 1.3 %convolution_add_fusion = f32[128,2560]{1,0:T(8,128)S(1)} fusion(f32[128,2560]{1,0:T(8,128)S(1)} %convolution_add_fusion.1, bf16[128,1536]{1,0:T(8,128)(2,1)S(1)} %pad_maximum_fusion.20, bf16[1536,2560]{1,0:T(8,128)(2,1)S(1)} %shard_map.116), kind=kOutput, calls=%fused_computation | convolution fusion | flops 1006960640 | bytes 10878976 | tf_op jit(solution)/shard_map/dot_general | solution.py:36
  115.7 0.3 convolution_add_fusion.14
  116.1 1.6 %collective-permute-done.24 = bf16[64,2688]{1,0:T(8,128)(2,1)S(1)} collective-permute-done((bf16[64,2688]{1,0:T(8,128)(2,1)S(1)}, bf16[64,2688]{1,0:T(8,128)(2,1)S(1)}, u32[]{:S(2)}, u32[]{:S(2)}) %collective-permute-start.24) | collective-permute-done | bytes 344096 | tf_op jit(solution)/shard_map/ppermute | solution.py:101
  117.8 1.0 fusion.49
  (154 shorter events, 6.8 us)
Async XLA Ops:
  0.0 117.8 %copy-start = (bf16[128,2560]{1,0:T(8,128)(2,1)S(1)}, bf16[128,2560]{1,0:T(8,128)(2,1)}, u32[]{:S(2)}) copy-start(bf16[128,2560]{1,0:T(8,128)(2,1)} %param.21) | copy-start | bytes 1966084
  0.0 7.0 %collective-permute-start.2 = (bf16[64,2560]{1,0:T(8,128)(2,1)}, bf16[64,2560]{1,0:T(8,128)(2,1)S(1)}, u32[]{:S(2)}, u32[]{:S(2)}) collective-permute-start(bf16[64,2560]{1,0:T(8,128)(2,1)} %param.11), channel_id=1, source_target_pairs={{0,1},{1,0},{2,3},{3,2},{4,5},{5,4},{6,7},{7,6},{8,9},{9,8},{10,11... | collective-permute-start | bytes 983048 | tf_op jit(solution)/shard_map/ppermute | solution.py:101
  0.5 15.5 %collective-permute-start = (bf16[64,2560]{1,0:T(8,128)(2,1)}, bf16[64,2560]{1,0:T(8,128)(2,1)S(1)}, u32[]{:S(2)}, u32[]{:S(2)}) collective-permute-start(bf16[64,2560]{1,0:T(8,128)(2,1)} %param.11), channel_id=1, source_target_pairs={{0,2},{1,3},{2,0},{3,1},{4,6},{5,7},{6,4},{7,5},{8,10},{9,11},{10,... | collective-permute-start | bytes 983048 | tf_op jit(solution)/shard_map/ppermute | solution.py:101
  3.0 0.7 copy-start.1
  3.7 3.3 %copy-start.5 = (bf16[64,2560]{1,0:T(8,128)(2,1)S(1)}, bf16[64,2560]{1,0:T(8,128)(2,1)}, u32[]{:S(2)}) copy-start(bf16[64,2560]{1,0:T(8,128)(2,1)} %param.11) | copy-start | bytes 983044
  3.7 3.4 %copy-start.4 = (bf16[2560,128]{1,0:T(8,128)(2,1)S(1)}, bf16[2560,128]{1,0:T(8,128)(2,1)}, u32[]{:S(2)}) copy-start(bf16[2560,128]{1,0:T(8,128)(2,1)} %param.16) | copy-start | bytes 1966084
  8.7 13.1 %collective-permute-start.3 = (bf16[288,768]{1,0:T(8,128)(2,1)S(1)}, bf16[288,768]{1,0:T(8,128)(2,1)S(1)}, u32[]{:S(2)}, u32[]{:S(2)}) collective-permute-start(bf16[288,768]{1,0:T(8,128)(2,1)S(1)} %pad_maximum_fusion.2.after_ref), channel_id=1, source_target_pairs={{0,4},{4,0},{8,12},{12,8},{1,5},{5,1},{9,13},{13,9},{2,6},{6,2},{1... | collective-permute-start | bytes 1327112 | tf_op jit(solution)/shard_map/ppermute | solution.py:104
  14.8 0.7 copy-start.2
  14.8 0.7 copy-start.8
  14.9 1.0 copy-start.6
  14.9 15.3 %collective-permute-start.4 = (bf16[256,768]{1,0:T(8,128)(2,1)S(1)}, bf16[256,768]{1,0:T(8,128)(2,1)S(1)}, u32[]{:S(2)}, u32[]{:S(2)}) collective-permute-start(bf16[256,768]{1,0:T(8,128)(2,1)S(1)} %pad_maximum_fusion.4), channel_id=1, source_target_pairs={{0,4},{4,0},{8,12},{12,8},{1,5},{5,1},{9,13},{13,9},{2,6},{6,2},{1... | collective-permute-start | bytes 1179656 | tf_op jit(solution)/shard_map/ppermute | solution.py:104
  15.9 1.7 %collective-permute-start.1 = (bf16[64,2560]{1,0:T(8,128)(2,1)S(1)}, bf16[64,2560]{1,0:T(8,128)(2,1)S(1)}, u32[]{:S(2)}, u32[]{:S(2)}) collective-permute-start(bf16[64,2560]{1,0:T(8,128)(2,1)S(1)} %collective-permute-done), channel_id=1, source_target_pairs={{0,1},{1,0},{2,3},{3,2},{4,5},{5,4},{6,7},{7,6},{8,9},{9,8},{10,11... | collective-permute-start | bytes 983048 | tf_op jit(solution)/shard_map/ppermute | solution.py:101
  19.3 22.8 %collective-permute-start.7 = (bf16[288,768]{1,0:T(8,128)(2,1)S(1)}, bf16[288,768]{1,0:T(8,128)(2,1)S(1)}, u32[]{:S(2)}, u32[]{:S(2)}) collective-permute-start(bf16[288,768]{1,0:T(8,128)(2,1)S(1)} %pad_maximum_fusion.3), channel_id=1, source_target_pairs={{0,4},{4,0},{8,12},{12,8},{1,5},{5,1},{9,13},{13,9},{2,6},{6,2},{1... | collective-permute-start | bytes 1327112 | tf_op jit(solution)/shard_map/ppermute | solution.py:104
  21.9 8.5 %collective-permute-start.5 = (bf16[288,768]{1,0:T(8,128)(2,1)S(1)}, bf16[288,768]{1,0:T(8,128)(2,1)S(1)}, u32[]{:S(2)}, u32[]{:S(2)}) collective-permute-start(bf16[288,768]{1,0:T(8,128)(2,1)S(1)} %add_convert_fusion.1), channel_id=1, source_target_pairs={{0,1},{1,0},{2,3},{3,2},{4,8},{5,9},{6,10},{7,11},{8,4},{9,5},{10,... | collective-permute-start | bytes 1327112 | tf_op jit(solution)/shard_map/ppermute | solution.py:107
  30.4 1.4 %copy-start.9 = (bf16[128,6144]{1,0:T(8,128)(2,1)S(1)}, bf16[128,6144]{1,0:T(8,128)(2,1)}, u32[]{:S(2)}) copy-start(bf16[128,6144]{1,0:T(8,128)(2,1)} %param.17) | copy-start | bytes 4718596
  30.4 12.0 %collective-permute-start.8 = (bf16[256,768]{1,0:T(8,128)(2,1)S(1)}, bf16[256,768]{1,0:T(8,128)(2,1)S(1)}, u32[]{:S(2)}, u32[]{:S(2)}) collective-permute-start(bf16[256,768]{1,0:T(8,128)(2,1)S(1)} %add_convert_fusion.7), channel_id=1, source_target_pairs={{0,1},{1,0},{2,3},{3,2},{4,8},{5,9},{6,10},{7,11},{8,4},{9,5},{10,... | collective-permute-start | bytes 1179656 | tf_op jit(solution)/shard_map/ppermute | solution.py:107
  32.4 18.3 %collective-permute-start.6 = (bf16[256,768]{1,0:T(8,128)(2,1)S(1)}, bf16[256,768]{1,0:T(8,128)(2,1)S(1)}, u32[]{:S(2)}, u32[]{:S(2)}) collective-permute-start(bf16[256,768]{1,0:T(8,128)(2,1)S(1)} %maximum_select_fusion.after_ref), channel_id=1, source_target_pairs={{0,4},{4,0},{8,12},{12,8},{1,5},{5,1},{9,13},{13,9},{2,6},{6,2},{1... | collective-permute-start | bytes 1179656 | tf_op jit(solution)/shard_map/ppermute | solution.py:104
  42.2 8.6 %collective-permute-start.9 = (bf16[288,768]{1,0:T(8,128)(2,1)S(1)}, bf16[288,768]{1,0:T(8,128)(2,1)S(1)}, u32[]{:S(2)}, u32[]{:S(2)}) collective-permute-start(bf16[288,768]{1,0:T(8,128)(2,1)S(1)} %add_convert_fusion), channel_id=1, source_target_pairs={{0,1},{1,0},{2,3},{3,2},{4,8},{5,9},{6,10},{7,11},{8,4},{9,5},{10,... | collective-permute-start | bytes 1327112 | tf_op jit(solution)/shard_map/ppermute | solution.py:107
  46.4 12.0 %collective-permute-start.10 = (bf16[256,768]{1,0:T(8,128)(2,1)S(1)}, bf16[256,768]{1,0:T(8,128)(2,1)S(1)}, u32[]{:S(2)}, u32[]{:S(2)}) collective-permute-start(bf16[256,768]{1,0:T(8,128)(2,1)S(1)} %get-tuple-element.156.after_ref), channel_id=1, source_target_pairs={{0,4},{4,0},{8,12},{12,8},{1,5},{5,1},{9,13},{13,9},{2,6},{6,2},{1... | collective-permute-start | bytes 1179656 | tf_op jit(solution)/shard_map/ppermute | solution.py:104
  50.8 7.8 %collective-permute-start.11 = (bf16[256,768]{1,0:T(8,128)(2,1)S(1)}, bf16[256,768]{1,0:T(8,128)(2,1)S(1)}, u32[]{:S(2)}, u32[]{:S(2)}) collective-permute-start(bf16[256,768]{1,0:T(8,128)(2,1)S(1)} %add_convert_fusion.6), channel_id=1, source_target_pairs={{0,1},{1,0},{2,3},{3,2},{4,8},{5,9},{6,10},{7,11},{8,4},{9,5},{10,... | collective-permute-start | bytes 1179656 | tf_op jit(solution)/shard_map/ppermute | solution.py:107
  51.6 15.5 %collective-permute-start.12 = (bf16[256,768]{1,0:T(8,128)(2,1)S(1)}, bf16[256,768]{1,0:T(8,128)(2,1)S(1)}, u32[]{:S(2)}, u32[]{:S(2)}) collective-permute-start(bf16[256,768]{1,0:T(8,128)(2,1)S(1)} %get-tuple-element.152.after_ref), channel_id=1, source_target_pairs={{0,4},{4,0},{8,12},{12,8},{1,5},{5,1},{9,13},{13,9},{2,6},{6,2},{1... | collective-permute-start | bytes 1179656 | tf_op jit(solution)/shard_map/ppermute | solution.py:104
  58.5 8.9 %collective-permute-start.13 = (bf16[256,768]{1,0:T(8,128)(2,1)S(1)}, bf16[256,768]{1,0:T(8,128)(2,1)S(1)}, u32[]{:S(2)}, u32[]{:S(2)}) collective-permute-start(bf16[256,768]{1,0:T(8,128)(2,1)S(1)} %add_convert_fusion.5), channel_id=1, source_target_pairs={{0,1},{1,0},{2,3},{3,2},{4,8},{5,9},{6,10},{7,11},{8,4},{9,5},{10,... | collective-permute-start | bytes 1179656 | tf_op jit(solution)/shard_map/ppermute | solution.py:107
  62.7 16.9 %collective-permute-start.14 = (bf16[256,768]{1,0:T(8,128)(2,1)S(1)}, bf16[256,768]{1,0:T(8,128)(2,1)S(1)}, u32[]{:S(2)}, u32[]{:S(2)}) collective-permute-start(bf16[256,768]{1,0:T(8,128)(2,1)S(1)} %get-tuple-element.144.after_ref), channel_id=1, source_target_pairs={{0,4},{4,0},{8,12},{12,8},{1,5},{5,1},{9,13},{13,9},{2,6},{6,2},{1... | collective-permute-start | bytes 1179656 | tf_op jit(solution)/shard_map/ppermute | solution.py:104
  67.3 12.6 %collective-permute-start.15 = (bf16[256,768]{1,0:T(8,128)(2,1)S(1)}, bf16[256,768]{1,0:T(8,128)(2,1)S(1)}, u32[]{:S(2)}, u32[]{:S(2)}) collective-permute-start(bf16[256,768]{1,0:T(8,128)(2,1)S(1)} %add_convert_fusion.4), channel_id=1, source_target_pairs={{0,1},{1,0},{2,3},{3,2},{4,8},{5,9},{6,10},{7,11},{8,4},{9,5},{10,... | collective-permute-start | bytes 1179656 | tf_op jit(solution)/shard_map/ppermute | solution.py:107
  71.4 12.5 %collective-permute-start.16 = (bf16[256,768]{1,0:T(8,128)(2,1)S(1)}, bf16[256,768]{1,0:T(8,128)(2,1)S(1)}, u32[]{:S(2)}, u32[]{:S(2)}) collective-permute-start(bf16[256,768]{1,0:T(8,128)(2,1)S(1)} %get-tuple-element.138.after_ref), channel_id=1, source_target_pairs={{0,4},{4,0},{8,12},{12,8},{1,5},{5,1},{9,13},{13,9},{2,6},{6,2},{1... | collective-permute-start | bytes 1179656 | tf_op jit(solution)/shard_map/ppermute | solution.py:104
  77.7 1.4 %copy-start.3 = (bf16[6144,128]{1,0:T(8,128)(2,1)S(1)}, bf16[6144,128]{1,0:T(8,128)(2,1)}, u32[]{:S(2)}) copy-start(bf16[6144,128]{1,0:T(8,128)(2,1)} %param.20) | copy-start | bytes 4718596
  79.8 10.8 %collective-permute-start.17 = (bf16[256,768]{1,0:T(8,128)(2,1)S(1)}, bf16[256,768]{1,0:T(8,128)(2,1)S(1)}, u32[]{:S(2)}, u32[]{:S(2)}) collective-permute-start(bf16[256,768]{1,0:T(8,128)(2,1)S(1)} %add_convert_fusion.3), channel_id=1, source_target_pairs={{0,1},{1,0},{2,3},{3,2},{4,8},{5,9},{6,10},{7,11},{8,4},{9,5},{10,... | collective-permute-start | bytes 1179656 | tf_op jit(solution)/shard_map/ppermute | solution.py:107
  84.0 14.6 %collective-permute-start.19 = (bf16[256,768]{1,0:T(8,128)(2,1)S(1)}, bf16[256,768]{1,0:T(8,128)(2,1)S(1)}, u32[]{:S(2)}, u32[]{:S(2)}) collective-permute-start(bf16[256,768]{1,0:T(8,128)(2,1)S(1)} %add_convert_fusion.2), channel_id=1, source_target_pairs={{0,1},{1,0},{2,3},{3,2},{4,8},{5,9},{6,10},{7,11},{8,4},{9,5},{10,... | collective-permute-start | bytes 1179656 | tf_op jit(solution)/shard_map/ppermute | solution.py:107
  84.1 13.0 %collective-permute-start.20 = (bf16[256,768]{1,0:T(8,128)(2,1)S(1)}, bf16[256,768]{1,0:T(8,128)(2,1)S(1)}, u32[]{:S(2)}, u32[]{:S(2)}) collective-permute-start(bf16[256,768]{1,0:T(8,128)(2,1)S(1)} %pad_maximum_fusion.11), channel_id=1, source_target_pairs={{0,4},{4,0},{8,12},{12,8},{1,5},{5,1},{9,13},{13,9},{2,6},{6,2},{1... | collective-permute-start | bytes 1179656 | tf_op jit(solution)/shard_map/ppermute | solution.py:104
  94.5 10.8 %collective-permute-start.18 = (bf16[256,768]{1,0:T(8,128)(2,1)S(1)}, bf16[256,768]{1,0:T(8,128)(2,1)S(1)}, u32[]{:S(2)}, u32[]{:S(2)}) collective-permute-start(bf16[256,768]{1,0:T(8,128)(2,1)S(1)} %pad_maximum_fusion.13.after_ref), channel_id=1, source_target_pairs={{0,4},{4,0},{8,12},{12,8},{1,5},{5,1},{9,13},{13,9},{2,6},{6,2},{1... | collective-permute-start | bytes 1179656 | tf_op jit(solution)/shard_map/ppermute | solution.py:104
  99.1 6.2 %collective-permute-start.22 = (bf16[64,2688]{1,0:T(8,128)(2,1)S(1)}, bf16[64,2688]{1,0:T(8,128)(2,1)S(1)}, u32[]{:S(2)}, u32[]{:S(2)}) collective-permute-start(bf16[64,2688]{1,0:T(8,128)(2,1)S(1)} %fusion.47), channel_id=1, source_target_pairs={{0,1},{1,0},{2,3},{3,2},{4,5},{5,4},{6,7},{7,6},{8,9},{9,8},{10,11... | collective-permute-start | bytes 1032200 | tf_op jit(solution)/shard_map/ppermute | solution.py:101
  99.7 12.8 %collective-permute-start.21 = (bf16[256,768]{1,0:T(8,128)(2,1)S(1)}, bf16[256,768]{1,0:T(8,128)(2,1)S(1)}, u32[]{:S(2)}, u32[]{:S(2)}) collective-permute-start(bf16[256,768]{1,0:T(8,128)(2,1)S(1)} %pad_maximum_fusion.18), channel_id=1, source_target_pairs={{0,4},{4,0},{8,12},{12,8},{1,5},{5,1},{9,13},{13,9},{2,6},{6,2},{1... | collective-permute-start | bytes 1179656 | tf_op jit(solution)/shard_map/ppermute | solution.py:104
  105.4 9.0 %collective-permute-start.23 = (bf16[64,2688]{1,0:T(8,128)(2,1)S(1)}, bf16[64,2688]{1,0:T(8,128)(2,1)S(1)}, u32[]{:S(2)}, u32[]{:S(2)}) collective-permute-start(bf16[64,2688]{1,0:T(8,128)(2,1)S(1)} %fusion.45), channel_id=1, source_target_pairs={{0,2},{1,3},{2,0},{3,1},{4,6},{5,7},{6,4},{7,5},{8,10},{9,11},{10,... | collective-permute-start | bytes 1032200 | tf_op jit(solution)/shard_map/ppermute | solution.py:101
  116.0 1.8 %copy-start.7 = (f32[2560]{0:T(1024)S(1)}, f32[2560]{0:T(1024)}, u32[]{:S(2)}) copy-start(f32[2560]{0:T(1024)} %param.19) | copy-start | bytes 30724
  116.0 1.7 %collective-permute-start.24 = (bf16[64,2688]{1,0:T(8,128)(2,1)S(1)}, bf16[64,2688]{1,0:T(8,128)(2,1)S(1)}, u32[]{:S(2)}, u32[]{:S(2)}) collective-permute-start(bf16[64,2688]{1,0:T(8,128)(2,1)S(1)} %fusion.46), channel_id=1, source_target_pairs={{0,1},{1,0},{2,3},{3,2},{4,5},{5,4},{6,7},{7,6},{8,9},{9,8},{10,11... | collective-permute-start | bytes 1032200 | tf_op jit(solution)/shard_map/ppermute | solution.py:101
